TPU v7x, 128 devices: a whole 4x4x4 slice. The times are simulated.
128 devices in a mesh: gx: 8 (over x, z_hi), gy: 16 (over y, z_lo, core).
Axes of the slice: x: 4, y: 4, z: 4 (z_hi: 2, z_lo: 2; z = z_hi * 2 + z_lo), core: 2. Of those that a mesh axis runs over, the one named last changes fastest.
Arguments:
- pre_act: bfloat16 [64, 64, 16, 512], P('gy', 'gx'), may hold values from -6 to 6
- cot: bfloat16 [64, 64, 16, 512], P('gy', 'gx'), may hold values from -6 to 6
- weight: bfloat16 [27, 512, 512], P(None, 'gy'), may hold values from -0.0546875 to 0.0546875
Outputs:
- grad_pre: bfloat16 [64, 64, 16, 512], P('gy', 'gx')
- grad_weight: float32 [27, 512, 512], P(None, 'gy')
All inputs are finite; a program needn't handle non-finite values.
Results may differ from a plain program's by a relative error of at most 0.0029.
Values may be sent and summed in bfloat16 or wider, within the bound.
No kernel may reach another device: no remote copies, remote signals or barrier semaphores. Data moves between devices by JAX's collectives and lax.ppermute only.
A program may use at most 192 MiB of HBM per device.

v0:
```python
import math

import jax
import jax.numpy as jnp
from jax import lax
from jax.sharding import PartitionSpec as P


def with_halo(block, sides, width):
    for axis, dim in sides:
        count = lax.axis_size(axis)
        forward = [(i, i + 1) for i in range(count - 1)]
        backward = [(target, source) for source, target in forward]
        low = lax.ppermute(
            lax.slice_in_dim(block, block.shape[dim] - width, None, axis=dim), axis, forward
        )
        high = lax.ppermute(lax.slice_in_dim(block, 0, width, axis=dim), axis, backward)
        block = jnp.concatenate([low, block, high], axis=dim)
    return block


def tap_offsets():
    return [(a, b, c) for a in (-1, 0, 1) for b in (-1, 0, 1) for c in (-1, 0, 1)]


def columns(padded, first_row, count, width, depth):
    pieces = []
    for a, b, c in tap_offsets():
        pieces.append(
            lax.dynamic_slice(
                padded, (first_row + 1 - a, 1 - b, 1 - c, 0), (count, width, depth, padded.shape[3])
            )
        )
    stacked = jnp.concatenate(pieces, axis=3)
    return stacked.reshape(count * width * depth, stacked.shape[3])


def body(pre_act, cot, weight):
    rows, width, depth, chan = pre_act.shape
    owned = weight.shape[1]
    norm = 1.0 / math.sqrt(rows * lax.axis_size("gy") * width * lax.axis_size("gx") * depth)
    pre32 = pre_act.astype(jnp.float32)
    sig = jax.nn.sigmoid(pre32)
    act = (pre32 * sig).astype(jnp.bfloat16)
    slab = lax.all_to_all(cot, "gy", split_axis=3, concat_axis=0, tiled=True)
    rimmed = with_halo(slab, (("gx", 1),), 1)
    padded = jnp.pad(rimmed, ((1, 1), (0, 0), (1, 1), (0, 0)))
    piece = lax.all_gather(act, "gy", axis=0, tiled=True)
    count = piece.shape[0]
    cols = columns(padded, jnp.int32(0), count, width, depth)
    flat = piece.reshape(count * width * depth, chan)
    summed = lax.dot_general(
        cols, flat, (((0,), (0,)), ((), ())), preferred_element_type=jnp.float32
    )
    grad_weight = (lax.psum(summed, "gx") * norm).reshape(27, owned, chan)
    flat_weight = weight.reshape(27 * owned, chan)
    count = rows * lax.axis_size("gy")
    cols = columns(padded, jnp.int32(0), count, width, depth)
    grad_act = lax.psum_scatter(
        jnp.dot(cols, flat_weight, preferred_element_type=jnp.float32).reshape(
            count, width, depth, chan
        ),
        "gy",
        scatter_dimension=0,
        tiled=True,
    )
    grad_pre = (grad_act * sig * (1.0 + pre32 * (1.0 - sig))).astype(jnp.bfloat16)
    return (grad_pre, grad_weight)


def solution(mesh):
    return jax.shard_map(
        body,
        mesh=mesh,
        in_specs=(P("gy", "gx", None, None), P("gy", "gx", None, None), P(None, "gy", None)),
        out_specs=(P("gy", "gx", None, None), P(None, "gy", None)),
        check_vma=False,
    )
```

profile of v0, /device:TPU:0, one launch (start us, length us, event | category | flops | bytes accessed | tf_op | source)
XLA Modules:
  0.0 516.8 jit_solution(13246402729821311652)
XLA Ops:
  7.2 0.0 copy-start
  7.2 0.0 reduce-scatter.2.cloned.1.call-start
  7.2 7.3 %copy.8 = bf16[4,8,16,512]{2,1,0,3:T(8,128)(2,1)} copy(bf16[4,8,16,512]{3,2,1,0:T(8,128)(2,1)} %param.4) | data formatting | bytes 1048576 | tf_op args[1]
  14.6 5.7 %reshape.20 = bf16[16,2,8192]{2,1,0:T(2,128)(2,1)S(1)} reshape(bf16[512,4,8,16]{3,2,1,0:T(8,128)(2,1)} %bitcast.26) | data formatting | bytes 1048576
  20.3 16.7 %all_to_all.18 = bf16[16,2,8192]{2,1,0:T(2,128)(2,1)S(1)} all-to-all(bf16[16,2,8192]{2,1,0:T(2,128)(2,1)S(1)} %reshape.20), channel_id=1, replica_groups=mesh['gx'=8,'gy'=16] {'gy'}, dimensions={0} | all-to-all | bytes 1048576 | tf_op jit(solution)/shard_map/all_to_all | solution.py:45
  37.0 4.1 reshape.21
  41.1 5.4 %copy.9 = bf16[4,8,16,16,32]{4,2,1,0,3:T(8,128)(2,1)S(1)} copy(bf16[4,8,16,16,32]{2,1,0,4,3:T(8,128)(2,1)} %bitcast.25) | data formatting | bytes 1048576 | tf_op jit(solution)/shard_map/all_to_all | solution.py:45
  46.5 5.5 %collective-permute-start = (bf16[64,1,16,32]{3,2,1,0:T(8,128)(2,1)S(1)}, bf16[64,1,16,32]{3,2,1,0:T(8,128)(2,1)S(1)}, u32[]{:S(2)}, u32[]{:S(2)}) collective-permute-start(bf16[64,1,16,32]{3,2,1,0:T(8,128)(2,1)S(1)} %get-tuple-element.28), channel_id=1, source_target_pairs={{0,16},{16,32},{32,48},{48,64},{64,80},{80,96},{96,112},{1,17},{17... | collective-permute-start | bytes 196616 | tf_op jit(solution)/shard_map/ppermute | solution.py:14
  52.1 1.5 collective-permute-start.1
  53.5 9.0 %collective-permute-done = bf16[64,1,16,32]{3,2,1,0:T(8,128)(2,1)S(1)} collective-permute-done((bf16[64,1,16,32]{3,2,1,0:T(8,128)(2,1)S(1)}, bf16[64,1,16,32]{3,2,1,0:T(8,128)(2,1)S(1)}, u32[]{:S(2)}, u32[]{:S(2)}) %collective-permute-start) | collective-permute-done | bytes 65568 | tf_op jit(solution)/shard_map/ppermute | solution.py:14
  62.6 0.0 collective-permute-done.1
  62.6 4.0 select_maximum_fusion
  66.6 5.6 %fusion.14 = (bf16[64,8,16,32]{3,2,1,0:T(8,128)(2,1)}, bf16[64,8,16,32]{3,2,1,0:T(8,128)(2,1)}, bf16[64,8,16,32]{3,2,1,0:T(8,128)(2,1)}, bf16[64,8,16,32]{3,2,1,0:T(8,128)(2,1)}, bf16[64,8,16,32]{3,2,1,0:T(8,128)(2,1)}) fusion(bf16[66,10,18,32]{3,2,1,0:T(8,128)(2,1)S(1)} %select_maximum_fusion), kind=kLoop, calls=%fused_computation.27 | loop fusion | bytes 5242880 | tf_op jit(solution)/shard_map/dynamic_slice | solution.py:30
  72.2 14.0 %fusion.13 = (bf16[64,8,16,32]{3,2,1,0:T(8,128)(2,1)}, bf16[64,8,16,32]{3,2,1,0:T(8,128)(2,1)}, bf16[64,8,16,32]{3,2,1,0:T(8,128)(2,1)}, bf16[64,8,16,32]{3,2,1,...) fusion(bf16[66,10,18,32]{3,2,1,0:T(8,128)(2,1)S(1)} %select_max, ...), kind=kLoop, calls=%fused_computation.26 | loop fusion | bytes 19922944 | tf_op jit(solution)/shard_map/dynamic_slice | solution.py:30
  86.1 2.5 pad_maximum_fusion
  88.6 50.9 %concatenate.16 = bf16[64,8,16,864]{3,2,1,0:T(8,128)(2,1)} concatenate(bf16[64,8,16,32]{3,2,1,0:T(8,128)(2,1)} %get-tuple-element.25, bf16[64,8,16,32]{3,2,1,0:T(8,128)(2,1)} %get-tuple-element.24, bf16[64,8,16,32]{3,2,1,0:T(8,128)(2,1)} %get-tuple-element.23, bf16[64,8,16,32]{3,2,1,0:T(8,128)(2,1)} %get-tuple-element.22, bf16[64,8,16,32]{3,2,1,0:T(8,128)(2,1)} %get-tuple-element.21, ...), dimensions={3} | concatenate | bytes 28311552 | tf_op jit(solution)/shard_map/concatenate | solution.py:34
  139.5 0.0 copy-done
  139.5 15.4 %fusion.16 = f32[64,8,16,512]{3,2,1,0:T(8,128)} fusion(bf16[64,8,16,864]{3,2,1,0:T(8,128)(2,1)} %concatenate.16, bf16[864,512,1,1]{1,0,3,2:T(8,128)(2,1)S(1)} %bitcast.20), kind=kOutput, calls=%fused_computation.29 | convolution fusion | flops 7247757312 | bytes 31817728 | tf_op jit(solution)/shard_map/dot_general | solution.py:60
  154.9 0.0 copy-start.1
  154.9 0.0 reduce-scatter.2.cloned.1.call-update
  154.9 0.0 all-gather.2.cloned.1.call-start
  155.0 176.8 %reduce-scatter.2.cloned.1.call-done = f32[4,8,16,512]{3,2,1,0:T(8,128)} async-done(((f32[64,8,16,512]{3,2,1,0:T(8,128)}), f32[4,8,16,512]{3,2,1,0:T(8,128)}) %reduce-scatter.2.cloned.1.call-update) | async-done | bytes 1048592 | tf_op jit(solution)/shard_map/reduce_scatter | solution.py:59
  331.7 0.0 copy-done.1
  331.7 2.6 fusion.12
  334.4 0.0 all-gather.2.cloned.1.call-update
  334.4 0.3 all-reduce.3.cloned.1.call-start
  334.7 57.3 %all-gather.2.cloned.1.call-done = bf16[64,8,16,512]{3,2,1,0:T(8,128)(2,1)} async-done(((bf16[4,8,16,512]{3,2,1,0:T(8,128)(2,1)}), bf16[64,8,16,512]{3,2,1,0:T(8,128)(2,1)}) %all-gather.2.cloned.1.call-update) | async-done | bytes 8388624 | tf_op jit(solution)/shard_map/all_gather | solution.py:48
  391.9 13.2 %convolution_bitcast_fusion = f32[864,512]{1,0:T(8,128)} fusion(bf16[64,8,16,864]{3,2,1,0:T(8,128)(2,1)} %concatenate.16, bf16[64,8,16,512]{3,2,1,0:T(8,128)(2,1)} %all-gather.2.cloned.1.call-done), kind=kOutput, calls=%fused_computation.17 | convolution fusion | flops 7247757312 | bytes 24313856 | tf_op jit(solution)/shard_map/dot_general | solution.py:52
  405.1 0.0 all-reduce.3.cloned.1.call-update
  405.2 102.2 %all-reduce.3.cloned.1.call-done = f32[864,512]{1,0:T(8,128)} async-done(((f32[864,512]{1,0:T(8,128)}), f32[864,512]{1,0:T(8,128)}) %all-reduce.3.cloned.1.call-update) | async-done | bytes 1769488 | tf_op jit(solution)/shard_map/psum | solution.py:55
  507.4 2.9 broadcast_multiply_fusion
  (1 shorter events, 0.0 us)
Async XLA Ops:
  7.2 132.3 %copy-start = (bf16[27,32,512]{2,1,0:T(8,128)(2,1)S(1)}, bf16[27,32,512]{2,1,0:T(8,128)(2,1)}, u32[]{:S(2)}) copy-start(bf16[27,32,512]{2,1,0:T(8,128)(2,1)} %param.5) | copy-start | bytes 2654212
  7.2 324.6 %reduce-scatter.2.cloned.1.call-start = ((), (), s32[]{:S(2)}) async-start(), calls=%async_computation.2 | async-start | bytes 17825792 | tf_op jit(solution)/shard_map/reduce_scatter | solution.py:59
  46.5 16.0 %collective-permute-start = (bf16[64,1,16,32]{3,2,1,0:T(8,128)(2,1)S(1)}, bf16[64,1,16,32]{3,2,1,0:T(8,128)(2,1)S(1)}, u32[]{:S(2)}, u32[]{:S(2)}) collective-permute-start(bf16[64,1,16,32]{3,2,1,0:T(8,128)(2,1)S(1)} %get-tuple-element.28), channel_id=1, source_target_pairs={{0,16},{16,32},{32,48},{48,64},{64,80},{80,96},{96,112},{1,17},{17... | collective-permute-start | bytes 196616 | tf_op jit(solution)/shard_map/ppermute | solution.py:14
  52.1 10.5 %collective-permute-start.1 = (bf16[64,1,16,32]{3,2,1,0:T(8,128)(2,1)S(1)}, bf16[64,1,16,32]{3,2,1,0:T(8,128)(2,1)S(1)}, u32[]{:S(2)}, u32[]{:S(2)}) collective-permute-start(bf16[64,1,16,32]{3,2,1,0:T(8,128)(2,1)S(1)} %get-tuple-element.29), channel_id=1, source_target_pairs={{16,0},{32,16},{48,32},{64,48},{80,64},{96,80},{112,96},{17,1},{33... | collective-permute-start | bytes 196616 | tf_op jit(solution)/shard_map/ppermute | solution.py:17
  154.9 176.8 %copy-start.1 = (bf16[4,8,16,512]{3,2,1,0:T(8,128)(2,1)S(1)}, bf16[4,8,16,512]{3,2,1,0:T(8,128)(2,1)}, u32[]{:S(2)}) copy-start(bf16[4,8,16,512]{3,2,1,0:T(8,128)(2,1)} %param.3) | copy-start | bytes 1572868
  154.9 237.0 %all-gather.2.cloned.1.call-start = ((), (), s32[]{:S(2)}) async-start(), calls=%async_computation.3 | async-start | bytes 8912896 | tf_op jit(solution)/shard_map/all_gather | solution.py:48
  334.4 172.9 %all-reduce.3.cloned.1.call-start = ((), (), s32[]{:S(2)}) async-start(), calls=%async_computation.4 | async-start | bytes 3538944 | tf_op jit(solution)/shard_map/psum | solution.py:55
Sparse Core Ops, SparseCore 0:
  155.1 176.6 reduce-scatter.1
  334.5 57.3 all-gather.1
  405.3 102.0 all-reduce.2
where the time goes:
time: 523 us; the launch traced here: 517 us
  waiting for transfers between devices  345 us (66%)
  local copies, waits for them, and re-layouts  93.1 us (18%)
  matrix products  28.6 us (5%)
  blocking collectives  16.7 us (3%)
  between operations  13.8 us (3%)
  other arithmetic  12 us (2%)
  starting transfers between devices  7.32 us (1%)
    reduce_scatter x1, waiting for transfers between devices, body(): lax.psum_scatter(jnp.dot(cols, flat_weight, preferred_element_type=jnp.fl...  177 us
    psum x1, waiting for transfers between devices, body(): grad_weight = (lax.psum(summed, 'gx') * norm).reshape(27, owned, chan)  102 us
    all_gather x1, waiting for transfers between devices, body(): piece = lax.all_gather(act, 'gy', axis=0, tiled=True)  57.3 us
    concatenate x1, local copies, waits for them, and re-layouts, columns(): stacked = jnp.concatenate(pieces, axis=3)  50.9 us
    dynamic_slice x2, local copies, waits for them, and re-layouts, columns(): lax.dynamic_slice(padded, (first_row + 1 - a, 1 - b, 1 - c, 0), (count, w...  19.6 us
    unnamed x7, local copies, waits for them, and re-layouts  17.2 us
    all_to_all x1, blocking collectives, body(): slab = lax.all_to_all(cot, 'gy', split_axis=3, concat_axis=0, tiled=True)  16.7 us
    dot_general x1, matrix products, body(): jnp.dot(cols, flat_weight, preferred_element_type=jnp.float32)  15.4 us
  transfers between devices with their start and end apart: 5, of which 4 were waited for; matrix products, arithmetic and copies ran while one was open for 0% of the time, Pallas kernels for 0%

commit v1 on v0

v1 whole, which is shorter than its diff:
```python
import functools
import math

import jax
import jax.numpy as jnp
from jax import lax
from jax.experimental import pallas as pl
from jax.experimental.pallas import tpu as pltpu
from jax.sharding import PartitionSpec as P

QUAD = 4
RING = 4
F32 = jnp.float32
BF16 = jnp.bfloat16
ANY = pl.BlockSpec(memory_space=pl.ANY)
VMEM = pl.BlockSpec(memory_space=pltpu.VMEM)
LIMIT = 56 * 1024 * 1024


def params():
    return pltpu.CompilerParams(vmem_limit_bytes=LIMIT)


def quad_place():
    return lax.rem(lax.axis_index("gy"), QUAD)


def x_place():
    return lax.div(lax.axis_index("gx"), 2)


def swap(block, k):
    count = lax.axis_size("gy")
    return lax.ppermute(block, "gy", [(g, g ^ k) for g in range(count)])


def swap_far(block, k):
    nx, ny = lax.axis_size("gx"), lax.axis_size("gy")
    far = (k >> 1) & 1
    pairs = [(g * ny + h, (g ^ far) * ny + (h ^ k)) for g in range(nx) for h in range(ny)]
    return lax.ppermute(block, ("gx", "gy"), pairs)


def along_y(block, step, ring):
    count = lax.axis_size("gy")
    pairs = [(g, g + QUAD * step) for g in range(count)]
    if ring:
        pairs = [(s, t % count) for s, t in pairs]
    return lax.ppermute(block, "gy", [(s, t) for s, t in pairs if 0 <= t < count])


def along_x(block, step):
    count = lax.axis_size("gx")
    return lax.ppermute(block, "gx", [(g, (g + 2 * step) % count) for g in range(count)])


def zero_at(value, z, edge):
    return jnp.where(z == edge, 0.0, value)


def act_kernel(p0, p1, p2, p3, out):
    j = quad_place()
    for k, p in enumerate((p0, p1, p2, p3)):
        rows, width, depth, q = p.shape
        cells = rows * width * depth
        pre = p[...].reshape(cells, q).astype(F32)
        act = pre * jax.nn.sigmoid(pre)
        z = lax.rem(lax.broadcasted_iota(jnp.int32, (cells, q), 0), depth)
        low = zero_at(pltpu.roll(act, 1, 0), z, 0)
        high = zero_at(pltpu.roll(act, cells - 1, 0), z, depth - 1)
        at = pl.multiple_of((j ^ k) * cells, cells)
        for c, moved in enumerate((low, act, high)):
            out[c * q:(c + 1) * q, pl.ds(at, cells)] = moved.T.astype(BF16)


def load_cot(pieces, rims, edges, held, sem):
    j = quad_place()
    rows, width = pieces[0].shape[:2]
    copies = []

    def copy(src, dst):
        copies.append(pltpu.make_async_copy(src, dst, sem.at[len(copies)]))
        copies[-1].start()

    for k in range(QUAD):
        at = 1 + (j ^ k) * rows
        copy(pieces[k], held.at[pl.ds(at, rows), pl.ds(1, width)])
        copy(rims[k].at[0], held.at[pl.ds(at, rows), 0])
        copy(rims[k].at[1], held.at[pl.ds(at, rows), width + 1])
    for side, edge in zip((0, held.shape[0] - 1), edges):
        copy(edge, held.at[side])
    for c in copies:
        c.wait()


def weight_kernel(first, count, norm, *refs):
    pieces, rims = refs[:4], refs[4:8]
    refs = refs[8:]
    edges, refs = ((), refs) if (first, count) == (0, 1) else (refs[:2], refs[2:])
    act, right, left, keep_right, keep_left, own, held, turned, sem = refs
    load_cot(pieces, rims, edges, held, sem)
    x = x_place()
    rows, width, depth, chan = held.shape
    rows, width = rows - 2, width - 2
    q = act.shape[0] // 3
    groups, _, small, _ = turned.shape
    half = groups // 2

    def step(n, carry):
        a = first + 2 * lax.div(n, 3) if count == 2 else first + lax.div(n, 3)
        b = lax.rem(n, 3) - 1
        moved = held[pl.ds(1 - a, rows), pl.ds(1 - b, width)].reshape(rows * width * depth, chan)
        term = jnp.dot(act[...], moved, preferred_element_type=F32) * norm
        for c in range(3):
            turned[...] = term[c * q:(c + 1) * q].T.reshape(turned.shape)
            tap = 3 * n + c

            def block(r):
                at = lax.rem(x + r, RING)
                v = turned[:, pl.ds(at, 1)].reshape(groups, small, q)
                return v[:half].reshape(half * small, q), v[half:].reshape(half * small, q)

            v0, v1 = block(2)
            right[0, tap] = v0.astype(BF16)
            left[0, tap] = v1.astype(BF16)
            v0, v1 = block(1)
            keep_right[tap] = v0
            right[1, tap] = v1.astype(BF16)
            v0, v1 = block(3)
            left[1, tap] = v0.astype(BF16)
            keep_left[tap] = v1
            v0, v1 = block(0)
            own[0, tap] = v0
            own[1, tap] = v1
        return carry

    lax.fori_loop(0, 3 * count, step, 0)


def weight_terms(first, count, norm, pieces, rims, edges, act):
    rows, width, depth, chan = pieces[0].shape
    q = chan // QUAD
    taps = 9 * count
    half = chan // RING // 2
    small = chan // 16 // RING
    cells = QUAD * rows * width * depth
    ins = (*pieces, *rims, *edges, act)
    shapes = [
        jax.ShapeDtypeStruct((2, taps, half, q), BF16),
        jax.ShapeDtypeStruct((2, taps, half, q), BF16),
        jax.ShapeDtypeStruct((taps, half, q), F32),
        jax.ShapeDtypeStruct((taps, half, q), F32),
        jax.ShapeDtypeStruct((2, taps, half, q), F32),
    ]
    return pl.pallas_call(
        functools.partial(weight_kernel, first, count, norm),
        out_shape=shapes,
        in_specs=[ANY] * (len(ins) - 1) + [VMEM],
        out_specs=[VMEM] * 5,
        scratch_shapes=[
            pltpu.VMEM((QUAD * rows + 2, width + 2, depth, chan), BF16),
            pltpu.VMEM((16, RING, small, q), F32),
            pltpu.SemaphoreType.DMA((14,)),
        ],
        compiler_params=params(),
        cost_estimate=pl.CostEstimate(
            flops=2 * taps * cells * chan * q, bytes_accessed=10_000_000, transcendentals=0
        ),
    )(*ins)


def input_kernel(*refs):
    pieces, rims, edges = refs[:4], refs[4:8], refs[8:10]
    parts = refs[10:14]
    pres = refs[14:18]
    outs = refs[18:22]
    held, weights, sem, wsem = refs[22:]
    j = quad_place()
    y = lax.div(lax.axis_index("gy"), QUAD)
    copies = []
    for s, part in enumerate(parts):
        own = part.shape[2]
        for k in range(QUAD):
            at = (lax.rem(y + s, RING) * QUAD + (j ^ k)) * own
            at = pl.multiple_of(at, own)
            copies.append(
                pltpu.make_async_copy(
                    part.at[k], weights.at[:, pl.ds(at, own)], wsem.at[s * QUAD + k]
                )
            )
            copies[-1].start()
    load_cot(pieces, rims, edges, held, sem)
    for c in copies:
        c.wait()
    rows, width, depth, q = pres[0].shape
    cells = rows * width * depth
    chan = held.shape[3]
    for k in range(QUAD):
        at = (j ^ k) * rows
        total = jnp.zeros((cells, 3 * q), F32)
        for n in range(9):
            a, b = n // 3 - 1, n % 3 - 1
            moved = held[pl.ds(at + 1 - a, rows), 1 - b:1 - b + width].reshape(cells, chan)
            total = total + jnp.dot(moved, weights[n], preferred_element_type=F32)
        z = lax.rem(lax.broadcasted_iota(jnp.int32, (cells, q), 0), depth)
        grad = total[:, q:2 * q]
        grad = grad + zero_at(pltpu.roll(total[:, :q], cells - 1, 0), z, depth - 1)
        grad = grad + zero_at(pltpu.roll(total[:, 2 * q:], 1, 0), z, 0)
        pre = pres[k][...].reshape(cells, q).astype(F32)
        s = jax.nn.sigmoid(pre)
        grad = grad * s * (1.0 + pre * (1.0 - s))
        outs[k][...] = grad.astype(BF16).reshape(outs[k].shape)


def input_terms(pieces, rims, edges, parts, pres):
    rows, width, depth, chan = pieces[0].shape
    q = chan // QUAD
    cells = QUAD * rows * width * depth
    return pl.pallas_call(
        input_kernel,
        out_shape=[jax.ShapeDtypeStruct((rows, width, depth, q), BF16)] * QUAD,
        in_specs=[ANY] * 14 + [VMEM] * 4,
        out_specs=[VMEM] * QUAD,
        scratch_shapes=[
            pltpu.VMEM((QUAD * rows + 2, width + 2, depth, chan), BF16),
            pltpu.VMEM((9, chan, 3 * q), BF16),
            pltpu.SemaphoreType.DMA((14,)),
            pltpu.SemaphoreType.DMA((16,)),
        ],
        compiler_params=params(),
        cost_estimate=pl.CostEstimate(
            flops=2 * 27 * cells * chan * q, bytes_accessed=10_000_000, transcendentals=0
        ),
    )(*pieces, *rims, *edges, *parts, *pres)


def join_kernel(axis, place, *refs):
    pieces, out, sem = refs[:-2], refs[-2], refs[-1]
    size = pieces[0].shape[axis]
    copies = []
    for k, piece in enumerate(pieces):
        at = pl.multiple_of(place(k) * size, size)
        spot = out.at[(slice(None),) * axis + (pl.ds(at, size),)]
        copies.append(pltpu.make_async_copy(piece, spot, sem.at[k]))
        copies[-1].start()
    for c in copies:
        c.wait()


def join(pieces, axis, place):
    shape = list(pieces[0].shape)
    shape[axis] *= len(pieces)
    return pl.pallas_call(
        functools.partial(join_kernel, axis, place),
        out_shape=jax.ShapeDtypeStruct(tuple(shape), pieces[0].dtype),
        in_specs=[ANY] * len(pieces),
        out_specs=ANY,
        scratch_shapes=[pltpu.SemaphoreType.DMA((len(pieces),))],
        compiler_params=params(),
    )(*pieces)


def reduce_x(right, left, keep_right, keep_left, own):
    from_left = along_x(right, 1)
    from_right = along_x(left, -1)
    next_right = (from_left[0].astype(F32) + keep_right).astype(BF16)
    next_left = (from_right[0].astype(F32) + keep_left).astype(BF16)
    last_left = along_x(next_right, 1)
    last_right = along_x(next_left, -1)
    low = own[0] + from_right[1].astype(F32) + last_left.astype(F32)
    high = own[1] + from_left[1].astype(F32) + last_right.astype(F32)
    return jnp.concatenate([low, high], axis=1)


def reduce_rest(total, owned):
    y = lax.div(lax.axis_index("gy"), QUAD)
    j = quad_place()
    size = total.shape[1] // RING

    def block(r):
        return lax.dynamic_slice_in_dim(total, lax.rem(y + r, RING) * size, size, axis=1)

    mine = block(0)
    for r in (1, 2, 3):
        mine = mine + along_y(block(r).astype(BF16), r, True).astype(F32)
    count = lax.axis_size("gx")
    other = lax.ppermute(mine.astype(BF16), "gx", [(g, g ^ 1) for g in range(count)])
    mine = mine + other.astype(F32)
    small = size // QUAD

    def part(k):
        return lax.dynamic_slice_in_dim(mine, (j ^ k) * small, small, axis=1)

    pieces = [part(0)] + [swap(part(k), k) for k in (1, 2, 3)]
    whole = join(pieces, 2, lambda k: quad_place() ^ k)
    parts = [whole, along_x(whole, 1), along_x(whole, 2), along_x(whole, -1)]
    return join(parts, 1, lambda k: lax.rem(x_place() + RING - k, RING))


def body(pre_act, cot, weight):
    rows, width, depth, chan = pre_act.shape
    owned = weight.shape[1]
    q = chan // QUAD
    norm = 1.0 / math.sqrt(rows * lax.axis_size("gy") * width * lax.axis_size("gx") * depth)
    j = quad_place()
    nx = lax.axis_size("gx")

    from_low = lax.ppermute(cot[:, width - 1], "gx", [(g, g + 1) for g in range(nx - 1)])
    from_high = lax.ppermute(cot[:, 0], "gx", [(g + 1, g) for g in range(nx - 1)])
    far = swap(cot, 2)
    pieces = [cot, swap(cot, 1), far, swap(far, 1)]
    rim = jnp.stack([from_low, from_high])
    rim_far = swap(rim, 2)
    rims = [rim, swap(rim, 1), rim_far, swap(rim_far, 1)]

    def edge_row(owner, row):
        k = j ^ owner
        parts = [
            jnp.concatenate([r[0, row][None], p[row], r[1, row][None]], axis=0)
            for p, r in zip(pieces, rims)
        ]
        return jnp.where(
            k < 2, jnp.where(k == 0, parts[0], parts[1]), jnp.where(k == 2, parts[2], parts[3])
        )

    edges = [
        along_y(edge_row(QUAD - 1, rows - 1), 1, False),
        along_y(edge_row(0, 0), -1, False),
    ]

    def quarter(k):
        return lax.dynamic_slice_in_dim(pre_act, (j ^ k) * q, q, axis=3)

    pres = [quarter(0)] + [swap(quarter(k), k) for k in (1, 2, 3)]

    taps = weight.reshape(9, 3, owned, chan)

    def weight_quarter(k):
        part = lax.dynamic_slice_in_dim(taps, (j ^ k) * q, q, axis=3)
        return part.transpose(0, 2, 1, 3).reshape(9, owned, 3 * q)

    near = jnp.stack([weight_quarter(0)] + [swap_far(weight_quarter(k), k) for k in (1, 2, 3)])
    above = along_y(near, -1, True)
    below = along_y(near, 1, True)
    across = jnp.concatenate([along_y(below[:2], 1, True), along_y(above[2:], -1, True)])
    parts = [near, above, across, below]

    act = pl.pallas_call(
        act_kernel,
        out_shape=jax.ShapeDtypeStruct((3 * q, QUAD * rows * width * depth), BF16),
        in_specs=[VMEM] * QUAD,
        out_specs=VMEM,
        compiler_params=params(),
    )(*pres)

    mid = reduce_x(*weight_terms(0, 1, norm, pieces, rims, [], act))
    rest = reduce_x(*weight_terms(-1, 2, norm, pieces, rims, edges, act))
    total = jnp.concatenate([rest[:9], mid, rest[9:]])
    grad_weight = reduce_rest(total, owned)

    outs = input_terms(pieces, rims, edges, parts, pres)
    outs = [outs[0]] + [swap(outs[k], k) for k in (1, 2, 3)]
    grad_pre = join(outs, 3, lambda k: quad_place() ^ k)
    return (grad_pre, grad_weight)


def solution(mesh):
    return jax.shard_map(
        body,
        mesh=mesh,
        in_specs=(P("gy", "gx", None, None), P("gy", "gx", None, None), P(None, "gy", None)),
        out_specs=(P("gy", "gx", None, None), P(None, "gy", None)),
        check_vma=False,
    )
```

time: 523 us -> 266 us (0.51)
  waiting for transfers between devices: 345 us -> 60.3 us
  Pallas kernels: 0 us -> 125 us
  local copies, waits for them, and re-layouts: 93.1 us -> 17 us
  starting transfers between devices: 7.32 us -> 53.3 us
  matrix products: 28.6 us -> 0 us
  blocking collectives: 16.7 us -> 0 us
  between operations: 13.8 us -> 1.48 us
  other arithmetic: 12 us -> 6.44 us
    reduce_scatter x1 -> x0, waiting for transfers between devices: 177 us -> none  [body(): lax.psum_scatter(jnp.dot(cols, flat_weight, preferred_element_type=jnp.fl...]
    pallas_call x0 -> x7, Pallas kernels: none -> 125 us  [the longest x3 86.3 us: join(): pl.pallas_call(functools.partial(join_kernel, axis, place), out_shape=jax...]
    psum x1 -> x0, waiting for transfers between devices: 102 us -> none  [body(): grad_weight = (lax.psum(summed, 'gx') * norm).reshape(27, owned, chan)]
    all_gather x1 -> x0, waiting for transfers between devices: 57.3 us -> none  [body(): piece = lax.all_gather(act, 'gy', axis=0, tiled=True)]
    ppermute x2 -> x41, waiting for transfers between devices: 9.03 us -> 60.3 us  [the longest x9 26.3 us: along_y(): lax.ppermute(block, 'gy', [(s, t) for s, t in pairs if 0 <= t < count])]
    concatenate x1 -> x0, local copies, waits for them, and re-layouts: 50.9 us -> none  [columns(): stacked = jnp.concatenate(pieces, axis=3)]
    ppermute x2 -> x41, starting transfers between devices: 6.98 us -> 53.3 us  [the longest x11 18.6 us: along_x(): lax.ppermute(block, 'gx', [(g, (g + 2 * step) % count) for g in range(cou...]
    dot_general x2 -> x0, matrix products: 28.6 us -> none  [the longest x1 15.4 us: body(): jnp.dot(cols, flat_weight, preferred_element_type=jnp.float32)]
  transfers between devices with their start and end apart: 5 -> 41, of which waited for: 4 -> 16; matrix products, arithmetic and copies ran while one was open for 0% -> 7% of each run, Pallas kernels for 0% -> 21%
where the time goes in v1:
time: 266 us; the launch traced here: 264 us
  Pallas kernels  125 us (47%)
  waiting for transfers between devices  60.3 us (23%)
  starting transfers between devices  53.3 us (20%)
  local copies, waits for them, and re-layouts  17 us (6%)
  other arithmetic  6.44 us (2%)
    pallas_call x3, Pallas kernels, join(): pl.pallas_call(functools.partial(join_kernel, axis, place), out_shape=jax...  86.3 us
    ppermute x9, waiting for transfers between devices, along_y(): lax.ppermute(block, 'gy', [(s, t) for s, t in pairs if 0 <= t < count])  26.3 us
    pallas_call x2, Pallas kernels, weight_terms(): pl.pallas_call(functools.partial(weight_kernel, first, count, norm), out_...  21 us
    ppermute x11, starting transfers between devices, along_x(): lax.ppermute(block, 'gx', [(g, (g + 2 * step) % count) for g in range(cou...  18.6 us
    ppermute x9, starting transfers between devices, along_y(): lax.ppermute(block, 'gy', [(s, t) for s, t in pairs if 0 <= t < count])  17.1 us
    pallas_call x1, Pallas kernels, input_terms(): pl.pallas_call(input_kernel, out_shape=[jax.ShapeDtypeStruct((rows, width...  14.9 us
    ppermute x11, waiting for transfers between devices, along_x(): lax.ppermute(block, 'gx', [(g, (g + 2 * step) % count) for g in range(cou...  12.9 us
    ppermute x15, waiting for transfers between devices, swap(): return lax.ppermute(block, 'gy', [(g, g ^ k) for g in range(count)])  12.3 us
  transfers between devices with their start and end apart: 41, of which 16 were waited for; matrix products, arithmetic and copies ran while one was open for 7% of the time, Pallas kernels for 21%

profile of v1, /device:TPU:0, one launch (start us, length us, event | category | flops | bytes accessed | tf_op | source)
XLA Modules:
  0.0 263.7 jit_solution(6062776450542892815)
XLA Ops:
  0.6 2.1 collective-permute-start.1
  3.6 1.3 collective-permute-start.4
  4.9 6.1 %collective-permute-start.3 = (bf16[4,16,512]{2,1,0:T(8,128)(2,1)S(1)}, bf16[4,16,512]{2,1,0:T(8,128)(2,1)S(1)}, u32[]{:S(2)}, u32[]{:S(2)}) collective-permute-start(bf16[4,16,512]{2,1,0:T(8,128)(2,1)S(1)} %get-tuple-element.53), channel_id=1, source_target_pairs={{0,16},{16,32},{32,48},{48,64},{64,80},{80,96},{96,112},{1,17},{17... | collective-permute-start | bytes 196616 | tf_op jit(solution)/shard_map/ppermute | solution.py:308
  11.1 1.8 constant_dynamic-slice_fusion.4
  12.9 1.0 slice_bitcast_fusion.10
  13.9 6.4 %collective-permute-done.4 = bf16[4,16,512]{2,1,0:T(8,128)(2,1)S(1)} collective-permute-done((bf16[4,16,512]{2,1,0:T(8,128)(2,1)S(1)}, bf16[4,16,512]{2,1,0:T(8,128)(2,1)S(1)}, u32[]{:S(2)}, u32[]{:S(2)}) %collective-permute-start.4) | collective-permute-done | bytes 65568 | tf_op jit(solution)/shard_map/ppermute | solution.py:309
  20.4 1.9 collective-permute-start
  22.5 2.9 %collective-permute-done.19.refs_17_.p3 = bf16[4,8,16,128]{3,2,1,0:T(8,128)(2,1)S(1)} collective-permute-done((bf16[4,8,16,128]{3,2,1,0:T(8,128)(2,1)S(1)}, bf16[4,8,16,128]{3,2,1,0:T(8,128)(2,1)S(1)}, u32[]{:S(2)}, u32[]{:S(2)}) %collective-permute-start.19) | collective-permute-done | bytes 131104 | tf_op jit(solution)/shard_map/ppermute | solution.py:34
  26.1 2.9 %shard_map.52.refs_10_.refs_8_ = bf16[384,2048]{1,0:T(8,128)(2,1)} custom-call(bf16[4,8,16,128]{3,2,1,0:T(8,128)(2,1)} %get-tuple-element.43.refs_14_.p0, bf16[4,8,16,128]{3,2,1,0:T(8,128)(2,1)} %copy-done.11, bf16[4,8,16,128]{3,2,1,0:T(8,128)(2,1)} %copy-done.12, bf16[4,8,16,128]{3,2,1,0:T(8,128)(2,1)} %copy-done.13), custom_call_target="tpu_custom_call" | custom-call | tf_op jit(solution)/shard_map/pallas_call | solution.py:348
  31.3 3.5 %collective-permute-start.8 = (bf16[10,16,512]{2,1,0:T(8,128)(2,1)S(1)}, bf16[10,16,512]{2,1,0:T(8,128)(2,1)S(1)}, u32[]{:S(2)}, u32[]{:S(2)}) collective-permute-start(bf16[10,16,512]{2,1,0:T(8,128)(2,1)S(1)} %fusion.6), channel_id=1, source_target_pairs={{0,4},{1,5},{2,6},{3,7},{4,8},{5,9},{6,10},{7,11},{8,12},{9,13},{1... | collective-permute-start | bytes 491528 | tf_op jit(solution)/shard_map/ppermute | solution.py:49
  34.9 1.3 collective-permute-start.9
  36.2 8.2 %shard_map.54 = (bf16[2,9,64,128]{3,2,1,0:T(8,128)(2,1)}, bf16[2,9,64,128]{3,2,1,0:T(8,128)(2,1)}, f32[9,64,128]{2,1,0:T(8,128)}, f32[9,64,128]{2,1,0:T(8,128)}, f32[2,9,64,128]{3,2,1,0:T(8,128)}) custom-call(bf16[4,8,16,512]{3,2,1,0:T(8,128)(2,1)} %refs_0_.5, bf16[4,8,16,512]{3,2,1,0:T(8,128)(2,1)} %copy-done.15, bf16[4,8,16,512]{3,2,1,0:T(8,128)(2,1)} %copy-done.14, ...), custom_call_target="tpu_custom_call" | custom-call | flops 2415919104 | bytes 10000000 | tf_op jit(solution)/shard_map/pallas_call | solution.py:155
  44.5 3.4 %collective-permute-start.28 = (bf16[2,9,64,128]{3,2,1,0:T(8,128)(2,1)}, bf16[2,9,64,128]{3,2,1,0:T(8,128)(2,1)S(1)}, u32[]{:S(2)}, u32[]{:S(2)}) collective-permute-start(bf16[2,9,64,128]{3,2,1,0:T(8,128)(2,1)} %get-tuple-element.27), channel_id=1, source_target_pairs={{0,32},{16,48},{32,64},{48,80},{64,96},{80,112},{96,0},{112,16},{1... | collective-permute-start | bytes 884744 | tf_op jit(solution)/shard_map/ppermute | solution.py:54
  47.9 1.4 collective-permute-start.27
  50.6 12.8 %shard_map.53 = (bf16[2,18,64,128]{3,2,1,0:T(8,128)(2,1)}, bf16[2,18,64,128]{3,2,1,0:T(8,128)(2,1)}, f32[18,64,128]{2,1,0:T(8,128)}, f32[18,64,128]{2,1,0:T(8,128)}, f32[2,18,64,128]{3,2,1,0:T(8,128)}) custom-call(bf16[4,8,16,512]{3,2,1,0:T(8,128)(2,1)} %refs_0_.5, bf16[4,8,16,512]{3,2,1,0:T(8,128)(2,1)} %copy-done.15, bf16[4,8,16,512]{3,2,1,0:T(8,128)(2,1)} %copy-done.14, ...), custom_call_target="tpu_custom_call" | custom-call | flops 4831838208 | bytes 10000000 | tf_op jit(solution)/shard_map/pallas_call | solution.py:155
  65.4 0.9 reshape.34
  66.4 2.1 collective-permute-start.11
  69.9 3.0 %collective-permute-start.23 = (bf16[2,18,64,128]{3,2,1,0:T(8,128)(2,1)}, bf16[2,18,64,128]{3,2,1,0:T(8,128)(2,1)S(1)}, u32[]{:S(2)}, u32[]{:S(2)}) collective-permute-start(bf16[2,18,64,128]{3,2,1,0:T(8,128)(2,1)} %get-tuple-element.21), channel_id=1, source_target_pairs={{0,96},{16,112},{32,0},{48,16},{64,32},{80,48},{96,64},{112,80},{1... | collective-permute-start | bytes 1769480 | tf_op jit(solution)/shard_map/ppermute | solution.py:54
  72.9 1.0 fusion.5
  74.4 5.5 %collective-permute-done.24 = bf16[2,18,64,128]{3,2,1,0:T(8,128)(2,1)S(1)} collective-permute-done((bf16[2,18,64,128]{3,2,1,0:T(8,128)(2,1)}, bf16[2,18,64,128]{3,2,1,0:T(8,128)(2,1)S(1)}, u32[]{:S(2)}, u32[]{:S(2)}) %collective-permute-start.24) | collective-permute-done | bytes 589856 | tf_op jit(solution)/shard_map/ppermute | solution.py:54
  80.0 6.7 %collective-permute-done.23 = bf16[2,18,64,128]{3,2,1,0:T(8,128)(2,1)S(1)} collective-permute-done((bf16[2,18,64,128]{3,2,1,0:T(8,128)(2,1)}, bf16[2,18,64,128]{3,2,1,0:T(8,128)(2,1)S(1)}, u32[]{:S(2)}, u32[]{:S(2)}) %collective-permute-start.23) | collective-permute-done | bytes 589856 | tf_op jit(solution)/shard_map/ppermute | solution.py:54
  86.6 3.6 %collective-permute-start.30 = (bf16[9,64,128]{2,1,0:T(8,128)(2,1)S(1)}, bf16[9,64,128]{2,1,0:T(8,128)(2,1)S(1)}, u32[]{:S(2)}, u32[]{:S(2)}) collective-permute-start(bf16[9,64,128]{2,1,0:T(8,128)(2,1)S(1)} %fusion.4), channel_id=1, source_target_pairs={{0,96},{16,112},{32,0},{48,16},{64,32},{80,48},{96,64},{112,80},{1... | collective-permute-start | bytes 442376 | tf_op jit(solution)/shard_map/ppermute | solution.py:54
  90.4 3.2 %collective-permute-start.26 = (bf16[18,64,128]{2,1,0:T(8,128)(2,1)S(1)}, bf16[18,64,128]{2,1,0:T(8,128)(2,1)S(1)}, u32[]{:S(2)}, u32[]{:S(2)}) collective-permute-start(bf16[18,64,128]{2,1,0:T(8,128)(2,1)S(1)} %fusion.2), channel_id=1, source_target_pairs={{0,96},{16,112},{32,0},{48,16},{64,32},{80,48},{96,64},{112,80},{1... | collective-permute-start | bytes 884744 | tf_op jit(solution)/shard_map/ppermute | solution.py:54
  93.6 1.3 pad_maximum_fusion.refs_10_
  94.9 4.3 %collective-permute-start.13 = (bf16[4,9,32,384]{3,2,1,0:T(8,128)(2,1)S(1)}, bf16[4,9,32,384]{3,2,1,0:T(8,128)(2,1)}, u32[]{:S(2)}, u32[]{:S(2)}) collective-permute-start(bf16[4,9,32,384]{3,2,1,0:T(8,128)(2,1)S(1)} %pad_maximum_fusion.refs_10_), channel_id=1, source_target_pairs={{0,12},{1,13},{2,14},{3,15},{4,0},{5,1},{6,2},{7,3},{8,4},{9,5},{1... | collective-permute-start | bytes 2654216 | tf_op jit(solution)/shard_map/ppermute | solution.py:49
  100.6 0.9 dynamic-slice_convert_fusion.2
  101.5 4.3 %collective-permute-start.33 = (bf16[27,32,128]{2,1,0:T(8,128)(2,1)}, bf16[27,32,128]{2,1,0:T(8,128)(2,1)S(1)}, u32[]{:S(2)}, u32[]{:S(2)}) collective-permute-start(bf16[27,32,128]{2,1,0:T(8,128)(2,1)} %get-tuple-element.31), channel_id=1, source_target_pairs={{0,12},{1,13},{2,14},{3,15},{4,0},{5,1},{6,2},{7,3},{8,4},{9,5},{1... | collective-permute-start | bytes 663560 | tf_op jit(solution)/shard_map/ppermute | solution.py:49
  106.4 1.0 collective-permute-start.31
  107.4 19.8 %collective-permute-done.33 = bf16[27,32,128]{2,1,0:T(8,128)(2,1)S(1)} collective-permute-done((bf16[27,32,128]{2,1,0:T(8,128)(2,1)}, bf16[27,32,128]{2,1,0:T(8,128)(2,1)S(1)}, u32[]{:S(2)}, u32[]{:S(2)}) %collective-permute-start.33) | collective-permute-done | bytes 221216 | tf_op jit(solution)/shard_map/ppermute | solution.py:49
  127.2 3.3 %collective-permute-done.31 = bf16[27,32,128]{2,1,0:T(8,128)(2,1)S(1)} collective-permute-done((bf16[27,32,128]{2,1,0:T(8,128)(2,1)S(1)}, bf16[27,32,128]{2,1,0:T(8,128)(2,1)S(1)}, u32[]{:S(2)}, u32[]{:S(2)}) %collective-permute-start.31) | collective-permute-done | bytes 221216 | tf_op jit(solution)/shard_map/ppermute | solution.py:49
  130.7 1.9 slice.191
  132.8 1.1 slice.190
  133.9 1.8 collective-permute-start.15
  135.7 2.5 collective-permute-done.34
  138.2 1.1 convert_add_fusion.2
  140.0 1.9 collective-permute-start.37
  141.9 1.2 collective-permute-done.16
  143.0 2.0 collective-permute-done.15
  145.0 2.0 pad_maximum_fusion.1.refs_12_
  148.1 14.5 %shard_map.55.refs_0_ = f32[27,8,512]{2,1,0:T(8,128)} custom-call(f32[27,8,128]{2,1,0:T(8,128)} %get-tuple-element.58.refs_0_, f32[27,8,128]{2,1,0:T(8,128)} %copy-done.21, f32[27,8,128]{2,1,0:T(8,128)} %copy-done.22, f32[27,8,128]{2,1,0:T(8,128)} %copy-done.23), custom_call_target="tpu_custom_call" | custom-call | tf_op jit(solution)/shard_map/pallas_call | solution.py:253
  162.7 2.0 collective-permute-start.39
  164.8 1.2 collective-permute-start.40
  166.0 14.9 %shard_map.50 = (bf16[4,8,16,128]{3,2,1,0:T(8,128)(2,1)}, bf16[4,8,16,128]{3,2,1,0:T(8,128)(2,1)}, bf16[4,8,16,128]{3,2,1,0:T(8,128)(2,1)}, bf16[4,8,16,128]{3,2,1,0:T(8,128)(2,1)}) custom-call(bf16[4,8,16,512]{3,2,1,0:T(8,128)(2,1)} %refs_0_.5, bf16[4,8,16,512]{3,2,1,0:T(8,128)(2,1)} %copy-done.15, bf16[4,8,16,512]{3,2,1,0:T(8,128)(2,1)} %copy-done.14, ...), custom_call_target="tpu_custom_call" | custom-call | flops 7247757312 | bytes 10000000 | tf_op jit(solution)/shard_map/pallas_call | solution.py:219
  181.5 1.0 collective-permute-done.20.refs_1_
  182.8 4.7 %collective-permute-done.21.refs_2_ = bf16[4,8,16,128]{3,2,1,0:T(8,128)(2,1)S(1)} collective-permute-done((bf16[4,8,16,128]{3,2,1,0:T(8,128)(2,1)}, bf16[4,8,16,128]{3,2,1,0:T(8,128)(2,1)S(1)}, u32[]{:S(2)}, u32[]{:S(2)}) %collective-permute-start.21) | collective-permute-done | bytes 131104 | tf_op jit(solution)/shard_map/ppermute | solution.py:34
  187.6 1.9 collective-permute-done.22.refs_3_
  190.1 17.0 %shard_map.51 = bf16[4,8,16,512]{3,2,1,0:T(8,128)(2,1)} custom-call(bf16[4,8,16,128]{3,2,1,0:T(8,128)(2,1)} %get-tuple-element.16.refs_0_, bf16[4,8,16,128]{3,2,1,0:T(8,128)(2,1)} %copy-done.18, bf16[4,8,16,128]{3,2,1,0:T(8,128)(2,1)} %copy-done.19, bf16[4,8,16,128]{3,2,1,0:T(8,128)(2,1)} %copy-done.20), custom_call_target="tpu_custom_call" | custom-call | tf_op jit(solution)/shard_map/pallas_call | solution.py:253
  208.8 54.7 %shard_map.56 = f32[27,32,512]{2,1,0:T(8,128)} custom-call(f32[27,8,512]{2,1,0:T(8,128)} %shard_map.55.refs_0_, f32[27,8,512]{2,1,0:T(8,128)} %copy-done.6, f32[27,8,512]{2,1,0:T(8,128)} %copy-done.7, f32[27,8,512]{2,1,0:T(8,128)} %copy-done.8), custom_call_target="tpu_custom_call" | custom-call | tf_op jit(solution)/shard_map/pallas_call | solution.py:253
  (138 shorter events, 17.2 us)
Async XLA Ops:
  0.6 19.8 %copy-start.10 = (bf16[4,8,16,512]{3,2,1,0:T(8,128)(2,1)S(1)}, bf16[4,8,16,512]{3,2,1,0:T(8,128)(2,1)}, u32[]{:S(2)}) copy-start(bf16[4,8,16,512]{3,2,1,0:T(8,128)(2,1)} %refs_0_.5) | copy-start | bytes 1572868
  0.6 28.4 %collective-permute-start.1 = (bf16[4,8,16,512]{3,2,1,0:T(8,128)(2,1)}, bf16[4,8,16,512]{3,2,1,0:T(8,128)(2,1)S(1)}, u32[]{:S(2)}, u32[]{:S(2)}) collective-permute-start(bf16[4,8,16,512]{3,2,1,0:T(8,128)(2,1)} %refs_0_.5), channel_id=1, source_target_pairs={{0,2},{1,3},{2,0},{3,1},{4,6},{5,7},{6,4},{7,5},{8,10},{9,11},{10,... | collective-permute-start | bytes 1572872 | tf_op jit(solution)/shard_map/ppermute | solution.py:34
  3.6 16.6 %collective-permute-start.4 = (bf16[4,16,512]{2,1,0:T(8,128)(2,1)S(1)}, bf16[4,16,512]{2,1,0:T(8,128)(2,1)S(1)}, u32[]{:S(2)}, u32[]{:S(2)}) collective-permute-start(bf16[4,16,512]{2,1,0:T(8,128)(2,1)S(1)} %get-tuple-element.54), channel_id=1, source_target_pairs={{16,0},{32,16},{48,32},{64,48},{80,64},{96,80},{112,96},{17,1},{33... | collective-permute-start | bytes 196616 | tf_op jit(solution)/shard_map/ppermute | solution.py:309
  4.9 15.4 %collective-permute-start.3 = (bf16[4,16,512]{2,1,0:T(8,128)(2,1)S(1)}, bf16[4,16,512]{2,1,0:T(8,128)(2,1)S(1)}, u32[]{:S(2)}, u32[]{:S(2)}) collective-permute-start(bf16[4,16,512]{2,1,0:T(8,128)(2,1)S(1)} %get-tuple-element.53), channel_id=1, source_target_pairs={{0,16},{16,32},{32,48},{48,64},{64,80},{80,96},{96,112},{1,17},{17... | collective-permute-start | bytes 196616 | tf_op jit(solution)/shard_map/ppermute | solution.py:308
  12.9 7.5 %collective-permute-start.17 = (bf16[4,8,16,128]{3,2,1,0:T(8,128)(2,1)S(1)}, bf16[4,8,16,128]{3,2,1,0:T(8,128)(2,1)S(1)}, u32[]{:S(2)}, u32[]{:S(2)}) collective-permute-start(bf16[4,8,16,128]{3,2,1,0:T(8,128)(2,1)S(1)} %get-tuple-element.42), channel_id=1, source_target_pairs={{0,1},{1,0},{2,3},{3,2},{4,5},{5,4},{6,7},{7,6},{8,9},{9,8},{10,11... | collective-permute-start | bytes 393224 | tf_op jit(solution)/shard_map/ppermute | solution.py:34
  12.9 9.5 %collective-permute-start.18 = (bf16[4,8,16,128]{3,2,1,0:T(8,128)(2,1)S(1)}, bf16[4,8,16,128]{3,2,1,0:T(8,128)(2,1)S(1)}, u32[]{:S(2)}, u32[]{:S(2)}) collective-permute-start(bf16[4,8,16,128]{3,2,1,0:T(8,128)(2,1)S(1)} %get-tuple-element.44), channel_id=1, source_target_pairs={{0,2},{1,3},{2,0},{3,1},{4,6},{5,7},{6,4},{7,5},{8,10},{9,11},{10,... | collective-permute-start | bytes 393224 | tf_op jit(solution)/shard_map/ppermute | solution.py:34
  20.3 5.1 %collective-permute-start.19 = (bf16[4,8,16,128]{3,2,1,0:T(8,128)(2,1)S(1)}, bf16[4,8,16,128]{3,2,1,0:T(8,128)(2,1)S(1)}, u32[]{:S(2)}, u32[]{:S(2)}) collective-permute-start(bf16[4,8,16,128]{3,2,1,0:T(8,128)(2,1)S(1)} %get-tuple-element.41), channel_id=1, source_target_pairs={{0,3},{1,2},{2,1},{3,0},{4,7},{5,6},{6,5},{7,4},{8,11},{9,10},{10,... | collective-permute-start | bytes 393224 | tf_op jit(solution)/shard_map/ppermute | solution.py:34
  20.3 15.9 %copy-start.17 = (bf16[2,4,16,512]{3,2,1,0:T(8,128)(2,1)}, bf16[2,4,16,512]{3,2,1,0:T(8,128)(2,1)S(1)}, u32[]{:S(2)}) copy-start(bf16[2,4,16,512]{3,2,1,0:T(8,128)(2,1)S(1)} %pad_maximum_fusion.2.refs_4_) | copy-start | bytes 393220
  20.3 8.7 %collective-permute-start.6 = (bf16[2,4,16,512]{3,2,1,0:T(8,128)(2,1)S(1)}, bf16[2,4,16,512]{3,2,1,0:T(8,128)(2,1)S(1)}, u32[]{:S(2)}, u32[]{:S(2)}) collective-permute-start(bf16[2,4,16,512]{3,2,1,0:T(8,128)(2,1)S(1)} %pad_maximum_fusion.2.refs_4_), channel_id=1, source_target_pairs={{0,2},{1,3},{2,0},{3,1},{4,6},{5,7},{6,4},{7,5},{8,10},{9,11},{10,... | collective-permute-start | bytes 393224 | tf_op jit(solution)/shard_map/ppermute | solution.py:34
  20.4 9.9 %collective-permute-start = (bf16[4,8,16,512]{3,2,1,0:T(8,128)(2,1)S(1)}, bf16[4,8,16,512]{3,2,1,0:T(8,128)(2,1)S(1)}, u32[]{:S(2)}, u32[]{:S(2)}) collective-permute-start(bf16[4,8,16,512]{3,2,1,0:T(8,128)(2,1)S(1)} %copy-done.10), channel_id=1, source_target_pairs={{0,1},{1,0},{2,3},{3,2},{4,5},{5,4},{6,7},{7,6},{8,9},{9,8},{10,11... | collective-permute-start | bytes 1572872 | tf_op jit(solution)/shard_map/ppermute | solution.py:34
  22.3 6.7 %collective-permute-start.5 = (bf16[2,4,16,512]{3,2,1,0:T(8,128)(2,1)S(1)}, bf16[2,4,16,512]{3,2,1,0:T(8,128)(2,1)S(1)}, u32[]{:S(2)}, u32[]{:S(2)}) collective-permute-start(bf16[2,4,16,512]{3,2,1,0:T(8,128)(2,1)S(1)} %pad_maximum_fusion.2.refs_4_), channel_id=1, source_target_pairs={{0,1},{1,0},{2,3},{3,2},{4,5},{5,4},{6,7},{7,6},{8,9},{9,8},{10,11... | collective-permute-start | bytes 393224 | tf_op jit(solution)/shard_map/ppermute | solution.py:34
  29.0 1.3 collective-permute-start.7
  29.1 2.1 collective-permute-start.2
  31.3 18.0 %collective-permute-start.8 = (bf16[10,16,512]{2,1,0:T(8,128)(2,1)S(1)}, bf16[10,16,512]{2,1,0:T(8,128)(2,1)S(1)}, u32[]{:S(2)}, u32[]{:S(2)}) collective-permute-start(bf16[10,16,512]{2,1,0:T(8,128)(2,1)S(1)} %fusion.6), channel_id=1, source_target_pairs={{0,4},{1,5},{2,6},{3,7},{4,8},{5,9},{6,10},{7,11},{8,12},{9,13},{1... | collective-permute-start | bytes 491528 | tf_op jit(solution)/shard_map/ppermute | solution.py:49
  34.9 14.4 %collective-permute-start.9 = (bf16[10,16,512]{2,1,0:T(8,128)(2,1)S(1)}, bf16[10,16,512]{2,1,0:T(8,128)(2,1)S(1)}, u32[]{:S(2)}, u32[]{:S(2)}) collective-permute-start(bf16[10,16,512]{2,1,0:T(8,128)(2,1)S(1)} %fusion.7), channel_id=1, source_target_pairs={{4,0},{5,1},{6,2},{7,3},{8,4},{9,5},{10,6},{11,7},{12,8},{13,9},{1... | collective-permute-start | bytes 491528 | tf_op jit(solution)/shard_map/ppermute | solution.py:49
  44.5 25.4 %collective-permute-start.28 = (bf16[2,9,64,128]{3,2,1,0:T(8,128)(2,1)}, bf16[2,9,64,128]{3,2,1,0:T(8,128)(2,1)S(1)}, u32[]{:S(2)}, u32[]{:S(2)}) collective-permute-start(bf16[2,9,64,128]{3,2,1,0:T(8,128)(2,1)} %get-tuple-element.27), channel_id=1, source_target_pairs={{0,32},{16,48},{32,64},{48,80},{64,96},{80,112},{96,0},{112,16},{1... | collective-permute-start | bytes 884744 | tf_op jit(solution)/shard_map/ppermute | solution.py:54
  47.9 16.2 %copy-start.2 = (bf16[27,32,512]{2,1,0:T(8,128)(2,1)S(1)}, bf16[27,32,512]{2,1,0:T(8,128)(2,1)}, u32[]{:S(2)}) copy-start(bf16[27,32,512]{2,1,0:T(8,128)(2,1)} %param.5) | copy-start | bytes 2654212
  47.9 26.0 %collective-permute-start.27 = (bf16[2,9,64,128]{3,2,1,0:T(8,128)(2,1)}, bf16[2,9,64,128]{3,2,1,0:T(8,128)(2,1)S(1)}, u32[]{:S(2)}, u32[]{:S(2)}) collective-permute-start(bf16[2,9,64,128]{3,2,1,0:T(8,128)(2,1)} %get-tuple-element.26), channel_id=1, source_target_pairs={{0,96},{16,112},{32,0},{48,16},{64,32},{80,48},{96,64},{112,80},{1... | collective-permute-start | bytes 884744 | tf_op jit(solution)/shard_map/ppermute | solution.py:54
  63.4 16.5 %collective-permute-start.24 = (bf16[2,18,64,128]{3,2,1,0:T(8,128)(2,1)}, bf16[2,18,64,128]{3,2,1,0:T(8,128)(2,1)S(1)}, u32[]{:S(2)}, u32[]{:S(2)}) collective-permute-start(bf16[2,18,64,128]{3,2,1,0:T(8,128)(2,1)} %get-tuple-element.22), channel_id=1, source_target_pairs={{0,32},{16,48},{32,64},{48,80},{64,96},{80,112},{96,0},{112,16},{1... | collective-permute-start | bytes 1769480 | tf_op jit(solution)/shard_map/ppermute | solution.py:54
  65.3 25.0 %collective-permute-start.12 = (bf16[9,32,384]{2,1,0:T(8,128)(2,1)}, bf16[9,32,384]{2,1,0:T(8,128)(2,1)}, u32[]{:S(2)}, u32[]{:S(2)}) collective-permute-start(bf16[9,32,384]{2,1,0:T(8,128)(2,1)} %reshape.35), channel_id=1, source_target_pairs={{0,19},{1,18},{2,17},{3,16},{4,23},{5,22},{6,21},{7,20},{8,27},{9,... | collective-permute-start | bytes 663560 | tf_op jit(solution)/shard_map/ppermute | solution.py:41
  65.4 8.9 %copy-start.9 = (f32[9,64,128]{2,1,0:T(8,128)S(1)}, f32[9,64,128]{2,1,0:T(8,128)}, u32[]{:S(2)}) copy-start(f32[9,64,128]{2,1,0:T(8,128)} %get-tuple-element.29) | copy-start | bytes 884740
  66.4 13.5 %copy-start.5 = (f32[18,64,128]{2,1,0:T(8,128)S(1)}, f32[18,64,128]{2,1,0:T(8,128)}, u32[]{:S(2)}) copy-start(f32[18,64,128]{2,1,0:T(8,128)} %get-tuple-element.23) | copy-start | bytes 1769476
  66.4 24.0 %collective-permute-start.11 = (bf16[9,32,384]{2,1,0:T(8,128)(2,1)}, bf16[9,32,384]{2,1,0:T(8,128)(2,1)}, u32[]{:S(2)}, u32[]{:S(2)}) collective-permute-start(bf16[9,32,384]{2,1,0:T(8,128)(2,1)} %reshape.34), channel_id=1, source_target_pairs={{0,18},{1,19},{2,16},{3,17},{4,22},{5,23},{6,20},{7,21},{8,26},{9,... | collective-permute-start | bytes 663560 | tf_op jit(solution)/shard_map/ppermute | solution.py:41
  69.5 20.7 %copy-start.4 = (f32[18,64,128]{2,1,0:T(8,128)S(1)}, f32[18,64,128]{2,1,0:T(8,128)}, u32[]{:S(2)}) copy-start(f32[18,64,128]{2,1,0:T(8,128)} %get-tuple-element.24) | copy-start | bytes 1769476
  69.9 16.7 %collective-permute-start.23 = (bf16[2,18,64,128]{3,2,1,0:T(8,128)(2,1)}, bf16[2,18,64,128]{3,2,1,0:T(8,128)(2,1)S(1)}, u32[]{:S(2)}, u32[]{:S(2)}) collective-permute-start(bf16[2,18,64,128]{3,2,1,0:T(8,128)(2,1)} %get-tuple-element.21), channel_id=1, source_target_pairs={{0,96},{16,112},{32,0},{48,16},{64,32},{80,48},{96,64},{112,80},{1... | collective-permute-start | bytes 1769480 | tf_op jit(solution)/shard_map/ppermute | solution.py:54
  73.9 19.8 %collective-permute-start.10 = (bf16[9,32,384]{2,1,0:T(8,128)(2,1)}, bf16[9,32,384]{2,1,0:T(8,128)(2,1)S(1)}, u32[]{:S(2)}, u32[]{:S(2)}) collective-permute-start(bf16[9,32,384]{2,1,0:T(8,128)(2,1)} %reshape.33), channel_id=1, source_target_pairs={{0,1},{1,0},{2,3},{3,2},{4,5},{5,4},{6,7},{7,6},{8,9},{9,8},{10,11... | collective-permute-start | bytes 663560 | tf_op jit(solution)/shard_map/ppermute | solution.py:41
  79.9 19.3 %collective-permute-start.29 = (bf16[9,64,128]{2,1,0:T(8,128)(2,1)S(1)}, bf16[9,64,128]{2,1,0:T(8,128)(2,1)S(1)}, u32[]{:S(2)}, u32[]{:S(2)}) collective-permute-start(bf16[9,64,128]{2,1,0:T(8,128)(2,1)S(1)} %fusion.5), channel_id=1, source_target_pairs={{0,32},{16,48},{32,64},{48,80},{64,96},{80,112},{96,0},{112,16},{1... | collective-permute-start | bytes 442376 | tf_op jit(solution)/shard_map/ppermute | solution.py:54
  80.0 19.3 %copy-start.3 = (f32[2,9,64,128]{3,2,1,0:T(8,128)S(1)}, f32[2,9,64,128]{3,2,1,0:T(8,128)}, u32[]{:S(2)}) copy-start(f32[2,9,64,128]{3,2,1,0:T(8,128)} %get-tuple-element.25) | copy-start | bytes 1769476
  86.6 12.6 %collective-permute-start.30 = (bf16[9,64,128]{2,1,0:T(8,128)(2,1)S(1)}, bf16[9,64,128]{2,1,0:T(8,128)(2,1)S(1)}, u32[]{:S(2)}, u32[]{:S(2)}) collective-permute-start(bf16[9,64,128]{2,1,0:T(8,128)(2,1)S(1)} %fusion.4), channel_id=1, source_target_pairs={{0,96},{16,112},{32,0},{48,16},{64,32},{80,48},{96,64},{112,80},{1... | collective-permute-start | bytes 442376 | tf_op jit(solution)/shard_map/ppermute | solution.py:54
  90.3 9.8 %collective-permute-start.25 = (bf16[18,64,128]{2,1,0:T(8,128)(2,1)S(1)}, bf16[18,64,128]{2,1,0:T(8,128)(2,1)S(1)}, u32[]{:S(2)}, u32[]{:S(2)}) collective-permute-start(bf16[18,64,128]{2,1,0:T(8,128)(2,1)S(1)} %fusion.3), channel_id=1, source_target_pairs={{0,32},{16,48},{32,64},{48,80},{64,96},{80,112},{96,0},{112,16},{1... | collective-permute-start | bytes 884744 | tf_op jit(solution)/shard_map/ppermute | solution.py:54
  90.4 9.7 %collective-permute-start.26 = (bf16[18,64,128]{2,1,0:T(8,128)(2,1)S(1)}, bf16[18,64,128]{2,1,0:T(8,128)(2,1)S(1)}, u32[]{:S(2)}, u32[]{:S(2)}) collective-permute-start(bf16[18,64,128]{2,1,0:T(8,128)(2,1)S(1)} %fusion.2), channel_id=1, source_target_pairs={{0,96},{16,112},{32,0},{48,16},{64,32},{80,48},{96,64},{112,80},{1... | collective-permute-start | bytes 884744 | tf_op jit(solution)/shard_map/ppermute | solution.py:54
  94.9 35.8 %collective-permute-start.13 = (bf16[4,9,32,384]{3,2,1,0:T(8,128)(2,1)S(1)}, bf16[4,9,32,384]{3,2,1,0:T(8,128)(2,1)}, u32[]{:S(2)}, u32[]{:S(2)}) collective-permute-start(bf16[4,9,32,384]{3,2,1,0:T(8,128)(2,1)S(1)} %pad_maximum_fusion.refs_10_), channel_id=1, source_target_pairs={{0,12},{1,13},{2,14},{3,15},{4,0},{5,1},{6,2},{7,3},{8,4},{9,5},{1... | collective-permute-start | bytes 2654216 | tf_op jit(solution)/shard_map/ppermute | solution.py:49
  99.2 33.6 %collective-permute-start.14 = (bf16[4,9,32,384]{3,2,1,0:T(8,128)(2,1)S(1)}, bf16[4,9,32,384]{3,2,1,0:T(8,128)(2,1)}, u32[]{:S(2)}, u32[]{:S(2)}) collective-permute-start(bf16[4,9,32,384]{3,2,1,0:T(8,128)(2,1)S(1)} %pad_maximum_fusion.refs_10_), channel_id=1, source_target_pairs={{0,4},{1,5},{2,6},{3,7},{4,8},{5,9},{6,10},{7,11},{8,12},{9,13},{1... | collective-permute-start | bytes 2654216 | tf_op jit(solution)/shard_map/ppermute | solution.py:49
  101.5 25.6 %collective-permute-start.33 = (bf16[27,32,128]{2,1,0:T(8,128)(2,1)}, bf16[27,32,128]{2,1,0:T(8,128)(2,1)S(1)}, u32[]{:S(2)}, u32[]{:S(2)}) collective-permute-start(bf16[27,32,128]{2,1,0:T(8,128)(2,1)} %get-tuple-element.31), channel_id=1, source_target_pairs={{0,12},{1,13},{2,14},{3,15},{4,0},{5,1},{6,2},{7,3},{8,4},{9,5},{1... | collective-permute-start | bytes 663560 | tf_op jit(solution)/shard_map/ppermute | solution.py:49
  105.8 21.3 %collective-permute-start.32 = (bf16[27,32,128]{2,1,0:T(8,128)(2,1)}, bf16[27,32,128]{2,1,0:T(8,128)(2,1)S(1)}, u32[]{:S(2)}, u32[]{:S(2)}) collective-permute-start(bf16[27,32,128]{2,1,0:T(8,128)(2,1)} %get-tuple-element.32), channel_id=1, source_target_pairs={{0,8},{1,9},{2,10},{3,11},{4,12},{5,13},{6,14},{7,15},{8,0},{9,1},... | collective-permute-start | bytes 663560 | tf_op jit(solution)/shard_map/ppermute | solution.py:49
  106.4 24.0 %collective-permute-start.31 = (bf16[27,32,128]{2,1,0:T(8,128)(2,1)S(1)}, bf16[27,32,128]{2,1,0:T(8,128)(2,1)S(1)}, u32[]{:S(2)}, u32[]{:S(2)}) collective-permute-start(bf16[27,32,128]{2,1,0:T(8,128)(2,1)S(1)} %get-tuple-element.30), channel_id=1, source_target_pairs={{0,4},{1,5},{2,6},{3,7},{4,8},{5,9},{6,10},{7,11},{8,12},{9,13},{1... | collective-permute-start | bytes 663560 | tf_op jit(solution)/shard_map/ppermute | solution.py:49
  130.6 7.6 %collective-permute-start.34 = (bf16[27,32,128]{2,1,0:T(8,128)(2,1)S(1)}, bf16[27,32,128]{2,1,0:T(8,128)(2,1)}, u32[]{:S(2)}, u32[]{:S(2)}) collective-permute-start(bf16[27,32,128]{2,1,0:T(8,128)(2,1)S(1)} %fusion.8), channel_id=1, source_target_pairs={{0,16},{16,0},{32,48},{48,32},{64,80},{80,64},{96,112},{112,96},{1... | collective-permute-start | bytes 663560 | tf_op jit(solution)/shard_map/ppermute | solution.py:287
  132.5 10.5 %collective-permute-start.16 = (bf16[2,9,32,384]{3,2,1,0:T(8,128)(2,1)}, bf16[2,9,32,384]{3,2,1,0:T(8,128)(2,1)}, u32[]{:S(2)}, u32[]{:S(2)}) collective-permute-start(bf16[2,9,32,384]{3,2,1,0:T(8,128)(2,1)} %slice.191), channel_id=1, source_target_pairs={{0,12},{1,13},{2,14},{3,15},{4,0},{5,1},{6,2},{7,3},{8,4},{9,5},{1... | collective-permute-start | bytes 1327112 | tf_op jit(solution)/shard_map/ppermute | solution.py:49
  133.9 11.1 %collective-permute-start.15 = (bf16[2,9,32,384]{3,2,1,0:T(8,128)(2,1)S(1)}, bf16[2,9,32,384]{3,2,1,0:T(8,128)(2,1)S(1)}, u32[]{:S(2)}, u32[]{:S(2)}) collective-permute-start(bf16[2,9,32,384]{3,2,1,0:T(8,128)(2,1)S(1)} %slice.190), channel_id=1, source_target_pairs={{0,4},{1,5},{2,6},{3,7},{4,8},{5,9},{6,10},{7,11},{8,12},{9,13},{1... | collective-permute-start | bytes 1327112 | tf_op jit(solution)/shard_map/ppermute | solution.py:49
  140.0 7.1 %collective-permute-start.35 = (f32[27,8,128]{2,1,0:T(8,128)S(1)}, f32[27,8,128]{2,1,0:T(8,128)S(1)}, u32[]{:S(2)}, u32[]{:S(2)}) collective-permute-start(f32[27,8,128]{2,1,0:T(8,128)S(1)} %get-tuple-element.57), channel_id=1, source_target_pairs={{0,1},{1,0},{2,3},{3,2},{4,5},{5,4},{6,7},{7,6},{8,9},{9,8},{10,11... | collective-permute-start | bytes 331784 | tf_op jit(solution)/shard_map/ppermute | solution.py:34
  140.0 7.1 %collective-permute-start.36 = (f32[27,8,128]{2,1,0:T(8,128)S(1)}, f32[27,8,128]{2,1,0:T(8,128)S(1)}, u32[]{:S(2)}, u32[]{:S(2)}) collective-permute-start(f32[27,8,128]{2,1,0:T(8,128)S(1)} %get-tuple-element.56), channel_id=1, source_target_pairs={{0,2},{1,3},{2,0},{3,1},{4,6},{5,7},{6,4},{7,5},{8,10},{9,11},{10,... | collective-permute-start | bytes 331784 | tf_op jit(solution)/shard_map/ppermute | solution.py:34
  140.0 7.4 %collective-permute-start.37 = (f32[27,8,128]{2,1,0:T(8,128)S(1)}, f32[27,8,128]{2,1,0:T(8,128)S(1)}, u32[]{:S(2)}, u32[]{:S(2)}) collective-permute-start(f32[27,8,128]{2,1,0:T(8,128)S(1)} %get-tuple-element.55), channel_id=1, source_target_pairs={{0,3},{1,2},{2,1},{3,0},{4,7},{5,6},{6,5},{7,4},{8,11},{9,10},{10,... | collective-permute-start | bytes 331784 | tf_op jit(solution)/shard_map/ppermute | solution.py:34
  162.6 44.5 %collective-permute-start.38 = (f32[27,8,512]{2,1,0:T(8,128)}, f32[27,8,512]{2,1,0:T(8,128)S(1)}, u32[]{:S(2)}, u32[]{:S(2)}) collective-permute-start(f32[27,8,512]{2,1,0:T(8,128)} %shard_map.55.refs_0_), channel_id=1, source_target_pairs={{0,32},{16,48},{32,64},{48,80},{64,96},{80,112},{96,0},{112,16},{1... | collective-permute-start | bytes 1327112 | tf_op jit(solution)/shard_map/ppermute | solution.py:54
  162.7 44.4 %collective-permute-start.39 = (f32[27,8,512]{2,1,0:T(8,128)}, f32[27,8,512]{2,1,0:T(8,128)S(1)}, u32[]{:S(2)}, u32[]{:S(2)}) collective-permute-start(f32[27,8,512]{2,1,0:T(8,128)} %shard_map.55.refs_0_), channel_id=1, source_target_pairs={{0,64},{16,80},{32,96},{48,112},{64,0},{80,16},{96,32},{112,48},{1... | collective-permute-start | bytes 1327112 | tf_op jit(solution)/shard_map/ppermute | solution.py:54
  164.8 42.4 %collective-permute-start.40 = (f32[27,8,512]{2,1,0:T(8,128)}, f32[27,8,512]{2,1,0:T(8,128)S(1)}, u32[]{:S(2)}, u32[]{:S(2)}) collective-permute-start(f32[27,8,512]{2,1,0:T(8,128)} %shard_map.55.refs_0_), channel_id=1, source_target_pairs={{0,96},{16,112},{32,0},{48,16},{64,32},{80,48},{96,64},{112,80},{1... | collective-permute-start | bytes 1327112 | tf_op jit(solution)/shard_map/ppermute | solution.py:54
  180.9 1.6 collective-permute-start.20
  181.0 6.6 %collective-permute-start.21 = (bf16[4,8,16,128]{3,2,1,0:T(8,128)(2,1)}, bf16[4,8,16,128]{3,2,1,0:T(8,128)(2,1)S(1)}, u32[]{:S(2)}, u32[]{:S(2)}) collective-permute-start(bf16[4,8,16,128]{3,2,1,0:T(8,128)(2,1)} %get-tuple-element.18), channel_id=1, source_target_pairs={{0,2},{1,3},{2,0},{3,1},{4,6},{5,7},{6,4},{7,5},{8,10},{9,11},{10,... | collective-permute-start | bytes 393224 | tf_op jit(solution)/shard_map/ppermute | solution.py:34
  182.5 6.9 %collective-permute-start.22 = (bf16[4,8,16,128]{3,2,1,0:T(8,128)(2,1)}, bf16[4,8,16,128]{3,2,1,0:T(8,128)(2,1)S(1)}, u32[]{:S(2)}, u32[]{:S(2)}) collective-permute-start(bf16[4,8,16,128]{3,2,1,0:T(8,128)(2,1)} %get-tuple-element.19), channel_id=1, source_target_pairs={{0,3},{1,2},{2,1},{3,0},{4,7},{5,6},{6,5},{7,4},{8,11},{9,10},{10,... | collective-permute-start | bytes 393224 | tf_op jit(solution)/shard_map/ppermute | solution.py:34
  (22 other events, 72.8 us)

commit v2 on v0

v2 whole, which is shorter than its diff:
```python
import functools
import math

import jax
import jax.numpy as jnp
from jax import lax
from jax.experimental import pallas as pl
from jax.experimental.pallas import tpu as pltpu
from jax.sharding import PartitionSpec as P

QUAD = 4
RING = 4
F32 = jnp.float32
BF16 = jnp.bfloat16
ANY = pl.BlockSpec(memory_space=pl.ANY)
VMEM = pl.BlockSpec(memory_space=pltpu.VMEM)
LIMIT = 40 * 1024 * 1024


def params():
    return pltpu.CompilerParams(vmem_limit_bytes=LIMIT)


def quad_place():
    return lax.rem(lax.axis_index("gy"), QUAD)


def x_place():
    return lax.div(lax.axis_index("gx"), 2)


def swap(block, k):
    count = lax.axis_size("gy")
    return lax.ppermute(block, "gy", [(g, g ^ k) for g in range(count)])


def along_y(block, step, ring):
    count = lax.axis_size("gy")
    pairs = [(g, g + QUAD * step) for g in range(count)]
    if ring:
        pairs = [(s, t % count) for s, t in pairs]
    return lax.ppermute(block, "gy", [(s, t) for s, t in pairs if 0 <= t < count])


def along_x(block, step):
    count = lax.axis_size("gx")
    return lax.ppermute(block, "gx", [(g, (g + 2 * step) % count) for g in range(count)])


def rims_x(first, last):
    count = lax.axis_size("gx")
    low = lax.ppermute(last, "gx", [(g, g + 1) for g in range(count - 1)])
    high = lax.ppermute(first, "gx", [(g + 1, g) for g in range(count - 1)])
    return low, high


def zero_at(value, z, edge):
    return jnp.where(z == edge, 0.0, value)


def pick_kernel(cot, extra, low, high, *quarters):
    rows, width, depth, chan = cot.shape
    j = quad_place()
    q = chan // QUAD
    part = q // RING
    source = lax.broadcasted_iota(jnp.int32, (chan, q), 0)
    place = lax.broadcasted_iota(jnp.int32, (chan, q), 1)
    base = lax.div(place, part) * q + lax.rem(place, part)

    def take(block, pick):
        shape = block.shape
        flat = block[...].reshape(-1, chan)
        got = jnp.dot(flat, pick, preferred_element_type=F32)
        return got.astype(BF16).reshape(shape[:-1] + (q,))

    for k, out in enumerate(quarters):
        pick = jnp.where(source == base + (j ^ k) * part, 1.0, 0.0).astype(BF16)
        out[0:rows, 1:width + 1] = take(cot, pick)
        out[rows, 1:width + 1] = take(extra, pick)
        out[:, 0] = take(low, pick)
        out[:, width + 1] = take(high, pick)


def pick_channels(cot, extra, low, high):
    rows, width, depth, chan = cot.shape
    quarter = jax.ShapeDtypeStruct((rows + 1, width + 2, depth, chan // QUAD), BF16)
    return pl.pallas_call(
        pick_kernel,
        out_shape=[quarter] * QUAD,
        in_specs=[VMEM] * 4,
        out_specs=[VMEM] * QUAD,
        compiler_params=params(),
    )(cot, extra, low, high)


def turn_kernel(p0, p1, p2, p3, held, out):
    j, x = quad_place(), x_place()
    for k, p in enumerate((p0, p1, p2, p3)):
        rows = p.shape[0] - 1
        held[pl.ds(1 + (j ^ k) * rows, rows)] = p[0:rows]

        @pl.when((j ^ k) == 0)
        def _():
            held[0] = p[rows]

        @pl.when((j ^ k) == QUAD - 1)
        def _():
            held[held.shape[0] - 1] = p[rows]

    tall, width, depth, q = held.shape
    width -= 2
    cells = tall * width * depth
    part = q // RING
    small = part // RING
    place = lax.broadcasted_iota(jnp.int32, (q, q), 0)
    source = lax.broadcasted_iota(jnp.int32, (q, q), 1)
    xpart = lax.rem(lax.div(place, part) + x, RING)
    base = lax.div(lax.rem(place, part), small) * part + xpart * small + lax.rem(place, small)
    order = jnp.where(source == base, 1.0, 0.0).astype(BF16)
    z = lax.rem(lax.broadcasted_iota(jnp.int32, (q, cells), 1), depth)
    for b in (-1, 0, 1):
        moved = held[:, 1 - b:1 - b + width].reshape(cells, q)
        value = lax.dot_general(
            order, moved, (((1,), (1,)), ((), ())), preferred_element_type=F32
        )
        high = zero_at(pltpu.roll(value, cells - 1, 1), z, depth - 1)
        low = zero_at(pltpu.roll(value, 1, 1), z, 0)
        for c, v in enumerate((high, value, low)):
            at = ((b + 1) * 3 + c) * q
            out[at:at + q] = v.astype(BF16)


def turn(quarters):
    rows, width, depth, q = quarters[0].shape
    tall = QUAD * (rows - 1) + 2
    return pl.pallas_call(
        turn_kernel,
        out_shape=[
            jax.ShapeDtypeStruct((tall, width, depth, q), BF16),
            jax.ShapeDtypeStruct((9 * q, tall * (width - 2) * depth), BF16),
        ],
        in_specs=[VMEM] * QUAD,
        out_specs=[VMEM] * 2,
        compiler_params=params(),
    )(*quarters)


def run_copies(pairs, sem):
    copies = [pltpu.make_async_copy(s, d, sem.at[n]) for n, (s, d) in enumerate(pairs)]
    for c in copies:
        c.start()
    return copies


def weight_kernel(offsets, norm, own_act, near, far, across, cot, *refs):
    right, left, keep_right, keep_left, own, held, sem = refs
    j = quad_place()
    rows, width, depth, chan = own_act.shape
    pairs = []
    for k, piece in enumerate((own_act, near, far, across)):
        pairs.append((piece, held.at[pl.ds((j ^ k) * rows, rows)]))
    for c in run_copies(pairs, sem):
        c.wait()
    row = width * depth
    cells = QUAD * rows * row
    act = held[...].reshape(cells, chan)
    q = cot.shape[0] // 9
    part = q // RING
    half = part // 2
    for n in range(3 * len(offsets)):
        a, b = offsets[n // 3], n % 3
        moved = cot[3 * b * q:3 * (b + 1) * q, (1 - a) * row:(1 - a) * row + cells]
        term = jnp.dot(moved, act, preferred_element_type=F32) * norm
        for c in range(3):
            tap = 3 * n + c

            def block(r, h):
                at = c * q + r * part + h * half
                return term[at:at + half]

            right[0, tap] = block(2, 0).astype(BF16)
            left[0, tap] = block(2, 1).astype(BF16)
            keep_right[tap] = block(1, 0)
            right[1, tap] = block(1, 1).astype(BF16)
            left[1, tap] = block(3, 0).astype(BF16)
            keep_left[tap] = block(3, 1)
            own[0, tap] = block(0, 0)
            own[1, tap] = block(0, 1)


def weight_terms(offsets, norm, acts, cot):
    rows, width, depth, chan = acts[0].shape
    taps = 9 * len(offsets)
    q = chan // QUAD
    half = q // RING // 2
    held_cells = QUAD * rows * width * depth
    shapes = [
        jax.ShapeDtypeStruct((2, taps, half, chan), BF16),
        jax.ShapeDtypeStruct((2, taps, half, chan), BF16),
        jax.ShapeDtypeStruct((taps, half, chan), F32),
        jax.ShapeDtypeStruct((taps, half, chan), F32),
        jax.ShapeDtypeStruct((2, taps, half, chan), F32),
    ]
    return pl.pallas_call(
        functools.partial(weight_kernel, offsets, norm),
        out_shape=shapes,
        in_specs=[ANY] * 4 + [VMEM],
        out_specs=[VMEM] * 5,
        scratch_shapes=[
            pltpu.VMEM((QUAD * rows, width, depth, chan), BF16),
            pltpu.SemaphoreType.DMA((4,)),
        ],
        compiler_params=params(),
        cost_estimate=pl.CostEstimate(
            flops=2 * taps * q * held_cells * chan, bytes_accessed=10_000_000, transcendentals=0
        ),
    )(*acts, cot)


def input_kernel(held, own, above, across_low, across_high, below, *refs):
    send, keep, pass_on, weights, sem = refs
    j = quad_place()
    y = lax.div(lax.axis_index("gy"), QUAD)
    part = own.shape[1]
    low = across_low.shape[0]

    def at(s):
        return pl.ds(pl.multiple_of(lax.rem(y + s, RING) * part, part), part)

    pairs = [
        (own, weights.at[:, at(0)]),
        (above, weights.at[:, at(1)]),
        (across_low, weights.at[pl.ds(0, low), at(2)]),
        (across_high, weights.at[pl.ds(low, 27 - low), at(2)]),
        (below, weights.at[:, at(3)]),
    ]
    for c in run_copies(pairs, sem):
        c.wait()
    rows, width, depth, chan = keep.shape
    cells = rows * width * depth
    q = held.shape[3]
    taps = weights[...].reshape(9, 3, q, chan)
    for k, out in ((1, send.at[0]), (3, send.at[1]), (2, pass_on), (0, keep)):
        first = (j ^ k) * rows
        moved = []
        for n in range(9):
            a, b = n // 3 - 1, n % 3 - 1
            block = held[pl.ds(first + 1 - a, rows), 1 - b:1 - b + width]
            moved.append(block.reshape(cells, q))
        moved = jnp.concatenate(moved, axis=1)
        z = lax.rem(lax.broadcasted_iota(jnp.int32, (cells, chan), 0), depth)

        def term(c):
            return jnp.dot(moved, taps[:, c].reshape(9 * q, chan), preferred_element_type=F32)

        grad = term(1)
        grad = grad + zero_at(pltpu.roll(term(0), cells - 1, 0), z, depth - 1)
        grad = grad + zero_at(pltpu.roll(term(2), 1, 0), z, 0)
        out[...] = grad.reshape(rows, width, depth, chan)


def input_terms(held, parts):
    tall, width, depth, q = held.shape
    chan = QUAD * q
    block = ((tall - 2) // QUAD, width - 2, depth, chan)
    return pl.pallas_call(
        input_kernel,
        out_shape=[
            jax.ShapeDtypeStruct((2,) + block, F32),
            jax.ShapeDtypeStruct(block, F32),
            jax.ShapeDtypeStruct(block, F32),
        ],
        in_specs=[VMEM] + [ANY] * 5,
        out_specs=[VMEM] * 3,
        scratch_shapes=[pltpu.VMEM((27, q, chan), BF16), pltpu.SemaphoreType.DMA((5,))],
        compiler_params=params(),
        cost_estimate=pl.CostEstimate(
            flops=2 * 27 * tall * width * depth * q * chan, bytes_accessed=10_000_000, transcendentals=0
        ),
    )(held, *parts)


def finish_kernel(pre, keep, near, far, out):
    value = pre[...].astype(F32)
    s = jax.nn.sigmoid(value)
    grad = keep[...] + near[0] + far[...]
    out[...] = (grad * s * (1.0 + value * (1.0 - s))).astype(BF16)


def finish(pre_act, keep, near, far):
    return pl.pallas_call(
        finish_kernel,
        out_shape=jax.ShapeDtypeStruct(pre_act.shape, BF16),
        in_specs=[VMEM] * 4,
        out_specs=VMEM,
        compiler_params=params(),
    )(pre_act, keep, near, far)


def join_kernel(*refs):
    out = refs[-1]
    x = x_place()
    size = refs[0].shape[1]

    def put(first, piece, k):
        at = pl.ds(pl.multiple_of(lax.rem(x + k, RING) * size, size), size)
        out[first:first + piece.shape[0], at] = piece[...]

    first = 0
    for chunk in (refs[:5], refs[5:10]):
        own, below, above, low, high = chunk
        put(first, own, 0)
        put(first, below, 3)
        put(first, above, 1)
        put(first, low, 2)
        put(first + low.shape[0], high, 2)
        first += own.shape[0]


def join(first, second):
    _, size, chan = first[0].shape
    return pl.pallas_call(
        join_kernel,
        out_shape=jax.ShapeDtypeStruct((27, RING * size, chan), F32),
        in_specs=[VMEM] * 10,
        out_specs=VMEM,
        compiler_params=params(),
    )(*first, *second)


def reduce_x_first(right, left, *kept):
    return along_x(right, 1), along_x(left, -1), *kept


def reduce_x_last(from_left, from_right, keep_right, keep_left, own):
    next_right = (from_left[0].astype(F32) + keep_right).astype(BF16)
    next_left = (from_right[0].astype(F32) + keep_left).astype(BF16)
    last_left = along_x(next_right, 1)
    last_right = along_x(next_left, -1)
    low = own[0] + from_right[1].astype(F32) + last_left.astype(F32)
    high = own[1] + from_left[1].astype(F32) + last_right.astype(F32)
    return jnp.concatenate([low, high], axis=1)


def reduce_rest(total, beside=()):
    y = lax.div(lax.axis_index("gy"), QUAD)
    size = total.shape[1] // RING

    def block(r):
        return lax.dynamic_slice_in_dim(total, lax.rem(y + r, RING) * size, size, axis=1)

    others = [along_y(block(r).astype(BF16), r, True) for r in (1, 2, 3)]
    others, beside = lax.optimization_barrier((others, beside))
    mine = block(0)
    for other in others:
        mine = mine + other.astype(F32)
    count = lax.axis_size("gx")
    other = lax.ppermute(mine.astype(BF16), "gx", [(g, g ^ 1) for g in range(count)])
    whole = mine + other.astype(F32)
    below, above = along_x(whole, 1), along_x(whole, -1)
    taps = whole.shape[0] // 2
    return [whole, below, above, along_x(below[:taps], 1), along_x(above[taps:], -1)], beside


def body(pre_act, cot, weight):
    rows, width, depth, chan = pre_act.shape
    norm = 1.0 / math.sqrt(rows * lax.axis_size("gy") * width * lax.axis_size("gx") * depth)
    j = quad_place()

    count = lax.axis_size("gy")
    pairs = [(g, g + 1) for g in range(QUAD - 1, count - 1, QUAD)]
    pairs = pairs + [(t, s) for s, t in pairs]
    extra = lax.ppermute(jnp.where(j == 0, cot[0], cot[rows - 1]), "gy", pairs)
    act = jax.nn.silu(pre_act.astype(F32)).astype(BF16)
    far = swap(act, 2)
    near = swap(act, 1)
    above = along_y(weight, -1, True)
    below = along_y(weight, 1, True)
    sides = [jnp.concatenate([cot[:, x], extra[x][None]]) for x in (0, width - 1)]
    low, high = rims_x(*sides)
    quarters = pick_channels(cot, extra, low, high)
    quarters, near, far = lax.optimization_barrier((quarters, near, far))
    quarters = [quarters[0]] + [swap(quarters[k], k) for k in (1, 2, 3)]
    acts = [act, near, far, swap(far, 1)]
    held, turned = turn(quarters)

    turned, above, below = lax.optimization_barrier((turned, above, below))
    taps = 13
    parts = [weight, above, along_y(below[:taps], 1, True), along_y(above[taps:], -1, True), below]
    first = weight_terms((-1,), norm, acts, turned)
    turned, first = lax.optimization_barrier((turned, first))
    first = reduce_x_first(*first)
    second = weight_terms((0, 1), norm, acts, turned)
    held, first, second = lax.optimization_barrier((held, first, second))
    second = reduce_x_first(*second)
    grads = input_terms(held, parts)
    second, grads = lax.optimization_barrier((second, grads))
    send, keep, pass_on = grads
    got = swap(send, 1)
    far_grad = swap(pass_on + got[1], 2)
    first, _ = reduce_rest(reduce_x_last(*first))
    second, far_grad = reduce_rest(reduce_x_last(*second), far_grad)
    grad_weight = join(first, second)
    grad_pre = finish(pre_act, keep, got, far_grad)
    return (grad_pre, grad_weight)


def solution(mesh):
    return jax.shard_map(
        body,
        mesh=mesh,
        in_specs=(P("gy", "gx", None, None), P("gy", "gx", None, None), P(None, "gy", None)),
        out_specs=(P("gy", "gx", None, None), P(None, "gy", None)),
        check_vma=False,
    )
```

time: 523 us -> 167 us (0.32); the launches traced: 517 us -> 166 us
  waiting for transfers between devices: 345 us -> 42 us
  local copies, waits for them, and re-layouts: 93.1 us -> 11.3 us
  starting transfers between devices: 7.32 us -> 74.4 us
  matrix products: 28.6 us -> 0 us
  Pallas kernels: 0 us -> 26.4 us
  blocking collectives: 16.7 us -> 0 us
  between operations: 13.8 us -> 1.19 us
    reduce_scatter x1 -> x0, waiting for transfers between devices: 177 us -> none  [body(): lax.psum_scatter(jnp.dot(cols, flat_weight, preferred_element_type=jnp.fl...]
    psum x1 -> x0, waiting for transfers between devices: 102 us -> none  [body(): grad_weight = (lax.psum(summed, 'gx') * norm).reshape(27, owned, chan)]
    ppermute x2 -> x39, starting transfers between devices: 6.98 us -> 74.4 us  [the longest x16 24.9 us: along_x(): lax.ppermute(block, 'gx', [(g, (g + 2 * step) % count) for g in range(cou...]
    all_gather x1 -> x0, waiting for transfers between devices: 57.3 us -> none  [body(): piece = lax.all_gather(act, 'gy', axis=0, tiled=True)]
    concatenate x1 -> x0, local copies, waits for them, and re-layouts: 50.9 us -> none  [columns(): stacked = jnp.concatenate(pieces, axis=3)]
    ppermute x2 -> x39, waiting for transfers between devices: 9.03 us -> 42 us  [the longest x16 14.7 us: along_x(): lax.ppermute(block, 'gx', [(g, (g + 2 * step) % count) for g in range(cou...]
    dot_general x2 -> x0, matrix products: 28.6 us -> none  [the longest x1 15.4 us: body(): jnp.dot(cols, flat_weight, preferred_element_type=jnp.float32)]
    pallas_call x0 -> x7, Pallas kernels: none -> 26.4 us  [the longest x2 10 us: weight_terms(): pl.pallas_call(functools.partial(weight_kernel, offsets, norm), out_shape...]
  transfers between devices with their start and end apart: 5 -> 39, of which waited for: 4 -> 13; matrix products, arithmetic and copies ran while one was open for 0% -> 7% of each run, Pallas kernels for 0% -> 15%
where the time goes in v2:
time: 167 us; the launch traced here: 166 us
  starting transfers between devices  74.4 us (45%)
  waiting for transfers between devices  42 us (25%)
  Pallas kernels  26.4 us (16%)
  local copies, waits for them, and re-layouts  11.3 us (7%)
  other arithmetic  11.3 us (7%)
    ppermute x16, starting transfers between devices, along_x(): lax.ppermute(block, 'gx', [(g, (g + 2 * step) % count) for g in range(cou...  24.9 us
    ppermute x8, starting transfers between devices, swap(): return lax.ppermute(block, 'gy', [(g, g ^ k) for g in range(count)])  20.6 us
    ppermute x10, starting transfers between devices, along_y(): lax.ppermute(block, 'gy', [(s, t) for s, t in pairs if 0 <= t < count])  17.3 us
    ppermute x16, waiting for transfers between devices, along_x(): lax.ppermute(block, 'gx', [(g, (g + 2 * step) % count) for g in range(cou...  14.7 us
    ppermute x8, waiting for transfers between devices, swap(): return lax.ppermute(block, 'gy', [(g, g ^ k) for g in range(count)])  10.2 us
    pallas_call x2, Pallas kernels, weight_terms(): pl.pallas_call(functools.partial(weight_kernel, offsets, norm), out_shape...  10 us
    pallas_call x1, Pallas kernels, input_terms(): pl.pallas_call(input_kernel, out_shape=[jax.ShapeDtypeStruct((2,) + block...  9.76 us
    unnamed x68, local copies, waits for them, and re-layouts  8.99 us
  transfers between devices with their start and end apart: 39, of which 13 were waited for; matrix products, arithmetic and copies ran while one was open for 7% of the time, Pallas kernels for 15%

profile of v2, /device:TPU:0, one launch (start us, length us, event | category | flops | bytes accessed | tf_op | source)
XLA Modules:
  0.0 166.5 jit_solution(8824880195264073601)
XLA Ops:
  0.6 1.4 fusion.3.own_act
  2.2 2.1 %collective-permute-start.4 = (bf16[4,8,16,512]{3,2,1,0:T(8,128)(2,1)S(1)}, bf16[4,8,16,512]{3,2,1,0:T(8,128)(2,1)}, u32[]{:S(2)}, u32[]{:S(2)}) collective-permute-start(bf16[4,8,16,512]{3,2,1,0:T(8,128)(2,1)S(1)} %fusion.3.own_act), channel_id=1, source_target_pairs={{0,2},{1,3},{2,0},{3,1},{4,6},{5,7},{6,4},{7,5},{8,10},{9,11},{10,... | collective-permute-start | bytes 1572872 | tf_op jit(solution)/shard_map/ppermute | solution.py:34
  4.2 3.0 %collective-permute-start.8 = (bf16[27,32,512]{2,1,0:T(8,128)(2,1)}, bf16[27,32,512]{2,1,0:T(8,128)(2,1)S(1)}, u32[]{:S(2)}, u32[]{:S(2)}) collective-permute-start(bf16[27,32,512]{2,1,0:T(8,128)(2,1)} %own.1), channel_id=1, source_target_pairs={{0,12},{1,13},{2,14},{3,15},{4,0},{5,1},{6,2},{7,3},{8,4},{9,5},{1... | collective-permute-start | bytes 2654216 | tf_op jit(solution)/shard_map/ppermute | solution.py:42
  9.9 5.5 %collective-permute-start.1 = (bf16[5,16,512]{2,1,0:T(8,128)(2,1)S(1)}, bf16[5,16,512]{2,1,0:T(8,128)(2,1)S(1)}, u32[]{:S(2)}, u32[]{:S(2)}) collective-permute-start(bf16[5,16,512]{2,1,0:T(8,128)(2,1)S(1)} %pad_maximum_fusion), channel_id=1, source_target_pairs={{0,16},{16,32},{32,48},{48,64},{64,80},{80,96},{96,112},{1,17},{17... | collective-permute-start | bytes 245768 | tf_op jit(solution)/shard_map/ppermute | solution.py:52
  15.4 2.4 %collective-permute-done.1.low = bf16[5,16,512]{2,1,0:T(8,128)(2,1)S(1)} collective-permute-done((bf16[5,16,512]{2,1,0:T(8,128)(2,1)S(1)}, bf16[5,16,512]{2,1,0:T(8,128)(2,1)S(1)}, u32[]{:S(2)}, u32[]{:S(2)}) %collective-permute-start.1) | collective-permute-done | bytes 81952 | tf_op jit(solution)/shard_map/ppermute | solution.py:52
  17.8 1.3 collective-permute-start.2
  19.1 7.0 %collective-permute-done.2.high = bf16[5,16,512]{2,1,0:T(8,128)(2,1)S(1)} collective-permute-done((bf16[5,16,512]{2,1,0:T(8,128)(2,1)S(1)}, bf16[5,16,512]{2,1,0:T(8,128)(2,1)S(1)}, u32[]{:S(2)}, u32[]{:S(2)}) %collective-permute-start.2) | collective-permute-done | bytes 81952 | tf_op jit(solution)/shard_map/ppermute | solution.py:53
  27.7 15.9 %collective-permute-start.6 = (bf16[5,10,16,128]{3,2,1,0:T(8,128)(2,1)S(1)}, bf16[5,10,16,128]{3,2,1,0:T(8,128)(2,1)S(1)}, u32[]{:S(2)}, u32[]{:S(2)}) collective-permute-start(bf16[5,10,16,128]{3,2,1,0:T(8,128)(2,1)S(1)} %get-tuple-element.68), channel_id=1, source_target_pairs={{0,2},{1,3},{2,0},{3,1},{4,6},{5,7},{6,4},{7,5},{8,10},{9,11},{10,... | collective-permute-start | bytes 614408 | tf_op jit(solution)/shard_map/ppermute | solution.py:34
  43.6 1.7 %collective-permute-start.7 = (bf16[5,10,16,128]{3,2,1,0:T(8,128)(2,1)S(1)}, bf16[5,10,16,128]{3,2,1,0:T(8,128)(2,1)S(1)}, u32[]{:S(2)}, u32[]{:S(2)}) collective-permute-start(bf16[5,10,16,128]{3,2,1,0:T(8,128)(2,1)S(1)} %get-tuple-element.69), channel_id=1, source_target_pairs={{0,3},{1,2},{2,1},{3,0},{4,7},{5,6},{6,5},{7,4},{8,11},{9,10},{10,... | collective-permute-start | bytes 614408 | tf_op jit(solution)/shard_map/ppermute | solution.py:34
  45.3 4.2 %collective-permute-done.6.p2 = bf16[5,10,16,128]{3,2,1,0:T(8,128)(2,1)S(1)} collective-permute-done((bf16[5,10,16,128]{3,2,1,0:T(8,128)(2,1)S(1)}, bf16[5,10,16,128]{3,2,1,0:T(8,128)(2,1)S(1)}, u32[]{:S(2)}, u32[]{:S(2)}) %collective-permute-start.6) | collective-permute-done | bytes 204832 | tf_op jit(solution)/shard_map/ppermute | solution.py:34
  49.5 3.8 %collective-permute-done.7.p3 = bf16[5,10,16,128]{3,2,1,0:T(8,128)(2,1)S(1)} collective-permute-done((bf16[5,10,16,128]{3,2,1,0:T(8,128)(2,1)S(1)}, bf16[5,10,16,128]{3,2,1,0:T(8,128)(2,1)S(1)}, u32[]{:S(2)}, u32[]{:S(2)}) %collective-permute-start.7) | collective-permute-done | bytes 204832 | tf_op jit(solution)/shard_map/ppermute | solution.py:34
  53.4 1.8 %shard_map.51 = (bf16[18,10,16,128]{3,2,1,0:T(8,128)(2,1)S(1)}, bf16[1152,2304]{1,0:T(8,128)(2,1)S(1)}) custom-call(bf16[5,10,16,128]{3,2,1,0:T(8,128)(2,1)S(1)} %get-tuple-element.66.p0, bf16[5,10,16,128]{3,2,1,0:T(8,128)(2,1)S(1)} %collective-permute-done.5.p1, bf16[5,10,16,128]{3,2,1,0:T(8,128)(2,1)S(1)} %collective-permute-done.6.p2, ...), custom_call_target="tpu_custom_call" | custom-call | tf_op jit(solution)/shard_map/pallas_call | solution.py:136
  55.2 1.4 slice.81
  56.6 5.1 %collective-permute-start.15 = (bf16[13,32,512]{2,1,0:T(8,128)(2,1)S(1)}, bf16[13,32,512]{2,1,0:T(8,128)(2,1)S(1)}, u32[]{:S(2)}, u32[]{:S(2)}) collective-permute-start(bf16[13,32,512]{2,1,0:T(8,128)(2,1)S(1)} %slice.81), channel_id=1, source_target_pairs={{0,4},{1,5},{2,6},{3,7},{4,8},{5,9},{6,10},{7,11},{8,12},{9,13},{1... | collective-permute-start | bytes 1277960 | tf_op jit(solution)/shard_map/ppermute | solution.py:42
  62.3 3.7 %shard_map.52 = (bf16[2,9,16,512]{3,2,1,0:T(8,128)(2,1)S(1)}, bf16[2,9,16,512]{3,2,1,0:T(8,128)(2,1)S(1)}, f32[9,16,512]{2,1,0:T(8,128)S(1)}, f32[9,16,512]{2,1,0:T(8,128)S(1)}, f32[2,9,16,512]{3,2,1,0:T(8,128)S(1)}) custom-call(bf16[4,8,16,512]{3,2,1,0:T(8,128)(2,1)S(1)} %fusion.3.own_act, bf16[4,8,16,512]{3,2,1,0:T(8,128)(2,1)S(1)} %collective-permute-done.3.near, ...), custom_call_target="tpu_custom_call" | custom-call | flops 2415919104 | bytes 10000000 | tf_op jit(solution)/shard_map/pallas_call | solution.py:204
  68.3 2.8 %collective-permute-start.11 = (bf16[2,9,16,512]{3,2,1,0:T(8,128)(2,1)S(1)}, bf16[2,9,16,512]{3,2,1,0:T(8,128)(2,1)S(1)}, u32[]{:S(2)}, u32[]{:S(2)}) collective-permute-start(bf16[2,9,16,512]{3,2,1,0:T(8,128)(2,1)S(1)} %get-tuple-element.80), channel_id=1, source_target_pairs={{0,32},{16,48},{32,64},{48,80},{64,96},{80,112},{96,0},{112,16},{1... | collective-permute-start | bytes 884744 | tf_op jit(solution)/shard_map/ppermute | solution.py:47
  71.8 1.0 copy-done.12
  72.8 1.0 copy-done.19
  73.9 6.3 %shard_map.53 = (bf16[2,18,16,512]{3,2,1,0:T(8,128)(2,1)S(1)}, bf16[2,18,16,512]{3,2,1,0:T(8,128)(2,1)S(1)}, f32[18,16,512]{2,1,0:T(8,128)S(1)}, f32[18,16,512]{2,1,0:T(8,128)S(1)}, f32[2,18,16,512]{3,2,1,0:T(8,128)S(1)}) custom-call(bf16[4,8,16,512]{3,2,1,0:T(8,128)(2,1)S(1)} %copy-done.12, bf16[4,8,16,512]{3,2,1,0:T(8,128)(2,1)S(1)} %copy-done.19, ...), custom_call_target="tpu_custom_call" | custom-call | flops 4831838208 | bytes 10000000 | tf_op jit(solution)/shard_map/pallas_call | solution.py:204
  81.0 1.6 collective-permute-start.13
  82.7 1.9 %collective-permute-start.14 = (bf16[2,18,16,512]{3,2,1,0:T(8,128)(2,1)S(1)}, bf16[2,18,16,512]{3,2,1,0:T(8,128)(2,1)S(1)}, u32[]{:S(2)}, u32[]{:S(2)}) collective-permute-start(bf16[2,18,16,512]{3,2,1,0:T(8,128)(2,1)S(1)} %get-tuple-element.92), channel_id=1, source_target_pairs={{0,96},{16,112},{32,0},{48,16},{64,32},{80,48},{96,64},{112,80},{1... | collective-permute-start | bytes 1769480 | tf_op jit(solution)/shard_map/ppermute | solution.py:47
  84.5 9.8 %shard_map.54 = (f32[2,4,8,16,512]{4,3,2,1,0:T(8,128)}, f32[4,8,16,512]{3,2,1,0:T(8,128)S(1)}, f32[4,8,16,512]{3,2,1,0:T(8,128)S(1)}) custom-call(bf16[18,10,16,128]{3,2,1,0:T(8,128)(2,1)S(1)} %get-tuple-element.96.held, bf16[27,32,512]{2,1,0:T(8,128)(2,1)S(1)} %copy-done.17, bf16[27,32,512]{2,1,0:T(8,128)(2,1)S(1)} %copy-done.16, ...), custom_call_target="tpu_custom_call" | custom-call | flops 10192158720 | bytes 10000000 | tf_op jit(solution)/shard_map/pallas_call | solution.py:266
  96.3 1.6 collective-permute-done.13
  98.9 1.1 fusion.17
  100.0 2.8 %collective-permute-start.25 = (bf16[9,16,512]{2,1,0:T(8,128)(2,1)S(1)}, bf16[9,16,512]{2,1,0:T(8,128)(2,1)S(1)}, u32[]{:S(2)}, u32[]{:S(2)}) collective-permute-start(bf16[9,16,512]{2,1,0:T(8,128)(2,1)S(1)} %fusion.17), channel_id=1, source_target_pairs={{0,96},{16,112},{32,0},{48,16},{64,32},{80,48},{96,64},{112,80},{1... | collective-permute-start | bytes 442376 | tf_op jit(solution)/shard_map/ppermute | solution.py:47
  104.0 1.2 fusion.5
  105.3 3.3 %collective-permute-start.19 = (bf16[18,16,512]{2,1,0:T(8,128)(2,1)S(1)}, bf16[18,16,512]{2,1,0:T(8,128)(2,1)S(1)}, u32[]{:S(2)}, u32[]{:S(2)}) collective-permute-start(bf16[18,16,512]{2,1,0:T(8,128)(2,1)S(1)} %fusion.5), channel_id=1, source_target_pairs={{0,96},{16,112},{32,0},{48,16},{64,32},{80,48},{96,64},{112,80},{1... | collective-permute-start | bytes 884744 | tf_op jit(solution)/shard_map/ppermute | solution.py:47
  108.5 1.2 fusion.4
  112.1 1.3 collective-permute-start.26
  113.4 1.9 %collective-permute-start.27 = (bf16[9,8,512]{2,1,0:T(8,128)(2,1)S(1)}, bf16[9,8,512]{2,1,0:T(8,128)(2,1)}, u32[]{:S(2)}, u32[]{:S(2)}) collective-permute-start(bf16[9,8,512]{2,1,0:T(8,128)(2,1)S(1)} %get-tuple-element.133), channel_id=1, source_target_pairs={{0,8},{1,9},{2,10},{3,11},{4,12},{5,13},{6,14},{7,15},{8,0},{9,1},... | collective-permute-start | bytes 221192 | tf_op jit(solution)/shard_map/ppermute | solution.py:42
  115.3 4.4 %collective-permute-done.18 = bf16[18,16,512]{2,1,0:T(8,128)(2,1)S(1)} collective-permute-done((bf16[18,16,512]{2,1,0:T(8,128)(2,1)S(1)}, bf16[18,16,512]{2,1,0:T(8,128)(2,1)S(1)}, u32[]{:S(2)}, u32[]{:S(2)}) %collective-permute-start.18) | collective-permute-done | bytes 294944 | tf_op jit(solution)/shard_map/ppermute | solution.py:47
  121.7 1.3 collective-permute-start.20
  123.0 1.9 %collective-permute-start.21 = (bf16[18,8,512]{2,1,0:T(8,128)(2,1)S(1)}, bf16[18,8,512]{2,1,0:T(8,128)(2,1)S(1)}, u32[]{:S(2)}, u32[]{:S(2)}) collective-permute-start(bf16[18,8,512]{2,1,0:T(8,128)(2,1)S(1)} %get-tuple-element.128), channel_id=1, source_target_pairs={{0,8},{1,9},{2,10},{3,11},{4,12},{5,13},{6,14},{7,15},{8,0},{9,1},... | collective-permute-start | bytes 442376 | tf_op jit(solution)/shard_map/ppermute | solution.py:42
  124.9 1.1 collective-permute-start.22
  126.0 1.1 collective-permute-start.28
  127.1 5.5 %collective-permute-done.28 = bf16[9,8,512]{2,1,0:T(8,128)(2,1)} collective-permute-done((bf16[9,8,512]{2,1,0:T(8,128)(2,1)}, bf16[9,8,512]{2,1,0:T(8,128)(2,1)}, u32[]{:S(2)}, u32[]{:S(2)}) %collective-permute-start.28) | collective-permute-done | bytes 73760 | tf_op jit(solution)/shard_map/ppermute | solution.py:42
  132.6 2.2 %collective-permute-done.23.far = f32[4,8,16,512]{3,2,1,0:T(8,128)} collective-permute-done((f32[4,8,16,512]{3,2,1,0:T(8,128)}, f32[4,8,16,512]{3,2,1,0:T(8,128)}, u32[]{:S(2)}, u32[]{:S(2)}) %collective-permute-start.23) | collective-permute-done | bytes 1048608 | tf_op jit(solution)/shard_map/ppermute | solution.py:34
  134.8 1.1 fusion.29
  135.9 4.0 %collective-permute-start.34 = (bf16[18,8,512]{2,1,0:T(8,128)(2,1)S(1)}, bf16[18,8,512]{2,1,0:T(8,128)(2,1)S(1)}, u32[]{:S(2)}, u32[]{:S(2)}) collective-permute-start(bf16[18,8,512]{2,1,0:T(8,128)(2,1)S(1)} %get-tuple-element.122), channel_id=1, source_target_pairs={{0,16},{16,0},{32,48},{48,32},{64,80},{80,64},{96,112},{112,96},{1... | collective-permute-start | bytes 442376 | tf_op jit(solution)/shard_map/ppermute | solution.py:358
  141.0 1.9 %collective-permute-done.34 = bf16[18,8,512]{2,1,0:T(8,128)(2,1)S(1)} collective-permute-done((bf16[18,8,512]{2,1,0:T(8,128)(2,1)S(1)}, bf16[18,8,512]{2,1,0:T(8,128)(2,1)S(1)}, u32[]{:S(2)}, u32[]{:S(2)}) %collective-permute-start.34) | collective-permute-done | bytes 147488 | tf_op jit(solution)/shard_map/ppermute | solution.py:358
  143.3 3.2 %collective-permute-start.36 = (f32[18,8,512]{2,1,0:T(8,128)S(1)}, f32[18,8,512]{2,1,0:T(8,128)S(1)}, u32[]{:S(2)}, u32[]{:S(2)}) collective-permute-start(f32[18,8,512]{2,1,0:T(8,128)S(1)} %convert_add_fusion.4.refs_5_), channel_id=1, source_target_pairs={{0,96},{16,112},{32,0},{48,16},{64,32},{80,48},{96,64},{112,80},{1... | collective-permute-start | bytes 884744 | tf_op jit(solution)/shard_map/ppermute | solution.py:47
  147.2 1.7 %collective-permute-start.30 = (f32[9,8,512]{2,1,0:T(8,128)S(1)}, f32[9,8,512]{2,1,0:T(8,128)S(1)}, u32[]{:S(2)}, u32[]{:S(2)}) collective-permute-start(f32[9,8,512]{2,1,0:T(8,128)S(1)} %convert_add_fusion.5.refs_0_), channel_id=1, source_target_pairs={{0,32},{16,48},{32,64},{48,80},{64,96},{80,112},{96,0},{112,16},{1... | collective-permute-start | bytes 442376 | tf_op jit(solution)/shard_map/ppermute | solution.py:47
  148.9 4.7 %collective-permute-done.35.refs_6_ = f32[18,8,512]{2,1,0:T(8,128)S(1)} collective-permute-done((f32[18,8,512]{2,1,0:T(8,128)S(1)}, f32[18,8,512]{2,1,0:T(8,128)S(1)}, u32[]{:S(2)}, u32[]{:S(2)}) %collective-permute-start.35) | collective-permute-done | bytes 294944 | tf_op jit(solution)/shard_map/ppermute | solution.py:47
  153.7 3.3 %collective-permute-start.38 = (f32[9,8,512]{2,1,0:T(8,128)S(1)}, f32[9,8,512]{2,1,0:T(8,128)S(1)}, u32[]{:S(2)}, u32[]{:S(2)}) collective-permute-start(f32[9,8,512]{2,1,0:T(8,128)S(1)} %slice.106), channel_id=1, source_target_pairs={{0,96},{16,112},{32,0},{48,16},{64,32},{80,48},{96,64},{112,80},{1... | collective-permute-start | bytes 442376 | tf_op jit(solution)/shard_map/ppermute | solution.py:47
  157.0 2.6 %collective-permute-start.33 = (f32[5,8,512]{2,1,0:T(8,128)S(1)}, f32[5,8,512]{2,1,0:T(8,128)S(1)}, u32[]{:S(2)}, u32[]{:S(2)}) collective-permute-start(f32[5,8,512]{2,1,0:T(8,128)S(1)} %slice.104), channel_id=1, source_target_pairs={{0,96},{16,112},{32,0},{48,16},{64,32},{80,48},{96,64},{112,80},{1... | collective-permute-start | bytes 245768 | tf_op jit(solution)/shard_map/ppermute | solution.py:47
  159.7 2.4 %shard_map.55 = bf16[4,8,16,512]{3,2,1,0:T(8,128)(2,1)} custom-call(bf16[4,8,16,512]{3,2,1,0:T(8,128)(2,1)S(1)} %copy-done, f32[4,8,16,512]{3,2,1,0:T(8,128)S(1)} %copy-done.3, f32[2,4,8,16,512]{4,3,2,1,0:T(8,128)S(1)} %collective-permute-done.17.near, f32[4,8,16,512]{3,2,1,0:T(8,128)} %collective-permute-done.23.far), custom_call_target="tpu_custom_call" | custom-call | tf_op jit(solution)/shard_map/pallas_call | solution.py:291
  162.1 3.1 %collective-permute-done.32.refs_3_ = f32[4,8,512]{2,1,0:T(8,128)S(1)} collective-permute-done((f32[4,8,512]{2,1,0:T(8,128)S(1)}, f32[4,8,512]{2,1,0:T(8,128)S(1)}, u32[]{:S(2)}, u32[]{:S(2)}) %collective-permute-start.32) | collective-permute-done | bytes 65568 | tf_op jit(solution)/shard_map/ppermute | solution.py:47
  165.2 1.3 shard_map.56
  (130 shorter events, 19.4 us)
Async XLA Ops:
  0.6 25.4 %copy-start.1 = (bf16[4,8,16,512]{3,2,1,0:T(8,128)(2,1)S(1)}, bf16[4,8,16,512]{3,2,1,0:T(8,128)(2,1)}, u32[]{:S(2)}) copy-start(bf16[4,8,16,512]{3,2,1,0:T(8,128)(2,1)} %cot.1) | copy-start | bytes 1572868
  2.1 60.2 %copy-start.11 = (bf16[4,8,16,512]{3,2,1,0:T(8,128)(2,1)}, bf16[4,8,16,512]{3,2,1,0:T(8,128)(2,1)S(1)}, u32[]{:S(2)}) copy-start(bf16[4,8,16,512]{3,2,1,0:T(8,128)(2,1)S(1)} %fusion.3.own_act) | copy-start | bytes 1572868
  2.1 25.0 %collective-permute-start.3 = (bf16[4,8,16,512]{3,2,1,0:T(8,128)(2,1)S(1)}, bf16[4,8,16,512]{3,2,1,0:T(8,128)(2,1)S(1)}, u32[]{:S(2)}, u32[]{:S(2)}) collective-permute-start(bf16[4,8,16,512]{3,2,1,0:T(8,128)(2,1)S(1)} %fusion.3.own_act), channel_id=1, source_target_pairs={{0,1},{1,0},{2,3},{3,2},{4,5},{5,4},{6,7},{7,6},{8,9},{9,8},{10,11... | collective-permute-start | bytes 1572872 | tf_op jit(solution)/shard_map/ppermute | solution.py:34
  2.2 25.0 %collective-permute-start.4 = (bf16[4,8,16,512]{3,2,1,0:T(8,128)(2,1)S(1)}, bf16[4,8,16,512]{3,2,1,0:T(8,128)(2,1)}, u32[]{:S(2)}, u32[]{:S(2)}) collective-permute-start(bf16[4,8,16,512]{3,2,1,0:T(8,128)(2,1)S(1)} %fusion.3.own_act), channel_id=1, source_target_pairs={{0,2},{1,3},{2,0},{3,1},{4,6},{5,7},{6,4},{7,5},{8,10},{9,11},{10,... | collective-permute-start | bytes 1572872 | tf_op jit(solution)/shard_map/ppermute | solution.py:34
  4.2 51.0 %collective-permute-start.8 = (bf16[27,32,512]{2,1,0:T(8,128)(2,1)}, bf16[27,32,512]{2,1,0:T(8,128)(2,1)S(1)}, u32[]{:S(2)}, u32[]{:S(2)}) collective-permute-start(bf16[27,32,512]{2,1,0:T(8,128)(2,1)} %own.1), channel_id=1, source_target_pairs={{0,12},{1,13},{2,14},{3,15},{4,0},{5,1},{6,2},{7,3},{8,4},{9,5},{1... | collective-permute-start | bytes 2654216 | tf_op jit(solution)/shard_map/ppermute | solution.py:42
  7.3 48.0 %collective-permute-start.9 = (bf16[27,32,512]{2,1,0:T(8,128)(2,1)}, bf16[27,32,512]{2,1,0:T(8,128)(2,1)}, u32[]{:S(2)}, u32[]{:S(2)}) collective-permute-start(bf16[27,32,512]{2,1,0:T(8,128)(2,1)} %own.1), channel_id=1, source_target_pairs={{0,4},{1,5},{2,6},{3,7},{4,8},{5,9},{6,10},{7,11},{8,12},{9,13},{1... | collective-permute-start | bytes 2654216 | tf_op jit(solution)/shard_map/ppermute | solution.py:42
  8.2 1.6 collective-permute-start
  9.9 7.9 %collective-permute-start.1 = (bf16[5,16,512]{2,1,0:T(8,128)(2,1)S(1)}, bf16[5,16,512]{2,1,0:T(8,128)(2,1)S(1)}, u32[]{:S(2)}, u32[]{:S(2)}) collective-permute-start(bf16[5,16,512]{2,1,0:T(8,128)(2,1)S(1)} %pad_maximum_fusion), channel_id=1, source_target_pairs={{0,16},{16,32},{32,48},{48,64},{64,80},{80,96},{96,112},{1,17},{17... | collective-permute-start | bytes 245768 | tf_op jit(solution)/shard_map/ppermute | solution.py:52
  17.8 8.3 %collective-permute-start.2 = (bf16[5,16,512]{2,1,0:T(8,128)(2,1)S(1)}, bf16[5,16,512]{2,1,0:T(8,128)(2,1)S(1)}, u32[]{:S(2)}, u32[]{:S(2)}) collective-permute-start(bf16[5,16,512]{2,1,0:T(8,128)(2,1)S(1)} %pad_maximum_fusion.1), channel_id=1, source_target_pairs={{16,0},{32,16},{48,32},{64,48},{80,64},{96,80},{112,96},{17,1},{33... | collective-permute-start | bytes 245768 | tf_op jit(solution)/shard_map/ppermute | solution.py:53
  27.1 38.9 %copy-start.18 = (bf16[4,8,16,512]{3,2,1,0:T(8,128)(2,1)}, bf16[4,8,16,512]{3,2,1,0:T(8,128)(2,1)S(1)}, u32[]{:S(2)}) copy-start(bf16[4,8,16,512]{3,2,1,0:T(8,128)(2,1)S(1)} %collective-permute-done.3.near) | copy-start | bytes 1572868
  27.1 35.2 %collective-permute-start.10 = (bf16[4,8,16,512]{3,2,1,0:T(8,128)(2,1)}, bf16[4,8,16,512]{3,2,1,0:T(8,128)(2,1)S(1)}, u32[]{:S(2)}, u32[]{:S(2)}) collective-permute-start(bf16[4,8,16,512]{3,2,1,0:T(8,128)(2,1)} %collective-permute-done.4.far), channel_id=1, source_target_pairs={{0,1},{1,0},{2,3},{3,2},{4,5},{5,4},{6,7},{7,6},{8,9},{9,8},{10,11... | collective-permute-start | bytes 1572872 | tf_op jit(solution)/shard_map/ppermute | solution.py:34
  27.2 16.4 %collective-permute-start.5 = (bf16[5,10,16,128]{3,2,1,0:T(8,128)(2,1)S(1)}, bf16[5,10,16,128]{3,2,1,0:T(8,128)(2,1)S(1)}, u32[]{:S(2)}, u32[]{:S(2)}) collective-permute-start(bf16[5,10,16,128]{3,2,1,0:T(8,128)(2,1)S(1)} %get-tuple-element.67), channel_id=1, source_target_pairs={{0,1},{1,0},{2,3},{3,2},{4,5},{5,4},{6,7},{7,6},{8,9},{9,8},{10,11... | collective-permute-start | bytes 614408 | tf_op jit(solution)/shard_map/ppermute | solution.py:34
  27.7 21.8 %collective-permute-start.6 = (bf16[5,10,16,128]{3,2,1,0:T(8,128)(2,1)S(1)}, bf16[5,10,16,128]{3,2,1,0:T(8,128)(2,1)S(1)}, u32[]{:S(2)}, u32[]{:S(2)}) collective-permute-start(bf16[5,10,16,128]{3,2,1,0:T(8,128)(2,1)S(1)} %get-tuple-element.68), channel_id=1, source_target_pairs={{0,2},{1,3},{2,0},{3,1},{4,6},{5,7},{6,4},{7,5},{8,10},{9,11},{10,... | collective-permute-start | bytes 614408 | tf_op jit(solution)/shard_map/ppermute | solution.py:34
  43.6 9.8 %collective-permute-start.7 = (bf16[5,10,16,128]{3,2,1,0:T(8,128)(2,1)S(1)}, bf16[5,10,16,128]{3,2,1,0:T(8,128)(2,1)S(1)}, u32[]{:S(2)}, u32[]{:S(2)}) collective-permute-start(bf16[5,10,16,128]{3,2,1,0:T(8,128)(2,1)S(1)} %get-tuple-element.69), channel_id=1, source_target_pairs={{0,3},{1,2},{2,1},{3,0},{4,7},{5,6},{6,5},{7,4},{8,11},{9,10},{10,... | collective-permute-start | bytes 614408 | tf_op jit(solution)/shard_map/ppermute | solution.py:34
  56.6 27.9 %collective-permute-start.15 = (bf16[13,32,512]{2,1,0:T(8,128)(2,1)S(1)}, bf16[13,32,512]{2,1,0:T(8,128)(2,1)S(1)}, u32[]{:S(2)}, u32[]{:S(2)}) collective-permute-start(bf16[13,32,512]{2,1,0:T(8,128)(2,1)S(1)} %slice.81), channel_id=1, source_target_pairs={{0,4},{1,5},{2,6},{3,7},{4,8},{5,9},{6,10},{7,11},{8,12},{9,13},{1... | collective-permute-start | bytes 1277960 | tf_op jit(solution)/shard_map/ppermute | solution.py:42
  61.8 22.7 %collective-permute-start.16 = (bf16[14,32,512]{2,1,0:T(8,128)(2,1)S(1)}, bf16[14,32,512]{2,1,0:T(8,128)(2,1)S(1)}, u32[]{:S(2)}, u32[]{:S(2)}) collective-permute-start(bf16[14,32,512]{2,1,0:T(8,128)(2,1)S(1)} %slice.82), channel_id=1, source_target_pairs={{0,12},{1,13},{2,14},{3,15},{4,0},{5,1},{6,2},{7,3},{8,4},{9,5},{1... | collective-permute-start | bytes 1376264 | tf_op jit(solution)/shard_map/ppermute | solution.py:42
  68.3 12.7 %collective-permute-start.11 = (bf16[2,9,16,512]{3,2,1,0:T(8,128)(2,1)S(1)}, bf16[2,9,16,512]{3,2,1,0:T(8,128)(2,1)S(1)}, u32[]{:S(2)}, u32[]{:S(2)}) collective-permute-start(bf16[2,9,16,512]{3,2,1,0:T(8,128)(2,1)S(1)} %get-tuple-element.80), channel_id=1, source_target_pairs={{0,32},{16,48},{32,64},{48,80},{64,96},{80,112},{96,0},{112,16},{1... | collective-permute-start | bytes 884744 | tf_op jit(solution)/shard_map/ppermute | solution.py:47
  71.1 9.9 %collective-permute-start.12 = (bf16[2,9,16,512]{3,2,1,0:T(8,128)(2,1)S(1)}, bf16[2,9,16,512]{3,2,1,0:T(8,128)(2,1)S(1)}, u32[]{:S(2)}, u32[]{:S(2)}) collective-permute-start(bf16[2,9,16,512]{3,2,1,0:T(8,128)(2,1)S(1)} %get-tuple-element.81), channel_id=1, source_target_pairs={{0,96},{16,112},{32,0},{48,16},{64,32},{80,48},{96,64},{112,80},{1... | collective-permute-start | bytes 884744 | tf_op jit(solution)/shard_map/ppermute | solution.py:47
  81.0 13.3 %copy-start.30 = (bf16[2,9,16,512]{3,2,1,0:T(8,128)(2,1)}, bf16[2,9,16,512]{3,2,1,0:T(8,128)(2,1)S(1)}, u32[]{:S(2)}) copy-start(bf16[2,9,16,512]{3,2,1,0:T(8,128)(2,1)S(1)} %collective-permute-done.11) | copy-start | bytes 884740
  81.0 13.3 %copy-start.32 = (bf16[2,9,16,512]{3,2,1,0:T(8,128)(2,1)}, bf16[2,9,16,512]{3,2,1,0:T(8,128)(2,1)S(1)}, u32[]{:S(2)}) copy-start(bf16[2,9,16,512]{3,2,1,0:T(8,128)(2,1)S(1)} %collective-permute-done.12) | copy-start | bytes 884740
  81.0 16.8 %collective-permute-start.13 = (bf16[2,18,16,512]{3,2,1,0:T(8,128)(2,1)S(1)}, bf16[2,18,16,512]{3,2,1,0:T(8,128)(2,1)S(1)}, u32[]{:S(2)}, u32[]{:S(2)}) collective-permute-start(bf16[2,18,16,512]{3,2,1,0:T(8,128)(2,1)S(1)} %get-tuple-element.91), channel_id=1, source_target_pairs={{0,32},{16,48},{32,64},{48,80},{64,96},{80,112},{96,0},{112,16},{1... | collective-permute-start | bytes 1769480 | tf_op jit(solution)/shard_map/ppermute | solution.py:47
  82.7 15.2 %collective-permute-start.14 = (bf16[2,18,16,512]{3,2,1,0:T(8,128)(2,1)S(1)}, bf16[2,18,16,512]{3,2,1,0:T(8,128)(2,1)S(1)}, u32[]{:S(2)}, u32[]{:S(2)}) collective-permute-start(bf16[2,18,16,512]{3,2,1,0:T(8,128)(2,1)S(1)} %get-tuple-element.92), channel_id=1, source_target_pairs={{0,96},{16,112},{32,0},{48,16},{64,32},{80,48},{96,64},{112,80},{1... | collective-permute-start | bytes 1769480 | tf_op jit(solution)/shard_map/ppermute | solution.py:47
  98.9 9.7 %collective-permute-start.17 = (f32[2,4,8,16,512]{4,3,2,1,0:T(8,128)}, f32[2,4,8,16,512]{4,3,2,1,0:T(8,128)S(1)}, u32[]{:S(2)}, u32[]{:S(2)}) collective-permute-start(f32[2,4,8,16,512]{4,3,2,1,0:T(8,128)} %get-tuple-element.103), channel_id=1, source_target_pairs={{0,1},{1,0},{2,3},{3,2},{4,5},{5,4},{6,7},{7,6},{8,9},{9,8},{10,11... | collective-permute-start | bytes 6291464 | tf_op jit(solution)/shard_map/ppermute | solution.py:34
  100.0 10.2 %collective-permute-start.25 = (bf16[9,16,512]{2,1,0:T(8,128)(2,1)S(1)}, bf16[9,16,512]{2,1,0:T(8,128)(2,1)S(1)}, u32[]{:S(2)}, u32[]{:S(2)}) collective-permute-start(bf16[9,16,512]{2,1,0:T(8,128)(2,1)S(1)} %fusion.17), channel_id=1, source_target_pairs={{0,96},{16,112},{32,0},{48,16},{64,32},{80,48},{96,64},{112,80},{1... | collective-permute-start | bytes 442376 | tf_op jit(solution)/shard_map/ppermute | solution.py:47
  103.9 7.3 %collective-permute-start.24 = (bf16[9,16,512]{2,1,0:T(8,128)(2,1)S(1)}, bf16[9,16,512]{2,1,0:T(8,128)(2,1)S(1)}, u32[]{:S(2)}, u32[]{:S(2)}) collective-permute-start(bf16[9,16,512]{2,1,0:T(8,128)(2,1)S(1)} %fusion.18), channel_id=1, source_target_pairs={{0,32},{16,48},{32,64},{48,80},{64,96},{80,112},{96,0},{112,16},{1... | collective-permute-start | bytes 442376 | tf_op jit(solution)/shard_map/ppermute | solution.py:47
  105.3 10.1 %collective-permute-start.19 = (bf16[18,16,512]{2,1,0:T(8,128)(2,1)S(1)}, bf16[18,16,512]{2,1,0:T(8,128)(2,1)S(1)}, u32[]{:S(2)}, u32[]{:S(2)}) collective-permute-start(bf16[18,16,512]{2,1,0:T(8,128)(2,1)S(1)} %fusion.5), channel_id=1, source_target_pairs={{0,96},{16,112},{32,0},{48,16},{64,32},{80,48},{96,64},{112,80},{1... | collective-permute-start | bytes 884744 | tf_op jit(solution)/shard_map/ppermute | solution.py:47
  109.7 25.0 %collective-permute-start.23 = (f32[4,8,16,512]{3,2,1,0:T(8,128)}, f32[4,8,16,512]{3,2,1,0:T(8,128)}, u32[]{:S(2)}, u32[]{:S(2)}) collective-permute-start(f32[4,8,16,512]{3,2,1,0:T(8,128)} %fusion.4), channel_id=1, source_target_pairs={{0,2},{1,3},{2,0},{3,1},{4,6},{5,7},{6,4},{7,5},{8,10},{9,11},{10,... | collective-permute-start | bytes 3145736 | tf_op jit(solution)/shard_map/ppermute | solution.py:34
  110.1 9.6 %collective-permute-start.18 = (bf16[18,16,512]{2,1,0:T(8,128)(2,1)S(1)}, bf16[18,16,512]{2,1,0:T(8,128)(2,1)S(1)}, u32[]{:S(2)}, u32[]{:S(2)}) collective-permute-start(bf16[18,16,512]{2,1,0:T(8,128)(2,1)S(1)} %fusion.6), channel_id=1, source_target_pairs={{0,32},{16,48},{32,64},{48,80},{64,96},{80,112},{96,0},{112,16},{1... | collective-permute-start | bytes 884744 | tf_op jit(solution)/shard_map/ppermute | solution.py:47
  112.1 12.8 %collective-permute-start.26 = (bf16[9,8,512]{2,1,0:T(8,128)(2,1)S(1)}, bf16[9,8,512]{2,1,0:T(8,128)(2,1)S(1)}, u32[]{:S(2)}, u32[]{:S(2)}) collective-permute-start(bf16[9,8,512]{2,1,0:T(8,128)(2,1)S(1)} %get-tuple-element.132), channel_id=1, source_target_pairs={{0,4},{1,5},{2,6},{3,7},{4,8},{5,9},{6,10},{7,11},{8,12},{9,13},{1... | collective-permute-start | bytes 221192 | tf_op jit(solution)/shard_map/ppermute | solution.py:42
  113.4 12.6 %collective-permute-start.27 = (bf16[9,8,512]{2,1,0:T(8,128)(2,1)S(1)}, bf16[9,8,512]{2,1,0:T(8,128)(2,1)}, u32[]{:S(2)}, u32[]{:S(2)}) collective-permute-start(bf16[9,8,512]{2,1,0:T(8,128)(2,1)S(1)} %get-tuple-element.133), channel_id=1, source_target_pairs={{0,8},{1,9},{2,10},{3,11},{4,12},{5,13},{6,14},{7,15},{8,0},{9,1},... | collective-permute-start | bytes 221192 | tf_op jit(solution)/shard_map/ppermute | solution.py:42
  120.8 19.0 %copy-start.23 = (f32[9,16,512]{2,1,0:T(8,128)S(1)}, f32[9,16,512]{2,1,0:T(8,128)}, u32[]{:S(2)}) copy-start(f32[9,16,512]{2,1,0:T(8,128)} %copy-done.22) | copy-start | bytes 884740
  120.8 19.0 %copy-start.25 = (f32[9,16,512]{2,1,0:T(8,128)S(1)}, f32[9,16,512]{2,1,0:T(8,128)}, u32[]{:S(2)}) copy-start(f32[9,16,512]{2,1,0:T(8,128)} %copy-done.24) | copy-start | bytes 884740
  121.7 10.9 %collective-permute-start.20 = (bf16[18,8,512]{2,1,0:T(8,128)(2,1)}, bf16[18,8,512]{2,1,0:T(8,128)(2,1)S(1)}, u32[]{:S(2)}, u32[]{:S(2)}) collective-permute-start(bf16[18,8,512]{2,1,0:T(8,128)(2,1)} %get-tuple-element.127), channel_id=1, source_target_pairs={{0,4},{1,5},{2,6},{3,7},{4,8},{5,9},{6,10},{7,11},{8,12},{9,13},{1... | collective-permute-start | bytes 442376 | tf_op jit(solution)/shard_map/ppermute | solution.py:42
  123.0 9.6 %collective-permute-start.21 = (bf16[18,8,512]{2,1,0:T(8,128)(2,1)S(1)}, bf16[18,8,512]{2,1,0:T(8,128)(2,1)S(1)}, u32[]{:S(2)}, u32[]{:S(2)}) collective-permute-start(bf16[18,8,512]{2,1,0:T(8,128)(2,1)S(1)} %get-tuple-element.128), channel_id=1, source_target_pairs={{0,8},{1,9},{2,10},{3,11},{4,12},{5,13},{6,14},{7,15},{8,0},{9,1},... | collective-permute-start | bytes 442376 | tf_op jit(solution)/shard_map/ppermute | solution.py:42
  124.9 7.7 %collective-permute-start.22 = (bf16[18,8,512]{2,1,0:T(8,128)(2,1)S(1)}, bf16[18,8,512]{2,1,0:T(8,128)(2,1)S(1)}, u32[]{:S(2)}, u32[]{:S(2)}) collective-permute-start(bf16[18,8,512]{2,1,0:T(8,128)(2,1)S(1)} %get-tuple-element.126), channel_id=1, source_target_pairs={{0,12},{1,13},{2,14},{3,15},{4,0},{5,1},{6,2},{7,3},{8,4},{9,5},{1... | collective-permute-start | bytes 442376 | tf_op jit(solution)/shard_map/ppermute | solution.py:42
  126.0 6.6 %collective-permute-start.28 = (bf16[9,8,512]{2,1,0:T(8,128)(2,1)}, bf16[9,8,512]{2,1,0:T(8,128)(2,1)}, u32[]{:S(2)}, u32[]{:S(2)}) collective-permute-start(bf16[9,8,512]{2,1,0:T(8,128)(2,1)} %get-tuple-element.131), channel_id=1, source_target_pairs={{0,12},{1,13},{2,14},{3,15},{4,0},{5,1},{6,2},{7,3},{8,4},{9,5},{1... | collective-permute-start | bytes 221192 | tf_op jit(solution)/shard_map/ppermute | solution.py:42
  135.9 23.8 %copy-start = (bf16[4,8,16,512]{3,2,1,0:T(8,128)(2,1)S(1)}, bf16[4,8,16,512]{3,2,1,0:T(8,128)(2,1)}, u32[]{:S(2)}) copy-start(bf16[4,8,16,512]{3,2,1,0:T(8,128)(2,1)} %pre.1) | copy-start | bytes 1572868
  135.9 23.8 %copy-start.3 = (f32[4,8,16,512]{3,2,1,0:T(8,128)S(1)}, f32[4,8,16,512]{3,2,1,0:T(8,128)}, u32[]{:S(2)}) copy-start(f32[4,8,16,512]{3,2,1,0:T(8,128)} %copy-done.2) | copy-start | bytes 3145732
  135.9 7.1 %collective-permute-start.34 = (bf16[18,8,512]{2,1,0:T(8,128)(2,1)S(1)}, bf16[18,8,512]{2,1,0:T(8,128)(2,1)S(1)}, u32[]{:S(2)}, u32[]{:S(2)}) collective-permute-start(bf16[18,8,512]{2,1,0:T(8,128)(2,1)S(1)} %get-tuple-element.122), channel_id=1, source_target_pairs={{0,16},{16,0},{32,48},{48,32},{64,80},{80,64},{96,112},{112,96},{1... | collective-permute-start | bytes 442376 | tf_op jit(solution)/shard_map/ppermute | solution.py:358
  140.8 5.9 %collective-permute-start.29 = (bf16[9,8,512]{2,1,0:T(8,128)(2,1)S(1)}, bf16[9,8,512]{2,1,0:T(8,128)(2,1)S(1)}, u32[]{:S(2)}, u32[]{:S(2)}) collective-permute-start(bf16[9,8,512]{2,1,0:T(8,128)(2,1)S(1)} %get-tuple-element.124), channel_id=1, source_target_pairs={{0,16},{16,0},{32,48},{48,32},{64,80},{80,64},{96,112},{112,96},{1... | collective-permute-start | bytes 221192 | tf_op jit(solution)/shard_map/ppermute | solution.py:358
  143.0 10.5 %collective-permute-start.35 = (f32[18,8,512]{2,1,0:T(8,128)S(1)}, f32[18,8,512]{2,1,0:T(8,128)S(1)}, u32[]{:S(2)}, u32[]{:S(2)}) collective-permute-start(f32[18,8,512]{2,1,0:T(8,128)S(1)} %convert_add_fusion.4.refs_5_), channel_id=1, source_target_pairs={{0,32},{16,48},{32,64},{48,80},{64,96},{80,112},{96,0},{112,16},{1... | collective-permute-start | bytes 884744 | tf_op jit(solution)/shard_map/ppermute | solution.py:47
  143.3 10.3 %collective-permute-start.36 = (f32[18,8,512]{2,1,0:T(8,128)S(1)}, f32[18,8,512]{2,1,0:T(8,128)S(1)}, u32[]{:S(2)}, u32[]{:S(2)}) collective-permute-start(f32[18,8,512]{2,1,0:T(8,128)S(1)} %convert_add_fusion.4.refs_5_), channel_id=1, source_target_pairs={{0,96},{16,112},{32,0},{48,16},{64,32},{80,48},{96,64},{112,80},{1... | collective-permute-start | bytes 884744 | tf_op jit(solution)/shard_map/ppermute | solution.py:47
  146.8 10.2 %collective-permute-start.31 = (f32[9,8,512]{2,1,0:T(8,128)S(1)}, f32[9,8,512]{2,1,0:T(8,128)S(1)}, u32[]{:S(2)}, u32[]{:S(2)}) collective-permute-start(f32[9,8,512]{2,1,0:T(8,128)S(1)} %convert_add_fusion.5.refs_0_), channel_id=1, source_target_pairs={{0,96},{16,112},{32,0},{48,16},{64,32},{80,48},{96,64},{112,80},{1... | collective-permute-start | bytes 442376 | tf_op jit(solution)/shard_map/ppermute | solution.py:47
  147.2 12.4 %collective-permute-start.30 = (f32[9,8,512]{2,1,0:T(8,128)S(1)}, f32[9,8,512]{2,1,0:T(8,128)S(1)}, u32[]{:S(2)}, u32[]{:S(2)}) collective-permute-start(f32[9,8,512]{2,1,0:T(8,128)S(1)} %convert_add_fusion.5.refs_0_), channel_id=1, source_target_pairs={{0,32},{16,48},{32,64},{48,80},{64,96},{80,112},{96,0},{112,16},{1... | collective-permute-start | bytes 442376 | tf_op jit(solution)/shard_map/ppermute | solution.py:47
  153.6 11.6 %collective-permute-start.37 = (f32[9,8,512]{2,1,0:T(8,128)S(1)}, f32[9,8,512]{2,1,0:T(8,128)S(1)}, u32[]{:S(2)}, u32[]{:S(2)}) collective-permute-start(f32[9,8,512]{2,1,0:T(8,128)S(1)} %slice.105), channel_id=1, source_target_pairs={{0,32},{16,48},{32,64},{48,80},{64,96},{80,112},{96,0},{112,16},{1... | collective-permute-start | bytes 442376 | tf_op jit(solution)/shard_map/ppermute | solution.py:47
  153.7 11.5 %collective-permute-start.38 = (f32[9,8,512]{2,1,0:T(8,128)S(1)}, f32[9,8,512]{2,1,0:T(8,128)S(1)}, u32[]{:S(2)}, u32[]{:S(2)}) collective-permute-start(f32[9,8,512]{2,1,0:T(8,128)S(1)} %slice.106), channel_id=1, source_target_pairs={{0,96},{16,112},{32,0},{48,16},{64,32},{80,48},{96,64},{112,80},{1... | collective-permute-start | bytes 442376 | tf_op jit(solution)/shard_map/ppermute | solution.py:47
  157.0 8.2 %collective-permute-start.33 = (f32[5,8,512]{2,1,0:T(8,128)S(1)}, f32[5,8,512]{2,1,0:T(8,128)S(1)}, u32[]{:S(2)}, u32[]{:S(2)}) collective-permute-start(f32[5,8,512]{2,1,0:T(8,128)S(1)} %slice.104), channel_id=1, source_target_pairs={{0,96},{16,112},{32,0},{48,16},{64,32},{80,48},{96,64},{112,80},{1... | collective-permute-start | bytes 245768 | tf_op jit(solution)/shard_map/ppermute | solution.py:47
  159.6 5.5 %collective-permute-start.32 = (f32[4,8,512]{2,1,0:T(8,128)S(1)}, f32[4,8,512]{2,1,0:T(8,128)S(1)}, u32[]{:S(2)}, u32[]{:S(2)}) collective-permute-start(f32[4,8,512]{2,1,0:T(8,128)S(1)} %slice.103), channel_id=1, source_target_pairs={{0,32},{16,48},{32,64},{48,80},{64,96},{80,112},{96,0},{112,16},{1... | collective-permute-start | bytes 196616 | tf_op jit(solution)/shard_map/ppermute | solution.py:47
  (25 other events, 111.9 us)

commit v3 on v2

v3 whole, which is shorter than its diff:
```python
import functools
import math

import jax
import jax.numpy as jnp
from jax import lax
from jax.experimental import pallas as pl
from jax.experimental.pallas import tpu as pltpu
from jax.sharding import PartitionSpec as P

QUAD = 4
RING = 4
F32 = jnp.float32
BF16 = jnp.bfloat16
ANY = pl.BlockSpec(memory_space=pl.ANY)
VMEM = pl.BlockSpec(memory_space=pltpu.VMEM)
LIMIT = 60 * 1024 * 1024


def params():
    return pltpu.CompilerParams(vmem_limit_bytes=LIMIT)


def quad_place():
    return lax.rem(lax.axis_index("gy"), QUAD)


def x_place():
    return lax.div(lax.axis_index("gx"), 2)


def swap(block, k):
    count = lax.axis_size("gy")
    return lax.ppermute(block, "gy", [(g, g ^ k) for g in range(count)])


def along_y(block, step, ring):
    count = lax.axis_size("gy")
    pairs = [(g, g + QUAD * step) for g in range(count)]
    if ring:
        pairs = [(s, t % count) for s, t in pairs]
    return lax.ppermute(block, "gy", [(s, t) for s, t in pairs if 0 <= t < count])


def along_x(block, step):
    count = lax.axis_size("gx")
    return lax.ppermute(block, "gx", [(g, (g + 2 * step) % count) for g in range(count)])


def rims_x(first, last, pairs=None):
    nx, ny = lax.axis_size("gx"), lax.axis_size("gy")
    pairs = pairs or [(h, h) for h in range(ny)]
    up = [(g * ny + s, (g + 1) * ny + t) for g in range(nx - 1) for s, t in pairs]
    down = [((g + 1) * ny + s, g * ny + t) for g in range(nx - 1) for s, t in pairs]
    return lax.ppermute(last, ("gx", "gy"), up), lax.ppermute(first, ("gx", "gy"), down)


def zero_at(value, z, edge):
    return jnp.where(z == edge, 0.0, value)


def pick_kernel(cot, extra, low, high, extra_low, extra_high, *quarters):
    rows, width, depth, chan = cot.shape
    j = quad_place()
    q = chan // QUAD
    part = q // RING
    source = lax.broadcasted_iota(jnp.int32, (chan, q), 0)
    place = lax.broadcasted_iota(jnp.int32, (chan, q), 1)
    base = lax.div(place, part) * q + lax.rem(place, part)

    def take(block, pick):
        shape = block.shape
        flat = block[...].reshape(-1, chan)
        got = jnp.dot(flat, pick, preferred_element_type=F32)
        return got.astype(BF16).reshape(shape[:-1] + (q,))

    for k, out in enumerate(quarters):
        pick = jnp.where(source == base + (j ^ k) * part, 1.0, 0.0).astype(BF16)
        out[0:rows, 1:width + 1] = take(cot, pick)
        out[rows, 1:width + 1] = take(extra, pick)
        out[0:rows, 0] = take(low, pick)
        out[0:rows, width + 1] = take(high, pick)
        out[rows, 0] = take(extra_low, pick)
        out[rows, width + 1] = take(extra_high, pick)


def pick_channels(cot, *rims):
    rows, width, depth, chan = cot.shape
    quarter = jax.ShapeDtypeStruct((rows + 1, width + 2, depth, chan // QUAD), BF16)
    return pl.pallas_call(
        pick_kernel,
        out_shape=[quarter] * QUAD,
        in_specs=[VMEM] * 6,
        out_specs=[VMEM] * QUAD,
        compiler_params=params(),
    )(cot, *rims)


def turn_kernel(p0, p1, p2, p3, held, out):
    j, x = quad_place(), x_place()
    for k, p in enumerate((p0, p1, p2, p3)):
        rows = p.shape[0] - 1
        held[pl.ds(1 + (j ^ k) * rows, rows)] = p[0:rows]

        @pl.when((j ^ k) == 0)
        def _():
            held[0] = p[rows]

        @pl.when((j ^ k) == QUAD - 1)
        def _():
            held[held.shape[0] - 1] = p[rows]

    tall, width, depth, q = held.shape
    width -= 2
    cells = tall * width * depth
    part = q // RING
    small = part // RING
    place = lax.broadcasted_iota(jnp.int32, (q, q), 0)
    source = lax.broadcasted_iota(jnp.int32, (q, q), 1)
    xpart = lax.rem(lax.div(place, part) + x, RING)
    base = lax.div(lax.rem(place, part), small) * part + xpart * small + lax.rem(place, small)
    order = jnp.where(source == base, 1.0, 0.0).astype(BF16)
    z = lax.rem(lax.broadcasted_iota(jnp.int32, (q, cells), 1), depth)
    for b in (-1, 0, 1):
        moved = held[:, 1 - b:1 - b + width].reshape(cells, q)
        value = lax.dot_general(
            order, moved, (((1,), (1,)), ((), ())), preferred_element_type=F32
        )
        high = zero_at(pltpu.roll(value, cells - 1, 1), z, depth - 1)
        low = zero_at(pltpu.roll(value, 1, 1), z, 0)
        for c, v in enumerate((high, value, low)):
            at = ((b + 1) * 3 + c) * q
            out[at:at + q] = v.astype(BF16)


def turn(quarters):
    rows, width, depth, q = quarters[0].shape
    tall = QUAD * (rows - 1) + 2
    return pl.pallas_call(
        turn_kernel,
        out_shape=[
            jax.ShapeDtypeStruct((tall, width, depth, q), BF16),
            jax.ShapeDtypeStruct((9 * q, tall * (width - 2) * depth), BF16),
        ],
        in_specs=[VMEM] * QUAD,
        out_specs=[VMEM] * 2,
        compiler_params=params(),
    )(*quarters)


def run_copies(pairs, sem):
    copies = [pltpu.make_async_copy(s, d, sem.at[n]) for n, (s, d) in enumerate(pairs)]
    for c in copies:
        c.start()
    return copies


def weight_kernel(low, norm, own_act, near, far, across, cot, *refs):
    right, left, keep_right, keep_left, own, held, sem = refs
    j = quad_place()
    rows, width, depth, chan = own_act.shape

    @pl.when((pl.program_id(0) == 0) & (pl.program_id(1) == 0))
    def _():
        pairs = []
        for k, piece in enumerate((own_act, near, far, across)):
            pairs.append((piece, held.at[pl.ds((j ^ k) * rows, rows)]))
        for c in run_copies(pairs, sem):
            c.wait()

    row = width * depth
    cells = QUAD * rows * row
    q = cot.shape[0] // 3
    part = q // RING
    half = part // 2
    a = low + pl.program_id(1)
    moved = cot[:, pl.ds(pl.multiple_of((1 - a) * row, row), cells)]
    act = held[...].reshape(cells, chan)
    term = jnp.dot(moved, act, preferred_element_type=F32) * norm
    for c in range(3):

        def block(r, h):
            at = c * q + r * part + h * half
            return term[at:at + half]

        right[0, c] = block(2, 0).astype(BF16)
        left[0, c] = block(2, 1).astype(BF16)
        keep_right[c] = block(1, 0)
        right[1, c] = block(1, 1).astype(BF16)
        left[1, c] = block(3, 0).astype(BF16)
        keep_left[c] = block(3, 1)
        own[0, c] = block(0, 0)
        own[1, c] = block(0, 1)


def weight_terms(low, count, norm, acts, cot):
    rows, width, depth, chan = acts[0].shape
    taps = 9 * count
    q = chan // QUAD
    half = q // RING // 2
    cells = QUAD * rows * width * depth

    def pair(dtype):
        spec = pl.BlockSpec((2, 3, half, chan), lambda b, a: (0, 3 * a + b, 0, 0))
        return jax.ShapeDtypeStruct((2, taps, half, chan), dtype), spec

    def single(dtype):
        spec = pl.BlockSpec((3, half, chan), lambda b, a: (3 * a + b, 0, 0))
        return jax.ShapeDtypeStruct((taps, half, chan), dtype), spec

    outs = [pair(BF16), pair(BF16), single(F32), single(F32), pair(F32)]
    return pl.pallas_call(
        functools.partial(weight_kernel, low, norm),
        grid=(3, count),
        out_shape=[shape for shape, _ in outs],
        in_specs=[ANY] * 4 + [pl.BlockSpec((3 * q, cot.shape[1]), lambda b, a: (b, 0))],
        out_specs=[spec for _, spec in outs],
        scratch_shapes=[
            pltpu.VMEM((QUAD * rows, width, depth, chan), BF16),
            pltpu.SemaphoreType.DMA((4,)),
        ],
        compiler_params=params(),
        cost_estimate=pl.CostEstimate(
            flops=2 * taps * q * cells * chan, bytes_accessed=10_000_000, transcendentals=0
        ),
    )(*acts, cot)


def input_kernel(held, own, above, across_low, across_high, below, send, keep, weights, sem):
    j = quad_place()
    y = lax.div(lax.axis_index("gy"), QUAD)
    part = own.shape[1]
    low = across_low.shape[0]

    @pl.when(pl.program_id(0) == 0)
    def _():
        def at(s):
            return pl.ds(pl.multiple_of(lax.rem(y + s, RING) * part, part), part)

        pairs = [
            (own, weights.at[:, at(0)]),
            (above, weights.at[:, at(1)]),
            (across_low, weights.at[pl.ds(0, low), at(2)]),
            (across_high, weights.at[pl.ds(low, 27 - low), at(2)]),
            (below, weights.at[:, at(3)]),
        ]
        for c in run_copies(pairs, sem):
            c.wait()

    _, rows, width, depth, chan = send.shape
    cells = rows * width * depth
    q = held.shape[3]
    taps = weights[...].reshape(9, 3, q, chan)
    n = pl.program_id(0)
    first = (j ^ jnp.where(n == 0, 1, jnp.where(n == 1, 3, jnp.where(n == 2, 2, 0)))) * rows
    moved = []
    for tap in range(9):
        a, b = tap // 3 - 1, tap % 3 - 1
        block = held[pl.ds(first + 1 - a, rows), 1 - b:1 - b + width]
        moved.append(block.reshape(cells, q))
    moved = jnp.concatenate(moved, axis=1)
    z = lax.rem(lax.broadcasted_iota(jnp.int32, (cells, chan), 0), depth)

    def term(c):
        return jnp.dot(moved, taps[:, c].reshape(9 * q, chan), preferred_element_type=F32)

    grad = term(1)
    grad = grad + zero_at(pltpu.roll(term(0), cells - 1, 0), z, depth - 1)
    grad = grad + zero_at(pltpu.roll(term(2), 1, 0), z, 0)

    @pl.when(n < 2)
    def _():
        send[0] = grad.reshape(rows, width, depth, chan)

    @pl.when(n >= 2)
    def _():
        keep[0] = grad.reshape(rows, width, depth, chan)


def input_terms(held, parts):
    tall, width, depth, q = held.shape
    chan = QUAD * q
    block = ((tall - 2) // QUAD, width - 2, depth, chan)
    return pl.pallas_call(
        input_kernel,
        grid=(4,),
        out_shape=[jax.ShapeDtypeStruct((2,) + block, F32)] * 2,
        in_specs=[pl.BlockSpec(held.shape, lambda n: (0, 0, 0, 0))] + [ANY] * 5,
        out_specs=[
            pl.BlockSpec((1,) + block, lambda n: (jnp.minimum(n, 1), 0, 0, 0, 0)),
            pl.BlockSpec((1,) + block, lambda n: (jnp.maximum(n - 2, 0), 0, 0, 0, 0)),
        ],
        scratch_shapes=[pltpu.VMEM((27, q, chan), BF16), pltpu.SemaphoreType.DMA((5,))],
        compiler_params=params(),
        cost_estimate=pl.CostEstimate(
            flops=2 * 27 * tall * width * depth * q * chan, bytes_accessed=10_000_000, transcendentals=0
        ),
    )(held, *parts)


def finish_kernel(pre, keep, near, far_low, far_high, out):
    rows = far_low.shape[0]
    for at, far in ((0, far_low), (rows, far_high)):
        value = pre[at:at + rows].astype(F32)
        s = jax.nn.sigmoid(value)
        grad = keep[1, at:at + rows] + near[0, at:at + rows] + far[...]
        out[at:at + rows] = (grad * s * (1.0 + value * (1.0 - s))).astype(BF16)


def finish(pre_act, keep, near, *far):
    return pl.pallas_call(
        finish_kernel,
        out_shape=jax.ShapeDtypeStruct(pre_act.shape, BF16),
        in_specs=[VMEM] * 5,
        out_specs=VMEM,
        compiler_params=params(),
    )(pre_act, keep, near, *far)


def join_kernel(*refs):
    out = refs[-1]
    x = x_place()
    size = refs[0].shape[1]

    def put(first, piece, k):
        at = pl.ds(pl.multiple_of(lax.rem(x + k, RING) * size, size), size)
        out[first:first + piece.shape[0], at] = piece[...]

    first = 0
    for chunk in (refs[:5], refs[5:10]):
        own, below, above, low, high = chunk
        put(first, own, 0)
        put(first, below, 3)
        put(first, above, 1)
        put(first, low, 2)
        put(first + low.shape[0], high, 2)
        first += own.shape[0]


def join(first, second):
    _, size, chan = first[0].shape
    return pl.pallas_call(
        join_kernel,
        out_shape=jax.ShapeDtypeStruct((27, RING * size, chan), F32),
        in_specs=[VMEM] * 10,
        out_specs=VMEM,
        compiler_params=params(),
    )(*first, *second)


def reduce_x_first(right, left, *kept):
    return along_x(right, 1), along_x(left, -1), *kept


def reduce_x_next(from_left, from_right, keep_right, keep_left, own):
    next_right = (from_left[0].astype(F32) + keep_right).astype(BF16)
    next_left = (from_right[0].astype(F32) + keep_left).astype(BF16)
    return next_right, next_left, from_left[1], from_right[1], own


def reduce_x_last(next_right, next_left, from_left, from_right, own):
    last_left = along_x(next_right, 1)
    last_right = along_x(next_left, -1)
    low = own[0] + from_right.astype(F32) + last_left.astype(F32)
    high = own[1] + from_left.astype(F32) + last_right.astype(F32)
    return jnp.concatenate([low, high], axis=1)


def reduce_y_first(total):
    y = lax.div(lax.axis_index("gy"), QUAD)
    size = total.shape[1] // RING

    def block(r):
        return lax.dynamic_slice_in_dim(total, lax.rem(y + r, RING) * size, size, axis=1)

    return block(0), [along_y(block(r).astype(BF16), r, True) for r in (1, 2, 3)]


def reduce_y_last(mine, others):
    for other in others:
        mine = mine + other.astype(F32)
    return mine


def reduce_z(mine):
    count = lax.axis_size("gx")
    other = lax.ppermute(mine.astype(BF16), "gx", [(g, g ^ 1) for g in range(count)])
    return mine + other.astype(F32)


def gather_x(whole):
    below, above = along_x(whole, 1), along_x(whole, -1)
    taps = whole.shape[0] // 2
    return [whole, below, above, along_x(below[:taps], 1), along_x(above[taps:], -1)]


def body(pre_act, cot, weight):
    rows, width, depth, chan = pre_act.shape
    norm = 1.0 / math.sqrt(rows * lax.axis_size("gy") * width * lax.axis_size("gx") * depth)
    j = quad_place()
    barrier = lax.optimization_barrier

    count = lax.axis_size("gy")
    pairs = [(g, g + 1) for g in range(QUAD - 1, count - 1, QUAD)]
    pairs = pairs + [(t, s) for s, t in pairs]
    edge = jnp.where(j == 0, cot[0], cot[rows - 1])
    extra = lax.ppermute(edge, "gy", pairs)
    rims = [extra, *rims_x(cot[:, 0], cot[:, width - 1]), *rims_x(edge[0], edge[-1], pairs)]
    act = jax.nn.silu(pre_act.astype(F32)).astype(BF16)
    rims, act, weight = barrier((rims, act, weight))

    far = swap(act, 2)
    near = swap(act, 1)
    above = along_y(weight, -1, True)
    below = along_y(weight, 1, True)
    quarters = pick_channels(cot, *rims)
    quarters = [quarters[0]] + [swap(quarters[k], k) for k in (1, 2, 3)]
    quarters, near, far = barrier((quarters, near, far))
    acts = [act, near, far, swap(far, 1)]
    held, turned = turn(quarters)

    turned, above, below = barrier((turned, above, below))
    first = weight_terms(-1, 1, norm, acts, turned)
    turned, first = barrier((turned, first))
    taps = 13
    parts = [weight, above, along_y(below[:taps], 1, True), along_y(above[taps:], -1, True), below]
    first = reduce_x_first(*first)
    second = weight_terms(0, 2, norm, acts, turned)
    held, first, second = barrier((held, first, second))
    second = reduce_x_first(*second)
    first = reduce_x_last(*reduce_x_next(*first))
    send, keep = input_terms(held, parts)
    send, keep, first, second = barrier((send, keep, first, second))
    got = swap(send, 1)
    second = reduce_x_next(*second)
    first, second = barrier((first, second))
    second = reduce_x_last(*second)
    first = reduce_y_last(*reduce_y_first(first))
    second, first, got = barrier((second, first, got))
    half = rows // 2
    far_low = swap(keep[0, :half] + got[1, :half], 2)
    second = reduce_y_last(*reduce_y_first(second))
    first = reduce_z(first)
    second, first, far_low = barrier((second, first, far_low))
    first = gather_x(first)
    second = reduce_z(second)
    second, keep, got = barrier((second, keep, got))
    far_high = swap(keep[0, half:] + got[1, half:], 2)
    second = gather_x(second)
    grad_weight = join(first, second)
    grad_pre = finish(pre_act, keep, got, far_low, far_high)
    return (grad_pre, grad_weight)


def solution(mesh):
    return jax.shard_map(
        body,
        mesh=mesh,
        in_specs=(P("gy", "gx", None, None), P("gy", "gx", None, None), P(None, "gy", None)),
        out_specs=(P("gy", "gx", None, None), P(None, "gy", None)),
        check_vma=False,
    )
```

time: 167 us -> 186 us (1.11)
  Pallas kernels: 26.4 us -> 47.7 us
  waiting for transfers between devices: 42 us -> 51.6 us
  starting transfers between devices: 74.4 us -> 68.4 us
  local copies, waits for them, and re-layouts: 11.3 us -> 6.36 us
    pallas_call x3, Pallas kernels: 19.8 us -> 32.6 us  [the longest x2 18.9 us: weight_terms(): pl.pallas_call(functools.partial(weight_kernel, low, norm), grid=(3, coun...]
    ppermute x8 -> x9, waiting for transfers between devices: 10.2 us -> 18.9 us  [swap(): return lax.ppermute(block, 'gy', [(g, g ^ k) for g in range(count)])]
    ppermute x8 -> x9, starting transfers between devices: 20.6 us -> 14.2 us  [swap(): return lax.ppermute(block, 'gy', [(g, g ^ k) for g in range(count)])]
    ppermute x10, waiting for transfers between devices: 5.5 us -> 10.4 us  [along_y(): lax.ppermute(block, 'gy', [(s, t) for s, t in pairs if 0 <= t < count])]
    convert_element_type x8 -> x5, other arithmetic: 7.2 us -> 2.46 us  [the longest x2 2.39 us: reduce_x_next(): next_left = (from_right[0].astype(F32) + keep_left).astype(BF16)]
    pallas_call x1, Pallas kernels: 1.81 us -> 5.58 us  [turn(): pl.pallas_call(turn_kernel, out_shape=[jax.ShapeDtypeStruct((tall, width,...]
    unnamed x68 -> x60, local copies, waits for them, and re-layouts: 8.99 us -> 5.25 us
    ppermute x5 -> x7, waiting for transfers between devices: 11.6 us -> 7.94 us  [the longest x2 5.35 us: reduce_z(): lax.ppermute(mine.astype(BF16), 'gx', [(g, g ^ 1) for g in range(count)])]
  transfers between devices with their start and end apart: 39 -> 42, of which waited for: 13 -> 14; matrix products, arithmetic and copies ran while one was open for 7% -> 5% of each run, Pallas kernels for 15% -> 22%
where the time goes in v3:
time: 186 us; the launch traced here: 185 us
  starting transfers between devices  68.4 us (37%)
  waiting for transfers between devices  51.6 us (28%)
  Pallas kernels  47.7 us (26%)
  other arithmetic  9.92 us (5%)
  local copies, waits for them, and re-layouts  6.36 us (3%)
    ppermute x16, starting transfers between devices, along_x(): lax.ppermute(block, 'gx', [(g, (g + 2 * step) % count) for g in range(cou...  22.4 us
    ppermute x9, waiting for transfers between devices, swap(): return lax.ppermute(block, 'gy', [(g, g ^ k) for g in range(count)])  18.9 us
    pallas_call x2, Pallas kernels, weight_terms(): pl.pallas_call(functools.partial(weight_kernel, low, norm), grid=(3, coun...  18.9 us
    ppermute x10, starting transfers between devices, along_y(): lax.ppermute(block, 'gy', [(s, t) for s, t in pairs if 0 <= t < count])  17 us
    ppermute x16, waiting for transfers between devices, along_x(): lax.ppermute(block, 'gx', [(g, (g + 2 * step) % count) for g in range(cou...  14.3 us
    ppermute x9, starting transfers between devices, swap(): return lax.ppermute(block, 'gy', [(g, g ^ k) for g in range(count)])  14.2 us
    pallas_call x1, Pallas kernels, input_terms(): pl.pallas_call(input_kernel, grid=(4,), out_shape=[jax.ShapeDtypeStruct((...  13.7 us
    ppermute x10, waiting for transfers between devices, along_y(): lax.ppermute(block, 'gy', [(s, t) for s, t in pairs if 0 <= t < count])  10.4 us
  transfers between devices with their start and end apart: 42, of which 14 were waited for; matrix products, arithmetic and copies ran while one was open for 5% of the time, Pallas kernels for 22%

profile of v3, /device:TPU:0, one launch (start us, length us, event | category | flops | bytes accessed | tf_op | source)
XLA Modules:
  0.0 185.2 jit_solution(11096843041497745188)
XLA Ops:
  3.3 5.9 %collective-permute-start.1 = (bf16[4,16,512]{2,1,0:T(8,128)(2,1)S(1)}, bf16[4,16,512]{2,1,0:T(8,128)(2,1)S(1)}, u32[]{:S(2)}, u32[]{:S(2)}) collective-permute-start(bf16[4,16,512]{2,1,0:T(8,128)(2,1)S(1)} %get-tuple-element.161), channel_id=1, source_target_pairs={{0,16},{1,17},{2,18},{3,19},{4,20},{5,21},{6,22},{7,23},{8,24},{9,... | collective-permute-start | bytes 196616 | tf_op jit(solution)/shard_map/ppermute | solution.py:55
  9.2 1.3 collective-permute-start.2
  12.8 1.4 fusion.3.own_act
  14.2 2.6 %collective-permute-done.2.high = bf16[4,16,512]{2,1,0:T(8,128)(2,1)S(1)} collective-permute-done((bf16[4,16,512]{2,1,0:T(8,128)(2,1)S(1)}, bf16[4,16,512]{2,1,0:T(8,128)(2,1)S(1)}, u32[]{:S(2)}, u32[]{:S(2)}) %collective-permute-start.2) | collective-permute-done | bytes 65568 | tf_op jit(solution)/shard_map/ppermute | solution.py:55
  18.1 3.0 %shard_map.50 = (bf16[5,10,16,128]{3,2,1,0:T(8,128)(2,1)}, bf16[5,10,16,128]{3,2,1,0:T(8,128)(2,1)}, bf16[5,10,16,128]{3,2,1,0:T(8,128)(2,1)}, bf16[5,10,16,128]{3,2,1,0:T(8,128)(2,1)}) custom-call(bf16[4,8,16,512]{3,2,1,0:T(8,128)(2,1)} %cot.1, bf16[8,16,512]{2,1,0:T(8,128)(2,1)} %copy-done.21, bf16[4,16,512]{2,1,0:T(8,128)(2,1)} %copy-done.24, ...), custom_call_target="tpu_custom_call" | custom-call | tf_op jit(solution)/shard_map/pallas_call | solution.py:90
  21.6 9.5 %collective-permute-start.9 = (bf16[4,8,16,512]{3,2,1,0:T(8,128)(2,1)S(1)}, bf16[4,8,16,512]{3,2,1,0:T(8,128)(2,1)}, u32[]{:S(2)}, u32[]{:S(2)}) collective-permute-start(bf16[4,8,16,512]{3,2,1,0:T(8,128)(2,1)S(1)} %fusion.3.own_act), channel_id=1, source_target_pairs={{0,2},{1,3},{2,0},{3,1},{4,6},{5,7},{6,4},{7,5},{8,10},{9,11},{10,... | collective-permute-start | bytes 1572872 | tf_op jit(solution)/shard_map/ppermute | solution.py:34
  31.1 5.3 %collective-permute-start.10 = (bf16[27,32,512]{2,1,0:T(8,128)(2,1)S(1)}, bf16[27,32,512]{2,1,0:T(8,128)(2,1)S(1)}, u32[]{:S(2)}, u32[]{:S(2)}) collective-permute-start(bf16[27,32,512]{2,1,0:T(8,128)(2,1)S(1)} %copy-done.28), channel_id=1, source_target_pairs={{0,12},{1,13},{2,14},{3,15},{4,0},{5,1},{6,2},{7,3},{8,4},{9,5},{1... | collective-permute-start | bytes 2654216 | tf_op jit(solution)/shard_map/ppermute | solution.py:42
  36.4 11.6 %collective-permute-done.6.p2 = bf16[5,10,16,128]{3,2,1,0:T(8,128)(2,1)S(1)} collective-permute-done((bf16[5,10,16,128]{3,2,1,0:T(8,128)(2,1)}, bf16[5,10,16,128]{3,2,1,0:T(8,128)(2,1)S(1)}, u32[]{:S(2)}, u32[]{:S(2)}) %collective-permute-start.6) | collective-permute-done | bytes 204832 | tf_op jit(solution)/shard_map/ppermute | solution.py:34
  48.0 1.1 collective-permute-start.7
  49.1 6.2 %collective-permute-done.7.p3 = bf16[5,10,16,128]{3,2,1,0:T(8,128)(2,1)S(1)} collective-permute-done((bf16[5,10,16,128]{3,2,1,0:T(8,128)(2,1)}, bf16[5,10,16,128]{3,2,1,0:T(8,128)(2,1)S(1)}, u32[]{:S(2)}, u32[]{:S(2)}) %collective-permute-start.7) | collective-permute-done | bytes 204832 | tf_op jit(solution)/shard_map/ppermute | solution.py:34
  56.6 5.6 %shard_map.51 = (bf16[18,10,16,128]{3,2,1,0:T(8,128)(2,1)}, bf16[1152,2304]{1,0:T(8,128)(2,1)}) custom-call(bf16[5,10,16,128]{3,2,1,0:T(8,128)(2,1)} %get-tuple-element.86.p0, bf16[5,10,16,128]{3,2,1,0:T(8,128)(2,1)} %copy-done.16, bf16[5,10,16,128]{3,2,1,0:T(8,128)(2,1)} %copy-done.17, bf16[5,10,16,128]{3,2,1,0:T(8,128)(2,1)} %copy-done.18), custom_call_target="tpu_custom_call" | custom-call | tf_op jit(solution)/shard_map/pallas_call | solution.py:139
  63.2 2.4 %collective-permute-start.15 = (bf16[13,32,512]{2,1,0:T(8,128)(2,1)S(1)}, bf16[13,32,512]{2,1,0:T(8,128)(2,1)}, u32[]{:S(2)}, u32[]{:S(2)}) collective-permute-start(bf16[13,32,512]{2,1,0:T(8,128)(2,1)S(1)} %slice.92), channel_id=1, source_target_pairs={{0,4},{1,5},{2,6},{3,7},{4,8},{5,9},{6,10},{7,11},{8,12},{9,13},{1... | collective-permute-start | bytes 1277960 | tf_op jit(solution)/shard_map/ppermute | solution.py:42
  65.6 1.5 collective-permute-start.16
  67.1 7.7 %shard_map.52 = (bf16[2,9,16,512]{3,2,1,0:T(8,128)(2,1)}, bf16[2,9,16,512]{3,2,1,0:T(8,128)(2,1)}, f32[9,16,512]{2,1,0:T(8,128)}, f32[9,16,512]{2,1,0:T(8,128)}, f32[2,9,16,512]{3,2,1,0:T(8,128)}) custom-call(bf16[4,8,16,512]{3,2,1,0:T(8,128)(2,1)} %copy-done.9, bf16[4,8,16,512]{3,2,1,0:T(8,128)(2,1)} %copy-done.29, ...), custom_call_target="tpu_custom_call" | custom-call | flops 2415919104 | bytes 10000000 | tf_op jit(solution)/shard_map/pallas_call | solution.py:212
  74.9 1.6 collective-permute-start.13
  76.4 1.7 collective-permute-start.14
  78.2 11.2 %shard_map.53 = (bf16[2,18,16,512]{3,2,1,0:T(8,128)(2,1)}, bf16[2,18,16,512]{3,2,1,0:T(8,128)(2,1)}, f32[18,16,512]{2,1,0:T(8,128)}, f32[18,16,512]{2,1,0:T(8,128)}, f32[2,18,16,512]{3,2,1,0:T(8,128)}) custom-call(bf16[4,8,16,512]{3,2,1,0:T(8,128)(2,1)} %copy-done.9, bf16[4,8,16,512]{3,2,1,0:T(8,128)(2,1)} %copy-done.29, ...), custom_call_target="tpu_custom_call" | custom-call | flops 4831838208 | bytes 10000000 | tf_op jit(solution)/shard_map/pallas_call | solution.py:212
  89.9 3.0 %collective-permute-start.18 = (bf16[9,16,512]{2,1,0:T(8,128)(2,1)S(1)}, bf16[9,16,512]{2,1,0:T(8,128)(2,1)S(1)}, u32[]{:S(2)}, u32[]{:S(2)}) collective-permute-start(bf16[9,16,512]{2,1,0:T(8,128)(2,1)S(1)} %fusion.8), channel_id=1, source_target_pairs={{0,96},{16,112},{32,0},{48,16},{64,32},{80,48},{96,64},{112,80},{1... | collective-permute-start | bytes 442376 | tf_op jit(solution)/shard_map/ppermute | solution.py:47
  92.9 3.2 %collective-permute-start.20 = (bf16[2,18,16,512]{3,2,1,0:T(8,128)(2,1)}, bf16[2,18,16,512]{3,2,1,0:T(8,128)(2,1)S(1)}, u32[]{:S(2)}, u32[]{:S(2)}) collective-permute-start(bf16[2,18,16,512]{3,2,1,0:T(8,128)(2,1)} %get-tuple-element.123), channel_id=1, source_target_pairs={{0,96},{16,112},{32,0},{48,16},{64,32},{80,48},{96,64},{112,80},{1... | collective-permute-start | bytes 1769480 | tf_op jit(solution)/shard_map/ppermute | solution.py:47
  96.1 13.7 %shard_map.54 = (f32[2,4,8,16,512]{4,3,2,1,0:T(8,128)}, f32[2,4,8,16,512]{4,3,2,1,0:T(8,128)}) custom-call(bf16[18,10,16,128]{3,2,1,0:T(8,128)(2,1)} %get-tuple-element.112.held, bf16[27,32,512]{2,1,0:T(8,128)(2,1)} %own, bf16[27,32,512]{2,1,0:T(8,128)(2,1)} %copy-done.14, bf16[13,32,512]{2,1,0:T(8,128)(2,1)} %collective-permute-done.15.across_low, ...), custom_call_target="tpu_custom_call" | custom-call | flops 10192158720 | bytes 10000000 | tf_op jit(solution)/shard_map/pallas_call | solution.py:284
  110.3 2.4 %fusion.4 = (bf16[18,16,512]{2,1,0:T(8,128)(2,1)}, bf16[18,16,512]{2,1,0:T(8,128)(2,1)}) fusion(f32[18,16,512]{2,1,0:T(8,128)} %get-tuple-element.131, bf16[2,18,16,512]{3,2,1,0:T(8,128)(2,1)S(1)} %collective-permute-done.20, f32[18,16,512]{2,1,0:T(8,128)} %get-tuple-element.129, bf16[2,18,16,512]{3,2,1,0:T(8,128)(2,1)S(1)} %collective-permute-done.19), kind=kLoop, calls=%fused_computation.9 | loop fusion | flops 884736 | bytes 2359296 | tf_op jit(solution)/shard_map/convert_element_type | solution.py:357
  112.7 2.1 %collective-permute-start.25 = (bf16[9,8,512]{2,1,0:T(8,128)(2,1)S(1)}, bf16[9,8,512]{2,1,0:T(8,128)(2,1)S(1)}, u32[]{:S(2)}, u32[]{:S(2)}) collective-permute-start(bf16[9,8,512]{2,1,0:T(8,128)(2,1)S(1)} %get-tuple-element.156), channel_id=1, source_target_pairs={{0,12},{1,13},{2,14},{3,15},{4,0},{5,1},{6,2},{7,3},{8,4},{9,5},{1... | collective-permute-start | bytes 221192 | tf_op jit(solution)/shard_map/ppermute | solution.py:42
  116.4 2.1 %collective-permute-done.25 = bf16[9,8,512]{2,1,0:T(8,128)(2,1)S(1)} collective-permute-done((bf16[9,8,512]{2,1,0:T(8,128)(2,1)S(1)}, bf16[9,8,512]{2,1,0:T(8,128)(2,1)S(1)}, u32[]{:S(2)}, u32[]{:S(2)}) %collective-permute-start.25) | collective-permute-done | bytes 73760 | tf_op jit(solution)/shard_map/ppermute | solution.py:42
  118.5 1.7 collective-permute-start.22
  120.2 1.1 collective-permute-done.24
  122.2 4.1 %collective-permute-done.21 = bf16[18,16,512]{2,1,0:T(8,128)(2,1)S(1)} collective-permute-done((bf16[18,16,512]{2,1,0:T(8,128)(2,1)}, bf16[18,16,512]{2,1,0:T(8,128)(2,1)S(1)}, u32[]{:S(2)}, u32[]{:S(2)}) %collective-permute-start.21) | collective-permute-done | bytes 294944 | tf_op jit(solution)/shard_map/ppermute | solution.py:47
  126.3 1.2 fusion.7
  127.7 4.3 %collective-permute-start.30 = (bf16[9,8,512]{2,1,0:T(8,128)(2,1)S(1)}, bf16[9,8,512]{2,1,0:T(8,128)(2,1)S(1)}, u32[]{:S(2)}, u32[]{:S(2)}) collective-permute-start(bf16[9,8,512]{2,1,0:T(8,128)(2,1)S(1)} %convert_element_type.150), channel_id=1, source_target_pairs={{0,16},{16,0},{32,48},{48,32},{64,80},{80,64},{96,112},{112,96},{1... | collective-permute-start | bytes 221192 | tf_op jit(solution)/shard_map/ppermute | solution.py:387
  132.0 1.1 add_bitcast_fusion.1
  133.1 1.3 collective-permute-start.31
  134.5 2.2 %collective-permute-start.29 = (bf16[18,8,512]{2,1,0:T(8,128)(2,1)S(1)}, bf16[18,8,512]{2,1,0:T(8,128)(2,1)S(1)}, u32[]{:S(2)}, u32[]{:S(2)}) collective-permute-start(bf16[18,8,512]{2,1,0:T(8,128)(2,1)S(1)} %get-tuple-element.151), channel_id=1, source_target_pairs={{0,12},{1,13},{2,14},{3,15},{4,0},{5,1},{6,2},{7,3},{8,4},{9,5},{1... | collective-permute-start | bytes 442376 | tf_op jit(solution)/shard_map/ppermute | solution.py:42
  137.3 1.3 collective-permute-start.27
  138.6 2.7 %collective-permute-done.29 = bf16[18,8,512]{2,1,0:T(8,128)(2,1)S(1)} collective-permute-done((bf16[18,8,512]{2,1,0:T(8,128)(2,1)S(1)}, bf16[18,8,512]{2,1,0:T(8,128)(2,1)S(1)}, u32[]{:S(2)}, u32[]{:S(2)}) %collective-permute-start.29) | collective-permute-done | bytes 147488 | tf_op jit(solution)/shard_map/ppermute | solution.py:42
  141.3 2.2 %collective-permute-done.28 = bf16[18,8,512]{2,1,0:T(8,128)(2,1)S(1)} collective-permute-done((bf16[18,8,512]{2,1,0:T(8,128)(2,1)S(1)}, bf16[18,8,512]{2,1,0:T(8,128)(2,1)S(1)}, u32[]{:S(2)}, u32[]{:S(2)}) %collective-permute-start.28) | collective-permute-done | bytes 147488 | tf_op jit(solution)/shard_map/ppermute | solution.py:42
  143.5 1.5 collective-permute-done.27
  145.0 1.1 collective-permute-done.31.far_low
  146.1 1.4 collective-permute-start.32
  147.5 5.3 %collective-permute-done.32 = bf16[18,8,512]{2,1,0:T(8,128)(2,1)S(1)} collective-permute-done((bf16[18,8,512]{2,1,0:T(8,128)(2,1)S(1)}, bf16[18,8,512]{2,1,0:T(8,128)(2,1)S(1)}, u32[]{:S(2)}, u32[]{:S(2)}) %collective-permute-start.32) | collective-permute-done | bytes 147488 | tf_op jit(solution)/shard_map/ppermute | solution.py:387
  152.9 1.2 add_bitcast_fusion
  154.1 1.3 collective-permute-start.33
  155.5 3.2 %collective-permute-start.39 = (f32[18,8,512]{2,1,0:T(8,128)S(1)}, f32[18,8,512]{2,1,0:T(8,128)S(1)}, u32[]{:S(2)}, u32[]{:S(2)}) collective-permute-start(f32[18,8,512]{2,1,0:T(8,128)S(1)} %convert_add_fusion.4.refs_5_), channel_id=1, source_target_pairs={{0,96},{16,112},{32,0},{48,16},{64,32},{80,48},{96,64},{112,80},{1... | collective-permute-start | bytes 884744 | tf_op jit(solution)/shard_map/ppermute | solution.py:47
  158.7 1.7 collective-permute-start.35
  160.7 5.5 %collective-permute-done.38.refs_6_ = f32[18,8,512]{2,1,0:T(8,128)S(1)} collective-permute-done((f32[18,8,512]{2,1,0:T(8,128)S(1)}, f32[18,8,512]{2,1,0:T(8,128)S(1)}, u32[]{:S(2)}, u32[]{:S(2)}) %collective-permute-start.38) | collective-permute-done | bytes 294944 | tf_op jit(solution)/shard_map/ppermute | solution.py:47
  166.3 3.3 %collective-permute-start.41 = (f32[9,8,512]{2,1,0:T(8,128)S(1)}, f32[9,8,512]{2,1,0:T(8,128)S(1)}, u32[]{:S(2)}, u32[]{:S(2)}) collective-permute-start(f32[9,8,512]{2,1,0:T(8,128)S(1)} %slice.119), channel_id=1, source_target_pairs={{0,96},{16,112},{32,0},{48,16},{64,32},{80,48},{96,64},{112,80},{1... | collective-permute-start | bytes 442376 | tf_op jit(solution)/shard_map/ppermute | solution.py:47
  169.6 1.3 collective-permute-start.37
  171.8 4.7 %collective-permute-done.36.refs_3_ = f32[4,8,512]{2,1,0:T(8,128)S(1)} collective-permute-done((f32[4,8,512]{2,1,0:T(8,128)S(1)}, f32[4,8,512]{2,1,0:T(8,128)S(1)}, u32[]{:S(2)}, u32[]{:S(2)}) %collective-permute-start.36) | collective-permute-done | bytes 65568 | tf_op jit(solution)/shard_map/ppermute | solution.py:47
  177.9 2.8 %shard_map.56 = f32[27,32,512]{2,1,0:T(8,128)} custom-call(f32[9,8,512]{2,1,0:T(8,128)} %copy-done.6, f32[9,8,512]{2,1,0:T(8,128)} %copy-done.11, f32[9,8,512]{2,1,0:T(8,128)} %copy-done.10, f32[4,8,512]{2,1,0:T(8,128)} %copy-done.23, f32[5,8,512]{2,1,0:T(8,128)} %copy-done.22, f32[18,8,512]{2,1,0:T(8,128)} %copy-done.2, f32[18,8,512]{2,1,0:T(8,128)} %copy-done.3, ...), custom_call_target="tpu_custom_call" | custom-call | tf_op jit(solution)/shard_map/pallas_call | solution.py:342
  181.5 3.8 %shard_map.55 = bf16[4,8,16,512]{3,2,1,0:T(8,128)(2,1)} custom-call(bf16[4,8,16,512]{3,2,1,0:T(8,128)(2,1)} %pre.1, f32[2,4,8,16,512]{4,3,2,1,0:T(8,128)} %get-tuple-element.145.keep, f32[2,4,8,16,512]{4,3,2,1,0:T(8,128)} %collective-permute-done.26.near, f32[2,8,16,512]{3,2,1,0:T(8,128)} %copy-done.7, f32[2,8,16,512]{3,2,1,0:T(8,128)} %copy-done.8), custom_call_target="tpu_custom_call" | custom-call | tf_op jit(solution)/shard_map/pallas_call | solution.py:311
  (132 shorter events, 16.8 us)
Async XLA Ops:
  0.6 30.5 %copy-start.28 = (bf16[27,32,512]{2,1,0:T(8,128)(2,1)S(1)}, bf16[27,32,512]{2,1,0:T(8,128)(2,1)}, u32[]{:S(2)}) copy-start(bf16[27,32,512]{2,1,0:T(8,128)(2,1)} %own) | copy-start | bytes 2654212
  1.7 15.1 %collective-permute-start = (bf16[8,16,512]{2,1,0:T(8,128)(2,1)S(1)}, bf16[8,16,512]{2,1,0:T(8,128)(2,1)S(1)}, u32[]{:S(2)}, u32[]{:S(2)}) collective-permute-start(bf16[8,16,512]{2,1,0:T(8,128)(2,1)S(1)} %fusion.10), channel_id=1, source_target_pairs={{3,4},{7,8},{11,12},{4,3},{8,7},{12,11},{19,20},{23,24},{27,28},{2... | collective-permute-start | bytes 393224 | tf_op jit(solution)/shard_map/ppermute | solution.py:407
  3.3 10.9 %collective-permute-start.1 = (bf16[4,16,512]{2,1,0:T(8,128)(2,1)S(1)}, bf16[4,16,512]{2,1,0:T(8,128)(2,1)S(1)}, u32[]{:S(2)}, u32[]{:S(2)}) collective-permute-start(bf16[4,16,512]{2,1,0:T(8,128)(2,1)S(1)} %get-tuple-element.161), channel_id=1, source_target_pairs={{0,16},{1,17},{2,18},{3,19},{4,20},{5,21},{6,22},{7,23},{8,24},{9,... | collective-permute-start | bytes 196616 | tf_op jit(solution)/shard_map/ppermute | solution.py:55
  9.2 7.7 %collective-permute-start.2 = (bf16[4,16,512]{2,1,0:T(8,128)(2,1)S(1)}, bf16[4,16,512]{2,1,0:T(8,128)(2,1)S(1)}, u32[]{:S(2)}, u32[]{:S(2)}) collective-permute-start(bf16[4,16,512]{2,1,0:T(8,128)(2,1)S(1)} %get-tuple-element.160), channel_id=1, source_target_pairs={{16,0},{17,1},{18,2},{19,3},{20,4},{21,5},{22,6},{23,7},{24,8},{25... | collective-permute-start | bytes 196616 | tf_op jit(solution)/shard_map/ppermute | solution.py:55
  11.5 2.7 %collective-permute-start.3 = (bf16[16,512]{1,0:T(8,128)(2,1)S(1)}, bf16[16,512]{1,0:T(8,128)(2,1)S(1)}, u32[]{:S(2)}, u32[]{:S(2)}) collective-permute-start(bf16[16,512]{1,0:T(8,128)(2,1)S(1)} %get-tuple-element.163), channel_id=1, source_target_pairs={{3,20},{7,24},{11,28},{4,19},{8,23},{12,27},{19,36},{23,40},{27,44... | collective-permute-start | bytes 49160 | tf_op jit(solution)/shard_map/ppermute | solution.py:55
  12.1 2.1 %collective-permute-start.4 = (bf16[16,512]{1,0:T(8,128)(2,1)S(1)}, bf16[16,512]{1,0:T(8,128)(2,1)S(1)}, u32[]{:S(2)}, u32[]{:S(2)}) collective-permute-start(bf16[16,512]{1,0:T(8,128)(2,1)S(1)} %get-tuple-element.162), channel_id=1, source_target_pairs={{19,4},{23,8},{27,12},{20,3},{24,7},{28,11},{35,20},{39,24},{43,28... | collective-permute-start | bytes 49160 | tf_op jit(solution)/shard_map/ppermute | solution.py:55
  14.2 53.0 %copy-start.9 = (bf16[4,8,16,512]{3,2,1,0:T(8,128)(2,1)}, bf16[4,8,16,512]{3,2,1,0:T(8,128)(2,1)S(1)}, u32[]{:S(2)}) copy-start(bf16[4,8,16,512]{3,2,1,0:T(8,128)(2,1)S(1)} %fusion.3.own_act) | copy-start | bytes 1572868
  21.1 15.3 %collective-permute-start.5 = (bf16[5,10,16,128]{3,2,1,0:T(8,128)(2,1)}, bf16[5,10,16,128]{3,2,1,0:T(8,128)(2,1)S(1)}, u32[]{:S(2)}, u32[]{:S(2)}) collective-permute-start(bf16[5,10,16,128]{3,2,1,0:T(8,128)(2,1)} %get-tuple-element.82), channel_id=1, source_target_pairs={{0,1},{1,0},{2,3},{3,2},{4,5},{5,4},{6,7},{7,6},{8,9},{9,8},{10,11... | collective-permute-start | bytes 614408 | tf_op jit(solution)/shard_map/ppermute | solution.py:34
  21.1 34.2 %collective-permute-start.8 = (bf16[4,8,16,512]{3,2,1,0:T(8,128)(2,1)S(1)}, bf16[4,8,16,512]{3,2,1,0:T(8,128)(2,1)S(1)}, u32[]{:S(2)}, u32[]{:S(2)}) collective-permute-start(bf16[4,8,16,512]{3,2,1,0:T(8,128)(2,1)S(1)} %fusion.3.own_act), channel_id=1, source_target_pairs={{0,1},{1,0},{2,3},{3,2},{4,5},{5,4},{6,7},{7,6},{8,9},{9,8},{10,11... | collective-permute-start | bytes 1572872 | tf_op jit(solution)/shard_map/ppermute | solution.py:34
  21.6 33.7 %collective-permute-start.9 = (bf16[4,8,16,512]{3,2,1,0:T(8,128)(2,1)S(1)}, bf16[4,8,16,512]{3,2,1,0:T(8,128)(2,1)}, u32[]{:S(2)}, u32[]{:S(2)}) collective-permute-start(bf16[4,8,16,512]{3,2,1,0:T(8,128)(2,1)S(1)} %fusion.3.own_act), channel_id=1, source_target_pairs={{0,2},{1,3},{2,0},{3,1},{4,6},{5,7},{6,4},{7,5},{8,10},{9,11},{10,... | collective-permute-start | bytes 1572872 | tf_op jit(solution)/shard_map/ppermute | solution.py:34
  31.1 17.0 %collective-permute-start.6 = (bf16[5,10,16,128]{3,2,1,0:T(8,128)(2,1)}, bf16[5,10,16,128]{3,2,1,0:T(8,128)(2,1)S(1)}, u32[]{:S(2)}, u32[]{:S(2)}) collective-permute-start(bf16[5,10,16,128]{3,2,1,0:T(8,128)(2,1)} %get-tuple-element.83), channel_id=1, source_target_pairs={{0,2},{1,3},{2,0},{3,1},{4,6},{5,7},{6,4},{7,5},{8,10},{9,11},{10,... | collective-permute-start | bytes 614408 | tf_op jit(solution)/shard_map/ppermute | solution.py:34
  31.1 31.1 %collective-permute-start.10 = (bf16[27,32,512]{2,1,0:T(8,128)(2,1)S(1)}, bf16[27,32,512]{2,1,0:T(8,128)(2,1)S(1)}, u32[]{:S(2)}, u32[]{:S(2)}) collective-permute-start(bf16[27,32,512]{2,1,0:T(8,128)(2,1)S(1)} %copy-done.28), channel_id=1, source_target_pairs={{0,12},{1,13},{2,14},{3,15},{4,0},{5,1},{6,2},{7,3},{8,4},{9,5},{1... | collective-permute-start | bytes 2654216 | tf_op jit(solution)/shard_map/ppermute | solution.py:42
  36.4 20.2 %copy-start.16 = (bf16[5,10,16,128]{3,2,1,0:T(8,128)(2,1)}, bf16[5,10,16,128]{3,2,1,0:T(8,128)(2,1)S(1)}, u32[]{:S(2)}) copy-start(bf16[5,10,16,128]{3,2,1,0:T(8,128)(2,1)S(1)} %collective-permute-done.5.p1) | copy-start | bytes 614404
  36.4 25.8 %collective-permute-start.11 = (bf16[27,32,512]{2,1,0:T(8,128)(2,1)S(1)}, bf16[27,32,512]{2,1,0:T(8,128)(2,1)S(1)}, u32[]{:S(2)}, u32[]{:S(2)}) collective-permute-start(bf16[27,32,512]{2,1,0:T(8,128)(2,1)S(1)} %copy-done.28), channel_id=1, source_target_pairs={{0,4},{1,5},{2,6},{3,7},{4,8},{5,9},{6,10},{7,11},{8,12},{9,13},{1... | collective-permute-start | bytes 2654216 | tf_op jit(solution)/shard_map/ppermute | solution.py:42
  48.0 7.3 %collective-permute-start.7 = (bf16[5,10,16,128]{3,2,1,0:T(8,128)(2,1)}, bf16[5,10,16,128]{3,2,1,0:T(8,128)(2,1)S(1)}, u32[]{:S(2)}, u32[]{:S(2)}) collective-permute-start(bf16[5,10,16,128]{3,2,1,0:T(8,128)(2,1)} %get-tuple-element.84), channel_id=1, source_target_pairs={{0,3},{1,2},{2,1},{3,0},{4,7},{5,6},{6,5},{7,4},{8,11},{9,10},{10,... | collective-permute-start | bytes 614408 | tf_op jit(solution)/shard_map/ppermute | solution.py:34
  56.2 10.9 %collective-permute-start.12 = (bf16[4,8,16,512]{3,2,1,0:T(8,128)(2,1)}, bf16[4,8,16,512]{3,2,1,0:T(8,128)(2,1)}, u32[]{:S(2)}, u32[]{:S(2)}) collective-permute-start(bf16[4,8,16,512]{3,2,1,0:T(8,128)(2,1)} %collective-permute-done.9.far), channel_id=1, source_target_pairs={{0,1},{1,0},{2,3},{3,2},{4,5},{5,4},{6,7},{7,6},{8,9},{9,8},{10,11... | collective-permute-start | bytes 1572872 | tf_op jit(solution)/shard_map/ppermute | solution.py:34
  63.2 29.7 %collective-permute-start.15 = (bf16[13,32,512]{2,1,0:T(8,128)(2,1)S(1)}, bf16[13,32,512]{2,1,0:T(8,128)(2,1)}, u32[]{:S(2)}, u32[]{:S(2)}) collective-permute-start(bf16[13,32,512]{2,1,0:T(8,128)(2,1)S(1)} %slice.92), channel_id=1, source_target_pairs={{0,4},{1,5},{2,6},{3,7},{4,8},{5,9},{6,10},{7,11},{8,12},{9,13},{1... | collective-permute-start | bytes 1277960 | tf_op jit(solution)/shard_map/ppermute | solution.py:42
  65.6 30.5 %collective-permute-start.16 = (bf16[14,32,512]{2,1,0:T(8,128)(2,1)S(1)}, bf16[14,32,512]{2,1,0:T(8,128)(2,1)}, u32[]{:S(2)}, u32[]{:S(2)}) collective-permute-start(bf16[14,32,512]{2,1,0:T(8,128)(2,1)S(1)} %slice.93), channel_id=1, source_target_pairs={{0,12},{1,13},{2,14},{3,15},{4,0},{5,1},{6,2},{7,3},{8,4},{9,5},{1... | collective-permute-start | bytes 1376264 | tf_op jit(solution)/shard_map/ppermute | solution.py:42
  74.9 14.5 %collective-permute-start.13 = (bf16[2,9,16,512]{3,2,1,0:T(8,128)(2,1)}, bf16[2,9,16,512]{3,2,1,0:T(8,128)(2,1)S(1)}, u32[]{:S(2)}, u32[]{:S(2)}) collective-permute-start(bf16[2,9,16,512]{3,2,1,0:T(8,128)(2,1)} %get-tuple-element.101), channel_id=1, source_target_pairs={{0,32},{16,48},{32,64},{48,80},{64,96},{80,112},{96,0},{112,16},{1... | collective-permute-start | bytes 884744 | tf_op jit(solution)/shard_map/ppermute | solution.py:47
  76.4 13.0 %collective-permute-start.14 = (bf16[2,9,16,512]{3,2,1,0:T(8,128)(2,1)}, bf16[2,9,16,512]{3,2,1,0:T(8,128)(2,1)S(1)}, u32[]{:S(2)}, u32[]{:S(2)}) collective-permute-start(bf16[2,9,16,512]{3,2,1,0:T(8,128)(2,1)} %get-tuple-element.102), channel_id=1, source_target_pairs={{0,96},{16,112},{32,0},{48,16},{64,32},{80,48},{96,64},{112,80},{1... | collective-permute-start | bytes 884744 | tf_op jit(solution)/shard_map/ppermute | solution.py:47
  89.5 20.4 %collective-permute-start.17 = (bf16[9,16,512]{2,1,0:T(8,128)(2,1)S(1)}, bf16[9,16,512]{2,1,0:T(8,128)(2,1)S(1)}, u32[]{:S(2)}, u32[]{:S(2)}) collective-permute-start(bf16[9,16,512]{2,1,0:T(8,128)(2,1)S(1)} %fusion.9), channel_id=1, source_target_pairs={{0,32},{16,48},{32,64},{48,80},{64,96},{80,112},{96,0},{112,16},{1... | collective-permute-start | bytes 442376 | tf_op jit(solution)/shard_map/ppermute | solution.py:47
  89.9 20.0 %collective-permute-start.18 = (bf16[9,16,512]{2,1,0:T(8,128)(2,1)S(1)}, bf16[9,16,512]{2,1,0:T(8,128)(2,1)S(1)}, u32[]{:S(2)}, u32[]{:S(2)}) collective-permute-start(bf16[9,16,512]{2,1,0:T(8,128)(2,1)S(1)} %fusion.8), channel_id=1, source_target_pairs={{0,96},{16,112},{32,0},{48,16},{64,32},{80,48},{96,64},{112,80},{1... | collective-permute-start | bytes 442376 | tf_op jit(solution)/shard_map/ppermute | solution.py:47
  92.9 17.2 %collective-permute-start.19 = (bf16[2,18,16,512]{3,2,1,0:T(8,128)(2,1)}, bf16[2,18,16,512]{3,2,1,0:T(8,128)(2,1)S(1)}, u32[]{:S(2)}, u32[]{:S(2)}) collective-permute-start(bf16[2,18,16,512]{3,2,1,0:T(8,128)(2,1)} %get-tuple-element.122), channel_id=1, source_target_pairs={{0,32},{16,48},{32,64},{48,80},{64,96},{80,112},{96,0},{112,16},{1... | collective-permute-start | bytes 1769480 | tf_op jit(solution)/shard_map/ppermute | solution.py:47
  92.9 17.2 %collective-permute-start.20 = (bf16[2,18,16,512]{3,2,1,0:T(8,128)(2,1)}, bf16[2,18,16,512]{3,2,1,0:T(8,128)(2,1)S(1)}, u32[]{:S(2)}, u32[]{:S(2)}) collective-permute-start(bf16[2,18,16,512]{3,2,1,0:T(8,128)(2,1)} %get-tuple-element.123), channel_id=1, source_target_pairs={{0,96},{16,112},{32,0},{48,16},{64,32},{80,48},{96,64},{112,80},{1... | collective-permute-start | bytes 1769480 | tf_op jit(solution)/shard_map/ppermute | solution.py:47
  110.1 17.6 %collective-permute-start.26 = (f32[2,4,8,16,512]{4,3,2,1,0:T(8,128)}, f32[2,4,8,16,512]{4,3,2,1,0:T(8,128)}, u32[]{:S(2)}, u32[]{:S(2)}) collective-permute-start(f32[2,4,8,16,512]{4,3,2,1,0:T(8,128)} %get-tuple-element.139), channel_id=1, source_target_pairs={{0,1},{1,0},{2,3},{3,2},{4,5},{5,4},{6,7},{7,6},{8,9},{9,8},{10,11... | collective-permute-start | bytes 6291464 | tf_op jit(solution)/shard_map/ppermute | solution.py:34
  112.7 5.8 %collective-permute-start.25 = (bf16[9,8,512]{2,1,0:T(8,128)(2,1)S(1)}, bf16[9,8,512]{2,1,0:T(8,128)(2,1)S(1)}, u32[]{:S(2)}, u32[]{:S(2)}) collective-permute-start(bf16[9,8,512]{2,1,0:T(8,128)(2,1)S(1)} %get-tuple-element.156), channel_id=1, source_target_pairs={{0,12},{1,13},{2,14},{3,15},{4,0},{5,1},{6,2},{7,3},{8,4},{9,5},{1... | collective-permute-start | bytes 221192 | tf_op jit(solution)/shard_map/ppermute | solution.py:42
  114.8 6.6 %collective-permute-start.24 = (bf16[9,8,512]{2,1,0:T(8,128)(2,1)S(1)}, bf16[9,8,512]{2,1,0:T(8,128)(2,1)S(1)}, u32[]{:S(2)}, u32[]{:S(2)}) collective-permute-start(bf16[9,8,512]{2,1,0:T(8,128)(2,1)S(1)} %get-tuple-element.157), channel_id=1, source_target_pairs={{0,8},{1,9},{2,10},{3,11},{4,12},{5,13},{6,14},{7,15},{8,0},{9,1},... | collective-permute-start | bytes 221192 | tf_op jit(solution)/shard_map/ppermute | solution.py:42
  115.4 6.8 %collective-permute-start.23 = (bf16[9,8,512]{2,1,0:T(8,128)(2,1)S(1)}, bf16[9,8,512]{2,1,0:T(8,128)(2,1)S(1)}, u32[]{:S(2)}, u32[]{:S(2)}) collective-permute-start(bf16[9,8,512]{2,1,0:T(8,128)(2,1)S(1)} %get-tuple-element.155), channel_id=1, source_target_pairs={{0,4},{1,5},{2,6},{3,7},{4,8},{5,9},{6,10},{7,11},{8,12},{9,13},{1... | collective-permute-start | bytes 221192 | tf_op jit(solution)/shard_map/ppermute | solution.py:42
  116.4 9.9 %collective-permute-start.21 = (bf16[18,16,512]{2,1,0:T(8,128)(2,1)}, bf16[18,16,512]{2,1,0:T(8,128)(2,1)S(1)}, u32[]{:S(2)}, u32[]{:S(2)}) collective-permute-start(bf16[18,16,512]{2,1,0:T(8,128)(2,1)} %get-tuple-element.135), channel_id=1, source_target_pairs={{0,32},{16,48},{32,64},{48,80},{64,96},{80,112},{96,0},{112,16},{1... | collective-permute-start | bytes 884744 | tf_op jit(solution)/shard_map/ppermute | solution.py:47
  118.5 7.8 %collective-permute-start.22 = (bf16[18,16,512]{2,1,0:T(8,128)(2,1)}, bf16[18,16,512]{2,1,0:T(8,128)(2,1)}, u32[]{:S(2)}, u32[]{:S(2)}) collective-permute-start(bf16[18,16,512]{2,1,0:T(8,128)(2,1)} %get-tuple-element.137), channel_id=1, source_target_pairs={{0,96},{16,112},{32,0},{48,16},{64,32},{80,48},{96,64},{112,80},{1... | collective-permute-start | bytes 884744 | tf_op jit(solution)/shard_map/ppermute | solution.py:47
  127.7 10.9 %collective-permute-start.30 = (bf16[9,8,512]{2,1,0:T(8,128)(2,1)S(1)}, bf16[9,8,512]{2,1,0:T(8,128)(2,1)S(1)}, u32[]{:S(2)}, u32[]{:S(2)}) collective-permute-start(bf16[9,8,512]{2,1,0:T(8,128)(2,1)S(1)} %convert_element_type.150), channel_id=1, source_target_pairs={{0,16},{16,0},{32,48},{48,32},{64,80},{80,64},{96,112},{112,96},{1... | collective-permute-start | bytes 221192 | tf_op jit(solution)/shard_map/ppermute | solution.py:387
  133.1 13.0 %collective-permute-start.31 = (f32[2,8,16,512]{3,2,1,0:T(8,128)S(1)}, f32[2,8,16,512]{3,2,1,0:T(8,128)S(1)}, u32[]{:S(2)}, u32[]{:S(2)}) collective-permute-start(f32[2,8,16,512]{3,2,1,0:T(8,128)S(1)} %add_bitcast_fusion.1), channel_id=1, source_target_pairs={{0,2},{1,3},{2,0},{3,1},{4,6},{5,7},{6,4},{7,5},{8,10},{9,11},{10,... | collective-permute-start | bytes 1572872 | tf_op jit(solution)/shard_map/ppermute | solution.py:34
  134.5 6.8 %collective-permute-start.29 = (bf16[18,8,512]{2,1,0:T(8,128)(2,1)S(1)}, bf16[18,8,512]{2,1,0:T(8,128)(2,1)S(1)}, u32[]{:S(2)}, u32[]{:S(2)}) collective-permute-start(bf16[18,8,512]{2,1,0:T(8,128)(2,1)S(1)} %get-tuple-element.151), channel_id=1, source_target_pairs={{0,12},{1,13},{2,14},{3,15},{4,0},{5,1},{6,2},{7,3},{8,4},{9,5},{1... | collective-permute-start | bytes 442376 | tf_op jit(solution)/shard_map/ppermute | solution.py:42
  136.7 6.8 %collective-permute-start.28 = (bf16[18,8,512]{2,1,0:T(8,128)(2,1)S(1)}, bf16[18,8,512]{2,1,0:T(8,128)(2,1)S(1)}, u32[]{:S(2)}, u32[]{:S(2)}) collective-permute-start(bf16[18,8,512]{2,1,0:T(8,128)(2,1)S(1)} %get-tuple-element.152), channel_id=1, source_target_pairs={{0,8},{1,9},{2,10},{3,11},{4,12},{5,13},{6,14},{7,15},{8,0},{9,1},... | collective-permute-start | bytes 442376 | tf_op jit(solution)/shard_map/ppermute | solution.py:42
  137.3 7.7 %collective-permute-start.27 = (bf16[18,8,512]{2,1,0:T(8,128)(2,1)S(1)}, bf16[18,8,512]{2,1,0:T(8,128)(2,1)S(1)}, u32[]{:S(2)}, u32[]{:S(2)}) collective-permute-start(bf16[18,8,512]{2,1,0:T(8,128)(2,1)S(1)} %get-tuple-element.150), channel_id=1, source_target_pairs={{0,4},{1,5},{2,6},{3,7},{4,8},{5,9},{6,10},{7,11},{8,12},{9,13},{1... | collective-permute-start | bytes 442376 | tf_op jit(solution)/shard_map/ppermute | solution.py:42
  138.6 21.7 %copy-start.6 = (f32[9,8,512]{2,1,0:T(8,128)}, f32[9,8,512]{2,1,0:T(8,128)S(1)}, u32[]{:S(2)}) copy-start(f32[9,8,512]{2,1,0:T(8,128)S(1)} %convert_add_fusion.6.refs_0_) | copy-start | bytes 442372
  146.1 24.8 %copy-start.7 = (f32[2,8,16,512]{3,2,1,0:T(8,128)}, f32[2,8,16,512]{3,2,1,0:T(8,128)S(1)}, u32[]{:S(2)}) copy-start(f32[2,8,16,512]{3,2,1,0:T(8,128)S(1)} %collective-permute-done.31.far_low) | copy-start | bytes 1572868
  146.1 6.7 %collective-permute-start.32 = (bf16[18,8,512]{2,1,0:T(8,128)(2,1)S(1)}, bf16[18,8,512]{2,1,0:T(8,128)(2,1)S(1)}, u32[]{:S(2)}, u32[]{:S(2)}) collective-permute-start(bf16[18,8,512]{2,1,0:T(8,128)(2,1)S(1)} %convert_element_type.152), channel_id=1, source_target_pairs={{0,16},{16,0},{32,48},{48,32},{64,80},{80,64},{96,112},{112,96},{1... | collective-permute-start | bytes 442376 | tf_op jit(solution)/shard_map/ppermute | solution.py:387
  152.9 23.6 %copy-start.2 = (f32[18,8,512]{2,1,0:T(8,128)}, f32[18,8,512]{2,1,0:T(8,128)S(1)}, u32[]{:S(2)}) copy-start(f32[18,8,512]{2,1,0:T(8,128)S(1)} %convert_add_fusion.4.refs_5_) | copy-start | bytes 884740
  154.1 26.5 %collective-permute-start.33 = (f32[2,8,16,512]{3,2,1,0:T(8,128)S(1)}, f32[2,8,16,512]{3,2,1,0:T(8,128)S(1)}, u32[]{:S(2)}, u32[]{:S(2)}) collective-permute-start(f32[2,8,16,512]{3,2,1,0:T(8,128)S(1)} %add_bitcast_fusion), channel_id=1, source_target_pairs={{0,2},{1,3},{2,0},{3,1},{4,6},{5,7},{6,4},{7,5},{8,10},{9,11},{10,... | collective-permute-start | bytes 1572872 | tf_op jit(solution)/shard_map/ppermute | solution.py:34
  155.4 10.8 %collective-permute-start.38 = (f32[18,8,512]{2,1,0:T(8,128)S(1)}, f32[18,8,512]{2,1,0:T(8,128)S(1)}, u32[]{:S(2)}, u32[]{:S(2)}) collective-permute-start(f32[18,8,512]{2,1,0:T(8,128)S(1)} %convert_add_fusion.4.refs_5_), channel_id=1, source_target_pairs={{0,32},{16,48},{32,64},{48,80},{64,96},{80,112},{96,0},{112,16},{1... | collective-permute-start | bytes 884744 | tf_op jit(solution)/shard_map/ppermute | solution.py:47
  155.5 10.8 %collective-permute-start.39 = (f32[18,8,512]{2,1,0:T(8,128)S(1)}, f32[18,8,512]{2,1,0:T(8,128)S(1)}, u32[]{:S(2)}, u32[]{:S(2)}) collective-permute-start(f32[18,8,512]{2,1,0:T(8,128)S(1)} %convert_add_fusion.4.refs_5_), channel_id=1, source_target_pairs={{0,96},{16,112},{32,0},{48,16},{64,32},{80,48},{96,64},{112,80},{1... | collective-permute-start | bytes 884744 | tf_op jit(solution)/shard_map/ppermute | solution.py:47
  158.7 10.9 %collective-permute-start.35 = (f32[9,8,512]{2,1,0:T(8,128)S(1)}, f32[9,8,512]{2,1,0:T(8,128)S(1)}, u32[]{:S(2)}, u32[]{:S(2)}) collective-permute-start(f32[9,8,512]{2,1,0:T(8,128)S(1)} %convert_add_fusion.6.refs_0_), channel_id=1, source_target_pairs={{0,96},{16,112},{32,0},{48,16},{64,32},{80,48},{96,64},{112,80},{1... | collective-permute-start | bytes 442376 | tf_op jit(solution)/shard_map/ppermute | solution.py:47
  160.3 10.6 %collective-permute-start.34 = (f32[9,8,512]{2,1,0:T(8,128)S(1)}, f32[9,8,512]{2,1,0:T(8,128)S(1)}, u32[]{:S(2)}, u32[]{:S(2)}) collective-permute-start(f32[9,8,512]{2,1,0:T(8,128)S(1)} %convert_add_fusion.6.refs_0_), channel_id=1, source_target_pairs={{0,32},{16,48},{32,64},{48,80},{64,96},{80,112},{96,0},{112,16},{1... | collective-permute-start | bytes 442376 | tf_op jit(solution)/shard_map/ppermute | solution.py:47
  166.2 10.3 %collective-permute-start.40 = (f32[9,8,512]{2,1,0:T(8,128)S(1)}, f32[9,8,512]{2,1,0:T(8,128)S(1)}, u32[]{:S(2)}, u32[]{:S(2)}) collective-permute-start(f32[9,8,512]{2,1,0:T(8,128)S(1)} %slice.118), channel_id=1, source_target_pairs={{0,32},{16,48},{32,64},{48,80},{64,96},{80,112},{96,0},{112,16},{1... | collective-permute-start | bytes 442376 | tf_op jit(solution)/shard_map/ppermute | solution.py:47
  166.3 10.2 %collective-permute-start.41 = (f32[9,8,512]{2,1,0:T(8,128)S(1)}, f32[9,8,512]{2,1,0:T(8,128)S(1)}, u32[]{:S(2)}, u32[]{:S(2)}) collective-permute-start(f32[9,8,512]{2,1,0:T(8,128)S(1)} %slice.119), channel_id=1, source_target_pairs={{0,96},{16,112},{32,0},{48,16},{64,32},{80,48},{96,64},{112,80},{1... | collective-permute-start | bytes 442376 | tf_op jit(solution)/shard_map/ppermute | solution.py:47
  169.6 6.9 %collective-permute-start.37 = (f32[5,8,512]{2,1,0:T(8,128)S(1)}, f32[5,8,512]{2,1,0:T(8,128)S(1)}, u32[]{:S(2)}, u32[]{:S(2)}) collective-permute-start(f32[5,8,512]{2,1,0:T(8,128)S(1)} %slice.117), channel_id=1, source_target_pairs={{0,96},{16,112},{32,0},{48,16},{64,32},{80,48},{96,64},{112,80},{1... | collective-permute-start | bytes 245768 | tf_op jit(solution)/shard_map/ppermute | solution.py:47
  171.0 5.5 %collective-permute-start.36 = (f32[4,8,512]{2,1,0:T(8,128)S(1)}, f32[4,8,512]{2,1,0:T(8,128)S(1)}, u32[]{:S(2)}, u32[]{:S(2)}) collective-permute-start(f32[4,8,512]{2,1,0:T(8,128)S(1)} %slice.116), channel_id=1, source_target_pairs={{0,32},{16,48},{32,64},{48,80},{64,96},{80,112},{96,0},{112,16},{1... | collective-permute-start | bytes 196616 | tf_op jit(solution)/shard_map/ppermute | solution.py:47
  (24 other events, 140.2 us)

commit v4 on v2

--- a/solution.py
+++ b/solution.py
@@ -14,7 +14,7 @@
 BF16 = jnp.bfloat16
 ANY = pl.BlockSpec(memory_space=pl.ANY)
 VMEM = pl.BlockSpec(memory_space=pltpu.VMEM)
-LIMIT = 40 * 1024 * 1024
+LIMIT = 24 * 1024 * 1024
 
 
 def params():
@@ -297,35 +297,60 @@
     )(pre_act, keep, near, far)
 
 
-def join_kernel(*refs):
-    out = refs[-1]
+def split_kernel(*refs):
+    parts, outs, total = refs[:10], refs[10:14], refs[14]
+    y = lax.div(lax.axis_index("gy"), QUAD)
+    taps = 0
+    for own, from_left, from_right, last_left, last_right in (parts[:5], parts[5:]):
+        count, rows = own.shape[1:3]
+        low = own[0] + from_right[1].astype(F32) + last_left[...].astype(F32)
+        high = own[1] + from_left[1].astype(F32) + last_right[...].astype(F32)
+        at = slice(taps, taps + count)
+        for half, value in enumerate((low, high)):
+            for sub in range(2):
+                total[2 * half + sub, at] = value[:, sub * (rows // 2):(sub + 1) * (rows // 2)]
+        taps += count
+    for r, out in enumerate(outs):
+        out[...] = total[lax.rem(y + r, RING)].astype(out.dtype)
+
+
+def split(first, second):
+    _, count, rows, chan = first[0].shape
+    shape = (3 * count, rows // 2, chan)
+    return pl.pallas_call(
+        split_kernel,
+        out_shape=[jax.ShapeDtypeStruct(shape, F32)] + [jax.ShapeDtypeStruct(shape, BF16)] * 3,
+        in_specs=[VMEM] * 10,
+        out_specs=[VMEM] * 4,
+        scratch_shapes=[pltpu.VMEM((RING,) + shape, F32)],
+        compiler_params=params(),
+    )(*first, *second)
+
+
+def join_kernel(own, below, above, low, high, out):
     x = x_place()
-    size = refs[0].shape[1]
+    size = own.shape[1]
 
     def put(first, piece, k):
         at = pl.ds(pl.multiple_of(lax.rem(x + k, RING) * size, size), size)
         out[first:first + piece.shape[0], at] = piece[...]
 
-    first = 0
-    for chunk in (refs[:5], refs[5:10]):
-        own, below, above, low, high = chunk
-        put(first, own, 0)
-        put(first, below, 3)
-        put(first, above, 1)
-        put(first, low, 2)
-        put(first + low.shape[0], high, 2)
-        first += own.shape[0]
-
-
-def join(first, second):
-    _, size, chan = first[0].shape
+    put(0, own, 0)
+    put(0, below, 3)
+    put(0, above, 1)
+    put(0, low, 2)
+    put(low.shape[0], high, 2)
+
+
+def join(pieces):
+    taps, size, chan = pieces[0].shape
     return pl.pallas_call(
         join_kernel,
-        out_shape=jax.ShapeDtypeStruct((27, RING * size, chan), F32),
-        in_specs=[VMEM] * 10,
+        out_shape=jax.ShapeDtypeStruct((taps, RING * size, chan), F32),
+        in_specs=[VMEM] * 5,
         out_specs=VMEM,
         compiler_params=params(),
-    )(*first, *second)
+    )(*pieces)
 
 
 def reduce_x_first(right, left, *kept):
@@ -335,72 +360,64 @@
 def reduce_x_last(from_left, from_right, keep_right, keep_left, own):
     next_right = (from_left[0].astype(F32) + keep_right).astype(BF16)
     next_left = (from_right[0].astype(F32) + keep_left).astype(BF16)
-    last_left = along_x(next_right, 1)
-    last_right = along_x(next_left, -1)
-    low = own[0] + from_right[1].astype(F32) + last_left.astype(F32)
-    high = own[1] + from_left[1].astype(F32) + last_right.astype(F32)
-    return jnp.concatenate([low, high], axis=1)
-
-
-def reduce_rest(total, beside=()):
-    y = lax.div(lax.axis_index("gy"), QUAD)
-    size = total.shape[1] // RING
-
-    def block(r):
-        return lax.dynamic_slice_in_dim(total, lax.rem(y + r, RING) * size, size, axis=1)
-
-    others = [along_y(block(r).astype(BF16), r, True) for r in (1, 2, 3)]
-    others, beside = lax.optimization_barrier((others, beside))
-    mine = block(0)
-    for other in others:
-        mine = mine + other.astype(F32)
-    count = lax.axis_size("gx")
-    other = lax.ppermute(mine.astype(BF16), "gx", [(g, g ^ 1) for g in range(count)])
-    whole = mine + other.astype(F32)
+    return own, from_left, from_right, along_x(next_right, 1), along_x(next_left, -1)
+
+
+def gather_x(whole):
     below, above = along_x(whole, 1), along_x(whole, -1)
     taps = whole.shape[0] // 2
-    return [whole, below, above, along_x(below[:taps], 1), along_x(above[taps:], -1)], beside
+    return [whole, below, above, along_x(below[:taps], 1), along_x(above[taps:], -1)]
 
 
 def body(pre_act, cot, weight):
     rows, width, depth, chan = pre_act.shape
     norm = 1.0 / math.sqrt(rows * lax.axis_size("gy") * width * lax.axis_size("gx") * depth)
     j = quad_place()
+    barrier = lax.optimization_barrier
 
     count = lax.axis_size("gy")
     pairs = [(g, g + 1) for g in range(QUAD - 1, count - 1, QUAD)]
     pairs = pairs + [(t, s) for s, t in pairs]
     extra = lax.ppermute(jnp.where(j == 0, cot[0], cot[rows - 1]), "gy", pairs)
+    extra, weight = barrier((extra, weight))
     act = jax.nn.silu(pre_act.astype(F32)).astype(BF16)
     far = swap(act, 2)
     near = swap(act, 1)
     above = along_y(weight, -1, True)
     below = along_y(weight, 1, True)
     sides = [jnp.concatenate([cot[:, x], extra[x][None]]) for x in (0, width - 1)]
+    sides = barrier(sides)
     low, high = rims_x(*sides)
     quarters = pick_channels(cot, extra, low, high)
-    quarters, near, far = lax.optimization_barrier((quarters, near, far))
+    quarters, near, far = barrier((quarters, near, far))
     quarters = [quarters[0]] + [swap(quarters[k], k) for k in (1, 2, 3)]
     acts = [act, near, far, swap(far, 1)]
     held, turned = turn(quarters)
 
-    turned, above, below = lax.optimization_barrier((turned, above, below))
+    turned, above, below = barrier((turned, above, below))
+    first = weight_terms((-1,), norm, acts, turned)
+    turned, first = barrier((turned, first))
     taps = 13
     parts = [weight, above, along_y(below[:taps], 1, True), along_y(above[taps:], -1, True), below]
-    first = weight_terms((-1,), norm, acts, turned)
-    turned, first = lax.optimization_barrier((turned, first))
     first = reduce_x_first(*first)
     second = weight_terms((0, 1), norm, acts, turned)
-    held, first, second = lax.optimization_barrier((held, first, second))
+    held, first, second = barrier((held, first, second))
     second = reduce_x_first(*second)
+    first = reduce_x_last(*first)
     grads = input_terms(held, parts)
-    second, grads = lax.optimization_barrier((second, grads))
+    grads, first, second = barrier((grads, first, second))
+    second = reduce_x_last(*second)
     send, keep, pass_on = grads
     got = swap(send, 1)
     far_grad = swap(pass_on + got[1], 2)
-    first, _ = reduce_rest(reduce_x_last(*first))
-    second, far_grad = reduce_rest(reduce_x_last(*second), far_grad)
-    grad_weight = join(first, second)
+    mine, *others = split(first, second)
+    others = [along_y(block, r, True) for r, block in zip((1, 2, 3), others)]
+    others, far_grad = barrier((others, far_grad))
+    for other in others:
+        mine = mine + other.astype(F32)
+    count = lax.axis_size("gx")
+    other = lax.ppermute(mine.astype(BF16), "gx", [(g, g ^ 1) for g in range(count)])
+    grad_weight = join(gather_x(mine + other.astype(F32)))
     grad_pre = finish(pre_act, keep, got, far_grad)
     return (grad_pre, grad_weight)
 

time: 167 us -> 147 us (0.88)
  waiting for transfers between devices: 42 us -> 65.4 us
  starting transfers between devices: 74.4 us -> 53.8 us
  local copies, waits for them, and re-layouts: 11.3 us -> 1 us
  other arithmetic: 11.3 us -> 3.11 us
  Pallas kernels: 26.4 us -> 22.6 us
    ppermute x8, starting transfers between devices: 20.6 us -> 3.02 us  [swap(): return lax.ppermute(block, 'gy', [(g, g ^ k) for g in range(count)])]
    ppermute x16 -> x12, waiting for transfers between devices: 14.7 us -> 27 us  [along_x(): lax.ppermute(block, 'gx', [(g, (g + 2 * step) % count) for g in range(cou...]
    unnamed x68 -> x6, local copies, waits for them, and re-layouts: 8.99 us -> 0.02 us
    ppermute x8, waiting for transfers between devices: 10.2 us -> 15.4 us  [swap(): return lax.ppermute(block, 'gy', [(g, g ^ k) for g in range(count)])]
    ppermute x16 -> x12, starting transfers between devices: 24.9 us -> 20.7 us  [along_x(): lax.ppermute(block, 'gx', [(g, (g + 2 * step) % count) for g in range(cou...]
    convert_element_type x4 -> x1, other arithmetic: 3.73 us -> 0.12 us  [body(): mine.astype(BF16)]
    ppermute x10 -> x7, waiting for transfers between devices: 5.5 us -> 9.09 us  [along_y(): lax.ppermute(block, 'gy', [(s, t) for s, t in pairs if 0 <= t < count])]
    ppermute x2 -> x1, waiting for transfers between devices: 2.16 us -> 4.9 us  [body(): lax.ppermute(mine.astype(BF16), 'gx', [(g, g ^ 1) for g in range(count)])]
  transfers between devices with their start and end apart: 39 -> 31, of which waited for: 13 -> 17; matrix products, arithmetic and copies ran while one was open for 7% -> 2% of each run, Pallas kernels for 15% -> 14%
where the time goes in v4:
time: 147 us
  waiting for transfers between devices  65.4 us (44%)
  starting transfers between devices  53.8 us (37%)
  Pallas kernels  22.6 us (15%)
  other arithmetic  3.11 us (2%)
    ppermute x12, waiting for transfers between devices, along_x(): lax.ppermute(block, 'gx', [(g, (g + 2 * step) % count) for g in range(cou...  27 us
    ppermute x12, starting transfers between devices, along_x(): lax.ppermute(block, 'gx', [(g, (g + 2 * step) % count) for g in range(cou...  20.7 us
    ppermute x7, starting transfers between devices, along_y(): lax.ppermute(block, 'gy', [(s, t) for s, t in pairs if 0 <= t < count])  18.5 us
    ppermute x8, waiting for transfers between devices, swap(): return lax.ppermute(block, 'gy', [(g, g ^ k) for g in range(count)])  15.4 us
    ppermute x7, waiting for transfers between devices, along_y(): lax.ppermute(block, 'gy', [(s, t) for s, t in pairs if 0 <= t < count])  9.09 us
    pallas_call x1, Pallas kernels, input_terms(): pl.pallas_call(input_kernel, out_shape=[jax.ShapeDtypeStruct((2,) + block...  8.7 us
    pallas_call x2, Pallas kernels, weight_terms(): pl.pallas_call(functools.partial(weight_kernel, offsets, norm), out_shape...  7.99 us
    ppermute x1, waiting for transfers between devices, rims_x(): high = lax.ppermute(first, 'gx', [(g + 1, g) for g in range(count - 1)])  6.91 us
  transfers between devices with their start and end apart: 31, of which 17 were waited for; matrix products, arithmetic and copies ran while one was open for 2% of the time, Pallas kernels for 14%

profile of v4, /device:TPU:0, one launch (start us, length us, event | category | flops | bytes accessed | tf_op | source)
XLA Modules:
  0.0 146.7 jit_solution(6211594384594688589)
XLA Ops:
  0.6 1.4 fusion.3.own_act
  2.2 2.1 %collective-permute-start.4 = (bf16[4,8,16,512]{3,2,1,0:T(8,128)(2,1)S(1)}, bf16[4,8,16,512]{3,2,1,0:T(8,128)(2,1)S(1)}, u32[]{:S(2)}, u32[]{:S(2)}) collective-permute-start(bf16[4,8,16,512]{3,2,1,0:T(8,128)(2,1)S(1)} %fusion.3.own_act), channel_id=1, source_target_pairs={{0,2},{1,3},{2,0},{3,1},{4,6},{5,7},{6,4},{7,5},{8,10},{9,11},{10,... | collective-permute-start | bytes 1572872 | tf_op jit(solution)/shard_map/ppermute | solution.py:34
  4.2 1.0 select_bitcast_fusion
  5.2 0.7 collective-permute-start
  5.9 0.9 slice_bitcast_fusion.1
  6.8 10.0 %collective-permute-start.8 = (bf16[27,32,512]{2,1,0:T(8,128)(2,1)}, bf16[27,32,512]{2,1,0:T(8,128)(2,1)S(1)}, u32[]{:S(2)}, u32[]{:S(2)}) collective-permute-start(bf16[27,32,512]{2,1,0:T(8,128)(2,1)} %own), channel_id=1, source_target_pairs={{0,12},{1,13},{2,14},{3,15},{4,0},{5,1},{6,2},{7,3},{8,4},{9,5},{1... | collective-permute-start | bytes 2654216 | tf_op jit(solution)/shard_map/ppermute | solution.py:42
  16.9 5.3 %collective-permute-start.1 = (bf16[5,16,512]{2,1,0:T(8,128)(2,1)S(1)}, bf16[5,16,512]{2,1,0:T(8,128)(2,1)S(1)}, u32[]{:S(2)}, u32[]{:S(2)}) collective-permute-start(bf16[5,16,512]{2,1,0:T(8,128)(2,1)S(1)} %get-tuple-element.73), channel_id=1, source_target_pairs={{0,16},{16,32},{32,48},{48,64},{64,80},{80,96},{96,112},{1,17},{17... | collective-permute-start | bytes 245768 | tf_op jit(solution)/shard_map/ppermute | solution.py:52
  22.1 2.0 %collective-permute-done.1.low = bf16[5,16,512]{2,1,0:T(8,128)(2,1)S(1)} collective-permute-done((bf16[5,16,512]{2,1,0:T(8,128)(2,1)S(1)}, bf16[5,16,512]{2,1,0:T(8,128)(2,1)S(1)}, u32[]{:S(2)}, u32[]{:S(2)}) %collective-permute-start.1) | collective-permute-done | bytes 81952 | tf_op jit(solution)/shard_map/ppermute | solution.py:52
  24.2 1.3 collective-permute-start.2
  25.4 6.9 %collective-permute-done.2.high = bf16[5,16,512]{2,1,0:T(8,128)(2,1)S(1)} collective-permute-done((bf16[5,16,512]{2,1,0:T(8,128)(2,1)S(1)}, bf16[5,16,512]{2,1,0:T(8,128)(2,1)S(1)}, u32[]{:S(2)}, u32[]{:S(2)}) %collective-permute-start.2) | collective-permute-done | bytes 81952 | tf_op jit(solution)/shard_map/ppermute | solution.py:53
  32.4 1.0 shard_map.50
  33.5 0.5 collective-permute-start.5
  34.0 1.7 %collective-permute-done.5.p1 = bf16[5,10,16,128]{3,2,1,0:T(8,128)(2,1)S(1)} collective-permute-done((bf16[5,10,16,128]{3,2,1,0:T(8,128)(2,1)S(1)}, bf16[5,10,16,128]{3,2,1,0:T(8,128)(2,1)S(1)}, u32[]{:S(2)}, u32[]{:S(2)}) %collective-permute-start.5) | collective-permute-done | bytes 204832 | tf_op jit(solution)/shard_map/ppermute | solution.py:34
  35.7 6.2 %collective-permute-done.6.p2 = bf16[5,10,16,128]{3,2,1,0:T(8,128)(2,1)S(1)} collective-permute-done((bf16[5,10,16,128]{3,2,1,0:T(8,128)(2,1)S(1)}, bf16[5,10,16,128]{3,2,1,0:T(8,128)(2,1)S(1)}, u32[]{:S(2)}, u32[]{:S(2)}) %collective-permute-start.6) | collective-permute-done | bytes 204832 | tf_op jit(solution)/shard_map/ppermute | solution.py:34
  41.9 2.7 %collective-permute-done.7.p3 = bf16[5,10,16,128]{3,2,1,0:T(8,128)(2,1)S(1)} collective-permute-done((bf16[5,10,16,128]{3,2,1,0:T(8,128)(2,1)S(1)}, bf16[5,10,16,128]{3,2,1,0:T(8,128)(2,1)S(1)}, u32[]{:S(2)}, u32[]{:S(2)}) %collective-permute-start.7) | collective-permute-done | bytes 204832 | tf_op jit(solution)/shard_map/ppermute | solution.py:34
  44.6 1.8 %shard_map.51 = (bf16[18,10,16,128]{3,2,1,0:T(8,128)(2,1)S(1)}, bf16[1152,2304]{1,0:T(8,128)(2,1)S(1)}) custom-call(bf16[5,10,16,128]{3,2,1,0:T(8,128)(2,1)S(1)} %get-tuple-element.79.p0, bf16[5,10,16,128]{3,2,1,0:T(8,128)(2,1)S(1)} %collective-permute-done.5.p1, bf16[5,10,16,128]{3,2,1,0:T(8,128)(2,1)S(1)} %collective-permute-done.6.p2, ...), custom_call_target="tpu_custom_call" | custom-call | tf_op jit(solution)/shard_map/pallas_call | solution.py:136
  46.5 0.4 collective-permute-start.13
  47.0 3.8 %collective-permute-start.14 = (bf16[14,32,512]{2,1,0:T(8,128)(2,1)S(1)}, bf16[14,32,512]{2,1,0:T(8,128)(2,1)S(1)}, u32[]{:S(2)}, u32[]{:S(2)}) collective-permute-start(bf16[14,32,512]{2,1,0:T(8,128)(2,1)S(1)} %slice.52), channel_id=1, source_target_pairs={{0,12},{1,13},{2,14},{3,15},{4,0},{5,1},{6,2},{7,3},{8,4},{9,5},{1... | collective-permute-start | bytes 1376264 | tf_op jit(solution)/shard_map/ppermute | solution.py:42
  50.8 2.8 %shard_map.52 = (bf16[2,9,16,512]{3,2,1,0:T(8,128)(2,1)S(1)}, bf16[2,9,16,512]{3,2,1,0:T(8,128)(2,1)S(1)}, f32[9,16,512]{2,1,0:T(8,128)S(1)}, f32[9,16,512]{2,1,0:T(8,128)S(1)}, f32[2,9,16,512]{3,2,1,0:T(8,128)S(1)}) custom-call(bf16[4,8,16,512]{3,2,1,0:T(8,128)(2,1)S(1)} %fusion.3.own_act, bf16[4,8,16,512]{3,2,1,0:T(8,128)(2,1)S(1)} %collective-permute-done.3.near, ...), custom_call_target="tpu_custom_call" | custom-call | flops 2415919104 | bytes 10000000 | tf_op jit(solution)/shard_map/pallas_call | solution.py:204
  53.6 1.8 %collective-permute-start.11 = (bf16[2,9,16,512]{3,2,1,0:T(8,128)(2,1)S(1)}, bf16[2,9,16,512]{3,2,1,0:T(8,128)(2,1)S(1)}, u32[]{:S(2)}, u32[]{:S(2)}) collective-permute-start(bf16[2,9,16,512]{3,2,1,0:T(8,128)(2,1)S(1)} %get-tuple-element.94), channel_id=1, source_target_pairs={{0,32},{16,48},{32,64},{48,80},{64,96},{80,112},{96,0},{112,16},{1... | collective-permute-start | bytes 884744 | tf_op jit(solution)/shard_map/ppermute | solution.py:47
  55.4 1.5 %collective-permute-start.12 = (bf16[2,9,16,512]{3,2,1,0:T(8,128)(2,1)S(1)}, bf16[2,9,16,512]{3,2,1,0:T(8,128)(2,1)S(1)}, u32[]{:S(2)}, u32[]{:S(2)}) collective-permute-start(bf16[2,9,16,512]{3,2,1,0:T(8,128)(2,1)S(1)} %get-tuple-element.95), channel_id=1, source_target_pairs={{0,96},{16,112},{32,0},{48,16},{64,32},{80,48},{96,64},{112,80},{1... | collective-permute-start | bytes 884744 | tf_op jit(solution)/shard_map/ppermute | solution.py:47
  56.9 5.2 %shard_map.53 = (bf16[2,18,16,512]{3,2,1,0:T(8,128)(2,1)S(1)}, bf16[2,18,16,512]{3,2,1,0:T(8,128)(2,1)S(1)}, f32[18,16,512]{2,1,0:T(8,128)S(1)}, f32[18,16,512]{2,1,0:T(8,128)S(1)}, f32[2,18,16,512]{3,2,1,0:T(8,128)S(1)}) custom-call(bf16[4,8,16,512]{3,2,1,0:T(8,128)(2,1)S(1)} %fusion.3.own_act, bf16[4,8,16,512]{3,2,1,0:T(8,128)(2,1)S(1)} %collective-permute-done.3.near, ...), custom_call_target="tpu_custom_call" | custom-call | flops 4831838208 | bytes 10000000 | tf_op jit(solution)/shard_map/pallas_call | solution.py:204
  62.1 2.1 %collective-permute-done.11.refs_1_ = bf16[2,9,16,512]{3,2,1,0:T(8,128)(2,1)S(1)} collective-permute-done((bf16[2,9,16,512]{3,2,1,0:T(8,128)(2,1)S(1)}, bf16[2,9,16,512]{3,2,1,0:T(8,128)(2,1)S(1)}, u32[]{:S(2)}, u32[]{:S(2)}) %collective-permute-start.11) | collective-permute-done | bytes 294944 | tf_op jit(solution)/shard_map/ppermute | solution.py:47
  64.4 1.7 %collective-permute-start.15 = (bf16[9,16,512]{2,1,0:T(8,128)(2,1)S(1)}, bf16[9,16,512]{2,1,0:T(8,128)(2,1)S(1)}, u32[]{:S(2)}, u32[]{:S(2)}) collective-permute-start(bf16[9,16,512]{2,1,0:T(8,128)(2,1)S(1)} %fusion.8), channel_id=1, source_target_pairs={{0,32},{16,48},{32,64},{48,80},{64,96},{80,112},{96,0},{112,16},{1... | collective-permute-start | bytes 442376 | tf_op jit(solution)/shard_map/ppermute | solution.py:47
  66.2 1.8 %collective-permute-start.16 = (bf16[9,16,512]{2,1,0:T(8,128)(2,1)S(1)}, bf16[9,16,512]{2,1,0:T(8,128)(2,1)S(1)}, u32[]{:S(2)}, u32[]{:S(2)}) collective-permute-start(bf16[9,16,512]{2,1,0:T(8,128)(2,1)S(1)} %fusion.7), channel_id=1, source_target_pairs={{0,96},{16,112},{32,0},{48,16},{64,32},{80,48},{96,64},{112,80},{1... | collective-permute-start | bytes 442376 | tf_op jit(solution)/shard_map/ppermute | solution.py:47
  68.0 0.3 collective-permute-start.17
  68.3 3.0 %collective-permute-start.18 = (bf16[2,18,16,512]{3,2,1,0:T(8,128)(2,1)S(1)}, bf16[2,18,16,512]{3,2,1,0:T(8,128)(2,1)S(1)}, u32[]{:S(2)}, u32[]{:S(2)}) collective-permute-start(bf16[2,18,16,512]{3,2,1,0:T(8,128)(2,1)S(1)} %get-tuple-element.117), channel_id=1, source_target_pairs={{0,96},{16,112},{32,0},{48,16},{64,32},{80,48},{96,64},{112,80},{1... | collective-permute-start | bytes 1769480 | tf_op jit(solution)/shard_map/ppermute | solution.py:47
  71.2 8.7 %shard_map.54 = (f32[2,4,8,16,512]{4,3,2,1,0:T(8,128)S(1)}, f32[4,8,16,512]{3,2,1,0:T(8,128)S(1)}, f32[4,8,16,512]{3,2,1,0:T(8,128)S(1)}) custom-call(bf16[18,10,16,128]{3,2,1,0:T(8,128)(2,1)S(1)} %get-tuple-element.105.held, bf16[27,32,512]{2,1,0:T(8,128)(2,1)S(1)} %copy-done.2, bf16[27,32,512]{2,1,0:T(8,128)(2,1)S(1)} %collective-permute-done.8.above, ...), custom_call_target="tpu_custom_call" | custom-call | flops 10192158720 | bytes 10000000 | tf_op jit(solution)/shard_map/pallas_call | solution.py:266
  80.0 3.8 %collective-permute-done.17.refs_6_ = bf16[2,18,16,512]{3,2,1,0:T(8,128)(2,1)S(1)} collective-permute-done((bf16[2,18,16,512]{3,2,1,0:T(8,128)(2,1)S(1)}, bf16[2,18,16,512]{3,2,1,0:T(8,128)(2,1)S(1)}, u32[]{:S(2)}, u32[]{:S(2)}) %collective-permute-start.17) | collective-permute-done | bytes 589856 | tf_op jit(solution)/shard_map/ppermute | solution.py:47
  83.8 4.2 %collective-permute-done.19.near = f32[2,4,8,16,512]{4,3,2,1,0:T(8,128)S(1)} collective-permute-done((f32[2,4,8,16,512]{4,3,2,1,0:T(8,128)S(1)}, f32[2,4,8,16,512]{4,3,2,1,0:T(8,128)S(1)}, u32[]{:S(2)}, u32[]{:S(2)}) %collective-permute-start.19) | collective-permute-done | bytes 2097184 | tf_op jit(solution)/shard_map/ppermute | solution.py:34
  88.5 0.9 collective-permute-start.20
  89.5 2.6 %collective-permute-start.21 = (bf16[18,16,512]{2,1,0:T(8,128)(2,1)S(1)}, bf16[18,16,512]{2,1,0:T(8,128)(2,1)S(1)}, u32[]{:S(2)}, u32[]{:S(2)}) collective-permute-start(bf16[18,16,512]{2,1,0:T(8,128)(2,1)S(1)} %fusion.5), channel_id=1, source_target_pairs={{0,96},{16,112},{32,0},{48,16},{64,32},{80,48},{96,64},{112,80},{1... | collective-permute-start | bytes 884744 | tf_op jit(solution)/shard_map/ppermute | solution.py:47
  92.1 6.9 %collective-permute-done.20.refs_8_ = bf16[18,16,512]{2,1,0:T(8,128)(2,1)S(1)} collective-permute-done((bf16[18,16,512]{2,1,0:T(8,128)(2,1)S(1)}, bf16[18,16,512]{2,1,0:T(8,128)(2,1)S(1)}, u32[]{:S(2)}, u32[]{:S(2)}) %collective-permute-start.20) | collective-permute-done | bytes 294944 | tf_op jit(solution)/shard_map/ppermute | solution.py:47
  98.9 0.5 shard_map.55
  99.5 3.2 %collective-permute-start.23 = (bf16[27,8,512]{2,1,0:T(8,128)(2,1)S(1)}, bf16[27,8,512]{2,1,0:T(8,128)(2,1)S(1)}, u32[]{:S(2)}, u32[]{:S(2)}) collective-permute-start(bf16[27,8,512]{2,1,0:T(8,128)(2,1)S(1)} %get-tuple-element.134), channel_id=1, source_target_pairs={{0,8},{1,9},{2,10},{3,11},{4,12},{5,13},{6,14},{7,15},{8,0},{9,1},... | collective-permute-start | bytes 663560 | tf_op jit(solution)/shard_map/ppermute | solution.py:42
  102.7 0.9 collective-permute-start.24
  103.7 5.4 %collective-permute-done.22 = bf16[27,8,512]{2,1,0:T(8,128)(2,1)S(1)} collective-permute-done((bf16[27,8,512]{2,1,0:T(8,128)(2,1)S(1)}, bf16[27,8,512]{2,1,0:T(8,128)(2,1)S(1)}, u32[]{:S(2)}, u32[]{:S(2)}) %collective-permute-start.22) | collective-permute-done | bytes 221216 | tf_op jit(solution)/shard_map/ppermute | solution.py:42
  109.0 3.1 %collective-permute-done.23 = bf16[27,8,512]{2,1,0:T(8,128)(2,1)S(1)} collective-permute-done((bf16[27,8,512]{2,1,0:T(8,128)(2,1)S(1)}, bf16[27,8,512]{2,1,0:T(8,128)(2,1)S(1)}, u32[]{:S(2)}, u32[]{:S(2)}) %collective-permute-start.23) | collective-permute-done | bytes 221216 | tf_op jit(solution)/shard_map/ppermute | solution.py:42
  112.1 0.6 collective-permute-done.24
  112.7 0.7 collective-permute-done.25.far
  113.5 4.4 %collective-permute-start.26 = (bf16[27,8,512]{2,1,0:T(8,128)(2,1)S(1)}, bf16[27,8,512]{2,1,0:T(8,128)(2,1)S(1)}, u32[]{:S(2)}, u32[]{:S(2)}) collective-permute-start(bf16[27,8,512]{2,1,0:T(8,128)(2,1)S(1)} %fusion.9), channel_id=1, source_target_pairs={{0,16},{16,0},{32,48},{48,32},{64,80},{80,64},{96,112},{112,96},{1... | collective-permute-start | bytes 663560 | tf_op jit(solution)/shard_map/ppermute | solution.py:419
  117.9 4.9 %collective-permute-done.26 = bf16[27,8,512]{2,1,0:T(8,128)(2,1)S(1)} collective-permute-done((bf16[27,8,512]{2,1,0:T(8,128)(2,1)S(1)}, bf16[27,8,512]{2,1,0:T(8,128)(2,1)S(1)}, u32[]{:S(2)}, u32[]{:S(2)}) %collective-permute-start.26) | collective-permute-done | bytes 221216 | tf_op jit(solution)/shard_map/ppermute | solution.py:419
  123.0 3.2 %collective-permute-start.28 = (f32[27,8,512]{2,1,0:T(8,128)S(1)}, f32[27,8,512]{2,1,0:T(8,128)S(1)}, u32[]{:S(2)}, u32[]{:S(2)}) collective-permute-start(f32[27,8,512]{2,1,0:T(8,128)S(1)} %convert_add_fusion.2.own), channel_id=1, source_target_pairs={{0,96},{16,112},{32,0},{48,16},{64,32},{80,48},{96,64},{112,80},{1... | collective-permute-start | bytes 1327112 | tf_op jit(solution)/shard_map/ppermute | solution.py:47
  126.2 8.3 %collective-permute-done.28.above = f32[27,8,512]{2,1,0:T(8,128)S(1)} collective-permute-done((f32[27,8,512]{2,1,0:T(8,128)S(1)}, f32[27,8,512]{2,1,0:T(8,128)S(1)}, u32[]{:S(2)}, u32[]{:S(2)}) %collective-permute-start.28) | collective-permute-done | bytes 442400 | tf_op jit(solution)/shard_map/ppermute | solution.py:47
  134.5 3.8 %collective-permute-start.30 = (f32[14,8,512]{2,1,0:T(8,128)S(1)}, f32[14,8,512]{2,1,0:T(8,128)S(1)}, u32[]{:S(2)}, u32[]{:S(2)}) collective-permute-start(f32[14,8,512]{2,1,0:T(8,128)S(1)} %slice.62), channel_id=1, source_target_pairs={{0,96},{16,112},{32,0},{48,16},{64,32},{80,48},{96,64},{112,80},{1... | collective-permute-start | bytes 688136 | tf_op jit(solution)/shard_map/ppermute | solution.py:47
  138.4 1.2 shard_map.56
  139.6 5.8 %collective-permute-done.29.low = f32[13,8,512]{2,1,0:T(8,128)S(1)} collective-permute-done((f32[13,8,512]{2,1,0:T(8,128)S(1)}, f32[13,8,512]{2,1,0:T(8,128)S(1)}, u32[]{:S(2)}, u32[]{:S(2)}) %collective-permute-start.29) | collective-permute-done | bytes 213024 | tf_op jit(solution)/shard_map/ppermute | solution.py:47
  145.4 1.3 shard_map.57
  (44 shorter events, 1.6 us)
Async XLA Ops:
  0.6 31.7 %copy-start.1 = (bf16[4,8,16,512]{3,2,1,0:T(8,128)(2,1)S(1)}, bf16[4,8,16,512]{3,2,1,0:T(8,128)(2,1)}, u32[]{:S(2)}) copy-start(bf16[4,8,16,512]{3,2,1,0:T(8,128)(2,1)} %cot.1) | copy-start | bytes 1572868
  2.1 31.3 %collective-permute-start.3 = (bf16[4,8,16,512]{3,2,1,0:T(8,128)(2,1)S(1)}, bf16[4,8,16,512]{3,2,1,0:T(8,128)(2,1)S(1)}, u32[]{:S(2)}, u32[]{:S(2)}) collective-permute-start(bf16[4,8,16,512]{3,2,1,0:T(8,128)(2,1)S(1)} %fusion.3.own_act), channel_id=1, source_target_pairs={{0,1},{1,0},{2,3},{3,2},{4,5},{5,4},{6,7},{7,6},{8,9},{9,8},{10,11... | collective-permute-start | bytes 1572872 | tf_op jit(solution)/shard_map/ppermute | solution.py:34
  2.2 31.3 %collective-permute-start.4 = (bf16[4,8,16,512]{3,2,1,0:T(8,128)(2,1)S(1)}, bf16[4,8,16,512]{3,2,1,0:T(8,128)(2,1)S(1)}, u32[]{:S(2)}, u32[]{:S(2)}) collective-permute-start(bf16[4,8,16,512]{3,2,1,0:T(8,128)(2,1)S(1)} %fusion.3.own_act), channel_id=1, source_target_pairs={{0,2},{1,3},{2,0},{3,1},{4,6},{5,7},{6,4},{7,5},{8,10},{9,11},{10,... | collective-permute-start | bytes 1572872 | tf_op jit(solution)/shard_map/ppermute | solution.py:34
  5.2 1.6 %collective-permute-start = (bf16[8,16,512]{2,1,0:T(8,128)(2,1)S(1)}, bf16[8,16,512]{2,1,0:T(8,128)(2,1)S(1)}, u32[]{:S(2)}, u32[]{:S(2)}) collective-permute-start(bf16[8,16,512]{2,1,0:T(8,128)(2,1)S(1)} %select_bitcast_fusion), channel_id=1, source_target_pairs={{3,4},{7,8},{11,12},{4,3},{8,7},{12,11},{19,20},{23,24},{27,28},{2... | collective-permute-start | bytes 393224 | tf_op jit(solution)/shard_map/ppermute | solution.py:381
  6.8 39.6 %collective-permute-start.8 = (bf16[27,32,512]{2,1,0:T(8,128)(2,1)}, bf16[27,32,512]{2,1,0:T(8,128)(2,1)S(1)}, u32[]{:S(2)}, u32[]{:S(2)}) collective-permute-start(bf16[27,32,512]{2,1,0:T(8,128)(2,1)} %own), channel_id=1, source_target_pairs={{0,12},{1,13},{2,14},{3,15},{4,0},{5,1},{6,2},{7,3},{8,4},{9,5},{1... | collective-permute-start | bytes 2654216 | tf_op jit(solution)/shard_map/ppermute | solution.py:42
  16.8 29.6 %collective-permute-start.9 = (bf16[27,32,512]{2,1,0:T(8,128)(2,1)}, bf16[27,32,512]{2,1,0:T(8,128)(2,1)S(1)}, u32[]{:S(2)}, u32[]{:S(2)}) collective-permute-start(bf16[27,32,512]{2,1,0:T(8,128)(2,1)} %own), channel_id=1, source_target_pairs={{0,4},{1,5},{2,6},{3,7},{4,8},{5,9},{6,10},{7,11},{8,12},{9,13},{1... | collective-permute-start | bytes 2654216 | tf_op jit(solution)/shard_map/ppermute | solution.py:42
  16.9 7.3 %collective-permute-start.1 = (bf16[5,16,512]{2,1,0:T(8,128)(2,1)S(1)}, bf16[5,16,512]{2,1,0:T(8,128)(2,1)S(1)}, u32[]{:S(2)}, u32[]{:S(2)}) collective-permute-start(bf16[5,16,512]{2,1,0:T(8,128)(2,1)S(1)} %get-tuple-element.73), channel_id=1, source_target_pairs={{0,16},{16,32},{32,48},{48,64},{64,80},{80,96},{96,112},{1,17},{17... | collective-permute-start | bytes 245768 | tf_op jit(solution)/shard_map/ppermute | solution.py:52
  24.2 8.2 %collective-permute-start.2 = (bf16[5,16,512]{2,1,0:T(8,128)(2,1)S(1)}, bf16[5,16,512]{2,1,0:T(8,128)(2,1)S(1)}, u32[]{:S(2)}, u32[]{:S(2)}) collective-permute-start(bf16[5,16,512]{2,1,0:T(8,128)(2,1)S(1)} %get-tuple-element.74), channel_id=1, source_target_pairs={{16,0},{32,16},{48,32},{64,48},{80,64},{96,80},{112,96},{17,1},{33... | collective-permute-start | bytes 245768 | tf_op jit(solution)/shard_map/ppermute | solution.py:53
  33.4 17.4 %collective-permute-start.10 = (bf16[4,8,16,512]{3,2,1,0:T(8,128)(2,1)S(1)}, bf16[4,8,16,512]{3,2,1,0:T(8,128)(2,1)S(1)}, u32[]{:S(2)}, u32[]{:S(2)}) collective-permute-start(bf16[4,8,16,512]{3,2,1,0:T(8,128)(2,1)S(1)} %collective-permute-done.4.far), channel_id=1, source_target_pairs={{0,1},{1,0},{2,3},{3,2},{4,5},{5,4},{6,7},{7,6},{8,9},{9,8},{10,11... | collective-permute-start | bytes 1572872 | tf_op jit(solution)/shard_map/ppermute | solution.py:34
  33.5 2.2 %collective-permute-start.5 = (bf16[5,10,16,128]{3,2,1,0:T(8,128)(2,1)S(1)}, bf16[5,10,16,128]{3,2,1,0:T(8,128)(2,1)S(1)}, u32[]{:S(2)}, u32[]{:S(2)}) collective-permute-start(bf16[5,10,16,128]{3,2,1,0:T(8,128)(2,1)S(1)} %get-tuple-element.80), channel_id=1, source_target_pairs={{0,1},{1,0},{2,3},{3,2},{4,5},{5,4},{6,7},{7,6},{8,9},{9,8},{10,11... | collective-permute-start | bytes 614408 | tf_op jit(solution)/shard_map/ppermute | solution.py:34
  34.0 7.9 %collective-permute-start.6 = (bf16[5,10,16,128]{3,2,1,0:T(8,128)(2,1)S(1)}, bf16[5,10,16,128]{3,2,1,0:T(8,128)(2,1)S(1)}, u32[]{:S(2)}, u32[]{:S(2)}) collective-permute-start(bf16[5,10,16,128]{3,2,1,0:T(8,128)(2,1)S(1)} %get-tuple-element.81), channel_id=1, source_target_pairs={{0,2},{1,3},{2,0},{3,1},{4,6},{5,7},{6,4},{7,5},{8,10},{9,11},{10,... | collective-permute-start | bytes 614408 | tf_op jit(solution)/shard_map/ppermute | solution.py:34
  35.7 8.9 %collective-permute-start.7 = (bf16[5,10,16,128]{3,2,1,0:T(8,128)(2,1)S(1)}, bf16[5,10,16,128]{3,2,1,0:T(8,128)(2,1)S(1)}, u32[]{:S(2)}, u32[]{:S(2)}) collective-permute-start(bf16[5,10,16,128]{3,2,1,0:T(8,128)(2,1)S(1)} %get-tuple-element.82), channel_id=1, source_target_pairs={{0,3},{1,2},{2,1},{3,0},{4,7},{5,6},{6,5},{7,4},{8,11},{9,10},{10,... | collective-permute-start | bytes 614408 | tf_op jit(solution)/shard_map/ppermute | solution.py:34
  46.5 21.8 %collective-permute-start.13 = (bf16[13,32,512]{2,1,0:T(8,128)(2,1)S(1)}, bf16[13,32,512]{2,1,0:T(8,128)(2,1)S(1)}, u32[]{:S(2)}, u32[]{:S(2)}) collective-permute-start(bf16[13,32,512]{2,1,0:T(8,128)(2,1)S(1)} %slice.51), channel_id=1, source_target_pairs={{0,4},{1,5},{2,6},{3,7},{4,8},{5,9},{6,10},{7,11},{8,12},{9,13},{1... | collective-permute-start | bytes 1277960 | tf_op jit(solution)/shard_map/ppermute | solution.py:42
  47.0 24.3 %collective-permute-start.14 = (bf16[14,32,512]{2,1,0:T(8,128)(2,1)S(1)}, bf16[14,32,512]{2,1,0:T(8,128)(2,1)S(1)}, u32[]{:S(2)}, u32[]{:S(2)}) collective-permute-start(bf16[14,32,512]{2,1,0:T(8,128)(2,1)S(1)} %slice.52), channel_id=1, source_target_pairs={{0,12},{1,13},{2,14},{3,15},{4,0},{5,1},{6,2},{7,3},{8,4},{9,5},{1... | collective-permute-start | bytes 1376264 | tf_op jit(solution)/shard_map/ppermute | solution.py:42
  53.6 17.7 %copy-start.2 = (bf16[27,32,512]{2,1,0:T(8,128)(2,1)S(1)}, bf16[27,32,512]{2,1,0:T(8,128)(2,1)}, u32[]{:S(2)}) copy-start(bf16[27,32,512]{2,1,0:T(8,128)(2,1)} %own) | copy-start | bytes 2654212
  53.6 10.6 %collective-permute-start.11 = (bf16[2,9,16,512]{3,2,1,0:T(8,128)(2,1)S(1)}, bf16[2,9,16,512]{3,2,1,0:T(8,128)(2,1)S(1)}, u32[]{:S(2)}, u32[]{:S(2)}) collective-permute-start(bf16[2,9,16,512]{3,2,1,0:T(8,128)(2,1)S(1)} %get-tuple-element.94), channel_id=1, source_target_pairs={{0,32},{16,48},{32,64},{48,80},{64,96},{80,112},{96,0},{112,16},{1... | collective-permute-start | bytes 884744 | tf_op jit(solution)/shard_map/ppermute | solution.py:47
  55.4 9.0 %collective-permute-start.12 = (bf16[2,9,16,512]{3,2,1,0:T(8,128)(2,1)S(1)}, bf16[2,9,16,512]{3,2,1,0:T(8,128)(2,1)S(1)}, u32[]{:S(2)}, u32[]{:S(2)}) collective-permute-start(bf16[2,9,16,512]{3,2,1,0:T(8,128)(2,1)S(1)} %get-tuple-element.95), channel_id=1, source_target_pairs={{0,96},{16,112},{32,0},{48,16},{64,32},{80,48},{96,64},{112,80},{1... | collective-permute-start | bytes 884744 | tf_op jit(solution)/shard_map/ppermute | solution.py:47
  64.4 15.5 %collective-permute-start.15 = (bf16[9,16,512]{2,1,0:T(8,128)(2,1)S(1)}, bf16[9,16,512]{2,1,0:T(8,128)(2,1)S(1)}, u32[]{:S(2)}, u32[]{:S(2)}) collective-permute-start(bf16[9,16,512]{2,1,0:T(8,128)(2,1)S(1)} %fusion.8), channel_id=1, source_target_pairs={{0,32},{16,48},{32,64},{48,80},{64,96},{80,112},{96,0},{112,16},{1... | collective-permute-start | bytes 442376 | tf_op jit(solution)/shard_map/ppermute | solution.py:47
  66.2 13.8 %collective-permute-start.16 = (bf16[9,16,512]{2,1,0:T(8,128)(2,1)S(1)}, bf16[9,16,512]{2,1,0:T(8,128)(2,1)S(1)}, u32[]{:S(2)}, u32[]{:S(2)}) collective-permute-start(bf16[9,16,512]{2,1,0:T(8,128)(2,1)S(1)} %fusion.7), channel_id=1, source_target_pairs={{0,96},{16,112},{32,0},{48,16},{64,32},{80,48},{96,64},{112,80},{1... | collective-permute-start | bytes 442376 | tf_op jit(solution)/shard_map/ppermute | solution.py:47
  68.0 15.8 %collective-permute-start.17 = (bf16[2,18,16,512]{3,2,1,0:T(8,128)(2,1)S(1)}, bf16[2,18,16,512]{3,2,1,0:T(8,128)(2,1)S(1)}, u32[]{:S(2)}, u32[]{:S(2)}) collective-permute-start(bf16[2,18,16,512]{3,2,1,0:T(8,128)(2,1)S(1)} %get-tuple-element.116), channel_id=1, source_target_pairs={{0,32},{16,48},{32,64},{48,80},{64,96},{80,112},{96,0},{112,16},{1... | collective-permute-start | bytes 1769480 | tf_op jit(solution)/shard_map/ppermute | solution.py:47
  68.3 15.5 %collective-permute-start.18 = (bf16[2,18,16,512]{3,2,1,0:T(8,128)(2,1)S(1)}, bf16[2,18,16,512]{3,2,1,0:T(8,128)(2,1)S(1)}, u32[]{:S(2)}, u32[]{:S(2)}) collective-permute-start(bf16[2,18,16,512]{3,2,1,0:T(8,128)(2,1)S(1)} %get-tuple-element.117), channel_id=1, source_target_pairs={{0,96},{16,112},{32,0},{48,16},{64,32},{80,48},{96,64},{112,80},{1... | collective-permute-start | bytes 1769480 | tf_op jit(solution)/shard_map/ppermute | solution.py:47
  83.8 4.2 %collective-permute-start.19 = (f32[2,4,8,16,512]{4,3,2,1,0:T(8,128)S(1)}, f32[2,4,8,16,512]{4,3,2,1,0:T(8,128)S(1)}, u32[]{:S(2)}, u32[]{:S(2)}) collective-permute-start(f32[2,4,8,16,512]{4,3,2,1,0:T(8,128)S(1)} %get-tuple-element.122), channel_id=1, source_target_pairs={{0,1},{1,0},{2,3},{3,2},{4,5},{5,4},{6,7},{7,6},{8,9},{9,8},{10,11... | collective-permute-start | bytes 6291464 | tf_op jit(solution)/shard_map/ppermute | solution.py:34
  88.1 25.3 %collective-permute-start.25 = (f32[4,8,16,512]{3,2,1,0:T(8,128)S(1)}, f32[4,8,16,512]{3,2,1,0:T(8,128)S(1)}, u32[]{:S(2)}, u32[]{:S(2)}) collective-permute-start(f32[4,8,16,512]{3,2,1,0:T(8,128)S(1)} %fusion.4), channel_id=1, source_target_pairs={{0,2},{1,3},{2,0},{3,1},{4,6},{5,7},{6,4},{7,5},{8,10},{9,11},{10,... | collective-permute-start | bytes 3145736 | tf_op jit(solution)/shard_map/ppermute | solution.py:34
  88.5 10.4 %collective-permute-start.20 = (bf16[18,16,512]{2,1,0:T(8,128)(2,1)S(1)}, bf16[18,16,512]{2,1,0:T(8,128)(2,1)S(1)}, u32[]{:S(2)}, u32[]{:S(2)}) collective-permute-start(bf16[18,16,512]{2,1,0:T(8,128)(2,1)S(1)} %fusion.6), channel_id=1, source_target_pairs={{0,32},{16,48},{32,64},{48,80},{64,96},{80,112},{96,0},{112,16},{1... | collective-permute-start | bytes 884744 | tf_op jit(solution)/shard_map/ppermute | solution.py:47
  89.5 9.5 %collective-permute-start.21 = (bf16[18,16,512]{2,1,0:T(8,128)(2,1)S(1)}, bf16[18,16,512]{2,1,0:T(8,128)(2,1)S(1)}, u32[]{:S(2)}, u32[]{:S(2)}) collective-permute-start(bf16[18,16,512]{2,1,0:T(8,128)(2,1)S(1)} %fusion.5), channel_id=1, source_target_pairs={{0,96},{16,112},{32,0},{48,16},{64,32},{80,48},{96,64},{112,80},{1... | collective-permute-start | bytes 884744 | tf_op jit(solution)/shard_map/ppermute | solution.py:47
  99.4 38.9 %copy-start = (bf16[4,8,16,512]{3,2,1,0:T(8,128)(2,1)S(1)}, bf16[4,8,16,512]{3,2,1,0:T(8,128)(2,1)}, u32[]{:S(2)}) copy-start(bf16[4,8,16,512]{3,2,1,0:T(8,128)(2,1)} %pre.1) | copy-start | bytes 1572868
  99.4 9.6 %collective-permute-start.22 = (bf16[27,8,512]{2,1,0:T(8,128)(2,1)S(1)}, bf16[27,8,512]{2,1,0:T(8,128)(2,1)S(1)}, u32[]{:S(2)}, u32[]{:S(2)}) collective-permute-start(bf16[27,8,512]{2,1,0:T(8,128)(2,1)S(1)} %get-tuple-element.133), channel_id=1, source_target_pairs={{0,4},{1,5},{2,6},{3,7},{4,8},{5,9},{6,10},{7,11},{8,12},{9,13},{1... | collective-permute-start | bytes 663560 | tf_op jit(solution)/shard_map/ppermute | solution.py:42
  99.5 12.6 %collective-permute-start.23 = (bf16[27,8,512]{2,1,0:T(8,128)(2,1)S(1)}, bf16[27,8,512]{2,1,0:T(8,128)(2,1)S(1)}, u32[]{:S(2)}, u32[]{:S(2)}) collective-permute-start(bf16[27,8,512]{2,1,0:T(8,128)(2,1)S(1)} %get-tuple-element.134), channel_id=1, source_target_pairs={{0,8},{1,9},{2,10},{3,11},{4,12},{5,13},{6,14},{7,15},{8,0},{9,1},... | collective-permute-start | bytes 663560 | tf_op jit(solution)/shard_map/ppermute | solution.py:42
  102.7 10.0 %collective-permute-start.24 = (bf16[27,8,512]{2,1,0:T(8,128)(2,1)S(1)}, bf16[27,8,512]{2,1,0:T(8,128)(2,1)S(1)}, u32[]{:S(2)}, u32[]{:S(2)}) collective-permute-start(bf16[27,8,512]{2,1,0:T(8,128)(2,1)S(1)} %get-tuple-element.135), channel_id=1, source_target_pairs={{0,12},{1,13},{2,14},{3,15},{4,0},{5,1},{6,2},{7,3},{8,4},{9,5},{1... | collective-permute-start | bytes 663560 | tf_op jit(solution)/shard_map/ppermute | solution.py:42
  113.5 9.3 %collective-permute-start.26 = (bf16[27,8,512]{2,1,0:T(8,128)(2,1)S(1)}, bf16[27,8,512]{2,1,0:T(8,128)(2,1)S(1)}, u32[]{:S(2)}, u32[]{:S(2)}) collective-permute-start(bf16[27,8,512]{2,1,0:T(8,128)(2,1)S(1)} %fusion.9), channel_id=1, source_target_pairs={{0,16},{16,0},{32,48},{48,32},{64,80},{80,64},{96,112},{112,96},{1... | collective-permute-start | bytes 663560 | tf_op jit(solution)/shard_map/ppermute | solution.py:419
  123.0 11.5 %collective-permute-start.28 = (f32[27,8,512]{2,1,0:T(8,128)S(1)}, f32[27,8,512]{2,1,0:T(8,128)S(1)}, u32[]{:S(2)}, u32[]{:S(2)}) collective-permute-start(f32[27,8,512]{2,1,0:T(8,128)S(1)} %convert_add_fusion.2.own), channel_id=1, source_target_pairs={{0,96},{16,112},{32,0},{48,16},{64,32},{80,48},{96,64},{112,80},{1... | collective-permute-start | bytes 1327112 | tf_op jit(solution)/shard_map/ppermute | solution.py:47
  126.2 12.1 %collective-permute-start.27 = (f32[27,8,512]{2,1,0:T(8,128)S(1)}, f32[27,8,512]{2,1,0:T(8,128)S(1)}, u32[]{:S(2)}, u32[]{:S(2)}) collective-permute-start(f32[27,8,512]{2,1,0:T(8,128)S(1)} %convert_add_fusion.2.own), channel_id=1, source_target_pairs={{0,32},{16,48},{32,64},{48,80},{64,96},{80,112},{96,0},{112,16},{1... | collective-permute-start | bytes 1327112 | tf_op jit(solution)/shard_map/ppermute | solution.py:47
  134.5 10.9 %collective-permute-start.30 = (f32[14,8,512]{2,1,0:T(8,128)S(1)}, f32[14,8,512]{2,1,0:T(8,128)S(1)}, u32[]{:S(2)}, u32[]{:S(2)}) collective-permute-start(f32[14,8,512]{2,1,0:T(8,128)S(1)} %slice.62), channel_id=1, source_target_pairs={{0,96},{16,112},{32,0},{48,16},{64,32},{80,48},{96,64},{112,80},{1... | collective-permute-start | bytes 688136 | tf_op jit(solution)/shard_map/ppermute | solution.py:47
  138.3 7.1 %collective-permute-start.29 = (f32[13,8,512]{2,1,0:T(8,128)S(1)}, f32[13,8,512]{2,1,0:T(8,128)S(1)}, u32[]{:S(2)}, u32[]{:S(2)}) collective-permute-start(f32[13,8,512]{2,1,0:T(8,128)S(1)} %slice.61), channel_id=1, source_target_pairs={{0,32},{16,48},{32,64},{48,80},{64,96},{80,112},{96,0},{112,16},{1... | collective-permute-start | bytes 638984 | tf_op jit(solution)/shard_map/ppermute | solution.py:47

commit v5 on v4

--- a/solution.py
+++ b/solution.py
@@ -47,41 +47,83 @@
     return lax.ppermute(block, "gx", [(g, (g + 2 * step) % count) for g in range(count)])
 
 
-def rims_x(first, last):
+def swap_x(block, first):
     count = lax.axis_size("gx")
-    low = lax.ppermute(last, "gx", [(g, g + 1) for g in range(count - 1)])
-    high = lax.ppermute(first, "gx", [(g + 1, g) for g in range(count - 1)])
-    return low, high
+    pairs = [(g, g + 1) for g in range(first, count - 1, 2)]
+    return lax.ppermute(block, "gx", pairs + [(t, s) for s, t in pairs])
 
 
 def zero_at(value, z, edge):
     return jnp.where(z == edge, 0.0, value)
 
 
-def pick_kernel(cot, extra, low, high, *quarters):
+def start_kernel(pre, cot, act, edge):
+    value = pre[...].astype(F32)
+    act[...] = (value * jax.nn.sigmoid(value)).astype(BF16)
+    edge[...] = jnp.where(quad_place() == 0, cot[0], cot[cot.shape[0] - 1])
+
+
+def start(pre_act, cot):
+    return pl.pallas_call(
+        start_kernel,
+        out_shape=[
+            jax.ShapeDtypeStruct(pre_act.shape, BF16),
+            jax.ShapeDtypeStruct(cot.shape[1:], BF16),
+        ],
+        in_specs=[VMEM] * 2,
+        out_specs=[VMEM] * 2,
+        compiler_params=params(),
+    )(pre_act, cot)
+
+
+def side_kernel(cot, extra, even, odd):
+    rows, width = cot.shape[:2]
+    is_odd = lax.rem(lax.axis_index("gx"), 2) == 1
+
+    def put(out, upper):
+        out[0:rows] = jnp.where(upper, cot[:, width - 1], cot[:, 0])
+        out[rows] = jnp.where(upper, extra[width - 1], extra[0])
+
+    put(even, jnp.logical_not(is_odd))
+    put(odd, is_odd)
+
+
+def sides(cot, extra):
+    rows, width, depth, chan = cot.shape
+    return pl.pallas_call(
+        side_kernel,
+        out_shape=[jax.ShapeDtypeStruct((rows + 1, depth, chan), BF16)] * 2,
+        in_specs=[VMEM] * 2,
+        out_specs=[VMEM] * 2,
+        compiler_params=params(),
+    )(cot, extra)
+
+
+def pick_kernel(cot, extra, even, odd, *quarters):
     rows, width, depth, chan = cot.shape
     j = quad_place()
+    is_odd = lax.rem(lax.axis_index("gx"), 2) == 1
     q = chan // QUAD
     part = q // RING
     source = lax.broadcasted_iota(jnp.int32, (chan, q), 0)
     place = lax.broadcasted_iota(jnp.int32, (chan, q), 1)
     base = lax.div(place, part) * q + lax.rem(place, part)
+    low = jnp.where(is_odd, even[...], odd[...])
+    high = jnp.where(is_odd, odd[...], even[...])
 
     def take(block, pick):
-        shape = block.shape
-        flat = block[...].reshape(-1, chan)
-        got = jnp.dot(flat, pick, preferred_element_type=F32)
-        return got.astype(BF16).reshape(shape[:-1] + (q,))
+        got = jnp.dot(block.reshape(-1, chan), pick, preferred_element_type=F32)
+        return got.astype(BF16).reshape(block.shape[:-1] + (q,))
 
     for k, out in enumerate(quarters):
         pick = jnp.where(source == base + (j ^ k) * part, 1.0, 0.0).astype(BF16)
-        out[0:rows, 1:width + 1] = take(cot, pick)
-        out[rows, 1:width + 1] = take(extra, pick)
+        out[0:rows, 1:width + 1] = take(cot[...], pick)
+        out[rows, 1:width + 1] = take(extra[...], pick)
         out[:, 0] = take(low, pick)
         out[:, width + 1] = take(high, pick)
 
 
-def pick_channels(cot, extra, low, high):
+def pick_channels(cot, *rims):
     rows, width, depth, chan = cot.shape
     quarter = jax.ShapeDtypeStruct((rows + 1, width + 2, depth, chan // QUAD), BF16)
     return pl.pallas_call(
@@ -90,7 +132,7 @@
         in_specs=[VMEM] * 4,
         out_specs=[VMEM] * QUAD,
         compiler_params=params(),
-    )(cot, extra, low, high)
+    )(cot, *rims)
 
 
 def turn_kernel(p0, p1, p2, p3, held, out):
@@ -152,7 +194,7 @@
     return copies
 
 
-def weight_kernel(offsets, norm, own_act, near, far, across, cot, *refs):
+def weight_kernel(norm, own_act, near, far, across, cot, *refs):
     right, left, keep_right, keep_left, own, held, sem = refs
     j = quad_place()
     rows, width, depth, chan = own_act.shape
@@ -167,8 +209,8 @@
     q = cot.shape[0] // 9
     part = q // RING
     half = part // 2
-    for n in range(3 * len(offsets)):
-        a, b = offsets[n // 3], n % 3
+    for n in range(9):
+        a, b = n // 3 - 1, n % 3
         moved = cot[3 * b * q:3 * (b + 1) * q, (1 - a) * row:(1 - a) * row + cells]
         term = jnp.dot(moved, act, preferred_element_type=F32) * norm
         for c in range(3):
@@ -188,22 +230,16 @@
             own[1, tap] = block(0, 1)
 
 
-def weight_terms(offsets, norm, acts, cot):
+def weight_terms(norm, acts, cot):
     rows, width, depth, chan = acts[0].shape
-    taps = 9 * len(offsets)
     q = chan // QUAD
-    half = q // RING // 2
-    held_cells = QUAD * rows * width * depth
-    shapes = [
-        jax.ShapeDtypeStruct((2, taps, half, chan), BF16),
-        jax.ShapeDtypeStruct((2, taps, half, chan), BF16),
-        jax.ShapeDtypeStruct((taps, half, chan), F32),
-        jax.ShapeDtypeStruct((taps, half, chan), F32),
-        jax.ShapeDtypeStruct((2, taps, half, chan), F32),
-    ]
-    return pl.pallas_call(
-        functools.partial(weight_kernel, offsets, norm),
-        out_shape=shapes,
+    shape = (27, q // RING // 2, chan)
+    cells = QUAD * rows * width * depth
+    return pl.pallas_call(
+        functools.partial(weight_kernel, norm),
+        out_shape=[jax.ShapeDtypeStruct((2,) + shape, BF16)] * 2
+        + [jax.ShapeDtypeStruct(shape, F32)] * 2
+        + [jax.ShapeDtypeStruct((2,) + shape, F32)],
         in_specs=[ANY] * 4 + [VMEM],
         out_specs=[VMEM] * 5,
         scratch_shapes=[
@@ -212,7 +248,7 @@
         ],
         compiler_params=params(),
         cost_estimate=pl.CostEstimate(
-            flops=2 * taps * q * held_cells * chan, bytes_accessed=10_000_000, transcendentals=0
+            flops=2 * 27 * q * cells * chan, bytes_accessed=10_000_000, transcendentals=0
         ),
     )(*acts, cot)
 
@@ -297,76 +333,56 @@
     )(pre_act, keep, near, far)
 
 
-def split_kernel(*refs):
-    parts, outs, total = refs[:10], refs[10:14], refs[14]
+def split_kernel(own, from_left, from_right, last_left, last_right, *refs):
+    outs, total = refs[:-1], refs[-1]
     y = lax.div(lax.axis_index("gy"), QUAD)
-    taps = 0
-    for own, from_left, from_right, last_left, last_right in (parts[:5], parts[5:]):
-        count, rows = own.shape[1:3]
-        low = own[0] + from_right[1].astype(F32) + last_left[...].astype(F32)
-        high = own[1] + from_left[1].astype(F32) + last_right[...].astype(F32)
-        at = slice(taps, taps + count)
-        for half, value in enumerate((low, high)):
-            for sub in range(2):
-                total[2 * half + sub, at] = value[:, sub * (rows // 2):(sub + 1) * (rows // 2)]
-        taps += count
+    size = own.shape[2] // 2
+    low = own[0] + from_right[1].astype(F32) + last_left[...].astype(F32)
+    high = own[1] + from_left[1].astype(F32) + last_right[...].astype(F32)
+    for half, value in enumerate((low, high)):
+        for sub in range(2):
+            total[2 * half + sub] = value[:, sub * size:(sub + 1) * size]
     for r, out in enumerate(outs):
         out[...] = total[lax.rem(y + r, RING)].astype(out.dtype)
 
 
-def split(first, second):
-    _, count, rows, chan = first[0].shape
-    shape = (3 * count, rows // 2, chan)
+def split(*parts):
+    _, taps, rows, chan = parts[0].shape
+    shape = (taps, rows // 2, chan)
     return pl.pallas_call(
         split_kernel,
         out_shape=[jax.ShapeDtypeStruct(shape, F32)] + [jax.ShapeDtypeStruct(shape, BF16)] * 3,
-        in_specs=[VMEM] * 10,
+        in_specs=[VMEM] * 5,
         out_specs=[VMEM] * 4,
         scratch_shapes=[pltpu.VMEM((RING,) + shape, F32)],
         compiler_params=params(),
-    )(*first, *second)
-
-
-def join_kernel(own, below, above, low, high, out):
+    )(*parts)
+
+
+def join_kernel(*refs):
+    out = refs[-1]
     x = x_place()
-    size = own.shape[1]
-
-    def put(first, piece, k):
+    size = refs[0].shape[1]
+    low = refs[0].shape[0]
+    for piece, part, k in zip(refs, (0, 1) * RING, (0, 0, 3, 3, 1, 1, 2, 2)):
         at = pl.ds(pl.multiple_of(lax.rem(x + k, RING) * size, size), size)
+        first = part * low
         out[first:first + piece.shape[0], at] = piece[...]
 
-    put(0, own, 0)
-    put(0, below, 3)
-    put(0, above, 1)
-    put(0, low, 2)
-    put(low.shape[0], high, 2)
-
-
-def join(pieces):
-    taps, size, chan = pieces[0].shape
+
+def gather_x(low, high):
+    low_below, high_above = along_x(low, 1), along_x(high, -1)
+    high_below, low_above = along_x(high, 1), along_x(low, -1)
+    low_far, high_far = along_x(low_below, 1), along_x(high_above, -1)
+    _, size, chan = low.shape
+    pieces = (low, high, low_below, high_below, low_above, high_above, low_far, high_far)
     return pl.pallas_call(
         join_kernel,
-        out_shape=jax.ShapeDtypeStruct((taps, RING * size, chan), F32),
-        in_specs=[VMEM] * 5,
+        out_shape=jax.ShapeDtypeStruct((27, RING * size, chan), F32),
+        in_specs=[VMEM] * 8,
         out_specs=VMEM,
         compiler_params=params(),
     )(*pieces)
-
-
-def reduce_x_first(right, left, *kept):
-    return along_x(right, 1), along_x(left, -1), *kept
-
-
-def reduce_x_last(from_left, from_right, keep_right, keep_left, own):
-    next_right = (from_left[0].astype(F32) + keep_right).astype(BF16)
-    next_left = (from_right[0].astype(F32) + keep_left).astype(BF16)
-    return own, from_left, from_right, along_x(next_right, 1), along_x(next_left, -1)
-
-
-def gather_x(whole):
-    below, above = along_x(whole, 1), along_x(whole, -1)
-    taps = whole.shape[0] // 2
-    return [whole, below, above, along_x(below[:taps], 1), along_x(above[taps:], -1)]
 
 
 def body(pre_act, cot, weight):
@@ -378,46 +394,45 @@
     count = lax.axis_size("gy")
     pairs = [(g, g + 1) for g in range(QUAD - 1, count - 1, QUAD)]
     pairs = pairs + [(t, s) for s, t in pairs]
-    extra = lax.ppermute(jnp.where(j == 0, cot[0], cot[rows - 1]), "gy", pairs)
-    extra, weight = barrier((extra, weight))
-    act = jax.nn.silu(pre_act.astype(F32)).astype(BF16)
+    act, edge = start(pre_act, cot)
+    extra = lax.ppermute(edge, "gy", pairs)
     far = swap(act, 2)
     near = swap(act, 1)
+    extra, near, weight = barrier((extra, near, weight))
     above = along_y(weight, -1, True)
     below = along_y(weight, 1, True)
-    sides = [jnp.concatenate([cot[:, x], extra[x][None]]) for x in (0, width - 1)]
-    sides = barrier(sides)
-    low, high = rims_x(*sides)
-    quarters = pick_channels(cot, extra, low, high)
-    quarters, near, far = barrier((quarters, near, far))
+    even, odd = sides(cot, extra)
+    quarters = pick_channels(cot, extra, swap_x(even, 0), swap_x(odd, 1))
+    quarters, far = barrier((quarters, far))
     quarters = [quarters[0]] + [swap(quarters[k], k) for k in (1, 2, 3)]
+    quarters, far = barrier((quarters, far))
     acts = [act, near, far, swap(far, 1)]
     held, turned = turn(quarters)
 
     turned, above, below = barrier((turned, above, below))
-    first = weight_terms((-1,), norm, acts, turned)
-    turned, first = barrier((turned, first))
     taps = 13
     parts = [weight, above, along_y(below[:taps], 1, True), along_y(above[taps:], -1, True), below]
-    first = reduce_x_first(*first)
-    second = weight_terms((0, 1), norm, acts, turned)
-    held, first, second = barrier((held, first, second))
-    second = reduce_x_first(*second)
-    first = reduce_x_last(*first)
+    right, left, *kept = weight_terms(norm, acts, turned)
+    held, right, left = barrier((held, right, left))
+    from_left, from_right = along_x(right, 1), along_x(left, -1)
     grads = input_terms(held, parts)
-    grads, first, second = barrier((grads, first, second))
-    second = reduce_x_last(*second)
     send, keep, pass_on = grads
     got = swap(send, 1)
-    far_grad = swap(pass_on + got[1], 2)
-    mine, *others = split(first, second)
+    passed, from_left, from_right = barrier((pass_on + got[1], from_left, from_right))
+    far_grad = swap(passed, 2)
+    keep_right, keep_left, own = kept
+    right = (from_left[0].astype(F32) + keep_right).astype(BF16)
+    left = (from_right[0].astype(F32) + keep_left).astype(BF16)
+    mine, *others = split(own, from_left, from_right, along_x(right, 1), along_x(left, -1))
+
     others = [along_y(block, r, True) for r, block in zip((1, 2, 3), others)]
     others, far_grad = barrier((others, far_grad))
     for other in others:
         mine = mine + other.astype(F32)
     count = lax.axis_size("gx")
     other = lax.ppermute(mine.astype(BF16), "gx", [(g, g ^ 1) for g in range(count)])
-    grad_weight = join(gather_x(mine + other.astype(F32)))
+    low, high = [mine[s] + other[s].astype(F32) for s in (slice(0, taps), slice(taps, 27))]
+    grad_weight = gather_x(low, high)
     grad_pre = finish(pre_act, keep, got, far_grad)
     return (grad_pre, grad_weight)
 

time: 147 us -> 147 us (level)
  starting transfers between devices: 53.8 us -> 50.3 us
  waiting for transfers between devices: 65.4 us -> 68.4 us
  other arithmetic: 3.11 us -> 0.69 us
  local copies, waits for them, and re-layouts: 1 us -> 3.19 us
    ppermute x12 -> x10, waiting for transfers between devices: 27 us -> 38 us  [along_x(): lax.ppermute(block, 'gx', [(g, (g + 2 * step) % count) for g in range(cou...]
    ppermute x3, waiting for transfers between devices: 8.95 us -> 2.03 us  [the longest x2 2.02 us: swap_x(): return lax.ppermute(block, 'gx', pairs + [(t, s) for s, t in pairs])]
    ppermute x8, waiting for transfers between devices: 15.4 us -> 9.55 us  [swap(): return lax.ppermute(block, 'gy', [(g, g ^ k) for g in range(count)])]
    ppermute x1, starting transfers between devices: 4.39 us -> 0.09 us  [body(): lax.ppermute(mine.astype(BF16), 'gx', [(g, g ^ 1) for g in range(count)])]
    unnamed x6 -> x10, local copies, waits for them, and re-layouts: 0.02 us -> 3.13 us
    ppermute x1, waiting for transfers between devices: 4.9 us -> 7.42 us  [body(): lax.ppermute(mine.astype(BF16), 'gx', [(g, g ^ 1) for g in range(count)])]
    ppermute x7, waiting for transfers between devices: 9.09 us -> 11.4 us  [along_y(): lax.ppermute(block, 'gy', [(s, t) for s, t in pairs if 0 <= t < count])]
    ppermute x3, starting transfers between devices: 7.21 us -> 4.98 us  [the longest x2 4.32 us: swap_x(): return lax.ppermute(block, 'gx', pairs + [(t, s) for s, t in pairs])]
  transfers between devices with their start and end apart: 31 -> 29, of which waited for: 17 -> 15; matrix products, arithmetic and copies ran while one was open for 2% -> 0% of each run, Pallas kernels for 14% -> 8%
where the time goes in v5:
time: 147 us; the launch traced here: 146 us
  waiting for transfers between devices  68.4 us (47%)
  starting transfers between devices  50.3 us (34%)
  Pallas kernels  22.4 us (15%)
  local copies, waits for them, and re-layouts  3.19 us (2%)
    ppermute x10, waiting for transfers between devices, along_x(): lax.ppermute(block, 'gx', [(g, (g + 2 * step) % count) for g in range(cou...  38 us
    ppermute x10, starting transfers between devices, along_x(): lax.ppermute(block, 'gx', [(g, (g + 2 * step) % count) for g in range(cou...  20.1 us
    ppermute x7, starting transfers between devices, along_y(): lax.ppermute(block, 'gy', [(s, t) for s, t in pairs if 0 <= t < count])  20.1 us
    ppermute x7, waiting for transfers between devices, along_y(): lax.ppermute(block, 'gy', [(s, t) for s, t in pairs if 0 <= t < count])  11.4 us
    ppermute x8, waiting for transfers between devices, swap(): return lax.ppermute(block, 'gy', [(g, g ^ k) for g in range(count)])  9.55 us
    pallas_call x1, Pallas kernels, input_terms(): pl.pallas_call(input_kernel, out_shape=[jax.ShapeDtypeStruct((2,) + block...  8.7 us
    pallas_call x1, Pallas kernels, weight_terms(): pl.pallas_call(functools.partial(weight_kernel, norm), out_shape=[jax.Sha...  7.64 us
    ppermute x1, waiting for transfers between devices, body(): lax.ppermute(mine.astype(BF16), 'gx', [(g, g ^ 1) for g in range(count)])  7.42 us
  transfers between devices with their start and end apart: 29, of which 15 were waited for; matrix products, arithmetic and copies ran while one was open for 0% of the time, Pallas kernels for 8%

profile of v5, /device:TPU:0, one launch (start us, length us, event | category | flops | bytes accessed | tf_op | source)
XLA Modules:
  0.0 145.8 jit_solution(5347202839881132921)
XLA Ops:
  0.6 1.0 copy-done
  1.7 1.0 copy-done.2
  2.7 0.2 shard_map.50
  3.0 2.1 %collective-permute-start.4 = (bf16[4,8,16,512]{3,2,1,0:T(8,128)(2,1)S(1)}, bf16[4,8,16,512]{3,2,1,0:T(8,128)(2,1)S(1)}, u32[]{:S(2)}, u32[]{:S(2)}) collective-permute-start(bf16[4,8,16,512]{3,2,1,0:T(8,128)(2,1)S(1)} %get-tuple-element.51.own_act), channel_id=1, source_target_pairs={{0,2},{1,3},{2,0},{3,1},{4,6},{5,7},{6,4},{7,5},{8,10},{9,11},{10,... | collective-permute-start | bytes 1572872 | tf_op jit(solution)/shard_map/ppermute | solution.py:34
  5.1 0.7 collective-permute-start
  5.7 9.4 %collective-permute-start.10 = (bf16[27,32,512]{2,1,0:T(8,128)(2,1)}, bf16[27,32,512]{2,1,0:T(8,128)(2,1)S(1)}, u32[]{:S(2)}, u32[]{:S(2)}) collective-permute-start(bf16[27,32,512]{2,1,0:T(8,128)(2,1)} %own), channel_id=1, source_target_pairs={{0,4},{1,5},{2,6},{3,7},{4,8},{5,9},{6,10},{7,11},{8,12},{9,13},{1... | collective-permute-start | bytes 2654216 | tf_op jit(solution)/shard_map/ppermute | solution.py:42
  15.2 1.4 collective-permute-start.9
  16.6 1.0 copy-done.1
  17.7 3.7 %collective-permute-start.2 = (bf16[5,16,512]{2,1,0:T(8,128)(2,1)S(1)}, bf16[5,16,512]{2,1,0:T(8,128)(2,1)S(1)}, u32[]{:S(2)}, u32[]{:S(2)}) collective-permute-start(bf16[5,16,512]{2,1,0:T(8,128)(2,1)S(1)} %get-tuple-element.53), channel_id=1, source_target_pairs={{0,16},{32,48},{64,80},{96,112},{16,0},{48,32},{80,64},{112,96},{1... | collective-permute-start | bytes 245768 | tf_op jit(solution)/shard_map/ppermute | solution.py:53
  21.4 0.7 collective-permute-start.3
  22.0 2.0 %collective-permute-done.2.even = bf16[5,16,512]{2,1,0:T(8,128)(2,1)S(1)} collective-permute-done((bf16[5,16,512]{2,1,0:T(8,128)(2,1)S(1)}, bf16[5,16,512]{2,1,0:T(8,128)(2,1)S(1)}, u32[]{:S(2)}, u32[]{:S(2)}) %collective-permute-start.2) | collective-permute-done | bytes 81952 | tf_op jit(solution)/shard_map/ppermute | solution.py:53
  24.0 1.0 shard_map.52
  25.3 1.8 %collective-permute-start.7 = (bf16[5,10,16,128]{3,2,1,0:T(8,128)(2,1)S(1)}, bf16[5,10,16,128]{3,2,1,0:T(8,128)(2,1)S(1)}, u32[]{:S(2)}, u32[]{:S(2)}) collective-permute-start(bf16[5,10,16,128]{3,2,1,0:T(8,128)(2,1)S(1)} %get-tuple-element.62), channel_id=1, source_target_pairs={{0,3},{1,2},{2,1},{3,0},{4,7},{5,6},{6,5},{7,4},{8,11},{9,10},{10,... | collective-permute-start | bytes 614408 | tf_op jit(solution)/shard_map/ppermute | solution.py:34
  27.0 6.1 %collective-permute-done.6.p2 = bf16[5,10,16,128]{3,2,1,0:T(8,128)(2,1)S(1)} collective-permute-done((bf16[5,10,16,128]{3,2,1,0:T(8,128)(2,1)S(1)}, bf16[5,10,16,128]{3,2,1,0:T(8,128)(2,1)S(1)}, u32[]{:S(2)}, u32[]{:S(2)}) %collective-permute-start.6) | collective-permute-done | bytes 204832 | tf_op jit(solution)/shard_map/ppermute | solution.py:34
  33.1 3.4 %collective-permute-done.7.p3 = bf16[5,10,16,128]{3,2,1,0:T(8,128)(2,1)S(1)} collective-permute-done((bf16[5,10,16,128]{3,2,1,0:T(8,128)(2,1)S(1)}, bf16[5,10,16,128]{3,2,1,0:T(8,128)(2,1)S(1)}, u32[]{:S(2)}, u32[]{:S(2)}) %collective-permute-start.7) | collective-permute-done | bytes 204832 | tf_op jit(solution)/shard_map/ppermute | solution.py:34
  36.6 0.3 collective-permute-start.8
  36.9 1.8 %shard_map.53 = (bf16[18,10,16,128]{3,2,1,0:T(8,128)(2,1)S(1)}, bf16[1152,2304]{1,0:T(8,128)(2,1)S(1)}) custom-call(bf16[5,10,16,128]{3,2,1,0:T(8,128)(2,1)S(1)} %get-tuple-element.64.p0, bf16[5,10,16,128]{3,2,1,0:T(8,128)(2,1)S(1)} %collective-permute-done.5.p1, bf16[5,10,16,128]{3,2,1,0:T(8,128)(2,1)S(1)} %collective-permute-done.6.p2, ...), custom_call_target="tpu_custom_call" | custom-call | tf_op jit(solution)/shard_map/pallas_call | solution.py:178
  38.8 1.6 %collective-permute-start.11 = (bf16[13,32,512]{2,1,0:T(8,128)(2,1)S(1)}, bf16[13,32,512]{2,1,0:T(8,128)(2,1)S(1)}, u32[]{:S(2)}, u32[]{:S(2)}) collective-permute-start(bf16[13,32,512]{2,1,0:T(8,128)(2,1)S(1)} %slice.27), channel_id=1, source_target_pairs={{0,4},{1,5},{2,6},{3,7},{4,8},{5,9},{6,10},{7,11},{8,12},{9,13},{1... | collective-permute-start | bytes 1277960 | tf_op jit(solution)/shard_map/ppermute | solution.py:42
  40.5 1.9 %collective-permute-start.12 = (bf16[14,32,512]{2,1,0:T(8,128)(2,1)S(1)}, bf16[14,32,512]{2,1,0:T(8,128)(2,1)S(1)}, u32[]{:S(2)}, u32[]{:S(2)}) collective-permute-start(bf16[14,32,512]{2,1,0:T(8,128)(2,1)S(1)} %slice.28), channel_id=1, source_target_pairs={{0,12},{1,13},{2,14},{3,15},{4,0},{5,1},{6,2},{7,3},{8,4},{9,5},{1... | collective-permute-start | bytes 1376264 | tf_op jit(solution)/shard_map/ppermute | solution.py:42
  42.4 7.6 %shard_map.54 = (bf16[2,27,16,512]{3,2,1,0:T(8,128)(2,1)S(1)}, bf16[2,27,16,512]{3,2,1,0:T(8,128)(2,1)S(1)}, f32[27,16,512]{2,1,0:T(8,128)S(1)}, f32[27,16,512]{2,1,0:T(8,128)S(1)}, f32[2,27,16,512]{3,2,1,0:T(8,128)S(1)}) custom-call(bf16[4,8,16,512]{3,2,1,0:T(8,128)(2,1)S(1)} %get-tuple-element.51.own_act, ...), custom_call_target="tpu_custom_call" | custom-call | flops 7247757312 | bytes 10000000 | tf_op jit(solution)/shard_map/pallas_call | solution.py:238
  50.0 2.0 %collective-permute-done.11.across_low = bf16[13,32,512]{2,1,0:T(8,128)(2,1)S(1)} collective-permute-done((bf16[13,32,512]{2,1,0:T(8,128)(2,1)S(1)}, bf16[13,32,512]{2,1,0:T(8,128)(2,1)S(1)}, u32[]{:S(2)}, u32[]{:S(2)}) %collective-permute-start.11) | collective-permute-done | bytes 426016 | tf_op jit(solution)/shard_map/ppermute | solution.py:42
  52.0 1.1 collective-permute-done.12.across_high
  53.1 8.7 %shard_map.55 = (f32[2,4,8,16,512]{4,3,2,1,0:T(8,128)S(1)}, f32[4,8,16,512]{3,2,1,0:T(8,128)S(1)}, f32[4,8,16,512]{3,2,1,0:T(8,128)S(1)}) custom-call(bf16[18,10,16,128]{3,2,1,0:T(8,128)(2,1)S(1)} %get-tuple-element.76.held, bf16[27,32,512]{2,1,0:T(8,128)(2,1)S(1)} %copy-done.4, bf16[27,32,512]{2,1,0:T(8,128)(2,1)S(1)} %collective-permute-done.9.above, ...), custom_call_target="tpu_custom_call" | custom-call | flops 10192158720 | bytes 10000000 | tf_op jit(solution)/shard_map/pallas_call | solution.py:302
  61.9 6.8 %collective-permute-start.14 = (bf16[2,27,16,512]{3,2,1,0:T(8,128)(2,1)S(1)}, bf16[2,27,16,512]{3,2,1,0:T(8,128)(2,1)S(1)}, u32[]{:S(2)}, u32[]{:S(2)}) collective-permute-start(bf16[2,27,16,512]{3,2,1,0:T(8,128)(2,1)S(1)} %get-tuple-element.83), channel_id=1, source_target_pairs={{0,32},{16,48},{32,64},{48,80},{64,96},{80,112},{96,0},{112,16},{1... | collective-permute-start | bytes 2654216 | tf_op jit(solution)/shard_map/ppermute | solution.py:47
  68.6 1.4 collective-permute-start.15
  70.0 0.2 fusion
  70.2 19.9 %collective-permute-done.14.from_left = bf16[2,27,16,512]{3,2,1,0:T(8,128)(2,1)S(1)} collective-permute-done((bf16[2,27,16,512]{3,2,1,0:T(8,128)(2,1)S(1)}, bf16[2,27,16,512]{3,2,1,0:T(8,128)(2,1)S(1)}, u32[]{:S(2)}, u32[]{:S(2)}) %collective-permute-start.14) | collective-permute-done | bytes 884768 | tf_op jit(solution)/shard_map/ppermute | solution.py:47
  90.2 0.2 collective-permute-done.15.from_right
  90.4 0.5 collective-permute-start.21
  90.8 0.2 fusion.2
  91.0 1.5 %collective-permute-start.16 = (bf16[27,16,512]{2,1,0:T(8,128)(2,1)S(1)}, bf16[27,16,512]{2,1,0:T(8,128)(2,1)S(1)}, u32[]{:S(2)}, u32[]{:S(2)}) collective-permute-start(bf16[27,16,512]{2,1,0:T(8,128)(2,1)S(1)} %fusion.2), channel_id=1, source_target_pairs={{0,32},{16,48},{32,64},{48,80},{64,96},{80,112},{96,0},{112,16},{1... | collective-permute-start | bytes 1327112 | tf_op jit(solution)/shard_map/ppermute | solution.py:47
  92.7 1.8 %collective-permute-start.17 = (bf16[27,16,512]{2,1,0:T(8,128)(2,1)S(1)}, bf16[27,16,512]{2,1,0:T(8,128)(2,1)S(1)}, u32[]{:S(2)}, u32[]{:S(2)}) collective-permute-start(bf16[27,16,512]{2,1,0:T(8,128)(2,1)S(1)} %fusion.1), channel_id=1, source_target_pairs={{0,96},{16,112},{32,0},{48,16},{64,32},{80,48},{96,64},{112,80},{1... | collective-permute-start | bytes 1327112 | tf_op jit(solution)/shard_map/ppermute | solution.py:47
  94.6 9.2 %collective-permute-done.16.last_left = bf16[27,16,512]{2,1,0:T(8,128)(2,1)S(1)} collective-permute-done((bf16[27,16,512]{2,1,0:T(8,128)(2,1)S(1)}, bf16[27,16,512]{2,1,0:T(8,128)(2,1)S(1)}, u32[]{:S(2)}, u32[]{:S(2)}) %collective-permute-start.16) | collective-permute-done | bytes 442400 | tf_op jit(solution)/shard_map/ppermute | solution.py:47
  103.8 0.5 shard_map.56
  104.3 1.7 %collective-permute-start.18 = (bf16[27,8,512]{2,1,0:T(8,128)(2,1)S(1)}, bf16[27,8,512]{2,1,0:T(8,128)(2,1)S(1)}, u32[]{:S(2)}, u32[]{:S(2)}) collective-permute-start(bf16[27,8,512]{2,1,0:T(8,128)(2,1)S(1)} %get-tuple-element.89), channel_id=1, source_target_pairs={{0,4},{1,5},{2,6},{3,7},{4,8},{5,9},{6,10},{7,11},{8,12},{9,13},{1... | collective-permute-start | bytes 663560 | tf_op jit(solution)/shard_map/ppermute | solution.py:42
  106.0 3.7 %collective-permute-start.19 = (bf16[27,8,512]{2,1,0:T(8,128)(2,1)S(1)}, bf16[27,8,512]{2,1,0:T(8,128)(2,1)S(1)}, u32[]{:S(2)}, u32[]{:S(2)}) collective-permute-start(bf16[27,8,512]{2,1,0:T(8,128)(2,1)S(1)} %get-tuple-element.90), channel_id=1, source_target_pairs={{0,8},{1,9},{2,10},{3,11},{4,12},{5,13},{6,14},{7,15},{8,0},{9,1},... | collective-permute-start | bytes 663560 | tf_op jit(solution)/shard_map/ppermute | solution.py:42
  109.8 0.2 collective-permute-start.20
  110.0 3.8 %collective-permute-done.18 = bf16[27,8,512]{2,1,0:T(8,128)(2,1)S(1)} collective-permute-done((bf16[27,8,512]{2,1,0:T(8,128)(2,1)S(1)}, bf16[27,8,512]{2,1,0:T(8,128)(2,1)S(1)}, u32[]{:S(2)}, u32[]{:S(2)}) %collective-permute-start.18) | collective-permute-done | bytes 221216 | tf_op jit(solution)/shard_map/ppermute | solution.py:42
  113.7 4.5 %collective-permute-done.19 = bf16[27,8,512]{2,1,0:T(8,128)(2,1)S(1)} collective-permute-done((bf16[27,8,512]{2,1,0:T(8,128)(2,1)S(1)}, bf16[27,8,512]{2,1,0:T(8,128)(2,1)S(1)}, u32[]{:S(2)}, u32[]{:S(2)}) %collective-permute-start.19) | collective-permute-done | bytes 221216 | tf_op jit(solution)/shard_map/ppermute | solution.py:42
  118.5 7.4 %collective-permute-done.22 = bf16[27,8,512]{2,1,0:T(8,128)(2,1)S(1)} collective-permute-done((bf16[27,8,512]{2,1,0:T(8,128)(2,1)S(1)}, bf16[27,8,512]{2,1,0:T(8,128)(2,1)S(1)}, u32[]{:S(2)}, u32[]{:S(2)}) %collective-permute-start.22) | collective-permute-done | bytes 221216 | tf_op jit(solution)/shard_map/ppermute | solution.py:433
  125.9 3.0 %collective-permute-start.26 = (f32[14,8,512]{2,1,0:T(8,128)S(1)}, f32[14,8,512]{2,1,0:T(8,128)S(1)}, u32[]{:S(2)}, u32[]{:S(2)}) collective-permute-start(f32[14,8,512]{2,1,0:T(8,128)S(1)} %slice_add_fusion.refs_1_), channel_id=1, source_target_pairs={{0,96},{16,112},{32,0},{48,16},{64,32},{80,48},{96,64},{112,80},{1... | collective-permute-start | bytes 688136 | tf_op jit(solution)/shard_map/ppermute | solution.py:47
  129.1 4.7 %collective-permute-done.26.refs_5_ = f32[14,8,512]{2,1,0:T(8,128)S(1)} collective-permute-done((f32[14,8,512]{2,1,0:T(8,128)S(1)}, f32[14,8,512]{2,1,0:T(8,128)S(1)}, u32[]{:S(2)}, u32[]{:S(2)}) %collective-permute-start.26) | collective-permute-done | bytes 229408 | tf_op jit(solution)/shard_map/ppermute | solution.py:47
  133.8 3.5 %collective-permute-start.28 = (f32[14,8,512]{2,1,0:T(8,128)S(1)}, f32[14,8,512]{2,1,0:T(8,128)S(1)}, u32[]{:S(2)}, u32[]{:S(2)}) collective-permute-start(f32[14,8,512]{2,1,0:T(8,128)S(1)} %collective-permute-done.26.refs_5_), channel_id=1, source_target_pairs={{0,96},{16,112},{32,0},{48,16},{64,32},{80,48},{96,64},{112,80},{1... | collective-permute-start | bytes 688136 | tf_op jit(solution)/shard_map/ppermute | solution.py:47
  137.5 1.9 %collective-permute-start.27 = (f32[13,8,512]{2,1,0:T(8,128)S(1)}, f32[13,8,512]{2,1,0:T(8,128)S(1)}, u32[]{:S(2)}, u32[]{:S(2)}) collective-permute-start(f32[13,8,512]{2,1,0:T(8,128)S(1)} %collective-permute-done.23.refs_2_), channel_id=1, source_target_pairs={{0,32},{16,48},{32,64},{48,80},{64,96},{80,112},{96,0},{112,16},{1... | collective-permute-start | bytes 638984 | tf_op jit(solution)/shard_map/ppermute | solution.py:47
  139.4 1.2 shard_map.57
  140.6 2.6 %collective-permute-done.25.refs_4_ = f32[13,8,512]{2,1,0:T(8,128)S(1)} collective-permute-done((f32[13,8,512]{2,1,0:T(8,128)S(1)}, f32[13,8,512]{2,1,0:T(8,128)S(1)}, u32[]{:S(2)}, u32[]{:S(2)}) %collective-permute-start.25) | collective-permute-done | bytes 213024 | tf_op jit(solution)/shard_map/ppermute | solution.py:47
  143.2 1.3 collective-permute-done.27.refs_6_
  144.5 1.3 shard_map.58
  (37 shorter events, 1.2 us)
Async XLA Ops:
  0.6 1.0 copy-start
  1.7 1.0 copy-start.2
  2.9 2.9 %collective-permute-start.1 = (bf16[4,8,16,512]{3,2,1,0:T(8,128)(2,1)S(1)}, bf16[4,8,16,512]{3,2,1,0:T(8,128)(2,1)S(1)}, u32[]{:S(2)}, u32[]{:S(2)}) collective-permute-start(bf16[4,8,16,512]{3,2,1,0:T(8,128)(2,1)S(1)} %get-tuple-element.51.own_act), channel_id=1, source_target_pairs={{0,1},{1,0},{2,3},{3,2},{4,5},{5,4},{6,7},{7,6},{8,9},{9,8},{10,11... | collective-permute-start | bytes 1572872 | tf_op jit(solution)/shard_map/ppermute | solution.py:34
  3.0 22.1 %collective-permute-start.4 = (bf16[4,8,16,512]{3,2,1,0:T(8,128)(2,1)S(1)}, bf16[4,8,16,512]{3,2,1,0:T(8,128)(2,1)S(1)}, u32[]{:S(2)}, u32[]{:S(2)}) collective-permute-start(bf16[4,8,16,512]{3,2,1,0:T(8,128)(2,1)S(1)} %get-tuple-element.51.own_act), channel_id=1, source_target_pairs={{0,2},{1,3},{2,0},{3,1},{4,6},{5,7},{6,4},{7,5},{8,10},{9,11},{10,... | collective-permute-start | bytes 1572872 | tf_op jit(solution)/shard_map/ppermute | solution.py:34
  5.1 0.7 collective-permute-start
  5.7 33.0 %collective-permute-start.10 = (bf16[27,32,512]{2,1,0:T(8,128)(2,1)}, bf16[27,32,512]{2,1,0:T(8,128)(2,1)S(1)}, u32[]{:S(2)}, u32[]{:S(2)}) collective-permute-start(bf16[27,32,512]{2,1,0:T(8,128)(2,1)} %own), channel_id=1, source_target_pairs={{0,4},{1,5},{2,6},{3,7},{4,8},{5,9},{6,10},{7,11},{8,12},{9,13},{1... | collective-permute-start | bytes 2654216 | tf_op jit(solution)/shard_map/ppermute | solution.py:42
  15.2 23.5 %collective-permute-start.9 = (bf16[27,32,512]{2,1,0:T(8,128)(2,1)}, bf16[27,32,512]{2,1,0:T(8,128)(2,1)S(1)}, u32[]{:S(2)}, u32[]{:S(2)}) collective-permute-start(bf16[27,32,512]{2,1,0:T(8,128)(2,1)} %own), channel_id=1, source_target_pairs={{0,12},{1,13},{2,14},{3,15},{4,0},{5,1},{6,2},{7,3},{8,4},{9,5},{1... | collective-permute-start | bytes 2654216 | tf_op jit(solution)/shard_map/ppermute | solution.py:42
  16.6 1.0 copy-start.1
  17.7 6.3 %collective-permute-start.2 = (bf16[5,16,512]{2,1,0:T(8,128)(2,1)S(1)}, bf16[5,16,512]{2,1,0:T(8,128)(2,1)S(1)}, u32[]{:S(2)}, u32[]{:S(2)}) collective-permute-start(bf16[5,16,512]{2,1,0:T(8,128)(2,1)S(1)} %get-tuple-element.53), channel_id=1, source_target_pairs={{0,16},{32,48},{64,80},{96,112},{16,0},{48,32},{80,64},{112,96},{1... | collective-permute-start | bytes 245768 | tf_op jit(solution)/shard_map/ppermute | solution.py:53
  21.4 2.7 %collective-permute-start.3 = (bf16[5,16,512]{2,1,0:T(8,128)(2,1)S(1)}, bf16[5,16,512]{2,1,0:T(8,128)(2,1)S(1)}, u32[]{:S(2)}, u32[]{:S(2)}) collective-permute-start(bf16[5,16,512]{2,1,0:T(8,128)(2,1)S(1)} %get-tuple-element.54), channel_id=1, source_target_pairs={{16,32},{48,64},{80,96},{32,16},{64,48},{96,80},{17,33},{49,65},{8... | collective-permute-start | bytes 245768 | tf_op jit(solution)/shard_map/ppermute | solution.py:53
  25.1 2.0 %collective-permute-start.5 = (bf16[5,10,16,128]{3,2,1,0:T(8,128)(2,1)S(1)}, bf16[5,10,16,128]{3,2,1,0:T(8,128)(2,1)S(1)}, u32[]{:S(2)}, u32[]{:S(2)}) collective-permute-start(bf16[5,10,16,128]{3,2,1,0:T(8,128)(2,1)S(1)} %get-tuple-element.60), channel_id=1, source_target_pairs={{0,1},{1,0},{2,3},{3,2},{4,5},{5,4},{6,7},{7,6},{8,9},{9,8},{10,11... | collective-permute-start | bytes 614408 | tf_op jit(solution)/shard_map/ppermute | solution.py:34
  25.2 8.0 %collective-permute-start.6 = (bf16[5,10,16,128]{3,2,1,0:T(8,128)(2,1)S(1)}, bf16[5,10,16,128]{3,2,1,0:T(8,128)(2,1)S(1)}, u32[]{:S(2)}, u32[]{:S(2)}) collective-permute-start(bf16[5,10,16,128]{3,2,1,0:T(8,128)(2,1)S(1)} %get-tuple-element.61), channel_id=1, source_target_pairs={{0,2},{1,3},{2,0},{3,1},{4,6},{5,7},{6,4},{7,5},{8,10},{9,11},{10,... | collective-permute-start | bytes 614408 | tf_op jit(solution)/shard_map/ppermute | solution.py:34
  25.3 11.3 %collective-permute-start.7 = (bf16[5,10,16,128]{3,2,1,0:T(8,128)(2,1)S(1)}, bf16[5,10,16,128]{3,2,1,0:T(8,128)(2,1)S(1)}, u32[]{:S(2)}, u32[]{:S(2)}) collective-permute-start(bf16[5,10,16,128]{3,2,1,0:T(8,128)(2,1)S(1)} %get-tuple-element.62), channel_id=1, source_target_pairs={{0,3},{1,2},{2,1},{3,0},{4,7},{5,6},{6,5},{7,4},{8,11},{9,10},{10,... | collective-permute-start | bytes 614408 | tf_op jit(solution)/shard_map/ppermute | solution.py:34
  36.6 5.8 %collective-permute-start.8 = (bf16[4,8,16,512]{3,2,1,0:T(8,128)(2,1)S(1)}, bf16[4,8,16,512]{3,2,1,0:T(8,128)(2,1)S(1)}, u32[]{:S(2)}, u32[]{:S(2)}) collective-permute-start(bf16[4,8,16,512]{3,2,1,0:T(8,128)(2,1)S(1)} %collective-permute-done.4.far), channel_id=1, source_target_pairs={{0,1},{1,0},{2,3},{3,2},{4,5},{5,4},{6,7},{7,6},{8,9},{9,8},{10,11... | collective-permute-start | bytes 1572872 | tf_op jit(solution)/shard_map/ppermute | solution.py:34
  38.8 13.2 %collective-permute-start.11 = (bf16[13,32,512]{2,1,0:T(8,128)(2,1)S(1)}, bf16[13,32,512]{2,1,0:T(8,128)(2,1)S(1)}, u32[]{:S(2)}, u32[]{:S(2)}) collective-permute-start(bf16[13,32,512]{2,1,0:T(8,128)(2,1)S(1)} %slice.27), channel_id=1, source_target_pairs={{0,4},{1,5},{2,6},{3,7},{4,8},{5,9},{6,10},{7,11},{8,12},{9,13},{1... | collective-permute-start | bytes 1277960 | tf_op jit(solution)/shard_map/ppermute | solution.py:42
  40.4 12.6 %copy-start.4 = (bf16[27,32,512]{2,1,0:T(8,128)(2,1)S(1)}, bf16[27,32,512]{2,1,0:T(8,128)(2,1)}, u32[]{:S(2)}) copy-start(bf16[27,32,512]{2,1,0:T(8,128)(2,1)} %own) | copy-start | bytes 2654212
  40.5 12.6 %collective-permute-start.12 = (bf16[14,32,512]{2,1,0:T(8,128)(2,1)S(1)}, bf16[14,32,512]{2,1,0:T(8,128)(2,1)S(1)}, u32[]{:S(2)}, u32[]{:S(2)}) collective-permute-start(bf16[14,32,512]{2,1,0:T(8,128)(2,1)S(1)} %slice.28), channel_id=1, source_target_pairs={{0,12},{1,13},{2,14},{3,15},{4,0},{5,1},{6,2},{7,3},{8,4},{9,5},{1... | collective-permute-start | bytes 1376264 | tf_op jit(solution)/shard_map/ppermute | solution.py:42
  61.8 8.3 %collective-permute-start.13 = (f32[2,4,8,16,512]{4,3,2,1,0:T(8,128)S(1)}, f32[2,4,8,16,512]{4,3,2,1,0:T(8,128)S(1)}, u32[]{:S(2)}, u32[]{:S(2)}) collective-permute-start(f32[2,4,8,16,512]{4,3,2,1,0:T(8,128)S(1)} %get-tuple-element.80), channel_id=1, source_target_pairs={{0,1},{1,0},{2,3},{3,2},{4,5},{5,4},{6,7},{7,6},{8,9},{9,8},{10,11... | collective-permute-start | bytes 6291464 | tf_op jit(solution)/shard_map/ppermute | solution.py:34
  61.9 28.3 %collective-permute-start.14 = (bf16[2,27,16,512]{3,2,1,0:T(8,128)(2,1)S(1)}, bf16[2,27,16,512]{3,2,1,0:T(8,128)(2,1)S(1)}, u32[]{:S(2)}, u32[]{:S(2)}) collective-permute-start(bf16[2,27,16,512]{3,2,1,0:T(8,128)(2,1)S(1)} %get-tuple-element.83), channel_id=1, source_target_pairs={{0,32},{16,48},{32,64},{48,80},{64,96},{80,112},{96,0},{112,16},{1... | collective-permute-start | bytes 2654216 | tf_op jit(solution)/shard_map/ppermute | solution.py:47
  68.6 21.7 %collective-permute-start.15 = (bf16[2,27,16,512]{3,2,1,0:T(8,128)(2,1)S(1)}, bf16[2,27,16,512]{3,2,1,0:T(8,128)(2,1)S(1)}, u32[]{:S(2)}, u32[]{:S(2)}) collective-permute-start(bf16[2,27,16,512]{3,2,1,0:T(8,128)(2,1)S(1)} %get-tuple-element.84), channel_id=1, source_target_pairs={{0,96},{16,112},{32,0},{48,16},{64,32},{80,48},{96,64},{112,80},{1... | collective-permute-start | bytes 2654216 | tf_op jit(solution)/shard_map/ppermute | solution.py:47
  90.4 27.9 %collective-permute-start.21 = (f32[4,8,16,512]{3,2,1,0:T(8,128)S(1)}, f32[4,8,16,512]{3,2,1,0:T(8,128)S(1)}, u32[]{:S(2)}, u32[]{:S(2)}) collective-permute-start(f32[4,8,16,512]{3,2,1,0:T(8,128)S(1)} %fusion), channel_id=1, source_target_pairs={{0,2},{1,3},{2,0},{3,1},{4,6},{5,7},{6,4},{7,5},{8,10},{9,11},{10,... | collective-permute-start | bytes 3145736 | tf_op jit(solution)/shard_map/ppermute | solution.py:34
  91.0 12.7 %collective-permute-start.16 = (bf16[27,16,512]{2,1,0:T(8,128)(2,1)S(1)}, bf16[27,16,512]{2,1,0:T(8,128)(2,1)S(1)}, u32[]{:S(2)}, u32[]{:S(2)}) collective-permute-start(bf16[27,16,512]{2,1,0:T(8,128)(2,1)S(1)} %fusion.2), channel_id=1, source_target_pairs={{0,32},{16,48},{32,64},{48,80},{64,96},{80,112},{96,0},{112,16},{1... | collective-permute-start | bytes 1327112 | tf_op jit(solution)/shard_map/ppermute | solution.py:47
  92.7 11.1 %collective-permute-start.17 = (bf16[27,16,512]{2,1,0:T(8,128)(2,1)S(1)}, bf16[27,16,512]{2,1,0:T(8,128)(2,1)S(1)}, u32[]{:S(2)}, u32[]{:S(2)}) collective-permute-start(bf16[27,16,512]{2,1,0:T(8,128)(2,1)S(1)} %fusion.1), channel_id=1, source_target_pairs={{0,96},{16,112},{32,0},{48,16},{64,32},{80,48},{96,64},{112,80},{1... | collective-permute-start | bytes 1327112 | tf_op jit(solution)/shard_map/ppermute | solution.py:47
  104.3 35.1 %copy-start.3 = (bf16[4,8,16,512]{3,2,1,0:T(8,128)(2,1)S(1)}, bf16[4,8,16,512]{3,2,1,0:T(8,128)(2,1)}, u32[]{:S(2)}) copy-start(bf16[4,8,16,512]{3,2,1,0:T(8,128)(2,1)} %pre.3) | copy-start | bytes 1572868
  104.3 9.4 %collective-permute-start.18 = (bf16[27,8,512]{2,1,0:T(8,128)(2,1)S(1)}, bf16[27,8,512]{2,1,0:T(8,128)(2,1)S(1)}, u32[]{:S(2)}, u32[]{:S(2)}) collective-permute-start(bf16[27,8,512]{2,1,0:T(8,128)(2,1)S(1)} %get-tuple-element.89), channel_id=1, source_target_pairs={{0,4},{1,5},{2,6},{3,7},{4,8},{5,9},{6,10},{7,11},{8,12},{9,13},{1... | collective-permute-start | bytes 663560 | tf_op jit(solution)/shard_map/ppermute | solution.py:42
  106.0 12.3 %collective-permute-start.19 = (bf16[27,8,512]{2,1,0:T(8,128)(2,1)S(1)}, bf16[27,8,512]{2,1,0:T(8,128)(2,1)S(1)}, u32[]{:S(2)}, u32[]{:S(2)}) collective-permute-start(bf16[27,8,512]{2,1,0:T(8,128)(2,1)S(1)} %get-tuple-element.90), channel_id=1, source_target_pairs={{0,8},{1,9},{2,10},{3,11},{4,12},{5,13},{6,14},{7,15},{8,0},{9,1},... | collective-permute-start | bytes 663560 | tf_op jit(solution)/shard_map/ppermute | solution.py:42
  109.8 8.5 %collective-permute-start.20 = (bf16[27,8,512]{2,1,0:T(8,128)(2,1)S(1)}, bf16[27,8,512]{2,1,0:T(8,128)(2,1)S(1)}, u32[]{:S(2)}, u32[]{:S(2)}) collective-permute-start(bf16[27,8,512]{2,1,0:T(8,128)(2,1)S(1)} %get-tuple-element.91), channel_id=1, source_target_pairs={{0,12},{1,13},{2,14},{3,15},{4,0},{5,1},{6,2},{7,3},{8,4},{9,5},{1... | collective-permute-start | bytes 663560 | tf_op jit(solution)/shard_map/ppermute | solution.py:42
  118.4 7.5 %collective-permute-start.22 = (bf16[27,8,512]{2,1,0:T(8,128)(2,1)S(1)}, bf16[27,8,512]{2,1,0:T(8,128)(2,1)S(1)}, u32[]{:S(2)}, u32[]{:S(2)}) collective-permute-start(bf16[27,8,512]{2,1,0:T(8,128)(2,1)S(1)} %get-tuple-element.98), channel_id=1, source_target_pairs={{0,16},{16,0},{32,48},{48,32},{64,80},{80,64},{96,112},{112,96},{1... | collective-permute-start | bytes 663560 | tf_op jit(solution)/shard_map/ppermute | solution.py:433
  125.9 7.8 %collective-permute-start.26 = (f32[14,8,512]{2,1,0:T(8,128)S(1)}, f32[14,8,512]{2,1,0:T(8,128)S(1)}, u32[]{:S(2)}, u32[]{:S(2)}) collective-permute-start(f32[14,8,512]{2,1,0:T(8,128)S(1)} %slice_add_fusion.refs_1_), channel_id=1, source_target_pairs={{0,96},{16,112},{32,0},{48,16},{64,32},{80,48},{96,64},{112,80},{1... | collective-permute-start | bytes 688136 | tf_op jit(solution)/shard_map/ppermute | solution.py:47
  128.9 8.5 %collective-permute-start.23 = (f32[13,8,512]{2,1,0:T(8,128)S(1)}, f32[13,8,512]{2,1,0:T(8,128)S(1)}, u32[]{:S(2)}, u32[]{:S(2)}) collective-permute-start(f32[13,8,512]{2,1,0:T(8,128)S(1)} %slice_add_fusion.1.refs_0_), channel_id=1, source_target_pairs={{0,32},{16,48},{32,64},{48,80},{64,96},{80,112},{96,0},{112,16},{1... | collective-permute-start | bytes 638984 | tf_op jit(solution)/shard_map/ppermute | solution.py:47
  129.0 14.2 %collective-permute-start.24 = (f32[14,8,512]{2,1,0:T(8,128)S(1)}, f32[14,8,512]{2,1,0:T(8,128)S(1)}, u32[]{:S(2)}, u32[]{:S(2)}) collective-permute-start(f32[14,8,512]{2,1,0:T(8,128)S(1)} %slice_add_fusion.refs_1_), channel_id=1, source_target_pairs={{0,32},{16,48},{32,64},{48,80},{64,96},{80,112},{96,0},{112,16},{1... | collective-permute-start | bytes 688136 | tf_op jit(solution)/shard_map/ppermute | solution.py:47
  133.8 10.7 %collective-permute-start.28 = (f32[14,8,512]{2,1,0:T(8,128)S(1)}, f32[14,8,512]{2,1,0:T(8,128)S(1)}, u32[]{:S(2)}, u32[]{:S(2)}) collective-permute-start(f32[14,8,512]{2,1,0:T(8,128)S(1)} %collective-permute-done.26.refs_5_), channel_id=1, source_target_pairs={{0,96},{16,112},{32,0},{48,16},{64,32},{80,48},{96,64},{112,80},{1... | collective-permute-start | bytes 688136 | tf_op jit(solution)/shard_map/ppermute | solution.py:47
  137.3 5.8 %collective-permute-start.25 = (f32[13,8,512]{2,1,0:T(8,128)S(1)}, f32[13,8,512]{2,1,0:T(8,128)S(1)}, u32[]{:S(2)}, u32[]{:S(2)}) collective-permute-start(f32[13,8,512]{2,1,0:T(8,128)S(1)} %slice_add_fusion.1.refs_0_), channel_id=1, source_target_pairs={{0,96},{16,112},{32,0},{48,16},{64,32},{80,48},{96,64},{112,80},{1... | collective-permute-start | bytes 638984 | tf_op jit(solution)/shard_map/ppermute | solution.py:47
  137.5 7.1 %collective-permute-start.27 = (f32[13,8,512]{2,1,0:T(8,128)S(1)}, f32[13,8,512]{2,1,0:T(8,128)S(1)}, u32[]{:S(2)}, u32[]{:S(2)}) collective-permute-start(f32[13,8,512]{2,1,0:T(8,128)S(1)} %collective-permute-done.23.refs_2_), channel_id=1, source_target_pairs={{0,32},{16,48},{32,64},{48,80},{64,96},{80,112},{96,0},{112,16},{1... | collective-permute-start | bytes 638984 | tf_op jit(solution)/shard_map/ppermute | solution.py:47

commit v6 on v5

--- a/solution.py
+++ b/solution.py
@@ -76,40 +76,14 @@
     )(pre_act, cot)
 
 
-def side_kernel(cot, extra, even, odd):
-    rows, width = cot.shape[:2]
-    is_odd = lax.rem(lax.axis_index("gx"), 2) == 1
-
-    def put(out, upper):
-        out[0:rows] = jnp.where(upper, cot[:, width - 1], cot[:, 0])
-        out[rows] = jnp.where(upper, extra[width - 1], extra[0])
-
-    put(even, jnp.logical_not(is_odd))
-    put(odd, is_odd)
-
-
-def sides(cot, extra):
-    rows, width, depth, chan = cot.shape
-    return pl.pallas_call(
-        side_kernel,
-        out_shape=[jax.ShapeDtypeStruct((rows + 1, depth, chan), BF16)] * 2,
-        in_specs=[VMEM] * 2,
-        out_specs=[VMEM] * 2,
-        compiler_params=params(),
-    )(cot, extra)
-
-
-def pick_kernel(cot, extra, even, odd, *quarters):
-    rows, width, depth, chan = cot.shape
+def pick_kernel(cot, extra, *quarters):
+    rows, _, _, chan = cot.shape
     j = quad_place()
-    is_odd = lax.rem(lax.axis_index("gx"), 2) == 1
     q = chan // QUAD
     part = q // RING
     source = lax.broadcasted_iota(jnp.int32, (chan, q), 0)
     place = lax.broadcasted_iota(jnp.int32, (chan, q), 1)
     base = lax.div(place, part) * q + lax.rem(place, part)
-    low = jnp.where(is_odd, even[...], odd[...])
-    high = jnp.where(is_odd, odd[...], even[...])
 
     def take(block, pick):
         got = jnp.dot(block.reshape(-1, chan), pick, preferred_element_type=F32)
@@ -117,37 +91,58 @@
 
     for k, out in enumerate(quarters):
         pick = jnp.where(source == base + (j ^ k) * part, 1.0, 0.0).astype(BF16)
-        out[0:rows, 1:width + 1] = take(cot[...], pick)
-        out[rows, 1:width + 1] = take(extra[...], pick)
-        out[:, 0] = take(low, pick)
-        out[:, width + 1] = take(high, pick)
-
-
-def pick_channels(cot, *rims):
+        out[0:rows] = take(cot[...], pick)
+        out[rows] = take(extra[...], pick)
+
+
+def pick_channels(cot, extra):
     rows, width, depth, chan = cot.shape
-    quarter = jax.ShapeDtypeStruct((rows + 1, width + 2, depth, chan // QUAD), BF16)
+    quarter = jax.ShapeDtypeStruct((rows + 1, width, depth, chan // QUAD), BF16)
     return pl.pallas_call(
         pick_kernel,
         out_shape=[quarter] * QUAD,
-        in_specs=[VMEM] * 4,
+        in_specs=[VMEM] * 2,
         out_specs=[VMEM] * QUAD,
         compiler_params=params(),
-    )(cot, *rims)
-
-
-def turn_kernel(p0, p1, p2, p3, held, out):
+    )(cot, extra)
+
+
+def side_kernel(p0, p1, p2, p3, even, odd):
+    width = p0.shape[1]
+    is_odd = lax.rem(lax.axis_index("gx"), 2) == 1
+    for k, p in enumerate((p0, p1, p2, p3)):
+        first, last = p[:, 0], p[:, width - 1]
+        even[k] = jnp.where(is_odd, first, last)
+        odd[k] = jnp.where(is_odd, last, first)
+
+
+def sides(quarters):
+    rows, _, depth, q = quarters[0].shape
+    return pl.pallas_call(
+        side_kernel,
+        out_shape=[jax.ShapeDtypeStruct((QUAD, rows, depth, q), BF16)] * 2,
+        in_specs=[VMEM] * QUAD,
+        out_specs=[VMEM] * 2,
+        compiler_params=params(),
+    )(*quarters)
+
+
+def turn_kernel(p0, p1, p2, p3, even, odd, held, out):
     j, x = quad_place(), x_place()
+    is_odd = lax.rem(lax.axis_index("gx"), 2) == 1
     for k, p in enumerate((p0, p1, p2, p3)):
-        rows = p.shape[0] - 1
-        held[pl.ds(1 + (j ^ k) * rows, rows)] = p[0:rows]
-
-        @pl.when((j ^ k) == 0)
-        def _():
-            held[0] = p[rows]
-
-        @pl.when((j ^ k) == QUAD - 1)
-        def _():
-            held[held.shape[0] - 1] = p[rows]
+        rows, width = p.shape[0] - 1, p.shape[1]
+        low = jnp.where(is_odd, even[k], odd[k])
+        high = jnp.where(is_odd, odd[k], even[k])
+
+        def put(at, part):
+            held[at, 1:width + 1] = p[part]
+            held[at, 0] = low[part]
+            held[at, width + 1] = high[part]
+
+        put(pl.ds(1 + (j ^ k) * rows, rows), slice(0, rows))
+        pl.when((j ^ k) == 0)(functools.partial(put, 0, rows))
+        pl.when((j ^ k) == QUAD - 1)(functools.partial(put, held.shape[0] - 1, rows))
 
     tall, width, depth, q = held.shape
     width -= 2
@@ -172,8 +167,9 @@
             out[at:at + q] = v.astype(BF16)
 
 
-def turn(quarters):
+def turn(quarters, even, odd):
     rows, width, depth, q = quarters[0].shape
+    width += 2
     tall = QUAD * (rows - 1) + 2
     return pl.pallas_call(
         turn_kernel,
@@ -181,10 +177,10 @@
             jax.ShapeDtypeStruct((tall, width, depth, q), BF16),
             jax.ShapeDtypeStruct((9 * q, tall * (width - 2) * depth), BF16),
         ],
-        in_specs=[VMEM] * QUAD,
+        in_specs=[VMEM] * (QUAD + 2),
         out_specs=[VMEM] * 2,
         compiler_params=params(),
-    )(*quarters)
+    )(*quarters, even, odd)
 
 
 def run_copies(pairs, sem):
@@ -316,21 +312,23 @@
     )(held, *parts)
 
 
-def finish_kernel(pre, keep, near, far, out):
-    value = pre[...].astype(F32)
-    s = jax.nn.sigmoid(value)
-    grad = keep[...] + near[0] + far[...]
-    out[...] = (grad * s * (1.0 + value * (1.0 - s))).astype(BF16)
-
-
-def finish(pre_act, keep, near, far):
+def finish_kernel(pre, keep, near, far_low, far_high, out):
+    rows = far_low.shape[0]
+    for at, far in ((0, far_low), (rows, far_high)):
+        value = pre[at:at + rows].astype(F32)
+        s = jax.nn.sigmoid(value)
+        grad = keep[at:at + rows] + near[0, at:at + rows] + far[...]
+        out[at:at + rows] = (grad * s * (1.0 + value * (1.0 - s))).astype(BF16)
+
+
+def finish(pre_act, keep, near, *far):
     return pl.pallas_call(
         finish_kernel,
         out_shape=jax.ShapeDtypeStruct(pre_act.shape, BF16),
-        in_specs=[VMEM] * 4,
+        in_specs=[VMEM] * 5,
         out_specs=VMEM,
         compiler_params=params(),
-    )(pre_act, keep, near, far)
+    )(pre_act, keep, near, *far)
 
 
 def split_kernel(own, from_left, from_right, last_left, last_right, *refs):
@@ -401,39 +399,44 @@
     extra, near, weight = barrier((extra, near, weight))
     above = along_y(weight, -1, True)
     below = along_y(weight, 1, True)
-    even, odd = sides(cot, extra)
-    quarters = pick_channels(cot, extra, swap_x(even, 0), swap_x(odd, 1))
-    quarters, far = barrier((quarters, far))
+    quarters = pick_channels(cot, extra)
     quarters = [quarters[0]] + [swap(quarters[k], k) for k in (1, 2, 3)]
     quarters, far = barrier((quarters, far))
     acts = [act, near, far, swap(far, 1)]
-    held, turned = turn(quarters)
+    even, odd = sides(quarters)
+    held, turned = turn(quarters, swap_x(even, 0), swap_x(odd, 1))
 
     turned, above, below = barrier((turned, above, below))
+    right, left, *kept = weight_terms(norm, acts, turned)
+    held, right, left, above, below = barrier((held, right, left, above, below))
     taps = 13
     parts = [weight, above, along_y(below[:taps], 1, True), along_y(above[taps:], -1, True), below]
-    right, left, *kept = weight_terms(norm, acts, turned)
-    held, right, left = barrier((held, right, left))
     from_left, from_right = along_x(right, 1), along_x(left, -1)
     grads = input_terms(held, parts)
+    grads, from_left, from_right = barrier((grads, from_left, from_right))
     send, keep, pass_on = grads
     got = swap(send, 1)
-    passed, from_left, from_right = barrier((pass_on + got[1], from_left, from_right))
-    far_grad = swap(passed, 2)
     keep_right, keep_left, own = kept
     right = (from_left[0].astype(F32) + keep_right).astype(BF16)
     left = (from_right[0].astype(F32) + keep_left).astype(BF16)
-    mine, *others = split(own, from_left, from_right, along_x(right, 1), along_x(left, -1))
+    last_left, last_right = along_x(right, 1), along_x(left, -1)
+    half = rows // 2
+    passed = [pass_on[s] + got[1, s] for s in (slice(0, half), slice(half, rows))]
+    last_left, last_right, passed = barrier((last_left, last_right, passed))
+    far_low = swap(passed[0], 2)
+    mine, *others = split(own, from_left, from_right, last_left, last_right)
 
     others = [along_y(block, r, True) for r, block in zip((1, 2, 3), others)]
-    others, far_grad = barrier((others, far_grad))
+    others, far_low = barrier((others, far_low))
     for other in others:
         mine = mine + other.astype(F32)
     count = lax.axis_size("gx")
     other = lax.ppermute(mine.astype(BF16), "gx", [(g, g ^ 1) for g in range(count)])
+    other, passed = barrier((other, passed))
+    far_high = swap(passed[1], 2)
     low, high = [mine[s] + other[s].astype(F32) for s in (slice(0, taps), slice(taps, 27))]
     grad_weight = gather_x(low, high)
-    grad_pre = finish(pre_act, keep, got, far_grad)
+    grad_pre = finish(pre_act, keep, got, far_low, far_high)
     return (grad_pre, grad_weight)
 
 

time: 147 us -> 135 us (0.918)
  waiting for transfers between devices: 68.4 us -> 56.8 us
    ppermute x10, waiting for transfers between devices: 38 us -> 27.5 us  [along_x(): lax.ppermute(block, 'gx', [(g, (g + 2 * step) % count) for g in range(cou...]
    ppermute x7, starting transfers between devices: 20.1 us -> 17.6 us  [along_y(): lax.ppermute(block, 'gy', [(s, t) for s, t in pairs if 0 <= t < count])]
    ppermute x8 -> x9, starting transfers between devices: 4.99 us -> 6.92 us  [swap(): return lax.ppermute(block, 'gy', [(g, g ^ k) for g in range(count)])]
    ppermute x8 -> x9, waiting for transfers between devices: 9.55 us -> 8.26 us  [swap(): return lax.ppermute(block, 'gy', [(g, g ^ k) for g in range(count)])]
  transfers between devices with their start and end apart: 29 -> 30, of which waited for: 15 -> 17; matrix products, arithmetic and copies ran while one was open for 0% -> 0% of each run, Pallas kernels for 8% -> 10%
where the time goes in v6:
time: 135 us; the launch traced here: 134 us
  waiting for transfers between devices  56.8 us (42%)
  starting transfers between devices  49.9 us (37%)
  Pallas kernels  22.3 us (17%)
  local copies, waits for them, and re-layouts  3.19 us (2%)
    ppermute x10, waiting for transfers between devices, along_x(): lax.ppermute(block, 'gx', [(g, (g + 2 * step) % count) for g in range(cou...  27.5 us
    ppermute x10, starting transfers between devices, along_x(): lax.ppermute(block, 'gx', [(g, (g + 2 * step) % count) for g in range(cou...  19.7 us
    ppermute x7, starting transfers between devices, along_y(): lax.ppermute(block, 'gy', [(s, t) for s, t in pairs if 0 <= t < count])  17.6 us
    ppermute x7, waiting for transfers between devices, along_y(): lax.ppermute(block, 'gy', [(s, t) for s, t in pairs if 0 <= t < count])  12.3 us
    pallas_call x1, Pallas kernels, input_terms(): pl.pallas_call(input_kernel, out_shape=[jax.ShapeDtypeStruct((2,) + block...  8.7 us
    ppermute x9, waiting for transfers between devices, swap(): return lax.ppermute(block, 'gy', [(g, g ^ k) for g in range(count)])  8.26 us
    pallas_call x1, Pallas kernels, weight_terms(): pl.pallas_call(functools.partial(weight_kernel, norm), out_shape=[jax.Sha...  7.66 us
    ppermute x9, starting transfers between devices, swap(): return lax.ppermute(block, 'gy', [(g, g ^ k) for g in range(count)])  6.92 us
  transfers between devices with their start and end apart: 30, of which 17 were waited for; matrix products, arithmetic and copies ran while one was open for 0% of the time, Pallas kernels for 10%

profile of v6, /device:TPU:0, one launch (start us, length us, event | category | flops | bytes accessed | tf_op | source)
XLA Modules:
  0.0 133.8 jit_solution(3365355010564624740)
XLA Ops:
  0.6 1.0 copy-done
  1.7 1.0 copy-done.2
  3.0 2.1 %collective-permute-start.5 = (bf16[4,8,16,512]{3,2,1,0:T(8,128)(2,1)S(1)}, bf16[4,8,16,512]{3,2,1,0:T(8,128)(2,1)S(1)}, u32[]{:S(2)}, u32[]{:S(2)}) collective-permute-start(bf16[4,8,16,512]{3,2,1,0:T(8,128)(2,1)S(1)} %get-tuple-element.56.own_act), channel_id=1, source_target_pairs={{0,2},{1,3},{2,0},{3,1},{4,6},{5,7},{6,4},{7,5},{8,10},{9,11},{10,... | collective-permute-start | bytes 1572872 | tf_op jit(solution)/shard_map/ppermute | solution.py:34
  5.1 0.7 collective-permute-start
  5.7 9.4 %collective-permute-start.10 = (bf16[27,32,512]{2,1,0:T(8,128)(2,1)}, bf16[27,32,512]{2,1,0:T(8,128)(2,1)S(1)}, u32[]{:S(2)}, u32[]{:S(2)}) collective-permute-start(bf16[27,32,512]{2,1,0:T(8,128)(2,1)} %own), channel_id=1, source_target_pairs={{0,4},{1,5},{2,6},{3,7},{4,8},{5,9},{6,10},{7,11},{8,12},{9,13},{1... | collective-permute-start | bytes 2654216 | tf_op jit(solution)/shard_map/ppermute | solution.py:42
  15.2 1.4 %collective-permute-start.9 = (bf16[27,32,512]{2,1,0:T(8,128)(2,1)}, bf16[27,32,512]{2,1,0:T(8,128)(2,1)S(1)}, u32[]{:S(2)}, u32[]{:S(2)}) collective-permute-start(bf16[27,32,512]{2,1,0:T(8,128)(2,1)} %own), channel_id=1, source_target_pairs={{0,12},{1,13},{2,14},{3,15},{4,0},{5,1},{6,2},{7,3},{8,4},{9,5},{1... | collective-permute-start | bytes 2654216 | tf_op jit(solution)/shard_map/ppermute | solution.py:42
  16.6 1.0 copy-done.3
  17.7 0.9 shard_map.51
  18.6 0.5 collective-permute-start.3
  19.1 1.4 %collective-permute-start.4 = (bf16[5,8,16,128]{3,2,1,0:T(8,128)(2,1)S(1)}, bf16[5,8,16,128]{3,2,1,0:T(8,128)(2,1)S(1)}, u32[]{:S(2)}, u32[]{:S(2)}) collective-permute-start(bf16[5,8,16,128]{3,2,1,0:T(8,128)(2,1)S(1)} %get-tuple-element.61), channel_id=1, source_target_pairs={{0,3},{1,2},{2,1},{3,0},{4,7},{5,6},{6,5},{7,4},{8,11},{9,10},{10,... | collective-permute-start | bytes 491528 | tf_op jit(solution)/shard_map/ppermute | solution.py:34
  20.5 5.2 %collective-permute-done.3.p2 = bf16[5,8,16,128]{3,2,1,0:T(8,128)(2,1)S(1)} collective-permute-done((bf16[5,8,16,128]{3,2,1,0:T(8,128)(2,1)S(1)}, bf16[5,8,16,128]{3,2,1,0:T(8,128)(2,1)S(1)}, u32[]{:S(2)}, u32[]{:S(2)}) %collective-permute-start.3) | collective-permute-done | bytes 163872 | tf_op jit(solution)/shard_map/ppermute | solution.py:34
  25.7 2.6 %collective-permute-done.4.p3 = bf16[5,8,16,128]{3,2,1,0:T(8,128)(2,1)S(1)} collective-permute-done((bf16[5,8,16,128]{3,2,1,0:T(8,128)(2,1)S(1)}, bf16[5,8,16,128]{3,2,1,0:T(8,128)(2,1)S(1)}, u32[]{:S(2)}, u32[]{:S(2)}) %collective-permute-start.4) | collective-permute-done | bytes 163872 | tf_op jit(solution)/shard_map/ppermute | solution.py:34
  28.3 0.6 collective-permute-start.8
  28.9 3.7 %collective-permute-start.6 = (bf16[4,5,16,128]{3,2,1,0:T(8,128)(2,1)S(1)}, bf16[4,5,16,128]{3,2,1,0:T(8,128)(2,1)S(1)}, u32[]{:S(2)}, u32[]{:S(2)}) collective-permute-start(bf16[4,5,16,128]{3,2,1,0:T(8,128)(2,1)S(1)} %get-tuple-element.66), channel_id=1, source_target_pairs={{0,16},{32,48},{64,80},{96,112},{16,0},{48,32},{80,64},{112,96},{1... | collective-permute-start | bytes 245768 | tf_op jit(solution)/shard_map/ppermute | solution.py:53
  32.6 0.7 collective-permute-start.7
  33.2 2.0 %collective-permute-done.6.even = bf16[4,5,16,128]{3,2,1,0:T(8,128)(2,1)S(1)} collective-permute-done((bf16[4,5,16,128]{3,2,1,0:T(8,128)(2,1)S(1)}, bf16[4,5,16,128]{3,2,1,0:T(8,128)(2,1)S(1)}, u32[]{:S(2)}, u32[]{:S(2)}) %collective-permute-start.6) | collective-permute-done | bytes 81952 | tf_op jit(solution)/shard_map/ppermute | solution.py:53
  35.2 1.8 %shard_map.53 = (bf16[18,10,16,128]{3,2,1,0:T(8,128)(2,1)S(1)}, bf16[1152,2304]{1,0:T(8,128)(2,1)S(1)}) custom-call(bf16[5,8,16,128]{3,2,1,0:T(8,128)(2,1)S(1)} %get-tuple-element.62.p0, bf16[5,8,16,128]{3,2,1,0:T(8,128)(2,1)S(1)} %collective-permute-done.2.p1, bf16[5,8,16,128]{3,2,1,0:T(8,128)(2,1)S(1)} %collective-permute-done.3.p2, ...), custom_call_target="tpu_custom_call" | custom-call | tf_op jit(solution)/shard_map/pallas_call | solution.py:174
  37.1 7.7 %shard_map.54 = (bf16[2,27,16,512]{3,2,1,0:T(8,128)(2,1)S(1)}, bf16[2,27,16,512]{3,2,1,0:T(8,128)(2,1)S(1)}, f32[27,16,512]{2,1,0:T(8,128)S(1)}, f32[27,16,512]{2,1,0:T(8,128)S(1)}, f32[2,27,16,512]{3,2,1,0:T(8,128)S(1)}) custom-call(bf16[4,8,16,512]{3,2,1,0:T(8,128)(2,1)S(1)} %get-tuple-element.56.own_act, ...), custom_call_target="tpu_custom_call" | custom-call | flops 7247757312 | bytes 10000000 | tf_op jit(solution)/shard_map/pallas_call | solution.py:234
  44.8 2.1 %collective-permute-start.12 = (bf16[14,32,512]{2,1,0:T(8,128)(2,1)S(1)}, bf16[14,32,512]{2,1,0:T(8,128)(2,1)S(1)}, u32[]{:S(2)}, u32[]{:S(2)}) collective-permute-start(bf16[14,32,512]{2,1,0:T(8,128)(2,1)S(1)} %slice.37), channel_id=1, source_target_pairs={{0,12},{1,13},{2,14},{3,15},{4,0},{5,1},{6,2},{7,3},{8,4},{9,5},{1... | collective-permute-start | bytes 1376264 | tf_op jit(solution)/shard_map/ppermute | solution.py:42
  47.0 7.7 %collective-permute-start.13 = (bf16[2,27,16,512]{3,2,1,0:T(8,128)(2,1)S(1)}, bf16[2,27,16,512]{3,2,1,0:T(8,128)(2,1)S(1)}, u32[]{:S(2)}, u32[]{:S(2)}) collective-permute-start(bf16[2,27,16,512]{3,2,1,0:T(8,128)(2,1)S(1)} %get-tuple-element.84), channel_id=1, source_target_pairs={{0,32},{16,48},{32,64},{48,80},{64,96},{80,112},{96,0},{112,16},{1... | collective-permute-start | bytes 2654216 | tf_op jit(solution)/shard_map/ppermute | solution.py:47
  54.6 1.5 %collective-permute-start.14 = (bf16[2,27,16,512]{3,2,1,0:T(8,128)(2,1)S(1)}, bf16[2,27,16,512]{3,2,1,0:T(8,128)(2,1)S(1)}, u32[]{:S(2)}, u32[]{:S(2)}) collective-permute-start(bf16[2,27,16,512]{3,2,1,0:T(8,128)(2,1)S(1)} %get-tuple-element.85), channel_id=1, source_target_pairs={{0,96},{16,112},{32,0},{48,16},{64,32},{80,48},{96,64},{112,80},{1... | collective-permute-start | bytes 2654216 | tf_op jit(solution)/shard_map/ppermute | solution.py:47
  56.2 2.9 %collective-permute-done.11.across_low = bf16[13,32,512]{2,1,0:T(8,128)(2,1)S(1)} collective-permute-done((bf16[13,32,512]{2,1,0:T(8,128)(2,1)S(1)}, bf16[13,32,512]{2,1,0:T(8,128)(2,1)S(1)}, u32[]{:S(2)}, u32[]{:S(2)}) %collective-permute-start.11) | collective-permute-done | bytes 426016 | tf_op jit(solution)/shard_map/ppermute | solution.py:42
  59.1 8.7 %shard_map.55 = (f32[2,4,8,16,512]{4,3,2,1,0:T(8,128)S(1)}, f32[4,8,16,512]{3,2,1,0:T(8,128)S(1)}, f32[4,8,16,512]{3,2,1,0:T(8,128)S(1)}) custom-call(bf16[18,10,16,128]{3,2,1,0:T(8,128)(2,1)S(1)} %get-tuple-element.78.held, bf16[27,32,512]{2,1,0:T(8,128)(2,1)S(1)} %copy-done.4, bf16[27,32,512]{2,1,0:T(8,128)(2,1)S(1)} %collective-permute-done.9.above, ...), custom_call_target="tpu_custom_call" | custom-call | flops 10192158720 | bytes 10000000 | tf_op jit(solution)/shard_map/pallas_call | solution.py:298
  67.8 6.2 %collective-permute-done.13.from_left = bf16[2,27,16,512]{3,2,1,0:T(8,128)(2,1)S(1)} collective-permute-done((bf16[2,27,16,512]{3,2,1,0:T(8,128)(2,1)S(1)}, bf16[2,27,16,512]{3,2,1,0:T(8,128)(2,1)S(1)}, u32[]{:S(2)}, u32[]{:S(2)}) %collective-permute-start.13) | collective-permute-done | bytes 884768 | tf_op jit(solution)/shard_map/ppermute | solution.py:47
  74.0 0.2 collective-permute-done.14.from_right
  74.4 1.6 %collective-permute-start.16 = (bf16[27,16,512]{2,1,0:T(8,128)(2,1)S(1)}, bf16[27,16,512]{2,1,0:T(8,128)(2,1)S(1)}, u32[]{:S(2)}, u32[]{:S(2)}) collective-permute-start(bf16[27,16,512]{2,1,0:T(8,128)(2,1)S(1)} %fusion.1), channel_id=1, source_target_pairs={{0,32},{16,48},{32,64},{48,80},{64,96},{80,112},{96,0},{112,16},{1... | collective-permute-start | bytes 1327112 | tf_op jit(solution)/shard_map/ppermute | solution.py:47
  76.1 1.8 %collective-permute-start.17 = (bf16[27,16,512]{2,1,0:T(8,128)(2,1)S(1)}, bf16[27,16,512]{2,1,0:T(8,128)(2,1)S(1)}, u32[]{:S(2)}, u32[]{:S(2)}) collective-permute-start(bf16[27,16,512]{2,1,0:T(8,128)(2,1)S(1)} %fusion), channel_id=1, source_target_pairs={{0,96},{16,112},{32,0},{48,16},{64,32},{80,48},{96,64},{112,80},{1... | collective-permute-start | bytes 1327112 | tf_op jit(solution)/shard_map/ppermute | solution.py:47
  77.9 0.5 collective-permute-done.15.near
  78.4 0.2 fusion.2
  78.6 9.7 %collective-permute-done.16.last_left = bf16[27,16,512]{2,1,0:T(8,128)(2,1)S(1)} collective-permute-done((bf16[27,16,512]{2,1,0:T(8,128)(2,1)S(1)}, bf16[27,16,512]{2,1,0:T(8,128)(2,1)S(1)}, u32[]{:S(2)}, u32[]{:S(2)}) %collective-permute-start.16) | collective-permute-done | bytes 442400 | tf_op jit(solution)/shard_map/ppermute | solution.py:47
  88.5 0.5 shard_map.56
  89.0 0.3 collective-permute-start.18
  89.3 4.1 %collective-permute-start.19 = (bf16[27,8,512]{2,1,0:T(8,128)(2,1)S(1)}, bf16[27,8,512]{2,1,0:T(8,128)(2,1)S(1)}, u32[]{:S(2)}, u32[]{:S(2)}) collective-permute-start(bf16[27,8,512]{2,1,0:T(8,128)(2,1)S(1)} %get-tuple-element.97), channel_id=1, source_target_pairs={{0,8},{1,9},{2,10},{3,11},{4,12},{5,13},{6,14},{7,15},{8,0},{9,1},... | collective-permute-start | bytes 663560 | tf_op jit(solution)/shard_map/ppermute | solution.py:42
  93.6 4.3 %collective-permute-done.18 = bf16[27,8,512]{2,1,0:T(8,128)(2,1)S(1)} collective-permute-done((bf16[27,8,512]{2,1,0:T(8,128)(2,1)S(1)}, bf16[27,8,512]{2,1,0:T(8,128)(2,1)S(1)}, u32[]{:S(2)}, u32[]{:S(2)}) %collective-permute-start.18) | collective-permute-done | bytes 221216 | tf_op jit(solution)/shard_map/ppermute | solution.py:42
  97.8 5.1 %collective-permute-done.19 = bf16[27,8,512]{2,1,0:T(8,128)(2,1)S(1)} collective-permute-done((bf16[27,8,512]{2,1,0:T(8,128)(2,1)S(1)}, bf16[27,8,512]{2,1,0:T(8,128)(2,1)S(1)}, u32[]{:S(2)}, u32[]{:S(2)}) %collective-permute-start.19) | collective-permute-done | bytes 221216 | tf_op jit(solution)/shard_map/ppermute | solution.py:42
  103.1 0.7 collective-permute-start.22
  103.8 6.8 %collective-permute-done.22 = bf16[27,8,512]{2,1,0:T(8,128)(2,1)S(1)} collective-permute-done((bf16[27,8,512]{2,1,0:T(8,128)(2,1)S(1)}, bf16[27,8,512]{2,1,0:T(8,128)(2,1)S(1)}, u32[]{:S(2)}, u32[]{:S(2)}) %collective-permute-start.22) | collective-permute-done | bytes 221216 | tf_op jit(solution)/shard_map/ppermute | solution.py:434
  110.7 3.0 %collective-permute-start.27 = (f32[14,8,512]{2,1,0:T(8,128)S(1)}, f32[14,8,512]{2,1,0:T(8,128)S(1)}, u32[]{:S(2)}, u32[]{:S(2)}) collective-permute-start(f32[14,8,512]{2,1,0:T(8,128)S(1)} %slice_add_fusion.refs_1_), channel_id=1, source_target_pairs={{0,96},{16,112},{32,0},{48,16},{64,32},{80,48},{96,64},{112,80},{1... | collective-permute-start | bytes 688136 | tf_op jit(solution)/shard_map/ppermute | solution.py:47
  113.6 2.2 %collective-permute-start.23 = (f32[2,8,16,512]{3,2,1,0:T(8,128)S(1)}, f32[2,8,16,512]{3,2,1,0:T(8,128)S(1)}, u32[]{:S(2)}, u32[]{:S(2)}) collective-permute-start(f32[2,8,16,512]{3,2,1,0:T(8,128)S(1)} %get-tuple-element.106), channel_id=1, source_target_pairs={{0,2},{1,3},{2,0},{3,1},{4,6},{5,7},{6,4},{7,5},{8,10},{9,11},{10,... | collective-permute-start | bytes 1572872 | tf_op jit(solution)/shard_map/ppermute | solution.py:34
  116.0 1.1 collective-permute-done.27.refs_5_
  117.2 3.7 %collective-permute-start.29 = (f32[14,8,512]{2,1,0:T(8,128)S(1)}, f32[14,8,512]{2,1,0:T(8,128)S(1)}, u32[]{:S(2)}, u32[]{:S(2)}) collective-permute-start(f32[14,8,512]{2,1,0:T(8,128)S(1)} %collective-permute-done.27.refs_5_), channel_id=1, source_target_pairs={{0,96},{16,112},{32,0},{48,16},{64,32},{80,48},{96,64},{112,80},{1... | collective-permute-start | bytes 688136 | tf_op jit(solution)/shard_map/ppermute | solution.py:47
  120.9 0.3 collective-permute-start.26
  121.2 3.0 %collective-permute-done.24.refs_2_ = f32[13,8,512]{2,1,0:T(8,128)S(1)} collective-permute-done((f32[13,8,512]{2,1,0:T(8,128)S(1)}, f32[13,8,512]{2,1,0:T(8,128)S(1)}, u32[]{:S(2)}, u32[]{:S(2)}) %collective-permute-start.24) | collective-permute-done | bytes 213024 | tf_op jit(solution)/shard_map/ppermute | solution.py:47
  124.2 2.5 %collective-permute-done.26.refs_4_ = f32[13,8,512]{2,1,0:T(8,128)S(1)} collective-permute-done((f32[13,8,512]{2,1,0:T(8,128)S(1)}, f32[13,8,512]{2,1,0:T(8,128)S(1)}, u32[]{:S(2)}, u32[]{:S(2)}) %collective-permute-start.26) | collective-permute-done | bytes 213024 | tf_op jit(solution)/shard_map/ppermute | solution.py:47
  126.7 1.1 collective-permute-done.25.refs_3_
  127.9 3.4 %collective-permute-done.28.refs_6_ = f32[13,8,512]{2,1,0:T(8,128)S(1)} collective-permute-done((f32[13,8,512]{2,1,0:T(8,128)S(1)}, f32[13,8,512]{2,1,0:T(8,128)S(1)}, u32[]{:S(2)}, u32[]{:S(2)}) %collective-permute-start.28) | collective-permute-done | bytes 213024 | tf_op jit(solution)/shard_map/ppermute | solution.py:47
  131.3 1.3 shard_map.58
  132.6 1.2 shard_map.57
  (39 shorter events, 1.5 us)
Async XLA Ops:
  0.6 1.0 copy-start
  1.7 1.0 copy-start.2
  2.9 2.9 %collective-permute-start.1 = (bf16[4,8,16,512]{3,2,1,0:T(8,128)(2,1)S(1)}, bf16[4,8,16,512]{3,2,1,0:T(8,128)(2,1)S(1)}, u32[]{:S(2)}, u32[]{:S(2)}) collective-permute-start(bf16[4,8,16,512]{3,2,1,0:T(8,128)(2,1)S(1)} %get-tuple-element.56.own_act), channel_id=1, source_target_pairs={{0,1},{1,0},{2,3},{3,2},{4,5},{5,4},{6,7},{7,6},{8,9},{9,8},{10,11... | collective-permute-start | bytes 1572872 | tf_op jit(solution)/shard_map/ppermute | solution.py:34
  3.0 16.1 %collective-permute-start.5 = (bf16[4,8,16,512]{3,2,1,0:T(8,128)(2,1)S(1)}, bf16[4,8,16,512]{3,2,1,0:T(8,128)(2,1)S(1)}, u32[]{:S(2)}, u32[]{:S(2)}) collective-permute-start(bf16[4,8,16,512]{3,2,1,0:T(8,128)(2,1)S(1)} %get-tuple-element.56.own_act), channel_id=1, source_target_pairs={{0,2},{1,3},{2,0},{3,1},{4,6},{5,7},{6,4},{7,5},{8,10},{9,11},{10,... | collective-permute-start | bytes 1572872 | tf_op jit(solution)/shard_map/ppermute | solution.py:34
  5.1 0.7 collective-permute-start
  5.7 31.3 %collective-permute-start.10 = (bf16[27,32,512]{2,1,0:T(8,128)(2,1)}, bf16[27,32,512]{2,1,0:T(8,128)(2,1)S(1)}, u32[]{:S(2)}, u32[]{:S(2)}) collective-permute-start(bf16[27,32,512]{2,1,0:T(8,128)(2,1)} %own), channel_id=1, source_target_pairs={{0,4},{1,5},{2,6},{3,7},{4,8},{5,9},{6,10},{7,11},{8,12},{9,13},{1... | collective-permute-start | bytes 2654216 | tf_op jit(solution)/shard_map/ppermute | solution.py:42
  15.2 21.8 %collective-permute-start.9 = (bf16[27,32,512]{2,1,0:T(8,128)(2,1)}, bf16[27,32,512]{2,1,0:T(8,128)(2,1)S(1)}, u32[]{:S(2)}, u32[]{:S(2)}) collective-permute-start(bf16[27,32,512]{2,1,0:T(8,128)(2,1)} %own), channel_id=1, source_target_pairs={{0,12},{1,13},{2,14},{3,15},{4,0},{5,1},{6,2},{7,3},{8,4},{9,5},{1... | collective-permute-start | bytes 2654216 | tf_op jit(solution)/shard_map/ppermute | solution.py:42
  16.6 1.0 copy-start.3
  18.5 2.0 %collective-permute-start.2 = (bf16[5,8,16,128]{3,2,1,0:T(8,128)(2,1)S(1)}, bf16[5,8,16,128]{3,2,1,0:T(8,128)(2,1)S(1)}, u32[]{:S(2)}, u32[]{:S(2)}) collective-permute-start(bf16[5,8,16,128]{3,2,1,0:T(8,128)(2,1)S(1)} %get-tuple-element.59), channel_id=1, source_target_pairs={{0,1},{1,0},{2,3},{3,2},{4,5},{5,4},{6,7},{7,6},{8,9},{9,8},{10,11... | collective-permute-start | bytes 491528 | tf_op jit(solution)/shard_map/ppermute | solution.py:34
  18.6 7.1 %collective-permute-start.3 = (bf16[5,8,16,128]{3,2,1,0:T(8,128)(2,1)S(1)}, bf16[5,8,16,128]{3,2,1,0:T(8,128)(2,1)S(1)}, u32[]{:S(2)}, u32[]{:S(2)}) collective-permute-start(bf16[5,8,16,128]{3,2,1,0:T(8,128)(2,1)S(1)} %get-tuple-element.60), channel_id=1, source_target_pairs={{0,2},{1,3},{2,0},{3,1},{4,6},{5,7},{6,4},{7,5},{8,10},{9,11},{10,... | collective-permute-start | bytes 491528 | tf_op jit(solution)/shard_map/ppermute | solution.py:34
  19.1 9.1 %collective-permute-start.4 = (bf16[5,8,16,128]{3,2,1,0:T(8,128)(2,1)S(1)}, bf16[5,8,16,128]{3,2,1,0:T(8,128)(2,1)S(1)}, u32[]{:S(2)}, u32[]{:S(2)}) collective-permute-start(bf16[5,8,16,128]{3,2,1,0:T(8,128)(2,1)S(1)} %get-tuple-element.61), channel_id=1, source_target_pairs={{0,3},{1,2},{2,1},{3,0},{4,7},{5,6},{6,5},{7,4},{8,11},{9,10},{10,... | collective-permute-start | bytes 491528 | tf_op jit(solution)/shard_map/ppermute | solution.py:34
  28.3 8.8 %collective-permute-start.8 = (bf16[4,8,16,512]{3,2,1,0:T(8,128)(2,1)S(1)}, bf16[4,8,16,512]{3,2,1,0:T(8,128)(2,1)S(1)}, u32[]{:S(2)}, u32[]{:S(2)}) collective-permute-start(bf16[4,8,16,512]{3,2,1,0:T(8,128)(2,1)S(1)} %collective-permute-done.5.far), channel_id=1, source_target_pairs={{0,1},{1,0},{2,3},{3,2},{4,5},{5,4},{6,7},{7,6},{8,9},{9,8},{10,11... | collective-permute-start | bytes 1572872 | tf_op jit(solution)/shard_map/ppermute | solution.py:34
  28.9 6.3 %collective-permute-start.6 = (bf16[4,5,16,128]{3,2,1,0:T(8,128)(2,1)S(1)}, bf16[4,5,16,128]{3,2,1,0:T(8,128)(2,1)S(1)}, u32[]{:S(2)}, u32[]{:S(2)}) collective-permute-start(bf16[4,5,16,128]{3,2,1,0:T(8,128)(2,1)S(1)} %get-tuple-element.66), channel_id=1, source_target_pairs={{0,16},{32,48},{64,80},{96,112},{16,0},{48,32},{80,64},{112,96},{1... | collective-permute-start | bytes 245768 | tf_op jit(solution)/shard_map/ppermute | solution.py:53
  32.6 2.6 %collective-permute-start.7 = (bf16[4,5,16,128]{3,2,1,0:T(8,128)(2,1)S(1)}, bf16[4,5,16,128]{3,2,1,0:T(8,128)(2,1)S(1)}, u32[]{:S(2)}, u32[]{:S(2)}) collective-permute-start(bf16[4,5,16,128]{3,2,1,0:T(8,128)(2,1)S(1)} %get-tuple-element.67), channel_id=1, source_target_pairs={{16,32},{48,64},{80,96},{32,16},{64,48},{96,80},{17,33},{49,65},{8... | collective-permute-start | bytes 245768 | tf_op jit(solution)/shard_map/ppermute | solution.py:53
  37.0 22.0 %copy-start.4 = (bf16[27,32,512]{2,1,0:T(8,128)(2,1)S(1)}, bf16[27,32,512]{2,1,0:T(8,128)(2,1)}, u32[]{:S(2)}) copy-start(bf16[27,32,512]{2,1,0:T(8,128)(2,1)} %own) | copy-start | bytes 2654212
  44.8 14.3 %collective-permute-start.12 = (bf16[14,32,512]{2,1,0:T(8,128)(2,1)S(1)}, bf16[14,32,512]{2,1,0:T(8,128)(2,1)S(1)}, u32[]{:S(2)}, u32[]{:S(2)}) collective-permute-start(bf16[14,32,512]{2,1,0:T(8,128)(2,1)S(1)} %slice.37), channel_id=1, source_target_pairs={{0,12},{1,13},{2,14},{3,15},{4,0},{5,1},{6,2},{7,3},{8,4},{9,5},{1... | collective-permute-start | bytes 1376264 | tf_op jit(solution)/shard_map/ppermute | solution.py:42
  46.9 12.2 %collective-permute-start.11 = (bf16[13,32,512]{2,1,0:T(8,128)(2,1)S(1)}, bf16[13,32,512]{2,1,0:T(8,128)(2,1)S(1)}, u32[]{:S(2)}, u32[]{:S(2)}) collective-permute-start(bf16[13,32,512]{2,1,0:T(8,128)(2,1)S(1)} %slice.36), channel_id=1, source_target_pairs={{0,4},{1,5},{2,6},{3,7},{4,8},{5,9},{6,10},{7,11},{8,12},{9,13},{1... | collective-permute-start | bytes 1277960 | tf_op jit(solution)/shard_map/ppermute | solution.py:42
  47.0 27.0 %collective-permute-start.13 = (bf16[2,27,16,512]{3,2,1,0:T(8,128)(2,1)S(1)}, bf16[2,27,16,512]{3,2,1,0:T(8,128)(2,1)S(1)}, u32[]{:S(2)}, u32[]{:S(2)}) collective-permute-start(bf16[2,27,16,512]{3,2,1,0:T(8,128)(2,1)S(1)} %get-tuple-element.84), channel_id=1, source_target_pairs={{0,32},{16,48},{32,64},{48,80},{64,96},{80,112},{96,0},{112,16},{1... | collective-permute-start | bytes 2654216 | tf_op jit(solution)/shard_map/ppermute | solution.py:47
  54.6 19.6 %collective-permute-start.14 = (bf16[2,27,16,512]{3,2,1,0:T(8,128)(2,1)S(1)}, bf16[2,27,16,512]{3,2,1,0:T(8,128)(2,1)S(1)}, u32[]{:S(2)}, u32[]{:S(2)}) collective-permute-start(bf16[2,27,16,512]{3,2,1,0:T(8,128)(2,1)S(1)} %get-tuple-element.85), channel_id=1, source_target_pairs={{0,96},{16,112},{32,0},{48,16},{64,32},{80,48},{96,64},{112,80},{1... | collective-permute-start | bytes 2654216 | tf_op jit(solution)/shard_map/ppermute | solution.py:47
  74.2 4.2 %collective-permute-start.15 = (f32[2,4,8,16,512]{4,3,2,1,0:T(8,128)S(1)}, f32[2,4,8,16,512]{4,3,2,1,0:T(8,128)S(1)}, u32[]{:S(2)}, u32[]{:S(2)}) collective-permute-start(f32[2,4,8,16,512]{4,3,2,1,0:T(8,128)S(1)} %get-tuple-element.87), channel_id=1, source_target_pairs={{0,1},{1,0},{2,3},{3,2},{4,5},{5,4},{6,7},{7,6},{8,9},{9,8},{10,11... | collective-permute-start | bytes 6291464 | tf_op jit(solution)/shard_map/ppermute | solution.py:34
  74.4 13.9 %collective-permute-start.16 = (bf16[27,16,512]{2,1,0:T(8,128)(2,1)S(1)}, bf16[27,16,512]{2,1,0:T(8,128)(2,1)S(1)}, u32[]{:S(2)}, u32[]{:S(2)}) collective-permute-start(bf16[27,16,512]{2,1,0:T(8,128)(2,1)S(1)} %fusion.1), channel_id=1, source_target_pairs={{0,32},{16,48},{32,64},{48,80},{64,96},{80,112},{96,0},{112,16},{1... | collective-permute-start | bytes 1327112 | tf_op jit(solution)/shard_map/ppermute | solution.py:47
  76.1 12.4 %collective-permute-start.17 = (bf16[27,16,512]{2,1,0:T(8,128)(2,1)S(1)}, bf16[27,16,512]{2,1,0:T(8,128)(2,1)S(1)}, u32[]{:S(2)}, u32[]{:S(2)}) collective-permute-start(bf16[27,16,512]{2,1,0:T(8,128)(2,1)S(1)} %fusion), channel_id=1, source_target_pairs={{0,96},{16,112},{32,0},{48,16},{64,32},{80,48},{96,64},{112,80},{1... | collective-permute-start | bytes 1327112 | tf_op jit(solution)/shard_map/ppermute | solution.py:47
  88.5 14.5 %collective-permute-start.21 = (f32[2,8,16,512]{3,2,1,0:T(8,128)S(1)}, f32[2,8,16,512]{3,2,1,0:T(8,128)S(1)}, u32[]{:S(2)}, u32[]{:S(2)}) collective-permute-start(f32[2,8,16,512]{3,2,1,0:T(8,128)S(1)} %get-tuple-element.99), channel_id=1, source_target_pairs={{0,2},{1,3},{2,0},{3,1},{4,6},{5,7},{6,4},{7,5},{8,10},{9,11},{10,... | collective-permute-start | bytes 1572872 | tf_op jit(solution)/shard_map/ppermute | solution.py:34
  89.0 8.8 %collective-permute-start.18 = (bf16[27,8,512]{2,1,0:T(8,128)(2,1)S(1)}, bf16[27,8,512]{2,1,0:T(8,128)(2,1)S(1)}, u32[]{:S(2)}, u32[]{:S(2)}) collective-permute-start(bf16[27,8,512]{2,1,0:T(8,128)(2,1)S(1)} %get-tuple-element.96), channel_id=1, source_target_pairs={{0,4},{1,5},{2,6},{3,7},{4,8},{5,9},{6,10},{7,11},{8,12},{9,13},{1... | collective-permute-start | bytes 663560 | tf_op jit(solution)/shard_map/ppermute | solution.py:42
  89.3 13.7 %collective-permute-start.19 = (bf16[27,8,512]{2,1,0:T(8,128)(2,1)S(1)}, bf16[27,8,512]{2,1,0:T(8,128)(2,1)S(1)}, u32[]{:S(2)}, u32[]{:S(2)}) collective-permute-start(bf16[27,8,512]{2,1,0:T(8,128)(2,1)S(1)} %get-tuple-element.97), channel_id=1, source_target_pairs={{0,8},{1,9},{2,10},{3,11},{4,12},{5,13},{6,14},{7,15},{8,0},{9,1},... | collective-permute-start | bytes 663560 | tf_op jit(solution)/shard_map/ppermute | solution.py:42
  93.4 9.6 %collective-permute-start.20 = (bf16[27,8,512]{2,1,0:T(8,128)(2,1)S(1)}, bf16[27,8,512]{2,1,0:T(8,128)(2,1)S(1)}, u32[]{:S(2)}, u32[]{:S(2)}) collective-permute-start(bf16[27,8,512]{2,1,0:T(8,128)(2,1)S(1)} %get-tuple-element.98), channel_id=1, source_target_pairs={{0,12},{1,13},{2,14},{3,15},{4,0},{5,1},{6,2},{7,3},{8,4},{9,5},{1... | collective-permute-start | bytes 663560 | tf_op jit(solution)/shard_map/ppermute | solution.py:42
  103.1 7.5 %collective-permute-start.22 = (bf16[27,8,512]{2,1,0:T(8,128)(2,1)S(1)}, bf16[27,8,512]{2,1,0:T(8,128)(2,1)S(1)}, u32[]{:S(2)}, u32[]{:S(2)}) collective-permute-start(bf16[27,8,512]{2,1,0:T(8,128)(2,1)S(1)} %get-tuple-element.108), channel_id=1, source_target_pairs={{0,16},{16,0},{32,48},{48,32},{64,80},{80,64},{96,112},{112,96},{1... | collective-permute-start | bytes 663560 | tf_op jit(solution)/shard_map/ppermute | solution.py:434
  110.7 21.9 %copy-start.1 = (bf16[4,8,16,512]{3,2,1,0:T(8,128)(2,1)S(1)}, bf16[4,8,16,512]{3,2,1,0:T(8,128)(2,1)}, u32[]{:S(2)}) copy-start(bf16[4,8,16,512]{3,2,1,0:T(8,128)(2,1)} %pre.3) | copy-start | bytes 1572868
  110.7 6.5 %collective-permute-start.27 = (f32[14,8,512]{2,1,0:T(8,128)S(1)}, f32[14,8,512]{2,1,0:T(8,128)S(1)}, u32[]{:S(2)}, u32[]{:S(2)}) collective-permute-start(f32[14,8,512]{2,1,0:T(8,128)S(1)} %slice_add_fusion.refs_1_), channel_id=1, source_target_pairs={{0,96},{16,112},{32,0},{48,16},{64,32},{80,48},{96,64},{112,80},{1... | collective-permute-start | bytes 688136 | tf_op jit(solution)/shard_map/ppermute | solution.py:47
  113.6 19.0 %collective-permute-start.23 = (f32[2,8,16,512]{3,2,1,0:T(8,128)S(1)}, f32[2,8,16,512]{3,2,1,0:T(8,128)S(1)}, u32[]{:S(2)}, u32[]{:S(2)}) collective-permute-start(f32[2,8,16,512]{3,2,1,0:T(8,128)S(1)} %get-tuple-element.106), channel_id=1, source_target_pairs={{0,2},{1,3},{2,0},{3,1},{4,6},{5,7},{6,4},{7,5},{8,10},{9,11},{10,... | collective-permute-start | bytes 1572872 | tf_op jit(solution)/shard_map/ppermute | solution.py:34
  115.9 8.3 %collective-permute-start.24 = (f32[13,8,512]{2,1,0:T(8,128)S(1)}, f32[13,8,512]{2,1,0:T(8,128)S(1)}, u32[]{:S(2)}, u32[]{:S(2)}) collective-permute-start(f32[13,8,512]{2,1,0:T(8,128)S(1)} %slice_add_fusion.1.refs_0_), channel_id=1, source_target_pairs={{0,32},{16,48},{32,64},{48,80},{64,96},{80,112},{96,0},{112,16},{1... | collective-permute-start | bytes 638984 | tf_op jit(solution)/shard_map/ppermute | solution.py:47
  115.9 11.9 %collective-permute-start.25 = (f32[14,8,512]{2,1,0:T(8,128)S(1)}, f32[14,8,512]{2,1,0:T(8,128)S(1)}, u32[]{:S(2)}, u32[]{:S(2)}) collective-permute-start(f32[14,8,512]{2,1,0:T(8,128)S(1)} %slice_add_fusion.refs_1_), channel_id=1, source_target_pairs={{0,32},{16,48},{32,64},{48,80},{64,96},{80,112},{96,0},{112,16},{1... | collective-permute-start | bytes 688136 | tf_op jit(solution)/shard_map/ppermute | solution.py:47
  117.2 14.1 %collective-permute-start.29 = (f32[14,8,512]{2,1,0:T(8,128)S(1)}, f32[14,8,512]{2,1,0:T(8,128)S(1)}, u32[]{:S(2)}, u32[]{:S(2)}) collective-permute-start(f32[14,8,512]{2,1,0:T(8,128)S(1)} %collective-permute-done.27.refs_5_), channel_id=1, source_target_pairs={{0,96},{16,112},{32,0},{48,16},{64,32},{80,48},{96,64},{112,80},{1... | collective-permute-start | bytes 688136 | tf_op jit(solution)/shard_map/ppermute | solution.py:47
  120.9 5.9 %collective-permute-start.26 = (f32[13,8,512]{2,1,0:T(8,128)S(1)}, f32[13,8,512]{2,1,0:T(8,128)S(1)}, u32[]{:S(2)}, u32[]{:S(2)}) collective-permute-start(f32[13,8,512]{2,1,0:T(8,128)S(1)} %slice_add_fusion.1.refs_0_), channel_id=1, source_target_pairs={{0,96},{16,112},{32,0},{48,16},{64,32},{80,48},{96,64},{112,80},{1... | collective-permute-start | bytes 638984 | tf_op jit(solution)/shard_map/ppermute | solution.py:47
  124.2 7.1 %collective-permute-start.28 = (f32[13,8,512]{2,1,0:T(8,128)S(1)}, f32[13,8,512]{2,1,0:T(8,128)S(1)}, u32[]{:S(2)}, u32[]{:S(2)}) collective-permute-start(f32[13,8,512]{2,1,0:T(8,128)S(1)} %collective-permute-done.24.refs_2_), channel_id=1, source_target_pairs={{0,32},{16,48},{32,64},{48,80},{64,96},{80,112},{96,0},{112,16},{1... | collective-permute-start | bytes 638984 | tf_op jit(solution)/shard_map/ppermute | solution.py:47

commit v7 on v6

--- a/solution.py
+++ b/solution.py
@@ -10,6 +10,7 @@
 
 QUAD = 4
 RING = 4
+XTAPS = 13
 F32 = jnp.float32
 BF16 = jnp.bfloat16
 ANY = pl.BlockSpec(memory_space=pl.ANY)
@@ -27,6 +28,10 @@
 
 def x_place():
     return lax.div(lax.axis_index("gx"), 2)
+
+
+def y_place():
+    return lax.div(lax.axis_index("gy"), QUAD)
 
 
 def swap(block, k):
@@ -152,7 +157,8 @@
     place = lax.broadcasted_iota(jnp.int32, (q, q), 0)
     source = lax.broadcasted_iota(jnp.int32, (q, q), 1)
     xpart = lax.rem(lax.div(place, part) + x, RING)
-    base = lax.div(lax.rem(place, part), small) * part + xpart * small + lax.rem(place, small)
+    ypart = lax.rem(lax.div(lax.rem(place, part), small) + y_place(), RING)
+    base = ypart * part + xpart * small + lax.rem(place, small)
     order = jnp.where(source == base, 1.0, 0.0).astype(BF16)
     z = lax.rem(lax.broadcasted_iota(jnp.int32, (q, cells), 1), depth)
     for b in (-1, 0, 1):
@@ -191,7 +197,7 @@
 
 
 def weight_kernel(norm, own_act, near, far, across, cot, *refs):
-    right, left, keep_right, keep_left, own, held, sem = refs
+    groups, held, sem = (refs[:5], refs[5:10]), *refs[10:]
     j = quad_place()
     rows, width, depth, chan = own_act.shape
     pairs = []
@@ -203,25 +209,28 @@
     cells = QUAD * rows * row
     act = held[...].reshape(cells, chan)
     q = cot.shape[0] // 9
-    part = q // RING
-    half = part // 2
+    small = q // RING // RING
     for n in range(9):
         a, b = n // 3 - 1, n % 3
         moved = cot[3 * b * q:3 * (b + 1) * q, (1 - a) * row:(1 - a) * row + cells]
         term = jnp.dot(moved, act, preferred_element_type=F32) * norm
         for c in range(3):
             tap = 3 * n + c
+            by_y = tap >= XTAPS
+            up, down, keep_up, keep_down, own = groups[by_y]
+            tap -= XTAPS * by_y
 
             def block(r, h):
-                at = c * q + r * part + h * half
-                return term[at:at + half]
-
-            right[0, tap] = block(2, 0).astype(BF16)
-            left[0, tap] = block(2, 1).astype(BF16)
-            keep_right[tap] = block(1, 0)
-            right[1, tap] = block(1, 1).astype(BF16)
-            left[1, tap] = block(3, 0).astype(BF16)
-            keep_left[tap] = block(3, 1)
+                spots = [(2 * h, r), (2 * h + 1, r)] if by_y else [(r, 2 * h), (r, 2 * h + 1)]
+                starts = [c * q + (xr * RING + yr) * small for xr, yr in spots]
+                return jnp.concatenate([term[at:at + small] for at in starts], axis=0)
+
+            up[0, tap] = block(2, 0).astype(BF16)
+            down[0, tap] = block(2, 1).astype(BF16)
+            keep_up[tap] = block(1, 0)
+            up[1, tap] = block(1, 1).astype(BF16)
+            down[1, tap] = block(3, 0).astype(BF16)
+            keep_down[tap] = block(3, 1)
             own[0, tap] = block(0, 0)
             own[1, tap] = block(0, 1)
 
@@ -229,15 +238,18 @@
 def weight_terms(norm, acts, cot):
     rows, width, depth, chan = acts[0].shape
     q = chan // QUAD
-    shape = (27, q // RING // 2, chan)
     cells = QUAD * rows * width * depth
+    shapes = []
+    for taps in (XTAPS, 27 - XTAPS):
+        shape = (taps, q // RING // 2, chan)
+        shapes += [jax.ShapeDtypeStruct((2,) + shape, BF16)] * 2
+        shapes += [jax.ShapeDtypeStruct(shape, F32)] * 2
+        shapes += [jax.ShapeDtypeStruct((2,) + shape, F32)]
     return pl.pallas_call(
         functools.partial(weight_kernel, norm),
-        out_shape=[jax.ShapeDtypeStruct((2,) + shape, BF16)] * 2
-        + [jax.ShapeDtypeStruct(shape, F32)] * 2
-        + [jax.ShapeDtypeStruct((2,) + shape, F32)],
+        out_shape=shapes,
         in_specs=[ANY] * 4 + [VMEM],
-        out_specs=[VMEM] * 5,
+        out_specs=[VMEM] * 10,
         scratch_shapes=[
             pltpu.VMEM((QUAD * rows, width, depth, chan), BF16),
             pltpu.SemaphoreType.DMA((4,)),
@@ -252,7 +264,7 @@
 def input_kernel(held, own, above, across_low, across_high, below, *refs):
     send, keep, pass_on, weights, sem = refs
     j = quad_place()
-    y = lax.div(lax.axis_index("gy"), QUAD)
+    y = y_place()
     part = own.shape[1]
     low = across_low.shape[0]
 
@@ -312,47 +324,63 @@
     )(held, *parts)
 
 
-def finish_kernel(pre, keep, near, far_low, far_high, out):
-    rows = far_low.shape[0]
-    for at, far in ((0, far_low), (rows, far_high)):
-        value = pre[at:at + rows].astype(F32)
-        s = jax.nn.sigmoid(value)
-        grad = keep[at:at + rows] + near[0, at:at + rows] + far[...]
-        out[at:at + rows] = (grad * s * (1.0 + value * (1.0 - s))).astype(BF16)
-
-
-def finish(pre_act, keep, near, *far):
+def finish_kernel(pre, keep, near, far, out):
+    value = pre[...].astype(F32)
+    s = jax.nn.sigmoid(value)
+    grad = keep[...] + near[0] + far[...]
+    out[...] = (grad * s * (1.0 + value * (1.0 - s))).astype(BF16)
+
+
+def finish(pre_act, keep, near, far):
     return pl.pallas_call(
         finish_kernel,
         out_shape=jax.ShapeDtypeStruct(pre_act.shape, BF16),
-        in_specs=[VMEM] * 5,
+        in_specs=[VMEM] * 4,
         out_specs=VMEM,
         compiler_params=params(),
-    )(pre_act, keep, near, *far)
-
-
-def split_kernel(own, from_left, from_right, last_left, last_right, *refs):
-    outs, total = refs[:-1], refs[-1]
-    y = lax.div(lax.axis_index("gy"), QUAD)
-    size = own.shape[2] // 2
-    low = own[0] + from_right[1].astype(F32) + last_left[...].astype(F32)
-    high = own[1] + from_left[1].astype(F32) + last_right[...].astype(F32)
-    for half, value in enumerate((low, high)):
-        for sub in range(2):
-            total[2 * half + sub] = value[:, sub * size:(sub + 1) * size]
-    for r, out in enumerate(outs):
-        out[...] = total[lax.rem(y + r, RING)].astype(out.dtype)
+    )(pre_act, keep, near, far)
+
+
+def next_kernel(*refs):
+    for n, out in enumerate(refs[8:]):
+        came, keep = refs[2 * n:2 * n + 2]
+        out[...] = (came[0].astype(F32) + keep[...]).astype(BF16)
+
+
+def next_step(*parts):
+    keeps = parts[1::2]
+    return pl.pallas_call(
+        next_kernel,
+        out_shape=[jax.ShapeDtypeStruct(k.shape, BF16) for k in keeps],
+        in_specs=[VMEM] * 8,
+        out_specs=[VMEM] * 4,
+        compiler_params=params(),
+    )(*parts)
+
+
+def split_kernel(*refs):
+    for group in range(2):
+        own, from_low, from_high, last_low, last_high = refs[5 * group:5 * group + 5]
+        outs = refs[10 + 4 * group:14 + 4 * group]
+        size = own.shape[2] // 2
+        low = own[0] + from_high[1].astype(F32) + last_low[...].astype(F32)
+        high = own[1] + from_low[1].astype(F32) + last_high[...].astype(F32)
+        blocks = (low[:, :size], low[:, size:], high[:, :size], high[:, size:])
+        for block, out in zip(blocks, outs):
+            out[...] = block.astype(out.dtype)
 
 
 def split(*parts):
-    _, taps, rows, chan = parts[0].shape
-    shape = (taps, rows // 2, chan)
+    shapes = []
+    for own in parts[::5]:
+        _, taps, rows, chan = own.shape
+        shape = (taps, rows // 2, chan)
+        shapes += [jax.ShapeDtypeStruct(shape, F32)] + [jax.ShapeDtypeStruct(shape, BF16)] * 3
     return pl.pallas_call(
         split_kernel,
-        out_shape=[jax.ShapeDtypeStruct(shape, F32)] + [jax.ShapeDtypeStruct(shape, BF16)] * 3,
-        in_specs=[VMEM] * 5,
-        out_specs=[VMEM] * 4,
-        scratch_shapes=[pltpu.VMEM((RING,) + shape, F32)],
+        out_shape=shapes,
+        in_specs=[VMEM] * 10,
+        out_specs=[VMEM] * 8,
         compiler_params=params(),
     )(*parts)
 
@@ -404,39 +432,45 @@
     quarters, far = barrier((quarters, far))
     acts = [act, near, far, swap(far, 1)]
     even, odd = sides(quarters)
-    held, turned = turn(quarters, swap_x(even, 0), swap_x(odd, 1))
-
-    turned, above, below = barrier((turned, above, below))
-    right, left, *kept = weight_terms(norm, acts, turned)
-    held, right, left, above, below = barrier((held, right, left, above, below))
-    taps = 13
+    even, odd = swap_x(even, 0), swap_x(odd, 1)
+    even, odd, above, below = barrier((even, odd, above, below))
+    taps = XTAPS
     parts = [weight, above, along_y(below[:taps], 1, True), along_y(above[taps:], -1, True), below]
-    from_left, from_right = along_x(right, 1), along_x(left, -1)
+    held, turned = turn(quarters, even, odd)
+
+    terms = weight_terms(norm, acts, turned)
+    held, terms = barrier((held, terms))
+    xup, xdown, xkeep_up, xkeep_down, xown = terms[:5]
+    yup, ydown, ykeep_up, ykeep_down, yown = terms[5:]
+    xlow, xhigh = along_x(xup, 1), along_x(xdown, -1)
+    ylow, yhigh = along_y(yup, 1, True), along_y(ydown, -1, True)
     grads = input_terms(held, parts)
-    grads, from_left, from_right = barrier((grads, from_left, from_right))
+    grads, xlow, xhigh, ylow, yhigh = barrier((grads, xlow, xhigh, ylow, yhigh))
     send, keep, pass_on = grads
     got = swap(send, 1)
-    keep_right, keep_left, own = kept
-    right = (from_left[0].astype(F32) + keep_right).astype(BF16)
-    left = (from_right[0].astype(F32) + keep_left).astype(BF16)
-    last_left, last_right = along_x(right, 1), along_x(left, -1)
-    half = rows // 2
-    passed = [pass_on[s] + got[1, s] for s in (slice(0, half), slice(half, rows))]
-    last_left, last_right, passed = barrier((last_left, last_right, passed))
-    far_low = swap(passed[0], 2)
-    mine, *others = split(own, from_left, from_right, last_left, last_right)
-
-    others = [along_y(block, r, True) for r, block in zip((1, 2, 3), others)]
-    others, far_low = barrier((others, far_low))
-    for other in others:
-        mine = mine + other.astype(F32)
+    xup, xdown, yup, ydown = next_step(
+        xlow, xkeep_up, xhigh, xkeep_down, ylow, ykeep_up, yhigh, ykeep_down
+    )
+    xlast = along_x(xup, 1), along_x(xdown, -1)
+    ylast = along_y(yup, 1, True), along_y(ydown, -1, True)
+    xlast, ylast, got = barrier((xlast, ylast, got))
+    blocks = split(xown, xlow, xhigh, *xlast, yown, ylow, yhigh, *ylast)
+
+    low, high = blocks[0], blocks[4]
+    lows = [along_y(block, r, True) for r, block in zip((1, 2, 3), blocks[1:4])]
+    highs = [along_x(block, r) for r, block in zip((1, 2, 3), blocks[5:])]
+    for other in lows:
+        low = low + other.astype(F32)
+    for other in highs:
+        high = high + other.astype(F32)
     count = lax.axis_size("gx")
-    other = lax.ppermute(mine.astype(BF16), "gx", [(g, g ^ 1) for g in range(count)])
-    other, passed = barrier((other, passed))
-    far_high = swap(passed[1], 2)
-    low, high = [mine[s] + other[s].astype(F32) for s in (slice(0, taps), slice(taps, 27))]
+    mine = jnp.concatenate([low.astype(BF16), high.astype(BF16)])
+    other = lax.ppermute(mine, "gx", [(g, g ^ 1) for g in range(count)])
+    other, passed = barrier((other, pass_on + got[1]))
+    far_grad = swap(passed, 2)
+    low, high = low + other[:taps].astype(F32), high + other[taps:].astype(F32)
     grad_weight = gather_x(low, high)
-    grad_pre = finish(pre_act, keep, got, far_low, far_high)
+    grad_pre = finish(pre_act, keep, got, far_grad)
     return (grad_pre, grad_weight)
 
 

time: 135 us -> 126 us (0.933)
  waiting for transfers between devices: 56.8 us -> 41.4 us
  starting transfers between devices: 49.9 us -> 56.3 us
    ppermute x7 -> x11, waiting for transfers between devices: 12.3 us -> 2.38 us  [along_y(): lax.ppermute(block, 'gy', [(s, t) for s, t in pairs if 0 <= t < count])]
    ppermute x10 -> x13, waiting for transfers between devices: 27.5 us -> 20.1 us  [along_x(): lax.ppermute(block, 'gx', [(g, (g + 2 * step) % count) for g in range(cou...]
    ppermute x7 -> x11, starting transfers between devices: 17.6 us -> 23.4 us  [along_y(): lax.ppermute(block, 'gy', [(s, t) for s, t in pairs if 0 <= t < count])]
    ppermute x10 -> x13, starting transfers between devices: 19.7 us -> 22.6 us  [along_x(): lax.ppermute(block, 'gx', [(g, (g + 2 * step) % count) for g in range(cou...]
    ppermute x1, waiting for transfers between devices: 6.8 us -> 9.16 us  [body(): other = lax.ppermute(mine, 'gx', [(g, g ^ 1) for g in range(count)])]
    ppermute x9 -> x8, starting transfers between devices: 6.92 us -> 4.78 us  [swap(): return lax.ppermute(block, 'gy', [(g, g ^ k) for g in range(count)])]
    ppermute x9 -> x8, waiting for transfers between devices: 8.26 us -> 7.8 us  [swap(): return lax.ppermute(block, 'gy', [(g, g ^ k) for g in range(count)])]
    pallas_call x2 -> x3, Pallas kernels: 8.2 us -> 8.07 us  [the longest x1 7.66 us: weight_terms(): pl.pallas_call(functools.partial(weight_kernel, norm), out_shape=shapes,...]
  transfers between devices with their start and end apart: 30 -> 36, of which waited for: 17 -> 13; matrix products, arithmetic and copies ran while one was open for 0% -> 0% of each run, Pallas kernels for 10% -> 16%
where the time goes in v7:
time: 126 us; the launch traced here: 124 us
  starting transfers between devices  56.3 us (45%)
  waiting for transfers between devices  41.4 us (33%)
  Pallas kernels  22.1 us (18%)
  local copies, waits for them, and re-layouts  3.19 us (3%)
    ppermute x11, starting transfers between devices, along_y(): lax.ppermute(block, 'gy', [(s, t) for s, t in pairs if 0 <= t < count])  23.4 us
    ppermute x13, starting transfers between devices, along_x(): lax.ppermute(block, 'gx', [(g, (g + 2 * step) % count) for g in range(cou...  22.6 us
    ppermute x13, waiting for transfers between devices, along_x(): lax.ppermute(block, 'gx', [(g, (g + 2 * step) % count) for g in range(cou...  20.1 us
    ppermute x1, waiting for transfers between devices, body(): other = lax.ppermute(mine, 'gx', [(g, g ^ 1) for g in range(count)])  9.16 us
    pallas_call x1, Pallas kernels, input_terms(): pl.pallas_call(input_kernel, out_shape=[jax.ShapeDtypeStruct((2,) + block...  8.65 us
    ppermute x8, waiting for transfers between devices, swap(): return lax.ppermute(block, 'gy', [(g, g ^ k) for g in range(count)])  7.8 us
    pallas_call x1, Pallas kernels, weight_terms(): pl.pallas_call(functools.partial(weight_kernel, norm), out_shape=shapes,...  7.66 us
    ppermute x8, starting transfers between devices, swap(): return lax.ppermute(block, 'gy', [(g, g ^ k) for g in range(count)])  4.78 us
  transfers between devices with their start and end apart: 36, of which 13 were waited for; matrix products, arithmetic and copies ran while one was open for 0% of the time, Pallas kernels for 16%

profile of v7, /device:TPU:0, one launch (start us, length us, event | category | flops | bytes accessed | tf_op | source)
XLA Modules:
  0.0 124.4 jit_solution(7394582527119629131)
XLA Ops:
  0.6 1.0 copy-done
  1.7 1.0 copy-done.2
  3.0 2.1 %collective-permute-start.5 = (bf16[4,8,16,512]{3,2,1,0:T(8,128)(2,1)S(1)}, bf16[4,8,16,512]{3,2,1,0:T(8,128)(2,1)S(1)}, u32[]{:S(2)}, u32[]{:S(2)}) collective-permute-start(bf16[4,8,16,512]{3,2,1,0:T(8,128)(2,1)S(1)} %get-tuple-element.75.own_act), channel_id=1, source_target_pairs={{0,2},{1,3},{2,0},{3,1},{4,6},{5,7},{6,4},{7,5},{8,10},{9,11},{10,... | collective-permute-start | bytes 1572872 | tf_op jit(solution)/shard_map/ppermute | solution.py:39
  5.1 0.7 collective-permute-start
  5.7 10.9 %collective-permute-start.8 = (bf16[27,32,512]{2,1,0:T(8,128)(2,1)}, bf16[27,32,512]{2,1,0:T(8,128)(2,1)S(1)}, u32[]{:S(2)}, u32[]{:S(2)}) collective-permute-start(bf16[27,32,512]{2,1,0:T(8,128)(2,1)} %own), channel_id=1, source_target_pairs={{0,12},{1,13},{2,14},{3,15},{4,0},{5,1},{6,2},{7,3},{8,4},{9,5},{1... | collective-permute-start | bytes 2654216 | tf_op jit(solution)/shard_map/ppermute | solution.py:47
  16.7 1.0 copy-done.3
  17.7 0.9 shard_map.51
  18.8 1.8 %collective-permute-start.4 = (bf16[5,8,16,128]{3,2,1,0:T(8,128)(2,1)S(1)}, bf16[5,8,16,128]{3,2,1,0:T(8,128)(2,1)S(1)}, u32[]{:S(2)}, u32[]{:S(2)}) collective-permute-start(bf16[5,8,16,128]{3,2,1,0:T(8,128)(2,1)S(1)} %get-tuple-element.80), channel_id=1, source_target_pairs={{0,3},{1,2},{2,1},{3,0},{4,7},{5,6},{6,5},{7,4},{8,11},{9,10},{10,... | collective-permute-start | bytes 491528 | tf_op jit(solution)/shard_map/ppermute | solution.py:39
  20.5 5.2 %collective-permute-done.3.p2 = bf16[5,8,16,128]{3,2,1,0:T(8,128)(2,1)S(1)} collective-permute-done((bf16[5,8,16,128]{3,2,1,0:T(8,128)(2,1)S(1)}, bf16[5,8,16,128]{3,2,1,0:T(8,128)(2,1)S(1)}, u32[]{:S(2)}, u32[]{:S(2)}) %collective-permute-start.3) | collective-permute-done | bytes 163872 | tf_op jit(solution)/shard_map/ppermute | solution.py:39
  25.7 2.6 %collective-permute-done.4.p3 = bf16[5,8,16,128]{3,2,1,0:T(8,128)(2,1)S(1)} collective-permute-done((bf16[5,8,16,128]{3,2,1,0:T(8,128)(2,1)S(1)}, bf16[5,8,16,128]{3,2,1,0:T(8,128)(2,1)S(1)}, u32[]{:S(2)}, u32[]{:S(2)}) %collective-permute-start.4) | collective-permute-done | bytes 163872 | tf_op jit(solution)/shard_map/ppermute | solution.py:39
  28.3 0.6 collective-permute-start.10
  28.9 3.7 %collective-permute-start.6 = (bf16[4,5,16,128]{3,2,1,0:T(8,128)(2,1)S(1)}, bf16[4,5,16,128]{3,2,1,0:T(8,128)(2,1)S(1)}, u32[]{:S(2)}, u32[]{:S(2)}) collective-permute-start(bf16[4,5,16,128]{3,2,1,0:T(8,128)(2,1)S(1)} %get-tuple-element.85), channel_id=1, source_target_pairs={{0,16},{32,48},{64,80},{96,112},{16,0},{48,32},{80,64},{112,96},{1... | collective-permute-start | bytes 245768 | tf_op jit(solution)/shard_map/ppermute | solution.py:58
  32.6 0.7 collective-permute-start.7
  33.3 2.0 %collective-permute-done.6.even = bf16[4,5,16,128]{3,2,1,0:T(8,128)(2,1)S(1)} collective-permute-done((bf16[4,5,16,128]{3,2,1,0:T(8,128)(2,1)S(1)}, bf16[4,5,16,128]{3,2,1,0:T(8,128)(2,1)S(1)}, u32[]{:S(2)}, u32[]{:S(2)}) %collective-permute-start.6) | collective-permute-done | bytes 81952 | tf_op jit(solution)/shard_map/ppermute | solution.py:58
  35.3 0.2 collective-permute-start.11
  35.5 3.2 %collective-permute-start.12 = (bf16[14,32,512]{2,1,0:T(8,128)(2,1)S(1)}, bf16[14,32,512]{2,1,0:T(8,128)(2,1)S(1)}, u32[]{:S(2)}, u32[]{:S(2)}) collective-permute-start(bf16[14,32,512]{2,1,0:T(8,128)(2,1)S(1)} %slice.16), channel_id=1, source_target_pairs={{0,12},{1,13},{2,14},{3,15},{4,0},{5,1},{6,2},{7,3},{8,4},{9,5},{1... | collective-permute-start | bytes 1376264 | tf_op jit(solution)/shard_map/ppermute | solution.py:47
  38.7 1.8 %shard_map.53 = (bf16[18,10,16,128]{3,2,1,0:T(8,128)(2,1)S(1)}, bf16[1152,2304]{1,0:T(8,128)(2,1)S(1)}) custom-call(bf16[5,8,16,128]{3,2,1,0:T(8,128)(2,1)S(1)} %get-tuple-element.81.p0, bf16[5,8,16,128]{3,2,1,0:T(8,128)(2,1)S(1)} %collective-permute-done.2.p1, bf16[5,8,16,128]{3,2,1,0:T(8,128)(2,1)S(1)} %collective-permute-done.3.p2, ...), custom_call_target="tpu_custom_call" | custom-call | tf_op jit(solution)/shard_map/pallas_call | solution.py:180
  40.5 7.7 %shard_map.54 = (bf16[2,13,16,512]{3,2,1,0:T(8,128)(2,1)S(1)}, bf16[2,13,16,512]{3,2,1,0:T(8,128)(2,1)S(1)}, f32[13,16,512]{2,1,0:T(8,128)S(1)}, f32[13,16,512]{...) custom-call(bf16[4,8,16,512]{3,2,1,0:T(8,128)(2,1)S(1)} %get-tuple-e, ...), custom_call_target="tpu_custom_call" | custom-call | flops 7247757312 | bytes 10000000 | tf_op jit(solution)/shard_map/pallas_call | solution.py:248
  48.2 7.7 %collective-permute-start.13 = (bf16[2,13,16,512]{3,2,1,0:T(8,128)(2,1)S(1)}, bf16[2,13,16,512]{3,2,1,0:T(8,128)(2,1)S(1)}, u32[]{:S(2)}, u32[]{:S(2)}) collective-permute-start(bf16[2,13,16,512]{3,2,1,0:T(8,128)(2,1)S(1)} %get-tuple-element.110), channel_id=1, source_target_pairs={{0,32},{16,48},{32,64},{48,80},{64,96},{80,112},{96,0},{112,16},{1... | collective-permute-start | bytes 1277960 | tf_op jit(solution)/shard_map/ppermute | solution.py:52
  55.9 1.4 %collective-permute-start.14 = (bf16[2,13,16,512]{3,2,1,0:T(8,128)(2,1)S(1)}, bf16[2,13,16,512]{3,2,1,0:T(8,128)(2,1)S(1)}, u32[]{:S(2)}, u32[]{:S(2)}) collective-permute-start(bf16[2,13,16,512]{3,2,1,0:T(8,128)(2,1)S(1)} %get-tuple-element.111), channel_id=1, source_target_pairs={{0,96},{16,112},{32,0},{48,16},{64,32},{80,48},{96,64},{112,80},{1... | collective-permute-start | bytes 1277960 | tf_op jit(solution)/shard_map/ppermute | solution.py:52
  57.2 3.2 %collective-permute-start.16 = (bf16[2,14,16,512]{3,2,1,0:T(8,128)(2,1)S(1)}, bf16[2,14,16,512]{3,2,1,0:T(8,128)(2,1)S(1)}, u32[]{:S(2)}, u32[]{:S(2)}) collective-permute-start(bf16[2,14,16,512]{3,2,1,0:T(8,128)(2,1)S(1)} %get-tuple-element.113), channel_id=1, source_target_pairs={{0,12},{1,13},{2,14},{3,15},{4,0},{5,1},{6,2},{7,3},{8,4},{9,5},{1... | collective-permute-start | bytes 1376264 | tf_op jit(solution)/shard_map/ppermute | solution.py:47
  60.5 8.6 %shard_map.55 = (f32[2,4,8,16,512]{4,3,2,1,0:T(8,128)S(1)}, f32[4,8,16,512]{3,2,1,0:T(8,128)S(1)}, f32[4,8,16,512]{3,2,1,0:T(8,128)S(1)}) custom-call(bf16[18,10,16,128]{3,2,1,0:T(8,128)(2,1)S(1)} %get-tuple-element.104.held, bf16[27,32,512]{2,1,0:T(8,128)(2,1)S(1)} %copy-done.4, bf16[27,32,512]{2,1,0:T(8,128)(2,1)S(1)} %collective-permute-done.8.above, ...), custom_call_target="tpu_custom_call" | custom-call | flops 10192158720 | bytes 10000000 | tf_op jit(solution)/shard_map/pallas_call | solution.py:310
  69.5 3.2 %collective-permute-start.20 = (bf16[14,16,512]{2,1,0:T(8,128)(2,1)S(1)}, bf16[14,16,512]{2,1,0:T(8,128)(2,1)S(1)}, u32[]{:S(2)}, u32[]{:S(2)}) collective-permute-start(bf16[14,16,512]{2,1,0:T(8,128)(2,1)S(1)} %get-tuple-element.126), channel_id=1, source_target_pairs={{0,12},{1,13},{2,14},{3,15},{4,0},{5,1},{6,2},{7,3},{8,4},{9,5},{1... | collective-permute-start | bytes 688136 | tf_op jit(solution)/shard_map/ppermute | solution.py:47
  72.7 0.7 collective-permute-start.17
  73.4 2.6 %collective-permute-start.18 = (bf16[13,16,512]{2,1,0:T(8,128)(2,1)S(1)}, bf16[13,16,512]{2,1,0:T(8,128)(2,1)S(1)}, u32[]{:S(2)}, u32[]{:S(2)}) collective-permute-start(bf16[13,16,512]{2,1,0:T(8,128)(2,1)S(1)} %get-tuple-element.124), channel_id=1, source_target_pairs={{0,96},{16,112},{32,0},{48,16},{64,32},{80,48},{96,64},{112,80},{1... | collective-permute-start | bytes 638984 | tf_op jit(solution)/shard_map/ppermute | solution.py:52
  76.0 5.1 %collective-permute-done.17.refs_3_ = bf16[13,16,512]{2,1,0:T(8,128)(2,1)S(1)} collective-permute-done((bf16[13,16,512]{2,1,0:T(8,128)(2,1)S(1)}, bf16[13,16,512]{2,1,0:T(8,128)(2,1)S(1)}, u32[]{:S(2)}, u32[]{:S(2)}) %collective-permute-start.17) | collective-permute-done | bytes 213024 | tf_op jit(solution)/shard_map/ppermute | solution.py:52
  81.0 0.3 shard_map.57
  81.3 1.4 %collective-permute-start.24 = (bf16[13,8,512]{2,1,0:T(8,128)(2,1)S(1)}, bf16[13,8,512]{2,1,0:T(8,128)(2,1)S(1)}, u32[]{:S(2)}, u32[]{:S(2)}) collective-permute-start(bf16[13,8,512]{2,1,0:T(8,128)(2,1)S(1)} %get-tuple-element.138), channel_id=1, source_target_pairs={{0,12},{1,13},{2,14},{3,15},{4,0},{5,1},{6,2},{7,3},{8,4},{9,5},{1... | collective-permute-start | bytes 319496 | tf_op jit(solution)/shard_map/ppermute | solution.py:47
  82.7 1.1 collective-permute-start.22
  83.8 2.9 %collective-permute-start.27 = (bf16[14,8,512]{2,1,0:T(8,128)(2,1)S(1)}, bf16[14,8,512]{2,1,0:T(8,128)(2,1)S(1)}, u32[]{:S(2)}, u32[]{:S(2)}) collective-permute-start(bf16[14,8,512]{2,1,0:T(8,128)(2,1)S(1)} %get-tuple-element.142), channel_id=1, source_target_pairs={{0,96},{16,112},{32,0},{48,16},{64,32},{80,48},{96,64},{112,80},{1... | collective-permute-start | bytes 344072 | tf_op jit(solution)/shard_map/ppermute | solution.py:52
  86.8 0.9 collective-permute-start.25
  87.6 1.5 %collective-permute-done.23 = bf16[13,8,512]{2,1,0:T(8,128)(2,1)S(1)} collective-permute-done((bf16[13,8,512]{2,1,0:T(8,128)(2,1)S(1)}, bf16[13,8,512]{2,1,0:T(8,128)(2,1)S(1)}, u32[]{:S(2)}, u32[]{:S(2)}) %collective-permute-start.23) | collective-permute-done | bytes 106528 | tf_op jit(solution)/shard_map/ppermute | solution.py:47
  89.1 0.9 collective-permute-done.22
  90.1 0.3 collective-permute-done.27
  90.4 2.8 %collective-permute-done.26 = bf16[14,8,512]{2,1,0:T(8,128)(2,1)S(1)} collective-permute-done((bf16[14,8,512]{2,1,0:T(8,128)(2,1)S(1)}, bf16[14,8,512]{2,1,0:T(8,128)(2,1)S(1)}, u32[]{:S(2)}, u32[]{:S(2)}) %collective-permute-start.26) | collective-permute-done | bytes 114720 | tf_op jit(solution)/shard_map/ppermute | solution.py:52
  93.2 0.8 collective-permute-done.25
  94.1 0.5 collective-permute-start.28
  94.6 0.2 bitcast_add_fusion
  94.8 9.2 %collective-permute-done.28 = bf16[27,8,512]{2,1,0:T(8,128)(2,1)S(1)} collective-permute-done((bf16[27,8,512]{2,1,0:T(8,128)(2,1)S(1)}, bf16[27,8,512]{2,1,0:T(8,128)(2,1)S(1)}, u32[]{:S(2)}, u32[]{:S(2)}) %collective-permute-start.28) | collective-permute-done | bytes 221216 | tf_op jit(solution)/shard_map/ppermute | solution.py:468
  104.1 1.0 collective-permute-start.33
  105.1 1.2 collective-permute-start.30
  106.4 6.0 %collective-permute-done.33.refs_5_ = f32[14,8,512]{2,1,0:T(8,128)S(1)} collective-permute-done((f32[14,8,512]{2,1,0:T(8,128)S(1)}, f32[14,8,512]{2,1,0:T(8,128)S(1)}, u32[]{:S(2)}, u32[]{:S(2)}) %collective-permute-start.33) | collective-permute-done | bytes 229408 | tf_op jit(solution)/shard_map/ppermute | solution.py:52
  112.4 2.3 %collective-permute-start.35 = (f32[14,8,512]{2,1,0:T(8,128)S(1)}, f32[14,8,512]{2,1,0:T(8,128)S(1)}, u32[]{:S(2)}, u32[]{:S(2)}) collective-permute-start(f32[14,8,512]{2,1,0:T(8,128)S(1)} %collective-permute-done.33.refs_5_), channel_id=1, source_target_pairs={{0,96},{16,112},{32,0},{48,16},{64,32},{80,48},{96,64},{112,80},{1... | collective-permute-start | bytes 688136 | tf_op jit(solution)/shard_map/ppermute | solution.py:52
  114.8 2.0 %collective-permute-start.34 = (f32[13,8,512]{2,1,0:T(8,128)S(1)}, f32[13,8,512]{2,1,0:T(8,128)S(1)}, u32[]{:S(2)}, u32[]{:S(2)}) collective-permute-start(f32[13,8,512]{2,1,0:T(8,128)S(1)} %collective-permute-done.30.refs_2_), channel_id=1, source_target_pairs={{0,32},{16,48},{32,64},{48,80},{64,96},{80,112},{96,0},{112,16},{1... | collective-permute-start | bytes 638984 | tf_op jit(solution)/shard_map/ppermute | solution.py:52
  116.8 4.0 %collective-permute-done.32.refs_4_ = f32[13,8,512]{2,1,0:T(8,128)S(1)} collective-permute-done((f32[13,8,512]{2,1,0:T(8,128)S(1)}, f32[13,8,512]{2,1,0:T(8,128)S(1)}, u32[]{:S(2)}, u32[]{:S(2)}) %collective-permute-start.32) | collective-permute-done | bytes 213024 | tf_op jit(solution)/shard_map/ppermute | solution.py:52
  120.7 1.1 collective-permute-done.34.refs_6_
  121.8 1.3 %shard_map.59 = f32[27,32,512]{2,1,0:T(8,128)} custom-call(f32[13,8,512]{2,1,0:T(8,128)S(1)} %convert_add_fusion.2.refs_0_, f32[14,8,512]{2,1,0:T(8,128)S(1)} %convert_add_fusion.refs_1_, f32[13,8,512]{2,1,0:T(8,128)S(1)} %collective-permute-done.30.refs_2_, f32[14,8,512]{2,1,0:T(8,128)S(1)} %collective-permute-done.31.refs_3_, ...), custom_call_target="tpu_custom_call" | custom-call | tf_op jit(solution)/shard_map/pallas_call | solution.py:405
  123.2 1.2 shard_map.58
  (52 shorter events, 1.3 us)
Async XLA Ops:
  0.6 1.0 copy-start
  1.7 1.0 copy-start.2
  2.9 2.9 %collective-permute-start.1 = (bf16[4,8,16,512]{3,2,1,0:T(8,128)(2,1)S(1)}, bf16[4,8,16,512]{3,2,1,0:T(8,128)(2,1)S(1)}, u32[]{:S(2)}, u32[]{:S(2)}) collective-permute-start(bf16[4,8,16,512]{3,2,1,0:T(8,128)(2,1)S(1)} %get-tuple-element.75.own_act), channel_id=1, source_target_pairs={{0,1},{1,0},{2,3},{3,2},{4,5},{5,4},{6,7},{7,6},{8,9},{9,8},{10,11... | collective-permute-start | bytes 1572872 | tf_op jit(solution)/shard_map/ppermute | solution.py:39
  3.0 15.8 %collective-permute-start.5 = (bf16[4,8,16,512]{3,2,1,0:T(8,128)(2,1)S(1)}, bf16[4,8,16,512]{3,2,1,0:T(8,128)(2,1)S(1)}, u32[]{:S(2)}, u32[]{:S(2)}) collective-permute-start(bf16[4,8,16,512]{3,2,1,0:T(8,128)(2,1)S(1)} %get-tuple-element.75.own_act), channel_id=1, source_target_pairs={{0,2},{1,3},{2,0},{3,1},{4,6},{5,7},{6,4},{7,5},{8,10},{9,11},{10,... | collective-permute-start | bytes 1572872 | tf_op jit(solution)/shard_map/ppermute | solution.py:39
  5.1 0.7 collective-permute-start
  5.7 29.5 %collective-permute-start.8 = (bf16[27,32,512]{2,1,0:T(8,128)(2,1)}, bf16[27,32,512]{2,1,0:T(8,128)(2,1)S(1)}, u32[]{:S(2)}, u32[]{:S(2)}) collective-permute-start(bf16[27,32,512]{2,1,0:T(8,128)(2,1)} %own), channel_id=1, source_target_pairs={{0,12},{1,13},{2,14},{3,15},{4,0},{5,1},{6,2},{7,3},{8,4},{9,5},{1... | collective-permute-start | bytes 2654216 | tf_op jit(solution)/shard_map/ppermute | solution.py:47
  16.7 18.6 %collective-permute-start.9 = (bf16[27,32,512]{2,1,0:T(8,128)(2,1)}, bf16[27,32,512]{2,1,0:T(8,128)(2,1)S(1)}, u32[]{:S(2)}, u32[]{:S(2)}) collective-permute-start(bf16[27,32,512]{2,1,0:T(8,128)(2,1)} %own), channel_id=1, source_target_pairs={{0,4},{1,5},{2,6},{3,7},{4,8},{5,9},{6,10},{7,11},{8,12},{9,13},{1... | collective-permute-start | bytes 2654216 | tf_op jit(solution)/shard_map/ppermute | solution.py:47
  16.7 1.0 copy-start.3
  18.6 2.0 %collective-permute-start.2 = (bf16[5,8,16,128]{3,2,1,0:T(8,128)(2,1)S(1)}, bf16[5,8,16,128]{3,2,1,0:T(8,128)(2,1)S(1)}, u32[]{:S(2)}, u32[]{:S(2)}) collective-permute-start(bf16[5,8,16,128]{3,2,1,0:T(8,128)(2,1)S(1)} %get-tuple-element.78), channel_id=1, source_target_pairs={{0,1},{1,0},{2,3},{3,2},{4,5},{5,4},{6,7},{7,6},{8,9},{9,8},{10,11... | collective-permute-start | bytes 491528 | tf_op jit(solution)/shard_map/ppermute | solution.py:39
  18.7 7.1 %collective-permute-start.3 = (bf16[5,8,16,128]{3,2,1,0:T(8,128)(2,1)S(1)}, bf16[5,8,16,128]{3,2,1,0:T(8,128)(2,1)S(1)}, u32[]{:S(2)}, u32[]{:S(2)}) collective-permute-start(bf16[5,8,16,128]{3,2,1,0:T(8,128)(2,1)S(1)} %get-tuple-element.79), channel_id=1, source_target_pairs={{0,2},{1,3},{2,0},{3,1},{4,6},{5,7},{6,4},{7,5},{8,10},{9,11},{10,... | collective-permute-start | bytes 491528 | tf_op jit(solution)/shard_map/ppermute | solution.py:39
  18.8 9.5 %collective-permute-start.4 = (bf16[5,8,16,128]{3,2,1,0:T(8,128)(2,1)S(1)}, bf16[5,8,16,128]{3,2,1,0:T(8,128)(2,1)S(1)}, u32[]{:S(2)}, u32[]{:S(2)}) collective-permute-start(bf16[5,8,16,128]{3,2,1,0:T(8,128)(2,1)S(1)} %get-tuple-element.80), channel_id=1, source_target_pairs={{0,3},{1,2},{2,1},{3,0},{4,7},{5,6},{6,5},{7,4},{8,11},{9,10},{10,... | collective-permute-start | bytes 491528 | tf_op jit(solution)/shard_map/ppermute | solution.py:39
  28.3 12.2 %collective-permute-start.10 = (bf16[4,8,16,512]{3,2,1,0:T(8,128)(2,1)S(1)}, bf16[4,8,16,512]{3,2,1,0:T(8,128)(2,1)S(1)}, u32[]{:S(2)}, u32[]{:S(2)}) collective-permute-start(bf16[4,8,16,512]{3,2,1,0:T(8,128)(2,1)S(1)} %collective-permute-done.5.far), channel_id=1, source_target_pairs={{0,1},{1,0},{2,3},{3,2},{4,5},{5,4},{6,7},{7,6},{8,9},{9,8},{10,11... | collective-permute-start | bytes 1572872 | tf_op jit(solution)/shard_map/ppermute | solution.py:39
  28.9 6.3 %collective-permute-start.6 = (bf16[4,5,16,128]{3,2,1,0:T(8,128)(2,1)S(1)}, bf16[4,5,16,128]{3,2,1,0:T(8,128)(2,1)S(1)}, u32[]{:S(2)}, u32[]{:S(2)}) collective-permute-start(bf16[4,5,16,128]{3,2,1,0:T(8,128)(2,1)S(1)} %get-tuple-element.85), channel_id=1, source_target_pairs={{0,16},{32,48},{64,80},{96,112},{16,0},{48,32},{80,64},{112,96},{1... | collective-permute-start | bytes 245768 | tf_op jit(solution)/shard_map/ppermute | solution.py:58
  32.6 2.6 %collective-permute-start.7 = (bf16[4,5,16,128]{3,2,1,0:T(8,128)(2,1)S(1)}, bf16[4,5,16,128]{3,2,1,0:T(8,128)(2,1)S(1)}, u32[]{:S(2)}, u32[]{:S(2)}) collective-permute-start(bf16[4,5,16,128]{3,2,1,0:T(8,128)(2,1)S(1)} %get-tuple-element.86), channel_id=1, source_target_pairs={{16,32},{48,64},{80,96},{32,16},{64,48},{96,80},{17,33},{49,65},{8... | collective-permute-start | bytes 245768 | tf_op jit(solution)/shard_map/ppermute | solution.py:58
  35.3 22.0 %collective-permute-start.11 = (bf16[13,32,512]{2,1,0:T(8,128)(2,1)S(1)}, bf16[13,32,512]{2,1,0:T(8,128)(2,1)S(1)}, u32[]{:S(2)}, u32[]{:S(2)}) collective-permute-start(bf16[13,32,512]{2,1,0:T(8,128)(2,1)S(1)} %slice.15), channel_id=1, source_target_pairs={{0,4},{1,5},{2,6},{3,7},{4,8},{5,9},{6,10},{7,11},{8,12},{9,13},{1... | collective-permute-start | bytes 1277960 | tf_op jit(solution)/shard_map/ppermute | solution.py:47
  35.5 24.9 %collective-permute-start.12 = (bf16[14,32,512]{2,1,0:T(8,128)(2,1)S(1)}, bf16[14,32,512]{2,1,0:T(8,128)(2,1)S(1)}, u32[]{:S(2)}, u32[]{:S(2)}) collective-permute-start(bf16[14,32,512]{2,1,0:T(8,128)(2,1)S(1)} %slice.16), channel_id=1, source_target_pairs={{0,12},{1,13},{2,14},{3,15},{4,0},{5,1},{6,2},{7,3},{8,4},{9,5},{1... | collective-permute-start | bytes 1376264 | tf_op jit(solution)/shard_map/ppermute | solution.py:47
  40.5 19.9 %copy-start.4 = (bf16[27,32,512]{2,1,0:T(8,128)(2,1)S(1)}, bf16[27,32,512]{2,1,0:T(8,128)(2,1)}, u32[]{:S(2)}) copy-start(bf16[27,32,512]{2,1,0:T(8,128)(2,1)} %own) | copy-start | bytes 2654212
  48.2 20.9 %collective-permute-start.13 = (bf16[2,13,16,512]{3,2,1,0:T(8,128)(2,1)S(1)}, bf16[2,13,16,512]{3,2,1,0:T(8,128)(2,1)S(1)}, u32[]{:S(2)}, u32[]{:S(2)}) collective-permute-start(bf16[2,13,16,512]{3,2,1,0:T(8,128)(2,1)S(1)} %get-tuple-element.110), channel_id=1, source_target_pairs={{0,32},{16,48},{32,64},{48,80},{64,96},{80,112},{96,0},{112,16},{1... | collective-permute-start | bytes 1277960 | tf_op jit(solution)/shard_map/ppermute | solution.py:52
  55.9 13.3 %collective-permute-start.14 = (bf16[2,13,16,512]{3,2,1,0:T(8,128)(2,1)S(1)}, bf16[2,13,16,512]{3,2,1,0:T(8,128)(2,1)S(1)}, u32[]{:S(2)}, u32[]{:S(2)}) collective-permute-start(bf16[2,13,16,512]{3,2,1,0:T(8,128)(2,1)S(1)} %get-tuple-element.111), channel_id=1, source_target_pairs={{0,96},{16,112},{32,0},{48,16},{64,32},{80,48},{96,64},{112,80},{1... | collective-permute-start | bytes 1277960 | tf_op jit(solution)/shard_map/ppermute | solution.py:52
  57.2 11.9 %collective-permute-start.15 = (bf16[2,14,16,512]{3,2,1,0:T(8,128)(2,1)S(1)}, bf16[2,14,16,512]{3,2,1,0:T(8,128)(2,1)S(1)}, u32[]{:S(2)}, u32[]{:S(2)}) collective-permute-start(bf16[2,14,16,512]{3,2,1,0:T(8,128)(2,1)S(1)} %get-tuple-element.112), channel_id=1, source_target_pairs={{0,4},{1,5},{2,6},{3,7},{4,8},{5,9},{6,10},{7,11},{8,12},{9,13},{1... | collective-permute-start | bytes 1376264 | tf_op jit(solution)/shard_map/ppermute | solution.py:47
  57.2 11.9 %collective-permute-start.16 = (bf16[2,14,16,512]{3,2,1,0:T(8,128)(2,1)S(1)}, bf16[2,14,16,512]{3,2,1,0:T(8,128)(2,1)S(1)}, u32[]{:S(2)}, u32[]{:S(2)}) collective-permute-start(bf16[2,14,16,512]{3,2,1,0:T(8,128)(2,1)S(1)} %get-tuple-element.113), channel_id=1, source_target_pairs={{0,12},{1,13},{2,14},{3,15},{4,0},{5,1},{6,2},{7,3},{8,4},{9,5},{1... | collective-permute-start | bytes 1376264 | tf_op jit(solution)/shard_map/ppermute | solution.py:47
  69.2 11.9 %collective-permute-start.21 = (f32[2,4,8,16,512]{4,3,2,1,0:T(8,128)S(1)}, f32[2,4,8,16,512]{4,3,2,1,0:T(8,128)S(1)}, u32[]{:S(2)}, u32[]{:S(2)}) collective-permute-start(f32[2,4,8,16,512]{4,3,2,1,0:T(8,128)S(1)} %get-tuple-element.127), channel_id=1, source_target_pairs={{0,1},{1,0},{2,3},{3,2},{4,5},{5,4},{6,7},{7,6},{8,9},{9,8},{10,11... | collective-permute-start | bytes 6291464 | tf_op jit(solution)/shard_map/ppermute | solution.py:39
  69.4 11.6 %collective-permute-start.19 = (bf16[14,16,512]{2,1,0:T(8,128)(2,1)S(1)}, bf16[14,16,512]{2,1,0:T(8,128)(2,1)S(1)}, u32[]{:S(2)}, u32[]{:S(2)}) collective-permute-start(bf16[14,16,512]{2,1,0:T(8,128)(2,1)S(1)} %get-tuple-element.125), channel_id=1, source_target_pairs={{0,4},{1,5},{2,6},{3,7},{4,8},{5,9},{6,10},{7,11},{8,12},{9,13},{1... | collective-permute-start | bytes 688136 | tf_op jit(solution)/shard_map/ppermute | solution.py:47
  69.5 11.5 %collective-permute-start.20 = (bf16[14,16,512]{2,1,0:T(8,128)(2,1)S(1)}, bf16[14,16,512]{2,1,0:T(8,128)(2,1)S(1)}, u32[]{:S(2)}, u32[]{:S(2)}) collective-permute-start(bf16[14,16,512]{2,1,0:T(8,128)(2,1)S(1)} %get-tuple-element.126), channel_id=1, source_target_pairs={{0,12},{1,13},{2,14},{3,15},{4,0},{5,1},{6,2},{7,3},{8,4},{9,5},{1... | collective-permute-start | bytes 688136 | tf_op jit(solution)/shard_map/ppermute | solution.py:47
  72.7 8.3 %collective-permute-start.17 = (bf16[13,16,512]{2,1,0:T(8,128)(2,1)S(1)}, bf16[13,16,512]{2,1,0:T(8,128)(2,1)S(1)}, u32[]{:S(2)}, u32[]{:S(2)}) collective-permute-start(bf16[13,16,512]{2,1,0:T(8,128)(2,1)S(1)} %get-tuple-element.123), channel_id=1, source_target_pairs={{0,32},{16,48},{32,64},{48,80},{64,96},{80,112},{96,0},{112,16},{1... | collective-permute-start | bytes 638984 | tf_op jit(solution)/shard_map/ppermute | solution.py:52
  73.4 7.6 %collective-permute-start.18 = (bf16[13,16,512]{2,1,0:T(8,128)(2,1)S(1)}, bf16[13,16,512]{2,1,0:T(8,128)(2,1)S(1)}, u32[]{:S(2)}, u32[]{:S(2)}) collective-permute-start(bf16[13,16,512]{2,1,0:T(8,128)(2,1)S(1)} %get-tuple-element.124), channel_id=1, source_target_pairs={{0,96},{16,112},{32,0},{48,16},{64,32},{80,48},{96,64},{112,80},{1... | collective-permute-start | bytes 638984 | tf_op jit(solution)/shard_map/ppermute | solution.py:52
  81.3 5.5 %collective-permute-start.24 = (bf16[13,8,512]{2,1,0:T(8,128)(2,1)S(1)}, bf16[13,8,512]{2,1,0:T(8,128)(2,1)S(1)}, u32[]{:S(2)}, u32[]{:S(2)}) collective-permute-start(bf16[13,8,512]{2,1,0:T(8,128)(2,1)S(1)} %get-tuple-element.138), channel_id=1, source_target_pairs={{0,12},{1,13},{2,14},{3,15},{4,0},{5,1},{6,2},{7,3},{8,4},{9,5},{1... | collective-permute-start | bytes 319496 | tf_op jit(solution)/shard_map/ppermute | solution.py:47
  82.7 6.4 %collective-permute-start.23 = (bf16[13,8,512]{2,1,0:T(8,128)(2,1)S(1)}, bf16[13,8,512]{2,1,0:T(8,128)(2,1)S(1)}, u32[]{:S(2)}, u32[]{:S(2)}) collective-permute-start(bf16[13,8,512]{2,1,0:T(8,128)(2,1)S(1)} %get-tuple-element.137), channel_id=1, source_target_pairs={{0,8},{1,9},{2,10},{3,11},{4,12},{5,13},{6,14},{7,15},{8,0},{9,1},... | collective-permute-start | bytes 319496 | tf_op jit(solution)/shard_map/ppermute | solution.py:47
  82.7 7.3 %collective-permute-start.22 = (bf16[13,8,512]{2,1,0:T(8,128)(2,1)S(1)}, bf16[13,8,512]{2,1,0:T(8,128)(2,1)S(1)}, u32[]{:S(2)}, u32[]{:S(2)}) collective-permute-start(bf16[13,8,512]{2,1,0:T(8,128)(2,1)S(1)} %get-tuple-element.136), channel_id=1, source_target_pairs={{0,4},{1,5},{2,6},{3,7},{4,8},{5,9},{6,10},{7,11},{8,12},{9,13},{1... | collective-permute-start | bytes 319496 | tf_op jit(solution)/shard_map/ppermute | solution.py:47
  83.8 6.5 %collective-permute-start.27 = (bf16[14,8,512]{2,1,0:T(8,128)(2,1)S(1)}, bf16[14,8,512]{2,1,0:T(8,128)(2,1)S(1)}, u32[]{:S(2)}, u32[]{:S(2)}) collective-permute-start(bf16[14,8,512]{2,1,0:T(8,128)(2,1)S(1)} %get-tuple-element.142), channel_id=1, source_target_pairs={{0,96},{16,112},{32,0},{48,16},{64,32},{80,48},{96,64},{112,80},{1... | collective-permute-start | bytes 344072 | tf_op jit(solution)/shard_map/ppermute | solution.py:52
  86.8 6.4 %collective-permute-start.26 = (bf16[14,8,512]{2,1,0:T(8,128)(2,1)S(1)}, bf16[14,8,512]{2,1,0:T(8,128)(2,1)S(1)}, u32[]{:S(2)}, u32[]{:S(2)}) collective-permute-start(bf16[14,8,512]{2,1,0:T(8,128)(2,1)S(1)} %get-tuple-element.141), channel_id=1, source_target_pairs={{0,64},{16,80},{32,96},{48,112},{64,0},{80,16},{96,32},{112,48},{1... | collective-permute-start | bytes 344072 | tf_op jit(solution)/shard_map/ppermute | solution.py:52
  86.8 7.2 %collective-permute-start.25 = (bf16[14,8,512]{2,1,0:T(8,128)(2,1)S(1)}, bf16[14,8,512]{2,1,0:T(8,128)(2,1)S(1)}, u32[]{:S(2)}, u32[]{:S(2)}) collective-permute-start(bf16[14,8,512]{2,1,0:T(8,128)(2,1)S(1)} %get-tuple-element.140), channel_id=1, source_target_pairs={{0,32},{16,48},{32,64},{48,80},{64,96},{80,112},{96,0},{112,16},{1... | collective-permute-start | bytes 344072 | tf_op jit(solution)/shard_map/ppermute | solution.py:52
  94.1 9.9 %collective-permute-start.28 = (bf16[27,8,512]{2,1,0:T(8,128)(2,1)S(1)}, bf16[27,8,512]{2,1,0:T(8,128)(2,1)S(1)}, u32[]{:S(2)}, u32[]{:S(2)}) collective-permute-start(bf16[27,8,512]{2,1,0:T(8,128)(2,1)S(1)} %pad_maximum_fusion), channel_id=1, source_target_pairs={{0,16},{16,0},{32,48},{48,32},{64,80},{80,64},{96,112},{112,96},{1... | collective-permute-start | bytes 663560 | tf_op jit(solution)/shard_map/ppermute | solution.py:468
  104.0 19.2 %collective-permute-start.29 = (f32[4,8,16,512]{3,2,1,0:T(8,128)S(1)}, f32[4,8,16,512]{3,2,1,0:T(8,128)S(1)}, u32[]{:S(2)}, u32[]{:S(2)}) collective-permute-start(f32[4,8,16,512]{3,2,1,0:T(8,128)S(1)} %bitcast_add_fusion), channel_id=1, source_target_pairs={{0,2},{1,3},{2,0},{3,1},{4,6},{5,7},{6,4},{7,5},{8,10},{9,11},{10,... | collective-permute-start | bytes 3145736 | tf_op jit(solution)/shard_map/ppermute | solution.py:39
  104.1 19.1 %copy-start.1 = (bf16[4,8,16,512]{3,2,1,0:T(8,128)(2,1)S(1)}, bf16[4,8,16,512]{3,2,1,0:T(8,128)(2,1)}, u32[]{:S(2)}) copy-start(bf16[4,8,16,512]{3,2,1,0:T(8,128)(2,1)} %pre.3) | copy-start | bytes 1572868
  104.1 8.3 %collective-permute-start.33 = (f32[14,8,512]{2,1,0:T(8,128)S(1)}, f32[14,8,512]{2,1,0:T(8,128)S(1)}, u32[]{:S(2)}, u32[]{:S(2)}) collective-permute-start(f32[14,8,512]{2,1,0:T(8,128)S(1)} %convert_add_fusion.refs_1_), channel_id=1, source_target_pairs={{0,96},{16,112},{32,0},{48,16},{64,32},{80,48},{96,64},{112,80},{1... | collective-permute-start | bytes 688136 | tf_op jit(solution)/shard_map/ppermute | solution.py:52
  105.1 9.6 %collective-permute-start.30 = (f32[13,8,512]{2,1,0:T(8,128)S(1)}, f32[13,8,512]{2,1,0:T(8,128)S(1)}, u32[]{:S(2)}, u32[]{:S(2)}) collective-permute-start(f32[13,8,512]{2,1,0:T(8,128)S(1)} %convert_add_fusion.2.refs_0_), channel_id=1, source_target_pairs={{0,32},{16,48},{32,64},{48,80},{64,96},{80,112},{96,0},{112,16},{1... | collective-permute-start | bytes 638984 | tf_op jit(solution)/shard_map/ppermute | solution.py:52
  106.3 14.4 %collective-permute-start.31 = (f32[14,8,512]{2,1,0:T(8,128)S(1)}, f32[14,8,512]{2,1,0:T(8,128)S(1)}, u32[]{:S(2)}, u32[]{:S(2)}) collective-permute-start(f32[14,8,512]{2,1,0:T(8,128)S(1)} %convert_add_fusion.refs_1_), channel_id=1, source_target_pairs={{0,32},{16,48},{32,64},{48,80},{64,96},{80,112},{96,0},{112,16},{1... | collective-permute-start | bytes 688136 | tf_op jit(solution)/shard_map/ppermute | solution.py:52
  112.4 9.4 %collective-permute-start.35 = (f32[14,8,512]{2,1,0:T(8,128)S(1)}, f32[14,8,512]{2,1,0:T(8,128)S(1)}, u32[]{:S(2)}, u32[]{:S(2)}) collective-permute-start(f32[14,8,512]{2,1,0:T(8,128)S(1)} %collective-permute-done.33.refs_5_), channel_id=1, source_target_pairs={{0,96},{16,112},{32,0},{48,16},{64,32},{80,48},{96,64},{112,80},{1... | collective-permute-start | bytes 688136 | tf_op jit(solution)/shard_map/ppermute | solution.py:52
  114.7 6.0 %collective-permute-start.32 = (f32[13,8,512]{2,1,0:T(8,128)S(1)}, f32[13,8,512]{2,1,0:T(8,128)S(1)}, u32[]{:S(2)}, u32[]{:S(2)}) collective-permute-start(f32[13,8,512]{2,1,0:T(8,128)S(1)} %convert_add_fusion.2.refs_0_), channel_id=1, source_target_pairs={{0,96},{16,112},{32,0},{48,16},{64,32},{80,48},{96,64},{112,80},{1... | collective-permute-start | bytes 638984 | tf_op jit(solution)/shard_map/ppermute | solution.py:52
  114.8 7.1 %collective-permute-start.34 = (f32[13,8,512]{2,1,0:T(8,128)S(1)}, f32[13,8,512]{2,1,0:T(8,128)S(1)}, u32[]{:S(2)}, u32[]{:S(2)}) collective-permute-start(f32[13,8,512]{2,1,0:T(8,128)S(1)} %collective-permute-done.30.refs_2_), channel_id=1, source_target_pairs={{0,32},{16,48},{32,64},{48,80},{64,96},{80,112},{96,0},{112,16},{1... | collective-permute-start | bytes 638984 | tf_op jit(solution)/shard_map/ppermute | solution.py:52

commit v8 on v7

--- a/solution.py
+++ b/solution.py
@@ -22,6 +22,10 @@
     return pltpu.CompilerParams(vmem_limit_bytes=LIMIT)
 
 
+def small_cost():
+    return pl.CostEstimate(flops=1000, bytes_accessed=1000, transcendentals=0)
+
+
 def quad_place():
     return lax.rem(lax.axis_index("gy"), QUAD)
 
@@ -60,25 +64,6 @@
 
 def zero_at(value, z, edge):
     return jnp.where(z == edge, 0.0, value)
-
-
-def start_kernel(pre, cot, act, edge):
-    value = pre[...].astype(F32)
-    act[...] = (value * jax.nn.sigmoid(value)).astype(BF16)
-    edge[...] = jnp.where(quad_place() == 0, cot[0], cot[cot.shape[0] - 1])
-
-
-def start(pre_act, cot):
-    return pl.pallas_call(
-        start_kernel,
-        out_shape=[
-            jax.ShapeDtypeStruct(pre_act.shape, BF16),
-            jax.ShapeDtypeStruct(cot.shape[1:], BF16),
-        ],
-        in_specs=[VMEM] * 2,
-        out_specs=[VMEM] * 2,
-        compiler_params=params(),
-    )(pre_act, cot)
 
 
 def pick_kernel(cot, extra, *quarters):
@@ -109,6 +94,7 @@
         in_specs=[VMEM] * 2,
         out_specs=[VMEM] * QUAD,
         compiler_params=params(),
+        cost_estimate=small_cost(),
     )(cot, extra)
 
 
@@ -129,6 +115,7 @@
         in_specs=[VMEM] * QUAD,
         out_specs=[VMEM] * 2,
         compiler_params=params(),
+        cost_estimate=small_cost(),
     )(*quarters)
 
 
@@ -186,6 +173,7 @@
         in_specs=[VMEM] * (QUAD + 2),
         out_specs=[VMEM] * 2,
         compiler_params=params(),
+        cost_estimate=small_cost(),
     )(*quarters, even, odd)
 
 
@@ -420,20 +408,20 @@
     count = lax.axis_size("gy")
     pairs = [(g, g + 1) for g in range(QUAD - 1, count - 1, QUAD)]
     pairs = pairs + [(t, s) for s, t in pairs]
-    act, edge = start(pre_act, cot)
-    extra = lax.ppermute(edge, "gy", pairs)
-    far = swap(act, 2)
+    extra = lax.ppermute(jnp.where(j == 0, cot[0], cot[rows - 1]), "gy", pairs)
+    act = jax.nn.silu(pre_act.astype(F32)).astype(BF16)
     near = swap(act, 1)
     extra, near, weight = barrier((extra, near, weight))
     above = along_y(weight, -1, True)
     below = along_y(weight, 1, True)
     quarters = pick_channels(cot, extra)
     quarters = [quarters[0]] + [swap(quarters[k], k) for k in (1, 2, 3)]
-    quarters, far = barrier((quarters, far))
-    acts = [act, near, far, swap(far, 1)]
+    quarters, act = barrier((quarters, act))
+    far = swap(act, 2)
     even, odd = sides(quarters)
     even, odd = swap_x(even, 0), swap_x(odd, 1)
-    even, odd, above, below = barrier((even, odd, above, below))
+    even, odd, above, below, far = barrier((even, odd, above, below, far))
+    acts = [act, near, far, swap(far, 1)]
     taps = XTAPS
     parts = [weight, above, along_y(below[:taps], 1, True), along_y(above[taps:], -1, True), below]
     held, turned = turn(quarters, even, odd)

time: 126 us -> 133 us (1.056)
  waiting for transfers between devices: 41.4 us -> 54.5 us
  starting transfers between devices: 56.3 us -> 50.8 us
  other arithmetic: 0.51 us -> 2.85 us
  local copies, waits for them, and re-layouts: 3.19 us -> 1.11 us
    ppermute x2, waiting for transfers between devices: 1.95 us -> 13.7 us  [swap_x(): return lax.ppermute(block, 'gx', pairs + [(t, s) for s, t in pairs])]
    ppermute x13, starting transfers between devices: 22.6 us -> 18.6 us  [along_x(): lax.ppermute(block, 'gx', [(g, (g + 2 * step) % count) for g in range(cou...]
    unnamed x10 -> x6, local copies, waits for them, and re-layouts: 3.13 us -> 1.05 us
    convert_element_type x0 -> x1, other arithmetic: none -> 1.36 us  [body(): act = jax.nn.silu(pre_act.astype(F32)).astype(BF16)]
  transfers between devices with their start and end apart: 36 -> 36, of which waited for: 13 -> 15; matrix products, arithmetic and copies ran while one was open for 0% -> 1% of each run, Pallas kernels for 16% -> 16%
where the time goes in v8:
time: 133 us; the launch traced here: 132 us
  waiting for transfers between devices  54.5 us (41%)
  starting transfers between devices  50.8 us (38%)
  Pallas kernels  22 us (17%)
  other arithmetic  2.85 us (2%)
    ppermute x11, starting transfers between devices, along_y(): lax.ppermute(block, 'gy', [(s, t) for s, t in pairs if 0 <= t < count])  23.1 us
    ppermute x13, waiting for transfers between devices, along_x(): lax.ppermute(block, 'gx', [(g, (g + 2 * step) % count) for g in range(cou...  19.9 us
    ppermute x13, starting transfers between devices, along_x(): lax.ppermute(block, 'gx', [(g, (g + 2 * step) % count) for g in range(cou...  18.6 us
    ppermute x2, waiting for transfers between devices, swap_x(): return lax.ppermute(block, 'gx', pairs + [(t, s) for s, t in pairs])  13.7 us
    ppermute x1, waiting for transfers between devices, body(): other = lax.ppermute(mine, 'gx', [(g, g ^ 1) for g in range(count)])  9.27 us
    pallas_call x1, Pallas kernels, input_terms(): pl.pallas_call(input_kernel, out_shape=[jax.ShapeDtypeStruct((2,) + block...  8.65 us
    ppermute x8, waiting for transfers between devices, swap(): return lax.ppermute(block, 'gy', [(g, g ^ k) for g in range(count)])  8.01 us
    pallas_call x1, Pallas kernels, weight_terms(): pl.pallas_call(functools.partial(weight_kernel, norm), out_shape=shapes,...  7.66 us
  transfers between devices with their start and end apart: 36, of which 15 were waited for; matrix products, arithmetic and copies ran while one was open for 1% of the time, Pallas kernels for 16%

profile of v8, /device:TPU:0, one launch (start us, length us, event | category | flops | bytes accessed | tf_op | source)
XLA Modules:
  0.0 132.2 jit_solution(12677488657286029446)
XLA Ops:
  0.6 1.4 %fusion.3.own_act = bf16[4,8,16,512]{3,2,1,0:T(8,128)(2,1)S(1)} fusion(bf16[4,8,16,512]{3,2,1,0:T(8,128)(2,1)} %pre.1), kind=kLoop, calls=%fused_computation.5 | loop fusion | flops 1572864 | bytes 1048576 | tf_op jit(solution)/shard_map/convert_element_type | solution.py:412
  2.1 1.0 select_bitcast_fusion
  3.1 0.7 collective-permute-start
  3.8 0.2 collective-permute-done.1.near
  4.0 10.2 %collective-permute-start.7 = (bf16[27,32,512]{2,1,0:T(8,128)(2,1)}, bf16[27,32,512]{2,1,0:T(8,128)(2,1)S(1)}, u32[]{:S(2)}, u32[]{:S(2)}) collective-permute-start(bf16[27,32,512]{2,1,0:T(8,128)(2,1)} %own), channel_id=1, source_target_pairs={{0,12},{1,13},{2,14},{3,15},{4,0},{5,1},{6,2},{7,3},{8,4},{9,5},{1... | collective-permute-start | bytes 2654216 | tf_op jit(solution)/shard_map/ppermute | solution.py:51
  14.2 1.0 copy-done.1
  15.3 0.9 shard_map.50
  16.2 1.7 %collective-permute-start.3 = (bf16[5,8,16,128]{3,2,1,0:T(8,128)(2,1)S(1)}, bf16[5,8,16,128]{3,2,1,0:T(8,128)(2,1)S(1)}, u32[]{:S(2)}, u32[]{:S(2)}) collective-permute-start(bf16[5,8,16,128]{3,2,1,0:T(8,128)(2,1)S(1)} %get-tuple-element.76), channel_id=1, source_target_pairs={{0,2},{1,3},{2,0},{3,1},{4,6},{5,7},{6,4},{7,5},{8,10},{9,11},{10,... | collective-permute-start | bytes 491528 | tf_op jit(solution)/shard_map/ppermute | solution.py:43
  18.1 5.2 %collective-permute-done.3.p2 = bf16[5,8,16,128]{3,2,1,0:T(8,128)(2,1)S(1)} collective-permute-done((bf16[5,8,16,128]{3,2,1,0:T(8,128)(2,1)S(1)}, bf16[5,8,16,128]{3,2,1,0:T(8,128)(2,1)S(1)}, u32[]{:S(2)}, u32[]{:S(2)}) %collective-permute-start.3) | collective-permute-done | bytes 163872 | tf_op jit(solution)/shard_map/ppermute | solution.py:43
  23.3 2.6 %collective-permute-done.4.p3 = bf16[5,8,16,128]{3,2,1,0:T(8,128)(2,1)S(1)} collective-permute-done((bf16[5,8,16,128]{3,2,1,0:T(8,128)(2,1)S(1)}, bf16[5,8,16,128]{3,2,1,0:T(8,128)(2,1)S(1)}, u32[]{:S(2)}, u32[]{:S(2)}) %collective-permute-start.4) | collective-permute-done | bytes 163872 | tf_op jit(solution)/shard_map/ppermute | solution.py:43
  25.9 0.9 collective-permute-start.9
  26.9 3.7 %collective-permute-start.5 = (bf16[4,5,16,128]{3,2,1,0:T(8,128)(2,1)S(1)}, bf16[4,5,16,128]{3,2,1,0:T(8,128)(2,1)S(1)}, u32[]{:S(2)}, u32[]{:S(2)}) collective-permute-start(bf16[4,5,16,128]{3,2,1,0:T(8,128)(2,1)S(1)} %get-tuple-element.82), channel_id=1, source_target_pairs={{0,16},{32,48},{64,80},{96,112},{16,0},{48,32},{80,64},{112,96},{1... | collective-permute-start | bytes 245768 | tf_op jit(solution)/shard_map/ppermute | solution.py:62
  30.5 0.7 collective-permute-start.6
  31.2 13.7 %collective-permute-done.5.even = bf16[4,5,16,128]{3,2,1,0:T(8,128)(2,1)S(1)} collective-permute-done((bf16[4,5,16,128]{3,2,1,0:T(8,128)(2,1)S(1)}, bf16[4,5,16,128]{3,2,1,0:T(8,128)(2,1)S(1)}, u32[]{:S(2)}, u32[]{:S(2)}) %collective-permute-start.5) | collective-permute-done | bytes 81952 | tf_op jit(solution)/shard_map/ppermute | solution.py:62
  45.2 1.0 collective-permute-start.11
  46.2 2.4 %collective-permute-start.12 = (bf16[14,32,512]{2,1,0:T(8,128)(2,1)S(1)}, bf16[14,32,512]{2,1,0:T(8,128)(2,1)S(1)}, u32[]{:S(2)}, u32[]{:S(2)}) collective-permute-start(bf16[14,32,512]{2,1,0:T(8,128)(2,1)S(1)} %slice.24), channel_id=1, source_target_pairs={{0,12},{1,13},{2,14},{3,15},{4,0},{5,1},{6,2},{7,3},{8,4},{9,5},{1... | collective-permute-start | bytes 1376264 | tf_op jit(solution)/shard_map/ppermute | solution.py:51
  48.6 1.8 %shard_map.52 = (bf16[18,10,16,128]{3,2,1,0:T(8,128)(2,1)S(1)}, bf16[1152,2304]{1,0:T(8,128)(2,1)S(1)}) custom-call(bf16[5,8,16,128]{3,2,1,0:T(8,128)(2,1)S(1)} %get-tuple-element.78.p0, bf16[5,8,16,128]{3,2,1,0:T(8,128)(2,1)S(1)} %collective-permute-done.2.p1, bf16[5,8,16,128]{3,2,1,0:T(8,128)(2,1)S(1)} %collective-permute-done.3.p2, ...), custom_call_target="tpu_custom_call" | custom-call | flops 1000 | bytes 1000 | tf_op jit(solution)/shard_map/pallas_call | solution.py:167
  50.5 7.7 %shard_map.53 = (bf16[2,13,16,512]{3,2,1,0:T(8,128)(2,1)S(1)}, bf16[2,13,16,512]{3,2,1,0:T(8,128)(2,1)S(1)}, f32[13,16,512]{2,1,0:T(8,128)S(1)}, f32[13,16,512]{...) custom-call(bf16[4,8,16,512]{3,2,1,0:T(8,128)(2,1)S(1)} %fusion.3.ow, ...), custom_call_target="tpu_custom_call" | custom-call | flops 7247757312 | bytes 10000000 | tf_op jit(solution)/shard_map/pallas_call | solution.py:236
  58.1 3.3 %collective-permute-start.13 = (bf16[2,13,16,512]{3,2,1,0:T(8,128)(2,1)S(1)}, bf16[2,13,16,512]{3,2,1,0:T(8,128)(2,1)S(1)}, u32[]{:S(2)}, u32[]{:S(2)}) collective-permute-start(bf16[2,13,16,512]{3,2,1,0:T(8,128)(2,1)S(1)} %get-tuple-element.108), channel_id=1, source_target_pairs={{0,32},{16,48},{32,64},{48,80},{64,96},{80,112},{96,0},{112,16},{1... | collective-permute-start | bytes 1277960 | tf_op jit(solution)/shard_map/ppermute | solution.py:56
  61.5 1.4 %collective-permute-start.14 = (bf16[2,13,16,512]{3,2,1,0:T(8,128)(2,1)S(1)}, bf16[2,13,16,512]{3,2,1,0:T(8,128)(2,1)S(1)}, u32[]{:S(2)}, u32[]{:S(2)}) collective-permute-start(bf16[2,13,16,512]{3,2,1,0:T(8,128)(2,1)S(1)} %get-tuple-element.109), channel_id=1, source_target_pairs={{0,96},{16,112},{32,0},{48,16},{64,32},{80,48},{96,64},{112,80},{1... | collective-permute-start | bytes 1277960 | tf_op jit(solution)/shard_map/ppermute | solution.py:56
  62.8 3.2 %collective-permute-start.16 = (bf16[2,14,16,512]{3,2,1,0:T(8,128)(2,1)S(1)}, bf16[2,14,16,512]{3,2,1,0:T(8,128)(2,1)S(1)}, u32[]{:S(2)}, u32[]{:S(2)}) collective-permute-start(bf16[2,14,16,512]{3,2,1,0:T(8,128)(2,1)S(1)} %get-tuple-element.111), channel_id=1, source_target_pairs={{0,12},{1,13},{2,14},{3,15},{4,0},{5,1},{6,2},{7,3},{8,4},{9,5},{1... | collective-permute-start | bytes 1376264 | tf_op jit(solution)/shard_map/ppermute | solution.py:51
  66.1 8.6 %shard_map.54 = (f32[2,4,8,16,512]{4,3,2,1,0:T(8,128)S(1)}, f32[4,8,16,512]{3,2,1,0:T(8,128)S(1)}, f32[4,8,16,512]{3,2,1,0:T(8,128)S(1)}) custom-call(bf16[18,10,16,128]{3,2,1,0:T(8,128)(2,1)S(1)} %get-tuple-element.102.held, bf16[27,32,512]{2,1,0:T(8,128)(2,1)S(1)} %copy-done.2, bf16[27,32,512]{2,1,0:T(8,128)(2,1)S(1)} %collective-permute-done.7.above, ...), custom_call_target="tpu_custom_call" | custom-call | flops 10192158720 | bytes 10000000 | tf_op jit(solution)/shard_map/pallas_call | solution.py:298
  74.7 1.2 collective-permute-done.15.refs_4_.refs_6_
  76.2 3.2 %collective-permute-start.20 = (bf16[14,16,512]{2,1,0:T(8,128)(2,1)S(1)}, bf16[14,16,512]{2,1,0:T(8,128)(2,1)S(1)}, u32[]{:S(2)}, u32[]{:S(2)}) collective-permute-start(bf16[14,16,512]{2,1,0:T(8,128)(2,1)S(1)} %get-tuple-element.124), channel_id=1, source_target_pairs={{0,12},{1,13},{2,14},{3,15},{4,0},{5,1},{6,2},{7,3},{8,4},{9,5},{1... | collective-permute-start | bytes 688136 | tf_op jit(solution)/shard_map/ppermute | solution.py:51
  79.4 0.4 collective-permute-start.17
  79.8 2.8 %collective-permute-start.18 = (bf16[13,16,512]{2,1,0:T(8,128)(2,1)S(1)}, bf16[13,16,512]{2,1,0:T(8,128)(2,1)S(1)}, u32[]{:S(2)}, u32[]{:S(2)}) collective-permute-start(bf16[13,16,512]{2,1,0:T(8,128)(2,1)S(1)} %get-tuple-element.122), channel_id=1, source_target_pairs={{0,96},{16,112},{32,0},{48,16},{64,32},{80,48},{96,64},{112,80},{1... | collective-permute-start | bytes 638984 | tf_op jit(solution)/shard_map/ppermute | solution.py:56
  82.7 5.2 %collective-permute-done.17.refs_3_ = bf16[13,16,512]{2,1,0:T(8,128)(2,1)S(1)} collective-permute-done((bf16[13,16,512]{2,1,0:T(8,128)(2,1)S(1)}, bf16[13,16,512]{2,1,0:T(8,128)(2,1)S(1)}, u32[]{:S(2)}, u32[]{:S(2)}) %collective-permute-start.17) | collective-permute-done | bytes 213024 | tf_op jit(solution)/shard_map/ppermute | solution.py:56
  87.8 0.3 shard_map.56
  88.1 1.7 %collective-permute-start.24 = (bf16[13,8,512]{2,1,0:T(8,128)(2,1)S(1)}, bf16[13,8,512]{2,1,0:T(8,128)(2,1)S(1)}, u32[]{:S(2)}, u32[]{:S(2)}) collective-permute-start(bf16[13,8,512]{2,1,0:T(8,128)(2,1)S(1)} %get-tuple-element.136), channel_id=1, source_target_pairs={{0,12},{1,13},{2,14},{3,15},{4,0},{5,1},{6,2},{7,3},{8,4},{9,5},{1... | collective-permute-start | bytes 319496 | tf_op jit(solution)/shard_map/ppermute | solution.py:51
  89.8 1.1 collective-permute-start.22
  91.0 2.9 %collective-permute-start.27 = (bf16[14,8,512]{2,1,0:T(8,128)(2,1)S(1)}, bf16[14,8,512]{2,1,0:T(8,128)(2,1)S(1)}, u32[]{:S(2)}, u32[]{:S(2)}) collective-permute-start(bf16[14,8,512]{2,1,0:T(8,128)(2,1)S(1)} %get-tuple-element.140), channel_id=1, source_target_pairs={{0,96},{16,112},{32,0},{48,16},{64,32},{80,48},{96,64},{112,80},{1... | collective-permute-start | bytes 344072 | tf_op jit(solution)/shard_map/ppermute | solution.py:56
  93.9 0.9 collective-permute-start.25
  94.8 1.5 %collective-permute-done.23 = bf16[13,8,512]{2,1,0:T(8,128)(2,1)S(1)} collective-permute-done((bf16[13,8,512]{2,1,0:T(8,128)(2,1)S(1)}, bf16[13,8,512]{2,1,0:T(8,128)(2,1)S(1)}, u32[]{:S(2)}, u32[]{:S(2)}) %collective-permute-start.23) | collective-permute-done | bytes 106528 | tf_op jit(solution)/shard_map/ppermute | solution.py:51
  96.3 0.9 collective-permute-done.22
  97.2 0.3 collective-permute-done.27
  97.5 2.8 %collective-permute-done.26 = bf16[14,8,512]{2,1,0:T(8,128)(2,1)S(1)} collective-permute-done((bf16[14,8,512]{2,1,0:T(8,128)(2,1)S(1)}, bf16[14,8,512]{2,1,0:T(8,128)(2,1)S(1)}, u32[]{:S(2)}, u32[]{:S(2)}) %collective-permute-start.26) | collective-permute-done | bytes 114720 | tf_op jit(solution)/shard_map/ppermute | solution.py:56
  100.3 0.8 collective-permute-done.25
  101.6 9.3 %collective-permute-done.28 = bf16[27,8,512]{2,1,0:T(8,128)(2,1)S(1)} collective-permute-done((bf16[27,8,512]{2,1,0:T(8,128)(2,1)S(1)}, bf16[27,8,512]{2,1,0:T(8,128)(2,1)S(1)}, u32[]{:S(2)}, u32[]{:S(2)}) %collective-permute-start.28) | collective-permute-done | bytes 221216 | tf_op jit(solution)/shard_map/ppermute | solution.py:456
  110.9 0.8 collective-permute-start.29
  111.8 0.9 collective-permute-start.33
  112.8 1.2 collective-permute-start.30
  114.1 5.7 %collective-permute-done.33.refs_5_ = f32[14,8,512]{2,1,0:T(8,128)S(1)} collective-permute-done((f32[14,8,512]{2,1,0:T(8,128)S(1)}, f32[14,8,512]{2,1,0:T(8,128)S(1)}, u32[]{:S(2)}, u32[]{:S(2)}) %collective-permute-start.33) | collective-permute-done | bytes 229408 | tf_op jit(solution)/shard_map/ppermute | solution.py:56
  119.9 2.6 %collective-permute-start.35 = (f32[14,8,512]{2,1,0:T(8,128)S(1)}, f32[14,8,512]{2,1,0:T(8,128)S(1)}, u32[]{:S(2)}, u32[]{:S(2)}) collective-permute-start(f32[14,8,512]{2,1,0:T(8,128)S(1)} %collective-permute-done.33.refs_5_), channel_id=1, source_target_pairs={{0,96},{16,112},{32,0},{48,16},{64,32},{80,48},{96,64},{112,80},{1... | collective-permute-start | bytes 688136 | tf_op jit(solution)/shard_map/ppermute | solution.py:56
  122.6 2.0 %collective-permute-start.34 = (f32[13,8,512]{2,1,0:T(8,128)S(1)}, f32[13,8,512]{2,1,0:T(8,128)S(1)}, u32[]{:S(2)}, u32[]{:S(2)}) collective-permute-start(f32[13,8,512]{2,1,0:T(8,128)S(1)} %collective-permute-done.30.refs_2_), channel_id=1, source_target_pairs={{0,32},{16,48},{32,64},{48,80},{64,96},{80,112},{96,0},{112,16},{1... | collective-permute-start | bytes 638984 | tf_op jit(solution)/shard_map/ppermute | solution.py:56
  124.5 3.8 %collective-permute-done.32.refs_4_ = f32[13,8,512]{2,1,0:T(8,128)S(1)} collective-permute-done((f32[13,8,512]{2,1,0:T(8,128)S(1)}, f32[13,8,512]{2,1,0:T(8,128)S(1)}, u32[]{:S(2)}, u32[]{:S(2)}) %collective-permute-start.32) | collective-permute-done | bytes 213024 | tf_op jit(solution)/shard_map/ppermute | solution.py:56
  128.4 1.2 collective-permute-done.34.refs_6_
  129.6 1.3 %shard_map.58 = f32[27,32,512]{2,1,0:T(8,128)} custom-call(f32[13,8,512]{2,1,0:T(8,128)S(1)} %convert_add_fusion.2.refs_0_, f32[14,8,512]{2,1,0:T(8,128)S(1)} %convert_add_fusion.refs_1_, f32[13,8,512]{2,1,0:T(8,128)S(1)} %collective-permute-done.30.refs_2_, f32[14,8,512]{2,1,0:T(8,128)S(1)} %collective-permute-done.31.refs_3_, ...), custom_call_target="tpu_custom_call" | custom-call | tf_op jit(solution)/shard_map/pallas_call | solution.py:393
  131.0 1.2 shard_map.57
  (49 shorter events, 1.6 us)
Async XLA Ops:
  2.0 2.0 %collective-permute-start.1 = (bf16[4,8,16,512]{3,2,1,0:T(8,128)(2,1)S(1)}, bf16[4,8,16,512]{3,2,1,0:T(8,128)(2,1)S(1)}, u32[]{:S(2)}, u32[]{:S(2)}) collective-permute-start(bf16[4,8,16,512]{3,2,1,0:T(8,128)(2,1)S(1)} %fusion.3.own_act), channel_id=1, source_target_pairs={{0,1},{1,0},{2,3},{3,2},{4,5},{5,4},{6,7},{7,6},{8,9},{9,8},{10,11... | collective-permute-start | bytes 1572872 | tf_op jit(solution)/shard_map/ppermute | solution.py:43
  3.1 0.7 collective-permute-start
  4.0 41.0 %collective-permute-start.7 = (bf16[27,32,512]{2,1,0:T(8,128)(2,1)}, bf16[27,32,512]{2,1,0:T(8,128)(2,1)S(1)}, u32[]{:S(2)}, u32[]{:S(2)}) collective-permute-start(bf16[27,32,512]{2,1,0:T(8,128)(2,1)} %own), channel_id=1, source_target_pairs={{0,12},{1,13},{2,14},{3,15},{4,0},{5,1},{6,2},{7,3},{8,4},{9,5},{1... | collective-permute-start | bytes 2654216 | tf_op jit(solution)/shard_map/ppermute | solution.py:51
  14.2 30.7 %collective-permute-start.8 = (bf16[27,32,512]{2,1,0:T(8,128)(2,1)}, bf16[27,32,512]{2,1,0:T(8,128)(2,1)S(1)}, u32[]{:S(2)}, u32[]{:S(2)}) collective-permute-start(bf16[27,32,512]{2,1,0:T(8,128)(2,1)} %own), channel_id=1, source_target_pairs={{0,4},{1,5},{2,6},{3,7},{4,8},{5,9},{6,10},{7,11},{8,12},{9,13},{1... | collective-permute-start | bytes 2654216 | tf_op jit(solution)/shard_map/ppermute | solution.py:51
  14.2 1.0 copy-start.1
  16.1 2.0 %collective-permute-start.2 = (bf16[5,8,16,128]{3,2,1,0:T(8,128)(2,1)S(1)}, bf16[5,8,16,128]{3,2,1,0:T(8,128)(2,1)S(1)}, u32[]{:S(2)}, u32[]{:S(2)}) collective-permute-start(bf16[5,8,16,128]{3,2,1,0:T(8,128)(2,1)S(1)} %get-tuple-element.75), channel_id=1, source_target_pairs={{0,1},{1,0},{2,3},{3,2},{4,5},{5,4},{6,7},{7,6},{8,9},{9,8},{10,11... | collective-permute-start | bytes 491528 | tf_op jit(solution)/shard_map/ppermute | solution.py:43
  16.2 7.1 %collective-permute-start.3 = (bf16[5,8,16,128]{3,2,1,0:T(8,128)(2,1)S(1)}, bf16[5,8,16,128]{3,2,1,0:T(8,128)(2,1)S(1)}, u32[]{:S(2)}, u32[]{:S(2)}) collective-permute-start(bf16[5,8,16,128]{3,2,1,0:T(8,128)(2,1)S(1)} %get-tuple-element.76), channel_id=1, source_target_pairs={{0,2},{1,3},{2,0},{3,1},{4,6},{5,7},{6,4},{7,5},{8,10},{9,11},{10,... | collective-permute-start | bytes 491528 | tf_op jit(solution)/shard_map/ppermute | solution.py:43
  18.0 7.9 %collective-permute-start.4 = (bf16[5,8,16,128]{3,2,1,0:T(8,128)(2,1)S(1)}, bf16[5,8,16,128]{3,2,1,0:T(8,128)(2,1)S(1)}, u32[]{:S(2)}, u32[]{:S(2)}) collective-permute-start(bf16[5,8,16,128]{3,2,1,0:T(8,128)(2,1)S(1)} %get-tuple-element.77), channel_id=1, source_target_pairs={{0,3},{1,2},{2,1},{3,0},{4,7},{5,6},{6,5},{7,4},{8,11},{9,10},{10,... | collective-permute-start | bytes 491528 | tf_op jit(solution)/shard_map/ppermute | solution.py:43
  25.9 19.1 %collective-permute-start.9 = (bf16[4,8,16,512]{3,2,1,0:T(8,128)(2,1)S(1)}, bf16[4,8,16,512]{3,2,1,0:T(8,128)(2,1)S(1)}, u32[]{:S(2)}, u32[]{:S(2)}) collective-permute-start(bf16[4,8,16,512]{3,2,1,0:T(8,128)(2,1)S(1)} %fusion.3.own_act), channel_id=1, source_target_pairs={{0,2},{1,3},{2,0},{3,1},{4,6},{5,7},{6,4},{7,5},{8,10},{9,11},{10,... | collective-permute-start | bytes 1572872 | tf_op jit(solution)/shard_map/ppermute | solution.py:43
  26.9 18.1 %collective-permute-start.5 = (bf16[4,5,16,128]{3,2,1,0:T(8,128)(2,1)S(1)}, bf16[4,5,16,128]{3,2,1,0:T(8,128)(2,1)S(1)}, u32[]{:S(2)}, u32[]{:S(2)}) collective-permute-start(bf16[4,5,16,128]{3,2,1,0:T(8,128)(2,1)S(1)} %get-tuple-element.82), channel_id=1, source_target_pairs={{0,16},{32,48},{64,80},{96,112},{16,0},{48,32},{80,64},{112,96},{1... | collective-permute-start | bytes 245768 | tf_op jit(solution)/shard_map/ppermute | solution.py:62
  30.5 14.4 %collective-permute-start.6 = (bf16[4,5,16,128]{3,2,1,0:T(8,128)(2,1)S(1)}, bf16[4,5,16,128]{3,2,1,0:T(8,128)(2,1)S(1)}, u32[]{:S(2)}, u32[]{:S(2)}) collective-permute-start(bf16[4,5,16,128]{3,2,1,0:T(8,128)(2,1)S(1)} %get-tuple-element.83), channel_id=1, source_target_pairs={{16,32},{48,64},{80,96},{32,16},{64,48},{96,80},{17,33},{49,65},{8... | collective-permute-start | bytes 245768 | tf_op jit(solution)/shard_map/ppermute | solution.py:62
  44.9 5.5 %collective-permute-start.10 = (bf16[4,8,16,512]{3,2,1,0:T(8,128)(2,1)S(1)}, bf16[4,8,16,512]{3,2,1,0:T(8,128)(2,1)S(1)}, u32[]{:S(2)}, u32[]{:S(2)}) collective-permute-start(bf16[4,8,16,512]{3,2,1,0:T(8,128)(2,1)S(1)} %collective-permute-done.9.far), channel_id=1, source_target_pairs={{0,1},{1,0},{2,3},{3,2},{4,5},{5,4},{6,7},{7,6},{8,9},{9,8},{10,11... | collective-permute-start | bytes 1572872 | tf_op jit(solution)/shard_map/ppermute | solution.py:43
  45.2 17.6 %collective-permute-start.11 = (bf16[13,32,512]{2,1,0:T(8,128)(2,1)S(1)}, bf16[13,32,512]{2,1,0:T(8,128)(2,1)S(1)}, u32[]{:S(2)}, u32[]{:S(2)}) collective-permute-start(bf16[13,32,512]{2,1,0:T(8,128)(2,1)S(1)} %slice.23), channel_id=1, source_target_pairs={{0,4},{1,5},{2,6},{3,7},{4,8},{5,9},{6,10},{7,11},{8,12},{9,13},{1... | collective-permute-start | bytes 1277960 | tf_op jit(solution)/shard_map/ppermute | solution.py:51
  46.2 19.9 %collective-permute-start.12 = (bf16[14,32,512]{2,1,0:T(8,128)(2,1)S(1)}, bf16[14,32,512]{2,1,0:T(8,128)(2,1)S(1)}, u32[]{:S(2)}, u32[]{:S(2)}) collective-permute-start(bf16[14,32,512]{2,1,0:T(8,128)(2,1)S(1)} %slice.24), channel_id=1, source_target_pairs={{0,12},{1,13},{2,14},{3,15},{4,0},{5,1},{6,2},{7,3},{8,4},{9,5},{1... | collective-permute-start | bytes 1376264 | tf_op jit(solution)/shard_map/ppermute | solution.py:51
  50.5 15.6 %copy-start.2 = (bf16[27,32,512]{2,1,0:T(8,128)(2,1)S(1)}, bf16[27,32,512]{2,1,0:T(8,128)(2,1)}, u32[]{:S(2)}) copy-start(bf16[27,32,512]{2,1,0:T(8,128)(2,1)} %own) | copy-start | bytes 2654212
  58.1 16.6 %collective-permute-start.13 = (bf16[2,13,16,512]{3,2,1,0:T(8,128)(2,1)S(1)}, bf16[2,13,16,512]{3,2,1,0:T(8,128)(2,1)S(1)}, u32[]{:S(2)}, u32[]{:S(2)}) collective-permute-start(bf16[2,13,16,512]{3,2,1,0:T(8,128)(2,1)S(1)} %get-tuple-element.108), channel_id=1, source_target_pairs={{0,32},{16,48},{32,64},{48,80},{64,96},{80,112},{96,0},{112,16},{1... | collective-permute-start | bytes 1277960 | tf_op jit(solution)/shard_map/ppermute | solution.py:56
  61.5 13.3 %collective-permute-start.14 = (bf16[2,13,16,512]{3,2,1,0:T(8,128)(2,1)S(1)}, bf16[2,13,16,512]{3,2,1,0:T(8,128)(2,1)S(1)}, u32[]{:S(2)}, u32[]{:S(2)}) collective-permute-start(bf16[2,13,16,512]{3,2,1,0:T(8,128)(2,1)S(1)} %get-tuple-element.109), channel_id=1, source_target_pairs={{0,96},{16,112},{32,0},{48,16},{64,32},{80,48},{96,64},{112,80},{1... | collective-permute-start | bytes 1277960 | tf_op jit(solution)/shard_map/ppermute | solution.py:56
  62.8 13.2 %collective-permute-start.15 = (bf16[2,14,16,512]{3,2,1,0:T(8,128)(2,1)S(1)}, bf16[2,14,16,512]{3,2,1,0:T(8,128)(2,1)S(1)}, u32[]{:S(2)}, u32[]{:S(2)}) collective-permute-start(bf16[2,14,16,512]{3,2,1,0:T(8,128)(2,1)S(1)} %get-tuple-element.110), channel_id=1, source_target_pairs={{0,4},{1,5},{2,6},{3,7},{4,8},{5,9},{6,10},{7,11},{8,12},{9,13},{1... | collective-permute-start | bytes 1376264 | tf_op jit(solution)/shard_map/ppermute | solution.py:51
  62.8 13.1 %collective-permute-start.16 = (bf16[2,14,16,512]{3,2,1,0:T(8,128)(2,1)S(1)}, bf16[2,14,16,512]{3,2,1,0:T(8,128)(2,1)S(1)}, u32[]{:S(2)}, u32[]{:S(2)}) collective-permute-start(bf16[2,14,16,512]{3,2,1,0:T(8,128)(2,1)S(1)} %get-tuple-element.111), channel_id=1, source_target_pairs={{0,12},{1,13},{2,14},{3,15},{4,0},{5,1},{6,2},{7,3},{8,4},{9,5},{1... | collective-permute-start | bytes 1376264 | tf_op jit(solution)/shard_map/ppermute | solution.py:51
  76.0 11.9 %collective-permute-start.21 = (f32[2,4,8,16,512]{4,3,2,1,0:T(8,128)S(1)}, f32[2,4,8,16,512]{4,3,2,1,0:T(8,128)S(1)}, u32[]{:S(2)}, u32[]{:S(2)}) collective-permute-start(f32[2,4,8,16,512]{4,3,2,1,0:T(8,128)S(1)} %get-tuple-element.125), channel_id=1, source_target_pairs={{0,1},{1,0},{2,3},{3,2},{4,5},{5,4},{6,7},{7,6},{8,9},{9,8},{10,11... | collective-permute-start | bytes 6291464 | tf_op jit(solution)/shard_map/ppermute | solution.py:43
  76.1 11.7 %collective-permute-start.19 = (bf16[14,16,512]{2,1,0:T(8,128)(2,1)S(1)}, bf16[14,16,512]{2,1,0:T(8,128)(2,1)S(1)}, u32[]{:S(2)}, u32[]{:S(2)}) collective-permute-start(bf16[14,16,512]{2,1,0:T(8,128)(2,1)S(1)} %get-tuple-element.123), channel_id=1, source_target_pairs={{0,4},{1,5},{2,6},{3,7},{4,8},{5,9},{6,10},{7,11},{8,12},{9,13},{1... | collective-permute-start | bytes 688136 | tf_op jit(solution)/shard_map/ppermute | solution.py:51
  76.2 11.6 %collective-permute-start.20 = (bf16[14,16,512]{2,1,0:T(8,128)(2,1)S(1)}, bf16[14,16,512]{2,1,0:T(8,128)(2,1)S(1)}, u32[]{:S(2)}, u32[]{:S(2)}) collective-permute-start(bf16[14,16,512]{2,1,0:T(8,128)(2,1)S(1)} %get-tuple-element.124), channel_id=1, source_target_pairs={{0,12},{1,13},{2,14},{3,15},{4,0},{5,1},{6,2},{7,3},{8,4},{9,5},{1... | collective-permute-start | bytes 688136 | tf_op jit(solution)/shard_map/ppermute | solution.py:51
  79.4 8.4 %collective-permute-start.17 = (bf16[13,16,512]{2,1,0:T(8,128)(2,1)S(1)}, bf16[13,16,512]{2,1,0:T(8,128)(2,1)S(1)}, u32[]{:S(2)}, u32[]{:S(2)}) collective-permute-start(bf16[13,16,512]{2,1,0:T(8,128)(2,1)S(1)} %get-tuple-element.121), channel_id=1, source_target_pairs={{0,32},{16,48},{32,64},{48,80},{64,96},{80,112},{96,0},{112,16},{1... | collective-permute-start | bytes 638984 | tf_op jit(solution)/shard_map/ppermute | solution.py:56
  79.8 8.0 %collective-permute-start.18 = (bf16[13,16,512]{2,1,0:T(8,128)(2,1)S(1)}, bf16[13,16,512]{2,1,0:T(8,128)(2,1)S(1)}, u32[]{:S(2)}, u32[]{:S(2)}) collective-permute-start(bf16[13,16,512]{2,1,0:T(8,128)(2,1)S(1)} %get-tuple-element.122), channel_id=1, source_target_pairs={{0,96},{16,112},{32,0},{48,16},{64,32},{80,48},{96,64},{112,80},{1... | collective-permute-start | bytes 638984 | tf_op jit(solution)/shard_map/ppermute | solution.py:56
  88.1 5.8 %collective-permute-start.24 = (bf16[13,8,512]{2,1,0:T(8,128)(2,1)S(1)}, bf16[13,8,512]{2,1,0:T(8,128)(2,1)S(1)}, u32[]{:S(2)}, u32[]{:S(2)}) collective-permute-start(bf16[13,8,512]{2,1,0:T(8,128)(2,1)S(1)} %get-tuple-element.136), channel_id=1, source_target_pairs={{0,12},{1,13},{2,14},{3,15},{4,0},{5,1},{6,2},{7,3},{8,4},{9,5},{1... | collective-permute-start | bytes 319496 | tf_op jit(solution)/shard_map/ppermute | solution.py:51
  89.8 6.4 %collective-permute-start.23 = (bf16[13,8,512]{2,1,0:T(8,128)(2,1)S(1)}, bf16[13,8,512]{2,1,0:T(8,128)(2,1)S(1)}, u32[]{:S(2)}, u32[]{:S(2)}) collective-permute-start(bf16[13,8,512]{2,1,0:T(8,128)(2,1)S(1)} %get-tuple-element.135), channel_id=1, source_target_pairs={{0,8},{1,9},{2,10},{3,11},{4,12},{5,13},{6,14},{7,15},{8,0},{9,1},... | collective-permute-start | bytes 319496 | tf_op jit(solution)/shard_map/ppermute | solution.py:51
  89.8 7.3 %collective-permute-start.22 = (bf16[13,8,512]{2,1,0:T(8,128)(2,1)S(1)}, bf16[13,8,512]{2,1,0:T(8,128)(2,1)S(1)}, u32[]{:S(2)}, u32[]{:S(2)}) collective-permute-start(bf16[13,8,512]{2,1,0:T(8,128)(2,1)S(1)} %get-tuple-element.134), channel_id=1, source_target_pairs={{0,4},{1,5},{2,6},{3,7},{4,8},{5,9},{6,10},{7,11},{8,12},{9,13},{1... | collective-permute-start | bytes 319496 | tf_op jit(solution)/shard_map/ppermute | solution.py:51
  91.0 6.5 %collective-permute-start.27 = (bf16[14,8,512]{2,1,0:T(8,128)(2,1)S(1)}, bf16[14,8,512]{2,1,0:T(8,128)(2,1)S(1)}, u32[]{:S(2)}, u32[]{:S(2)}) collective-permute-start(bf16[14,8,512]{2,1,0:T(8,128)(2,1)S(1)} %get-tuple-element.140), channel_id=1, source_target_pairs={{0,96},{16,112},{32,0},{48,16},{64,32},{80,48},{96,64},{112,80},{1... | collective-permute-start | bytes 344072 | tf_op jit(solution)/shard_map/ppermute | solution.py:56
  93.9 6.4 %collective-permute-start.26 = (bf16[14,8,512]{2,1,0:T(8,128)(2,1)S(1)}, bf16[14,8,512]{2,1,0:T(8,128)(2,1)S(1)}, u32[]{:S(2)}, u32[]{:S(2)}) collective-permute-start(bf16[14,8,512]{2,1,0:T(8,128)(2,1)S(1)} %get-tuple-element.139), channel_id=1, source_target_pairs={{0,64},{16,80},{32,96},{48,112},{64,0},{80,16},{96,32},{112,48},{1... | collective-permute-start | bytes 344072 | tf_op jit(solution)/shard_map/ppermute | solution.py:56
  93.9 7.2 %collective-permute-start.25 = (bf16[14,8,512]{2,1,0:T(8,128)(2,1)S(1)}, bf16[14,8,512]{2,1,0:T(8,128)(2,1)S(1)}, u32[]{:S(2)}, u32[]{:S(2)}) collective-permute-start(bf16[14,8,512]{2,1,0:T(8,128)(2,1)S(1)} %get-tuple-element.138), channel_id=1, source_target_pairs={{0,32},{16,48},{32,64},{48,80},{64,96},{80,112},{96,0},{112,16},{1... | collective-permute-start | bytes 344072 | tf_op jit(solution)/shard_map/ppermute | solution.py:56
  101.3 9.6 %collective-permute-start.28 = (bf16[27,8,512]{2,1,0:T(8,128)(2,1)S(1)}, bf16[27,8,512]{2,1,0:T(8,128)(2,1)S(1)}, u32[]{:S(2)}, u32[]{:S(2)}) collective-permute-start(bf16[27,8,512]{2,1,0:T(8,128)(2,1)S(1)} %pad_maximum_fusion), channel_id=1, source_target_pairs={{0,16},{16,0},{32,48},{48,32},{64,80},{80,64},{96,112},{112,96},{1... | collective-permute-start | bytes 663560 | tf_op jit(solution)/shard_map/ppermute | solution.py:456
  110.9 20.1 %collective-permute-start.29 = (f32[4,8,16,512]{3,2,1,0:T(8,128)S(1)}, f32[4,8,16,512]{3,2,1,0:T(8,128)S(1)}, u32[]{:S(2)}, u32[]{:S(2)}) collective-permute-start(f32[4,8,16,512]{3,2,1,0:T(8,128)S(1)} %bitcast_add_fusion), channel_id=1, source_target_pairs={{0,2},{1,3},{2,0},{3,1},{4,6},{5,7},{6,4},{7,5},{8,10},{9,11},{10,... | collective-permute-start | bytes 3145736 | tf_op jit(solution)/shard_map/ppermute | solution.py:43
  111.8 19.1 %copy-start = (bf16[4,8,16,512]{3,2,1,0:T(8,128)(2,1)S(1)}, bf16[4,8,16,512]{3,2,1,0:T(8,128)(2,1)}, u32[]{:S(2)}) copy-start(bf16[4,8,16,512]{3,2,1,0:T(8,128)(2,1)} %pre.1) | copy-start | bytes 1572868
  111.8 8.1 %collective-permute-start.33 = (f32[14,8,512]{2,1,0:T(8,128)S(1)}, f32[14,8,512]{2,1,0:T(8,128)S(1)}, u32[]{:S(2)}, u32[]{:S(2)}) collective-permute-start(f32[14,8,512]{2,1,0:T(8,128)S(1)} %convert_add_fusion.refs_1_), channel_id=1, source_target_pairs={{0,96},{16,112},{32,0},{48,16},{64,32},{80,48},{96,64},{112,80},{1... | collective-permute-start | bytes 688136 | tf_op jit(solution)/shard_map/ppermute | solution.py:56
  112.8 9.7 %collective-permute-start.30 = (f32[13,8,512]{2,1,0:T(8,128)S(1)}, f32[13,8,512]{2,1,0:T(8,128)S(1)}, u32[]{:S(2)}, u32[]{:S(2)}) collective-permute-start(f32[13,8,512]{2,1,0:T(8,128)S(1)} %convert_add_fusion.2.refs_0_), channel_id=1, source_target_pairs={{0,32},{16,48},{32,64},{48,80},{64,96},{80,112},{96,0},{112,16},{1... | collective-permute-start | bytes 638984 | tf_op jit(solution)/shard_map/ppermute | solution.py:56
  114.1 14.3 %collective-permute-start.31 = (f32[14,8,512]{2,1,0:T(8,128)S(1)}, f32[14,8,512]{2,1,0:T(8,128)S(1)}, u32[]{:S(2)}, u32[]{:S(2)}) collective-permute-start(f32[14,8,512]{2,1,0:T(8,128)S(1)} %convert_add_fusion.refs_1_), channel_id=1, source_target_pairs={{0,32},{16,48},{32,64},{48,80},{64,96},{80,112},{96,0},{112,16},{1... | collective-permute-start | bytes 688136 | tf_op jit(solution)/shard_map/ppermute | solution.py:56
  119.9 9.7 %collective-permute-start.35 = (f32[14,8,512]{2,1,0:T(8,128)S(1)}, f32[14,8,512]{2,1,0:T(8,128)S(1)}, u32[]{:S(2)}, u32[]{:S(2)}) collective-permute-start(f32[14,8,512]{2,1,0:T(8,128)S(1)} %collective-permute-done.33.refs_5_), channel_id=1, source_target_pairs={{0,96},{16,112},{32,0},{48,16},{64,32},{80,48},{96,64},{112,80},{1... | collective-permute-start | bytes 688136 | tf_op jit(solution)/shard_map/ppermute | solution.py:56
  122.5 5.8 %collective-permute-start.32 = (f32[13,8,512]{2,1,0:T(8,128)S(1)}, f32[13,8,512]{2,1,0:T(8,128)S(1)}, u32[]{:S(2)}, u32[]{:S(2)}) collective-permute-start(f32[13,8,512]{2,1,0:T(8,128)S(1)} %convert_add_fusion.2.refs_0_), channel_id=1, source_target_pairs={{0,96},{16,112},{32,0},{48,16},{64,32},{80,48},{96,64},{112,80},{1... | collective-permute-start | bytes 638984 | tf_op jit(solution)/shard_map/ppermute | solution.py:56
  122.6 7.1 %collective-permute-start.34 = (f32[13,8,512]{2,1,0:T(8,128)S(1)}, f32[13,8,512]{2,1,0:T(8,128)S(1)}, u32[]{:S(2)}, u32[]{:S(2)}) collective-permute-start(f32[13,8,512]{2,1,0:T(8,128)S(1)} %collective-permute-done.30.refs_2_), channel_id=1, source_target_pairs={{0,32},{16,48},{32,64},{48,80},{64,96},{80,112},{96,0},{112,16},{1... | collective-permute-start | bytes 638984 | tf_op jit(solution)/shard_map/ppermute | solution.py:56

commit v9 on v8

--- a/solution.py
+++ b/solution.py
@@ -62,40 +62,42 @@
     return lax.ppermute(block, "gx", pairs + [(t, s) for s, t in pairs])
 
 
+def swap_y(block, first):
+    count = lax.axis_size("gy")
+    pairs = [(g, g + QUAD) for g in range(count - QUAD) if (g // QUAD - first) % 2 == 0]
+    return lax.ppermute(block, "gy", pairs + [(t, s) for s, t in pairs])
+
+
 def zero_at(value, z, edge):
     return jnp.where(z == edge, 0.0, value)
 
 
-def pick_kernel(cot, extra, *quarters):
-    rows, _, _, chan = cot.shape
+def pick_kernel(cot, *quarters):
+    chan = cot.shape[3]
     j = quad_place()
     q = chan // QUAD
     part = q // RING
     source = lax.broadcasted_iota(jnp.int32, (chan, q), 0)
     place = lax.broadcasted_iota(jnp.int32, (chan, q), 1)
     base = lax.div(place, part) * q + lax.rem(place, part)
-
-    def take(block, pick):
-        got = jnp.dot(block.reshape(-1, chan), pick, preferred_element_type=F32)
-        return got.astype(BF16).reshape(block.shape[:-1] + (q,))
-
+    flat = cot[...].reshape(-1, chan)
     for k, out in enumerate(quarters):
         pick = jnp.where(source == base + (j ^ k) * part, 1.0, 0.0).astype(BF16)
-        out[0:rows] = take(cot[...], pick)
-        out[rows] = take(extra[...], pick)
-
-
-def pick_channels(cot, extra):
+        got = jnp.dot(flat, pick, preferred_element_type=F32)
+        out[...] = got.astype(BF16).reshape(out.shape)
+
+
+def pick_channels(cot):
     rows, width, depth, chan = cot.shape
-    quarter = jax.ShapeDtypeStruct((rows + 1, width, depth, chan // QUAD), BF16)
+    quarter = jax.ShapeDtypeStruct((rows, width, depth, chan // QUAD), BF16)
     return pl.pallas_call(
         pick_kernel,
         out_shape=[quarter] * QUAD,
-        in_specs=[VMEM] * 2,
+        in_specs=[VMEM],
         out_specs=[VMEM] * QUAD,
         compiler_params=params(),
         cost_estimate=small_cost(),
-    )(cot, extra)
+    )(cot)
 
 
 def side_kernel(p0, p1, p2, p3, even, odd):
@@ -119,22 +121,55 @@
     )(*quarters)
 
 
-def turn_kernel(p0, p1, p2, p3, even, odd, held, out):
+def rim_of(even, odd, k):
+    is_odd = lax.rem(lax.axis_index("gx"), 2) == 1
+    return jnp.where(is_odd, even[k], odd[k]), jnp.where(is_odd, odd[k], even[k])
+
+
+def edge_kernel(p0, p1, p2, p3, even, odd, first, second):
+    j = quad_place()
+    is_odd = lax.rem(y_place(), 2) == 1
+    rows, width = p0.shape[:2]
+
+    def put(out, p, k, row):
+        low, high = rim_of(even, odd, k)
+        out[1:width + 1] = p[row]
+        out[0] = low[row]
+        out[width + 1] = high[row]
+
+    for k, p in enumerate((p0, p1, p2, p3)):
+        is_top, is_bottom = (j ^ k) == QUAD - 1, (j ^ k) == 0
+        not_odd = jnp.logical_not(is_odd)
+        pl.when(is_top & not_odd)(functools.partial(put, first, p, k, rows - 1))
+        pl.when(is_top & is_odd)(functools.partial(put, second, p, k, rows - 1))
+        pl.when(is_bottom & not_odd)(functools.partial(put, second, p, k, 0))
+        pl.when(is_bottom & is_odd)(functools.partial(put, first, p, k, 0))
+
+
+def edge_rows(quarters, even, odd):
+    _, width, depth, q = quarters[0].shape
+    return pl.pallas_call(
+        edge_kernel,
+        out_shape=[jax.ShapeDtypeStruct((width + 2, depth, q), BF16)] * 2,
+        in_specs=[VMEM] * (QUAD + 2),
+        out_specs=[VMEM] * 2,
+        compiler_params=params(),
+        cost_estimate=small_cost(),
+    )(*quarters, even, odd)
+
+
+def turn_kernel(p0, p1, p2, p3, even, odd, first, second, held, out):
     j, x = quad_place(), x_place()
-    is_odd = lax.rem(lax.axis_index("gx"), 2) == 1
+    is_odd = lax.rem(y_place(), 2) == 1
+    held[0] = jnp.where(is_odd, first[...], second[...])
+    held[held.shape[0] - 1] = jnp.where(is_odd, second[...], first[...])
     for k, p in enumerate((p0, p1, p2, p3)):
-        rows, width = p.shape[0] - 1, p.shape[1]
-        low = jnp.where(is_odd, even[k], odd[k])
-        high = jnp.where(is_odd, odd[k], even[k])
-
-        def put(at, part):
-            held[at, 1:width + 1] = p[part]
-            held[at, 0] = low[part]
-            held[at, width + 1] = high[part]
-
-        put(pl.ds(1 + (j ^ k) * rows, rows), slice(0, rows))
-        pl.when((j ^ k) == 0)(functools.partial(put, 0, rows))
-        pl.when((j ^ k) == QUAD - 1)(functools.partial(put, held.shape[0] - 1, rows))
+        rows, width = p.shape[:2]
+        low, high = rim_of(even, odd, k)
+        at = pl.ds(1 + (j ^ k) * rows, rows)
+        held[at, 1:width + 1] = p[...]
+        held[at, 0] = low
+        held[at, width + 1] = high
 
     tall, width, depth, q = held.shape
     width -= 2
@@ -160,21 +195,21 @@
             out[at:at + q] = v.astype(BF16)
 
 
-def turn(quarters, even, odd):
+def turn(quarters, *rims):
     rows, width, depth, q = quarters[0].shape
     width += 2
-    tall = QUAD * (rows - 1) + 2
+    tall = QUAD * rows + 2
     return pl.pallas_call(
         turn_kernel,
         out_shape=[
             jax.ShapeDtypeStruct((tall, width, depth, q), BF16),
             jax.ShapeDtypeStruct((9 * q, tall * (width - 2) * depth), BF16),
         ],
-        in_specs=[VMEM] * (QUAD + 2),
+        in_specs=[VMEM] * (QUAD + 4),
         out_specs=[VMEM] * 2,
         compiler_params=params(),
         cost_estimate=small_cost(),
-    )(*quarters, even, odd)
+    )(*quarters, *rims)
 
 
 def run_copies(pairs, sem):
@@ -402,29 +437,25 @@
 def body(pre_act, cot, weight):
     rows, width, depth, chan = pre_act.shape
     norm = 1.0 / math.sqrt(rows * lax.axis_size("gy") * width * lax.axis_size("gx") * depth)
-    j = quad_place()
     barrier = lax.optimization_barrier
 
-    count = lax.axis_size("gy")
-    pairs = [(g, g + 1) for g in range(QUAD - 1, count - 1, QUAD)]
-    pairs = pairs + [(t, s) for s, t in pairs]
-    extra = lax.ppermute(jnp.where(j == 0, cot[0], cot[rows - 1]), "gy", pairs)
+    quarters = pick_channels(cot)
+    quarters = [quarters[0]] + [swap(quarters[k], k) for k in (1, 2, 3)]
     act = jax.nn.silu(pre_act.astype(F32)).astype(BF16)
     near = swap(act, 1)
-    extra, near, weight = barrier((extra, near, weight))
     above = along_y(weight, -1, True)
     below = along_y(weight, 1, True)
-    quarters = pick_channels(cot, extra)
-    quarters = [quarters[0]] + [swap(quarters[k], k) for k in (1, 2, 3)]
-    quarters, act = barrier((quarters, act))
+    even, odd = sides(quarters)
+    even, odd, act = barrier((even, odd, act))
+    even, odd = swap_x(even, 0), swap_x(odd, 1)
     far = swap(act, 2)
-    even, odd = sides(quarters)
-    even, odd = swap_x(even, 0), swap_x(odd, 1)
-    even, odd, above, below, far = barrier((even, odd, above, below, far))
+    first, second = edge_rows(quarters, even, odd)
+    first, second = swap_y(first, 0), swap_y(second, 1)
+    first, second, above, below, far = barrier((first, second, above, below, far))
     acts = [act, near, far, swap(far, 1)]
     taps = XTAPS
     parts = [weight, above, along_y(below[:taps], 1, True), along_y(above[taps:], -1, True), below]
-    held, turned = turn(quarters, even, odd)
+    held, turned = turn(quarters, even, odd, first, second)
 
     terms = weight_terms(norm, acts, turned)
     held, terms = barrier((held, terms))

time: 133 us -> 127 us (0.955)
  starting transfers between devices: 50.8 us -> 44.6 us
    ppermute x11, starting transfers between devices: 23.1 us -> 16.5 us  [along_y(): lax.ppermute(block, 'gy', [(s, t) for s, t in pairs if 0 <= t < count])]
    ppermute x8, waiting for transfers between devices: 8.01 us -> 5.18 us  [swap(): return lax.ppermute(block, 'gy', [(g, g ^ k) for g in range(count)])]
    ppermute x1 -> x2, waiting for transfers between devices: 0.01 us -> 2.77 us  [swap_y(): return lax.ppermute(block, 'gy', pairs + [(t, s) for s, t in pairs])]
  transfers between devices with their start and end apart: 36 -> 37, of which waited for: 15 -> 16; matrix products, arithmetic and copies ran while one was open for 1% -> 1% of each run, Pallas kernels for 16% -> 16%
where the time goes in v9:
time: 127 us; the launch traced here: 126 us
  waiting for transfers between devices  55.2 us (43%)
  starting transfers between devices  44.6 us (35%)
  Pallas kernels  22.1 us (17%)
  other arithmetic  1.86 us (1%)
    ppermute x13, waiting for transfers between devices, along_x(): lax.ppermute(block, 'gx', [(g, (g + 2 * step) % count) for g in range(cou...  20.2 us
    ppermute x13, starting transfers between devices, along_x(): lax.ppermute(block, 'gx', [(g, (g + 2 * step) % count) for g in range(cou...  18 us
    ppermute x11, starting transfers between devices, along_y(): lax.ppermute(block, 'gy', [(s, t) for s, t in pairs if 0 <= t < count])  16.5 us
    ppermute x2, waiting for transfers between devices, swap_x(): return lax.ppermute(block, 'gx', pairs + [(t, s) for s, t in pairs])  13.1 us
    ppermute x1, waiting for transfers between devices, body(): other = lax.ppermute(mine, 'gx', [(g, g ^ 1) for g in range(count)])  9.46 us
    pallas_call x1, Pallas kernels, input_terms(): pl.pallas_call(input_kernel, out_shape=[jax.ShapeDtypeStruct((2,) + block...  8.65 us
    pallas_call x1, Pallas kernels, weight_terms(): pl.pallas_call(functools.partial(weight_kernel, norm), out_shape=shapes,...  7.66 us
    ppermute x8, waiting for transfers between devices, swap(): return lax.ppermute(block, 'gy', [(g, g ^ k) for g in range(count)])  5.18 us
  transfers between devices with their start and end apart: 37, of which 16 were waited for; matrix products, arithmetic and copies ran while one was open for 1% of the time, Pallas kernels for 16%

profile of v9, /device:TPU:0, one launch (start us, length us, event | category | flops | bytes accessed | tf_op | source)
XLA Modules:
  0.0 125.8 jit_solution(8107141874460885991)
XLA Ops:
  0.6 3.2 %collective-permute-start.7 = (bf16[27,32,512]{2,1,0:T(8,128)(2,1)}, bf16[27,32,512]{2,1,0:T(8,128)(2,1)S(1)}, u32[]{:S(2)}, u32[]{:S(2)}) collective-permute-start(bf16[27,32,512]{2,1,0:T(8,128)(2,1)} %own.1), channel_id=1, source_target_pairs={{0,12},{1,13},{2,14},{3,15},{4,0},{5,1},{6,2},{7,3},{8,4},{9,5},{1... | collective-permute-start | bytes 2654216 | tf_op jit(solution)/shard_map/ppermute | solution.py:51
  3.8 1.0 copy-done.1
  4.8 0.7 shard_map.50
  5.7 2.0 %collective-permute-start.1 = (bf16[4,8,16,128]{3,2,1,0:T(8,128)(2,1)S(1)}, bf16[4,8,16,128]{3,2,1,0:T(8,128)(2,1)S(1)}, u32[]{:S(2)}, u32[]{:S(2)}) collective-permute-start(bf16[4,8,16,128]{3,2,1,0:T(8,128)(2,1)S(1)} %get-tuple-element.72), channel_id=1, source_target_pairs={{0,2},{1,3},{2,0},{3,1},{4,6},{5,7},{6,4},{7,5},{8,10},{9,11},{10,... | collective-permute-start | bytes 393224 | tf_op jit(solution)/shard_map/ppermute | solution.py:43
  7.7 1.4 %fusion.3.own_act = bf16[4,8,16,512]{3,2,1,0:T(8,128)(2,1)S(1)} fusion(bf16[4,8,16,512]{3,2,1,0:T(8,128)(2,1)} %pre.1), kind=kLoop, calls=%fused_computation.5 | loop fusion | flops 1572864 | bytes 1048576 | tf_op jit(solution)/shard_map/convert_element_type | solution.py:444
  9.1 2.9 %collective-permute-done.1.p2 = bf16[4,8,16,128]{3,2,1,0:T(8,128)(2,1)S(1)} collective-permute-done((bf16[4,8,16,128]{3,2,1,0:T(8,128)(2,1)S(1)}, bf16[4,8,16,128]{3,2,1,0:T(8,128)(2,1)S(1)}, u32[]{:S(2)}, u32[]{:S(2)}) %collective-permute-start.1) | collective-permute-done | bytes 131104 | tf_op jit(solution)/shard_map/ppermute | solution.py:43
  12.0 2.2 %collective-permute-done.2.p3 = bf16[4,8,16,128]{3,2,1,0:T(8,128)(2,1)S(1)} collective-permute-done((bf16[4,8,16,128]{3,2,1,0:T(8,128)(2,1)S(1)}, bf16[4,8,16,128]{3,2,1,0:T(8,128)(2,1)S(1)}, u32[]{:S(2)}, u32[]{:S(2)}) %collective-permute-start.2) | collective-permute-done | bytes 131104 | tf_op jit(solution)/shard_map/ppermute | solution.py:43
  14.3 1.7 %collective-permute-start.9 = (bf16[4,8,16,512]{3,2,1,0:T(8,128)(2,1)S(1)}, bf16[4,8,16,512]{3,2,1,0:T(8,128)(2,1)S(1)}, u32[]{:S(2)}, u32[]{:S(2)}) collective-permute-start(bf16[4,8,16,512]{3,2,1,0:T(8,128)(2,1)S(1)} %fusion.3.own_act), channel_id=1, source_target_pairs={{0,2},{1,3},{2,0},{3,1},{4,6},{5,7},{6,4},{7,5},{8,10},{9,11},{10,... | collective-permute-start | bytes 1572872 | tf_op jit(solution)/shard_map/ppermute | solution.py:43
  15.9 3.6 %collective-permute-start.3 = (bf16[4,4,16,128]{3,2,1,0:T(8,128)(2,1)S(1)}, bf16[4,4,16,128]{3,2,1,0:T(8,128)(2,1)S(1)}, u32[]{:S(2)}, u32[]{:S(2)}) collective-permute-start(bf16[4,4,16,128]{3,2,1,0:T(8,128)(2,1)S(1)} %get-tuple-element.76), channel_id=1, source_target_pairs={{0,16},{32,48},{64,80},{96,112},{16,0},{48,32},{80,64},{112,96},{1... | collective-permute-start | bytes 196616 | tf_op jit(solution)/shard_map/ppermute | solution.py:62
  19.5 0.7 collective-permute-start.4
  20.2 13.1 %collective-permute-done.3.even = bf16[4,4,16,128]{3,2,1,0:T(8,128)(2,1)S(1)} collective-permute-done((bf16[4,4,16,128]{3,2,1,0:T(8,128)(2,1)S(1)}, bf16[4,4,16,128]{3,2,1,0:T(8,128)(2,1)S(1)}, u32[]{:S(2)}, u32[]{:S(2)}) %collective-permute-start.3) | collective-permute-done | bytes 65568 | tf_op jit(solution)/shard_map/ppermute | solution.py:62
  33.4 0.7 collective-permute-start.5
  34.1 0.7 collective-permute-start.6
  34.7 2.8 %collective-permute-done.5.first = bf16[10,16,128]{2,1,0:T(8,128)(2,1)S(1)} collective-permute-done((bf16[10,16,128]{2,1,0:T(8,128)(2,1)S(1)}, bf16[10,16,128]{2,1,0:T(8,128)(2,1)S(1)}, u32[]{:S(2)}, u32[]{:S(2)}) %collective-permute-start.5) | collective-permute-done | bytes 40992 | tf_op jit(solution)/shard_map/ppermute | solution.py:68
  37.5 0.6 collective-permute-start.11
  38.1 4.1 %collective-permute-start.12 = (bf16[13,32,512]{2,1,0:T(8,128)(2,1)S(1)}, bf16[13,32,512]{2,1,0:T(8,128)(2,1)S(1)}, u32[]{:S(2)}, u32[]{:S(2)}) collective-permute-start(bf16[13,32,512]{2,1,0:T(8,128)(2,1)S(1)} %slice.15), channel_id=1, source_target_pairs={{0,4},{1,5},{2,6},{3,7},{4,8},{5,9},{6,10},{7,11},{8,12},{9,13},{1... | collective-permute-start | bytes 1277960 | tf_op jit(solution)/shard_map/ppermute | solution.py:51
  42.3 2.0 %shard_map.53 = (bf16[18,10,16,128]{3,2,1,0:T(8,128)(2,1)S(1)}, bf16[1152,2304]{1,0:T(8,128)(2,1)S(1)}) custom-call(bf16[4,8,16,128]{3,2,1,0:T(8,128)(2,1)S(1)} %get-tuple-element.70.p0, bf16[4,8,16,128]{3,2,1,0:T(8,128)(2,1)S(1)} %collective-permute-done.p1, bf16[4,8,16,128]{3,2,1,0:T(8,128)(2,1)S(1)} %collective-permute-done.1.p2, ...), custom_call_target="tpu_custom_call" | custom-call | flops 1000 | bytes 1000 | tf_op jit(solution)/shard_map/pallas_call | solution.py:202
  44.4 7.7 %shard_map.54 = (bf16[2,13,16,512]{3,2,1,0:T(8,128)(2,1)S(1)}, bf16[2,13,16,512]{3,2,1,0:T(8,128)(2,1)S(1)}, f32[13,16,512]{2,1,0:T(8,128)S(1)}, f32[13,16,512]{...) custom-call(bf16[4,8,16,512]{3,2,1,0:T(8,128)(2,1)S(1)} %fusion.3.ow, ...), custom_call_target="tpu_custom_call" | custom-call | flops 7247757312 | bytes 10000000 | tf_op jit(solution)/shard_map/pallas_call | solution.py:271
  52.1 3.0 %collective-permute-start.14 = (bf16[2,13,16,512]{3,2,1,0:T(8,128)(2,1)S(1)}, bf16[2,13,16,512]{3,2,1,0:T(8,128)(2,1)S(1)}, u32[]{:S(2)}, u32[]{:S(2)}) collective-permute-start(bf16[2,13,16,512]{3,2,1,0:T(8,128)(2,1)S(1)} %get-tuple-element.102), channel_id=1, source_target_pairs={{0,32},{16,48},{32,64},{48,80},{64,96},{80,112},{96,0},{112,16},{1... | collective-permute-start | bytes 1277960 | tf_op jit(solution)/shard_map/ppermute | solution.py:56
  55.0 1.4 %collective-permute-start.15 = (bf16[2,13,16,512]{3,2,1,0:T(8,128)(2,1)S(1)}, bf16[2,13,16,512]{3,2,1,0:T(8,128)(2,1)S(1)}, u32[]{:S(2)}, u32[]{:S(2)}) collective-permute-start(bf16[2,13,16,512]{3,2,1,0:T(8,128)(2,1)S(1)} %get-tuple-element.103), channel_id=1, source_target_pairs={{0,96},{16,112},{32,0},{48,16},{64,32},{80,48},{96,64},{112,80},{1... | collective-permute-start | bytes 1277960 | tf_op jit(solution)/shard_map/ppermute | solution.py:56
  56.4 2.0 %collective-permute-start.16 = (bf16[2,14,16,512]{3,2,1,0:T(8,128)(2,1)S(1)}, bf16[2,14,16,512]{3,2,1,0:T(8,128)(2,1)S(1)}, u32[]{:S(2)}, u32[]{:S(2)}) collective-permute-start(bf16[2,14,16,512]{3,2,1,0:T(8,128)(2,1)S(1)} %get-tuple-element.104), channel_id=1, source_target_pairs={{0,4},{1,5},{2,6},{3,7},{4,8},{5,9},{6,10},{7,11},{8,12},{9,13},{1... | collective-permute-start | bytes 1376264 | tf_op jit(solution)/shard_map/ppermute | solution.py:51
  58.4 1.2 collective-permute-start.17
  59.6 8.6 %shard_map.55 = (f32[2,4,8,16,512]{4,3,2,1,0:T(8,128)S(1)}, f32[4,8,16,512]{3,2,1,0:T(8,128)S(1)}, f32[4,8,16,512]{3,2,1,0:T(8,128)S(1)}) custom-call(bf16[18,10,16,128]{3,2,1,0:T(8,128)(2,1)S(1)} %get-tuple-element.96.held, bf16[27,32,512]{2,1,0:T(8,128)(2,1)S(1)} %copy-done.2, bf16[27,32,512]{2,1,0:T(8,128)(2,1)S(1)} %collective-permute-done.7.above, ...), custom_call_target="tpu_custom_call" | custom-call | flops 10192158720 | bytes 10000000 | tf_op jit(solution)/shard_map/pallas_call | solution.py:333
  68.3 1.6 %collective-permute-done.16.refs_4_.refs_6_ = bf16[2,14,16,512]{3,2,1,0:T(8,128)(2,1)S(1)} collective-permute-done((bf16[2,14,16,512]{3,2,1,0:T(8,128)(2,1)S(1)}, bf16[2,14,16,512]{3,2,1,0:T(8,128)(2,1)S(1)}, u32[]{:S(2)}, u32[]{:S(2)}) %collective-permute-start.16) | collective-permute-done | bytes 458784 | tf_op jit(solution)/shard_map/ppermute | solution.py:51
  69.9 0.5 collective-permute-done.17.refs_6_.refs_7_
  70.6 1.8 %collective-permute-start.20 = (bf16[14,16,512]{2,1,0:T(8,128)(2,1)S(1)}, bf16[14,16,512]{2,1,0:T(8,128)(2,1)S(1)}, u32[]{:S(2)}, u32[]{:S(2)}) collective-permute-start(bf16[14,16,512]{2,1,0:T(8,128)(2,1)S(1)} %get-tuple-element.117), channel_id=1, source_target_pairs={{0,4},{1,5},{2,6},{3,7},{4,8},{5,9},{6,10},{7,11},{8,12},{9,13},{1... | collective-permute-start | bytes 688136 | tf_op jit(solution)/shard_map/ppermute | solution.py:51
  72.4 1.5 %collective-permute-start.21 = (bf16[14,16,512]{2,1,0:T(8,128)(2,1)S(1)}, bf16[14,16,512]{2,1,0:T(8,128)(2,1)S(1)}, u32[]{:S(2)}, u32[]{:S(2)}) collective-permute-start(bf16[14,16,512]{2,1,0:T(8,128)(2,1)S(1)} %get-tuple-element.118), channel_id=1, source_target_pairs={{0,12},{1,13},{2,14},{3,15},{4,0},{5,1},{6,2},{7,3},{8,4},{9,5},{1... | collective-permute-start | bytes 688136 | tf_op jit(solution)/shard_map/ppermute | solution.py:51
  73.9 0.4 collective-permute-start.18
  74.3 2.8 %collective-permute-start.19 = (bf16[13,16,512]{2,1,0:T(8,128)(2,1)S(1)}, bf16[13,16,512]{2,1,0:T(8,128)(2,1)S(1)}, u32[]{:S(2)}, u32[]{:S(2)}) collective-permute-start(bf16[13,16,512]{2,1,0:T(8,128)(2,1)S(1)} %get-tuple-element.116), channel_id=1, source_target_pairs={{0,96},{16,112},{32,0},{48,16},{64,32},{80,48},{96,64},{112,80},{1... | collective-permute-start | bytes 638984 | tf_op jit(solution)/shard_map/ppermute | solution.py:56
  77.2 5.1 %collective-permute-done.18.refs_3_ = bf16[13,16,512]{2,1,0:T(8,128)(2,1)S(1)} collective-permute-done((bf16[13,16,512]{2,1,0:T(8,128)(2,1)S(1)}, bf16[13,16,512]{2,1,0:T(8,128)(2,1)S(1)}, u32[]{:S(2)}, u32[]{:S(2)}) %collective-permute-start.18) | collective-permute-done | bytes 213024 | tf_op jit(solution)/shard_map/ppermute | solution.py:56
  82.5 1.3 %collective-permute-start.25 = (bf16[13,8,512]{2,1,0:T(8,128)(2,1)S(1)}, bf16[13,8,512]{2,1,0:T(8,128)(2,1)S(1)}, u32[]{:S(2)}, u32[]{:S(2)}) collective-permute-start(bf16[13,8,512]{2,1,0:T(8,128)(2,1)S(1)} %get-tuple-element.130), channel_id=1, source_target_pairs={{0,12},{1,13},{2,14},{3,15},{4,0},{5,1},{6,2},{7,3},{8,4},{9,5},{1... | collective-permute-start | bytes 319496 | tf_op jit(solution)/shard_map/ppermute | solution.py:51
  83.8 1.4 %collective-permute-start.24 = (bf16[13,8,512]{2,1,0:T(8,128)(2,1)S(1)}, bf16[13,8,512]{2,1,0:T(8,128)(2,1)S(1)}, u32[]{:S(2)}, u32[]{:S(2)}) collective-permute-start(bf16[13,8,512]{2,1,0:T(8,128)(2,1)S(1)} %get-tuple-element.129), channel_id=1, source_target_pairs={{0,8},{1,9},{2,10},{3,11},{4,12},{5,13},{6,14},{7,15},{8,0},{9,1},... | collective-permute-start | bytes 319496 | tf_op jit(solution)/shard_map/ppermute | solution.py:51
  85.2 2.9 %collective-permute-start.28 = (bf16[14,8,512]{2,1,0:T(8,128)(2,1)S(1)}, bf16[14,8,512]{2,1,0:T(8,128)(2,1)S(1)}, u32[]{:S(2)}, u32[]{:S(2)}) collective-permute-start(bf16[14,8,512]{2,1,0:T(8,128)(2,1)S(1)} %get-tuple-element.134), channel_id=1, source_target_pairs={{0,96},{16,112},{32,0},{48,16},{64,32},{80,48},{96,64},{112,80},{1... | collective-permute-start | bytes 344072 | tf_op jit(solution)/shard_map/ppermute | solution.py:56
  88.1 0.9 collective-permute-start.26
  89.0 1.2 collective-permute-done.24
  90.2 1.1 collective-permute-done.23
  91.7 2.8 %collective-permute-done.27 = bf16[14,8,512]{2,1,0:T(8,128)(2,1)S(1)} collective-permute-done((bf16[14,8,512]{2,1,0:T(8,128)(2,1)S(1)}, bf16[14,8,512]{2,1,0:T(8,128)(2,1)S(1)}, u32[]{:S(2)}, u32[]{:S(2)}) %collective-permute-start.27) | collective-permute-done | bytes 114720 | tf_op jit(solution)/shard_map/ppermute | solution.py:56
  94.5 0.8 collective-permute-done.26
  95.8 9.5 %collective-permute-done.29 = bf16[27,8,512]{2,1,0:T(8,128)(2,1)S(1)} collective-permute-done((bf16[27,8,512]{2,1,0:T(8,128)(2,1)S(1)}, bf16[27,8,512]{2,1,0:T(8,128)(2,1)S(1)}, u32[]{:S(2)}, u32[]{:S(2)}) %collective-permute-start.29) | collective-permute-done | bytes 221216 | tf_op jit(solution)/shard_map/ppermute | solution.py:487
  105.4 1.0 collective-permute-start.34
  106.5 1.1 collective-permute-start.31
  107.7 6.0 %collective-permute-done.34.refs_5_ = f32[14,8,512]{2,1,0:T(8,128)S(1)} collective-permute-done((f32[14,8,512]{2,1,0:T(8,128)S(1)}, f32[14,8,512]{2,1,0:T(8,128)S(1)}, u32[]{:S(2)}, u32[]{:S(2)}) %collective-permute-start.34) | collective-permute-done | bytes 229408 | tf_op jit(solution)/shard_map/ppermute | solution.py:56
  113.8 2.4 %collective-permute-start.36 = (f32[14,8,512]{2,1,0:T(8,128)S(1)}, f32[14,8,512]{2,1,0:T(8,128)S(1)}, u32[]{:S(2)}, u32[]{:S(2)}) collective-permute-start(f32[14,8,512]{2,1,0:T(8,128)S(1)} %collective-permute-done.34.refs_5_), channel_id=1, source_target_pairs={{0,96},{16,112},{32,0},{48,16},{64,32},{80,48},{96,64},{112,80},{1... | collective-permute-start | bytes 688136 | tf_op jit(solution)/shard_map/ppermute | solution.py:56
  116.2 2.0 %collective-permute-start.35 = (f32[13,8,512]{2,1,0:T(8,128)S(1)}, f32[13,8,512]{2,1,0:T(8,128)S(1)}, u32[]{:S(2)}, u32[]{:S(2)}) collective-permute-start(f32[13,8,512]{2,1,0:T(8,128)S(1)} %collective-permute-done.31.refs_2_), channel_id=1, source_target_pairs={{0,32},{16,48},{32,64},{48,80},{64,96},{80,112},{96,0},{112,16},{1... | collective-permute-start | bytes 638984 | tf_op jit(solution)/shard_map/ppermute | solution.py:56
  118.1 3.9 %collective-permute-done.33.refs_4_ = f32[13,8,512]{2,1,0:T(8,128)S(1)} collective-permute-done((f32[13,8,512]{2,1,0:T(8,128)S(1)}, f32[13,8,512]{2,1,0:T(8,128)S(1)}, u32[]{:S(2)}, u32[]{:S(2)}) %collective-permute-start.33) | collective-permute-done | bytes 213024 | tf_op jit(solution)/shard_map/ppermute | solution.py:56
  122.1 1.1 collective-permute-done.35.refs_6_
  123.2 1.3 %shard_map.59 = f32[27,32,512]{2,1,0:T(8,128)} custom-call(f32[13,8,512]{2,1,0:T(8,128)S(1)} %convert_add_fusion.2.refs_0_, f32[14,8,512]{2,1,0:T(8,128)S(1)} %convert_add_fusion.refs_1_, f32[13,8,512]{2,1,0:T(8,128)S(1)} %collective-permute-done.31.refs_2_, f32[14,8,512]{2,1,0:T(8,128)S(1)} %collective-permute-done.32.refs_3_, ...), custom_call_target="tpu_custom_call" | custom-call | tf_op jit(solution)/shard_map/pallas_call | solution.py:428
  124.6 1.2 shard_map.58
  (51 shorter events, 2.0 us)
Async XLA Ops:
  0.6 36.9 %collective-permute-start.7 = (bf16[27,32,512]{2,1,0:T(8,128)(2,1)}, bf16[27,32,512]{2,1,0:T(8,128)(2,1)S(1)}, u32[]{:S(2)}, u32[]{:S(2)}) collective-permute-start(bf16[27,32,512]{2,1,0:T(8,128)(2,1)} %own.1), channel_id=1, source_target_pairs={{0,12},{1,13},{2,14},{3,15},{4,0},{5,1},{6,2},{7,3},{8,4},{9,5},{1... | collective-permute-start | bytes 2654216 | tf_op jit(solution)/shard_map/ppermute | solution.py:51
  3.8 33.7 %collective-permute-start.8 = (bf16[27,32,512]{2,1,0:T(8,128)(2,1)}, bf16[27,32,512]{2,1,0:T(8,128)(2,1)S(1)}, u32[]{:S(2)}, u32[]{:S(2)}) collective-permute-start(bf16[27,32,512]{2,1,0:T(8,128)(2,1)} %own.1), channel_id=1, source_target_pairs={{0,4},{1,5},{2,6},{3,7},{4,8},{5,9},{6,10},{7,11},{8,12},{9,13},{1... | collective-permute-start | bytes 2654216 | tf_op jit(solution)/shard_map/ppermute | solution.py:51
  3.8 1.0 copy-start.1
  5.6 3.5 %collective-permute-start = (bf16[4,8,16,128]{3,2,1,0:T(8,128)(2,1)S(1)}, bf16[4,8,16,128]{3,2,1,0:T(8,128)(2,1)S(1)}, u32[]{:S(2)}, u32[]{:S(2)}) collective-permute-start(bf16[4,8,16,128]{3,2,1,0:T(8,128)(2,1)S(1)} %get-tuple-element.71), channel_id=1, source_target_pairs={{0,1},{1,0},{2,3},{3,2},{4,5},{5,4},{6,7},{7,6},{8,9},{9,8},{10,11... | collective-permute-start | bytes 393224 | tf_op jit(solution)/shard_map/ppermute | solution.py:43
  5.7 6.4 %collective-permute-start.1 = (bf16[4,8,16,128]{3,2,1,0:T(8,128)(2,1)S(1)}, bf16[4,8,16,128]{3,2,1,0:T(8,128)(2,1)S(1)}, u32[]{:S(2)}, u32[]{:S(2)}) collective-permute-start(bf16[4,8,16,128]{3,2,1,0:T(8,128)(2,1)S(1)} %get-tuple-element.72), channel_id=1, source_target_pairs={{0,2},{1,3},{2,0},{3,1},{4,6},{5,7},{6,4},{7,5},{8,10},{9,11},{10,... | collective-permute-start | bytes 393224 | tf_op jit(solution)/shard_map/ppermute | solution.py:43
  7.7 6.6 %collective-permute-start.2 = (bf16[4,8,16,128]{3,2,1,0:T(8,128)(2,1)S(1)}, bf16[4,8,16,128]{3,2,1,0:T(8,128)(2,1)S(1)}, u32[]{:S(2)}, u32[]{:S(2)}) collective-permute-start(bf16[4,8,16,128]{3,2,1,0:T(8,128)(2,1)S(1)} %get-tuple-element.73), channel_id=1, source_target_pairs={{0,3},{1,2},{2,1},{3,0},{4,7},{5,6},{6,5},{7,4},{8,11},{9,10},{10,... | collective-permute-start | bytes 393224 | tf_op jit(solution)/shard_map/ppermute | solution.py:43
  14.3 23.2 %collective-permute-start.9 = (bf16[4,8,16,512]{3,2,1,0:T(8,128)(2,1)S(1)}, bf16[4,8,16,512]{3,2,1,0:T(8,128)(2,1)S(1)}, u32[]{:S(2)}, u32[]{:S(2)}) collective-permute-start(bf16[4,8,16,512]{3,2,1,0:T(8,128)(2,1)S(1)} %fusion.3.own_act), channel_id=1, source_target_pairs={{0,2},{1,3},{2,0},{3,1},{4,6},{5,7},{6,4},{7,5},{8,10},{9,11},{10,... | collective-permute-start | bytes 1572872 | tf_op jit(solution)/shard_map/ppermute | solution.py:43
  15.9 17.4 %collective-permute-start.3 = (bf16[4,4,16,128]{3,2,1,0:T(8,128)(2,1)S(1)}, bf16[4,4,16,128]{3,2,1,0:T(8,128)(2,1)S(1)}, u32[]{:S(2)}, u32[]{:S(2)}) collective-permute-start(bf16[4,4,16,128]{3,2,1,0:T(8,128)(2,1)S(1)} %get-tuple-element.76), channel_id=1, source_target_pairs={{0,16},{32,48},{64,80},{96,112},{16,0},{48,32},{80,64},{112,96},{1... | collective-permute-start | bytes 196616 | tf_op jit(solution)/shard_map/ppermute | solution.py:62
  19.5 13.8 %collective-permute-start.4 = (bf16[4,4,16,128]{3,2,1,0:T(8,128)(2,1)S(1)}, bf16[4,4,16,128]{3,2,1,0:T(8,128)(2,1)S(1)}, u32[]{:S(2)}, u32[]{:S(2)}) collective-permute-start(bf16[4,4,16,128]{3,2,1,0:T(8,128)(2,1)S(1)} %get-tuple-element.77), channel_id=1, source_target_pairs={{16,32},{48,64},{80,96},{32,16},{64,48},{96,80},{17,33},{49,65},{8... | collective-permute-start | bytes 196616 | tf_op jit(solution)/shard_map/ppermute | solution.py:62
  33.4 4.1 %collective-permute-start.5 = (bf16[10,16,128]{2,1,0:T(8,128)(2,1)S(1)}, bf16[10,16,128]{2,1,0:T(8,128)(2,1)S(1)}, u32[]{:S(2)}, u32[]{:S(2)}) collective-permute-start(bf16[10,16,128]{2,1,0:T(8,128)(2,1)S(1)} %get-tuple-element.78), channel_id=1, source_target_pairs={{0,4},{1,5},{2,6},{3,7},{8,12},{9,13},{10,14},{11,15},{4,0},{5,1},... | collective-permute-start | bytes 122888 | tf_op jit(solution)/shard_map/ppermute | solution.py:68
  34.1 3.4 %collective-permute-start.6 = (bf16[10,16,128]{2,1,0:T(8,128)(2,1)S(1)}, bf16[10,16,128]{2,1,0:T(8,128)(2,1)S(1)}, u32[]{:S(2)}, u32[]{:S(2)}) collective-permute-start(bf16[10,16,128]{2,1,0:T(8,128)(2,1)S(1)} %get-tuple-element.79), channel_id=1, source_target_pairs={{4,8},{5,9},{6,10},{7,11},{8,4},{9,5},{10,6},{11,7},{20,24},{21,25... | collective-permute-start | bytes 122888 | tf_op jit(solution)/shard_map/ppermute | solution.py:68
  37.5 6.9 %collective-permute-start.10 = (bf16[4,8,16,512]{3,2,1,0:T(8,128)(2,1)S(1)}, bf16[4,8,16,512]{3,2,1,0:T(8,128)(2,1)S(1)}, u32[]{:S(2)}, u32[]{:S(2)}) collective-permute-start(bf16[4,8,16,512]{3,2,1,0:T(8,128)(2,1)S(1)} %fusion.3.own_act), channel_id=1, source_target_pairs={{0,1},{1,0},{2,3},{3,2},{4,5},{5,4},{6,7},{7,6},{8,9},{9,8},{10,11... | collective-permute-start | bytes 1572872 | tf_op jit(solution)/shard_map/ppermute | solution.py:43
  37.5 6.8 %collective-permute-start.11 = (bf16[4,8,16,512]{3,2,1,0:T(8,128)(2,1)S(1)}, bf16[4,8,16,512]{3,2,1,0:T(8,128)(2,1)S(1)}, u32[]{:S(2)}, u32[]{:S(2)}) collective-permute-start(bf16[4,8,16,512]{3,2,1,0:T(8,128)(2,1)S(1)} %collective-permute-done.9.far), channel_id=1, source_target_pairs={{0,1},{1,0},{2,3},{3,2},{4,5},{5,4},{6,7},{7,6},{8,9},{9,8},{10,11... | collective-permute-start | bytes 1572872 | tf_op jit(solution)/shard_map/ppermute | solution.py:43
  38.1 20.3 %collective-permute-start.12 = (bf16[13,32,512]{2,1,0:T(8,128)(2,1)S(1)}, bf16[13,32,512]{2,1,0:T(8,128)(2,1)S(1)}, u32[]{:S(2)}, u32[]{:S(2)}) collective-permute-start(bf16[13,32,512]{2,1,0:T(8,128)(2,1)S(1)} %slice.15), channel_id=1, source_target_pairs={{0,4},{1,5},{2,6},{3,7},{4,8},{5,9},{6,10},{7,11},{8,12},{9,13},{1... | collective-permute-start | bytes 1277960 | tf_op jit(solution)/shard_map/ppermute | solution.py:51
  42.3 17.4 %collective-permute-start.13 = (bf16[14,32,512]{2,1,0:T(8,128)(2,1)S(1)}, bf16[14,32,512]{2,1,0:T(8,128)(2,1)S(1)}, u32[]{:S(2)}, u32[]{:S(2)}) collective-permute-start(bf16[14,32,512]{2,1,0:T(8,128)(2,1)S(1)} %slice.16), channel_id=1, source_target_pairs={{0,12},{1,13},{2,14},{3,15},{4,0},{5,1},{6,2},{7,3},{8,4},{9,5},{1... | collective-permute-start | bytes 1376264 | tf_op jit(solution)/shard_map/ppermute | solution.py:51
  44.4 15.3 %copy-start.2 = (bf16[27,32,512]{2,1,0:T(8,128)(2,1)S(1)}, bf16[27,32,512]{2,1,0:T(8,128)(2,1)}, u32[]{:S(2)}) copy-start(bf16[27,32,512]{2,1,0:T(8,128)(2,1)} %own.1) | copy-start | bytes 2654212
  52.1 16.2 %collective-permute-start.14 = (bf16[2,13,16,512]{3,2,1,0:T(8,128)(2,1)S(1)}, bf16[2,13,16,512]{3,2,1,0:T(8,128)(2,1)S(1)}, u32[]{:S(2)}, u32[]{:S(2)}) collective-permute-start(bf16[2,13,16,512]{3,2,1,0:T(8,128)(2,1)S(1)} %get-tuple-element.102), channel_id=1, source_target_pairs={{0,32},{16,48},{32,64},{48,80},{64,96},{80,112},{96,0},{112,16},{1... | collective-permute-start | bytes 1277960 | tf_op jit(solution)/shard_map/ppermute | solution.py:56
  55.0 13.3 %collective-permute-start.15 = (bf16[2,13,16,512]{3,2,1,0:T(8,128)(2,1)S(1)}, bf16[2,13,16,512]{3,2,1,0:T(8,128)(2,1)S(1)}, u32[]{:S(2)}, u32[]{:S(2)}) collective-permute-start(bf16[2,13,16,512]{3,2,1,0:T(8,128)(2,1)S(1)} %get-tuple-element.103), channel_id=1, source_target_pairs={{0,96},{16,112},{32,0},{48,16},{64,32},{80,48},{96,64},{112,80},{1... | collective-permute-start | bytes 1277960 | tf_op jit(solution)/shard_map/ppermute | solution.py:56
  56.4 13.5 %collective-permute-start.16 = (bf16[2,14,16,512]{3,2,1,0:T(8,128)(2,1)S(1)}, bf16[2,14,16,512]{3,2,1,0:T(8,128)(2,1)S(1)}, u32[]{:S(2)}, u32[]{:S(2)}) collective-permute-start(bf16[2,14,16,512]{3,2,1,0:T(8,128)(2,1)S(1)} %get-tuple-element.104), channel_id=1, source_target_pairs={{0,4},{1,5},{2,6},{3,7},{4,8},{5,9},{6,10},{7,11},{8,12},{9,13},{1... | collective-permute-start | bytes 1376264 | tf_op jit(solution)/shard_map/ppermute | solution.py:51
  58.4 12.1 %collective-permute-start.17 = (bf16[2,14,16,512]{3,2,1,0:T(8,128)(2,1)S(1)}, bf16[2,14,16,512]{3,2,1,0:T(8,128)(2,1)S(1)}, u32[]{:S(2)}, u32[]{:S(2)}) collective-permute-start(bf16[2,14,16,512]{3,2,1,0:T(8,128)(2,1)S(1)} %get-tuple-element.105), channel_id=1, source_target_pairs={{0,12},{1,13},{2,14},{3,15},{4,0},{5,1},{6,2},{7,3},{8,4},{9,5},{1... | collective-permute-start | bytes 1376264 | tf_op jit(solution)/shard_map/ppermute | solution.py:51
  70.5 11.8 %collective-permute-start.22 = (f32[2,4,8,16,512]{4,3,2,1,0:T(8,128)S(1)}, f32[2,4,8,16,512]{4,3,2,1,0:T(8,128)S(1)}, u32[]{:S(2)}, u32[]{:S(2)}) collective-permute-start(f32[2,4,8,16,512]{4,3,2,1,0:T(8,128)S(1)} %get-tuple-element.119), channel_id=1, source_target_pairs={{0,1},{1,0},{2,3},{3,2},{4,5},{5,4},{6,7},{7,6},{8,9},{9,8},{10,11... | collective-permute-start | bytes 6291464 | tf_op jit(solution)/shard_map/ppermute | solution.py:43
  70.6 11.6 %collective-permute-start.20 = (bf16[14,16,512]{2,1,0:T(8,128)(2,1)S(1)}, bf16[14,16,512]{2,1,0:T(8,128)(2,1)S(1)}, u32[]{:S(2)}, u32[]{:S(2)}) collective-permute-start(bf16[14,16,512]{2,1,0:T(8,128)(2,1)S(1)} %get-tuple-element.117), channel_id=1, source_target_pairs={{0,4},{1,5},{2,6},{3,7},{4,8},{5,9},{6,10},{7,11},{8,12},{9,13},{1... | collective-permute-start | bytes 688136 | tf_op jit(solution)/shard_map/ppermute | solution.py:51
  72.4 9.8 %collective-permute-start.21 = (bf16[14,16,512]{2,1,0:T(8,128)(2,1)S(1)}, bf16[14,16,512]{2,1,0:T(8,128)(2,1)S(1)}, u32[]{:S(2)}, u32[]{:S(2)}) collective-permute-start(bf16[14,16,512]{2,1,0:T(8,128)(2,1)S(1)} %get-tuple-element.118), channel_id=1, source_target_pairs={{0,12},{1,13},{2,14},{3,15},{4,0},{5,1},{6,2},{7,3},{8,4},{9,5},{1... | collective-permute-start | bytes 688136 | tf_op jit(solution)/shard_map/ppermute | solution.py:51
  73.9 8.3 %collective-permute-start.18 = (bf16[13,16,512]{2,1,0:T(8,128)(2,1)S(1)}, bf16[13,16,512]{2,1,0:T(8,128)(2,1)S(1)}, u32[]{:S(2)}, u32[]{:S(2)}) collective-permute-start(bf16[13,16,512]{2,1,0:T(8,128)(2,1)S(1)} %get-tuple-element.115), channel_id=1, source_target_pairs={{0,32},{16,48},{32,64},{48,80},{64,96},{80,112},{96,0},{112,16},{1... | collective-permute-start | bytes 638984 | tf_op jit(solution)/shard_map/ppermute | solution.py:56
  74.3 7.9 %collective-permute-start.19 = (bf16[13,16,512]{2,1,0:T(8,128)(2,1)S(1)}, bf16[13,16,512]{2,1,0:T(8,128)(2,1)S(1)}, u32[]{:S(2)}, u32[]{:S(2)}) collective-permute-start(bf16[13,16,512]{2,1,0:T(8,128)(2,1)S(1)} %get-tuple-element.116), channel_id=1, source_target_pairs={{0,96},{16,112},{32,0},{48,16},{64,32},{80,48},{96,64},{112,80},{1... | collective-permute-start | bytes 638984 | tf_op jit(solution)/shard_map/ppermute | solution.py:56
  82.5 5.6 %collective-permute-start.25 = (bf16[13,8,512]{2,1,0:T(8,128)(2,1)S(1)}, bf16[13,8,512]{2,1,0:T(8,128)(2,1)S(1)}, u32[]{:S(2)}, u32[]{:S(2)}) collective-permute-start(bf16[13,8,512]{2,1,0:T(8,128)(2,1)S(1)} %get-tuple-element.130), channel_id=1, source_target_pairs={{0,12},{1,13},{2,14},{3,15},{4,0},{5,1},{6,2},{7,3},{8,4},{9,5},{1... | collective-permute-start | bytes 319496 | tf_op jit(solution)/shard_map/ppermute | solution.py:51
  83.8 6.3 %collective-permute-start.24 = (bf16[13,8,512]{2,1,0:T(8,128)(2,1)S(1)}, bf16[13,8,512]{2,1,0:T(8,128)(2,1)S(1)}, u32[]{:S(2)}, u32[]{:S(2)}) collective-permute-start(bf16[13,8,512]{2,1,0:T(8,128)(2,1)S(1)} %get-tuple-element.129), channel_id=1, source_target_pairs={{0,8},{1,9},{2,10},{3,11},{4,12},{5,13},{6,14},{7,15},{8,0},{9,1},... | collective-permute-start | bytes 319496 | tf_op jit(solution)/shard_map/ppermute | solution.py:51
  85.2 6.1 %collective-permute-start.23 = (bf16[13,8,512]{2,1,0:T(8,128)(2,1)S(1)}, bf16[13,8,512]{2,1,0:T(8,128)(2,1)S(1)}, u32[]{:S(2)}, u32[]{:S(2)}) collective-permute-start(bf16[13,8,512]{2,1,0:T(8,128)(2,1)S(1)} %get-tuple-element.128), channel_id=1, source_target_pairs={{0,4},{1,5},{2,6},{3,7},{4,8},{5,9},{6,10},{7,11},{8,12},{9,13},{1... | collective-permute-start | bytes 319496 | tf_op jit(solution)/shard_map/ppermute | solution.py:51
  85.2 6.5 %collective-permute-start.28 = (bf16[14,8,512]{2,1,0:T(8,128)(2,1)S(1)}, bf16[14,8,512]{2,1,0:T(8,128)(2,1)S(1)}, u32[]{:S(2)}, u32[]{:S(2)}) collective-permute-start(bf16[14,8,512]{2,1,0:T(8,128)(2,1)S(1)} %get-tuple-element.134), channel_id=1, source_target_pairs={{0,96},{16,112},{32,0},{48,16},{64,32},{80,48},{96,64},{112,80},{1... | collective-permute-start | bytes 344072 | tf_op jit(solution)/shard_map/ppermute | solution.py:56
  88.1 6.4 %collective-permute-start.27 = (bf16[14,8,512]{2,1,0:T(8,128)(2,1)S(1)}, bf16[14,8,512]{2,1,0:T(8,128)(2,1)S(1)}, u32[]{:S(2)}, u32[]{:S(2)}) collective-permute-start(bf16[14,8,512]{2,1,0:T(8,128)(2,1)S(1)} %get-tuple-element.133), channel_id=1, source_target_pairs={{0,64},{16,80},{32,96},{48,112},{64,0},{80,16},{96,32},{112,48},{1... | collective-permute-start | bytes 344072 | tf_op jit(solution)/shard_map/ppermute | solution.py:56
  88.1 7.2 %collective-permute-start.26 = (bf16[14,8,512]{2,1,0:T(8,128)(2,1)S(1)}, bf16[14,8,512]{2,1,0:T(8,128)(2,1)S(1)}, u32[]{:S(2)}, u32[]{:S(2)}) collective-permute-start(bf16[14,8,512]{2,1,0:T(8,128)(2,1)S(1)} %get-tuple-element.132), channel_id=1, source_target_pairs={{0,32},{16,48},{32,64},{48,80},{64,96},{80,112},{96,0},{112,16},{1... | collective-permute-start | bytes 344072 | tf_op jit(solution)/shard_map/ppermute | solution.py:56
  95.5 9.8 %collective-permute-start.29 = (bf16[27,8,512]{2,1,0:T(8,128)(2,1)S(1)}, bf16[27,8,512]{2,1,0:T(8,128)(2,1)S(1)}, u32[]{:S(2)}, u32[]{:S(2)}) collective-permute-start(bf16[27,8,512]{2,1,0:T(8,128)(2,1)S(1)} %pad_maximum_fusion), channel_id=1, source_target_pairs={{0,16},{16,0},{32,48},{48,32},{64,80},{80,64},{96,112},{112,96},{1... | collective-permute-start | bytes 663560 | tf_op jit(solution)/shard_map/ppermute | solution.py:487
  105.3 19.3 %collective-permute-start.30 = (f32[4,8,16,512]{3,2,1,0:T(8,128)S(1)}, f32[4,8,16,512]{3,2,1,0:T(8,128)S(1)}, u32[]{:S(2)}, u32[]{:S(2)}) collective-permute-start(f32[4,8,16,512]{3,2,1,0:T(8,128)S(1)} %bitcast_add_fusion), channel_id=1, source_target_pairs={{0,2},{1,3},{2,0},{3,1},{4,6},{5,7},{6,4},{7,5},{8,10},{9,11},{10,... | collective-permute-start | bytes 3145736 | tf_op jit(solution)/shard_map/ppermute | solution.py:43
  105.4 19.2 %copy-start = (bf16[4,8,16,512]{3,2,1,0:T(8,128)(2,1)S(1)}, bf16[4,8,16,512]{3,2,1,0:T(8,128)(2,1)}, u32[]{:S(2)}) copy-start(bf16[4,8,16,512]{3,2,1,0:T(8,128)(2,1)} %pre.1) | copy-start | bytes 1572868
  105.4 8.4 %collective-permute-start.34 = (f32[14,8,512]{2,1,0:T(8,128)S(1)}, f32[14,8,512]{2,1,0:T(8,128)S(1)}, u32[]{:S(2)}, u32[]{:S(2)}) collective-permute-start(f32[14,8,512]{2,1,0:T(8,128)S(1)} %convert_add_fusion.refs_1_), channel_id=1, source_target_pairs={{0,96},{16,112},{32,0},{48,16},{64,32},{80,48},{96,64},{112,80},{1... | collective-permute-start | bytes 688136 | tf_op jit(solution)/shard_map/ppermute | solution.py:56
  106.5 9.6 %collective-permute-start.31 = (f32[13,8,512]{2,1,0:T(8,128)S(1)}, f32[13,8,512]{2,1,0:T(8,128)S(1)}, u32[]{:S(2)}, u32[]{:S(2)}) collective-permute-start(f32[13,8,512]{2,1,0:T(8,128)S(1)} %convert_add_fusion.2.refs_0_), channel_id=1, source_target_pairs={{0,32},{16,48},{32,64},{48,80},{64,96},{80,112},{96,0},{112,16},{1... | collective-permute-start | bytes 638984 | tf_op jit(solution)/shard_map/ppermute | solution.py:56
  107.6 14.4 %collective-permute-start.32 = (f32[14,8,512]{2,1,0:T(8,128)S(1)}, f32[14,8,512]{2,1,0:T(8,128)S(1)}, u32[]{:S(2)}, u32[]{:S(2)}) collective-permute-start(f32[14,8,512]{2,1,0:T(8,128)S(1)} %convert_add_fusion.refs_1_), channel_id=1, source_target_pairs={{0,32},{16,48},{32,64},{48,80},{64,96},{80,112},{96,0},{112,16},{1... | collective-permute-start | bytes 688136 | tf_op jit(solution)/shard_map/ppermute | solution.py:56
  113.8 9.5 %collective-permute-start.36 = (f32[14,8,512]{2,1,0:T(8,128)S(1)}, f32[14,8,512]{2,1,0:T(8,128)S(1)}, u32[]{:S(2)}, u32[]{:S(2)}) collective-permute-start(f32[14,8,512]{2,1,0:T(8,128)S(1)} %collective-permute-done.34.refs_5_), channel_id=1, source_target_pairs={{0,96},{16,112},{32,0},{48,16},{64,32},{80,48},{96,64},{112,80},{1... | collective-permute-start | bytes 688136 | tf_op jit(solution)/shard_map/ppermute | solution.py:56
  116.1 5.9 %collective-permute-start.33 = (f32[13,8,512]{2,1,0:T(8,128)S(1)}, f32[13,8,512]{2,1,0:T(8,128)S(1)}, u32[]{:S(2)}, u32[]{:S(2)}) collective-permute-start(f32[13,8,512]{2,1,0:T(8,128)S(1)} %convert_add_fusion.2.refs_0_), channel_id=1, source_target_pairs={{0,96},{16,112},{32,0},{48,16},{64,32},{80,48},{96,64},{112,80},{1... | collective-permute-start | bytes 638984 | tf_op jit(solution)/shard_map/ppermute | solution.py:56
  116.2 7.1 %collective-permute-start.35 = (f32[13,8,512]{2,1,0:T(8,128)S(1)}, f32[13,8,512]{2,1,0:T(8,128)S(1)}, u32[]{:S(2)}, u32[]{:S(2)}) collective-permute-start(f32[13,8,512]{2,1,0:T(8,128)S(1)} %collective-permute-done.31.refs_2_), channel_id=1, source_target_pairs={{0,32},{16,48},{32,64},{48,80},{64,96},{80,112},{96,0},{112,16},{1... | collective-permute-start | bytes 638984 | tf_op jit(solution)/shard_map/ppermute | solution.py:56

commit v10 on v9

--- a/solution.py
+++ b/solution.py
@@ -219,13 +219,21 @@
     return copies
 
 
-def weight_kernel(norm, own_act, near, far, across, cot, *refs):
+def weight_kernel(norm, own_act, near, far_low, across_low, far_high, across_high, cot, *refs):
     groups, held, sem = (refs[:5], refs[5:10]), *refs[10:]
     j = quad_place()
     rows, width, depth, chan = own_act.shape
-    pairs = []
-    for k, piece in enumerate((own_act, near, far, across)):
-        pairs.append((piece, held.at[pl.ds((j ^ k) * rows, rows)]))
+    pairs = [
+        (piece, held.at[pl.ds((j ^ k) * rows + first, piece.shape[0])])
+        for piece, k, first in (
+            (own_act, 0, 0),
+            (near, 1, 0),
+            (far_low, 2, 0),
+            (across_low, 3, 0),
+            (far_high, 2, far_low.shape[0]),
+            (across_high, 3, far_low.shape[0]),
+        )
+    ]
     for c in run_copies(pairs, sem):
         c.wait()
     row = width * depth
@@ -271,11 +279,11 @@
     return pl.pallas_call(
         functools.partial(weight_kernel, norm),
         out_shape=shapes,
-        in_specs=[ANY] * 4 + [VMEM],
+        in_specs=[ANY] * 6 + [VMEM],
         out_specs=[VMEM] * 10,
         scratch_shapes=[
             pltpu.VMEM((QUAD * rows, width, depth, chan), BF16),
-            pltpu.SemaphoreType.DMA((4,)),
+            pltpu.SemaphoreType.DMA((6,)),
         ],
         compiler_params=params(),
         cost_estimate=pl.CostEstimate(
@@ -442,17 +450,20 @@
     quarters = pick_channels(cot)
     quarters = [quarters[0]] + [swap(quarters[k], k) for k in (1, 2, 3)]
     act = jax.nn.silu(pre_act.astype(F32)).astype(BF16)
+    half = rows // 2
     near = swap(act, 1)
+    far_low = swap(act[:half], 2)
     above = along_y(weight, -1, True)
     below = along_y(weight, 1, True)
+    quarters, far_low = barrier((quarters, far_low))
     even, odd = sides(quarters)
-    even, odd, act = barrier((even, odd, act))
     even, odd = swap_x(even, 0), swap_x(odd, 1)
-    far = swap(act, 2)
+    even, odd, above, below, act_high = barrier((even, odd, above, below, act[half:]))
+    far_high = swap(act_high, 2)
     first, second = edge_rows(quarters, even, odd)
     first, second = swap_y(first, 0), swap_y(second, 1)
-    first, second, above, below, far = barrier((first, second, above, below, far))
-    acts = [act, near, far, swap(far, 1)]
+    first, second, above, below, far_high = barrier((first, second, above, below, far_high))
+    acts = [act, near, far_low, swap(far_low, 1), far_high, swap(far_high, 1)]
     taps = XTAPS
     parts = [weight, above, along_y(below[:taps], 1, True), along_y(above[taps:], -1, True), below]
     held, turned = turn(quarters, even, odd, first, second)

time: 127 us -> 128 us (level)
  starting transfers between devices: 44.6 us -> 50.8 us
  waiting for transfers between devices: 55.2 us -> 50.5 us
    ppermute x2, waiting for transfers between devices: 13.1 us -> 2.12 us  [swap_x(): return lax.ppermute(block, 'gx', pairs + [(t, s) for s, t in pairs])]
    ppermute x8 -> x10, waiting for transfers between devices: 5.18 us -> 14.6 us  [swap(): return lax.ppermute(block, 'gy', [(g, g ^ k) for g in range(count)])]
    ppermute x8 -> x10, starting transfers between devices: 4.38 us -> 7.33 us  [swap(): return lax.ppermute(block, 'gy', [(g, g ^ k) for g in range(count)])]
    ppermute x13, starting transfers between devices: 18 us -> 20.7 us  [along_x(): lax.ppermute(block, 'gx', [(g, (g + 2 * step) % count) for g in range(cou...]
    ppermute x1, waiting for transfers between devices: 9.46 us -> 7.63 us  [body(): other = lax.ppermute(mine, 'gx', [(g, g ^ 1) for g in range(count)])]
  transfers between devices with their start and end apart: 37 -> 39, of which waited for: 16 -> 16; matrix products, arithmetic and copies ran while one was open for 1% -> 1% of each run, Pallas kernels for 16% -> 16%
where the time goes in v10:
time: 128 us; the launch traced here: 127 us
  starting transfers between devices  50.8 us (40%)
  waiting for transfers between devices  50.5 us (39%)
  Pallas kernels  22.1 us (17%)
  other arithmetic  1.86 us (1%)
    ppermute x13, starting transfers between devices, along_x(): lax.ppermute(block, 'gx', [(g, (g + 2 * step) % count) for g in range(cou...  20.7 us
    ppermute x13, waiting for transfers between devices, along_x(): lax.ppermute(block, 'gx', [(g, (g + 2 * step) % count) for g in range(cou...  19.5 us
    ppermute x11, starting transfers between devices, along_y(): lax.ppermute(block, 'gy', [(s, t) for s, t in pairs if 0 <= t < count])  16 us
    ppermute x10, waiting for transfers between devices, swap(): return lax.ppermute(block, 'gy', [(g, g ^ k) for g in range(count)])  14.6 us
    pallas_call x1, Pallas kernels, input_terms(): pl.pallas_call(input_kernel, out_shape=[jax.ShapeDtypeStruct((2,) + block...  8.7 us
    pallas_call x1, Pallas kernels, weight_terms(): pl.pallas_call(functools.partial(weight_kernel, norm), out_shape=shapes,...  7.68 us
    ppermute x1, waiting for transfers between devices, body(): other = lax.ppermute(mine, 'gx', [(g, g ^ 1) for g in range(count)])  7.63 us
    ppermute x10, starting transfers between devices, swap(): return lax.ppermute(block, 'gy', [(g, g ^ k) for g in range(count)])  7.33 us
  transfers between devices with their start and end apart: 39, of which 16 were waited for; matrix products, arithmetic and copies ran while one was open for 1% of the time, Pallas kernels for 16%

profile of v10, /device:TPU:0, one launch (start us, length us, event | category | flops | bytes accessed | tf_op | source)
XLA Modules:
  0.0 127.3 jit_solution(11906173944363193959)
XLA Ops:
  0.6 3.2 %collective-permute-start.6 = (bf16[27,32,512]{2,1,0:T(8,128)(2,1)}, bf16[27,32,512]{2,1,0:T(8,128)(2,1)S(1)}, u32[]{:S(2)}, u32[]{:S(2)}) collective-permute-start(bf16[27,32,512]{2,1,0:T(8,128)(2,1)} %own.1), channel_id=1, source_target_pairs={{0,12},{1,13},{2,14},{3,15},{4,0},{5,1},{6,2},{7,3},{8,4},{9,5},{1... | collective-permute-start | bytes 2654216 | tf_op jit(solution)/shard_map/ppermute | solution.py:51
  3.8 1.0 copy-done.1
  4.8 0.7 shard_map.50
  5.7 1.4 %fusion.3.own_act = bf16[4,8,16,512]{3,2,1,0:T(8,128)(2,1)S(1)} fusion(bf16[4,8,16,512]{3,2,1,0:T(8,128)(2,1)} %pre.1), kind=kLoop, calls=%fused_computation.5 | loop fusion | flops 1572864 | bytes 1048576 | tf_op jit(solution)/shard_map/convert_element_type | solution.py:452
  7.1 2.0 %collective-permute-start.3 = (bf16[2,8,16,512]{3,2,1,0:T(8,128)(2,1)S(1)}, bf16[2,8,16,512]{3,2,1,0:T(8,128)(2,1)S(1)}, u32[]{:S(2)}, u32[]{:S(2)}) collective-permute-start(bf16[2,8,16,512]{3,2,1,0:T(8,128)(2,1)S(1)} %get-tuple-element.153), channel_id=1, source_target_pairs={{0,2},{1,3},{2,0},{3,1},{4,6},{5,7},{6,4},{7,5},{8,10},{9,11},{10,... | collective-permute-start | bytes 786440 | tf_op jit(solution)/shard_map/ppermute | solution.py:43
  9.2 1.4 %collective-permute-start.2 = (bf16[4,8,16,128]{3,2,1,0:T(8,128)(2,1)S(1)}, bf16[4,8,16,128]{3,2,1,0:T(8,128)(2,1)S(1)}, u32[]{:S(2)}, u32[]{:S(2)}) collective-permute-start(bf16[4,8,16,128]{3,2,1,0:T(8,128)(2,1)S(1)} %get-tuple-element.80), channel_id=1, source_target_pairs={{0,3},{1,2},{2,1},{3,0},{4,7},{5,6},{6,5},{7,4},{8,11},{9,10},{10,... | collective-permute-start | bytes 393224 | tf_op jit(solution)/shard_map/ppermute | solution.py:43
  10.6 8.5 %collective-permute-done.1.p2 = bf16[4,8,16,128]{3,2,1,0:T(8,128)(2,1)S(1)} collective-permute-done((bf16[4,8,16,128]{3,2,1,0:T(8,128)(2,1)S(1)}, bf16[4,8,16,128]{3,2,1,0:T(8,128)(2,1)S(1)}, u32[]{:S(2)}, u32[]{:S(2)}) %collective-permute-start.1) | collective-permute-done | bytes 131104 | tf_op jit(solution)/shard_map/ppermute | solution.py:43
  19.1 2.2 %collective-permute-done.2.p3 = bf16[4,8,16,128]{3,2,1,0:T(8,128)(2,1)S(1)} collective-permute-done((bf16[4,8,16,128]{3,2,1,0:T(8,128)(2,1)S(1)}, bf16[4,8,16,128]{3,2,1,0:T(8,128)(2,1)S(1)}, u32[]{:S(2)}, u32[]{:S(2)}) %collective-permute-start.2) | collective-permute-done | bytes 131104 | tf_op jit(solution)/shard_map/ppermute | solution.py:43
  21.4 3.7 %collective-permute-start.4 = (bf16[4,4,16,128]{3,2,1,0:T(8,128)(2,1)S(1)}, bf16[4,4,16,128]{3,2,1,0:T(8,128)(2,1)S(1)}, u32[]{:S(2)}, u32[]{:S(2)}) collective-permute-start(bf16[4,4,16,128]{3,2,1,0:T(8,128)(2,1)S(1)} %get-tuple-element.85), channel_id=1, source_target_pairs={{0,16},{32,48},{64,80},{96,112},{16,0},{48,32},{80,64},{112,96},{1... | collective-permute-start | bytes 196616 | tf_op jit(solution)/shard_map/ppermute | solution.py:62
  25.1 0.7 collective-permute-start.5
  25.7 2.1 %collective-permute-done.4.even = bf16[4,4,16,128]{3,2,1,0:T(8,128)(2,1)S(1)} collective-permute-done((bf16[4,4,16,128]{3,2,1,0:T(8,128)(2,1)S(1)}, bf16[4,4,16,128]{3,2,1,0:T(8,128)(2,1)S(1)}, u32[]{:S(2)}, u32[]{:S(2)}) %collective-permute-start.4) | collective-permute-done | bytes 65568 | tf_op jit(solution)/shard_map/ppermute | solution.py:62
  27.9 1.4 %collective-permute-start.10 = (bf16[2,8,16,512]{3,2,1,0:T(8,128)(2,1)S(1)}, bf16[2,8,16,512]{3,2,1,0:T(8,128)(2,1)S(1)}, u32[]{:S(2)}, u32[]{:S(2)}) collective-permute-start(bf16[2,8,16,512]{3,2,1,0:T(8,128)(2,1)S(1)} %get-tuple-element.93), channel_id=1, source_target_pairs={{0,2},{1,3},{2,0},{3,1},{4,6},{5,7},{6,4},{7,5},{8,10},{9,11},{10,... | collective-permute-start | bytes 786440 | tf_op jit(solution)/shard_map/ppermute | solution.py:43
  29.3 0.7 collective-permute-start.8
  30.9 2.5 %collective-permute-done.8.first = bf16[10,16,128]{2,1,0:T(8,128)(2,1)S(1)} collective-permute-done((bf16[10,16,128]{2,1,0:T(8,128)(2,1)S(1)}, bf16[10,16,128]{2,1,0:T(8,128)(2,1)S(1)}, u32[]{:S(2)}, u32[]{:S(2)}) %collective-permute-start.8) | collective-permute-done | bytes 40992 | tf_op jit(solution)/shard_map/ppermute | solution.py:68
  33.4 3.8 %collective-permute-done.10.far_high = bf16[2,8,16,512]{3,2,1,0:T(8,128)(2,1)S(1)} collective-permute-done((bf16[2,8,16,512]{3,2,1,0:T(8,128)(2,1)S(1)}, bf16[2,8,16,512]{3,2,1,0:T(8,128)(2,1)S(1)}, u32[]{:S(2)}, u32[]{:S(2)}) %collective-permute-start.10) | collective-permute-done | bytes 262176 | tf_op jit(solution)/shard_map/ppermute | solution.py:43
  37.3 0.7 collective-permute-start.14
  38.1 2.7 %collective-permute-start.15 = (bf16[14,32,512]{2,1,0:T(8,128)(2,1)S(1)}, bf16[14,32,512]{2,1,0:T(8,128)(2,1)S(1)}, u32[]{:S(2)}, u32[]{:S(2)}) collective-permute-start(bf16[14,32,512]{2,1,0:T(8,128)(2,1)S(1)} %slice.24), channel_id=1, source_target_pairs={{0,12},{1,13},{2,14},{3,15},{4,0},{5,1},{6,2},{7,3},{8,4},{9,5},{1... | collective-permute-start | bytes 1376264 | tf_op jit(solution)/shard_map/ppermute | solution.py:51
  40.7 2.0 %shard_map.53 = (bf16[18,10,16,128]{3,2,1,0:T(8,128)(2,1)S(1)}, bf16[1152,2304]{1,0:T(8,128)(2,1)S(1)}) custom-call(bf16[4,8,16,128]{3,2,1,0:T(8,128)(2,1)S(1)} %get-tuple-element.81.p0, bf16[4,8,16,128]{3,2,1,0:T(8,128)(2,1)S(1)} %collective-permute-done.p1, bf16[4,8,16,128]{3,2,1,0:T(8,128)(2,1)S(1)} %collective-permute-done.1.p2, ...), custom_call_target="tpu_custom_call" | custom-call | flops 1000 | bytes 1000 | tf_op jit(solution)/shard_map/pallas_call | solution.py:202
  42.8 7.7 %shard_map.54 = (bf16[2,13,16,512]{3,2,1,0:T(8,128)(2,1)S(1)}, bf16[2,13,16,512]{3,2,1,0:T(8,128)(2,1)S(1)}, f32[13,16,512]{2,1,0:T(8,128)S(1)}, f32[13,16,512]{...) custom-call(bf16[4,8,16,512]{3,2,1,0:T(8,128)(2,1)S(1)} %fusion.3.ow, ...), custom_call_target="tpu_custom_call" | custom-call | flops 7247757312 | bytes 10000000 | tf_op jit(solution)/shard_map/pallas_call | solution.py:279
  50.5 5.4 %collective-permute-start.16 = (bf16[2,13,16,512]{3,2,1,0:T(8,128)(2,1)S(1)}, bf16[2,13,16,512]{3,2,1,0:T(8,128)(2,1)S(1)}, u32[]{:S(2)}, u32[]{:S(2)}) collective-permute-start(bf16[2,13,16,512]{3,2,1,0:T(8,128)(2,1)S(1)} %get-tuple-element.116), channel_id=1, source_target_pairs={{0,32},{16,48},{32,64},{48,80},{64,96},{80,112},{96,0},{112,16},{1... | collective-permute-start | bytes 1277960 | tf_op jit(solution)/shard_map/ppermute | solution.py:56
  55.9 1.3 %collective-permute-start.17 = (bf16[2,13,16,512]{3,2,1,0:T(8,128)(2,1)S(1)}, bf16[2,13,16,512]{3,2,1,0:T(8,128)(2,1)S(1)}, u32[]{:S(2)}, u32[]{:S(2)}) collective-permute-start(bf16[2,13,16,512]{3,2,1,0:T(8,128)(2,1)S(1)} %get-tuple-element.117), channel_id=1, source_target_pairs={{0,96},{16,112},{32,0},{48,16},{64,32},{80,48},{96,64},{112,80},{1... | collective-permute-start | bytes 1277960 | tf_op jit(solution)/shard_map/ppermute | solution.py:56
  57.2 1.3 collective-permute-start.18
  58.5 2.0 %collective-permute-start.19 = (bf16[2,14,16,512]{3,2,1,0:T(8,128)(2,1)S(1)}, bf16[2,14,16,512]{3,2,1,0:T(8,128)(2,1)S(1)}, u32[]{:S(2)}, u32[]{:S(2)}) collective-permute-start(bf16[2,14,16,512]{3,2,1,0:T(8,128)(2,1)S(1)} %get-tuple-element.119), channel_id=1, source_target_pairs={{0,12},{1,13},{2,14},{3,15},{4,0},{5,1},{6,2},{7,3},{8,4},{9,5},{1... | collective-permute-start | bytes 1376264 | tf_op jit(solution)/shard_map/ppermute | solution.py:51
  60.5 8.7 %shard_map.55 = (f32[2,4,8,16,512]{4,3,2,1,0:T(8,128)S(1)}, f32[4,8,16,512]{3,2,1,0:T(8,128)S(1)}, f32[4,8,16,512]{3,2,1,0:T(8,128)S(1)}) custom-call(bf16[18,10,16,128]{3,2,1,0:T(8,128)(2,1)S(1)} %get-tuple-element.110.held, bf16[27,32,512]{2,1,0:T(8,128)(2,1)S(1)} %copy-done.2, bf16[27,32,512]{2,1,0:T(8,128)(2,1)S(1)} %collective-permute-done.6.above, ...), custom_call_target="tpu_custom_call" | custom-call | flops 10192158720 | bytes 10000000 | tf_op jit(solution)/shard_map/pallas_call | solution.py:341
  69.2 1.6 %collective-permute-done.18.refs_4_.refs_6_ = bf16[2,14,16,512]{3,2,1,0:T(8,128)(2,1)S(1)} collective-permute-done((bf16[2,14,16,512]{3,2,1,0:T(8,128)(2,1)S(1)}, bf16[2,14,16,512]{3,2,1,0:T(8,128)(2,1)S(1)}, u32[]{:S(2)}, u32[]{:S(2)}) %collective-permute-start.18) | collective-permute-done | bytes 458784 | tf_op jit(solution)/shard_map/ppermute | solution.py:51
  71.0 1.6 %collective-permute-start.22 = (bf16[14,16,512]{2,1,0:T(8,128)(2,1)S(1)}, bf16[14,16,512]{2,1,0:T(8,128)(2,1)S(1)}, u32[]{:S(2)}, u32[]{:S(2)}) collective-permute-start(bf16[14,16,512]{2,1,0:T(8,128)(2,1)S(1)} %get-tuple-element.131), channel_id=1, source_target_pairs={{0,4},{1,5},{2,6},{3,7},{4,8},{5,9},{6,10},{7,11},{8,12},{9,13},{1... | collective-permute-start | bytes 688136 | tf_op jit(solution)/shard_map/ppermute | solution.py:51
  72.5 1.7 %collective-permute-start.23 = (bf16[14,16,512]{2,1,0:T(8,128)(2,1)S(1)}, bf16[14,16,512]{2,1,0:T(8,128)(2,1)S(1)}, u32[]{:S(2)}, u32[]{:S(2)}) collective-permute-start(bf16[14,16,512]{2,1,0:T(8,128)(2,1)S(1)} %get-tuple-element.132), channel_id=1, source_target_pairs={{0,12},{1,13},{2,14},{3,15},{4,0},{5,1},{6,2},{7,3},{8,4},{9,5},{1... | collective-permute-start | bytes 688136 | tf_op jit(solution)/shard_map/ppermute | solution.py:51
  74.7 2.9 %collective-permute-start.21 = (bf16[13,16,512]{2,1,0:T(8,128)(2,1)S(1)}, bf16[13,16,512]{2,1,0:T(8,128)(2,1)S(1)}, u32[]{:S(2)}, u32[]{:S(2)}) collective-permute-start(bf16[13,16,512]{2,1,0:T(8,128)(2,1)S(1)} %get-tuple-element.130), channel_id=1, source_target_pairs={{0,96},{16,112},{32,0},{48,16},{64,32},{80,48},{96,64},{112,80},{1... | collective-permute-start | bytes 638984 | tf_op jit(solution)/shard_map/ppermute | solution.py:56
  77.5 5.2 %collective-permute-done.20.refs_3_ = bf16[13,16,512]{2,1,0:T(8,128)(2,1)S(1)} collective-permute-done((bf16[13,16,512]{2,1,0:T(8,128)(2,1)S(1)}, bf16[13,16,512]{2,1,0:T(8,128)(2,1)S(1)}, u32[]{:S(2)}, u32[]{:S(2)}) %collective-permute-start.20) | collective-permute-done | bytes 213024 | tf_op jit(solution)/shard_map/ppermute | solution.py:56
  83.0 1.7 %collective-permute-start.27 = (bf16[13,8,512]{2,1,0:T(8,128)(2,1)S(1)}, bf16[13,8,512]{2,1,0:T(8,128)(2,1)S(1)}, u32[]{:S(2)}, u32[]{:S(2)}) collective-permute-start(bf16[13,8,512]{2,1,0:T(8,128)(2,1)S(1)} %get-tuple-element.144), channel_id=1, source_target_pairs={{0,12},{1,13},{2,14},{3,15},{4,0},{5,1},{6,2},{7,3},{8,4},{9,5},{1... | collective-permute-start | bytes 319496 | tf_op jit(solution)/shard_map/ppermute | solution.py:51
  85.8 2.9 %collective-permute-start.30 = (bf16[14,8,512]{2,1,0:T(8,128)(2,1)S(1)}, bf16[14,8,512]{2,1,0:T(8,128)(2,1)S(1)}, u32[]{:S(2)}, u32[]{:S(2)}) collective-permute-start(bf16[14,8,512]{2,1,0:T(8,128)(2,1)S(1)} %get-tuple-element.148), channel_id=1, source_target_pairs={{0,96},{16,112},{32,0},{48,16},{64,32},{80,48},{96,64},{112,80},{1... | collective-permute-start | bytes 344072 | tf_op jit(solution)/shard_map/ppermute | solution.py:56
  88.8 0.9 collective-permute-start.28
  89.6 1.4 %collective-permute-done.26 = bf16[13,8,512]{2,1,0:T(8,128)(2,1)S(1)} collective-permute-done((bf16[13,8,512]{2,1,0:T(8,128)(2,1)S(1)}, bf16[13,8,512]{2,1,0:T(8,128)(2,1)S(1)}, u32[]{:S(2)}, u32[]{:S(2)}) %collective-permute-start.26) | collective-permute-done | bytes 106528 | tf_op jit(solution)/shard_map/ppermute | solution.py:51
  91.1 1.1 collective-permute-done.25
  92.4 2.8 %collective-permute-done.29 = bf16[14,8,512]{2,1,0:T(8,128)(2,1)S(1)} collective-permute-done((bf16[14,8,512]{2,1,0:T(8,128)(2,1)S(1)}, bf16[14,8,512]{2,1,0:T(8,128)(2,1)S(1)}, u32[]{:S(2)}, u32[]{:S(2)}) %collective-permute-start.29) | collective-permute-done | bytes 114720 | tf_op jit(solution)/shard_map/ppermute | solution.py:56
  95.2 0.8 collective-permute-done.28
  96.1 1.1 collective-permute-start.31
  97.5 7.6 %collective-permute-done.31 = bf16[27,8,512]{2,1,0:T(8,128)(2,1)S(1)} collective-permute-done((bf16[27,8,512]{2,1,0:T(8,128)(2,1)S(1)}, bf16[27,8,512]{2,1,0:T(8,128)(2,1)S(1)}, u32[]{:S(2)}, u32[]{:S(2)}) %collective-permute-start.31) | collective-permute-done | bytes 221216 | tf_op jit(solution)/shard_map/ppermute | solution.py:498
  105.1 2.0 %collective-permute-start.32 = (f32[4,8,16,512]{3,2,1,0:T(8,128)S(1)}, f32[4,8,16,512]{3,2,1,0:T(8,128)S(1)}, u32[]{:S(2)}, u32[]{:S(2)}) collective-permute-start(f32[4,8,16,512]{3,2,1,0:T(8,128)S(1)} %bitcast_add_fusion), channel_id=1, source_target_pairs={{0,2},{1,3},{2,0},{3,1},{4,6},{5,7},{6,4},{7,5},{8,10},{9,11},{10,... | collective-permute-start | bytes 3145736 | tf_op jit(solution)/shard_map/ppermute | solution.py:43
  107.2 0.7 collective-permute-start.36
  108.0 1.5 %collective-permute-start.33 = (f32[13,8,512]{2,1,0:T(8,128)S(1)}, f32[13,8,512]{2,1,0:T(8,128)S(1)}, u32[]{:S(2)}, u32[]{:S(2)}) collective-permute-start(f32[13,8,512]{2,1,0:T(8,128)S(1)} %convert_add_fusion.2.refs_0_), channel_id=1, source_target_pairs={{0,32},{16,48},{32,64},{48,80},{64,96},{80,112},{96,0},{112,16},{1... | collective-permute-start | bytes 638984 | tf_op jit(solution)/shard_map/ppermute | solution.py:56
  109.5 5.5 %collective-permute-done.36.refs_5_ = f32[14,8,512]{2,1,0:T(8,128)S(1)} collective-permute-done((f32[14,8,512]{2,1,0:T(8,128)S(1)}, f32[14,8,512]{2,1,0:T(8,128)S(1)}, u32[]{:S(2)}, u32[]{:S(2)}) %collective-permute-start.36) | collective-permute-done | bytes 229408 | tf_op jit(solution)/shard_map/ppermute | solution.py:56
  115.0 2.6 %collective-permute-start.38 = (f32[14,8,512]{2,1,0:T(8,128)S(1)}, f32[14,8,512]{2,1,0:T(8,128)S(1)}, u32[]{:S(2)}, u32[]{:S(2)}) collective-permute-start(f32[14,8,512]{2,1,0:T(8,128)S(1)} %collective-permute-done.36.refs_5_), channel_id=1, source_target_pairs={{0,96},{16,112},{32,0},{48,16},{64,32},{80,48},{96,64},{112,80},{1... | collective-permute-start | bytes 688136 | tf_op jit(solution)/shard_map/ppermute | solution.py:56
  117.7 2.0 %collective-permute-start.37 = (f32[13,8,512]{2,1,0:T(8,128)S(1)}, f32[13,8,512]{2,1,0:T(8,128)S(1)}, u32[]{:S(2)}, u32[]{:S(2)}) collective-permute-start(f32[13,8,512]{2,1,0:T(8,128)S(1)} %collective-permute-done.33.refs_2_), channel_id=1, source_target_pairs={{0,32},{16,48},{32,64},{48,80},{64,96},{80,112},{96,0},{112,16},{1... | collective-permute-start | bytes 638984 | tf_op jit(solution)/shard_map/ppermute | solution.py:56
  119.7 3.8 %collective-permute-done.35.refs_4_ = f32[13,8,512]{2,1,0:T(8,128)S(1)} collective-permute-done((f32[13,8,512]{2,1,0:T(8,128)S(1)}, f32[13,8,512]{2,1,0:T(8,128)S(1)}, u32[]{:S(2)}, u32[]{:S(2)}) %collective-permute-start.35) | collective-permute-done | bytes 213024 | tf_op jit(solution)/shard_map/ppermute | solution.py:56
  123.5 1.2 collective-permute-done.37.refs_6_
  124.7 1.3 %shard_map.59 = f32[27,32,512]{2,1,0:T(8,128)} custom-call(f32[13,8,512]{2,1,0:T(8,128)S(1)} %convert_add_fusion.2.refs_0_, f32[14,8,512]{2,1,0:T(8,128)S(1)} %convert_add_fusion.refs_1_, f32[13,8,512]{2,1,0:T(8,128)S(1)} %collective-permute-done.33.refs_2_, f32[14,8,512]{2,1,0:T(8,128)S(1)} %collective-permute-done.34.refs_3_, ...), custom_call_target="tpu_custom_call" | custom-call | tf_op jit(solution)/shard_map/pallas_call | solution.py:436
  126.1 1.2 shard_map.58
  (56 shorter events, 4.1 us)
Async XLA Ops:
  0.6 27.2 %collective-permute-start.6 = (bf16[27,32,512]{2,1,0:T(8,128)(2,1)}, bf16[27,32,512]{2,1,0:T(8,128)(2,1)S(1)}, u32[]{:S(2)}, u32[]{:S(2)}) collective-permute-start(bf16[27,32,512]{2,1,0:T(8,128)(2,1)} %own.1), channel_id=1, source_target_pairs={{0,12},{1,13},{2,14},{3,15},{4,0},{5,1},{6,2},{7,3},{8,4},{9,5},{1... | collective-permute-start | bytes 2654216 | tf_op jit(solution)/shard_map/ppermute | solution.py:51
  3.8 24.1 %collective-permute-start.7 = (bf16[27,32,512]{2,1,0:T(8,128)(2,1)}, bf16[27,32,512]{2,1,0:T(8,128)(2,1)S(1)}, u32[]{:S(2)}, u32[]{:S(2)}) collective-permute-start(bf16[27,32,512]{2,1,0:T(8,128)(2,1)} %own.1), channel_id=1, source_target_pairs={{0,4},{1,5},{2,6},{3,7},{4,8},{5,9},{6,10},{7,11},{8,12},{9,13},{1... | collective-permute-start | bytes 2654216 | tf_op jit(solution)/shard_map/ppermute | solution.py:51
  3.8 1.0 copy-start.1
  5.6 3.6 %collective-permute-start = (bf16[4,8,16,128]{3,2,1,0:T(8,128)(2,1)S(1)}, bf16[4,8,16,128]{3,2,1,0:T(8,128)(2,1)S(1)}, u32[]{:S(2)}, u32[]{:S(2)}) collective-permute-start(bf16[4,8,16,128]{3,2,1,0:T(8,128)(2,1)S(1)} %get-tuple-element.78), channel_id=1, source_target_pairs={{0,1},{1,0},{2,3},{3,2},{4,5},{5,4},{6,7},{7,6},{8,9},{9,8},{10,11... | collective-permute-start | bytes 393224 | tf_op jit(solution)/shard_map/ppermute | solution.py:43
  7.1 14.3 %collective-permute-start.3 = (bf16[2,8,16,512]{3,2,1,0:T(8,128)(2,1)S(1)}, bf16[2,8,16,512]{3,2,1,0:T(8,128)(2,1)S(1)}, u32[]{:S(2)}, u32[]{:S(2)}) collective-permute-start(bf16[2,8,16,512]{3,2,1,0:T(8,128)(2,1)S(1)} %get-tuple-element.153), channel_id=1, source_target_pairs={{0,2},{1,3},{2,0},{3,1},{4,6},{5,7},{6,4},{7,5},{8,10},{9,11},{10,... | collective-permute-start | bytes 786440 | tf_op jit(solution)/shard_map/ppermute | solution.py:43
  9.1 10.1 %collective-permute-start.1 = (bf16[4,8,16,128]{3,2,1,0:T(8,128)(2,1)S(1)}, bf16[4,8,16,128]{3,2,1,0:T(8,128)(2,1)S(1)}, u32[]{:S(2)}, u32[]{:S(2)}) collective-permute-start(bf16[4,8,16,128]{3,2,1,0:T(8,128)(2,1)S(1)} %get-tuple-element.79), channel_id=1, source_target_pairs={{0,2},{1,3},{2,0},{3,1},{4,6},{5,7},{6,4},{7,5},{8,10},{9,11},{10,... | collective-permute-start | bytes 393224 | tf_op jit(solution)/shard_map/ppermute | solution.py:43
  9.2 12.1 %collective-permute-start.2 = (bf16[4,8,16,128]{3,2,1,0:T(8,128)(2,1)S(1)}, bf16[4,8,16,128]{3,2,1,0:T(8,128)(2,1)S(1)}, u32[]{:S(2)}, u32[]{:S(2)}) collective-permute-start(bf16[4,8,16,128]{3,2,1,0:T(8,128)(2,1)S(1)} %get-tuple-element.80), channel_id=1, source_target_pairs={{0,3},{1,2},{2,1},{3,0},{4,7},{5,6},{6,5},{7,4},{8,11},{9,10},{10,... | collective-permute-start | bytes 393224 | tf_op jit(solution)/shard_map/ppermute | solution.py:43
  21.4 6.5 %collective-permute-start.4 = (bf16[4,4,16,128]{3,2,1,0:T(8,128)(2,1)S(1)}, bf16[4,4,16,128]{3,2,1,0:T(8,128)(2,1)S(1)}, u32[]{:S(2)}, u32[]{:S(2)}) collective-permute-start(bf16[4,4,16,128]{3,2,1,0:T(8,128)(2,1)S(1)} %get-tuple-element.85), channel_id=1, source_target_pairs={{0,16},{32,48},{64,80},{96,112},{16,0},{48,32},{80,64},{112,96},{1... | collective-permute-start | bytes 196616 | tf_op jit(solution)/shard_map/ppermute | solution.py:62
  25.1 2.8 %collective-permute-start.5 = (bf16[4,4,16,128]{3,2,1,0:T(8,128)(2,1)S(1)}, bf16[4,4,16,128]{3,2,1,0:T(8,128)(2,1)S(1)}, u32[]{:S(2)}, u32[]{:S(2)}) collective-permute-start(bf16[4,4,16,128]{3,2,1,0:T(8,128)(2,1)S(1)} %get-tuple-element.86), channel_id=1, source_target_pairs={{16,32},{48,64},{80,96},{32,16},{64,48},{96,80},{17,33},{49,65},{8... | collective-permute-start | bytes 196616 | tf_op jit(solution)/shard_map/ppermute | solution.py:62
  27.9 9.4 %collective-permute-start.10 = (bf16[2,8,16,512]{3,2,1,0:T(8,128)(2,1)S(1)}, bf16[2,8,16,512]{3,2,1,0:T(8,128)(2,1)S(1)}, u32[]{:S(2)}, u32[]{:S(2)}) collective-permute-start(bf16[2,8,16,512]{3,2,1,0:T(8,128)(2,1)S(1)} %get-tuple-element.93), channel_id=1, source_target_pairs={{0,2},{1,3},{2,0},{3,1},{4,6},{5,7},{6,4},{7,5},{8,10},{9,11},{10,... | collective-permute-start | bytes 786440 | tf_op jit(solution)/shard_map/ppermute | solution.py:43
  29.2 13.5 %collective-permute-start.11 = (bf16[4,8,16,512]{3,2,1,0:T(8,128)(2,1)S(1)}, bf16[4,8,16,512]{3,2,1,0:T(8,128)(2,1)S(1)}, u32[]{:S(2)}, u32[]{:S(2)}) collective-permute-start(bf16[4,8,16,512]{3,2,1,0:T(8,128)(2,1)S(1)} %fusion.3.own_act), channel_id=1, source_target_pairs={{0,1},{1,0},{2,3},{3,2},{4,5},{5,4},{6,7},{7,6},{8,9},{9,8},{10,11... | collective-permute-start | bytes 1572872 | tf_op jit(solution)/shard_map/ppermute | solution.py:43
  29.3 4.1 %collective-permute-start.8 = (bf16[10,16,128]{2,1,0:T(8,128)(2,1)S(1)}, bf16[10,16,128]{2,1,0:T(8,128)(2,1)S(1)}, u32[]{:S(2)}, u32[]{:S(2)}) collective-permute-start(bf16[10,16,128]{2,1,0:T(8,128)(2,1)S(1)} %get-tuple-element.89), channel_id=1, source_target_pairs={{0,4},{1,5},{2,6},{3,7},{8,12},{9,13},{10,14},{11,15},{4,0},{5,1},... | collective-permute-start | bytes 122888 | tf_op jit(solution)/shard_map/ppermute | solution.py:68
  30.0 3.4 %collective-permute-start.9 = (bf16[10,16,128]{2,1,0:T(8,128)(2,1)S(1)}, bf16[10,16,128]{2,1,0:T(8,128)(2,1)S(1)}, u32[]{:S(2)}, u32[]{:S(2)}) collective-permute-start(bf16[10,16,128]{2,1,0:T(8,128)(2,1)S(1)} %get-tuple-element.90), channel_id=1, source_target_pairs={{4,8},{5,9},{6,10},{7,11},{8,4},{9,5},{10,6},{11,7},{20,24},{21,25... | collective-permute-start | bytes 122888 | tf_op jit(solution)/shard_map/ppermute | solution.py:68
  30.6 12.1 %collective-permute-start.12 = (bf16[2,8,16,512]{3,2,1,0:T(8,128)(2,1)S(1)}, bf16[2,8,16,512]{3,2,1,0:T(8,128)(2,1)S(1)}, u32[]{:S(2)}, u32[]{:S(2)}) collective-permute-start(bf16[2,8,16,512]{3,2,1,0:T(8,128)(2,1)S(1)} %collective-permute-done.3.far_low), channel_id=1, source_target_pairs={{0,1},{1,0},{2,3},{3,2},{4,5},{5,4},{6,7},{7,6},{8,9},{9,8},{10,11... | collective-permute-start | bytes 786440 | tf_op jit(solution)/shard_map/ppermute | solution.py:43
  37.2 5.5 %collective-permute-start.13 = (bf16[2,8,16,512]{3,2,1,0:T(8,128)(2,1)S(1)}, bf16[2,8,16,512]{3,2,1,0:T(8,128)(2,1)S(1)}, u32[]{:S(2)}, u32[]{:S(2)}) collective-permute-start(bf16[2,8,16,512]{3,2,1,0:T(8,128)(2,1)S(1)} %collective-permute-done.10.far_high), channel_id=1, source_target_pairs={{0,1},{1,0},{2,3},{3,2},{4,5},{5,4},{6,7},{7,6},{8,9},{9,8},{10,11... | collective-permute-start | bytes 786440 | tf_op jit(solution)/shard_map/ppermute | solution.py:43
  37.3 21.2 %collective-permute-start.14 = (bf16[13,32,512]{2,1,0:T(8,128)(2,1)S(1)}, bf16[13,32,512]{2,1,0:T(8,128)(2,1)S(1)}, u32[]{:S(2)}, u32[]{:S(2)}) collective-permute-start(bf16[13,32,512]{2,1,0:T(8,128)(2,1)S(1)} %slice.23), channel_id=1, source_target_pairs={{0,4},{1,5},{2,6},{3,7},{4,8},{5,9},{6,10},{7,11},{8,12},{9,13},{1... | collective-permute-start | bytes 1277960 | tf_op jit(solution)/shard_map/ppermute | solution.py:51
  38.1 22.4 %collective-permute-start.15 = (bf16[14,32,512]{2,1,0:T(8,128)(2,1)S(1)}, bf16[14,32,512]{2,1,0:T(8,128)(2,1)S(1)}, u32[]{:S(2)}, u32[]{:S(2)}) collective-permute-start(bf16[14,32,512]{2,1,0:T(8,128)(2,1)S(1)} %slice.24), channel_id=1, source_target_pairs={{0,12},{1,13},{2,14},{3,15},{4,0},{5,1},{6,2},{7,3},{8,4},{9,5},{1... | collective-permute-start | bytes 1376264 | tf_op jit(solution)/shard_map/ppermute | solution.py:51
  42.7 17.7 %copy-start.2 = (bf16[27,32,512]{2,1,0:T(8,128)(2,1)S(1)}, bf16[27,32,512]{2,1,0:T(8,128)(2,1)}, u32[]{:S(2)}) copy-start(bf16[27,32,512]{2,1,0:T(8,128)(2,1)} %own.1) | copy-start | bytes 2654212
  50.5 18.7 %collective-permute-start.16 = (bf16[2,13,16,512]{3,2,1,0:T(8,128)(2,1)S(1)}, bf16[2,13,16,512]{3,2,1,0:T(8,128)(2,1)S(1)}, u32[]{:S(2)}, u32[]{:S(2)}) collective-permute-start(bf16[2,13,16,512]{3,2,1,0:T(8,128)(2,1)S(1)} %get-tuple-element.116), channel_id=1, source_target_pairs={{0,32},{16,48},{32,64},{48,80},{64,96},{80,112},{96,0},{112,16},{1... | collective-permute-start | bytes 1277960 | tf_op jit(solution)/shard_map/ppermute | solution.py:56
  55.9 13.3 %collective-permute-start.17 = (bf16[2,13,16,512]{3,2,1,0:T(8,128)(2,1)S(1)}, bf16[2,13,16,512]{3,2,1,0:T(8,128)(2,1)S(1)}, u32[]{:S(2)}, u32[]{:S(2)}) collective-permute-start(bf16[2,13,16,512]{3,2,1,0:T(8,128)(2,1)S(1)} %get-tuple-element.117), channel_id=1, source_target_pairs={{0,96},{16,112},{32,0},{48,16},{64,32},{80,48},{96,64},{112,80},{1... | collective-permute-start | bytes 1277960 | tf_op jit(solution)/shard_map/ppermute | solution.py:56
  57.2 13.6 %collective-permute-start.18 = (bf16[2,14,16,512]{3,2,1,0:T(8,128)(2,1)S(1)}, bf16[2,14,16,512]{3,2,1,0:T(8,128)(2,1)S(1)}, u32[]{:S(2)}, u32[]{:S(2)}) collective-permute-start(bf16[2,14,16,512]{3,2,1,0:T(8,128)(2,1)S(1)} %get-tuple-element.118), channel_id=1, source_target_pairs={{0,4},{1,5},{2,6},{3,7},{4,8},{5,9},{6,10},{7,11},{8,12},{9,13},{1... | collective-permute-start | bytes 1376264 | tf_op jit(solution)/shard_map/ppermute | solution.py:51
  58.5 12.3 %collective-permute-start.19 = (bf16[2,14,16,512]{3,2,1,0:T(8,128)(2,1)S(1)}, bf16[2,14,16,512]{3,2,1,0:T(8,128)(2,1)S(1)}, u32[]{:S(2)}, u32[]{:S(2)}) collective-permute-start(bf16[2,14,16,512]{3,2,1,0:T(8,128)(2,1)S(1)} %get-tuple-element.119), channel_id=1, source_target_pairs={{0,12},{1,13},{2,14},{3,15},{4,0},{5,1},{6,2},{7,3},{8,4},{9,5},{1... | collective-permute-start | bytes 1376264 | tf_op jit(solution)/shard_map/ppermute | solution.py:51
  70.8 11.9 %collective-permute-start.24 = (f32[2,4,8,16,512]{4,3,2,1,0:T(8,128)S(1)}, f32[2,4,8,16,512]{4,3,2,1,0:T(8,128)S(1)}, u32[]{:S(2)}, u32[]{:S(2)}) collective-permute-start(f32[2,4,8,16,512]{4,3,2,1,0:T(8,128)S(1)} %get-tuple-element.133), channel_id=1, source_target_pairs={{0,1},{1,0},{2,3},{3,2},{4,5},{5,4},{6,7},{7,6},{8,9},{9,8},{10,11... | collective-permute-start | bytes 6291464 | tf_op jit(solution)/shard_map/ppermute | solution.py:43
  71.0 11.7 %collective-permute-start.22 = (bf16[14,16,512]{2,1,0:T(8,128)(2,1)S(1)}, bf16[14,16,512]{2,1,0:T(8,128)(2,1)S(1)}, u32[]{:S(2)}, u32[]{:S(2)}) collective-permute-start(bf16[14,16,512]{2,1,0:T(8,128)(2,1)S(1)} %get-tuple-element.131), channel_id=1, source_target_pairs={{0,4},{1,5},{2,6},{3,7},{4,8},{5,9},{6,10},{7,11},{8,12},{9,13},{1... | collective-permute-start | bytes 688136 | tf_op jit(solution)/shard_map/ppermute | solution.py:51
  72.5 10.1 %collective-permute-start.23 = (bf16[14,16,512]{2,1,0:T(8,128)(2,1)S(1)}, bf16[14,16,512]{2,1,0:T(8,128)(2,1)S(1)}, u32[]{:S(2)}, u32[]{:S(2)}) collective-permute-start(bf16[14,16,512]{2,1,0:T(8,128)(2,1)S(1)} %get-tuple-element.132), channel_id=1, source_target_pairs={{0,12},{1,13},{2,14},{3,15},{4,0},{5,1},{6,2},{7,3},{8,4},{9,5},{1... | collective-permute-start | bytes 688136 | tf_op jit(solution)/shard_map/ppermute | solution.py:51
  74.3 8.4 %collective-permute-start.20 = (bf16[13,16,512]{2,1,0:T(8,128)(2,1)S(1)}, bf16[13,16,512]{2,1,0:T(8,128)(2,1)S(1)}, u32[]{:S(2)}, u32[]{:S(2)}) collective-permute-start(bf16[13,16,512]{2,1,0:T(8,128)(2,1)S(1)} %get-tuple-element.129), channel_id=1, source_target_pairs={{0,32},{16,48},{32,64},{48,80},{64,96},{80,112},{96,0},{112,16},{1... | collective-permute-start | bytes 638984 | tf_op jit(solution)/shard_map/ppermute | solution.py:56
  74.7 8.0 %collective-permute-start.21 = (bf16[13,16,512]{2,1,0:T(8,128)(2,1)S(1)}, bf16[13,16,512]{2,1,0:T(8,128)(2,1)S(1)}, u32[]{:S(2)}, u32[]{:S(2)}) collective-permute-start(bf16[13,16,512]{2,1,0:T(8,128)(2,1)S(1)} %get-tuple-element.130), channel_id=1, source_target_pairs={{0,96},{16,112},{32,0},{48,16},{64,32},{80,48},{96,64},{112,80},{1... | collective-permute-start | bytes 638984 | tf_op jit(solution)/shard_map/ppermute | solution.py:56
  83.0 5.8 %collective-permute-start.27 = (bf16[13,8,512]{2,1,0:T(8,128)(2,1)S(1)}, bf16[13,8,512]{2,1,0:T(8,128)(2,1)S(1)}, u32[]{:S(2)}, u32[]{:S(2)}) collective-permute-start(bf16[13,8,512]{2,1,0:T(8,128)(2,1)S(1)} %get-tuple-element.144), channel_id=1, source_target_pairs={{0,12},{1,13},{2,14},{3,15},{4,0},{5,1},{6,2},{7,3},{8,4},{9,5},{1... | collective-permute-start | bytes 319496 | tf_op jit(solution)/shard_map/ppermute | solution.py:51
  84.7 6.4 %collective-permute-start.26 = (bf16[13,8,512]{2,1,0:T(8,128)(2,1)S(1)}, bf16[13,8,512]{2,1,0:T(8,128)(2,1)S(1)}, u32[]{:S(2)}, u32[]{:S(2)}) collective-permute-start(bf16[13,8,512]{2,1,0:T(8,128)(2,1)S(1)} %get-tuple-element.143), channel_id=1, source_target_pairs={{0,8},{1,9},{2,10},{3,11},{4,12},{5,13},{6,14},{7,15},{8,0},{9,1},... | collective-permute-start | bytes 319496 | tf_op jit(solution)/shard_map/ppermute | solution.py:51
  85.3 6.9 %collective-permute-start.25 = (bf16[13,8,512]{2,1,0:T(8,128)(2,1)S(1)}, bf16[13,8,512]{2,1,0:T(8,128)(2,1)S(1)}, u32[]{:S(2)}, u32[]{:S(2)}) collective-permute-start(bf16[13,8,512]{2,1,0:T(8,128)(2,1)S(1)} %get-tuple-element.142), channel_id=1, source_target_pairs={{0,4},{1,5},{2,6},{3,7},{4,8},{5,9},{6,10},{7,11},{8,12},{9,13},{1... | collective-permute-start | bytes 319496 | tf_op jit(solution)/shard_map/ppermute | solution.py:51
  85.8 6.5 %collective-permute-start.30 = (bf16[14,8,512]{2,1,0:T(8,128)(2,1)S(1)}, bf16[14,8,512]{2,1,0:T(8,128)(2,1)S(1)}, u32[]{:S(2)}, u32[]{:S(2)}) collective-permute-start(bf16[14,8,512]{2,1,0:T(8,128)(2,1)S(1)} %get-tuple-element.148), channel_id=1, source_target_pairs={{0,96},{16,112},{32,0},{48,16},{64,32},{80,48},{96,64},{112,80},{1... | collective-permute-start | bytes 344072 | tf_op jit(solution)/shard_map/ppermute | solution.py:56
  88.8 6.4 %collective-permute-start.29 = (bf16[14,8,512]{2,1,0:T(8,128)(2,1)S(1)}, bf16[14,8,512]{2,1,0:T(8,128)(2,1)S(1)}, u32[]{:S(2)}, u32[]{:S(2)}) collective-permute-start(bf16[14,8,512]{2,1,0:T(8,128)(2,1)S(1)} %get-tuple-element.147), channel_id=1, source_target_pairs={{0,64},{16,80},{32,96},{48,112},{64,0},{80,16},{96,32},{112,48},{1... | collective-permute-start | bytes 344072 | tf_op jit(solution)/shard_map/ppermute | solution.py:56
  88.8 7.2 %collective-permute-start.28 = (bf16[14,8,512]{2,1,0:T(8,128)(2,1)S(1)}, bf16[14,8,512]{2,1,0:T(8,128)(2,1)S(1)}, u32[]{:S(2)}, u32[]{:S(2)}) collective-permute-start(bf16[14,8,512]{2,1,0:T(8,128)(2,1)S(1)} %get-tuple-element.146), channel_id=1, source_target_pairs={{0,32},{16,48},{32,64},{48,80},{64,96},{80,112},{96,0},{112,16},{1... | collective-permute-start | bytes 344072 | tf_op jit(solution)/shard_map/ppermute | solution.py:56
  96.1 9.0 %collective-permute-start.31 = (bf16[27,8,512]{2,1,0:T(8,128)(2,1)S(1)}, bf16[27,8,512]{2,1,0:T(8,128)(2,1)S(1)}, u32[]{:S(2)}, u32[]{:S(2)}) collective-permute-start(bf16[27,8,512]{2,1,0:T(8,128)(2,1)S(1)} %pad_maximum_fusion), channel_id=1, source_target_pairs={{0,16},{16,0},{32,48},{48,32},{64,80},{80,64},{96,112},{112,96},{1... | collective-permute-start | bytes 663560 | tf_op jit(solution)/shard_map/ppermute | solution.py:498
  105.1 21.0 %collective-permute-start.32 = (f32[4,8,16,512]{3,2,1,0:T(8,128)S(1)}, f32[4,8,16,512]{3,2,1,0:T(8,128)S(1)}, u32[]{:S(2)}, u32[]{:S(2)}) collective-permute-start(f32[4,8,16,512]{3,2,1,0:T(8,128)S(1)} %bitcast_add_fusion), channel_id=1, source_target_pairs={{0,2},{1,3},{2,0},{3,1},{4,6},{5,7},{6,4},{7,5},{8,10},{9,11},{10,... | collective-permute-start | bytes 3145736 | tf_op jit(solution)/shard_map/ppermute | solution.py:43
  107.2 18.9 %copy-start = (bf16[4,8,16,512]{3,2,1,0:T(8,128)(2,1)S(1)}, bf16[4,8,16,512]{3,2,1,0:T(8,128)(2,1)}, u32[]{:S(2)}) copy-start(bf16[4,8,16,512]{3,2,1,0:T(8,128)(2,1)} %pre.1) | copy-start | bytes 1572868
  107.2 7.8 %collective-permute-start.36 = (f32[14,8,512]{2,1,0:T(8,128)S(1)}, f32[14,8,512]{2,1,0:T(8,128)S(1)}, u32[]{:S(2)}, u32[]{:S(2)}) collective-permute-start(f32[14,8,512]{2,1,0:T(8,128)S(1)} %convert_add_fusion.refs_1_), channel_id=1, source_target_pairs={{0,96},{16,112},{32,0},{48,16},{64,32},{80,48},{96,64},{112,80},{1... | collective-permute-start | bytes 688136 | tf_op jit(solution)/shard_map/ppermute | solution.py:56
  108.0 9.7 %collective-permute-start.33 = (f32[13,8,512]{2,1,0:T(8,128)S(1)}, f32[13,8,512]{2,1,0:T(8,128)S(1)}, u32[]{:S(2)}, u32[]{:S(2)}) collective-permute-start(f32[13,8,512]{2,1,0:T(8,128)S(1)} %convert_add_fusion.2.refs_0_), channel_id=1, source_target_pairs={{0,32},{16,48},{32,64},{48,80},{64,96},{80,112},{96,0},{112,16},{1... | collective-permute-start | bytes 638984 | tf_op jit(solution)/shard_map/ppermute | solution.py:56
  109.4 14.0 %collective-permute-start.34 = (f32[14,8,512]{2,1,0:T(8,128)S(1)}, f32[14,8,512]{2,1,0:T(8,128)S(1)}, u32[]{:S(2)}, u32[]{:S(2)}) collective-permute-start(f32[14,8,512]{2,1,0:T(8,128)S(1)} %convert_add_fusion.refs_1_), channel_id=1, source_target_pairs={{0,32},{16,48},{32,64},{48,80},{64,96},{80,112},{96,0},{112,16},{1... | collective-permute-start | bytes 688136 | tf_op jit(solution)/shard_map/ppermute | solution.py:56
  115.0 9.7 %collective-permute-start.38 = (f32[14,8,512]{2,1,0:T(8,128)S(1)}, f32[14,8,512]{2,1,0:T(8,128)S(1)}, u32[]{:S(2)}, u32[]{:S(2)}) collective-permute-start(f32[14,8,512]{2,1,0:T(8,128)S(1)} %collective-permute-done.36.refs_5_), channel_id=1, source_target_pairs={{0,96},{16,112},{32,0},{48,16},{64,32},{80,48},{96,64},{112,80},{1... | collective-permute-start | bytes 688136 | tf_op jit(solution)/shard_map/ppermute | solution.py:56
  117.6 5.8 %collective-permute-start.35 = (f32[13,8,512]{2,1,0:T(8,128)S(1)}, f32[13,8,512]{2,1,0:T(8,128)S(1)}, u32[]{:S(2)}, u32[]{:S(2)}) collective-permute-start(f32[13,8,512]{2,1,0:T(8,128)S(1)} %convert_add_fusion.2.refs_0_), channel_id=1, source_target_pairs={{0,96},{16,112},{32,0},{48,16},{64,32},{80,48},{96,64},{112,80},{1... | collective-permute-start | bytes 638984 | tf_op jit(solution)/shard_map/ppermute | solution.py:56
  117.7 7.1 %collective-permute-start.37 = (f32[13,8,512]{2,1,0:T(8,128)S(1)}, f32[13,8,512]{2,1,0:T(8,128)S(1)}, u32[]{:S(2)}, u32[]{:S(2)}) collective-permute-start(f32[13,8,512]{2,1,0:T(8,128)S(1)} %collective-permute-done.33.refs_2_), channel_id=1, source_target_pairs={{0,32},{16,48},{32,64},{48,80},{64,96},{80,112},{96,0},{112,16},{1... | collective-permute-start | bytes 638984 | tf_op jit(solution)/shard_map/ppermute | solution.py:56

commit v11 on v8

--- a/solution.py
+++ b/solution.py
@@ -66,36 +66,43 @@
     return jnp.where(z == edge, 0.0, value)
 
 
-def pick_kernel(cot, extra, *quarters):
-    rows, _, _, chan = cot.shape
-    j = quad_place()
+def pick(block, k):
+    chan = block.shape[-1]
     q = chan // QUAD
     part = q // RING
     source = lax.broadcasted_iota(jnp.int32, (chan, q), 0)
     place = lax.broadcasted_iota(jnp.int32, (chan, q), 1)
-    base = lax.div(place, part) * q + lax.rem(place, part)
-
-    def take(block, pick):
-        got = jnp.dot(block.reshape(-1, chan), pick, preferred_element_type=F32)
-        return got.astype(BF16).reshape(block.shape[:-1] + (q,))
-
+    base = lax.div(place, part) * q + lax.rem(place, part) + (quad_place() ^ k) * part
+    matrix = jnp.where(source == base, 1.0, 0.0).astype(BF16)
+    got = jnp.dot(block.reshape(-1, chan), matrix, preferred_element_type=F32)
+    return got.astype(BF16).reshape(block.shape[:-1] + (q,))
+
+
+def own_kernel(cot, *quarters):
     for k, out in enumerate(quarters):
-        pick = jnp.where(source == base + (j ^ k) * part, 1.0, 0.0).astype(BF16)
-        out[0:rows] = take(cot[...], pick)
-        out[rows] = take(extra[...], pick)
-
-
-def pick_channels(cot, extra):
-    rows, width, depth, chan = cot.shape
-    quarter = jax.ShapeDtypeStruct((rows + 1, width, depth, chan // QUAD), BF16)
-    return pl.pallas_call(
-        pick_kernel,
+        out[...] = pick(cot[...], k)
+
+
+def extra_kernel(extra, q0, q1, q2, q3, *quarters):
+    for k, (own, out) in enumerate(zip((q0, q1, q2, q3), quarters)):
+        rows = own.shape[0]
+        out[0:rows] = own[...]
+        out[rows] = pick(extra[...], k)
+
+
+def quarters_of(kernel, rows, *ins):
+    width, depth, chan = ins[0].shape[-3:]
+    quarter = jax.ShapeDtypeStruct((rows, width, depth, chan // QUAD), BF16)
+    return pl.pallas_call(
+        kernel,
         out_shape=[quarter] * QUAD,
-        in_specs=[VMEM] * 2,
+        in_specs=[VMEM] * len(ins),
         out_specs=[VMEM] * QUAD,
         compiler_params=params(),
-        cost_estimate=small_cost(),
-    )(cot, extra)
+        cost_estimate=pl.CostEstimate(
+            flops=1000, bytes_accessed=40_000_000 if kernel is own_kernel else 1000, transcendentals=0
+        ),
+    )(*ins)
 
 
 def side_kernel(p0, p1, p2, p3, even, odd):
@@ -315,7 +322,7 @@
 def finish_kernel(pre, keep, near, far, out):
     value = pre[...].astype(F32)
     s = jax.nn.sigmoid(value)
-    grad = keep[...] + near[0] + far[...]
+    grad = keep[...] + near[0] + far[...].astype(F32)
     out[...] = (grad * s * (1.0 + value * (1.0 - s))).astype(BF16)
 
 
@@ -381,15 +388,18 @@
     for piece, part, k in zip(refs, (0, 1) * RING, (0, 0, 3, 3, 1, 1, 2, 2)):
         at = pl.ds(pl.multiple_of(lax.rem(x + k, RING) * size, size), size)
         first = part * low
-        out[first:first + piece.shape[0], at] = piece[...]
+        out[first:first + piece.shape[0], at] = piece[...].astype(F32)
 
 
 def gather_x(low, high):
     low_below, high_above = along_x(low, 1), along_x(high, -1)
-    high_below, low_above = along_x(high, 1), along_x(low, -1)
+    high_below, low_above = along_x(high.astype(BF16), 1), along_x(low.astype(BF16), -1)
     low_far, high_far = along_x(low_below, 1), along_x(high_above, -1)
-    _, size, chan = low.shape
-    pieces = (low, high, low_below, high_below, low_above, high_above, low_far, high_far)
+    return low, high, low_below, high_below, low_above, high_above, low_far, high_far
+
+
+def join(pieces):
+    _, size, chan = pieces[0].shape
     return pl.pallas_call(
         join_kernel,
         out_shape=jax.ShapeDtypeStruct((27, RING * size, chan), F32),
@@ -410,18 +420,20 @@
     pairs = pairs + [(t, s) for s, t in pairs]
     extra = lax.ppermute(jnp.where(j == 0, cot[0], cot[rows - 1]), "gy", pairs)
     act = jax.nn.silu(pre_act.astype(F32)).astype(BF16)
+    far = swap(act, 2)
     near = swap(act, 1)
-    extra, near, weight = barrier((extra, near, weight))
+    own_quarters = quarters_of(own_kernel, rows, cot)
+    extra, near, own_quarters = barrier((extra, near, own_quarters))
+    quarters = quarters_of(extra_kernel, rows + 1, extra, *own_quarters)
+    quarters, weight = barrier((quarters, weight))
     above = along_y(weight, -1, True)
     below = along_y(weight, 1, True)
-    quarters = pick_channels(cot, extra)
     quarters = [quarters[0]] + [swap(quarters[k], k) for k in (1, 2, 3)]
-    quarters, act = barrier((quarters, act))
-    far = swap(act, 2)
+    quarters, far = barrier((quarters, far))
+    acts = [act, near, far, swap(far, 1)]
     even, odd = sides(quarters)
     even, odd = swap_x(even, 0), swap_x(odd, 1)
-    even, odd, above, below, far = barrier((even, odd, above, below, far))
-    acts = [act, near, far, swap(far, 1)]
+    even, odd, above, below = barrier((even, odd, above, below))
     taps = XTAPS
     parts = [weight, above, along_y(below[:taps], 1, True), along_y(above[taps:], -1, True), below]
     held, turned = turn(quarters, even, odd)
@@ -454,12 +466,13 @@
     count = lax.axis_size("gx")
     mine = jnp.concatenate([low.astype(BF16), high.astype(BF16)])
     other = lax.ppermute(mine, "gx", [(g, g ^ 1) for g in range(count)])
-    other, passed = barrier((other, pass_on + got[1]))
+    other, passed = barrier((other, (pass_on + got[1]).astype(BF16)))
     far_grad = swap(passed, 2)
     low, high = low + other[:taps].astype(F32), high + other[taps:].astype(F32)
-    grad_weight = gather_x(low, high)
+    pieces = gather_x(low, high)
     grad_pre = finish(pre_act, keep, got, far_grad)
-    return (grad_pre, grad_weight)
+    grad_pre, pieces = barrier((grad_pre, pieces))
+    return (grad_pre, join(pieces))
 
 
 def solution(mesh):

time: 133 us -> 123 us (0.925)
  waiting for transfers between devices: 54.5 us -> 40.4 us
  starting transfers between devices: 50.8 us -> 53.9 us
    ppermute x2, waiting for transfers between devices: 13.7 us -> 1.96 us  [swap_x(): return lax.ppermute(block, 'gx', pairs + [(t, s) for s, t in pairs])]
    ppermute x13, starting transfers between devices: 18.6 us -> 23.5 us  [along_x(): lax.ppermute(block, 'gx', [(g, (g + 2 * step) % count) for g in range(cou...]
    ppermute x11, starting transfers between devices: 23.1 us -> 20.8 us  [along_y(): lax.ppermute(block, 'gy', [(s, t) for s, t in pairs if 0 <= t < count])]
    ppermute x13, waiting for transfers between devices: 19.9 us -> 17.8 us  [along_x(): lax.ppermute(block, 'gx', [(g, (g + 2 * step) % count) for g in range(cou...]
  transfers between devices with their start and end apart: 36 -> 36, of which waited for: 15 -> 15; matrix products, arithmetic and copies ran while one was open for 1% -> 1% of each run, Pallas kernels for 16% -> 17%
where the time goes in v11:
time: 123 us; the launch traced here: 122 us
  starting transfers between devices  53.9 us (44%)
  waiting for transfers between devices  40.4 us (33%)
  Pallas kernels  22.2 us (18%)
  other arithmetic  2.99 us (2%)
    ppermute x13, starting transfers between devices, along_x(): lax.ppermute(block, 'gx', [(g, (g + 2 * step) % count) for g in range(cou...  23.5 us
    ppermute x11, starting transfers between devices, along_y(): lax.ppermute(block, 'gy', [(s, t) for s, t in pairs if 0 <= t < count])  20.8 us
    ppermute x13, waiting for transfers between devices, along_x(): lax.ppermute(block, 'gx', [(g, (g + 2 * step) % count) for g in range(cou...  17.8 us
    ppermute x1, waiting for transfers between devices, body(): other = lax.ppermute(mine, 'gx', [(g, g ^ 1) for g in range(count)])  9.09 us
    pallas_call x1, Pallas kernels, input_terms(): pl.pallas_call(input_kernel, out_shape=[jax.ShapeDtypeStruct((2,) + block...  8.65 us
    ppermute x8, waiting for transfers between devices, swap(): return lax.ppermute(block, 'gy', [(g, g ^ k) for g in range(count)])  8.14 us
    pallas_call x1, Pallas kernels, weight_terms(): pl.pallas_call(functools.partial(weight_kernel, norm), out_shape=shapes,...  7.66 us
    ppermute x8, starting transfers between devices, swap(): return lax.ppermute(block, 'gy', [(g, g ^ k) for g in range(count)])  4.36 us
  transfers between devices with their start and end apart: 36, of which 15 were waited for; matrix products, arithmetic and copies ran while one was open for 1% of the time, Pallas kernels for 17%

profile of v11, /device:TPU:0, one launch (start us, length us, event | category | flops | bytes accessed | tf_op | source)
XLA Modules:
  0.0 121.6 jit_solution(16748165579580218670)
XLA Ops:
  0.6 1.4 %fusion.3.own_act = bf16[4,8,16,512]{3,2,1,0:T(8,128)(2,1)S(1)} fusion(bf16[4,8,16,512]{3,2,1,0:T(8,128)(2,1)} %pre.1), kind=kLoop, calls=%fused_computation.5 | loop fusion | flops 1572864 | bytes 1048576 | tf_op jit(solution)/shard_map/convert_element_type | solution.py:422
  2.2 2.1 %collective-permute-start.5 = (bf16[4,8,16,512]{3,2,1,0:T(8,128)(2,1)S(1)}, bf16[4,8,16,512]{3,2,1,0:T(8,128)(2,1)S(1)}, u32[]{:S(2)}, u32[]{:S(2)}) collective-permute-start(bf16[4,8,16,512]{3,2,1,0:T(8,128)(2,1)S(1)} %fusion.3.own_act), channel_id=1, source_target_pairs={{0,2},{1,3},{2,0},{3,1},{4,6},{5,7},{6,4},{7,5},{8,10},{9,11},{10,... | collective-permute-start | bytes 1572872 | tf_op jit(solution)/shard_map/ppermute | solution.py:43
  4.3 1.0 select_bitcast_fusion
  5.2 0.7 collective-permute-start
  5.9 1.0 copy-done.1
  7.0 0.7 shard_map.50
  7.7 0.3 shard_map.51
  8.0 8.3 %collective-permute-start.8 = (bf16[27,32,512]{2,1,0:T(8,128)(2,1)S(1)}, bf16[27,32,512]{2,1,0:T(8,128)(2,1)S(1)}, u32[]{:S(2)}, u32[]{:S(2)}) collective-permute-start(bf16[27,32,512]{2,1,0:T(8,128)(2,1)S(1)} %copy-done.2), channel_id=1, source_target_pairs={{0,12},{1,13},{2,14},{3,15},{4,0},{5,1},{6,2},{7,3},{8,4},{9,5},{1... | collective-permute-start | bytes 2654216 | tf_op jit(solution)/shard_map/ppermute | solution.py:51
  16.3 1.2 collective-permute-done.5.far
  17.6 1.6 %collective-permute-start.4 = (bf16[5,8,16,128]{3,2,1,0:T(8,128)(2,1)S(1)}, bf16[5,8,16,128]{3,2,1,0:T(8,128)(2,1)S(1)}, u32[]{:S(2)}, u32[]{:S(2)}) collective-permute-start(bf16[5,8,16,128]{3,2,1,0:T(8,128)(2,1)S(1)} %get-tuple-element.109), channel_id=1, source_target_pairs={{0,3},{1,2},{2,1},{3,0},{4,7},{5,6},{6,5},{7,4},{8,11},{9,10},{10,... | collective-permute-start | bytes 491528 | tf_op jit(solution)/shard_map/ppermute | solution.py:43
  19.2 4.2 %collective-permute-done.3.p2 = bf16[5,8,16,128]{3,2,1,0:T(8,128)(2,1)S(1)} collective-permute-done((bf16[5,8,16,128]{3,2,1,0:T(8,128)(2,1)S(1)}, bf16[5,8,16,128]{3,2,1,0:T(8,128)(2,1)S(1)}, u32[]{:S(2)}, u32[]{:S(2)}) %collective-permute-start.3) | collective-permute-done | bytes 163872 | tf_op jit(solution)/shard_map/ppermute | solution.py:43
  23.3 2.7 %collective-permute-done.4.p3 = bf16[5,8,16,128]{3,2,1,0:T(8,128)(2,1)S(1)} collective-permute-done((bf16[5,8,16,128]{3,2,1,0:T(8,128)(2,1)S(1)}, bf16[5,8,16,128]{3,2,1,0:T(8,128)(2,1)S(1)}, u32[]{:S(2)}, u32[]{:S(2)}) %collective-permute-start.4) | collective-permute-done | bytes 163872 | tf_op jit(solution)/shard_map/ppermute | solution.py:43
  26.1 0.5 collective-permute-start.10
  26.6 3.4 %collective-permute-start.6 = (bf16[4,5,16,128]{3,2,1,0:T(8,128)(2,1)S(1)}, bf16[4,5,16,128]{3,2,1,0:T(8,128)(2,1)S(1)}, u32[]{:S(2)}, u32[]{:S(2)}) collective-permute-start(bf16[4,5,16,128]{3,2,1,0:T(8,128)(2,1)S(1)} %get-tuple-element.114), channel_id=1, source_target_pairs={{0,16},{32,48},{64,80},{96,112},{16,0},{48,32},{80,64},{112,96},{1... | collective-permute-start | bytes 245768 | tf_op jit(solution)/shard_map/ppermute | solution.py:62
  30.0 0.7 collective-permute-start.7
  30.7 2.0 %collective-permute-done.6.even = bf16[4,5,16,128]{3,2,1,0:T(8,128)(2,1)S(1)} collective-permute-done((bf16[4,5,16,128]{3,2,1,0:T(8,128)(2,1)S(1)}, bf16[4,5,16,128]{3,2,1,0:T(8,128)(2,1)S(1)}, u32[]{:S(2)}, u32[]{:S(2)}) %collective-permute-start.6) | collective-permute-done | bytes 81952 | tf_op jit(solution)/shard_map/ppermute | solution.py:62
  32.7 1.1 collective-permute-done.9.below
  33.9 3.3 %collective-permute-start.12 = (bf16[14,32,512]{2,1,0:T(8,128)(2,1)S(1)}, bf16[14,32,512]{2,1,0:T(8,128)(2,1)S(1)}, u32[]{:S(2)}, u32[]{:S(2)}) collective-permute-start(bf16[14,32,512]{2,1,0:T(8,128)(2,1)S(1)} %slice.24), channel_id=1, source_target_pairs={{0,12},{1,13},{2,14},{3,15},{4,0},{5,1},{6,2},{7,3},{8,4},{9,5},{1... | collective-permute-start | bytes 1376264 | tf_op jit(solution)/shard_map/ppermute | solution.py:51
  37.2 1.8 %shard_map.53 = (bf16[18,10,16,128]{3,2,1,0:T(8,128)(2,1)S(1)}, bf16[1152,2304]{1,0:T(8,128)(2,1)S(1)}) custom-call(bf16[5,8,16,128]{3,2,1,0:T(8,128)(2,1)S(1)} %get-tuple-element.110.p0, bf16[5,8,16,128]{3,2,1,0:T(8,128)(2,1)S(1)} %collective-permute-done.2.p1, bf16[5,8,16,128]{3,2,1,0:T(8,128)(2,1)S(1)} %collective-permute-done.3.p2, ...), custom_call_target="tpu_custom_call" | custom-call | flops 1000 | bytes 1000 | tf_op jit(solution)/shard_map/pallas_call | solution.py:174
  39.1 7.7 %shard_map.54 = (bf16[2,13,16,512]{3,2,1,0:T(8,128)(2,1)S(1)}, bf16[2,13,16,512]{3,2,1,0:T(8,128)(2,1)S(1)}, f32[13,16,512]{2,1,0:T(8,128)S(1)}, f32[13,16,512]{...) custom-call(bf16[4,8,16,512]{3,2,1,0:T(8,128)(2,1)S(1)} %fusion.3.ow, ...), custom_call_target="tpu_custom_call" | custom-call | flops 7247757312 | bytes 10000000 | tf_op jit(solution)/shard_map/pallas_call | solution.py:243
  46.7 6.6 %collective-permute-start.13 = (bf16[2,13,16,512]{3,2,1,0:T(8,128)(2,1)S(1)}, bf16[2,13,16,512]{3,2,1,0:T(8,128)(2,1)S(1)}, u32[]{:S(2)}, u32[]{:S(2)}) collective-permute-start(bf16[2,13,16,512]{3,2,1,0:T(8,128)(2,1)S(1)} %get-tuple-element.139), channel_id=1, source_target_pairs={{0,32},{16,48},{32,64},{48,80},{64,96},{80,112},{96,0},{112,16},{1... | collective-permute-start | bytes 1277960 | tf_op jit(solution)/shard_map/ppermute | solution.py:56
  53.3 1.3 %collective-permute-start.14 = (bf16[2,13,16,512]{3,2,1,0:T(8,128)(2,1)S(1)}, bf16[2,13,16,512]{3,2,1,0:T(8,128)(2,1)S(1)}, u32[]{:S(2)}, u32[]{:S(2)}) collective-permute-start(bf16[2,13,16,512]{3,2,1,0:T(8,128)(2,1)S(1)} %get-tuple-element.140), channel_id=1, source_target_pairs={{0,96},{16,112},{32,0},{48,16},{64,32},{80,48},{96,64},{112,80},{1... | collective-permute-start | bytes 1277960 | tf_op jit(solution)/shard_map/ppermute | solution.py:56
  54.6 3.2 %collective-permute-start.16 = (bf16[2,14,16,512]{3,2,1,0:T(8,128)(2,1)S(1)}, bf16[2,14,16,512]{3,2,1,0:T(8,128)(2,1)S(1)}, u32[]{:S(2)}, u32[]{:S(2)}) collective-permute-start(bf16[2,14,16,512]{3,2,1,0:T(8,128)(2,1)S(1)} %get-tuple-element.142), channel_id=1, source_target_pairs={{0,12},{1,13},{2,14},{3,15},{4,0},{5,1},{6,2},{7,3},{8,4},{9,5},{1... | collective-permute-start | bytes 1376264 | tf_op jit(solution)/shard_map/ppermute | solution.py:51
  57.9 8.6 %shard_map.55 = (f32[2,4,8,16,512]{4,3,2,1,0:T(8,128)S(1)}, f32[4,8,16,512]{3,2,1,0:T(8,128)S(1)}, f32[4,8,16,512]{3,2,1,0:T(8,128)S(1)}) custom-call(bf16[18,10,16,128]{3,2,1,0:T(8,128)(2,1)S(1)} %get-tuple-element.133.held, bf16[27,32,512]{2,1,0:T(8,128)(2,1)S(1)} %copy-done.2, bf16[27,32,512]{2,1,0:T(8,128)(2,1)S(1)} %collective-permute-done.8.above, ...), custom_call_target="tpu_custom_call" | custom-call | flops 10192158720 | bytes 10000000 | tf_op jit(solution)/shard_map/pallas_call | solution.py:305
  66.9 3.2 %collective-permute-start.20 = (bf16[14,16,512]{2,1,0:T(8,128)(2,1)S(1)}, bf16[14,16,512]{2,1,0:T(8,128)(2,1)S(1)}, u32[]{:S(2)}, u32[]{:S(2)}) collective-permute-start(bf16[14,16,512]{2,1,0:T(8,128)(2,1)S(1)} %get-tuple-element.155), channel_id=1, source_target_pairs={{0,12},{1,13},{2,14},{3,15},{4,0},{5,1},{6,2},{7,3},{8,4},{9,5},{1... | collective-permute-start | bytes 688136 | tf_op jit(solution)/shard_map/ppermute | solution.py:51
  70.1 0.7 collective-permute-start.17
  70.8 2.6 %collective-permute-start.18 = (bf16[13,16,512]{2,1,0:T(8,128)(2,1)S(1)}, bf16[13,16,512]{2,1,0:T(8,128)(2,1)S(1)}, u32[]{:S(2)}, u32[]{:S(2)}) collective-permute-start(bf16[13,16,512]{2,1,0:T(8,128)(2,1)S(1)} %get-tuple-element.153), channel_id=1, source_target_pairs={{0,96},{16,112},{32,0},{48,16},{64,32},{80,48},{96,64},{112,80},{1... | collective-permute-start | bytes 638984 | tf_op jit(solution)/shard_map/ppermute | solution.py:56
  73.4 5.1 %collective-permute-done.17.refs_3_ = bf16[13,16,512]{2,1,0:T(8,128)(2,1)S(1)} collective-permute-done((bf16[13,16,512]{2,1,0:T(8,128)(2,1)S(1)}, bf16[13,16,512]{2,1,0:T(8,128)(2,1)S(1)}, u32[]{:S(2)}, u32[]{:S(2)}) %collective-permute-start.17) | collective-permute-done | bytes 213024 | tf_op jit(solution)/shard_map/ppermute | solution.py:56
  78.7 1.4 %collective-permute-start.24 = (bf16[13,8,512]{2,1,0:T(8,128)(2,1)S(1)}, bf16[13,8,512]{2,1,0:T(8,128)(2,1)S(1)}, u32[]{:S(2)}, u32[]{:S(2)}) collective-permute-start(bf16[13,8,512]{2,1,0:T(8,128)(2,1)S(1)} %get-tuple-element.167), channel_id=1, source_target_pairs={{0,12},{1,13},{2,14},{3,15},{4,0},{5,1},{6,2},{7,3},{8,4},{9,5},{1... | collective-permute-start | bytes 319496 | tf_op jit(solution)/shard_map/ppermute | solution.py:51
  80.2 1.1 collective-permute-start.22
  81.3 2.9 %collective-permute-start.27 = (bf16[14,8,512]{2,1,0:T(8,128)(2,1)S(1)}, bf16[14,8,512]{2,1,0:T(8,128)(2,1)S(1)}, u32[]{:S(2)}, u32[]{:S(2)}) collective-permute-start(bf16[14,8,512]{2,1,0:T(8,128)(2,1)S(1)} %get-tuple-element.171), channel_id=1, source_target_pairs={{0,96},{16,112},{32,0},{48,16},{64,32},{80,48},{96,64},{112,80},{1... | collective-permute-start | bytes 344072 | tf_op jit(solution)/shard_map/ppermute | solution.py:56
  84.3 0.9 collective-permute-start.25
  85.1 1.5 %collective-permute-done.23 = bf16[13,8,512]{2,1,0:T(8,128)(2,1)S(1)} collective-permute-done((bf16[13,8,512]{2,1,0:T(8,128)(2,1)S(1)}, bf16[13,8,512]{2,1,0:T(8,128)(2,1)S(1)}, u32[]{:S(2)}, u32[]{:S(2)}) %collective-permute-start.23) | collective-permute-done | bytes 106528 | tf_op jit(solution)/shard_map/ppermute | solution.py:51
  86.6 0.9 collective-permute-done.22
  87.5 0.3 collective-permute-done.27
  87.8 2.8 %collective-permute-done.26 = bf16[14,8,512]{2,1,0:T(8,128)(2,1)S(1)} collective-permute-done((bf16[14,8,512]{2,1,0:T(8,128)(2,1)S(1)}, bf16[14,8,512]{2,1,0:T(8,128)(2,1)S(1)}, u32[]{:S(2)}, u32[]{:S(2)}) %collective-permute-start.26) | collective-permute-done | bytes 114720 | tf_op jit(solution)/shard_map/ppermute | solution.py:56
  90.7 0.8 collective-permute-done.25
  91.6 0.5 collective-permute-start.28
  92.4 9.1 %collective-permute-done.28 = bf16[27,8,512]{2,1,0:T(8,128)(2,1)S(1)} collective-permute-done((bf16[27,8,512]{2,1,0:T(8,128)(2,1)S(1)}, bf16[27,8,512]{2,1,0:T(8,128)(2,1)S(1)}, u32[]{:S(2)}, u32[]{:S(2)}) %collective-permute-start.28) | collective-permute-done | bytes 221216 | tf_op jit(solution)/shard_map/ppermute | solution.py:468
  101.6 0.7 collective-permute-start.33
  102.3 1.5 %collective-permute-start.30 = (f32[13,8,512]{2,1,0:T(8,128)S(1)}, f32[13,8,512]{2,1,0:T(8,128)S(1)}, u32[]{:S(2)}, u32[]{:S(2)}) collective-permute-start(f32[13,8,512]{2,1,0:T(8,128)S(1)} %get-tuple-element.176.refs_0_), channel_id=1, source_target_pairs={{0,32},{16,48},{32,64},{48,80},{64,96},{80,112},{96,0},{112,16},{1... | collective-permute-start | bytes 638984 | tf_op jit(solution)/shard_map/ppermute | solution.py:56
  103.8 5.0 %collective-permute-done.33.refs_5_ = f32[14,8,512]{2,1,0:T(8,128)S(1)} collective-permute-done((f32[14,8,512]{2,1,0:T(8,128)S(1)}, f32[14,8,512]{2,1,0:T(8,128)S(1)}, u32[]{:S(2)}, u32[]{:S(2)}) %collective-permute-start.33) | collective-permute-done | bytes 229408 | tf_op jit(solution)/shard_map/ppermute | solution.py:56
  108.8 3.1 %collective-permute-start.35 = (f32[14,8,512]{2,1,0:T(8,128)S(1)}, f32[14,8,512]{2,1,0:T(8,128)S(1)}, u32[]{:S(2)}, u32[]{:S(2)}) collective-permute-start(f32[14,8,512]{2,1,0:T(8,128)S(1)} %collective-permute-done.33.refs_5_), channel_id=1, source_target_pairs={{0,96},{16,112},{32,0},{48,16},{64,32},{80,48},{96,64},{112,80},{1... | collective-permute-start | bytes 688136 | tf_op jit(solution)/shard_map/ppermute | solution.py:56
  111.9 3.3 %collective-permute-start.32 = (bf16[13,8,512]{2,1,0:T(8,128)(2,1)S(1)}, bf16[13,8,512]{2,1,0:T(8,128)(2,1)S(1)}, u32[]{:S(2)}, u32[]{:S(2)}) collective-permute-start(bf16[13,8,512]{2,1,0:T(8,128)(2,1)S(1)} %get-tuple-element.184), channel_id=1, source_target_pairs={{0,96},{16,112},{32,0},{48,16},{64,32},{80,48},{96,64},{112,80},{1... | collective-permute-start | bytes 319496 | tf_op jit(solution)/shard_map/ppermute | solution.py:56
  115.2 1.2 %shard_map.58 = bf16[4,8,16,512]{3,2,1,0:T(8,128)(2,1)} custom-call(bf16[4,8,16,512]{3,2,1,0:T(8,128)(2,1)S(1)} %copy-done, f32[4,8,16,512]{3,2,1,0:T(8,128)S(1)} %get-tuple-element.143.keep, f32[2,4,8,16,512]{4,3,2,1,0:T(8,128)S(1)} %collective-permute-done.21.near, bf16[4,8,16,512]{3,2,1,0:T(8,128)(2,1)S(1)} %collective-permute-done.29.far), custom_call_target="tpu_custom_call" | custom-call | tf_op jit(solution)/shard_map/pallas_call | solution.py:330
  116.4 1.1 collective-permute-done.32.refs_4_
  117.5 2.7 %collective-permute-done.31.refs_3_ = bf16[14,8,512]{2,1,0:T(8,128)(2,1)S(1)} collective-permute-done((bf16[14,8,512]{2,1,0:T(8,128)(2,1)S(1)}, bf16[14,8,512]{2,1,0:T(8,128)(2,1)S(1)}, u32[]{:S(2)}, u32[]{:S(2)}) %collective-permute-start.31) | collective-permute-done | bytes 114720 | tf_op jit(solution)/shard_map/ppermute | solution.py:56
  120.2 1.3 %shard_map.59 = f32[27,32,512]{2,1,0:T(8,128)} custom-call(f32[13,8,512]{2,1,0:T(8,128)S(1)} %get-tuple-element.176.refs_0_, f32[14,8,512]{2,1,0:T(8,128)S(1)} %get-tuple-element.177.refs_1_, f32[13,8,512]{2,1,0:T(8,128)S(1)} %collective-permute-done.30.refs_2_, bf16[14,8,512]{2,1,0:T(8,128)(2,1)S(1)} %collective-permute-done.31.refs_3_, ...), custom_call_target="tpu_custom_call" | custom-call | tf_op jit(solution)/shard_map/pallas_call | solution.py:403
  (50 shorter events, 1.5 us)
Async XLA Ops:
  0.6 7.4 %copy-start.2 = (bf16[27,32,512]{2,1,0:T(8,128)(2,1)S(1)}, bf16[27,32,512]{2,1,0:T(8,128)(2,1)}, u32[]{:S(2)}) copy-start(bf16[27,32,512]{2,1,0:T(8,128)(2,1)} %own) | copy-start | bytes 2654212
  2.1 5.6 %collective-permute-start.1 = (bf16[4,8,16,512]{3,2,1,0:T(8,128)(2,1)S(1)}, bf16[4,8,16,512]{3,2,1,0:T(8,128)(2,1)S(1)}, u32[]{:S(2)}, u32[]{:S(2)}) collective-permute-start(bf16[4,8,16,512]{3,2,1,0:T(8,128)(2,1)S(1)} %fusion.3.own_act), channel_id=1, source_target_pairs={{0,1},{1,0},{2,3},{3,2},{4,5},{5,4},{6,7},{7,6},{8,9},{9,8},{10,11... | collective-permute-start | bytes 1572872 | tf_op jit(solution)/shard_map/ppermute | solution.py:43
  2.2 15.4 %collective-permute-start.5 = (bf16[4,8,16,512]{3,2,1,0:T(8,128)(2,1)S(1)}, bf16[4,8,16,512]{3,2,1,0:T(8,128)(2,1)S(1)}, u32[]{:S(2)}, u32[]{:S(2)}) collective-permute-start(bf16[4,8,16,512]{3,2,1,0:T(8,128)(2,1)S(1)} %fusion.3.own_act), channel_id=1, source_target_pairs={{0,2},{1,3},{2,0},{3,1},{4,6},{5,7},{6,4},{7,5},{8,10},{9,11},{10,... | collective-permute-start | bytes 1572872 | tf_op jit(solution)/shard_map/ppermute | solution.py:43
  5.2 2.4 %collective-permute-start = (bf16[8,16,512]{2,1,0:T(8,128)(2,1)S(1)}, bf16[8,16,512]{2,1,0:T(8,128)(2,1)S(1)}, u32[]{:S(2)}, u32[]{:S(2)}) collective-permute-start(bf16[8,16,512]{2,1,0:T(8,128)(2,1)S(1)} %select_bitcast_fusion), channel_id=1, source_target_pairs={{3,4},{7,8},{11,12},{4,3},{8,7},{12,11},{19,20},{23,24},{27,28},{2... | collective-permute-start | bytes 393224 | tf_op jit(solution)/shard_map/ppermute | solution.py:421
  5.9 1.0 copy-start.1
  8.0 24.6 %collective-permute-start.8 = (bf16[27,32,512]{2,1,0:T(8,128)(2,1)S(1)}, bf16[27,32,512]{2,1,0:T(8,128)(2,1)S(1)}, u32[]{:S(2)}, u32[]{:S(2)}) collective-permute-start(bf16[27,32,512]{2,1,0:T(8,128)(2,1)S(1)} %copy-done.2), channel_id=1, source_target_pairs={{0,12},{1,13},{2,14},{3,15},{4,0},{5,1},{6,2},{7,3},{8,4},{9,5},{1... | collective-permute-start | bytes 2654216 | tf_op jit(solution)/shard_map/ppermute | solution.py:51
  16.3 17.4 %collective-permute-start.9 = (bf16[27,32,512]{2,1,0:T(8,128)(2,1)S(1)}, bf16[27,32,512]{2,1,0:T(8,128)(2,1)S(1)}, u32[]{:S(2)}, u32[]{:S(2)}) collective-permute-start(bf16[27,32,512]{2,1,0:T(8,128)(2,1)S(1)} %copy-done.2), channel_id=1, source_target_pairs={{0,4},{1,5},{2,6},{3,7},{4,8},{5,9},{6,10},{7,11},{8,12},{9,13},{1... | collective-permute-start | bytes 2654216 | tf_op jit(solution)/shard_map/ppermute | solution.py:51
  16.3 2.8 %collective-permute-start.2 = (bf16[5,8,16,128]{3,2,1,0:T(8,128)(2,1)S(1)}, bf16[5,8,16,128]{3,2,1,0:T(8,128)(2,1)S(1)}, u32[]{:S(2)}, u32[]{:S(2)}) collective-permute-start(bf16[5,8,16,128]{3,2,1,0:T(8,128)(2,1)S(1)} %get-tuple-element.107), channel_id=1, source_target_pairs={{0,1},{1,0},{2,3},{3,2},{4,5},{5,4},{6,7},{7,6},{8,9},{9,8},{10,11... | collective-permute-start | bytes 491528 | tf_op jit(solution)/shard_map/ppermute | solution.py:43
  16.3 7.0 %collective-permute-start.3 = (bf16[5,8,16,128]{3,2,1,0:T(8,128)(2,1)S(1)}, bf16[5,8,16,128]{3,2,1,0:T(8,128)(2,1)S(1)}, u32[]{:S(2)}, u32[]{:S(2)}) collective-permute-start(bf16[5,8,16,128]{3,2,1,0:T(8,128)(2,1)S(1)} %get-tuple-element.108), channel_id=1, source_target_pairs={{0,2},{1,3},{2,0},{3,1},{4,6},{5,7},{6,4},{7,5},{8,10},{9,11},{10,... | collective-permute-start | bytes 491528 | tf_op jit(solution)/shard_map/ppermute | solution.py:43
  17.6 8.5 %collective-permute-start.4 = (bf16[5,8,16,128]{3,2,1,0:T(8,128)(2,1)S(1)}, bf16[5,8,16,128]{3,2,1,0:T(8,128)(2,1)S(1)}, u32[]{:S(2)}, u32[]{:S(2)}) collective-permute-start(bf16[5,8,16,128]{3,2,1,0:T(8,128)(2,1)S(1)} %get-tuple-element.109), channel_id=1, source_target_pairs={{0,3},{1,2},{2,1},{3,0},{4,7},{5,6},{6,5},{7,4},{8,11},{9,10},{10,... | collective-permute-start | bytes 491528 | tf_op jit(solution)/shard_map/ppermute | solution.py:43
  26.1 13.0 %collective-permute-start.10 = (bf16[4,8,16,512]{3,2,1,0:T(8,128)(2,1)S(1)}, bf16[4,8,16,512]{3,2,1,0:T(8,128)(2,1)S(1)}, u32[]{:S(2)}, u32[]{:S(2)}) collective-permute-start(bf16[4,8,16,512]{3,2,1,0:T(8,128)(2,1)S(1)} %collective-permute-done.5.far), channel_id=1, source_target_pairs={{0,1},{1,0},{2,3},{3,2},{4,5},{5,4},{6,7},{7,6},{8,9},{9,8},{10,11... | collective-permute-start | bytes 1572872 | tf_op jit(solution)/shard_map/ppermute | solution.py:43
  26.6 6.0 %collective-permute-start.6 = (bf16[4,5,16,128]{3,2,1,0:T(8,128)(2,1)S(1)}, bf16[4,5,16,128]{3,2,1,0:T(8,128)(2,1)S(1)}, u32[]{:S(2)}, u32[]{:S(2)}) collective-permute-start(bf16[4,5,16,128]{3,2,1,0:T(8,128)(2,1)S(1)} %get-tuple-element.114), channel_id=1, source_target_pairs={{0,16},{32,48},{64,80},{96,112},{16,0},{48,32},{80,64},{112,96},{1... | collective-permute-start | bytes 245768 | tf_op jit(solution)/shard_map/ppermute | solution.py:62
  30.0 2.6 %collective-permute-start.7 = (bf16[4,5,16,128]{3,2,1,0:T(8,128)(2,1)S(1)}, bf16[4,5,16,128]{3,2,1,0:T(8,128)(2,1)S(1)}, u32[]{:S(2)}, u32[]{:S(2)}) collective-permute-start(bf16[4,5,16,128]{3,2,1,0:T(8,128)(2,1)S(1)} %get-tuple-element.115), channel_id=1, source_target_pairs={{16,32},{48,64},{80,96},{32,16},{64,48},{96,80},{17,33},{49,65},{8... | collective-permute-start | bytes 245768 | tf_op jit(solution)/shard_map/ppermute | solution.py:62
  33.8 20.8 %collective-permute-start.11 = (bf16[13,32,512]{2,1,0:T(8,128)(2,1)S(1)}, bf16[13,32,512]{2,1,0:T(8,128)(2,1)S(1)}, u32[]{:S(2)}, u32[]{:S(2)}) collective-permute-start(bf16[13,32,512]{2,1,0:T(8,128)(2,1)S(1)} %slice.23), channel_id=1, source_target_pairs={{0,4},{1,5},{2,6},{3,7},{4,8},{5,9},{6,10},{7,11},{8,12},{9,13},{1... | collective-permute-start | bytes 1277960 | tf_op jit(solution)/shard_map/ppermute | solution.py:51
  33.9 24.0 %collective-permute-start.12 = (bf16[14,32,512]{2,1,0:T(8,128)(2,1)S(1)}, bf16[14,32,512]{2,1,0:T(8,128)(2,1)S(1)}, u32[]{:S(2)}, u32[]{:S(2)}) collective-permute-start(bf16[14,32,512]{2,1,0:T(8,128)(2,1)S(1)} %slice.24), channel_id=1, source_target_pairs={{0,12},{1,13},{2,14},{3,15},{4,0},{5,1},{6,2},{7,3},{8,4},{9,5},{1... | collective-permute-start | bytes 1376264 | tf_op jit(solution)/shard_map/ppermute | solution.py:51
  46.7 19.8 %collective-permute-start.13 = (bf16[2,13,16,512]{3,2,1,0:T(8,128)(2,1)S(1)}, bf16[2,13,16,512]{3,2,1,0:T(8,128)(2,1)S(1)}, u32[]{:S(2)}, u32[]{:S(2)}) collective-permute-start(bf16[2,13,16,512]{3,2,1,0:T(8,128)(2,1)S(1)} %get-tuple-element.139), channel_id=1, source_target_pairs={{0,32},{16,48},{32,64},{48,80},{64,96},{80,112},{96,0},{112,16},{1... | collective-permute-start | bytes 1277960 | tf_op jit(solution)/shard_map/ppermute | solution.py:56
  53.3 13.3 %collective-permute-start.14 = (bf16[2,13,16,512]{3,2,1,0:T(8,128)(2,1)S(1)}, bf16[2,13,16,512]{3,2,1,0:T(8,128)(2,1)S(1)}, u32[]{:S(2)}, u32[]{:S(2)}) collective-permute-start(bf16[2,13,16,512]{3,2,1,0:T(8,128)(2,1)S(1)} %get-tuple-element.140), channel_id=1, source_target_pairs={{0,96},{16,112},{32,0},{48,16},{64,32},{80,48},{96,64},{112,80},{1... | collective-permute-start | bytes 1277960 | tf_op jit(solution)/shard_map/ppermute | solution.py:56
  54.6 11.9 %collective-permute-start.15 = (bf16[2,14,16,512]{3,2,1,0:T(8,128)(2,1)S(1)}, bf16[2,14,16,512]{3,2,1,0:T(8,128)(2,1)S(1)}, u32[]{:S(2)}, u32[]{:S(2)}) collective-permute-start(bf16[2,14,16,512]{3,2,1,0:T(8,128)(2,1)S(1)} %get-tuple-element.141), channel_id=1, source_target_pairs={{0,4},{1,5},{2,6},{3,7},{4,8},{5,9},{6,10},{7,11},{8,12},{9,13},{1... | collective-permute-start | bytes 1376264 | tf_op jit(solution)/shard_map/ppermute | solution.py:51
  54.6 11.9 %collective-permute-start.16 = (bf16[2,14,16,512]{3,2,1,0:T(8,128)(2,1)S(1)}, bf16[2,14,16,512]{3,2,1,0:T(8,128)(2,1)S(1)}, u32[]{:S(2)}, u32[]{:S(2)}) collective-permute-start(bf16[2,14,16,512]{3,2,1,0:T(8,128)(2,1)S(1)} %get-tuple-element.142), channel_id=1, source_target_pairs={{0,12},{1,13},{2,14},{3,15},{4,0},{5,1},{6,2},{7,3},{8,4},{9,5},{1... | collective-permute-start | bytes 1376264 | tf_op jit(solution)/shard_map/ppermute | solution.py:51
  66.6 11.9 %collective-permute-start.21 = (f32[2,4,8,16,512]{4,3,2,1,0:T(8,128)S(1)}, f32[2,4,8,16,512]{4,3,2,1,0:T(8,128)S(1)}, u32[]{:S(2)}, u32[]{:S(2)}) collective-permute-start(f32[2,4,8,16,512]{4,3,2,1,0:T(8,128)S(1)} %get-tuple-element.156), channel_id=1, source_target_pairs={{0,1},{1,0},{2,3},{3,2},{4,5},{5,4},{6,7},{7,6},{8,9},{9,8},{10,11... | collective-permute-start | bytes 6291464 | tf_op jit(solution)/shard_map/ppermute | solution.py:43
  66.8 11.6 %collective-permute-start.19 = (bf16[14,16,512]{2,1,0:T(8,128)(2,1)S(1)}, bf16[14,16,512]{2,1,0:T(8,128)(2,1)S(1)}, u32[]{:S(2)}, u32[]{:S(2)}) collective-permute-start(bf16[14,16,512]{2,1,0:T(8,128)(2,1)S(1)} %get-tuple-element.154), channel_id=1, source_target_pairs={{0,4},{1,5},{2,6},{3,7},{4,8},{5,9},{6,10},{7,11},{8,12},{9,13},{1... | collective-permute-start | bytes 688136 | tf_op jit(solution)/shard_map/ppermute | solution.py:51
  66.9 11.5 %collective-permute-start.20 = (bf16[14,16,512]{2,1,0:T(8,128)(2,1)S(1)}, bf16[14,16,512]{2,1,0:T(8,128)(2,1)S(1)}, u32[]{:S(2)}, u32[]{:S(2)}) collective-permute-start(bf16[14,16,512]{2,1,0:T(8,128)(2,1)S(1)} %get-tuple-element.155), channel_id=1, source_target_pairs={{0,12},{1,13},{2,14},{3,15},{4,0},{5,1},{6,2},{7,3},{8,4},{9,5},{1... | collective-permute-start | bytes 688136 | tf_op jit(solution)/shard_map/ppermute | solution.py:51
  70.1 8.3 %collective-permute-start.17 = (bf16[13,16,512]{2,1,0:T(8,128)(2,1)S(1)}, bf16[13,16,512]{2,1,0:T(8,128)(2,1)S(1)}, u32[]{:S(2)}, u32[]{:S(2)}) collective-permute-start(bf16[13,16,512]{2,1,0:T(8,128)(2,1)S(1)} %get-tuple-element.152), channel_id=1, source_target_pairs={{0,32},{16,48},{32,64},{48,80},{64,96},{80,112},{96,0},{112,16},{1... | collective-permute-start | bytes 638984 | tf_op jit(solution)/shard_map/ppermute | solution.py:56
  70.8 7.6 %collective-permute-start.18 = (bf16[13,16,512]{2,1,0:T(8,128)(2,1)S(1)}, bf16[13,16,512]{2,1,0:T(8,128)(2,1)S(1)}, u32[]{:S(2)}, u32[]{:S(2)}) collective-permute-start(bf16[13,16,512]{2,1,0:T(8,128)(2,1)S(1)} %get-tuple-element.153), channel_id=1, source_target_pairs={{0,96},{16,112},{32,0},{48,16},{64,32},{80,48},{96,64},{112,80},{1... | collective-permute-start | bytes 638984 | tf_op jit(solution)/shard_map/ppermute | solution.py:56
  78.7 5.5 %collective-permute-start.24 = (bf16[13,8,512]{2,1,0:T(8,128)(2,1)S(1)}, bf16[13,8,512]{2,1,0:T(8,128)(2,1)S(1)}, u32[]{:S(2)}, u32[]{:S(2)}) collective-permute-start(bf16[13,8,512]{2,1,0:T(8,128)(2,1)S(1)} %get-tuple-element.167), channel_id=1, source_target_pairs={{0,12},{1,13},{2,14},{3,15},{4,0},{5,1},{6,2},{7,3},{8,4},{9,5},{1... | collective-permute-start | bytes 319496 | tf_op jit(solution)/shard_map/ppermute | solution.py:51
  80.2 6.4 %collective-permute-start.23 = (bf16[13,8,512]{2,1,0:T(8,128)(2,1)S(1)}, bf16[13,8,512]{2,1,0:T(8,128)(2,1)S(1)}, u32[]{:S(2)}, u32[]{:S(2)}) collective-permute-start(bf16[13,8,512]{2,1,0:T(8,128)(2,1)S(1)} %get-tuple-element.166), channel_id=1, source_target_pairs={{0,8},{1,9},{2,10},{3,11},{4,12},{5,13},{6,14},{7,15},{8,0},{9,1},... | collective-permute-start | bytes 319496 | tf_op jit(solution)/shard_map/ppermute | solution.py:51
  80.2 7.3 %collective-permute-start.22 = (bf16[13,8,512]{2,1,0:T(8,128)(2,1)S(1)}, bf16[13,8,512]{2,1,0:T(8,128)(2,1)S(1)}, u32[]{:S(2)}, u32[]{:S(2)}) collective-permute-start(bf16[13,8,512]{2,1,0:T(8,128)(2,1)S(1)} %get-tuple-element.165), channel_id=1, source_target_pairs={{0,4},{1,5},{2,6},{3,7},{4,8},{5,9},{6,10},{7,11},{8,12},{9,13},{1... | collective-permute-start | bytes 319496 | tf_op jit(solution)/shard_map/ppermute | solution.py:51
  81.3 6.5 %collective-permute-start.27 = (bf16[14,8,512]{2,1,0:T(8,128)(2,1)S(1)}, bf16[14,8,512]{2,1,0:T(8,128)(2,1)S(1)}, u32[]{:S(2)}, u32[]{:S(2)}) collective-permute-start(bf16[14,8,512]{2,1,0:T(8,128)(2,1)S(1)} %get-tuple-element.171), channel_id=1, source_target_pairs={{0,96},{16,112},{32,0},{48,16},{64,32},{80,48},{96,64},{112,80},{1... | collective-permute-start | bytes 344072 | tf_op jit(solution)/shard_map/ppermute | solution.py:56
  84.3 6.4 %collective-permute-start.26 = (bf16[14,8,512]{2,1,0:T(8,128)(2,1)S(1)}, bf16[14,8,512]{2,1,0:T(8,128)(2,1)S(1)}, u32[]{:S(2)}, u32[]{:S(2)}) collective-permute-start(bf16[14,8,512]{2,1,0:T(8,128)(2,1)S(1)} %get-tuple-element.170), channel_id=1, source_target_pairs={{0,64},{16,80},{32,96},{48,112},{64,0},{80,16},{96,32},{112,48},{1... | collective-permute-start | bytes 344072 | tf_op jit(solution)/shard_map/ppermute | solution.py:56
  84.3 7.2 %collective-permute-start.25 = (bf16[14,8,512]{2,1,0:T(8,128)(2,1)S(1)}, bf16[14,8,512]{2,1,0:T(8,128)(2,1)S(1)}, u32[]{:S(2)}, u32[]{:S(2)}) collective-permute-start(bf16[14,8,512]{2,1,0:T(8,128)(2,1)S(1)} %get-tuple-element.169), channel_id=1, source_target_pairs={{0,32},{16,48},{32,64},{48,80},{64,96},{80,112},{96,0},{112,16},{1... | collective-permute-start | bytes 344072 | tf_op jit(solution)/shard_map/ppermute | solution.py:56
  91.6 23.6 %copy-start = (bf16[4,8,16,512]{3,2,1,0:T(8,128)(2,1)S(1)}, bf16[4,8,16,512]{3,2,1,0:T(8,128)(2,1)}, u32[]{:S(2)}) copy-start(bf16[4,8,16,512]{3,2,1,0:T(8,128)(2,1)} %pre.1) | copy-start | bytes 1572868
  91.6 9.9 %collective-permute-start.28 = (bf16[27,8,512]{2,1,0:T(8,128)(2,1)S(1)}, bf16[27,8,512]{2,1,0:T(8,128)(2,1)S(1)}, u32[]{:S(2)}, u32[]{:S(2)}) collective-permute-start(bf16[27,8,512]{2,1,0:T(8,128)(2,1)S(1)} %pad_maximum_fusion), channel_id=1, source_target_pairs={{0,16},{16,0},{32,48},{48,32},{64,80},{80,64},{96,112},{112,96},{1... | collective-permute-start | bytes 663560 | tf_op jit(solution)/shard_map/ppermute | solution.py:468
  101.5 13.7 %collective-permute-start.29 = (bf16[4,8,16,512]{3,2,1,0:T(8,128)(2,1)S(1)}, bf16[4,8,16,512]{3,2,1,0:T(8,128)(2,1)S(1)}, u32[]{:S(2)}, u32[]{:S(2)}) collective-permute-start(bf16[4,8,16,512]{3,2,1,0:T(8,128)(2,1)S(1)} %fusion.4), channel_id=1, source_target_pairs={{0,2},{1,3},{2,0},{3,1},{4,6},{5,7},{6,4},{7,5},{8,10},{9,11},{10,... | collective-permute-start | bytes 1572872 | tf_op jit(solution)/shard_map/ppermute | solution.py:43
  101.6 7.2 %collective-permute-start.33 = (f32[14,8,512]{2,1,0:T(8,128)S(1)}, f32[14,8,512]{2,1,0:T(8,128)S(1)}, u32[]{:S(2)}, u32[]{:S(2)}) collective-permute-start(f32[14,8,512]{2,1,0:T(8,128)S(1)} %get-tuple-element.177.refs_1_), channel_id=1, source_target_pairs={{0,96},{16,112},{32,0},{48,16},{64,32},{80,48},{96,64},{112,80},{1... | collective-permute-start | bytes 688136 | tf_op jit(solution)/shard_map/ppermute | solution.py:56
  102.3 9.6 %collective-permute-start.30 = (f32[13,8,512]{2,1,0:T(8,128)S(1)}, f32[13,8,512]{2,1,0:T(8,128)S(1)}, u32[]{:S(2)}, u32[]{:S(2)}) collective-permute-start(f32[13,8,512]{2,1,0:T(8,128)S(1)} %get-tuple-element.176.refs_0_), channel_id=1, source_target_pairs={{0,32},{16,48},{32,64},{48,80},{64,96},{80,112},{96,0},{112,16},{1... | collective-permute-start | bytes 638984 | tf_op jit(solution)/shard_map/ppermute | solution.py:56
  108.8 11.4 %collective-permute-start.35 = (f32[14,8,512]{2,1,0:T(8,128)S(1)}, f32[14,8,512]{2,1,0:T(8,128)S(1)}, u32[]{:S(2)}, u32[]{:S(2)}) collective-permute-start(f32[14,8,512]{2,1,0:T(8,128)S(1)} %collective-permute-done.33.refs_5_), channel_id=1, source_target_pairs={{0,96},{16,112},{32,0},{48,16},{64,32},{80,48},{96,64},{112,80},{1... | collective-permute-start | bytes 688136 | tf_op jit(solution)/shard_map/ppermute | solution.py:56
  111.9 8.3 %collective-permute-start.34 = (f32[13,8,512]{2,1,0:T(8,128)S(1)}, f32[13,8,512]{2,1,0:T(8,128)S(1)}, u32[]{:S(2)}, u32[]{:S(2)}) collective-permute-start(f32[13,8,512]{2,1,0:T(8,128)S(1)} %collective-permute-done.30.refs_2_), channel_id=1, source_target_pairs={{0,32},{16,48},{32,64},{48,80},{64,96},{80,112},{96,0},{112,16},{1... | collective-permute-start | bytes 638984 | tf_op jit(solution)/shard_map/ppermute | solution.py:56
  111.9 8.3 %collective-permute-start.31 = (bf16[14,8,512]{2,1,0:T(8,128)(2,1)S(1)}, bf16[14,8,512]{2,1,0:T(8,128)(2,1)S(1)}, u32[]{:S(2)}, u32[]{:S(2)}) collective-permute-start(bf16[14,8,512]{2,1,0:T(8,128)(2,1)S(1)} %get-tuple-element.186), channel_id=1, source_target_pairs={{0,32},{16,48},{32,64},{48,80},{64,96},{80,112},{96,0},{112,16},{1... | collective-permute-start | bytes 344072 | tf_op jit(solution)/shard_map/ppermute | solution.py:56
  111.9 5.5 %collective-permute-start.32 = (bf16[13,8,512]{2,1,0:T(8,128)(2,1)S(1)}, bf16[13,8,512]{2,1,0:T(8,128)(2,1)S(1)}, u32[]{:S(2)}, u32[]{:S(2)}) collective-permute-start(bf16[13,8,512]{2,1,0:T(8,128)(2,1)S(1)} %get-tuple-element.184), channel_id=1, source_target_pairs={{0,96},{16,112},{32,0},{48,16},{64,32},{80,48},{96,64},{112,80},{1... | collective-permute-start | bytes 319496 | tf_op jit(solution)/shard_map/ppermute | solution.py:56

commit v12 on v11

--- a/solution.py
+++ b/solution.py
@@ -57,9 +57,12 @@
 
 
 def swap_x(block, first):
-    count = lax.axis_size("gx")
-    pairs = [(g, g + 1) for g in range(first, count - 1, 2)]
-    return lax.ppermute(block, "gx", pairs + [(t, s) for s, t in pairs])
+    nx, ny = lax.axis_size("gx"), lax.axis_size("gy")
+    pairs = []
+    for g in range(first, nx - 1, 2):
+        for h in range(ny):
+            pairs += [(g * ny + h, (g + 1) * ny + (h ^ 2)), ((g + 1) * ny + h, g * ny + (h ^ 2))]
+    return lax.ppermute(block, ("gx", "gy"), pairs)
 
 
 def zero_at(value, z, edge):
@@ -78,70 +81,72 @@
     return got.astype(BF16).reshape(block.shape[:-1] + (q,))
 
 
-def own_kernel(cot, *quarters):
+def side_kernel(cot, extra, even, odd):
+    rows, width = cot.shape[:2]
+    is_odd = lax.rem(lax.axis_index("gx"), 2) == 1
+
+    def put(out, upper):
+        out[0:rows] = jnp.where(upper, cot[:, width - 1], cot[:, 0])
+        out[rows] = jnp.where(upper, extra[width - 1], extra[0])
+
+    put(even, jnp.logical_not(is_odd))
+    put(odd, is_odd)
+
+
+def sides(cot, extra):
+    rows, width, depth, chan = cot.shape
+    return pl.pallas_call(
+        side_kernel,
+        out_shape=[jax.ShapeDtypeStruct((rows + 1, depth, chan), BF16)] * 2,
+        in_specs=[VMEM] * 2,
+        out_specs=[VMEM] * 2,
+        compiler_params=params(),
+        cost_estimate=small_cost(),
+    )(cot, extra)
+
+
+def pick_kernel(cot, extra, even, odd, *quarters):
+    rows, width = cot.shape[:2]
+    is_odd = lax.rem(lax.axis_index("gx"), 2) == 1
+    low = jnp.where(is_odd, even[...], odd[...])
+    high = jnp.where(is_odd, odd[...], even[...])
     for k, out in enumerate(quarters):
-        out[...] = pick(cot[...], k)
-
-
-def extra_kernel(extra, q0, q1, q2, q3, *quarters):
-    for k, (own, out) in enumerate(zip((q0, q1, q2, q3), quarters)):
-        rows = own.shape[0]
-        out[0:rows] = own[...]
-        out[rows] = pick(extra[...], k)
-
-
-def quarters_of(kernel, rows, *ins):
-    width, depth, chan = ins[0].shape[-3:]
-    quarter = jax.ShapeDtypeStruct((rows, width, depth, chan // QUAD), BF16)
-    return pl.pallas_call(
-        kernel,
+        out[0:rows, 1:width + 1] = pick(cot[...], k)
+        out[rows, 1:width + 1] = pick(extra[...], k)
+        out[:, 0] = pick(low, k)
+        out[:, width + 1] = pick(high, k)
+
+
+def pick_channels(cot, *rims):
+    rows, width, depth, chan = cot.shape
+    quarter = jax.ShapeDtypeStruct((rows + 1, width + 2, depth, chan // QUAD), BF16)
+    return pl.pallas_call(
+        pick_kernel,
         out_shape=[quarter] * QUAD,
-        in_specs=[VMEM] * len(ins),
+        in_specs=[VMEM] * 4,
         out_specs=[VMEM] * QUAD,
         compiler_params=params(),
-        cost_estimate=pl.CostEstimate(
-            flops=1000, bytes_accessed=40_000_000 if kernel is own_kernel else 1000, transcendentals=0
-        ),
-    )(*ins)
-
-
-def side_kernel(p0, p1, p2, p3, even, odd):
-    width = p0.shape[1]
-    is_odd = lax.rem(lax.axis_index("gx"), 2) == 1
+        cost_estimate=small_cost(),
+    )(cot, *rims)
+
+
+def turn_kernel(p0, p1, p2, p3, held, out):
+    j, x = quad_place(), x_place()
+    last = held.shape[0] - 1
     for k, p in enumerate((p0, p1, p2, p3)):
-        first, last = p[:, 0], p[:, width - 1]
-        even[k] = jnp.where(is_odd, first, last)
-        odd[k] = jnp.where(is_odd, last, first)
-
-
-def sides(quarters):
-    rows, _, depth, q = quarters[0].shape
-    return pl.pallas_call(
-        side_kernel,
-        out_shape=[jax.ShapeDtypeStruct((QUAD, rows, depth, q), BF16)] * 2,
-        in_specs=[VMEM] * QUAD,
-        out_specs=[VMEM] * 2,
-        compiler_params=params(),
-        cost_estimate=small_cost(),
-    )(*quarters)
-
-
-def turn_kernel(p0, p1, p2, p3, even, odd, held, out):
-    j, x = quad_place(), x_place()
-    is_odd = lax.rem(lax.axis_index("gx"), 2) == 1
-    for k, p in enumerate((p0, p1, p2, p3)):
-        rows, width = p.shape[0] - 1, p.shape[1]
-        low = jnp.where(is_odd, even[k], odd[k])
-        high = jnp.where(is_odd, odd[k], even[k])
-
-        def put(at, part):
-            held[at, 1:width + 1] = p[part]
-            held[at, 0] = low[part]
-            held[at, width + 1] = high[part]
-
-        put(pl.ds(1 + (j ^ k) * rows, rows), slice(0, rows))
-        pl.when((j ^ k) == 0)(functools.partial(put, 0, rows))
-        pl.when((j ^ k) == QUAD - 1)(functools.partial(put, held.shape[0] - 1, rows))
+        rows, width = p.shape[0] - 1, p.shape[1] - 2
+
+        def put_own(at, part):
+            held[at, 1:width + 1] = p[part, 1:width + 1]
+
+        def put_rims(at, part):
+            held[at, 0] = p[part, 0]
+            held[at, width + 1] = p[part, width + 1]
+
+        for place, put in ((j ^ k, put_own), (j ^ k ^ 2, put_rims)):
+            put(pl.ds(1 + place * rows, rows), slice(0, rows))
+            pl.when(place == QUAD - 1)(functools.partial(put, 0, rows))
+            pl.when(place == 0)(functools.partial(put, last, rows))
 
     tall, width, depth, q = held.shape
     width -= 2
@@ -167,9 +172,8 @@
             out[at:at + q] = v.astype(BF16)
 
 
-def turn(quarters, even, odd):
+def turn(quarters):
     rows, width, depth, q = quarters[0].shape
-    width += 2
     tall = QUAD * (rows - 1) + 2
     return pl.pallas_call(
         turn_kernel,
@@ -177,11 +181,11 @@
             jax.ShapeDtypeStruct((tall, width, depth, q), BF16),
             jax.ShapeDtypeStruct((9 * q, tall * (width - 2) * depth), BF16),
         ],
-        in_specs=[VMEM] * (QUAD + 2),
+        in_specs=[VMEM] * QUAD,
         out_specs=[VMEM] * 2,
         compiler_params=params(),
         cost_estimate=small_cost(),
-    )(*quarters, even, odd)
+    )(*quarters)
 
 
 def run_copies(pairs, sem):
@@ -416,27 +420,24 @@
     barrier = lax.optimization_barrier
 
     count = lax.axis_size("gy")
-    pairs = [(g, g + 1) for g in range(QUAD - 1, count - 1, QUAD)]
-    pairs = pairs + [(t, s) for s, t in pairs]
+    pairs = [(g, g + QUAD) for g in range(QUAD - 1, count - QUAD, QUAD)]
+    pairs = pairs + [(g + QUAD, g) for g in range(0, count - QUAD, QUAD)]
     extra = lax.ppermute(jnp.where(j == 0, cot[0], cot[rows - 1]), "gy", pairs)
     act = jax.nn.silu(pre_act.astype(F32)).astype(BF16)
     far = swap(act, 2)
     near = swap(act, 1)
-    own_quarters = quarters_of(own_kernel, rows, cot)
-    extra, near, own_quarters = barrier((extra, near, own_quarters))
-    quarters = quarters_of(extra_kernel, rows + 1, extra, *own_quarters)
-    quarters, weight = barrier((quarters, weight))
+    extra, near, weight = barrier((extra, near, weight))
     above = along_y(weight, -1, True)
     below = along_y(weight, 1, True)
+    even, odd = sides(cot, extra)
+    quarters = pick_channels(cot, extra, swap_x(even, 0), swap_x(odd, 1))
     quarters = [quarters[0]] + [swap(quarters[k], k) for k in (1, 2, 3)]
     quarters, far = barrier((quarters, far))
     acts = [act, near, far, swap(far, 1)]
-    even, odd = sides(quarters)
-    even, odd = swap_x(even, 0), swap_x(odd, 1)
-    even, odd, above, below = barrier((even, odd, above, below))
+    quarters, above, below = barrier((quarters, above, below))
     taps = XTAPS
     parts = [weight, above, along_y(below[:taps], 1, True), along_y(above[taps:], -1, True), below]
-    held, turned = turn(quarters, even, odd)
+    held, turned = turn(quarters)
 
     terms = weight_terms(norm, acts, turned)
     held, terms = barrier((held, terms))

time: 123 us -> 125 us (1.016)
  waiting for transfers between devices: 40.4 us -> 47.6 us
  starting transfers between devices: 53.9 us -> 48.8 us
    ppermute x1, waiting for transfers between devices: 0.01 us -> 7.03 us  [body(): extra = lax.ppermute(jnp.where(j == 0, cot[0], cot[rows - 1]), 'gy', pairs)]
    ppermute x11, starting transfers between devices: 20.8 us -> 14.8 us  [along_y(): lax.ppermute(block, 'gy', [(s, t) for s, t in pairs if 0 <= t < count])]
    ppermute x1, waiting for transfers between devices: 9.09 us -> 4.44 us  [body(): other = lax.ppermute(mine, 'gx', [(g, g ^ 1) for g in range(count)])]
    ppermute x2, starting transfers between devices: 4.06 us -> 0.75 us  [swap_x(): return lax.ppermute(block, ('gx', 'gy'), pairs)]
    ppermute x8, starting transfers between devices: 4.36 us -> 7.64 us  [swap(): return lax.ppermute(block, 'gy', [(g, g ^ k) for g in range(count)])]
    ppermute x2, waiting for transfers between devices: 1.96 us -> 4.97 us  [swap_x(): return lax.ppermute(block, ('gx', 'gy'), pairs)]
    ppermute x1, starting transfers between devices: 0.52 us -> 2.82 us  [body(): other = lax.ppermute(mine, 'gx', [(g, g ^ 1) for g in range(count)])]
    ppermute x13, starting transfers between devices: 23.5 us -> 21.5 us  [along_x(): lax.ppermute(block, 'gx', [(g, (g + 2 * step) % count) for g in range(cou...]
where the time goes in v12:
time: 125 us; the launch traced here: 123 us
  starting transfers between devices  48.8 us (39%)
  waiting for transfers between devices  47.6 us (38%)
  Pallas kernels  22.2 us (18%)
  other arithmetic  2.91 us (2%)
    ppermute x13, starting transfers between devices, along_x(): lax.ppermute(block, 'gx', [(g, (g + 2 * step) % count) for g in range(cou...  21.5 us
    ppermute x13, waiting for transfers between devices, along_x(): lax.ppermute(block, 'gx', [(g, (g + 2 * step) % count) for g in range(cou...  18.2 us
    ppermute x11, starting transfers between devices, along_y(): lax.ppermute(block, 'gy', [(s, t) for s, t in pairs if 0 <= t < count])  14.8 us
    ppermute x8, waiting for transfers between devices, swap(): return lax.ppermute(block, 'gy', [(g, g ^ k) for g in range(count)])  9.55 us
    pallas_call x1, Pallas kernels, input_terms(): pl.pallas_call(input_kernel, out_shape=[jax.ShapeDtypeStruct((2,) + block...  8.65 us
    pallas_call x1, Pallas kernels, weight_terms(): pl.pallas_call(functools.partial(weight_kernel, norm), out_shape=shapes,...  7.66 us
    ppermute x8, starting transfers between devices, swap(): return lax.ppermute(block, 'gy', [(g, g ^ k) for g in range(count)])  7.64 us
    ppermute x1, waiting for transfers between devices, body(): extra = lax.ppermute(jnp.where(j == 0, cot[0], cot[rows - 1]), 'gy', pairs)  7.03 us
  transfers between devices with their start and end apart: 36, of which 15 were waited for; matrix products, arithmetic and copies ran while one was open for 1% of the time, Pallas kernels for 17%

profile of v12, /device:TPU:0, one launch (start us, length us, event | category | flops | bytes accessed | tf_op | source)
XLA Modules:
  0.0 123.4 jit_solution(2967885497698435262)
XLA Ops:
  0.6 1.4 %fusion.3.own_act = bf16[4,8,16,512]{3,2,1,0:T(8,128)(2,1)S(1)} fusion(bf16[4,8,16,512]{3,2,1,0:T(8,128)(2,1)} %pre.1), kind=kLoop, calls=%fused_computation.5 | loop fusion | flops 1572864 | bytes 1048576 | tf_op jit(solution)/shard_map/convert_element_type | solution.py:426
  2.1 2.1 %collective-permute-start.7 = (bf16[4,8,16,512]{3,2,1,0:T(8,128)(2,1)S(1)}, bf16[4,8,16,512]{3,2,1,0:T(8,128)(2,1)S(1)}, u32[]{:S(2)}, u32[]{:S(2)}) collective-permute-start(bf16[4,8,16,512]{3,2,1,0:T(8,128)(2,1)S(1)} %fusion.3.own_act), channel_id=1, source_target_pairs={{0,2},{1,3},{2,0},{3,1},{4,6},{5,7},{6,4},{7,5},{8,10},{9,11},{10,... | collective-permute-start | bytes 1572872 | tf_op jit(solution)/shard_map/ppermute | solution.py:43
  4.2 1.0 select_bitcast_fusion
  5.2 1.3 %collective-permute-start = (bf16[8,16,512]{2,1,0:T(8,128)(2,1)S(1)}, bf16[8,16,512]{2,1,0:T(8,128)(2,1)S(1)}, u32[]{:S(2)}, u32[]{:S(2)}) collective-permute-start(bf16[8,16,512]{2,1,0:T(8,128)(2,1)S(1)} %select_bitcast_fusion), channel_id=1, source_target_pairs={{3,7},{7,11},{11,15},{4,0},{8,4},{12,8},{19,23},{23,27},{27,31},{2... | collective-permute-start | bytes 393224 | tf_op jit(solution)/shard_map/ppermute | solution.py:425
  6.5 7.0 %collective-permute-done.extra = bf16[8,16,512]{2,1,0:T(8,128)(2,1)S(1)} collective-permute-done((bf16[8,16,512]{2,1,0:T(8,128)(2,1)S(1)}, bf16[8,16,512]{2,1,0:T(8,128)(2,1)S(1)}, u32[]{:S(2)}, u32[]{:S(2)}) %collective-permute-start) | collective-permute-done | bytes 131104 | tf_op jit(solution)/shard_map/ppermute | solution.py:425
  13.5 1.3 %collective-permute-start.8 = (bf16[27,32,512]{2,1,0:T(8,128)(2,1)}, bf16[27,32,512]{2,1,0:T(8,128)(2,1)S(1)}, u32[]{:S(2)}, u32[]{:S(2)}) collective-permute-start(bf16[27,32,512]{2,1,0:T(8,128)(2,1)} %own), channel_id=1, source_target_pairs={{0,12},{1,13},{2,14},{3,15},{4,0},{5,1},{6,2},{7,3},{8,4},{9,5},{1... | collective-permute-start | bytes 2654216 | tf_op jit(solution)/shard_map/ppermute | solution.py:51
  14.8 0.8 collective-permute-start.9
  15.5 1.0 copy-done
  16.7 0.7 collective-permute-start.3
  17.3 5.0 %collective-permute-done.2.even = bf16[5,16,512]{2,1,0:T(8,128)(2,1)S(1)} collective-permute-done((bf16[5,16,512]{2,1,0:T(8,128)(2,1)S(1)}, bf16[5,16,512]{2,1,0:T(8,128)(2,1)S(1)}, u32[]{:S(2)}, u32[]{:S(2)}) %collective-permute-start.2) | collective-permute-done | bytes 81952 | tf_op jit(solution)/shard_map/ppermute | solution.py:65
  22.3 1.0 shard_map.51
  23.4 0.6 collective-permute-start.5
  24.1 1.2 %collective-permute-start.6 = (bf16[5,10,16,128]{3,2,1,0:T(8,128)(2,1)S(1)}, bf16[5,10,16,128]{3,2,1,0:T(8,128)(2,1)S(1)}, u32[]{:S(2)}, u32[]{:S(2)}) collective-permute-start(bf16[5,10,16,128]{3,2,1,0:T(8,128)(2,1)S(1)} %get-tuple-element.89), channel_id=1, source_target_pairs={{0,3},{1,2},{2,1},{3,0},{4,7},{5,6},{6,5},{7,4},{8,11},{9,10},{10,... | collective-permute-start | bytes 614408 | tf_op jit(solution)/shard_map/ppermute | solution.py:43
  25.3 6.1 %collective-permute-done.5.p2 = bf16[5,10,16,128]{3,2,1,0:T(8,128)(2,1)S(1)} collective-permute-done((bf16[5,10,16,128]{3,2,1,0:T(8,128)(2,1)S(1)}, bf16[5,10,16,128]{3,2,1,0:T(8,128)(2,1)S(1)}, u32[]{:S(2)}, u32[]{:S(2)}) %collective-permute-start.5) | collective-permute-done | bytes 204832 | tf_op jit(solution)/shard_map/ppermute | solution.py:43
  31.4 3.4 %collective-permute-done.6.p3 = bf16[5,10,16,128]{3,2,1,0:T(8,128)(2,1)S(1)} collective-permute-done((bf16[5,10,16,128]{3,2,1,0:T(8,128)(2,1)S(1)}, bf16[5,10,16,128]{3,2,1,0:T(8,128)(2,1)S(1)}, u32[]{:S(2)}, u32[]{:S(2)}) %collective-permute-start.6) | collective-permute-done | bytes 204832 | tf_op jit(solution)/shard_map/ppermute | solution.py:43
  35.2 1.6 %collective-permute-start.11 = (bf16[13,32,512]{2,1,0:T(8,128)(2,1)S(1)}, bf16[13,32,512]{2,1,0:T(8,128)(2,1)S(1)}, u32[]{:S(2)}, u32[]{:S(2)}) collective-permute-start(bf16[13,32,512]{2,1,0:T(8,128)(2,1)S(1)} %slice.23), channel_id=1, source_target_pairs={{0,4},{1,5},{2,6},{3,7},{4,8},{5,9},{6,10},{7,11},{8,12},{9,13},{1... | collective-permute-start | bytes 1277960 | tf_op jit(solution)/shard_map/ppermute | solution.py:51
  36.9 1.7 %collective-permute-start.12 = (bf16[14,32,512]{2,1,0:T(8,128)(2,1)S(1)}, bf16[14,32,512]{2,1,0:T(8,128)(2,1)S(1)}, u32[]{:S(2)}, u32[]{:S(2)}) collective-permute-start(bf16[14,32,512]{2,1,0:T(8,128)(2,1)S(1)} %slice.24), channel_id=1, source_target_pairs={{0,12},{1,13},{2,14},{3,15},{4,0},{5,1},{6,2},{7,3},{8,4},{9,5},{1... | collective-permute-start | bytes 1376264 | tf_op jit(solution)/shard_map/ppermute | solution.py:51
  38.6 1.8 %shard_map.52 = (bf16[18,10,16,128]{3,2,1,0:T(8,128)(2,1)S(1)}, bf16[1152,2304]{1,0:T(8,128)(2,1)S(1)}) custom-call(bf16[5,10,16,128]{3,2,1,0:T(8,128)(2,1)S(1)} %get-tuple-element.95.p0, bf16[5,10,16,128]{3,2,1,0:T(8,128)(2,1)S(1)} %collective-permute-done.4.p1, bf16[5,10,16,128]{3,2,1,0:T(8,128)(2,1)S(1)} %collective-permute-done.5.p2, ...), custom_call_target="tpu_custom_call" | custom-call | flops 1000 | bytes 1000 | tf_op jit(solution)/shard_map/pallas_call | solution.py:178
  40.4 7.7 %shard_map.53 = (bf16[2,13,16,512]{3,2,1,0:T(8,128)(2,1)S(1)}, bf16[2,13,16,512]{3,2,1,0:T(8,128)(2,1)S(1)}, f32[13,16,512]{2,1,0:T(8,128)S(1)}, f32[13,16,512]{...) custom-call(bf16[4,8,16,512]{3,2,1,0:T(8,128)(2,1)S(1)} %fusion.3.ow, ...), custom_call_target="tpu_custom_call" | custom-call | flops 7247757312 | bytes 10000000 | tf_op jit(solution)/shard_map/pallas_call | solution.py:247
  48.1 4.9 %collective-permute-start.13 = (bf16[2,13,16,512]{3,2,1,0:T(8,128)(2,1)S(1)}, bf16[2,13,16,512]{3,2,1,0:T(8,128)(2,1)S(1)}, u32[]{:S(2)}, u32[]{:S(2)}) collective-permute-start(bf16[2,13,16,512]{3,2,1,0:T(8,128)(2,1)S(1)} %get-tuple-element.119), channel_id=1, source_target_pairs={{0,32},{16,48},{32,64},{48,80},{64,96},{80,112},{96,0},{112,16},{1... | collective-permute-start | bytes 1277960 | tf_op jit(solution)/shard_map/ppermute | solution.py:56
  53.0 1.4 %collective-permute-start.14 = (bf16[2,13,16,512]{3,2,1,0:T(8,128)(2,1)S(1)}, bf16[2,13,16,512]{3,2,1,0:T(8,128)(2,1)S(1)}, u32[]{:S(2)}, u32[]{:S(2)}) collective-permute-start(bf16[2,13,16,512]{3,2,1,0:T(8,128)(2,1)S(1)} %get-tuple-element.120), channel_id=1, source_target_pairs={{0,96},{16,112},{32,0},{48,16},{64,32},{80,48},{96,64},{112,80},{1... | collective-permute-start | bytes 1277960 | tf_op jit(solution)/shard_map/ppermute | solution.py:56
  54.8 2.8 %collective-permute-start.16 = (bf16[2,14,16,512]{3,2,1,0:T(8,128)(2,1)S(1)}, bf16[2,14,16,512]{3,2,1,0:T(8,128)(2,1)S(1)}, u32[]{:S(2)}, u32[]{:S(2)}) collective-permute-start(bf16[2,14,16,512]{3,2,1,0:T(8,128)(2,1)S(1)} %get-tuple-element.122), channel_id=1, source_target_pairs={{0,12},{1,13},{2,14},{3,15},{4,0},{5,1},{6,2},{7,3},{8,4},{9,5},{1... | collective-permute-start | bytes 1376264 | tf_op jit(solution)/shard_map/ppermute | solution.py:51
  57.6 8.6 %shard_map.54 = (f32[2,4,8,16,512]{4,3,2,1,0:T(8,128)S(1)}, f32[4,8,16,512]{3,2,1,0:T(8,128)S(1)}, f32[4,8,16,512]{3,2,1,0:T(8,128)S(1)}) custom-call(bf16[18,10,16,128]{3,2,1,0:T(8,128)(2,1)S(1)} %get-tuple-element.113.held, bf16[27,32,512]{2,1,0:T(8,128)(2,1)S(1)} %copy-done.2, bf16[27,32,512]{2,1,0:T(8,128)(2,1)S(1)} %collective-permute-done.8.above, ...), custom_call_target="tpu_custom_call" | custom-call | flops 10192158720 | bytes 10000000 | tf_op jit(solution)/shard_map/pallas_call | solution.py:309
  66.3 1.0 collective-permute-done.15.refs_4_.refs_6_
  67.5 0.6 collective-permute-start.19
  68.1 2.7 %collective-permute-start.20 = (bf16[14,16,512]{2,1,0:T(8,128)(2,1)S(1)}, bf16[14,16,512]{2,1,0:T(8,128)(2,1)S(1)}, u32[]{:S(2)}, u32[]{:S(2)}) collective-permute-start(bf16[14,16,512]{2,1,0:T(8,128)(2,1)S(1)} %get-tuple-element.135), channel_id=1, source_target_pairs={{0,12},{1,13},{2,14},{3,15},{4,0},{5,1},{6,2},{7,3},{8,4},{9,5},{1... | collective-permute-start | bytes 688136 | tf_op jit(solution)/shard_map/ppermute | solution.py:51
  71.2 2.8 %collective-permute-start.18 = (bf16[13,16,512]{2,1,0:T(8,128)(2,1)S(1)}, bf16[13,16,512]{2,1,0:T(8,128)(2,1)S(1)}, u32[]{:S(2)}, u32[]{:S(2)}) collective-permute-start(bf16[13,16,512]{2,1,0:T(8,128)(2,1)S(1)} %get-tuple-element.133), channel_id=1, source_target_pairs={{0,96},{16,112},{32,0},{48,16},{64,32},{80,48},{96,64},{112,80},{1... | collective-permute-start | bytes 638984 | tf_op jit(solution)/shard_map/ppermute | solution.py:56
  74.0 5.2 %collective-permute-done.17.refs_3_ = bf16[13,16,512]{2,1,0:T(8,128)(2,1)S(1)} collective-permute-done((bf16[13,16,512]{2,1,0:T(8,128)(2,1)S(1)}, bf16[13,16,512]{2,1,0:T(8,128)(2,1)S(1)}, u32[]{:S(2)}, u32[]{:S(2)}) %collective-permute-start.17) | collective-permute-done | bytes 213024 | tf_op jit(solution)/shard_map/ppermute | solution.py:56
  79.5 1.7 %collective-permute-start.24 = (bf16[13,8,512]{2,1,0:T(8,128)(2,1)S(1)}, bf16[13,8,512]{2,1,0:T(8,128)(2,1)S(1)}, u32[]{:S(2)}, u32[]{:S(2)}) collective-permute-start(bf16[13,8,512]{2,1,0:T(8,128)(2,1)S(1)} %get-tuple-element.147), channel_id=1, source_target_pairs={{0,12},{1,13},{2,14},{3,15},{4,0},{5,1},{6,2},{7,3},{8,4},{9,5},{1... | collective-permute-start | bytes 319496 | tf_op jit(solution)/shard_map/ppermute | solution.py:51
  81.2 1.1 collective-permute-start.22
  82.3 2.9 %collective-permute-start.27 = (bf16[14,8,512]{2,1,0:T(8,128)(2,1)S(1)}, bf16[14,8,512]{2,1,0:T(8,128)(2,1)S(1)}, u32[]{:S(2)}, u32[]{:S(2)}) collective-permute-start(bf16[14,8,512]{2,1,0:T(8,128)(2,1)S(1)} %get-tuple-element.151), channel_id=1, source_target_pairs={{0,96},{16,112},{32,0},{48,16},{64,32},{80,48},{96,64},{112,80},{1... | collective-permute-start | bytes 344072 | tf_op jit(solution)/shard_map/ppermute | solution.py:56
  85.3 0.9 collective-permute-start.25
  86.2 1.5 %collective-permute-done.23 = bf16[13,8,512]{2,1,0:T(8,128)(2,1)S(1)} collective-permute-done((bf16[13,8,512]{2,1,0:T(8,128)(2,1)S(1)}, bf16[13,8,512]{2,1,0:T(8,128)(2,1)S(1)}, u32[]{:S(2)}, u32[]{:S(2)}) %collective-permute-start.23) | collective-permute-done | bytes 106528 | tf_op jit(solution)/shard_map/ppermute | solution.py:51
  87.6 0.9 collective-permute-done.22
  88.9 2.8 %collective-permute-done.26 = bf16[14,8,512]{2,1,0:T(8,128)(2,1)S(1)} collective-permute-done((bf16[14,8,512]{2,1,0:T(8,128)(2,1)S(1)}, bf16[14,8,512]{2,1,0:T(8,128)(2,1)S(1)}, u32[]{:S(2)}, u32[]{:S(2)}) %collective-permute-start.26) | collective-permute-done | bytes 114720 | tf_op jit(solution)/shard_map/ppermute | solution.py:56
  91.7 0.8 collective-permute-done.25
  92.6 2.8 %collective-permute-start.28 = (bf16[27,8,512]{2,1,0:T(8,128)(2,1)S(1)}, bf16[27,8,512]{2,1,0:T(8,128)(2,1)S(1)}, u32[]{:S(2)}, u32[]{:S(2)}) collective-permute-start(bf16[27,8,512]{2,1,0:T(8,128)(2,1)S(1)} %pad_maximum_fusion), channel_id=1, source_target_pairs={{0,16},{16,0},{32,48},{48,32},{64,80},{80,64},{96,112},{112,96},{1... | collective-permute-start | bytes 663560 | tf_op jit(solution)/shard_map/ppermute | solution.py:469
  95.7 4.4 %collective-permute-done.28 = bf16[27,8,512]{2,1,0:T(8,128)(2,1)S(1)} collective-permute-done((bf16[27,8,512]{2,1,0:T(8,128)(2,1)S(1)}, bf16[27,8,512]{2,1,0:T(8,128)(2,1)S(1)}, u32[]{:S(2)}, u32[]{:S(2)}) %collective-permute-start.28) | collective-permute-done | bytes 221216 | tf_op jit(solution)/shard_map/ppermute | solution.py:469
  100.2 3.2 %collective-permute-start.29 = (bf16[4,8,16,512]{3,2,1,0:T(8,128)(2,1)S(1)}, bf16[4,8,16,512]{3,2,1,0:T(8,128)(2,1)S(1)}, u32[]{:S(2)}, u32[]{:S(2)}) collective-permute-start(bf16[4,8,16,512]{3,2,1,0:T(8,128)(2,1)S(1)} %fusion.4), channel_id=1, source_target_pairs={{0,2},{1,3},{2,0},{3,1},{4,6},{5,7},{6,4},{7,5},{8,10},{9,11},{10,... | collective-permute-start | bytes 1572872 | tf_op jit(solution)/shard_map/ppermute | solution.py:43
  103.5 0.6 collective-permute-start.33
  104.2 1.5 %collective-permute-start.30 = (f32[13,8,512]{2,1,0:T(8,128)S(1)}, f32[13,8,512]{2,1,0:T(8,128)S(1)}, u32[]{:S(2)}, u32[]{:S(2)}) collective-permute-start(f32[13,8,512]{2,1,0:T(8,128)S(1)} %get-tuple-element.156.refs_0_), channel_id=1, source_target_pairs={{0,32},{16,48},{32,64},{48,80},{64,96},{80,112},{96,0},{112,16},{1... | collective-permute-start | bytes 638984 | tf_op jit(solution)/shard_map/ppermute | solution.py:56
  105.7 5.3 %collective-permute-done.33.refs_5_ = f32[14,8,512]{2,1,0:T(8,128)S(1)} collective-permute-done((f32[14,8,512]{2,1,0:T(8,128)S(1)}, f32[14,8,512]{2,1,0:T(8,128)S(1)}, u32[]{:S(2)}, u32[]{:S(2)}) %collective-permute-start.33) | collective-permute-done | bytes 229408 | tf_op jit(solution)/shard_map/ppermute | solution.py:56
  111.1 2.8 %collective-permute-start.35 = (f32[14,8,512]{2,1,0:T(8,128)S(1)}, f32[14,8,512]{2,1,0:T(8,128)S(1)}, u32[]{:S(2)}, u32[]{:S(2)}) collective-permute-start(f32[14,8,512]{2,1,0:T(8,128)S(1)} %collective-permute-done.33.refs_5_), channel_id=1, source_target_pairs={{0,96},{16,112},{32,0},{48,16},{64,32},{80,48},{96,64},{112,80},{1... | collective-permute-start | bytes 688136 | tf_op jit(solution)/shard_map/ppermute | solution.py:56
  113.8 3.3 %collective-permute-start.32 = (bf16[13,8,512]{2,1,0:T(8,128)(2,1)S(1)}, bf16[13,8,512]{2,1,0:T(8,128)(2,1)S(1)}, u32[]{:S(2)}, u32[]{:S(2)}) collective-permute-start(bf16[13,8,512]{2,1,0:T(8,128)(2,1)S(1)} %get-tuple-element.164), channel_id=1, source_target_pairs={{0,96},{16,112},{32,0},{48,16},{64,32},{80,48},{96,64},{112,80},{1... | collective-permute-start | bytes 319496 | tf_op jit(solution)/shard_map/ppermute | solution.py:56
  117.1 1.2 shard_map.57
  118.3 1.1 collective-permute-done.32.refs_4_
  119.4 2.7 %collective-permute-done.31.refs_3_ = bf16[14,8,512]{2,1,0:T(8,128)(2,1)S(1)} collective-permute-done((bf16[14,8,512]{2,1,0:T(8,128)(2,1)S(1)}, bf16[14,8,512]{2,1,0:T(8,128)(2,1)S(1)}, u32[]{:S(2)}, u32[]{:S(2)}) %collective-permute-start.31) | collective-permute-done | bytes 114720 | tf_op jit(solution)/shard_map/ppermute | solution.py:56
  122.1 1.3 %shard_map.58 = f32[27,32,512]{2,1,0:T(8,128)} custom-call(f32[13,8,512]{2,1,0:T(8,128)S(1)} %get-tuple-element.156.refs_0_, f32[14,8,512]{2,1,0:T(8,128)S(1)} %get-tuple-element.157.refs_1_, f32[13,8,512]{2,1,0:T(8,128)S(1)} %collective-permute-done.30.refs_2_, bf16[14,8,512]{2,1,0:T(8,128)(2,1)S(1)} %collective-permute-done.31.refs_3_, ...), custom_call_target="tpu_custom_call" | custom-call | tf_op jit(solution)/shard_map/pallas_call | solution.py:407
  (49 shorter events, 2.8 us)
Async XLA Ops:
  2.0 11.5 %collective-permute-start.1 = (bf16[4,8,16,512]{3,2,1,0:T(8,128)(2,1)S(1)}, bf16[4,8,16,512]{3,2,1,0:T(8,128)(2,1)S(1)}, u32[]{:S(2)}, u32[]{:S(2)}) collective-permute-start(bf16[4,8,16,512]{3,2,1,0:T(8,128)(2,1)S(1)} %fusion.3.own_act), channel_id=1, source_target_pairs={{0,1},{1,0},{2,3},{3,2},{4,5},{5,4},{6,7},{7,6},{8,9},{9,8},{10,11... | collective-permute-start | bytes 1572872 | tf_op jit(solution)/shard_map/ppermute | solution.py:43
  2.1 22.0 %collective-permute-start.7 = (bf16[4,8,16,512]{3,2,1,0:T(8,128)(2,1)S(1)}, bf16[4,8,16,512]{3,2,1,0:T(8,128)(2,1)S(1)}, u32[]{:S(2)}, u32[]{:S(2)}) collective-permute-start(bf16[4,8,16,512]{3,2,1,0:T(8,128)(2,1)S(1)} %fusion.3.own_act), channel_id=1, source_target_pairs={{0,2},{1,3},{2,0},{3,1},{4,6},{5,7},{6,4},{7,5},{8,10},{9,11},{10,... | collective-permute-start | bytes 1572872 | tf_op jit(solution)/shard_map/ppermute | solution.py:43
  5.2 8.3 %collective-permute-start = (bf16[8,16,512]{2,1,0:T(8,128)(2,1)S(1)}, bf16[8,16,512]{2,1,0:T(8,128)(2,1)S(1)}, u32[]{:S(2)}, u32[]{:S(2)}) collective-permute-start(bf16[8,16,512]{2,1,0:T(8,128)(2,1)S(1)} %select_bitcast_fusion), channel_id=1, source_target_pairs={{3,7},{7,11},{11,15},{4,0},{8,4},{12,8},{19,23},{23,27},{27,31},{2... | collective-permute-start | bytes 393224 | tf_op jit(solution)/shard_map/ppermute | solution.py:425
  13.5 21.7 %collective-permute-start.8 = (bf16[27,32,512]{2,1,0:T(8,128)(2,1)}, bf16[27,32,512]{2,1,0:T(8,128)(2,1)S(1)}, u32[]{:S(2)}, u32[]{:S(2)}) collective-permute-start(bf16[27,32,512]{2,1,0:T(8,128)(2,1)} %own), channel_id=1, source_target_pairs={{0,12},{1,13},{2,14},{3,15},{4,0},{5,1},{6,2},{7,3},{8,4},{9,5},{1... | collective-permute-start | bytes 2654216 | tf_op jit(solution)/shard_map/ppermute | solution.py:51
  14.8 20.4 %collective-permute-start.9 = (bf16[27,32,512]{2,1,0:T(8,128)(2,1)}, bf16[27,32,512]{2,1,0:T(8,128)(2,1)S(1)}, u32[]{:S(2)}, u32[]{:S(2)}) collective-permute-start(bf16[27,32,512]{2,1,0:T(8,128)(2,1)} %own), channel_id=1, source_target_pairs={{0,4},{1,5},{2,6},{3,7},{4,8},{5,9},{6,10},{7,11},{8,12},{9,13},{1... | collective-permute-start | bytes 2654216 | tf_op jit(solution)/shard_map/ppermute | solution.py:51
  15.5 1.0 copy-start
  16.6 5.7 %collective-permute-start.2 = (bf16[5,16,512]{2,1,0:T(8,128)(2,1)S(1)}, bf16[5,16,512]{2,1,0:T(8,128)(2,1)S(1)}, u32[]{:S(2)}, u32[]{:S(2)}) collective-permute-start(bf16[5,16,512]{2,1,0:T(8,128)(2,1)S(1)} %get-tuple-element.84), channel_id=1, source_target_pairs={{0,18},{16,2},{1,19},{17,3},{2,16},{18,0},{3,17},{19,1},{4,22},{20... | collective-permute-start | bytes 245768 | tf_op jit(solution)/shard_map/ppermute | solution.py:65
  16.7 5.6 %collective-permute-start.3 = (bf16[5,16,512]{2,1,0:T(8,128)(2,1)S(1)}, bf16[5,16,512]{2,1,0:T(8,128)(2,1)S(1)}, u32[]{:S(2)}, u32[]{:S(2)}) collective-permute-start(bf16[5,16,512]{2,1,0:T(8,128)(2,1)S(1)} %get-tuple-element.85), channel_id=1, source_target_pairs={{16,34},{32,18},{17,35},{33,19},{18,32},{34,16},{19,33},{35,17},{2... | collective-permute-start | bytes 245768 | tf_op jit(solution)/shard_map/ppermute | solution.py:65
  23.3 2.0 %collective-permute-start.4 = (bf16[5,10,16,128]{3,2,1,0:T(8,128)(2,1)S(1)}, bf16[5,10,16,128]{3,2,1,0:T(8,128)(2,1)S(1)}, u32[]{:S(2)}, u32[]{:S(2)}) collective-permute-start(bf16[5,10,16,128]{3,2,1,0:T(8,128)(2,1)S(1)} %get-tuple-element.87), channel_id=1, source_target_pairs={{0,1},{1,0},{2,3},{3,2},{4,5},{5,4},{6,7},{7,6},{8,9},{9,8},{10,11... | collective-permute-start | bytes 614408 | tf_op jit(solution)/shard_map/ppermute | solution.py:43
  23.4 8.0 %collective-permute-start.5 = (bf16[5,10,16,128]{3,2,1,0:T(8,128)(2,1)S(1)}, bf16[5,10,16,128]{3,2,1,0:T(8,128)(2,1)S(1)}, u32[]{:S(2)}, u32[]{:S(2)}) collective-permute-start(bf16[5,10,16,128]{3,2,1,0:T(8,128)(2,1)S(1)} %get-tuple-element.88), channel_id=1, source_target_pairs={{0,2},{1,3},{2,0},{3,1},{4,6},{5,7},{6,4},{7,5},{8,10},{9,11},{10,... | collective-permute-start | bytes 614408 | tf_op jit(solution)/shard_map/ppermute | solution.py:43
  24.1 10.8 %collective-permute-start.6 = (bf16[5,10,16,128]{3,2,1,0:T(8,128)(2,1)S(1)}, bf16[5,10,16,128]{3,2,1,0:T(8,128)(2,1)S(1)}, u32[]{:S(2)}, u32[]{:S(2)}) collective-permute-start(bf16[5,10,16,128]{3,2,1,0:T(8,128)(2,1)S(1)} %get-tuple-element.89), channel_id=1, source_target_pairs={{0,3},{1,2},{2,1},{3,0},{4,7},{5,6},{6,5},{7,4},{8,11},{9,10},{10,... | collective-permute-start | bytes 614408 | tf_op jit(solution)/shard_map/ppermute | solution.py:43
  34.8 5.6 %collective-permute-start.10 = (bf16[4,8,16,512]{3,2,1,0:T(8,128)(2,1)S(1)}, bf16[4,8,16,512]{3,2,1,0:T(8,128)(2,1)S(1)}, u32[]{:S(2)}, u32[]{:S(2)}) collective-permute-start(bf16[4,8,16,512]{3,2,1,0:T(8,128)(2,1)S(1)} %collective-permute-done.7.far), channel_id=1, source_target_pairs={{0,1},{1,0},{2,3},{3,2},{4,5},{5,4},{6,7},{7,6},{8,9},{9,8},{10,11... | collective-permute-start | bytes 1572872 | tf_op jit(solution)/shard_map/ppermute | solution.py:43
  35.2 19.6 %collective-permute-start.11 = (bf16[13,32,512]{2,1,0:T(8,128)(2,1)S(1)}, bf16[13,32,512]{2,1,0:T(8,128)(2,1)S(1)}, u32[]{:S(2)}, u32[]{:S(2)}) collective-permute-start(bf16[13,32,512]{2,1,0:T(8,128)(2,1)S(1)} %slice.23), channel_id=1, source_target_pairs={{0,4},{1,5},{2,6},{3,7},{4,8},{5,9},{6,10},{7,11},{8,12},{9,13},{1... | collective-permute-start | bytes 1277960 | tf_op jit(solution)/shard_map/ppermute | solution.py:51
  36.9 20.8 %collective-permute-start.12 = (bf16[14,32,512]{2,1,0:T(8,128)(2,1)S(1)}, bf16[14,32,512]{2,1,0:T(8,128)(2,1)S(1)}, u32[]{:S(2)}, u32[]{:S(2)}) collective-permute-start(bf16[14,32,512]{2,1,0:T(8,128)(2,1)S(1)} %slice.24), channel_id=1, source_target_pairs={{0,12},{1,13},{2,14},{3,15},{4,0},{5,1},{6,2},{7,3},{8,4},{9,5},{1... | collective-permute-start | bytes 1376264 | tf_op jit(solution)/shard_map/ppermute | solution.py:51
  40.4 17.2 %copy-start.2 = (bf16[27,32,512]{2,1,0:T(8,128)(2,1)S(1)}, bf16[27,32,512]{2,1,0:T(8,128)(2,1)}, u32[]{:S(2)}) copy-start(bf16[27,32,512]{2,1,0:T(8,128)(2,1)} %own) | copy-start | bytes 2654212
  48.1 18.2 %collective-permute-start.13 = (bf16[2,13,16,512]{3,2,1,0:T(8,128)(2,1)S(1)}, bf16[2,13,16,512]{3,2,1,0:T(8,128)(2,1)S(1)}, u32[]{:S(2)}, u32[]{:S(2)}) collective-permute-start(bf16[2,13,16,512]{3,2,1,0:T(8,128)(2,1)S(1)} %get-tuple-element.119), channel_id=1, source_target_pairs={{0,32},{16,48},{32,64},{48,80},{64,96},{80,112},{96,0},{112,16},{1... | collective-permute-start | bytes 1277960 | tf_op jit(solution)/shard_map/ppermute | solution.py:56
  53.0 13.3 %collective-permute-start.14 = (bf16[2,13,16,512]{3,2,1,0:T(8,128)(2,1)S(1)}, bf16[2,13,16,512]{3,2,1,0:T(8,128)(2,1)S(1)}, u32[]{:S(2)}, u32[]{:S(2)}) collective-permute-start(bf16[2,13,16,512]{3,2,1,0:T(8,128)(2,1)S(1)} %get-tuple-element.120), channel_id=1, source_target_pairs={{0,96},{16,112},{32,0},{48,16},{64,32},{80,48},{96,64},{112,80},{1... | collective-permute-start | bytes 1277960 | tf_op jit(solution)/shard_map/ppermute | solution.py:56
  54.4 12.9 %collective-permute-start.15 = (bf16[2,14,16,512]{3,2,1,0:T(8,128)(2,1)S(1)}, bf16[2,14,16,512]{3,2,1,0:T(8,128)(2,1)S(1)}, u32[]{:S(2)}, u32[]{:S(2)}) collective-permute-start(bf16[2,14,16,512]{3,2,1,0:T(8,128)(2,1)S(1)} %get-tuple-element.121), channel_id=1, source_target_pairs={{0,4},{1,5},{2,6},{3,7},{4,8},{5,9},{6,10},{7,11},{8,12},{9,13},{1... | collective-permute-start | bytes 1376264 | tf_op jit(solution)/shard_map/ppermute | solution.py:51
  54.8 12.5 %collective-permute-start.16 = (bf16[2,14,16,512]{3,2,1,0:T(8,128)(2,1)S(1)}, bf16[2,14,16,512]{3,2,1,0:T(8,128)(2,1)S(1)}, u32[]{:S(2)}, u32[]{:S(2)}) collective-permute-start(bf16[2,14,16,512]{3,2,1,0:T(8,128)(2,1)S(1)} %get-tuple-element.122), channel_id=1, source_target_pairs={{0,12},{1,13},{2,14},{3,15},{4,0},{5,1},{6,2},{7,3},{8,4},{9,5},{1... | collective-permute-start | bytes 1376264 | tf_op jit(solution)/shard_map/ppermute | solution.py:51
  67.3 11.9 %collective-permute-start.21 = (f32[2,4,8,16,512]{4,3,2,1,0:T(8,128)S(1)}, f32[2,4,8,16,512]{4,3,2,1,0:T(8,128)S(1)}, u32[]{:S(2)}, u32[]{:S(2)}) collective-permute-start(f32[2,4,8,16,512]{4,3,2,1,0:T(8,128)S(1)} %get-tuple-element.136), channel_id=1, source_target_pairs={{0,1},{1,0},{2,3},{3,2},{4,5},{5,4},{6,7},{7,6},{8,9},{9,8},{10,11... | collective-permute-start | bytes 6291464 | tf_op jit(solution)/shard_map/ppermute | solution.py:43
  67.5 11.7 %collective-permute-start.19 = (bf16[14,16,512]{2,1,0:T(8,128)(2,1)S(1)}, bf16[14,16,512]{2,1,0:T(8,128)(2,1)S(1)}, u32[]{:S(2)}, u32[]{:S(2)}) collective-permute-start(bf16[14,16,512]{2,1,0:T(8,128)(2,1)S(1)} %get-tuple-element.134), channel_id=1, source_target_pairs={{0,4},{1,5},{2,6},{3,7},{4,8},{5,9},{6,10},{7,11},{8,12},{9,13},{1... | collective-permute-start | bytes 688136 | tf_op jit(solution)/shard_map/ppermute | solution.py:51
  68.1 11.1 %collective-permute-start.20 = (bf16[14,16,512]{2,1,0:T(8,128)(2,1)S(1)}, bf16[14,16,512]{2,1,0:T(8,128)(2,1)S(1)}, u32[]{:S(2)}, u32[]{:S(2)}) collective-permute-start(bf16[14,16,512]{2,1,0:T(8,128)(2,1)S(1)} %get-tuple-element.135), channel_id=1, source_target_pairs={{0,12},{1,13},{2,14},{3,15},{4,0},{5,1},{6,2},{7,3},{8,4},{9,5},{1... | collective-permute-start | bytes 688136 | tf_op jit(solution)/shard_map/ppermute | solution.py:51
  70.8 8.4 %collective-permute-start.17 = (bf16[13,16,512]{2,1,0:T(8,128)(2,1)S(1)}, bf16[13,16,512]{2,1,0:T(8,128)(2,1)S(1)}, u32[]{:S(2)}, u32[]{:S(2)}) collective-permute-start(bf16[13,16,512]{2,1,0:T(8,128)(2,1)S(1)} %get-tuple-element.132), channel_id=1, source_target_pairs={{0,32},{16,48},{32,64},{48,80},{64,96},{80,112},{96,0},{112,16},{1... | collective-permute-start | bytes 638984 | tf_op jit(solution)/shard_map/ppermute | solution.py:56
  71.2 8.0 %collective-permute-start.18 = (bf16[13,16,512]{2,1,0:T(8,128)(2,1)S(1)}, bf16[13,16,512]{2,1,0:T(8,128)(2,1)S(1)}, u32[]{:S(2)}, u32[]{:S(2)}) collective-permute-start(bf16[13,16,512]{2,1,0:T(8,128)(2,1)S(1)} %get-tuple-element.133), channel_id=1, source_target_pairs={{0,96},{16,112},{32,0},{48,16},{64,32},{80,48},{96,64},{112,80},{1... | collective-permute-start | bytes 638984 | tf_op jit(solution)/shard_map/ppermute | solution.py:56
  79.5 5.8 %collective-permute-start.24 = (bf16[13,8,512]{2,1,0:T(8,128)(2,1)S(1)}, bf16[13,8,512]{2,1,0:T(8,128)(2,1)S(1)}, u32[]{:S(2)}, u32[]{:S(2)}) collective-permute-start(bf16[13,8,512]{2,1,0:T(8,128)(2,1)S(1)} %get-tuple-element.147), channel_id=1, source_target_pairs={{0,12},{1,13},{2,14},{3,15},{4,0},{5,1},{6,2},{7,3},{8,4},{9,5},{1... | collective-permute-start | bytes 319496 | tf_op jit(solution)/shard_map/ppermute | solution.py:51
  81.2 6.4 %collective-permute-start.23 = (bf16[13,8,512]{2,1,0:T(8,128)(2,1)S(1)}, bf16[13,8,512]{2,1,0:T(8,128)(2,1)S(1)}, u32[]{:S(2)}, u32[]{:S(2)}) collective-permute-start(bf16[13,8,512]{2,1,0:T(8,128)(2,1)S(1)} %get-tuple-element.146), channel_id=1, source_target_pairs={{0,8},{1,9},{2,10},{3,11},{4,12},{5,13},{6,14},{7,15},{8,0},{9,1},... | collective-permute-start | bytes 319496 | tf_op jit(solution)/shard_map/ppermute | solution.py:51
  81.2 7.3 %collective-permute-start.22 = (bf16[13,8,512]{2,1,0:T(8,128)(2,1)S(1)}, bf16[13,8,512]{2,1,0:T(8,128)(2,1)S(1)}, u32[]{:S(2)}, u32[]{:S(2)}) collective-permute-start(bf16[13,8,512]{2,1,0:T(8,128)(2,1)S(1)} %get-tuple-element.145), channel_id=1, source_target_pairs={{0,4},{1,5},{2,6},{3,7},{4,8},{5,9},{6,10},{7,11},{8,12},{9,13},{1... | collective-permute-start | bytes 319496 | tf_op jit(solution)/shard_map/ppermute | solution.py:51
  82.3 6.5 %collective-permute-start.27 = (bf16[14,8,512]{2,1,0:T(8,128)(2,1)S(1)}, bf16[14,8,512]{2,1,0:T(8,128)(2,1)S(1)}, u32[]{:S(2)}, u32[]{:S(2)}) collective-permute-start(bf16[14,8,512]{2,1,0:T(8,128)(2,1)S(1)} %get-tuple-element.151), channel_id=1, source_target_pairs={{0,96},{16,112},{32,0},{48,16},{64,32},{80,48},{96,64},{112,80},{1... | collective-permute-start | bytes 344072 | tf_op jit(solution)/shard_map/ppermute | solution.py:56
  85.3 6.4 %collective-permute-start.26 = (bf16[14,8,512]{2,1,0:T(8,128)(2,1)S(1)}, bf16[14,8,512]{2,1,0:T(8,128)(2,1)S(1)}, u32[]{:S(2)}, u32[]{:S(2)}) collective-permute-start(bf16[14,8,512]{2,1,0:T(8,128)(2,1)S(1)} %get-tuple-element.150), channel_id=1, source_target_pairs={{0,64},{16,80},{32,96},{48,112},{64,0},{80,16},{96,32},{112,48},{1... | collective-permute-start | bytes 344072 | tf_op jit(solution)/shard_map/ppermute | solution.py:56
  85.3 7.2 %collective-permute-start.25 = (bf16[14,8,512]{2,1,0:T(8,128)(2,1)S(1)}, bf16[14,8,512]{2,1,0:T(8,128)(2,1)S(1)}, u32[]{:S(2)}, u32[]{:S(2)}) collective-permute-start(bf16[14,8,512]{2,1,0:T(8,128)(2,1)S(1)} %get-tuple-element.149), channel_id=1, source_target_pairs={{0,32},{16,48},{32,64},{48,80},{64,96},{80,112},{96,0},{112,16},{1... | collective-permute-start | bytes 344072 | tf_op jit(solution)/shard_map/ppermute | solution.py:56
  92.6 24.4 %copy-start.1 = (bf16[4,8,16,512]{3,2,1,0:T(8,128)(2,1)S(1)}, bf16[4,8,16,512]{3,2,1,0:T(8,128)(2,1)}, u32[]{:S(2)}) copy-start(bf16[4,8,16,512]{3,2,1,0:T(8,128)(2,1)} %pre.1) | copy-start | bytes 1572868
  92.6 7.5 %collective-permute-start.28 = (bf16[27,8,512]{2,1,0:T(8,128)(2,1)S(1)}, bf16[27,8,512]{2,1,0:T(8,128)(2,1)S(1)}, u32[]{:S(2)}, u32[]{:S(2)}) collective-permute-start(bf16[27,8,512]{2,1,0:T(8,128)(2,1)S(1)} %pad_maximum_fusion), channel_id=1, source_target_pairs={{0,16},{16,0},{32,48},{48,32},{64,80},{80,64},{96,112},{112,96},{1... | collective-permute-start | bytes 663560 | tf_op jit(solution)/shard_map/ppermute | solution.py:469
  100.2 16.9 %collective-permute-start.29 = (bf16[4,8,16,512]{3,2,1,0:T(8,128)(2,1)S(1)}, bf16[4,8,16,512]{3,2,1,0:T(8,128)(2,1)S(1)}, u32[]{:S(2)}, u32[]{:S(2)}) collective-permute-start(bf16[4,8,16,512]{3,2,1,0:T(8,128)(2,1)S(1)} %fusion.4), channel_id=1, source_target_pairs={{0,2},{1,3},{2,0},{3,1},{4,6},{5,7},{6,4},{7,5},{8,10},{9,11},{10,... | collective-permute-start | bytes 1572872 | tf_op jit(solution)/shard_map/ppermute | solution.py:43
  103.5 7.6 %collective-permute-start.33 = (f32[14,8,512]{2,1,0:T(8,128)S(1)}, f32[14,8,512]{2,1,0:T(8,128)S(1)}, u32[]{:S(2)}, u32[]{:S(2)}) collective-permute-start(f32[14,8,512]{2,1,0:T(8,128)S(1)} %get-tuple-element.157.refs_1_), channel_id=1, source_target_pairs={{0,96},{16,112},{32,0},{48,16},{64,32},{80,48},{96,64},{112,80},{1... | collective-permute-start | bytes 688136 | tf_op jit(solution)/shard_map/ppermute | solution.py:56
  104.2 9.6 %collective-permute-start.30 = (f32[13,8,512]{2,1,0:T(8,128)S(1)}, f32[13,8,512]{2,1,0:T(8,128)S(1)}, u32[]{:S(2)}, u32[]{:S(2)}) collective-permute-start(f32[13,8,512]{2,1,0:T(8,128)S(1)} %get-tuple-element.156.refs_0_), channel_id=1, source_target_pairs={{0,32},{16,48},{32,64},{48,80},{64,96},{80,112},{96,0},{112,16},{1... | collective-permute-start | bytes 638984 | tf_op jit(solution)/shard_map/ppermute | solution.py:56
  111.1 11.0 %collective-permute-start.35 = (f32[14,8,512]{2,1,0:T(8,128)S(1)}, f32[14,8,512]{2,1,0:T(8,128)S(1)}, u32[]{:S(2)}, u32[]{:S(2)}) collective-permute-start(f32[14,8,512]{2,1,0:T(8,128)S(1)} %collective-permute-done.33.refs_5_), channel_id=1, source_target_pairs={{0,96},{16,112},{32,0},{48,16},{64,32},{80,48},{96,64},{112,80},{1... | collective-permute-start | bytes 688136 | tf_op jit(solution)/shard_map/ppermute | solution.py:56
  113.8 8.3 %collective-permute-start.34 = (f32[13,8,512]{2,1,0:T(8,128)S(1)}, f32[13,8,512]{2,1,0:T(8,128)S(1)}, u32[]{:S(2)}, u32[]{:S(2)}) collective-permute-start(f32[13,8,512]{2,1,0:T(8,128)S(1)} %collective-permute-done.30.refs_2_), channel_id=1, source_target_pairs={{0,32},{16,48},{32,64},{48,80},{64,96},{80,112},{96,0},{112,16},{1... | collective-permute-start | bytes 638984 | tf_op jit(solution)/shard_map/ppermute | solution.py:56
  113.8 8.3 %collective-permute-start.31 = (bf16[14,8,512]{2,1,0:T(8,128)(2,1)S(1)}, bf16[14,8,512]{2,1,0:T(8,128)(2,1)S(1)}, u32[]{:S(2)}, u32[]{:S(2)}) collective-permute-start(bf16[14,8,512]{2,1,0:T(8,128)(2,1)S(1)} %get-tuple-element.166), channel_id=1, source_target_pairs={{0,32},{16,48},{32,64},{48,80},{64,96},{80,112},{96,0},{112,16},{1... | collective-permute-start | bytes 344072 | tf_op jit(solution)/shard_map/ppermute | solution.py:56
  113.8 5.5 %collective-permute-start.32 = (bf16[13,8,512]{2,1,0:T(8,128)(2,1)S(1)}, bf16[13,8,512]{2,1,0:T(8,128)(2,1)S(1)}, u32[]{:S(2)}, u32[]{:S(2)}) collective-permute-start(bf16[13,8,512]{2,1,0:T(8,128)(2,1)S(1)} %get-tuple-element.164), channel_id=1, source_target_pairs={{0,96},{16,112},{32,0},{48,16},{64,32},{80,48},{96,64},{112,80},{1... | collective-permute-start | bytes 319496 | tf_op jit(solution)/shard_map/ppermute | solution.py:56

commit v13 on v11

--- a/solution.py
+++ b/solution.py
@@ -392,8 +392,8 @@
 
 
 def gather_x(low, high):
-    low_below, high_above = along_x(low, 1), along_x(high, -1)
-    high_below, low_above = along_x(high.astype(BF16), 1), along_x(low.astype(BF16), -1)
+    low_below, high_above = along_x(low.astype(BF16), 1), along_x(high.astype(BF16), -1)
+    high_below, low_above = along_x(high, 1), along_x(low, -1)
     low_far, high_far = along_x(low_below, 1), along_x(high_above, -1)
     return low, high, low_below, high_below, low_above, high_above, low_far, high_far
 

time: 123 us -> 119 us (0.967)
  waiting for transfers between devices: 40.4 us -> 36.6 us
    ppermute x13, waiting for transfers between devices: 17.8 us -> 13.9 us  [along_x(): lax.ppermute(block, 'gx', [(g, (g + 2 * step) % count) for g in range(cou...]
  transfers between devices with their start and end apart: 36 -> 36, of which waited for: 15 -> 14; matrix products, arithmetic and copies ran while one was open for 1% -> 1% of each run, Pallas kernels for 17% -> 17%
where the time goes in v13:
time: 119 us; the launch traced here: 118 us
  starting transfers between devices  54.5 us (46%)
  waiting for transfers between devices  36.6 us (31%)
  Pallas kernels  22.2 us (19%)
  other arithmetic  2.99 us (3%)
    ppermute x13, starting transfers between devices, along_x(): lax.ppermute(block, 'gx', [(g, (g + 2 * step) % count) for g in range(cou...  24.2 us
    ppermute x11, starting transfers between devices, along_y(): lax.ppermute(block, 'gy', [(s, t) for s, t in pairs if 0 <= t < count])  20.8 us
    ppermute x13, waiting for transfers between devices, along_x(): lax.ppermute(block, 'gx', [(g, (g + 2 * step) % count) for g in range(cou...  13.9 us
    ppermute x1, waiting for transfers between devices, body(): other = lax.ppermute(mine, 'gx', [(g, g ^ 1) for g in range(count)])  9.09 us
    pallas_call x1, Pallas kernels, input_terms(): pl.pallas_call(input_kernel, out_shape=[jax.ShapeDtypeStruct((2,) + block...  8.65 us
    ppermute x8, waiting for transfers between devices, swap(): return lax.ppermute(block, 'gy', [(g, g ^ k) for g in range(count)])  8.14 us
    pallas_call x1, Pallas kernels, weight_terms(): pl.pallas_call(functools.partial(weight_kernel, norm), out_shape=shapes,...  7.66 us
    ppermute x8, starting transfers between devices, swap(): return lax.ppermute(block, 'gy', [(g, g ^ k) for g in range(count)])  4.36 us
  transfers between devices with their start and end apart: 36, of which 14 were waited for; matrix products, arithmetic and copies ran while one was open for 1% of the time, Pallas kernels for 17%

profile of v13, /device:TPU:0, one launch (start us, length us, event | category | flops | bytes accessed | tf_op | source)
XLA Modules:
  0.0 118.4 jit_solution(5004012930351905126)
XLA Ops:
  0.6 1.4 %fusion.3.own_act = bf16[4,8,16,512]{3,2,1,0:T(8,128)(2,1)S(1)} fusion(bf16[4,8,16,512]{3,2,1,0:T(8,128)(2,1)} %pre.1), kind=kLoop, calls=%fused_computation.5 | loop fusion | flops 1572864 | bytes 1048576 | tf_op jit(solution)/shard_map/convert_element_type | solution.py:422
  2.2 2.1 %collective-permute-start.5 = (bf16[4,8,16,512]{3,2,1,0:T(8,128)(2,1)S(1)}, bf16[4,8,16,512]{3,2,1,0:T(8,128)(2,1)S(1)}, u32[]{:S(2)}, u32[]{:S(2)}) collective-permute-start(bf16[4,8,16,512]{3,2,1,0:T(8,128)(2,1)S(1)} %fusion.3.own_act), channel_id=1, source_target_pairs={{0,2},{1,3},{2,0},{3,1},{4,6},{5,7},{6,4},{7,5},{8,10},{9,11},{10,... | collective-permute-start | bytes 1572872 | tf_op jit(solution)/shard_map/ppermute | solution.py:43
  4.3 1.0 select_bitcast_fusion
  5.2 0.7 collective-permute-start
  5.9 1.0 copy-done.1
  7.0 0.7 shard_map.50
  7.7 0.3 shard_map.51
  8.0 8.3 %collective-permute-start.8 = (bf16[27,32,512]{2,1,0:T(8,128)(2,1)S(1)}, bf16[27,32,512]{2,1,0:T(8,128)(2,1)S(1)}, u32[]{:S(2)}, u32[]{:S(2)}) collective-permute-start(bf16[27,32,512]{2,1,0:T(8,128)(2,1)S(1)} %copy-done.2), channel_id=1, source_target_pairs={{0,12},{1,13},{2,14},{3,15},{4,0},{5,1},{6,2},{7,3},{8,4},{9,5},{1... | collective-permute-start | bytes 2654216 | tf_op jit(solution)/shard_map/ppermute | solution.py:51
  16.3 1.2 %collective-permute-done.5.far = bf16[4,8,16,512]{3,2,1,0:T(8,128)(2,1)S(1)} collective-permute-done((bf16[4,8,16,512]{3,2,1,0:T(8,128)(2,1)S(1)}, bf16[4,8,16,512]{3,2,1,0:T(8,128)(2,1)S(1)}, u32[]{:S(2)}, u32[]{:S(2)}) %collective-permute-start.5) | collective-permute-done | bytes 524320 | tf_op jit(solution)/shard_map/ppermute | solution.py:43
  17.6 1.6 %collective-permute-start.4 = (bf16[5,8,16,128]{3,2,1,0:T(8,128)(2,1)S(1)}, bf16[5,8,16,128]{3,2,1,0:T(8,128)(2,1)S(1)}, u32[]{:S(2)}, u32[]{:S(2)}) collective-permute-start(bf16[5,8,16,128]{3,2,1,0:T(8,128)(2,1)S(1)} %get-tuple-element.109), channel_id=1, source_target_pairs={{0,3},{1,2},{2,1},{3,0},{4,7},{5,6},{6,5},{7,4},{8,11},{9,10},{10,... | collective-permute-start | bytes 491528 | tf_op jit(solution)/shard_map/ppermute | solution.py:43
  19.2 4.2 %collective-permute-done.3.p2 = bf16[5,8,16,128]{3,2,1,0:T(8,128)(2,1)S(1)} collective-permute-done((bf16[5,8,16,128]{3,2,1,0:T(8,128)(2,1)S(1)}, bf16[5,8,16,128]{3,2,1,0:T(8,128)(2,1)S(1)}, u32[]{:S(2)}, u32[]{:S(2)}) %collective-permute-start.3) | collective-permute-done | bytes 163872 | tf_op jit(solution)/shard_map/ppermute | solution.py:43
  23.3 2.7 %collective-permute-done.4.p3 = bf16[5,8,16,128]{3,2,1,0:T(8,128)(2,1)S(1)} collective-permute-done((bf16[5,8,16,128]{3,2,1,0:T(8,128)(2,1)S(1)}, bf16[5,8,16,128]{3,2,1,0:T(8,128)(2,1)S(1)}, u32[]{:S(2)}, u32[]{:S(2)}) %collective-permute-start.4) | collective-permute-done | bytes 163872 | tf_op jit(solution)/shard_map/ppermute | solution.py:43
  26.1 0.5 collective-permute-start.10
  26.6 3.4 %collective-permute-start.6 = (bf16[4,5,16,128]{3,2,1,0:T(8,128)(2,1)S(1)}, bf16[4,5,16,128]{3,2,1,0:T(8,128)(2,1)S(1)}, u32[]{:S(2)}, u32[]{:S(2)}) collective-permute-start(bf16[4,5,16,128]{3,2,1,0:T(8,128)(2,1)S(1)} %get-tuple-element.114), channel_id=1, source_target_pairs={{0,16},{32,48},{64,80},{96,112},{16,0},{48,32},{80,64},{112,96},{1... | collective-permute-start | bytes 245768 | tf_op jit(solution)/shard_map/ppermute | solution.py:62
  30.0 0.7 collective-permute-start.7
  30.7 2.0 %collective-permute-done.6.even = bf16[4,5,16,128]{3,2,1,0:T(8,128)(2,1)S(1)} collective-permute-done((bf16[4,5,16,128]{3,2,1,0:T(8,128)(2,1)S(1)}, bf16[4,5,16,128]{3,2,1,0:T(8,128)(2,1)S(1)}, u32[]{:S(2)}, u32[]{:S(2)}) %collective-permute-start.6) | collective-permute-done | bytes 81952 | tf_op jit(solution)/shard_map/ppermute | solution.py:62
  32.7 1.1 collective-permute-done.9.below
  33.9 3.3 %collective-permute-start.12 = (bf16[14,32,512]{2,1,0:T(8,128)(2,1)S(1)}, bf16[14,32,512]{2,1,0:T(8,128)(2,1)S(1)}, u32[]{:S(2)}, u32[]{:S(2)}) collective-permute-start(bf16[14,32,512]{2,1,0:T(8,128)(2,1)S(1)} %slice.24), channel_id=1, source_target_pairs={{0,12},{1,13},{2,14},{3,15},{4,0},{5,1},{6,2},{7,3},{8,4},{9,5},{1... | collective-permute-start | bytes 1376264 | tf_op jit(solution)/shard_map/ppermute | solution.py:51
  37.2 1.8 %shard_map.53 = (bf16[18,10,16,128]{3,2,1,0:T(8,128)(2,1)S(1)}, bf16[1152,2304]{1,0:T(8,128)(2,1)S(1)}) custom-call(bf16[5,8,16,128]{3,2,1,0:T(8,128)(2,1)S(1)} %get-tuple-element.110.p0, bf16[5,8,16,128]{3,2,1,0:T(8,128)(2,1)S(1)} %collective-permute-done.2.p1, bf16[5,8,16,128]{3,2,1,0:T(8,128)(2,1)S(1)} %collective-permute-done.3.p2, ...), custom_call_target="tpu_custom_call" | custom-call | flops 1000 | bytes 1000 | tf_op jit(solution)/shard_map/pallas_call | solution.py:174
  39.1 7.7 %shard_map.54 = (bf16[2,13,16,512]{3,2,1,0:T(8,128)(2,1)S(1)}, bf16[2,13,16,512]{3,2,1,0:T(8,128)(2,1)S(1)}, f32[13,16,512]{2,1,0:T(8,128)S(1)}, f32[13,16,512]{...) custom-call(bf16[4,8,16,512]{3,2,1,0:T(8,128)(2,1)S(1)} %fusion.3.ow, ...), custom_call_target="tpu_custom_call" | custom-call | flops 7247757312 | bytes 10000000 | tf_op jit(solution)/shard_map/pallas_call | solution.py:243
  46.7 6.6 %collective-permute-start.13 = (bf16[2,13,16,512]{3,2,1,0:T(8,128)(2,1)S(1)}, bf16[2,13,16,512]{3,2,1,0:T(8,128)(2,1)S(1)}, u32[]{:S(2)}, u32[]{:S(2)}) collective-permute-start(bf16[2,13,16,512]{3,2,1,0:T(8,128)(2,1)S(1)} %get-tuple-element.139), channel_id=1, source_target_pairs={{0,32},{16,48},{32,64},{48,80},{64,96},{80,112},{96,0},{112,16},{1... | collective-permute-start | bytes 1277960 | tf_op jit(solution)/shard_map/ppermute | solution.py:56
  53.3 1.3 %collective-permute-start.14 = (bf16[2,13,16,512]{3,2,1,0:T(8,128)(2,1)S(1)}, bf16[2,13,16,512]{3,2,1,0:T(8,128)(2,1)S(1)}, u32[]{:S(2)}, u32[]{:S(2)}) collective-permute-start(bf16[2,13,16,512]{3,2,1,0:T(8,128)(2,1)S(1)} %get-tuple-element.140), channel_id=1, source_target_pairs={{0,96},{16,112},{32,0},{48,16},{64,32},{80,48},{96,64},{112,80},{1... | collective-permute-start | bytes 1277960 | tf_op jit(solution)/shard_map/ppermute | solution.py:56
  54.6 3.2 %collective-permute-start.16 = (bf16[2,14,16,512]{3,2,1,0:T(8,128)(2,1)S(1)}, bf16[2,14,16,512]{3,2,1,0:T(8,128)(2,1)S(1)}, u32[]{:S(2)}, u32[]{:S(2)}) collective-permute-start(bf16[2,14,16,512]{3,2,1,0:T(8,128)(2,1)S(1)} %get-tuple-element.142), channel_id=1, source_target_pairs={{0,12},{1,13},{2,14},{3,15},{4,0},{5,1},{6,2},{7,3},{8,4},{9,5},{1... | collective-permute-start | bytes 1376264 | tf_op jit(solution)/shard_map/ppermute | solution.py:51
  57.9 8.6 %shard_map.55 = (f32[2,4,8,16,512]{4,3,2,1,0:T(8,128)S(1)}, f32[4,8,16,512]{3,2,1,0:T(8,128)S(1)}, f32[4,8,16,512]{3,2,1,0:T(8,128)S(1)}) custom-call(bf16[18,10,16,128]{3,2,1,0:T(8,128)(2,1)S(1)} %get-tuple-element.133.held, bf16[27,32,512]{2,1,0:T(8,128)(2,1)S(1)} %copy-done.2, bf16[27,32,512]{2,1,0:T(8,128)(2,1)S(1)} %collective-permute-done.8.above, ...), custom_call_target="tpu_custom_call" | custom-call | flops 10192158720 | bytes 10000000 | tf_op jit(solution)/shard_map/pallas_call | solution.py:305
  66.9 3.2 %collective-permute-start.20 = (bf16[14,16,512]{2,1,0:T(8,128)(2,1)S(1)}, bf16[14,16,512]{2,1,0:T(8,128)(2,1)S(1)}, u32[]{:S(2)}, u32[]{:S(2)}) collective-permute-start(bf16[14,16,512]{2,1,0:T(8,128)(2,1)S(1)} %get-tuple-element.155), channel_id=1, source_target_pairs={{0,12},{1,13},{2,14},{3,15},{4,0},{5,1},{6,2},{7,3},{8,4},{9,5},{1... | collective-permute-start | bytes 688136 | tf_op jit(solution)/shard_map/ppermute | solution.py:51
  70.1 0.7 collective-permute-start.17
  70.8 2.6 %collective-permute-start.18 = (bf16[13,16,512]{2,1,0:T(8,128)(2,1)S(1)}, bf16[13,16,512]{2,1,0:T(8,128)(2,1)S(1)}, u32[]{:S(2)}, u32[]{:S(2)}) collective-permute-start(bf16[13,16,512]{2,1,0:T(8,128)(2,1)S(1)} %get-tuple-element.153), channel_id=1, source_target_pairs={{0,96},{16,112},{32,0},{48,16},{64,32},{80,48},{96,64},{112,80},{1... | collective-permute-start | bytes 638984 | tf_op jit(solution)/shard_map/ppermute | solution.py:56
  73.4 5.1 %collective-permute-done.17.refs_3_ = bf16[13,16,512]{2,1,0:T(8,128)(2,1)S(1)} collective-permute-done((bf16[13,16,512]{2,1,0:T(8,128)(2,1)S(1)}, bf16[13,16,512]{2,1,0:T(8,128)(2,1)S(1)}, u32[]{:S(2)}, u32[]{:S(2)}) %collective-permute-start.17) | collective-permute-done | bytes 213024 | tf_op jit(solution)/shard_map/ppermute | solution.py:56
  78.5 0.3 shard_map.57
  78.7 1.4 %collective-permute-start.24 = (bf16[13,8,512]{2,1,0:T(8,128)(2,1)S(1)}, bf16[13,8,512]{2,1,0:T(8,128)(2,1)S(1)}, u32[]{:S(2)}, u32[]{:S(2)}) collective-permute-start(bf16[13,8,512]{2,1,0:T(8,128)(2,1)S(1)} %get-tuple-element.167), channel_id=1, source_target_pairs={{0,12},{1,13},{2,14},{3,15},{4,0},{5,1},{6,2},{7,3},{8,4},{9,5},{1... | collective-permute-start | bytes 319496 | tf_op jit(solution)/shard_map/ppermute | solution.py:51
  80.2 1.1 collective-permute-start.22
  81.3 2.9 %collective-permute-start.27 = (bf16[14,8,512]{2,1,0:T(8,128)(2,1)S(1)}, bf16[14,8,512]{2,1,0:T(8,128)(2,1)S(1)}, u32[]{:S(2)}, u32[]{:S(2)}) collective-permute-start(bf16[14,8,512]{2,1,0:T(8,128)(2,1)S(1)} %get-tuple-element.171), channel_id=1, source_target_pairs={{0,96},{16,112},{32,0},{48,16},{64,32},{80,48},{96,64},{112,80},{1... | collective-permute-start | bytes 344072 | tf_op jit(solution)/shard_map/ppermute | solution.py:56
  84.3 0.9 collective-permute-start.25
  85.1 1.5 %collective-permute-done.23 = bf16[13,8,512]{2,1,0:T(8,128)(2,1)S(1)} collective-permute-done((bf16[13,8,512]{2,1,0:T(8,128)(2,1)S(1)}, bf16[13,8,512]{2,1,0:T(8,128)(2,1)S(1)}, u32[]{:S(2)}, u32[]{:S(2)}) %collective-permute-start.23) | collective-permute-done | bytes 106528 | tf_op jit(solution)/shard_map/ppermute | solution.py:51
  86.6 0.9 collective-permute-done.22
  87.5 0.3 collective-permute-done.27
  87.8 2.8 %collective-permute-done.26 = bf16[14,8,512]{2,1,0:T(8,128)(2,1)S(1)} collective-permute-done((bf16[14,8,512]{2,1,0:T(8,128)(2,1)S(1)}, bf16[14,8,512]{2,1,0:T(8,128)(2,1)S(1)}, u32[]{:S(2)}, u32[]{:S(2)}) %collective-permute-start.26) | collective-permute-done | bytes 114720 | tf_op jit(solution)/shard_map/ppermute | solution.py:56
  90.7 0.8 collective-permute-done.25
  91.6 0.5 collective-permute-start.28
  92.1 0.3 fusion.4
  92.4 9.1 %collective-permute-done.28 = bf16[27,8,512]{2,1,0:T(8,128)(2,1)S(1)} collective-permute-done((bf16[27,8,512]{2,1,0:T(8,128)(2,1)S(1)}, bf16[27,8,512]{2,1,0:T(8,128)(2,1)S(1)}, u32[]{:S(2)}, u32[]{:S(2)}) %collective-permute-start.28) | collective-permute-done | bytes 221216 | tf_op jit(solution)/shard_map/ppermute | solution.py:468
  101.6 3.2 %collective-permute-start.33 = (bf16[14,8,512]{2,1,0:T(8,128)(2,1)S(1)}, bf16[14,8,512]{2,1,0:T(8,128)(2,1)S(1)}, u32[]{:S(2)}, u32[]{:S(2)}) collective-permute-start(bf16[14,8,512]{2,1,0:T(8,128)(2,1)S(1)} %get-tuple-element.184), channel_id=1, source_target_pairs={{0,96},{16,112},{32,0},{48,16},{64,32},{80,48},{96,64},{112,80},{1... | collective-permute-start | bytes 344072 | tf_op jit(solution)/shard_map/ppermute | solution.py:56
  105.0 3.2 %collective-permute-start.32 = (f32[13,8,512]{2,1,0:T(8,128)S(1)}, f32[13,8,512]{2,1,0:T(8,128)S(1)}, u32[]{:S(2)}, u32[]{:S(2)}) collective-permute-start(f32[13,8,512]{2,1,0:T(8,128)S(1)} %get-tuple-element.176.refs_0_), channel_id=1, source_target_pairs={{0,96},{16,112},{32,0},{48,16},{64,32},{80,48},{96,64},{112,80},{1... | collective-permute-start | bytes 638984 | tf_op jit(solution)/shard_map/ppermute | solution.py:56
  108.3 2.6 %collective-permute-start.35 = (bf16[14,8,512]{2,1,0:T(8,128)(2,1)S(1)}, bf16[14,8,512]{2,1,0:T(8,128)(2,1)S(1)}, u32[]{:S(2)}, u32[]{:S(2)}) collective-permute-start(bf16[14,8,512]{2,1,0:T(8,128)(2,1)S(1)} %collective-permute-done.33.refs_5_), channel_id=1, source_target_pairs={{0,96},{16,112},{32,0},{48,16},{64,32},{80,48},{96,64},{112,80},{1... | collective-permute-start | bytes 344072 | tf_op jit(solution)/shard_map/ppermute | solution.py:56
  110.9 0.2 collective-permute-done.30.refs_2_
  111.1 1.2 %shard_map.58 = bf16[4,8,16,512]{3,2,1,0:T(8,128)(2,1)} custom-call(bf16[4,8,16,512]{3,2,1,0:T(8,128)(2,1)S(1)} %copy-done, f32[4,8,16,512]{3,2,1,0:T(8,128)S(1)} %get-tuple-element.143.keep, f32[2,4,8,16,512]{4,3,2,1,0:T(8,128)S(1)} %collective-permute-done.21.near, bf16[4,8,16,512]{3,2,1,0:T(8,128)(2,1)S(1)} %collective-permute-done.29.far), custom_call_target="tpu_custom_call" | custom-call | tf_op jit(solution)/shard_map/pallas_call | solution.py:330
  112.3 4.7 %collective-permute-done.34.refs_6_ = bf16[13,8,512]{2,1,0:T(8,128)(2,1)S(1)} collective-permute-done((bf16[13,8,512]{2,1,0:T(8,128)(2,1)S(1)}, bf16[13,8,512]{2,1,0:T(8,128)(2,1)S(1)}, u32[]{:S(2)}, u32[]{:S(2)}) %collective-permute-start.34) | collective-permute-done | bytes 106528 | tf_op jit(solution)/shard_map/ppermute | solution.py:56
  117.0 1.3 %shard_map.59 = f32[27,32,512]{2,1,0:T(8,128)} custom-call(f32[13,8,512]{2,1,0:T(8,128)S(1)} %get-tuple-element.176.refs_0_, f32[14,8,512]{2,1,0:T(8,128)S(1)} %get-tuple-element.177.refs_1_, bf16[13,8,512]{2,1,0:T(8,128)(2,1)S(1)} %collective-permute-done.30.refs_2_, f32[14,8,512]{2,1,0:T(8,128)S(1)} %collective-permute-done.31.refs_3_, ...), custom_call_target="tpu_custom_call" | custom-call | tf_op jit(solution)/shard_map/pallas_call | solution.py:403
  (50 shorter events, 1.1 us)
Async XLA Ops:
  0.6 7.4 %copy-start.2 = (bf16[27,32,512]{2,1,0:T(8,128)(2,1)S(1)}, bf16[27,32,512]{2,1,0:T(8,128)(2,1)}, u32[]{:S(2)}) copy-start(bf16[27,32,512]{2,1,0:T(8,128)(2,1)} %own) | copy-start | bytes 2654212
  2.1 5.6 %collective-permute-start.1 = (bf16[4,8,16,512]{3,2,1,0:T(8,128)(2,1)S(1)}, bf16[4,8,16,512]{3,2,1,0:T(8,128)(2,1)S(1)}, u32[]{:S(2)}, u32[]{:S(2)}) collective-permute-start(bf16[4,8,16,512]{3,2,1,0:T(8,128)(2,1)S(1)} %fusion.3.own_act), channel_id=1, source_target_pairs={{0,1},{1,0},{2,3},{3,2},{4,5},{5,4},{6,7},{7,6},{8,9},{9,8},{10,11... | collective-permute-start | bytes 1572872 | tf_op jit(solution)/shard_map/ppermute | solution.py:43
  2.2 15.4 %collective-permute-start.5 = (bf16[4,8,16,512]{3,2,1,0:T(8,128)(2,1)S(1)}, bf16[4,8,16,512]{3,2,1,0:T(8,128)(2,1)S(1)}, u32[]{:S(2)}, u32[]{:S(2)}) collective-permute-start(bf16[4,8,16,512]{3,2,1,0:T(8,128)(2,1)S(1)} %fusion.3.own_act), channel_id=1, source_target_pairs={{0,2},{1,3},{2,0},{3,1},{4,6},{5,7},{6,4},{7,5},{8,10},{9,11},{10,... | collective-permute-start | bytes 1572872 | tf_op jit(solution)/shard_map/ppermute | solution.py:43
  5.2 2.4 %collective-permute-start = (bf16[8,16,512]{2,1,0:T(8,128)(2,1)S(1)}, bf16[8,16,512]{2,1,0:T(8,128)(2,1)S(1)}, u32[]{:S(2)}, u32[]{:S(2)}) collective-permute-start(bf16[8,16,512]{2,1,0:T(8,128)(2,1)S(1)} %select_bitcast_fusion), channel_id=1, source_target_pairs={{3,4},{7,8},{11,12},{4,3},{8,7},{12,11},{19,20},{23,24},{27,28},{2... | collective-permute-start | bytes 393224 | tf_op jit(solution)/shard_map/ppermute | solution.py:421
  5.9 1.0 copy-start.1
  8.0 24.6 %collective-permute-start.8 = (bf16[27,32,512]{2,1,0:T(8,128)(2,1)S(1)}, bf16[27,32,512]{2,1,0:T(8,128)(2,1)S(1)}, u32[]{:S(2)}, u32[]{:S(2)}) collective-permute-start(bf16[27,32,512]{2,1,0:T(8,128)(2,1)S(1)} %copy-done.2), channel_id=1, source_target_pairs={{0,12},{1,13},{2,14},{3,15},{4,0},{5,1},{6,2},{7,3},{8,4},{9,5},{1... | collective-permute-start | bytes 2654216 | tf_op jit(solution)/shard_map/ppermute | solution.py:51
  16.3 17.4 %collective-permute-start.9 = (bf16[27,32,512]{2,1,0:T(8,128)(2,1)S(1)}, bf16[27,32,512]{2,1,0:T(8,128)(2,1)S(1)}, u32[]{:S(2)}, u32[]{:S(2)}) collective-permute-start(bf16[27,32,512]{2,1,0:T(8,128)(2,1)S(1)} %copy-done.2), channel_id=1, source_target_pairs={{0,4},{1,5},{2,6},{3,7},{4,8},{5,9},{6,10},{7,11},{8,12},{9,13},{1... | collective-permute-start | bytes 2654216 | tf_op jit(solution)/shard_map/ppermute | solution.py:51
  16.3 2.8 %collective-permute-start.2 = (bf16[5,8,16,128]{3,2,1,0:T(8,128)(2,1)S(1)}, bf16[5,8,16,128]{3,2,1,0:T(8,128)(2,1)S(1)}, u32[]{:S(2)}, u32[]{:S(2)}) collective-permute-start(bf16[5,8,16,128]{3,2,1,0:T(8,128)(2,1)S(1)} %get-tuple-element.107), channel_id=1, source_target_pairs={{0,1},{1,0},{2,3},{3,2},{4,5},{5,4},{6,7},{7,6},{8,9},{9,8},{10,11... | collective-permute-start | bytes 491528 | tf_op jit(solution)/shard_map/ppermute | solution.py:43
  16.3 7.0 %collective-permute-start.3 = (bf16[5,8,16,128]{3,2,1,0:T(8,128)(2,1)S(1)}, bf16[5,8,16,128]{3,2,1,0:T(8,128)(2,1)S(1)}, u32[]{:S(2)}, u32[]{:S(2)}) collective-permute-start(bf16[5,8,16,128]{3,2,1,0:T(8,128)(2,1)S(1)} %get-tuple-element.108), channel_id=1, source_target_pairs={{0,2},{1,3},{2,0},{3,1},{4,6},{5,7},{6,4},{7,5},{8,10},{9,11},{10,... | collective-permute-start | bytes 491528 | tf_op jit(solution)/shard_map/ppermute | solution.py:43
  17.6 8.5 %collective-permute-start.4 = (bf16[5,8,16,128]{3,2,1,0:T(8,128)(2,1)S(1)}, bf16[5,8,16,128]{3,2,1,0:T(8,128)(2,1)S(1)}, u32[]{:S(2)}, u32[]{:S(2)}) collective-permute-start(bf16[5,8,16,128]{3,2,1,0:T(8,128)(2,1)S(1)} %get-tuple-element.109), channel_id=1, source_target_pairs={{0,3},{1,2},{2,1},{3,0},{4,7},{5,6},{6,5},{7,4},{8,11},{9,10},{10,... | collective-permute-start | bytes 491528 | tf_op jit(solution)/shard_map/ppermute | solution.py:43
  26.1 13.0 %collective-permute-start.10 = (bf16[4,8,16,512]{3,2,1,0:T(8,128)(2,1)S(1)}, bf16[4,8,16,512]{3,2,1,0:T(8,128)(2,1)S(1)}, u32[]{:S(2)}, u32[]{:S(2)}) collective-permute-start(bf16[4,8,16,512]{3,2,1,0:T(8,128)(2,1)S(1)} %collective-permute-done.5.far), channel_id=1, source_target_pairs={{0,1},{1,0},{2,3},{3,2},{4,5},{5,4},{6,7},{7,6},{8,9},{9,8},{10,11... | collective-permute-start | bytes 1572872 | tf_op jit(solution)/shard_map/ppermute | solution.py:43
  26.6 6.0 %collective-permute-start.6 = (bf16[4,5,16,128]{3,2,1,0:T(8,128)(2,1)S(1)}, bf16[4,5,16,128]{3,2,1,0:T(8,128)(2,1)S(1)}, u32[]{:S(2)}, u32[]{:S(2)}) collective-permute-start(bf16[4,5,16,128]{3,2,1,0:T(8,128)(2,1)S(1)} %get-tuple-element.114), channel_id=1, source_target_pairs={{0,16},{32,48},{64,80},{96,112},{16,0},{48,32},{80,64},{112,96},{1... | collective-permute-start | bytes 245768 | tf_op jit(solution)/shard_map/ppermute | solution.py:62
  30.0 2.6 %collective-permute-start.7 = (bf16[4,5,16,128]{3,2,1,0:T(8,128)(2,1)S(1)}, bf16[4,5,16,128]{3,2,1,0:T(8,128)(2,1)S(1)}, u32[]{:S(2)}, u32[]{:S(2)}) collective-permute-start(bf16[4,5,16,128]{3,2,1,0:T(8,128)(2,1)S(1)} %get-tuple-element.115), channel_id=1, source_target_pairs={{16,32},{48,64},{80,96},{32,16},{64,48},{96,80},{17,33},{49,65},{8... | collective-permute-start | bytes 245768 | tf_op jit(solution)/shard_map/ppermute | solution.py:62
  33.8 20.8 %collective-permute-start.11 = (bf16[13,32,512]{2,1,0:T(8,128)(2,1)S(1)}, bf16[13,32,512]{2,1,0:T(8,128)(2,1)S(1)}, u32[]{:S(2)}, u32[]{:S(2)}) collective-permute-start(bf16[13,32,512]{2,1,0:T(8,128)(2,1)S(1)} %slice.23), channel_id=1, source_target_pairs={{0,4},{1,5},{2,6},{3,7},{4,8},{5,9},{6,10},{7,11},{8,12},{9,13},{1... | collective-permute-start | bytes 1277960 | tf_op jit(solution)/shard_map/ppermute | solution.py:51
  33.9 24.0 %collective-permute-start.12 = (bf16[14,32,512]{2,1,0:T(8,128)(2,1)S(1)}, bf16[14,32,512]{2,1,0:T(8,128)(2,1)S(1)}, u32[]{:S(2)}, u32[]{:S(2)}) collective-permute-start(bf16[14,32,512]{2,1,0:T(8,128)(2,1)S(1)} %slice.24), channel_id=1, source_target_pairs={{0,12},{1,13},{2,14},{3,15},{4,0},{5,1},{6,2},{7,3},{8,4},{9,5},{1... | collective-permute-start | bytes 1376264 | tf_op jit(solution)/shard_map/ppermute | solution.py:51
  46.7 19.8 %collective-permute-start.13 = (bf16[2,13,16,512]{3,2,1,0:T(8,128)(2,1)S(1)}, bf16[2,13,16,512]{3,2,1,0:T(8,128)(2,1)S(1)}, u32[]{:S(2)}, u32[]{:S(2)}) collective-permute-start(bf16[2,13,16,512]{3,2,1,0:T(8,128)(2,1)S(1)} %get-tuple-element.139), channel_id=1, source_target_pairs={{0,32},{16,48},{32,64},{48,80},{64,96},{80,112},{96,0},{112,16},{1... | collective-permute-start | bytes 1277960 | tf_op jit(solution)/shard_map/ppermute | solution.py:56
  53.3 13.3 %collective-permute-start.14 = (bf16[2,13,16,512]{3,2,1,0:T(8,128)(2,1)S(1)}, bf16[2,13,16,512]{3,2,1,0:T(8,128)(2,1)S(1)}, u32[]{:S(2)}, u32[]{:S(2)}) collective-permute-start(bf16[2,13,16,512]{3,2,1,0:T(8,128)(2,1)S(1)} %get-tuple-element.140), channel_id=1, source_target_pairs={{0,96},{16,112},{32,0},{48,16},{64,32},{80,48},{96,64},{112,80},{1... | collective-permute-start | bytes 1277960 | tf_op jit(solution)/shard_map/ppermute | solution.py:56
  54.6 11.9 %collective-permute-start.15 = (bf16[2,14,16,512]{3,2,1,0:T(8,128)(2,1)S(1)}, bf16[2,14,16,512]{3,2,1,0:T(8,128)(2,1)S(1)}, u32[]{:S(2)}, u32[]{:S(2)}) collective-permute-start(bf16[2,14,16,512]{3,2,1,0:T(8,128)(2,1)S(1)} %get-tuple-element.141), channel_id=1, source_target_pairs={{0,4},{1,5},{2,6},{3,7},{4,8},{5,9},{6,10},{7,11},{8,12},{9,13},{1... | collective-permute-start | bytes 1376264 | tf_op jit(solution)/shard_map/ppermute | solution.py:51
  54.6 11.9 %collective-permute-start.16 = (bf16[2,14,16,512]{3,2,1,0:T(8,128)(2,1)S(1)}, bf16[2,14,16,512]{3,2,1,0:T(8,128)(2,1)S(1)}, u32[]{:S(2)}, u32[]{:S(2)}) collective-permute-start(bf16[2,14,16,512]{3,2,1,0:T(8,128)(2,1)S(1)} %get-tuple-element.142), channel_id=1, source_target_pairs={{0,12},{1,13},{2,14},{3,15},{4,0},{5,1},{6,2},{7,3},{8,4},{9,5},{1... | collective-permute-start | bytes 1376264 | tf_op jit(solution)/shard_map/ppermute | solution.py:51
  66.6 11.9 %collective-permute-start.21 = (f32[2,4,8,16,512]{4,3,2,1,0:T(8,128)S(1)}, f32[2,4,8,16,512]{4,3,2,1,0:T(8,128)S(1)}, u32[]{:S(2)}, u32[]{:S(2)}) collective-permute-start(f32[2,4,8,16,512]{4,3,2,1,0:T(8,128)S(1)} %get-tuple-element.156), channel_id=1, source_target_pairs={{0,1},{1,0},{2,3},{3,2},{4,5},{5,4},{6,7},{7,6},{8,9},{9,8},{10,11... | collective-permute-start | bytes 6291464 | tf_op jit(solution)/shard_map/ppermute | solution.py:43
  66.8 11.6 %collective-permute-start.19 = (bf16[14,16,512]{2,1,0:T(8,128)(2,1)S(1)}, bf16[14,16,512]{2,1,0:T(8,128)(2,1)S(1)}, u32[]{:S(2)}, u32[]{:S(2)}) collective-permute-start(bf16[14,16,512]{2,1,0:T(8,128)(2,1)S(1)} %get-tuple-element.154), channel_id=1, source_target_pairs={{0,4},{1,5},{2,6},{3,7},{4,8},{5,9},{6,10},{7,11},{8,12},{9,13},{1... | collective-permute-start | bytes 688136 | tf_op jit(solution)/shard_map/ppermute | solution.py:51
  66.9 11.5 %collective-permute-start.20 = (bf16[14,16,512]{2,1,0:T(8,128)(2,1)S(1)}, bf16[14,16,512]{2,1,0:T(8,128)(2,1)S(1)}, u32[]{:S(2)}, u32[]{:S(2)}) collective-permute-start(bf16[14,16,512]{2,1,0:T(8,128)(2,1)S(1)} %get-tuple-element.155), channel_id=1, source_target_pairs={{0,12},{1,13},{2,14},{3,15},{4,0},{5,1},{6,2},{7,3},{8,4},{9,5},{1... | collective-permute-start | bytes 688136 | tf_op jit(solution)/shard_map/ppermute | solution.py:51
  70.1 8.3 %collective-permute-start.17 = (bf16[13,16,512]{2,1,0:T(8,128)(2,1)S(1)}, bf16[13,16,512]{2,1,0:T(8,128)(2,1)S(1)}, u32[]{:S(2)}, u32[]{:S(2)}) collective-permute-start(bf16[13,16,512]{2,1,0:T(8,128)(2,1)S(1)} %get-tuple-element.152), channel_id=1, source_target_pairs={{0,32},{16,48},{32,64},{48,80},{64,96},{80,112},{96,0},{112,16},{1... | collective-permute-start | bytes 638984 | tf_op jit(solution)/shard_map/ppermute | solution.py:56
  70.8 7.6 %collective-permute-start.18 = (bf16[13,16,512]{2,1,0:T(8,128)(2,1)S(1)}, bf16[13,16,512]{2,1,0:T(8,128)(2,1)S(1)}, u32[]{:S(2)}, u32[]{:S(2)}) collective-permute-start(bf16[13,16,512]{2,1,0:T(8,128)(2,1)S(1)} %get-tuple-element.153), channel_id=1, source_target_pairs={{0,96},{16,112},{32,0},{48,16},{64,32},{80,48},{96,64},{112,80},{1... | collective-permute-start | bytes 638984 | tf_op jit(solution)/shard_map/ppermute | solution.py:56
  78.7 5.5 %collective-permute-start.24 = (bf16[13,8,512]{2,1,0:T(8,128)(2,1)S(1)}, bf16[13,8,512]{2,1,0:T(8,128)(2,1)S(1)}, u32[]{:S(2)}, u32[]{:S(2)}) collective-permute-start(bf16[13,8,512]{2,1,0:T(8,128)(2,1)S(1)} %get-tuple-element.167), channel_id=1, source_target_pairs={{0,12},{1,13},{2,14},{3,15},{4,0},{5,1},{6,2},{7,3},{8,4},{9,5},{1... | collective-permute-start | bytes 319496 | tf_op jit(solution)/shard_map/ppermute | solution.py:51
  80.2 6.4 %collective-permute-start.23 = (bf16[13,8,512]{2,1,0:T(8,128)(2,1)S(1)}, bf16[13,8,512]{2,1,0:T(8,128)(2,1)S(1)}, u32[]{:S(2)}, u32[]{:S(2)}) collective-permute-start(bf16[13,8,512]{2,1,0:T(8,128)(2,1)S(1)} %get-tuple-element.166), channel_id=1, source_target_pairs={{0,8},{1,9},{2,10},{3,11},{4,12},{5,13},{6,14},{7,15},{8,0},{9,1},... | collective-permute-start | bytes 319496 | tf_op jit(solution)/shard_map/ppermute | solution.py:51
  80.2 7.3 %collective-permute-start.22 = (bf16[13,8,512]{2,1,0:T(8,128)(2,1)S(1)}, bf16[13,8,512]{2,1,0:T(8,128)(2,1)S(1)}, u32[]{:S(2)}, u32[]{:S(2)}) collective-permute-start(bf16[13,8,512]{2,1,0:T(8,128)(2,1)S(1)} %get-tuple-element.165), channel_id=1, source_target_pairs={{0,4},{1,5},{2,6},{3,7},{4,8},{5,9},{6,10},{7,11},{8,12},{9,13},{1... | collective-permute-start | bytes 319496 | tf_op jit(solution)/shard_map/ppermute | solution.py:51
  81.3 6.5 %collective-permute-start.27 = (bf16[14,8,512]{2,1,0:T(8,128)(2,1)S(1)}, bf16[14,8,512]{2,1,0:T(8,128)(2,1)S(1)}, u32[]{:S(2)}, u32[]{:S(2)}) collective-permute-start(bf16[14,8,512]{2,1,0:T(8,128)(2,1)S(1)} %get-tuple-element.171), channel_id=1, source_target_pairs={{0,96},{16,112},{32,0},{48,16},{64,32},{80,48},{96,64},{112,80},{1... | collective-permute-start | bytes 344072 | tf_op jit(solution)/shard_map/ppermute | solution.py:56
  84.3 6.4 %collective-permute-start.26 = (bf16[14,8,512]{2,1,0:T(8,128)(2,1)S(1)}, bf16[14,8,512]{2,1,0:T(8,128)(2,1)S(1)}, u32[]{:S(2)}, u32[]{:S(2)}) collective-permute-start(bf16[14,8,512]{2,1,0:T(8,128)(2,1)S(1)} %get-tuple-element.170), channel_id=1, source_target_pairs={{0,64},{16,80},{32,96},{48,112},{64,0},{80,16},{96,32},{112,48},{1... | collective-permute-start | bytes 344072 | tf_op jit(solution)/shard_map/ppermute | solution.py:56
  84.3 7.2 %collective-permute-start.25 = (bf16[14,8,512]{2,1,0:T(8,128)(2,1)S(1)}, bf16[14,8,512]{2,1,0:T(8,128)(2,1)S(1)}, u32[]{:S(2)}, u32[]{:S(2)}) collective-permute-start(bf16[14,8,512]{2,1,0:T(8,128)(2,1)S(1)} %get-tuple-element.169), channel_id=1, source_target_pairs={{0,32},{16,48},{32,64},{48,80},{64,96},{80,112},{96,0},{112,16},{1... | collective-permute-start | bytes 344072 | tf_op jit(solution)/shard_map/ppermute | solution.py:56
  91.6 19.5 %copy-start = (bf16[4,8,16,512]{3,2,1,0:T(8,128)(2,1)S(1)}, bf16[4,8,16,512]{3,2,1,0:T(8,128)(2,1)}, u32[]{:S(2)}) copy-start(bf16[4,8,16,512]{3,2,1,0:T(8,128)(2,1)} %pre.1) | copy-start | bytes 1572868
  91.6 9.9 %collective-permute-start.28 = (bf16[27,8,512]{2,1,0:T(8,128)(2,1)S(1)}, bf16[27,8,512]{2,1,0:T(8,128)(2,1)S(1)}, u32[]{:S(2)}, u32[]{:S(2)}) collective-permute-start(bf16[27,8,512]{2,1,0:T(8,128)(2,1)S(1)} %pad_maximum_fusion), channel_id=1, source_target_pairs={{0,16},{16,0},{32,48},{48,32},{64,80},{80,64},{96,112},{112,96},{1... | collective-permute-start | bytes 663560 | tf_op jit(solution)/shard_map/ppermute | solution.py:468
  101.5 9.6 %collective-permute-start.29 = (bf16[4,8,16,512]{3,2,1,0:T(8,128)(2,1)S(1)}, bf16[4,8,16,512]{3,2,1,0:T(8,128)(2,1)S(1)}, u32[]{:S(2)}, u32[]{:S(2)}) collective-permute-start(bf16[4,8,16,512]{3,2,1,0:T(8,128)(2,1)S(1)} %fusion.4), channel_id=1, source_target_pairs={{0,2},{1,3},{2,0},{3,1},{4,6},{5,7},{6,4},{7,5},{8,10},{9,11},{10,... | collective-permute-start | bytes 1572872 | tf_op jit(solution)/shard_map/ppermute | solution.py:43
  101.6 15.5 %collective-permute-start.31 = (f32[14,8,512]{2,1,0:T(8,128)S(1)}, f32[14,8,512]{2,1,0:T(8,128)S(1)}, u32[]{:S(2)}, u32[]{:S(2)}) collective-permute-start(f32[14,8,512]{2,1,0:T(8,128)S(1)} %get-tuple-element.177.refs_1_), channel_id=1, source_target_pairs={{0,32},{16,48},{32,64},{48,80},{64,96},{80,112},{96,0},{112,16},{1... | collective-permute-start | bytes 688136 | tf_op jit(solution)/shard_map/ppermute | solution.py:56
  101.6 6.6 %collective-permute-start.33 = (bf16[14,8,512]{2,1,0:T(8,128)(2,1)S(1)}, bf16[14,8,512]{2,1,0:T(8,128)(2,1)S(1)}, u32[]{:S(2)}, u32[]{:S(2)}) collective-permute-start(bf16[14,8,512]{2,1,0:T(8,128)(2,1)S(1)} %get-tuple-element.184), channel_id=1, source_target_pairs={{0,96},{16,112},{32,0},{48,16},{64,32},{80,48},{96,64},{112,80},{1... | collective-permute-start | bytes 344072 | tf_op jit(solution)/shard_map/ppermute | solution.py:56
  105.0 6.1 %collective-permute-start.30 = (bf16[13,8,512]{2,1,0:T(8,128)(2,1)S(1)}, bf16[13,8,512]{2,1,0:T(8,128)(2,1)S(1)}, u32[]{:S(2)}, u32[]{:S(2)}) collective-permute-start(bf16[13,8,512]{2,1,0:T(8,128)(2,1)S(1)} %get-tuple-element.186), channel_id=1, source_target_pairs={{0,32},{16,48},{32,64},{48,80},{64,96},{80,112},{96,0},{112,16},{1... | collective-permute-start | bytes 319496 | tf_op jit(solution)/shard_map/ppermute | solution.py:56
  105.0 7.3 %collective-permute-start.32 = (f32[13,8,512]{2,1,0:T(8,128)S(1)}, f32[13,8,512]{2,1,0:T(8,128)S(1)}, u32[]{:S(2)}, u32[]{:S(2)}) collective-permute-start(f32[13,8,512]{2,1,0:T(8,128)S(1)} %get-tuple-element.176.refs_0_), channel_id=1, source_target_pairs={{0,96},{16,112},{32,0},{48,16},{64,32},{80,48},{96,64},{112,80},{1... | collective-permute-start | bytes 638984 | tf_op jit(solution)/shard_map/ppermute | solution.py:56
  108.3 8.8 %collective-permute-start.35 = (bf16[14,8,512]{2,1,0:T(8,128)(2,1)S(1)}, bf16[14,8,512]{2,1,0:T(8,128)(2,1)S(1)}, u32[]{:S(2)}, u32[]{:S(2)}) collective-permute-start(bf16[14,8,512]{2,1,0:T(8,128)(2,1)S(1)} %collective-permute-done.33.refs_5_), channel_id=1, source_target_pairs={{0,96},{16,112},{32,0},{48,16},{64,32},{80,48},{96,64},{112,80},{1... | collective-permute-start | bytes 344072 | tf_op jit(solution)/shard_map/ppermute | solution.py:56
  111.1 5.9 %collective-permute-start.34 = (bf16[13,8,512]{2,1,0:T(8,128)(2,1)S(1)}, bf16[13,8,512]{2,1,0:T(8,128)(2,1)S(1)}, u32[]{:S(2)}, u32[]{:S(2)}) collective-permute-start(bf16[13,8,512]{2,1,0:T(8,128)(2,1)S(1)} %collective-permute-done.30.refs_2_), channel_id=1, source_target_pairs={{0,32},{16,48},{32,64},{48,80},{64,96},{80,112},{96,0},{112,16},{1... | collective-permute-start | bytes 319496 | tf_op jit(solution)/shard_map/ppermute | solution.py:56

commit v14 on v13

--- a/solution.py
+++ b/solution.py
@@ -432,8 +432,8 @@
     quarters, far = barrier((quarters, far))
     acts = [act, near, far, swap(far, 1)]
     even, odd = sides(quarters)
-    even, odd = swap_x(even, 0), swap_x(odd, 1)
-    even, odd, above, below = barrier((even, odd, above, below))
+    odd, even = swap_x(odd, 1), swap_x(even, 0)
+    odd, even, above, below = barrier((odd, even, above, below))
     taps = XTAPS
     parts = [weight, above, along_y(below[:taps], 1, True), along_y(above[taps:], -1, True), below]
     held, turned = turn(quarters, even, odd)

time: 119 us -> 119 us (level)
  waiting for transfers between devices: 36.6 us -> 33.3 us
  starting transfers between devices: 54.5 us -> 57.1 us
    ppermute x1, waiting for transfers between devices: 9.09 us -> 5.53 us  [body(): other = lax.ppermute(mine, 'gx', [(g, g ^ 1) for g in range(count)])]
    ppermute x1, starting transfers between devices: 0.52 us -> 3.83 us  [body(): other = lax.ppermute(mine, 'gx', [(g, g ^ 1) for g in range(count)])]
    ppermute x13, starting transfers between devices: 24.2 us -> 20.9 us  [along_x(): lax.ppermute(block, 'gx', [(g, (g + 2 * step) % count) for g in range(cou...]
    ppermute x2, starting transfers between devices: 4.06 us -> 6.45 us  [swap_x(): return lax.ppermute(block, 'gx', pairs + [(t, s) for s, t in pairs])]
    ppermute x2, waiting for transfers between devices: 1.96 us -> 3.29 us  [swap_x(): return lax.ppermute(block, 'gx', pairs + [(t, s) for s, t in pairs])]
  transfers between devices with their start and end apart: 36 -> 36, of which waited for: 14 -> 13; matrix products, arithmetic and copies ran while one was open for 1% -> 1% of each run, Pallas kernels for 17% -> 18%
where the time goes in v14:
time: 119 us; the launch traced here: 118 us
  starting transfers between devices  57.1 us (48%)
  waiting for transfers between devices  33.3 us (28%)
  Pallas kernels  22.2 us (19%)
  other arithmetic  2.99 us (3%)
    ppermute x13, starting transfers between devices, along_x(): lax.ppermute(block, 'gx', [(g, (g + 2 * step) % count) for g in range(cou...  20.9 us
    ppermute x11, starting transfers between devices, along_y(): lax.ppermute(block, 'gy', [(s, t) for s, t in pairs if 0 <= t < count])  20.8 us
    ppermute x13, waiting for transfers between devices, along_x(): lax.ppermute(block, 'gx', [(g, (g + 2 * step) % count) for g in range(cou...  14 us
    pallas_call x1, Pallas kernels, input_terms(): pl.pallas_call(input_kernel, out_shape=[jax.ShapeDtypeStruct((2,) + block...  8.65 us
    ppermute x8, waiting for transfers between devices, swap(): return lax.ppermute(block, 'gy', [(g, g ^ k) for g in range(count)])  8.14 us
    pallas_call x1, Pallas kernels, weight_terms(): pl.pallas_call(functools.partial(weight_kernel, norm), out_shape=shapes,...  7.66 us
    ppermute x2, starting transfers between devices, swap_x(): return lax.ppermute(block, 'gx', pairs + [(t, s) for s, t in pairs])  6.45 us
    ppermute x1, waiting for transfers between devices, body(): other = lax.ppermute(mine, 'gx', [(g, g ^ 1) for g in range(count)])  5.53 us
  transfers between devices with their start and end apart: 36, of which 13 were waited for; matrix products, arithmetic and copies ran while one was open for 1% of the time, Pallas kernels for 18%

profile of v14, /device:TPU:0, one launch (start us, length us, event | category | flops | bytes accessed | tf_op | source)
XLA Modules:
  0.0 117.6 jit_solution(13524083873773533799)
XLA Ops:
  0.6 1.4 %fusion.3.own_act = bf16[4,8,16,512]{3,2,1,0:T(8,128)(2,1)S(1)} fusion(bf16[4,8,16,512]{3,2,1,0:T(8,128)(2,1)} %pre.1), kind=kLoop, calls=%fused_computation.5 | loop fusion | flops 1572864 | bytes 1048576 | tf_op jit(solution)/shard_map/convert_element_type | solution.py:422
  2.2 2.1 %collective-permute-start.5 = (bf16[4,8,16,512]{3,2,1,0:T(8,128)(2,1)S(1)}, bf16[4,8,16,512]{3,2,1,0:T(8,128)(2,1)S(1)}, u32[]{:S(2)}, u32[]{:S(2)}) collective-permute-start(bf16[4,8,16,512]{3,2,1,0:T(8,128)(2,1)S(1)} %fusion.3.own_act), channel_id=1, source_target_pairs={{0,2},{1,3},{2,0},{3,1},{4,6},{5,7},{6,4},{7,5},{8,10},{9,11},{10,... | collective-permute-start | bytes 1572872 | tf_op jit(solution)/shard_map/ppermute | solution.py:43
  4.3 1.0 select_bitcast_fusion
  5.2 0.7 collective-permute-start
  5.9 1.0 copy-done.1
  7.0 0.7 shard_map.50
  7.7 0.3 shard_map.51
  8.0 8.3 %collective-permute-start.8 = (bf16[27,32,512]{2,1,0:T(8,128)(2,1)S(1)}, bf16[27,32,512]{2,1,0:T(8,128)(2,1)S(1)}, u32[]{:S(2)}, u32[]{:S(2)}) collective-permute-start(bf16[27,32,512]{2,1,0:T(8,128)(2,1)S(1)} %copy-done.2), channel_id=1, source_target_pairs={{0,12},{1,13},{2,14},{3,15},{4,0},{5,1},{6,2},{7,3},{8,4},{9,5},{1... | collective-permute-start | bytes 2654216 | tf_op jit(solution)/shard_map/ppermute | solution.py:51
  16.3 1.2 %collective-permute-done.5.far = bf16[4,8,16,512]{3,2,1,0:T(8,128)(2,1)S(1)} collective-permute-done((bf16[4,8,16,512]{3,2,1,0:T(8,128)(2,1)S(1)}, bf16[4,8,16,512]{3,2,1,0:T(8,128)(2,1)S(1)}, u32[]{:S(2)}, u32[]{:S(2)}) %collective-permute-start.5) | collective-permute-done | bytes 524320 | tf_op jit(solution)/shard_map/ppermute | solution.py:43
  17.6 1.6 %collective-permute-start.4 = (bf16[5,8,16,128]{3,2,1,0:T(8,128)(2,1)S(1)}, bf16[5,8,16,128]{3,2,1,0:T(8,128)(2,1)S(1)}, u32[]{:S(2)}, u32[]{:S(2)}) collective-permute-start(bf16[5,8,16,128]{3,2,1,0:T(8,128)(2,1)S(1)} %get-tuple-element.109), channel_id=1, source_target_pairs={{0,3},{1,2},{2,1},{3,0},{4,7},{5,6},{6,5},{7,4},{8,11},{9,10},{10,... | collective-permute-start | bytes 491528 | tf_op jit(solution)/shard_map/ppermute | solution.py:43
  19.2 4.2 %collective-permute-done.3.p2 = bf16[5,8,16,128]{3,2,1,0:T(8,128)(2,1)S(1)} collective-permute-done((bf16[5,8,16,128]{3,2,1,0:T(8,128)(2,1)S(1)}, bf16[5,8,16,128]{3,2,1,0:T(8,128)(2,1)S(1)}, u32[]{:S(2)}, u32[]{:S(2)}) %collective-permute-start.3) | collective-permute-done | bytes 163872 | tf_op jit(solution)/shard_map/ppermute | solution.py:43
  23.3 2.7 %collective-permute-done.4.p3 = bf16[5,8,16,128]{3,2,1,0:T(8,128)(2,1)S(1)} collective-permute-done((bf16[5,8,16,128]{3,2,1,0:T(8,128)(2,1)S(1)}, bf16[5,8,16,128]{3,2,1,0:T(8,128)(2,1)S(1)}, u32[]{:S(2)}, u32[]{:S(2)}) %collective-permute-start.4) | collective-permute-done | bytes 163872 | tf_op jit(solution)/shard_map/ppermute | solution.py:43
  26.1 0.5 collective-permute-start.10
  26.6 0.7 collective-permute-start.6
  27.3 5.8 %collective-permute-start.7 = (bf16[4,5,16,128]{3,2,1,0:T(8,128)(2,1)S(1)}, bf16[4,5,16,128]{3,2,1,0:T(8,128)(2,1)S(1)}, u32[]{:S(2)}, u32[]{:S(2)}) collective-permute-start(bf16[4,5,16,128]{3,2,1,0:T(8,128)(2,1)S(1)} %get-tuple-element.115), channel_id=1, source_target_pairs={{0,16},{32,48},{64,80},{96,112},{16,0},{48,32},{80,64},{112,96},{1... | collective-permute-start | bytes 245768 | tf_op jit(solution)/shard_map/ppermute | solution.py:62
  33.1 3.3 %collective-permute-done.7.even = bf16[4,5,16,128]{3,2,1,0:T(8,128)(2,1)S(1)} collective-permute-done((bf16[4,5,16,128]{3,2,1,0:T(8,128)(2,1)S(1)}, bf16[4,5,16,128]{3,2,1,0:T(8,128)(2,1)S(1)}, u32[]{:S(2)}, u32[]{:S(2)}) %collective-permute-start.7) | collective-permute-done | bytes 81952 | tf_op jit(solution)/shard_map/ppermute | solution.py:62
  36.4 0.7 collective-permute-start.11
  37.1 2.7 %collective-permute-start.12 = (bf16[14,32,512]{2,1,0:T(8,128)(2,1)S(1)}, bf16[14,32,512]{2,1,0:T(8,128)(2,1)S(1)}, u32[]{:S(2)}, u32[]{:S(2)}) collective-permute-start(bf16[14,32,512]{2,1,0:T(8,128)(2,1)S(1)} %slice.24), channel_id=1, source_target_pairs={{0,12},{1,13},{2,14},{3,15},{4,0},{5,1},{6,2},{7,3},{8,4},{9,5},{1... | collective-permute-start | bytes 1376264 | tf_op jit(solution)/shard_map/ppermute | solution.py:51
  39.8 1.8 %shard_map.53 = (bf16[18,10,16,128]{3,2,1,0:T(8,128)(2,1)S(1)}, bf16[1152,2304]{1,0:T(8,128)(2,1)S(1)}) custom-call(bf16[5,8,16,128]{3,2,1,0:T(8,128)(2,1)S(1)} %get-tuple-element.110.p0, bf16[5,8,16,128]{3,2,1,0:T(8,128)(2,1)S(1)} %collective-permute-done.2.p1, bf16[5,8,16,128]{3,2,1,0:T(8,128)(2,1)S(1)} %collective-permute-done.3.p2, ...), custom_call_target="tpu_custom_call" | custom-call | flops 1000 | bytes 1000 | tf_op jit(solution)/shard_map/pallas_call | solution.py:174
  41.7 7.7 %shard_map.54 = (bf16[2,13,16,512]{3,2,1,0:T(8,128)(2,1)S(1)}, bf16[2,13,16,512]{3,2,1,0:T(8,128)(2,1)S(1)}, f32[13,16,512]{2,1,0:T(8,128)S(1)}, f32[13,16,512]{...) custom-call(bf16[4,8,16,512]{3,2,1,0:T(8,128)(2,1)S(1)} %fusion.3.ow, ...), custom_call_target="tpu_custom_call" | custom-call | flops 7247757312 | bytes 10000000 | tf_op jit(solution)/shard_map/pallas_call | solution.py:243
  49.3 3.1 %collective-permute-start.13 = (bf16[2,13,16,512]{3,2,1,0:T(8,128)(2,1)S(1)}, bf16[2,13,16,512]{3,2,1,0:T(8,128)(2,1)S(1)}, u32[]{:S(2)}, u32[]{:S(2)}) collective-permute-start(bf16[2,13,16,512]{3,2,1,0:T(8,128)(2,1)S(1)} %get-tuple-element.139), channel_id=1, source_target_pairs={{0,32},{16,48},{32,64},{48,80},{64,96},{80,112},{96,0},{112,16},{1... | collective-permute-start | bytes 1277960 | tf_op jit(solution)/shard_map/ppermute | solution.py:56
  52.4 1.6 %collective-permute-start.14 = (bf16[2,13,16,512]{3,2,1,0:T(8,128)(2,1)S(1)}, bf16[2,13,16,512]{3,2,1,0:T(8,128)(2,1)S(1)}, u32[]{:S(2)}, u32[]{:S(2)}) collective-permute-start(bf16[2,13,16,512]{3,2,1,0:T(8,128)(2,1)S(1)} %get-tuple-element.140), channel_id=1, source_target_pairs={{0,96},{16,112},{32,0},{48,16},{64,32},{80,48},{96,64},{112,80},{1... | collective-permute-start | bytes 1277960 | tf_op jit(solution)/shard_map/ppermute | solution.py:56
  54.0 3.2 %collective-permute-start.16 = (bf16[2,14,16,512]{3,2,1,0:T(8,128)(2,1)S(1)}, bf16[2,14,16,512]{3,2,1,0:T(8,128)(2,1)S(1)}, u32[]{:S(2)}, u32[]{:S(2)}) collective-permute-start(bf16[2,14,16,512]{3,2,1,0:T(8,128)(2,1)S(1)} %get-tuple-element.142), channel_id=1, source_target_pairs={{0,12},{1,13},{2,14},{3,15},{4,0},{5,1},{6,2},{7,3},{8,4},{9,5},{1... | collective-permute-start | bytes 1376264 | tf_op jit(solution)/shard_map/ppermute | solution.py:51
  57.3 8.6 %shard_map.55 = (f32[2,4,8,16,512]{4,3,2,1,0:T(8,128)S(1)}, f32[4,8,16,512]{3,2,1,0:T(8,128)S(1)}, f32[4,8,16,512]{3,2,1,0:T(8,128)S(1)}) custom-call(bf16[18,10,16,128]{3,2,1,0:T(8,128)(2,1)S(1)} %get-tuple-element.133.held, bf16[27,32,512]{2,1,0:T(8,128)(2,1)S(1)} %copy-done.2, bf16[27,32,512]{2,1,0:T(8,128)(2,1)S(1)} %collective-permute-done.8.above, ...), custom_call_target="tpu_custom_call" | custom-call | flops 10192158720 | bytes 10000000 | tf_op jit(solution)/shard_map/pallas_call | solution.py:305
  66.3 3.2 %collective-permute-start.20 = (bf16[14,16,512]{2,1,0:T(8,128)(2,1)S(1)}, bf16[14,16,512]{2,1,0:T(8,128)(2,1)S(1)}, u32[]{:S(2)}, u32[]{:S(2)}) collective-permute-start(bf16[14,16,512]{2,1,0:T(8,128)(2,1)S(1)} %get-tuple-element.155), channel_id=1, source_target_pairs={{0,12},{1,13},{2,14},{3,15},{4,0},{5,1},{6,2},{7,3},{8,4},{9,5},{1... | collective-permute-start | bytes 688136 | tf_op jit(solution)/shard_map/ppermute | solution.py:51
  69.5 0.4 collective-permute-start.17
  69.9 2.9 %collective-permute-start.18 = (bf16[13,16,512]{2,1,0:T(8,128)(2,1)S(1)}, bf16[13,16,512]{2,1,0:T(8,128)(2,1)S(1)}, u32[]{:S(2)}, u32[]{:S(2)}) collective-permute-start(bf16[13,16,512]{2,1,0:T(8,128)(2,1)S(1)} %get-tuple-element.153), channel_id=1, source_target_pairs={{0,96},{16,112},{32,0},{48,16},{64,32},{80,48},{96,64},{112,80},{1... | collective-permute-start | bytes 638984 | tf_op jit(solution)/shard_map/ppermute | solution.py:56
  72.8 5.1 %collective-permute-done.17.refs_3_ = bf16[13,16,512]{2,1,0:T(8,128)(2,1)S(1)} collective-permute-done((bf16[13,16,512]{2,1,0:T(8,128)(2,1)S(1)}, bf16[13,16,512]{2,1,0:T(8,128)(2,1)S(1)}, u32[]{:S(2)}, u32[]{:S(2)}) %collective-permute-start.17) | collective-permute-done | bytes 213024 | tf_op jit(solution)/shard_map/ppermute | solution.py:56
  77.9 0.3 shard_map.57
  78.1 1.4 %collective-permute-start.24 = (bf16[13,8,512]{2,1,0:T(8,128)(2,1)S(1)}, bf16[13,8,512]{2,1,0:T(8,128)(2,1)S(1)}, u32[]{:S(2)}, u32[]{:S(2)}) collective-permute-start(bf16[13,8,512]{2,1,0:T(8,128)(2,1)S(1)} %get-tuple-element.167), channel_id=1, source_target_pairs={{0,12},{1,13},{2,14},{3,15},{4,0},{5,1},{6,2},{7,3},{8,4},{9,5},{1... | collective-permute-start | bytes 319496 | tf_op jit(solution)/shard_map/ppermute | solution.py:51
  79.6 1.1 collective-permute-start.22
  80.7 2.9 %collective-permute-start.27 = (bf16[14,8,512]{2,1,0:T(8,128)(2,1)S(1)}, bf16[14,8,512]{2,1,0:T(8,128)(2,1)S(1)}, u32[]{:S(2)}, u32[]{:S(2)}) collective-permute-start(bf16[14,8,512]{2,1,0:T(8,128)(2,1)S(1)} %get-tuple-element.171), channel_id=1, source_target_pairs={{0,96},{16,112},{32,0},{48,16},{64,32},{80,48},{96,64},{112,80},{1... | collective-permute-start | bytes 344072 | tf_op jit(solution)/shard_map/ppermute | solution.py:56
  83.7 0.9 collective-permute-start.25
  84.5 1.5 %collective-permute-done.23 = bf16[13,8,512]{2,1,0:T(8,128)(2,1)S(1)} collective-permute-done((bf16[13,8,512]{2,1,0:T(8,128)(2,1)S(1)}, bf16[13,8,512]{2,1,0:T(8,128)(2,1)S(1)}, u32[]{:S(2)}, u32[]{:S(2)}) %collective-permute-start.23) | collective-permute-done | bytes 106528 | tf_op jit(solution)/shard_map/ppermute | solution.py:51
  86.0 0.9 collective-permute-done.22
  86.9 0.3 collective-permute-done.27
  87.2 2.8 %collective-permute-done.26 = bf16[14,8,512]{2,1,0:T(8,128)(2,1)S(1)} collective-permute-done((bf16[14,8,512]{2,1,0:T(8,128)(2,1)S(1)}, bf16[14,8,512]{2,1,0:T(8,128)(2,1)S(1)}, u32[]{:S(2)}, u32[]{:S(2)}) %collective-permute-start.26) | collective-permute-done | bytes 114720 | tf_op jit(solution)/shard_map/ppermute | solution.py:56
  90.1 0.8 collective-permute-done.25
  91.0 3.8 %collective-permute-start.28 = (bf16[27,8,512]{2,1,0:T(8,128)(2,1)S(1)}, bf16[27,8,512]{2,1,0:T(8,128)(2,1)S(1)}, u32[]{:S(2)}, u32[]{:S(2)}) collective-permute-start(bf16[27,8,512]{2,1,0:T(8,128)(2,1)S(1)} %pad_maximum_fusion), channel_id=1, source_target_pairs={{0,16},{16,0},{32,48},{48,32},{64,80},{80,64},{96,112},{112,96},{1... | collective-permute-start | bytes 663560 | tf_op jit(solution)/shard_map/ppermute | solution.py:468
  94.8 0.3 fusion.4
  95.1 5.5 %collective-permute-done.28 = bf16[27,8,512]{2,1,0:T(8,128)(2,1)S(1)} collective-permute-done((bf16[27,8,512]{2,1,0:T(8,128)(2,1)S(1)}, bf16[27,8,512]{2,1,0:T(8,128)(2,1)S(1)}, u32[]{:S(2)}, u32[]{:S(2)}) %collective-permute-start.28) | collective-permute-done | bytes 221216 | tf_op jit(solution)/shard_map/ppermute | solution.py:468
  100.8 3.2 %collective-permute-start.33 = (bf16[14,8,512]{2,1,0:T(8,128)(2,1)S(1)}, bf16[14,8,512]{2,1,0:T(8,128)(2,1)S(1)}, u32[]{:S(2)}, u32[]{:S(2)}) collective-permute-start(bf16[14,8,512]{2,1,0:T(8,128)(2,1)S(1)} %get-tuple-element.184), channel_id=1, source_target_pairs={{0,96},{16,112},{32,0},{48,16},{64,32},{80,48},{96,64},{112,80},{1... | collective-permute-start | bytes 344072 | tf_op jit(solution)/shard_map/ppermute | solution.py:56
  104.2 3.2 %collective-permute-start.32 = (f32[13,8,512]{2,1,0:T(8,128)S(1)}, f32[13,8,512]{2,1,0:T(8,128)S(1)}, u32[]{:S(2)}, u32[]{:S(2)}) collective-permute-start(f32[13,8,512]{2,1,0:T(8,128)S(1)} %get-tuple-element.176.refs_0_), channel_id=1, source_target_pairs={{0,96},{16,112},{32,0},{48,16},{64,32},{80,48},{96,64},{112,80},{1... | collective-permute-start | bytes 638984 | tf_op jit(solution)/shard_map/ppermute | solution.py:56
  107.4 2.6 %collective-permute-start.35 = (bf16[14,8,512]{2,1,0:T(8,128)(2,1)S(1)}, bf16[14,8,512]{2,1,0:T(8,128)(2,1)S(1)}, u32[]{:S(2)}, u32[]{:S(2)}) collective-permute-start(bf16[14,8,512]{2,1,0:T(8,128)(2,1)S(1)} %collective-permute-done.33.refs_5_), channel_id=1, source_target_pairs={{0,96},{16,112},{32,0},{48,16},{64,32},{80,48},{96,64},{112,80},{1... | collective-permute-start | bytes 344072 | tf_op jit(solution)/shard_map/ppermute | solution.py:56
  110.0 0.3 collective-permute-done.30.refs_2_
  110.3 1.2 %shard_map.58 = bf16[4,8,16,512]{3,2,1,0:T(8,128)(2,1)} custom-call(bf16[4,8,16,512]{3,2,1,0:T(8,128)(2,1)S(1)} %copy-done, f32[4,8,16,512]{3,2,1,0:T(8,128)S(1)} %get-tuple-element.143.keep, f32[2,4,8,16,512]{4,3,2,1,0:T(8,128)S(1)} %collective-permute-done.21.near, bf16[4,8,16,512]{3,2,1,0:T(8,128)(2,1)S(1)} %collective-permute-done.29.far), custom_call_target="tpu_custom_call" | custom-call | tf_op jit(solution)/shard_map/pallas_call | solution.py:330
  111.6 4.7 %collective-permute-done.34.refs_6_ = bf16[13,8,512]{2,1,0:T(8,128)(2,1)S(1)} collective-permute-done((bf16[13,8,512]{2,1,0:T(8,128)(2,1)S(1)}, bf16[13,8,512]{2,1,0:T(8,128)(2,1)S(1)}, u32[]{:S(2)}, u32[]{:S(2)}) %collective-permute-start.34) | collective-permute-done | bytes 106528 | tf_op jit(solution)/shard_map/ppermute | solution.py:56
  116.2 1.3 %shard_map.59 = f32[27,32,512]{2,1,0:T(8,128)} custom-call(f32[13,8,512]{2,1,0:T(8,128)S(1)} %get-tuple-element.176.refs_0_, f32[14,8,512]{2,1,0:T(8,128)S(1)} %get-tuple-element.177.refs_1_, bf16[13,8,512]{2,1,0:T(8,128)(2,1)S(1)} %collective-permute-done.30.refs_2_, f32[14,8,512]{2,1,0:T(8,128)S(1)} %collective-permute-done.31.refs_3_, ...), custom_call_target="tpu_custom_call" | custom-call | tf_op jit(solution)/shard_map/pallas_call | solution.py:403
  (50 shorter events, 1.1 us)
Async XLA Ops:
  0.6 7.4 %copy-start.2 = (bf16[27,32,512]{2,1,0:T(8,128)(2,1)S(1)}, bf16[27,32,512]{2,1,0:T(8,128)(2,1)}, u32[]{:S(2)}) copy-start(bf16[27,32,512]{2,1,0:T(8,128)(2,1)} %own) | copy-start | bytes 2654212
  2.1 5.6 %collective-permute-start.1 = (bf16[4,8,16,512]{3,2,1,0:T(8,128)(2,1)S(1)}, bf16[4,8,16,512]{3,2,1,0:T(8,128)(2,1)S(1)}, u32[]{:S(2)}, u32[]{:S(2)}) collective-permute-start(bf16[4,8,16,512]{3,2,1,0:T(8,128)(2,1)S(1)} %fusion.3.own_act), channel_id=1, source_target_pairs={{0,1},{1,0},{2,3},{3,2},{4,5},{5,4},{6,7},{7,6},{8,9},{9,8},{10,11... | collective-permute-start | bytes 1572872 | tf_op jit(solution)/shard_map/ppermute | solution.py:43
  2.2 15.4 %collective-permute-start.5 = (bf16[4,8,16,512]{3,2,1,0:T(8,128)(2,1)S(1)}, bf16[4,8,16,512]{3,2,1,0:T(8,128)(2,1)S(1)}, u32[]{:S(2)}, u32[]{:S(2)}) collective-permute-start(bf16[4,8,16,512]{3,2,1,0:T(8,128)(2,1)S(1)} %fusion.3.own_act), channel_id=1, source_target_pairs={{0,2},{1,3},{2,0},{3,1},{4,6},{5,7},{6,4},{7,5},{8,10},{9,11},{10,... | collective-permute-start | bytes 1572872 | tf_op jit(solution)/shard_map/ppermute | solution.py:43
  5.2 2.4 %collective-permute-start = (bf16[8,16,512]{2,1,0:T(8,128)(2,1)S(1)}, bf16[8,16,512]{2,1,0:T(8,128)(2,1)S(1)}, u32[]{:S(2)}, u32[]{:S(2)}) collective-permute-start(bf16[8,16,512]{2,1,0:T(8,128)(2,1)S(1)} %select_bitcast_fusion), channel_id=1, source_target_pairs={{3,4},{7,8},{11,12},{4,3},{8,7},{12,11},{19,20},{23,24},{27,28},{2... | collective-permute-start | bytes 393224 | tf_op jit(solution)/shard_map/ppermute | solution.py:421
  5.9 1.0 copy-start.1
  8.0 28.3 %collective-permute-start.8 = (bf16[27,32,512]{2,1,0:T(8,128)(2,1)S(1)}, bf16[27,32,512]{2,1,0:T(8,128)(2,1)S(1)}, u32[]{:S(2)}, u32[]{:S(2)}) collective-permute-start(bf16[27,32,512]{2,1,0:T(8,128)(2,1)S(1)} %copy-done.2), channel_id=1, source_target_pairs={{0,12},{1,13},{2,14},{3,15},{4,0},{5,1},{6,2},{7,3},{8,4},{9,5},{1... | collective-permute-start | bytes 2654216 | tf_op jit(solution)/shard_map/ppermute | solution.py:51
  16.3 20.0 %collective-permute-start.9 = (bf16[27,32,512]{2,1,0:T(8,128)(2,1)S(1)}, bf16[27,32,512]{2,1,0:T(8,128)(2,1)S(1)}, u32[]{:S(2)}, u32[]{:S(2)}) collective-permute-start(bf16[27,32,512]{2,1,0:T(8,128)(2,1)S(1)} %copy-done.2), channel_id=1, source_target_pairs={{0,4},{1,5},{2,6},{3,7},{4,8},{5,9},{6,10},{7,11},{8,12},{9,13},{1... | collective-permute-start | bytes 2654216 | tf_op jit(solution)/shard_map/ppermute | solution.py:51
  16.3 2.8 %collective-permute-start.2 = (bf16[5,8,16,128]{3,2,1,0:T(8,128)(2,1)S(1)}, bf16[5,8,16,128]{3,2,1,0:T(8,128)(2,1)S(1)}, u32[]{:S(2)}, u32[]{:S(2)}) collective-permute-start(bf16[5,8,16,128]{3,2,1,0:T(8,128)(2,1)S(1)} %get-tuple-element.107), channel_id=1, source_target_pairs={{0,1},{1,0},{2,3},{3,2},{4,5},{5,4},{6,7},{7,6},{8,9},{9,8},{10,11... | collective-permute-start | bytes 491528 | tf_op jit(solution)/shard_map/ppermute | solution.py:43
  16.3 7.0 %collective-permute-start.3 = (bf16[5,8,16,128]{3,2,1,0:T(8,128)(2,1)S(1)}, bf16[5,8,16,128]{3,2,1,0:T(8,128)(2,1)S(1)}, u32[]{:S(2)}, u32[]{:S(2)}) collective-permute-start(bf16[5,8,16,128]{3,2,1,0:T(8,128)(2,1)S(1)} %get-tuple-element.108), channel_id=1, source_target_pairs={{0,2},{1,3},{2,0},{3,1},{4,6},{5,7},{6,4},{7,5},{8,10},{9,11},{10,... | collective-permute-start | bytes 491528 | tf_op jit(solution)/shard_map/ppermute | solution.py:43
  17.6 8.5 %collective-permute-start.4 = (bf16[5,8,16,128]{3,2,1,0:T(8,128)(2,1)S(1)}, bf16[5,8,16,128]{3,2,1,0:T(8,128)(2,1)S(1)}, u32[]{:S(2)}, u32[]{:S(2)}) collective-permute-start(bf16[5,8,16,128]{3,2,1,0:T(8,128)(2,1)S(1)} %get-tuple-element.109), channel_id=1, source_target_pairs={{0,3},{1,2},{2,1},{3,0},{4,7},{5,6},{6,5},{7,4},{8,11},{9,10},{10,... | collective-permute-start | bytes 491528 | tf_op jit(solution)/shard_map/ppermute | solution.py:43
  26.1 15.6 %collective-permute-start.10 = (bf16[4,8,16,512]{3,2,1,0:T(8,128)(2,1)S(1)}, bf16[4,8,16,512]{3,2,1,0:T(8,128)(2,1)S(1)}, u32[]{:S(2)}, u32[]{:S(2)}) collective-permute-start(bf16[4,8,16,512]{3,2,1,0:T(8,128)(2,1)S(1)} %collective-permute-done.5.far), channel_id=1, source_target_pairs={{0,1},{1,0},{2,3},{3,2},{4,5},{5,4},{6,7},{7,6},{8,9},{9,8},{10,11... | collective-permute-start | bytes 1572872 | tf_op jit(solution)/shard_map/ppermute | solution.py:43
  26.6 6.5 %collective-permute-start.6 = (bf16[4,5,16,128]{3,2,1,0:T(8,128)(2,1)S(1)}, bf16[4,5,16,128]{3,2,1,0:T(8,128)(2,1)S(1)}, u32[]{:S(2)}, u32[]{:S(2)}) collective-permute-start(bf16[4,5,16,128]{3,2,1,0:T(8,128)(2,1)S(1)} %get-tuple-element.114), channel_id=1, source_target_pairs={{16,32},{48,64},{80,96},{32,16},{64,48},{96,80},{17,33},{49,65},{8... | collective-permute-start | bytes 245768 | tf_op jit(solution)/shard_map/ppermute | solution.py:62
  27.3 9.1 %collective-permute-start.7 = (bf16[4,5,16,128]{3,2,1,0:T(8,128)(2,1)S(1)}, bf16[4,5,16,128]{3,2,1,0:T(8,128)(2,1)S(1)}, u32[]{:S(2)}, u32[]{:S(2)}) collective-permute-start(bf16[4,5,16,128]{3,2,1,0:T(8,128)(2,1)S(1)} %get-tuple-element.115), channel_id=1, source_target_pairs={{0,16},{32,48},{64,80},{96,112},{16,0},{48,32},{80,64},{112,96},{1... | collective-permute-start | bytes 245768 | tf_op jit(solution)/shard_map/ppermute | solution.py:62
  36.4 17.6 %collective-permute-start.11 = (bf16[13,32,512]{2,1,0:T(8,128)(2,1)S(1)}, bf16[13,32,512]{2,1,0:T(8,128)(2,1)S(1)}, u32[]{:S(2)}, u32[]{:S(2)}) collective-permute-start(bf16[13,32,512]{2,1,0:T(8,128)(2,1)S(1)} %slice.23), channel_id=1, source_target_pairs={{0,4},{1,5},{2,6},{3,7},{4,8},{5,9},{6,10},{7,11},{8,12},{9,13},{1... | collective-permute-start | bytes 1277960 | tf_op jit(solution)/shard_map/ppermute | solution.py:51
  37.1 20.2 %collective-permute-start.12 = (bf16[14,32,512]{2,1,0:T(8,128)(2,1)S(1)}, bf16[14,32,512]{2,1,0:T(8,128)(2,1)S(1)}, u32[]{:S(2)}, u32[]{:S(2)}) collective-permute-start(bf16[14,32,512]{2,1,0:T(8,128)(2,1)S(1)} %slice.24), channel_id=1, source_target_pairs={{0,12},{1,13},{2,14},{3,15},{4,0},{5,1},{6,2},{7,3},{8,4},{9,5},{1... | collective-permute-start | bytes 1376264 | tf_op jit(solution)/shard_map/ppermute | solution.py:51
  49.3 16.6 %collective-permute-start.13 = (bf16[2,13,16,512]{3,2,1,0:T(8,128)(2,1)S(1)}, bf16[2,13,16,512]{3,2,1,0:T(8,128)(2,1)S(1)}, u32[]{:S(2)}, u32[]{:S(2)}) collective-permute-start(bf16[2,13,16,512]{3,2,1,0:T(8,128)(2,1)S(1)} %get-tuple-element.139), channel_id=1, source_target_pairs={{0,32},{16,48},{32,64},{48,80},{64,96},{80,112},{96,0},{112,16},{1... | collective-permute-start | bytes 1277960 | tf_op jit(solution)/shard_map/ppermute | solution.py:56
  52.4 13.6 %collective-permute-start.14 = (bf16[2,13,16,512]{3,2,1,0:T(8,128)(2,1)S(1)}, bf16[2,13,16,512]{3,2,1,0:T(8,128)(2,1)S(1)}, u32[]{:S(2)}, u32[]{:S(2)}) collective-permute-start(bf16[2,13,16,512]{3,2,1,0:T(8,128)(2,1)S(1)} %get-tuple-element.140), channel_id=1, source_target_pairs={{0,96},{16,112},{32,0},{48,16},{64,32},{80,48},{96,64},{112,80},{1... | collective-permute-start | bytes 1277960 | tf_op jit(solution)/shard_map/ppermute | solution.py:56
  54.0 11.9 %collective-permute-start.15 = (bf16[2,14,16,512]{3,2,1,0:T(8,128)(2,1)S(1)}, bf16[2,14,16,512]{3,2,1,0:T(8,128)(2,1)S(1)}, u32[]{:S(2)}, u32[]{:S(2)}) collective-permute-start(bf16[2,14,16,512]{3,2,1,0:T(8,128)(2,1)S(1)} %get-tuple-element.141), channel_id=1, source_target_pairs={{0,4},{1,5},{2,6},{3,7},{4,8},{5,9},{6,10},{7,11},{8,12},{9,13},{1... | collective-permute-start | bytes 1376264 | tf_op jit(solution)/shard_map/ppermute | solution.py:51
  54.0 11.9 %collective-permute-start.16 = (bf16[2,14,16,512]{3,2,1,0:T(8,128)(2,1)S(1)}, bf16[2,14,16,512]{3,2,1,0:T(8,128)(2,1)S(1)}, u32[]{:S(2)}, u32[]{:S(2)}) collective-permute-start(bf16[2,14,16,512]{3,2,1,0:T(8,128)(2,1)S(1)} %get-tuple-element.142), channel_id=1, source_target_pairs={{0,12},{1,13},{2,14},{3,15},{4,0},{5,1},{6,2},{7,3},{8,4},{9,5},{1... | collective-permute-start | bytes 1376264 | tf_op jit(solution)/shard_map/ppermute | solution.py:51
  66.0 11.9 %collective-permute-start.21 = (f32[2,4,8,16,512]{4,3,2,1,0:T(8,128)S(1)}, f32[2,4,8,16,512]{4,3,2,1,0:T(8,128)S(1)}, u32[]{:S(2)}, u32[]{:S(2)}) collective-permute-start(f32[2,4,8,16,512]{4,3,2,1,0:T(8,128)S(1)} %get-tuple-element.156), channel_id=1, source_target_pairs={{0,1},{1,0},{2,3},{3,2},{4,5},{5,4},{6,7},{7,6},{8,9},{9,8},{10,11... | collective-permute-start | bytes 6291464 | tf_op jit(solution)/shard_map/ppermute | solution.py:43
  66.2 11.6 %collective-permute-start.19 = (bf16[14,16,512]{2,1,0:T(8,128)(2,1)S(1)}, bf16[14,16,512]{2,1,0:T(8,128)(2,1)S(1)}, u32[]{:S(2)}, u32[]{:S(2)}) collective-permute-start(bf16[14,16,512]{2,1,0:T(8,128)(2,1)S(1)} %get-tuple-element.154), channel_id=1, source_target_pairs={{0,4},{1,5},{2,6},{3,7},{4,8},{5,9},{6,10},{7,11},{8,12},{9,13},{1... | collective-permute-start | bytes 688136 | tf_op jit(solution)/shard_map/ppermute | solution.py:51
  66.3 11.5 %collective-permute-start.20 = (bf16[14,16,512]{2,1,0:T(8,128)(2,1)S(1)}, bf16[14,16,512]{2,1,0:T(8,128)(2,1)S(1)}, u32[]{:S(2)}, u32[]{:S(2)}) collective-permute-start(bf16[14,16,512]{2,1,0:T(8,128)(2,1)S(1)} %get-tuple-element.155), channel_id=1, source_target_pairs={{0,12},{1,13},{2,14},{3,15},{4,0},{5,1},{6,2},{7,3},{8,4},{9,5},{1... | collective-permute-start | bytes 688136 | tf_op jit(solution)/shard_map/ppermute | solution.py:51
  69.5 8.3 %collective-permute-start.17 = (bf16[13,16,512]{2,1,0:T(8,128)(2,1)S(1)}, bf16[13,16,512]{2,1,0:T(8,128)(2,1)S(1)}, u32[]{:S(2)}, u32[]{:S(2)}) collective-permute-start(bf16[13,16,512]{2,1,0:T(8,128)(2,1)S(1)} %get-tuple-element.152), channel_id=1, source_target_pairs={{0,32},{16,48},{32,64},{48,80},{64,96},{80,112},{96,0},{112,16},{1... | collective-permute-start | bytes 638984 | tf_op jit(solution)/shard_map/ppermute | solution.py:56
  69.9 7.9 %collective-permute-start.18 = (bf16[13,16,512]{2,1,0:T(8,128)(2,1)S(1)}, bf16[13,16,512]{2,1,0:T(8,128)(2,1)S(1)}, u32[]{:S(2)}, u32[]{:S(2)}) collective-permute-start(bf16[13,16,512]{2,1,0:T(8,128)(2,1)S(1)} %get-tuple-element.153), channel_id=1, source_target_pairs={{0,96},{16,112},{32,0},{48,16},{64,32},{80,48},{96,64},{112,80},{1... | collective-permute-start | bytes 638984 | tf_op jit(solution)/shard_map/ppermute | solution.py:56
  78.1 5.5 %collective-permute-start.24 = (bf16[13,8,512]{2,1,0:T(8,128)(2,1)S(1)}, bf16[13,8,512]{2,1,0:T(8,128)(2,1)S(1)}, u32[]{:S(2)}, u32[]{:S(2)}) collective-permute-start(bf16[13,8,512]{2,1,0:T(8,128)(2,1)S(1)} %get-tuple-element.167), channel_id=1, source_target_pairs={{0,12},{1,13},{2,14},{3,15},{4,0},{5,1},{6,2},{7,3},{8,4},{9,5},{1... | collective-permute-start | bytes 319496 | tf_op jit(solution)/shard_map/ppermute | solution.py:51
  79.6 6.4 %collective-permute-start.23 = (bf16[13,8,512]{2,1,0:T(8,128)(2,1)S(1)}, bf16[13,8,512]{2,1,0:T(8,128)(2,1)S(1)}, u32[]{:S(2)}, u32[]{:S(2)}) collective-permute-start(bf16[13,8,512]{2,1,0:T(8,128)(2,1)S(1)} %get-tuple-element.166), channel_id=1, source_target_pairs={{0,8},{1,9},{2,10},{3,11},{4,12},{5,13},{6,14},{7,15},{8,0},{9,1},... | collective-permute-start | bytes 319496 | tf_op jit(solution)/shard_map/ppermute | solution.py:51
  79.6 7.3 %collective-permute-start.22 = (bf16[13,8,512]{2,1,0:T(8,128)(2,1)S(1)}, bf16[13,8,512]{2,1,0:T(8,128)(2,1)S(1)}, u32[]{:S(2)}, u32[]{:S(2)}) collective-permute-start(bf16[13,8,512]{2,1,0:T(8,128)(2,1)S(1)} %get-tuple-element.165), channel_id=1, source_target_pairs={{0,4},{1,5},{2,6},{3,7},{4,8},{5,9},{6,10},{7,11},{8,12},{9,13},{1... | collective-permute-start | bytes 319496 | tf_op jit(solution)/shard_map/ppermute | solution.py:51
  80.7 6.5 %collective-permute-start.27 = (bf16[14,8,512]{2,1,0:T(8,128)(2,1)S(1)}, bf16[14,8,512]{2,1,0:T(8,128)(2,1)S(1)}, u32[]{:S(2)}, u32[]{:S(2)}) collective-permute-start(bf16[14,8,512]{2,1,0:T(8,128)(2,1)S(1)} %get-tuple-element.171), channel_id=1, source_target_pairs={{0,96},{16,112},{32,0},{48,16},{64,32},{80,48},{96,64},{112,80},{1... | collective-permute-start | bytes 344072 | tf_op jit(solution)/shard_map/ppermute | solution.py:56
  83.7 6.4 %collective-permute-start.26 = (bf16[14,8,512]{2,1,0:T(8,128)(2,1)S(1)}, bf16[14,8,512]{2,1,0:T(8,128)(2,1)S(1)}, u32[]{:S(2)}, u32[]{:S(2)}) collective-permute-start(bf16[14,8,512]{2,1,0:T(8,128)(2,1)S(1)} %get-tuple-element.170), channel_id=1, source_target_pairs={{0,64},{16,80},{32,96},{48,112},{64,0},{80,16},{96,32},{112,48},{1... | collective-permute-start | bytes 344072 | tf_op jit(solution)/shard_map/ppermute | solution.py:56
  83.7 7.2 %collective-permute-start.25 = (bf16[14,8,512]{2,1,0:T(8,128)(2,1)S(1)}, bf16[14,8,512]{2,1,0:T(8,128)(2,1)S(1)}, u32[]{:S(2)}, u32[]{:S(2)}) collective-permute-start(bf16[14,8,512]{2,1,0:T(8,128)(2,1)S(1)} %get-tuple-element.169), channel_id=1, source_target_pairs={{0,32},{16,48},{32,64},{48,80},{64,96},{80,112},{96,0},{112,16},{1... | collective-permute-start | bytes 344072 | tf_op jit(solution)/shard_map/ppermute | solution.py:56
  91.0 19.3 %copy-start = (bf16[4,8,16,512]{3,2,1,0:T(8,128)(2,1)S(1)}, bf16[4,8,16,512]{3,2,1,0:T(8,128)(2,1)}, u32[]{:S(2)}) copy-start(bf16[4,8,16,512]{3,2,1,0:T(8,128)(2,1)} %pre.1) | copy-start | bytes 1572868
  91.0 9.6 %collective-permute-start.28 = (bf16[27,8,512]{2,1,0:T(8,128)(2,1)S(1)}, bf16[27,8,512]{2,1,0:T(8,128)(2,1)S(1)}, u32[]{:S(2)}, u32[]{:S(2)}) collective-permute-start(bf16[27,8,512]{2,1,0:T(8,128)(2,1)S(1)} %pad_maximum_fusion), channel_id=1, source_target_pairs={{0,16},{16,0},{32,48},{48,32},{64,80},{80,64},{96,112},{112,96},{1... | collective-permute-start | bytes 663560 | tf_op jit(solution)/shard_map/ppermute | solution.py:468
  100.6 9.7 %collective-permute-start.29 = (bf16[4,8,16,512]{3,2,1,0:T(8,128)(2,1)S(1)}, bf16[4,8,16,512]{3,2,1,0:T(8,128)(2,1)S(1)}, u32[]{:S(2)}, u32[]{:S(2)}) collective-permute-start(bf16[4,8,16,512]{3,2,1,0:T(8,128)(2,1)S(1)} %fusion.4), channel_id=1, source_target_pairs={{0,2},{1,3},{2,0},{3,1},{4,6},{5,7},{6,4},{7,5},{8,10},{9,11},{10,... | collective-permute-start | bytes 1572872 | tf_op jit(solution)/shard_map/ppermute | solution.py:43
  100.7 15.5 %collective-permute-start.31 = (f32[14,8,512]{2,1,0:T(8,128)S(1)}, f32[14,8,512]{2,1,0:T(8,128)S(1)}, u32[]{:S(2)}, u32[]{:S(2)}) collective-permute-start(f32[14,8,512]{2,1,0:T(8,128)S(1)} %get-tuple-element.177.refs_1_), channel_id=1, source_target_pairs={{0,32},{16,48},{32,64},{48,80},{64,96},{80,112},{96,0},{112,16},{1... | collective-permute-start | bytes 688136 | tf_op jit(solution)/shard_map/ppermute | solution.py:56
  100.8 6.6 %collective-permute-start.33 = (bf16[14,8,512]{2,1,0:T(8,128)(2,1)S(1)}, bf16[14,8,512]{2,1,0:T(8,128)(2,1)S(1)}, u32[]{:S(2)}, u32[]{:S(2)}) collective-permute-start(bf16[14,8,512]{2,1,0:T(8,128)(2,1)S(1)} %get-tuple-element.184), channel_id=1, source_target_pairs={{0,96},{16,112},{32,0},{48,16},{64,32},{80,48},{96,64},{112,80},{1... | collective-permute-start | bytes 344072 | tf_op jit(solution)/shard_map/ppermute | solution.py:56
  104.1 6.2 %collective-permute-start.30 = (bf16[13,8,512]{2,1,0:T(8,128)(2,1)S(1)}, bf16[13,8,512]{2,1,0:T(8,128)(2,1)S(1)}, u32[]{:S(2)}, u32[]{:S(2)}) collective-permute-start(bf16[13,8,512]{2,1,0:T(8,128)(2,1)S(1)} %get-tuple-element.186), channel_id=1, source_target_pairs={{0,32},{16,48},{32,64},{48,80},{64,96},{80,112},{96,0},{112,16},{1... | collective-permute-start | bytes 319496 | tf_op jit(solution)/shard_map/ppermute | solution.py:56
  104.2 7.3 %collective-permute-start.32 = (f32[13,8,512]{2,1,0:T(8,128)S(1)}, f32[13,8,512]{2,1,0:T(8,128)S(1)}, u32[]{:S(2)}, u32[]{:S(2)}) collective-permute-start(f32[13,8,512]{2,1,0:T(8,128)S(1)} %get-tuple-element.176.refs_0_), channel_id=1, source_target_pairs={{0,96},{16,112},{32,0},{48,16},{64,32},{80,48},{96,64},{112,80},{1... | collective-permute-start | bytes 638984 | tf_op jit(solution)/shard_map/ppermute | solution.py:56
  107.4 8.8 %collective-permute-start.35 = (bf16[14,8,512]{2,1,0:T(8,128)(2,1)S(1)}, bf16[14,8,512]{2,1,0:T(8,128)(2,1)S(1)}, u32[]{:S(2)}, u32[]{:S(2)}) collective-permute-start(bf16[14,8,512]{2,1,0:T(8,128)(2,1)S(1)} %collective-permute-done.33.refs_5_), channel_id=1, source_target_pairs={{0,96},{16,112},{32,0},{48,16},{64,32},{80,48},{96,64},{112,80},{1... | collective-permute-start | bytes 344072 | tf_op jit(solution)/shard_map/ppermute | solution.py:56
  110.3 5.9 %collective-permute-start.34 = (bf16[13,8,512]{2,1,0:T(8,128)(2,1)S(1)}, bf16[13,8,512]{2,1,0:T(8,128)(2,1)S(1)}, u32[]{:S(2)}, u32[]{:S(2)}) collective-permute-start(bf16[13,8,512]{2,1,0:T(8,128)(2,1)S(1)} %collective-permute-done.30.refs_2_), channel_id=1, source_target_pairs={{0,32},{16,48},{32,64},{48,80},{64,96},{80,112},{96,0},{112,16},{1... | collective-permute-start | bytes 319496 | tf_op jit(solution)/shard_map/ppermute | solution.py:56

commit v15 on v13

--- a/solution.py
+++ b/solution.py
@@ -126,7 +126,7 @@
     )(*quarters)
 
 
-def turn_kernel(p0, p1, p2, p3, even, odd, held, out):
+def turn(p0, p1, p2, p3, even, odd, held, out):
     j, x = quad_place(), x_place()
     is_odd = lax.rem(lax.axis_index("gx"), 2) == 1
     for k, p in enumerate((p0, p1, p2, p3)):
@@ -167,23 +167,6 @@
             out[at:at + q] = v.astype(BF16)
 
 
-def turn(quarters, even, odd):
-    rows, width, depth, q = quarters[0].shape
-    width += 2
-    tall = QUAD * (rows - 1) + 2
-    return pl.pallas_call(
-        turn_kernel,
-        out_shape=[
-            jax.ShapeDtypeStruct((tall, width, depth, q), BF16),
-            jax.ShapeDtypeStruct((9 * q, tall * (width - 2) * depth), BF16),
-        ],
-        in_specs=[VMEM] * (QUAD + 2),
-        out_specs=[VMEM] * 2,
-        compiler_params=params(),
-        cost_estimate=small_cost(),
-    )(*quarters, even, odd)
-
-
 def run_copies(pairs, sem):
     copies = [pltpu.make_async_copy(s, d, sem.at[n]) for n, (s, d) in enumerate(pairs)]
     for c in copies:
@@ -191,14 +174,17 @@
     return copies
 
 
-def weight_kernel(norm, own_act, near, far, across, cot, *refs):
-    groups, held, sem = (refs[:5], refs[5:10]), *refs[10:]
+def weight_kernel(norm, own_act, near, far, across, *refs):
+    quarters, cells_out, groups = refs[:6], refs[6], (refs[7:12], refs[12:17])
+    held, cot, sem = refs[17:]
     j = quad_place()
     rows, width, depth, chan = own_act.shape
     pairs = []
     for k, piece in enumerate((own_act, near, far, across)):
         pairs.append((piece, held.at[pl.ds((j ^ k) * rows, rows)]))
-    for c in run_copies(pairs, sem):
+    copies = run_copies(pairs, sem)
+    turn(*quarters, cells_out, cot)
+    for c in copies:
         c.wait()
     row = width * depth
     cells = QUAD * rows * row
@@ -230,11 +216,12 @@
             own[1, tap] = block(0, 1)
 
 
-def weight_terms(norm, acts, cot):
+def weight_terms(norm, acts, quarters):
     rows, width, depth, chan = acts[0].shape
     q = chan // QUAD
     cells = QUAD * rows * width * depth
-    shapes = []
+    tall = QUAD * rows + 2
+    shapes = [jax.ShapeDtypeStruct((tall, width + 2, depth, q), BF16)]
     for taps in (XTAPS, 27 - XTAPS):
         shape = (taps, q // RING // 2, chan)
         shapes += [jax.ShapeDtypeStruct((2,) + shape, BF16)] * 2
@@ -243,17 +230,18 @@
     return pl.pallas_call(
         functools.partial(weight_kernel, norm),
         out_shape=shapes,
-        in_specs=[ANY] * 4 + [VMEM],
-        out_specs=[VMEM] * 10,
+        in_specs=[ANY] * 4 + [VMEM] * 6,
+        out_specs=[VMEM] * 11,
         scratch_shapes=[
             pltpu.VMEM((QUAD * rows, width, depth, chan), BF16),
+            pltpu.VMEM((9 * q, tall * width * depth), BF16),
             pltpu.SemaphoreType.DMA((4,)),
         ],
         compiler_params=params(),
         cost_estimate=pl.CostEstimate(
             flops=2 * 27 * q * cells * chan, bytes_accessed=10_000_000, transcendentals=0
         ),
-    )(*acts, cot)
+    )(*acts, *quarters)
 
 
 def input_kernel(held, own, above, across_low, across_high, below, *refs):
@@ -436,9 +424,8 @@
     even, odd, above, below = barrier((even, odd, above, below))
     taps = XTAPS
     parts = [weight, above, along_y(below[:taps], 1, True), along_y(above[taps:], -1, True), below]
-    held, turned = turn(quarters, even, odd)
-
-    terms = weight_terms(norm, acts, turned)
+
+    held, *terms = weight_terms(norm, acts, [*quarters, even, odd])
     held, terms = barrier((held, terms))
     xup, xdown, xkeep_up, xkeep_down, xown = terms[:5]
     yup, ydown, ykeep_up, ykeep_down, yown = terms[5:]

time: 119 us -> 123 us (1.034)
  starting transfers between devices: 54.5 us -> 60.7 us
  waiting for transfers between devices: 36.6 us -> 34.2 us
    ppermute x13, starting transfers between devices: 24.2 us -> 28.6 us  [along_x(): lax.ppermute(block, 'gx', [(g, (g + 2 * step) % count) for g in range(cou...]
    ppermute x11, waiting for transfers between devices: 3.49 us -> 0.03 us  [along_y(): lax.ppermute(block, 'gy', [(s, t) for s, t in pairs if 0 <= t < count])]
    pallas_call x1, Pallas kernels: 7.66 us -> 9.64 us  [weight_terms(): pl.pallas_call(functools.partial(weight_kernel, norm), out_shape=shapes,...]
    pallas_call x1 -> x0, Pallas kernels: 1.82 us -> none  [turn(): pl.pallas_call(turn_kernel, out_shape=[jax.ShapeDtypeStruct((tall, width,...]
    ppermute x11, starting transfers between devices: 20.8 us -> 22.5 us  [along_y(): lax.ppermute(block, 'gy', [(s, t) for s, t in pairs if 0 <= t < count])]
    ppermute x13, waiting for transfers between devices: 13.9 us -> 15.6 us  [along_x(): lax.ppermute(block, 'gx', [(g, (g + 2 * step) % count) for g in range(cou...]
  transfers between devices with their start and end apart: 36 -> 36, of which waited for: 14 -> 11; matrix products, arithmetic and copies ran while one was open for 1% -> 1% of each run, Pallas kernels for 17% -> 17%
where the time goes in v15:
time: 123 us; the launch traced here: 122 us
  starting transfers between devices  60.7 us (49%)
  waiting for transfers between devices  34.2 us (28%)
  Pallas kernels  22.4 us (18%)
  other arithmetic  2.99 us (2%)
    ppermute x13, starting transfers between devices, along_x(): lax.ppermute(block, 'gx', [(g, (g + 2 * step) % count) for g in range(cou...  28.6 us
    ppermute x11, starting transfers between devices, along_y(): lax.ppermute(block, 'gy', [(s, t) for s, t in pairs if 0 <= t < count])  22.5 us
    ppermute x13, waiting for transfers between devices, along_x(): lax.ppermute(block, 'gx', [(g, (g + 2 * step) % count) for g in range(cou...  15.6 us
    pallas_call x1, Pallas kernels, weight_terms(): pl.pallas_call(functools.partial(weight_kernel, norm), out_shape=shapes,...  9.64 us
    pallas_call x1, Pallas kernels, input_terms(): pl.pallas_call(input_kernel, out_shape=[jax.ShapeDtypeStruct((2,) + block...  8.65 us
    ppermute x1, waiting for transfers between devices, body(): other = lax.ppermute(mine, 'gx', [(g, g ^ 1) for g in range(count)])  8.64 us
    ppermute x8, waiting for transfers between devices, swap(): return lax.ppermute(block, 'gy', [(g, g ^ k) for g in range(count)])  8.01 us
    ppermute x8, starting transfers between devices, swap(): return lax.ppermute(block, 'gy', [(g, g ^ k) for g in range(count)])  4.49 us
  transfers between devices with their start and end apart: 36, of which 11 were waited for; matrix products, arithmetic and copies ran while one was open for 1% of the time, Pallas kernels for 17%

profile of v15, /device:TPU:0, one launch (start us, length us, event | category | flops | bytes accessed | tf_op | source)
XLA Modules:
  0.0 122.3 jit_solution(4882551373390279898)
XLA Ops:
  0.6 1.4 %fusion.3.own_act = bf16[4,8,16,512]{3,2,1,0:T(8,128)(2,1)S(1)} fusion(bf16[4,8,16,512]{3,2,1,0:T(8,128)(2,1)} %pre.1), kind=kLoop, calls=%fused_computation.5 | loop fusion | flops 1572864 | bytes 1048576 | tf_op jit(solution)/shard_map/convert_element_type | solution.py:410
  2.2 2.1 %collective-permute-start.5 = (bf16[4,8,16,512]{3,2,1,0:T(8,128)(2,1)S(1)}, bf16[4,8,16,512]{3,2,1,0:T(8,128)(2,1)S(1)}, u32[]{:S(2)}, u32[]{:S(2)}) collective-permute-start(bf16[4,8,16,512]{3,2,1,0:T(8,128)(2,1)S(1)} %fusion.3.own_act), channel_id=1, source_target_pairs={{0,2},{1,3},{2,0},{3,1},{4,6},{5,7},{6,4},{7,5},{8,10},{9,11},{10,... | collective-permute-start | bytes 1572872 | tf_op jit(solution)/shard_map/ppermute | solution.py:43
  4.3 1.0 select_bitcast_fusion
  5.2 0.7 collective-permute-start
  5.9 1.0 copy-done.1
  7.0 0.7 shard_map.50
  7.7 0.3 shard_map.51
  8.0 7.6 %collective-permute-start.10 = (bf16[27,32,512]{2,1,0:T(8,128)(2,1)S(1)}, bf16[27,32,512]{2,1,0:T(8,128)(2,1)S(1)}, u32[]{:S(2)}, u32[]{:S(2)}) collective-permute-start(bf16[27,32,512]{2,1,0:T(8,128)(2,1)S(1)} %copy-done.2), channel_id=1, source_target_pairs={{0,4},{1,5},{2,6},{3,7},{4,8},{5,9},{6,10},{7,11},{8,12},{9,13},{1... | collective-permute-start | bytes 2654216 | tf_op jit(solution)/shard_map/ppermute | solution.py:51
  15.6 1.5 %collective-permute-start.9 = (bf16[27,32,512]{2,1,0:T(8,128)(2,1)S(1)}, bf16[27,32,512]{2,1,0:T(8,128)(2,1)S(1)}, u32[]{:S(2)}, u32[]{:S(2)}) collective-permute-start(bf16[27,32,512]{2,1,0:T(8,128)(2,1)S(1)} %copy-done.2), channel_id=1, source_target_pairs={{0,12},{1,13},{2,14},{3,15},{4,0},{5,1},{6,2},{7,3},{8,4},{9,5},{1... | collective-permute-start | bytes 2654216 | tf_op jit(solution)/shard_map/ppermute | solution.py:51
  17.1 0.3 collective-permute-done.5.far
  17.4 1.7 %collective-permute-start.4 = (bf16[5,8,16,128]{3,2,1,0:T(8,128)(2,1)S(1)}, bf16[5,8,16,128]{3,2,1,0:T(8,128)(2,1)S(1)}, u32[]{:S(2)}, u32[]{:S(2)}) collective-permute-start(bf16[5,8,16,128]{3,2,1,0:T(8,128)(2,1)S(1)} %get-tuple-element.98), channel_id=1, source_target_pairs={{0,3},{1,2},{2,1},{3,0},{4,7},{5,6},{6,5},{7,4},{8,11},{9,10},{10,... | collective-permute-start | bytes 491528 | tf_op jit(solution)/shard_map/ppermute | solution.py:43
  19.2 5.0 %collective-permute-done.3.p2.refs_2_ = bf16[5,8,16,128]{3,2,1,0:T(8,128)(2,1)S(1)} collective-permute-done((bf16[5,8,16,128]{3,2,1,0:T(8,128)(2,1)S(1)}, bf16[5,8,16,128]{3,2,1,0:T(8,128)(2,1)S(1)}, u32[]{:S(2)}, u32[]{:S(2)}) %collective-permute-start.3) | collective-permute-done | bytes 163872 | tf_op jit(solution)/shard_map/ppermute | solution.py:43
  24.1 2.7 %collective-permute-done.4.p3.refs_3_ = bf16[5,8,16,128]{3,2,1,0:T(8,128)(2,1)S(1)} collective-permute-done((bf16[5,8,16,128]{3,2,1,0:T(8,128)(2,1)S(1)}, bf16[5,8,16,128]{3,2,1,0:T(8,128)(2,1)S(1)}, u32[]{:S(2)}, u32[]{:S(2)}) %collective-permute-start.4) | collective-permute-done | bytes 163872 | tf_op jit(solution)/shard_map/ppermute | solution.py:43
  26.9 0.5 collective-permute-start.6
  27.4 3.4 %collective-permute-start.7 = (bf16[4,5,16,128]{3,2,1,0:T(8,128)(2,1)S(1)}, bf16[4,5,16,128]{3,2,1,0:T(8,128)(2,1)S(1)}, u32[]{:S(2)}, u32[]{:S(2)}) collective-permute-start(bf16[4,5,16,128]{3,2,1,0:T(8,128)(2,1)S(1)} %get-tuple-element.104), channel_id=1, source_target_pairs={{0,16},{32,48},{64,80},{96,112},{16,0},{48,32},{80,64},{112,96},{1... | collective-permute-start | bytes 245768 | tf_op jit(solution)/shard_map/ppermute | solution.py:62
  30.9 0.7 collective-permute-start.8
  31.5 2.0 %collective-permute-done.7.refs_4_ = bf16[4,5,16,128]{3,2,1,0:T(8,128)(2,1)S(1)} collective-permute-done((bf16[4,5,16,128]{3,2,1,0:T(8,128)(2,1)S(1)}, bf16[4,5,16,128]{3,2,1,0:T(8,128)(2,1)S(1)}, u32[]{:S(2)}, u32[]{:S(2)}) %collective-permute-start.7) | collective-permute-done | bytes 81952 | tf_op jit(solution)/shard_map/ppermute | solution.py:62
  33.5 0.6 collective-permute-start.11
  34.1 2.8 %collective-permute-start.12 = (bf16[14,32,512]{2,1,0:T(8,128)(2,1)S(1)}, bf16[14,32,512]{2,1,0:T(8,128)(2,1)S(1)}, u32[]{:S(2)}, u32[]{:S(2)}) collective-permute-start(bf16[14,32,512]{2,1,0:T(8,128)(2,1)S(1)} %slice.24), channel_id=1, source_target_pairs={{0,12},{1,13},{2,14},{3,15},{4,0},{5,1},{6,2},{7,3},{8,4},{9,5},{1... | collective-permute-start | bytes 1376264 | tf_op jit(solution)/shard_map/ppermute | solution.py:51
  36.9 9.6 %shard_map.53 = (bf16[18,10,16,128]{3,2,1,0:T(8,128)(2,1)S(1)}, bf16[2,13,16,512]{3,2,1,0:T(8,128)(2,1)S(1)}, bf16[2,13,16,512]{3,2,1,0:T(8,128)(2,1)S(1)}, f32[...) custom-call(bf16[4,8,16,512]{3,2,1,0:T(8,128)(2,1)S(1)} %fusion.3.ow, ...), custom_call_target="tpu_custom_call" | custom-call | flops 7247757312 | bytes 10000000 | tf_op jit(solution)/shard_map/pallas_call | solution.py:230
  46.6 7.7 %collective-permute-start.13 = (bf16[2,13,16,512]{3,2,1,0:T(8,128)(2,1)S(1)}, bf16[2,13,16,512]{3,2,1,0:T(8,128)(2,1)S(1)}, u32[]{:S(2)}, u32[]{:S(2)}) collective-permute-start(bf16[2,13,16,512]{3,2,1,0:T(8,128)(2,1)S(1)} %get-tuple-element.115), channel_id=1, source_target_pairs={{0,32},{16,48},{32,64},{48,80},{64,96},{80,112},{96,0},{112,16},{1... | collective-permute-start | bytes 1277960 | tf_op jit(solution)/shard_map/ppermute | solution.py:56
  54.2 1.5 %collective-permute-start.14 = (bf16[2,13,16,512]{3,2,1,0:T(8,128)(2,1)S(1)}, bf16[2,13,16,512]{3,2,1,0:T(8,128)(2,1)S(1)}, u32[]{:S(2)}, u32[]{:S(2)}) collective-permute-start(bf16[2,13,16,512]{3,2,1,0:T(8,128)(2,1)S(1)} %get-tuple-element.116), channel_id=1, source_target_pairs={{0,96},{16,112},{32,0},{48,16},{64,32},{80,48},{96,64},{112,80},{1... | collective-permute-start | bytes 1277960 | tf_op jit(solution)/shard_map/ppermute | solution.py:56
  55.8 3.2 %collective-permute-start.16 = (bf16[2,14,16,512]{3,2,1,0:T(8,128)(2,1)S(1)}, bf16[2,14,16,512]{3,2,1,0:T(8,128)(2,1)S(1)}, u32[]{:S(2)}, u32[]{:S(2)}) collective-permute-start(bf16[2,14,16,512]{3,2,1,0:T(8,128)(2,1)S(1)} %get-tuple-element.118), channel_id=1, source_target_pairs={{0,12},{1,13},{2,14},{3,15},{4,0},{5,1},{6,2},{7,3},{8,4},{9,5},{1... | collective-permute-start | bytes 1376264 | tf_op jit(solution)/shard_map/ppermute | solution.py:51
  59.0 8.6 %shard_map.54 = (f32[2,4,8,16,512]{4,3,2,1,0:T(8,128)S(1)}, f32[4,8,16,512]{3,2,1,0:T(8,128)S(1)}, f32[4,8,16,512]{3,2,1,0:T(8,128)S(1)}) custom-call(bf16[18,10,16,128]{3,2,1,0:T(8,128)(2,1)S(1)} %get-tuple-element.109.held, bf16[27,32,512]{2,1,0:T(8,128)(2,1)S(1)} %copy-done.2, bf16[27,32,512]{2,1,0:T(8,128)(2,1)S(1)} %collective-permute-done.9.above, ...), custom_call_target="tpu_custom_call" | custom-call | flops 10192158720 | bytes 10000000 | tf_op jit(solution)/shard_map/pallas_call | solution.py:293
  67.8 0.2 shard_map.55
  68.1 3.2 %collective-permute-start.20 = (bf16[14,16,512]{2,1,0:T(8,128)(2,1)S(1)}, bf16[14,16,512]{2,1,0:T(8,128)(2,1)S(1)}, u32[]{:S(2)}, u32[]{:S(2)}) collective-permute-start(bf16[14,16,512]{2,1,0:T(8,128)(2,1)S(1)} %get-tuple-element.131), channel_id=1, source_target_pairs={{0,12},{1,13},{2,14},{3,15},{4,0},{5,1},{6,2},{7,3},{8,4},{9,5},{1... | collective-permute-start | bytes 688136 | tf_op jit(solution)/shard_map/ppermute | solution.py:51
  71.3 0.5 collective-permute-start.17
  71.8 2.7 %collective-permute-start.18 = (bf16[13,16,512]{2,1,0:T(8,128)(2,1)S(1)}, bf16[13,16,512]{2,1,0:T(8,128)(2,1)S(1)}, u32[]{:S(2)}, u32[]{:S(2)}) collective-permute-start(bf16[13,16,512]{2,1,0:T(8,128)(2,1)S(1)} %get-tuple-element.129), channel_id=1, source_target_pairs={{0,96},{16,112},{32,0},{48,16},{64,32},{80,48},{96,64},{112,80},{1... | collective-permute-start | bytes 638984 | tf_op jit(solution)/shard_map/ppermute | solution.py:56
  74.5 5.1 %collective-permute-done.17.refs_3_ = bf16[13,16,512]{2,1,0:T(8,128)(2,1)S(1)} collective-permute-done((bf16[13,16,512]{2,1,0:T(8,128)(2,1)S(1)}, bf16[13,16,512]{2,1,0:T(8,128)(2,1)S(1)}, u32[]{:S(2)}, u32[]{:S(2)}) %collective-permute-start.17) | collective-permute-done | bytes 213024 | tf_op jit(solution)/shard_map/ppermute | solution.py:56
  79.6 0.3 shard_map.56
  80.0 2.5 %collective-permute-start.23 = (bf16[13,8,512]{2,1,0:T(8,128)(2,1)S(1)}, bf16[13,8,512]{2,1,0:T(8,128)(2,1)S(1)}, u32[]{:S(2)}, u32[]{:S(2)}) collective-permute-start(bf16[13,8,512]{2,1,0:T(8,128)(2,1)S(1)} %get-tuple-element.142), channel_id=1, source_target_pairs={{0,8},{1,9},{2,10},{3,11},{4,12},{5,13},{6,14},{7,15},{8,0},{9,1},... | collective-permute-start | bytes 319496 | tf_op jit(solution)/shard_map/ppermute | solution.py:51
  82.5 0.9 collective-permute-start.24
  83.4 0.3 collective-permute-start.25
  83.7 4.1 %collective-permute-start.26 = (bf16[14,8,512]{2,1,0:T(8,128)(2,1)S(1)}, bf16[14,8,512]{2,1,0:T(8,128)(2,1)S(1)}, u32[]{:S(2)}, u32[]{:S(2)}) collective-permute-start(bf16[14,8,512]{2,1,0:T(8,128)(2,1)S(1)} %get-tuple-element.146), channel_id=1, source_target_pairs={{0,64},{16,80},{32,96},{48,112},{64,0},{80,16},{96,32},{112,48},{1... | collective-permute-start | bytes 344072 | tf_op jit(solution)/shard_map/ppermute | solution.py:56
  87.8 2.2 %collective-permute-start.27 = (bf16[14,8,512]{2,1,0:T(8,128)(2,1)S(1)}, bf16[14,8,512]{2,1,0:T(8,128)(2,1)S(1)}, u32[]{:S(2)}, u32[]{:S(2)}) collective-permute-start(bf16[14,8,512]{2,1,0:T(8,128)(2,1)S(1)} %get-tuple-element.147), channel_id=1, source_target_pairs={{0,96},{16,112},{32,0},{48,16},{64,32},{80,48},{96,64},{112,80},{1... | collective-permute-start | bytes 344072 | tf_op jit(solution)/shard_map/ppermute | solution.py:56
  90.1 0.2 collective-permute-done.25
  90.3 1.5 %collective-permute-done.26 = bf16[14,8,512]{2,1,0:T(8,128)(2,1)S(1)} collective-permute-done((bf16[14,8,512]{2,1,0:T(8,128)(2,1)S(1)}, bf16[14,8,512]{2,1,0:T(8,128)(2,1)S(1)}, u32[]{:S(2)}, u32[]{:S(2)}) %collective-permute-start.26) | collective-permute-done | bytes 114720 | tf_op jit(solution)/shard_map/ppermute | solution.py:56
  91.8 0.8 collective-permute-done.27
  92.7 0.3 collective-permute-start.28
  93.1 0.3 fusion.4
  93.3 8.6 %collective-permute-done.28 = bf16[27,8,512]{2,1,0:T(8,128)(2,1)S(1)} collective-permute-done((bf16[27,8,512]{2,1,0:T(8,128)(2,1)S(1)}, bf16[27,8,512]{2,1,0:T(8,128)(2,1)S(1)}, u32[]{:S(2)}, u32[]{:S(2)}) %collective-permute-start.28) | collective-permute-done | bytes 221216 | tf_op jit(solution)/shard_map/ppermute | solution.py:455
  102.0 3.5 %collective-permute-start.33 = (bf16[14,8,512]{2,1,0:T(8,128)(2,1)S(1)}, bf16[14,8,512]{2,1,0:T(8,128)(2,1)S(1)}, u32[]{:S(2)}, u32[]{:S(2)}) collective-permute-start(bf16[14,8,512]{2,1,0:T(8,128)(2,1)S(1)} %get-tuple-element.160), channel_id=1, source_target_pairs={{0,96},{16,112},{32,0},{48,16},{64,32},{80,48},{96,64},{112,80},{1... | collective-permute-start | bytes 344072 | tf_op jit(solution)/shard_map/ppermute | solution.py:56
  105.7 3.3 %collective-permute-start.32 = (f32[13,8,512]{2,1,0:T(8,128)S(1)}, f32[13,8,512]{2,1,0:T(8,128)S(1)}, u32[]{:S(2)}, u32[]{:S(2)}) collective-permute-start(f32[13,8,512]{2,1,0:T(8,128)S(1)} %get-tuple-element.152.refs_0_), channel_id=1, source_target_pairs={{0,96},{16,112},{32,0},{48,16},{64,32},{80,48},{96,64},{112,80},{1... | collective-permute-start | bytes 638984 | tf_op jit(solution)/shard_map/ppermute | solution.py:56
  109.0 2.7 %collective-permute-start.35 = (bf16[14,8,512]{2,1,0:T(8,128)(2,1)S(1)}, bf16[14,8,512]{2,1,0:T(8,128)(2,1)S(1)}, u32[]{:S(2)}, u32[]{:S(2)}) collective-permute-start(bf16[14,8,512]{2,1,0:T(8,128)(2,1)S(1)} %collective-permute-done.33.refs_5_), channel_id=1, source_target_pairs={{0,96},{16,112},{32,0},{48,16},{64,32},{80,48},{96,64},{112,80},{1... | collective-permute-start | bytes 344072 | tf_op jit(solution)/shard_map/ppermute | solution.py:56
  111.7 3.3 %collective-permute-done.30.refs_2_ = bf16[13,8,512]{2,1,0:T(8,128)(2,1)S(1)} collective-permute-done((bf16[13,8,512]{2,1,0:T(8,128)(2,1)S(1)}, bf16[13,8,512]{2,1,0:T(8,128)(2,1)S(1)}, u32[]{:S(2)}, u32[]{:S(2)}) %collective-permute-start.30) | collective-permute-done | bytes 106528 | tf_op jit(solution)/shard_map/ppermute | solution.py:56
  115.1 1.2 %shard_map.57 = bf16[4,8,16,512]{3,2,1,0:T(8,128)(2,1)} custom-call(bf16[4,8,16,512]{3,2,1,0:T(8,128)(2,1)S(1)} %copy-done, f32[4,8,16,512]{3,2,1,0:T(8,128)S(1)} %get-tuple-element.119.keep, f32[2,4,8,16,512]{4,3,2,1,0:T(8,128)S(1)} %collective-permute-done.21.near, bf16[4,8,16,512]{3,2,1,0:T(8,128)(2,1)S(1)} %collective-permute-done.29.far), custom_call_target="tpu_custom_call" | custom-call | tf_op jit(solution)/shard_map/pallas_call | solution.py:318
  116.3 4.7 %collective-permute-done.34.refs_6_ = bf16[13,8,512]{2,1,0:T(8,128)(2,1)S(1)} collective-permute-done((bf16[13,8,512]{2,1,0:T(8,128)(2,1)S(1)}, bf16[13,8,512]{2,1,0:T(8,128)(2,1)S(1)}, u32[]{:S(2)}, u32[]{:S(2)}) %collective-permute-start.34) | collective-permute-done | bytes 106528 | tf_op jit(solution)/shard_map/ppermute | solution.py:56
  121.0 1.3 %shard_map.58 = f32[27,32,512]{2,1,0:T(8,128)} custom-call(f32[13,8,512]{2,1,0:T(8,128)S(1)} %get-tuple-element.152.refs_0_, f32[14,8,512]{2,1,0:T(8,128)S(1)} %get-tuple-element.153.refs_1_, bf16[13,8,512]{2,1,0:T(8,128)(2,1)S(1)} %collective-permute-done.30.refs_2_, f32[14,8,512]{2,1,0:T(8,128)S(1)} %collective-permute-done.31.refs_3_, ...), custom_call_target="tpu_custom_call" | custom-call | tf_op jit(solution)/shard_map/pallas_call | solution.py:391
  (49 shorter events, 0.9 us)
Async XLA Ops:
  0.6 7.4 %copy-start.2 = (bf16[27,32,512]{2,1,0:T(8,128)(2,1)S(1)}, bf16[27,32,512]{2,1,0:T(8,128)(2,1)}, u32[]{:S(2)}) copy-start(bf16[27,32,512]{2,1,0:T(8,128)(2,1)} %own) | copy-start | bytes 2654212
  2.1 5.6 %collective-permute-start.1 = (bf16[4,8,16,512]{3,2,1,0:T(8,128)(2,1)S(1)}, bf16[4,8,16,512]{3,2,1,0:T(8,128)(2,1)S(1)}, u32[]{:S(2)}, u32[]{:S(2)}) collective-permute-start(bf16[4,8,16,512]{3,2,1,0:T(8,128)(2,1)S(1)} %fusion.3.own_act), channel_id=1, source_target_pairs={{0,1},{1,0},{2,3},{3,2},{4,5},{5,4},{6,7},{7,6},{8,9},{9,8},{10,11... | collective-permute-start | bytes 1572872 | tf_op jit(solution)/shard_map/ppermute | solution.py:43
  2.2 15.3 %collective-permute-start.5 = (bf16[4,8,16,512]{3,2,1,0:T(8,128)(2,1)S(1)}, bf16[4,8,16,512]{3,2,1,0:T(8,128)(2,1)S(1)}, u32[]{:S(2)}, u32[]{:S(2)}) collective-permute-start(bf16[4,8,16,512]{3,2,1,0:T(8,128)(2,1)S(1)} %fusion.3.own_act), channel_id=1, source_target_pairs={{0,2},{1,3},{2,0},{3,1},{4,6},{5,7},{6,4},{7,5},{8,10},{9,11},{10,... | collective-permute-start | bytes 1572872 | tf_op jit(solution)/shard_map/ppermute | solution.py:43
  5.2 2.4 %collective-permute-start = (bf16[8,16,512]{2,1,0:T(8,128)(2,1)S(1)}, bf16[8,16,512]{2,1,0:T(8,128)(2,1)S(1)}, u32[]{:S(2)}, u32[]{:S(2)}) collective-permute-start(bf16[8,16,512]{2,1,0:T(8,128)(2,1)S(1)} %select_bitcast_fusion), channel_id=1, source_target_pairs={{3,4},{7,8},{11,12},{4,3},{8,7},{12,11},{19,20},{23,24},{27,28},{2... | collective-permute-start | bytes 393224 | tf_op jit(solution)/shard_map/ppermute | solution.py:409
  5.9 1.0 copy-start.1
  8.0 25.4 %collective-permute-start.10 = (bf16[27,32,512]{2,1,0:T(8,128)(2,1)S(1)}, bf16[27,32,512]{2,1,0:T(8,128)(2,1)S(1)}, u32[]{:S(2)}, u32[]{:S(2)}) collective-permute-start(bf16[27,32,512]{2,1,0:T(8,128)(2,1)S(1)} %copy-done.2), channel_id=1, source_target_pairs={{0,4},{1,5},{2,6},{3,7},{4,8},{5,9},{6,10},{7,11},{8,12},{9,13},{1... | collective-permute-start | bytes 2654216 | tf_op jit(solution)/shard_map/ppermute | solution.py:51
  15.6 17.9 %collective-permute-start.9 = (bf16[27,32,512]{2,1,0:T(8,128)(2,1)S(1)}, bf16[27,32,512]{2,1,0:T(8,128)(2,1)S(1)}, u32[]{:S(2)}, u32[]{:S(2)}) collective-permute-start(bf16[27,32,512]{2,1,0:T(8,128)(2,1)S(1)} %copy-done.2), channel_id=1, source_target_pairs={{0,12},{1,13},{2,14},{3,15},{4,0},{5,1},{6,2},{7,3},{8,4},{9,5},{1... | collective-permute-start | bytes 2654216 | tf_op jit(solution)/shard_map/ppermute | solution.py:51
  17.1 2.0 %collective-permute-start.2 = (bf16[5,8,16,128]{3,2,1,0:T(8,128)(2,1)S(1)}, bf16[5,8,16,128]{3,2,1,0:T(8,128)(2,1)S(1)}, u32[]{:S(2)}, u32[]{:S(2)}) collective-permute-start(bf16[5,8,16,128]{3,2,1,0:T(8,128)(2,1)S(1)} %get-tuple-element.96), channel_id=1, source_target_pairs={{0,1},{1,0},{2,3},{3,2},{4,5},{5,4},{6,7},{7,6},{8,9},{9,8},{10,11... | collective-permute-start | bytes 491528 | tf_op jit(solution)/shard_map/ppermute | solution.py:43
  17.1 7.0 %collective-permute-start.3 = (bf16[5,8,16,128]{3,2,1,0:T(8,128)(2,1)S(1)}, bf16[5,8,16,128]{3,2,1,0:T(8,128)(2,1)S(1)}, u32[]{:S(2)}, u32[]{:S(2)}) collective-permute-start(bf16[5,8,16,128]{3,2,1,0:T(8,128)(2,1)S(1)} %get-tuple-element.97), channel_id=1, source_target_pairs={{0,2},{1,3},{2,0},{3,1},{4,6},{5,7},{6,4},{7,5},{8,10},{9,11},{10,... | collective-permute-start | bytes 491528 | tf_op jit(solution)/shard_map/ppermute | solution.py:43
  17.4 9.4 %collective-permute-start.4 = (bf16[5,8,16,128]{3,2,1,0:T(8,128)(2,1)S(1)}, bf16[5,8,16,128]{3,2,1,0:T(8,128)(2,1)S(1)}, u32[]{:S(2)}, u32[]{:S(2)}) collective-permute-start(bf16[5,8,16,128]{3,2,1,0:T(8,128)(2,1)S(1)} %get-tuple-element.98), channel_id=1, source_target_pairs={{0,3},{1,2},{2,1},{3,0},{4,7},{5,6},{6,5},{7,4},{8,11},{9,10},{10,... | collective-permute-start | bytes 491528 | tf_op jit(solution)/shard_map/ppermute | solution.py:43
  26.9 10.1 %collective-permute-start.6 = (bf16[4,8,16,512]{3,2,1,0:T(8,128)(2,1)S(1)}, bf16[4,8,16,512]{3,2,1,0:T(8,128)(2,1)S(1)}, u32[]{:S(2)}, u32[]{:S(2)}) collective-permute-start(bf16[4,8,16,512]{3,2,1,0:T(8,128)(2,1)S(1)} %collective-permute-done.5.far), channel_id=1, source_target_pairs={{0,1},{1,0},{2,3},{3,2},{4,5},{5,4},{6,7},{7,6},{8,9},{9,8},{10,11... | collective-permute-start | bytes 1572872 | tf_op jit(solution)/shard_map/ppermute | solution.py:43
  27.4 6.1 %collective-permute-start.7 = (bf16[4,5,16,128]{3,2,1,0:T(8,128)(2,1)S(1)}, bf16[4,5,16,128]{3,2,1,0:T(8,128)(2,1)S(1)}, u32[]{:S(2)}, u32[]{:S(2)}) collective-permute-start(bf16[4,5,16,128]{3,2,1,0:T(8,128)(2,1)S(1)} %get-tuple-element.104), channel_id=1, source_target_pairs={{0,16},{32,48},{64,80},{96,112},{16,0},{48,32},{80,64},{112,96},{1... | collective-permute-start | bytes 245768 | tf_op jit(solution)/shard_map/ppermute | solution.py:62
  30.9 2.6 %collective-permute-start.8 = (bf16[4,5,16,128]{3,2,1,0:T(8,128)(2,1)S(1)}, bf16[4,5,16,128]{3,2,1,0:T(8,128)(2,1)S(1)}, u32[]{:S(2)}, u32[]{:S(2)}) collective-permute-start(bf16[4,5,16,128]{3,2,1,0:T(8,128)(2,1)S(1)} %get-tuple-element.105), channel_id=1, source_target_pairs={{16,32},{48,64},{80,96},{32,16},{64,48},{96,80},{17,33},{49,65},{8... | collective-permute-start | bytes 245768 | tf_op jit(solution)/shard_map/ppermute | solution.py:62
  33.5 22.3 %collective-permute-start.11 = (bf16[13,32,512]{2,1,0:T(8,128)(2,1)S(1)}, bf16[13,32,512]{2,1,0:T(8,128)(2,1)S(1)}, u32[]{:S(2)}, u32[]{:S(2)}) collective-permute-start(bf16[13,32,512]{2,1,0:T(8,128)(2,1)S(1)} %slice.23), channel_id=1, source_target_pairs={{0,4},{1,5},{2,6},{3,7},{4,8},{5,9},{6,10},{7,11},{8,12},{9,13},{1... | collective-permute-start | bytes 1277960 | tf_op jit(solution)/shard_map/ppermute | solution.py:51
  34.1 24.9 %collective-permute-start.12 = (bf16[14,32,512]{2,1,0:T(8,128)(2,1)S(1)}, bf16[14,32,512]{2,1,0:T(8,128)(2,1)S(1)}, u32[]{:S(2)}, u32[]{:S(2)}) collective-permute-start(bf16[14,32,512]{2,1,0:T(8,128)(2,1)S(1)} %slice.24), channel_id=1, source_target_pairs={{0,12},{1,13},{2,14},{3,15},{4,0},{5,1},{6,2},{7,3},{8,4},{9,5},{1... | collective-permute-start | bytes 1376264 | tf_op jit(solution)/shard_map/ppermute | solution.py:51
  46.6 21.1 %collective-permute-start.13 = (bf16[2,13,16,512]{3,2,1,0:T(8,128)(2,1)S(1)}, bf16[2,13,16,512]{3,2,1,0:T(8,128)(2,1)S(1)}, u32[]{:S(2)}, u32[]{:S(2)}) collective-permute-start(bf16[2,13,16,512]{3,2,1,0:T(8,128)(2,1)S(1)} %get-tuple-element.115), channel_id=1, source_target_pairs={{0,32},{16,48},{32,64},{48,80},{64,96},{80,112},{96,0},{112,16},{1... | collective-permute-start | bytes 1277960 | tf_op jit(solution)/shard_map/ppermute | solution.py:56
  54.2 13.4 %collective-permute-start.14 = (bf16[2,13,16,512]{3,2,1,0:T(8,128)(2,1)S(1)}, bf16[2,13,16,512]{3,2,1,0:T(8,128)(2,1)S(1)}, u32[]{:S(2)}, u32[]{:S(2)}) collective-permute-start(bf16[2,13,16,512]{3,2,1,0:T(8,128)(2,1)S(1)} %get-tuple-element.116), channel_id=1, source_target_pairs={{0,96},{16,112},{32,0},{48,16},{64,32},{80,48},{96,64},{112,80},{1... | collective-permute-start | bytes 1277960 | tf_op jit(solution)/shard_map/ppermute | solution.py:56
  55.8 11.9 %collective-permute-start.15 = (bf16[2,14,16,512]{3,2,1,0:T(8,128)(2,1)S(1)}, bf16[2,14,16,512]{3,2,1,0:T(8,128)(2,1)S(1)}, u32[]{:S(2)}, u32[]{:S(2)}) collective-permute-start(bf16[2,14,16,512]{3,2,1,0:T(8,128)(2,1)S(1)} %get-tuple-element.117), channel_id=1, source_target_pairs={{0,4},{1,5},{2,6},{3,7},{4,8},{5,9},{6,10},{7,11},{8,12},{9,13},{1... | collective-permute-start | bytes 1376264 | tf_op jit(solution)/shard_map/ppermute | solution.py:51
  55.8 11.9 %collective-permute-start.16 = (bf16[2,14,16,512]{3,2,1,0:T(8,128)(2,1)S(1)}, bf16[2,14,16,512]{3,2,1,0:T(8,128)(2,1)S(1)}, u32[]{:S(2)}, u32[]{:S(2)}) collective-permute-start(bf16[2,14,16,512]{3,2,1,0:T(8,128)(2,1)S(1)} %get-tuple-element.118), channel_id=1, source_target_pairs={{0,12},{1,13},{2,14},{3,15},{4,0},{5,1},{6,2},{7,3},{8,4},{9,5},{1... | collective-permute-start | bytes 1376264 | tf_op jit(solution)/shard_map/ppermute | solution.py:51
  67.7 11.9 %collective-permute-start.21 = (f32[2,4,8,16,512]{4,3,2,1,0:T(8,128)S(1)}, f32[2,4,8,16,512]{4,3,2,1,0:T(8,128)S(1)}, u32[]{:S(2)}, u32[]{:S(2)}) collective-permute-start(f32[2,4,8,16,512]{4,3,2,1,0:T(8,128)S(1)} %get-tuple-element.132), channel_id=1, source_target_pairs={{0,1},{1,0},{2,3},{3,2},{4,5},{5,4},{6,7},{7,6},{8,9},{9,8},{10,11... | collective-permute-start | bytes 6291464 | tf_op jit(solution)/shard_map/ppermute | solution.py:43
  68.0 11.6 %collective-permute-start.19 = (bf16[14,16,512]{2,1,0:T(8,128)(2,1)S(1)}, bf16[14,16,512]{2,1,0:T(8,128)(2,1)S(1)}, u32[]{:S(2)}, u32[]{:S(2)}) collective-permute-start(bf16[14,16,512]{2,1,0:T(8,128)(2,1)S(1)} %get-tuple-element.130), channel_id=1, source_target_pairs={{0,4},{1,5},{2,6},{3,7},{4,8},{5,9},{6,10},{7,11},{8,12},{9,13},{1... | collective-permute-start | bytes 688136 | tf_op jit(solution)/shard_map/ppermute | solution.py:51
  68.1 11.5 %collective-permute-start.20 = (bf16[14,16,512]{2,1,0:T(8,128)(2,1)S(1)}, bf16[14,16,512]{2,1,0:T(8,128)(2,1)S(1)}, u32[]{:S(2)}, u32[]{:S(2)}) collective-permute-start(bf16[14,16,512]{2,1,0:T(8,128)(2,1)S(1)} %get-tuple-element.131), channel_id=1, source_target_pairs={{0,12},{1,13},{2,14},{3,15},{4,0},{5,1},{6,2},{7,3},{8,4},{9,5},{1... | collective-permute-start | bytes 688136 | tf_op jit(solution)/shard_map/ppermute | solution.py:51
  71.3 8.3 %collective-permute-start.17 = (bf16[13,16,512]{2,1,0:T(8,128)(2,1)S(1)}, bf16[13,16,512]{2,1,0:T(8,128)(2,1)S(1)}, u32[]{:S(2)}, u32[]{:S(2)}) collective-permute-start(bf16[13,16,512]{2,1,0:T(8,128)(2,1)S(1)} %get-tuple-element.128), channel_id=1, source_target_pairs={{0,32},{16,48},{32,64},{48,80},{64,96},{80,112},{96,0},{112,16},{1... | collective-permute-start | bytes 638984 | tf_op jit(solution)/shard_map/ppermute | solution.py:56
  71.8 7.8 %collective-permute-start.18 = (bf16[13,16,512]{2,1,0:T(8,128)(2,1)S(1)}, bf16[13,16,512]{2,1,0:T(8,128)(2,1)S(1)}, u32[]{:S(2)}, u32[]{:S(2)}) collective-permute-start(bf16[13,16,512]{2,1,0:T(8,128)(2,1)S(1)} %get-tuple-element.129), channel_id=1, source_target_pairs={{0,96},{16,112},{32,0},{48,16},{64,32},{80,48},{96,64},{112,80},{1... | collective-permute-start | bytes 638984 | tf_op jit(solution)/shard_map/ppermute | solution.py:56
  79.9 7.9 %collective-permute-start.22 = (bf16[13,8,512]{2,1,0:T(8,128)(2,1)S(1)}, bf16[13,8,512]{2,1,0:T(8,128)(2,1)S(1)}, u32[]{:S(2)}, u32[]{:S(2)}) collective-permute-start(bf16[13,8,512]{2,1,0:T(8,128)(2,1)S(1)} %get-tuple-element.141), channel_id=1, source_target_pairs={{0,4},{1,5},{2,6},{3,7},{4,8},{5,9},{6,10},{7,11},{8,12},{9,13},{1... | collective-permute-start | bytes 319496 | tf_op jit(solution)/shard_map/ppermute | solution.py:51
  80.0 10.1 %collective-permute-start.23 = (bf16[13,8,512]{2,1,0:T(8,128)(2,1)S(1)}, bf16[13,8,512]{2,1,0:T(8,128)(2,1)S(1)}, u32[]{:S(2)}, u32[]{:S(2)}) collective-permute-start(bf16[13,8,512]{2,1,0:T(8,128)(2,1)S(1)} %get-tuple-element.142), channel_id=1, source_target_pairs={{0,8},{1,9},{2,10},{3,11},{4,12},{5,13},{6,14},{7,15},{8,0},{9,1},... | collective-permute-start | bytes 319496 | tf_op jit(solution)/shard_map/ppermute | solution.py:51
  82.5 7.5 %collective-permute-start.24 = (bf16[13,8,512]{2,1,0:T(8,128)(2,1)S(1)}, bf16[13,8,512]{2,1,0:T(8,128)(2,1)S(1)}, u32[]{:S(2)}, u32[]{:S(2)}) collective-permute-start(bf16[13,8,512]{2,1,0:T(8,128)(2,1)S(1)} %get-tuple-element.143), channel_id=1, source_target_pairs={{0,12},{1,13},{2,14},{3,15},{4,0},{5,1},{6,2},{7,3},{8,4},{9,5},{1... | collective-permute-start | bytes 319496 | tf_op jit(solution)/shard_map/ppermute | solution.py:51
  83.4 6.9 %collective-permute-start.25 = (bf16[14,8,512]{2,1,0:T(8,128)(2,1)S(1)}, bf16[14,8,512]{2,1,0:T(8,128)(2,1)S(1)}, u32[]{:S(2)}, u32[]{:S(2)}) collective-permute-start(bf16[14,8,512]{2,1,0:T(8,128)(2,1)S(1)} %get-tuple-element.145), channel_id=1, source_target_pairs={{0,32},{16,48},{32,64},{48,80},{64,96},{80,112},{96,0},{112,16},{1... | collective-permute-start | bytes 344072 | tf_op jit(solution)/shard_map/ppermute | solution.py:56
  83.7 8.1 %collective-permute-start.26 = (bf16[14,8,512]{2,1,0:T(8,128)(2,1)S(1)}, bf16[14,8,512]{2,1,0:T(8,128)(2,1)S(1)}, u32[]{:S(2)}, u32[]{:S(2)}) collective-permute-start(bf16[14,8,512]{2,1,0:T(8,128)(2,1)S(1)} %get-tuple-element.146), channel_id=1, source_target_pairs={{0,64},{16,80},{32,96},{48,112},{64,0},{80,16},{96,32},{112,48},{1... | collective-permute-start | bytes 344072 | tf_op jit(solution)/shard_map/ppermute | solution.py:56
  87.8 4.8 %collective-permute-start.27 = (bf16[14,8,512]{2,1,0:T(8,128)(2,1)S(1)}, bf16[14,8,512]{2,1,0:T(8,128)(2,1)S(1)}, u32[]{:S(2)}, u32[]{:S(2)}) collective-permute-start(bf16[14,8,512]{2,1,0:T(8,128)(2,1)S(1)} %get-tuple-element.147), channel_id=1, source_target_pairs={{0,96},{16,112},{32,0},{48,16},{64,32},{80,48},{96,64},{112,80},{1... | collective-permute-start | bytes 344072 | tf_op jit(solution)/shard_map/ppermute | solution.py:56
  92.7 22.4 %copy-start = (bf16[4,8,16,512]{3,2,1,0:T(8,128)(2,1)S(1)}, bf16[4,8,16,512]{3,2,1,0:T(8,128)(2,1)}, u32[]{:S(2)}) copy-start(bf16[4,8,16,512]{3,2,1,0:T(8,128)(2,1)} %pre.1) | copy-start | bytes 1572868
  92.7 9.2 %collective-permute-start.28 = (bf16[27,8,512]{2,1,0:T(8,128)(2,1)S(1)}, bf16[27,8,512]{2,1,0:T(8,128)(2,1)S(1)}, u32[]{:S(2)}, u32[]{:S(2)}) collective-permute-start(bf16[27,8,512]{2,1,0:T(8,128)(2,1)S(1)} %pad_maximum_fusion), channel_id=1, source_target_pairs={{0,16},{16,0},{32,48},{48,32},{64,80},{80,64},{96,112},{112,96},{1... | collective-permute-start | bytes 663560 | tf_op jit(solution)/shard_map/ppermute | solution.py:455
  102.0 13.1 %collective-permute-start.29 = (bf16[4,8,16,512]{3,2,1,0:T(8,128)(2,1)S(1)}, bf16[4,8,16,512]{3,2,1,0:T(8,128)(2,1)S(1)}, u32[]{:S(2)}, u32[]{:S(2)}) collective-permute-start(bf16[4,8,16,512]{3,2,1,0:T(8,128)(2,1)S(1)} %fusion.4), channel_id=1, source_target_pairs={{0,2},{1,3},{2,0},{3,1},{4,6},{5,7},{6,4},{7,5},{8,10},{9,11},{10,... | collective-permute-start | bytes 1572872 | tf_op jit(solution)/shard_map/ppermute | solution.py:43
  102.0 7.0 %collective-permute-start.33 = (bf16[14,8,512]{2,1,0:T(8,128)(2,1)S(1)}, bf16[14,8,512]{2,1,0:T(8,128)(2,1)S(1)}, u32[]{:S(2)}, u32[]{:S(2)}) collective-permute-start(bf16[14,8,512]{2,1,0:T(8,128)(2,1)S(1)} %get-tuple-element.160), channel_id=1, source_target_pairs={{0,96},{16,112},{32,0},{48,16},{64,32},{80,48},{96,64},{112,80},{1... | collective-permute-start | bytes 344072 | tf_op jit(solution)/shard_map/ppermute | solution.py:56
  105.6 15.4 %collective-permute-start.31 = (f32[14,8,512]{2,1,0:T(8,128)S(1)}, f32[14,8,512]{2,1,0:T(8,128)S(1)}, u32[]{:S(2)}, u32[]{:S(2)}) collective-permute-start(f32[14,8,512]{2,1,0:T(8,128)S(1)} %get-tuple-element.153.refs_1_), channel_id=1, source_target_pairs={{0,32},{16,48},{32,64},{48,80},{64,96},{80,112},{96,0},{112,16},{1... | collective-permute-start | bytes 688136 | tf_op jit(solution)/shard_map/ppermute | solution.py:56
  105.6 9.4 %collective-permute-start.30 = (bf16[13,8,512]{2,1,0:T(8,128)(2,1)S(1)}, bf16[13,8,512]{2,1,0:T(8,128)(2,1)S(1)}, u32[]{:S(2)}, u32[]{:S(2)}) collective-permute-start(bf16[13,8,512]{2,1,0:T(8,128)(2,1)S(1)} %get-tuple-element.162), channel_id=1, source_target_pairs={{0,32},{16,48},{32,64},{48,80},{64,96},{80,112},{96,0},{112,16},{1... | collective-permute-start | bytes 319496 | tf_op jit(solution)/shard_map/ppermute | solution.py:56
  105.7 15.3 %collective-permute-start.32 = (f32[13,8,512]{2,1,0:T(8,128)S(1)}, f32[13,8,512]{2,1,0:T(8,128)S(1)}, u32[]{:S(2)}, u32[]{:S(2)}) collective-permute-start(f32[13,8,512]{2,1,0:T(8,128)S(1)} %get-tuple-element.152.refs_0_), channel_id=1, source_target_pairs={{0,96},{16,112},{32,0},{48,16},{64,32},{80,48},{96,64},{112,80},{1... | collective-permute-start | bytes 638984 | tf_op jit(solution)/shard_map/ppermute | solution.py:56
  109.0 12.0 %collective-permute-start.35 = (bf16[14,8,512]{2,1,0:T(8,128)(2,1)S(1)}, bf16[14,8,512]{2,1,0:T(8,128)(2,1)S(1)}, u32[]{:S(2)}, u32[]{:S(2)}) collective-permute-start(bf16[14,8,512]{2,1,0:T(8,128)(2,1)S(1)} %collective-permute-done.33.refs_5_), channel_id=1, source_target_pairs={{0,96},{16,112},{32,0},{48,16},{64,32},{80,48},{96,64},{112,80},{1... | collective-permute-start | bytes 344072 | tf_op jit(solution)/shard_map/ppermute | solution.py:56
  115.1 5.9 %collective-permute-start.34 = (bf16[13,8,512]{2,1,0:T(8,128)(2,1)S(1)}, bf16[13,8,512]{2,1,0:T(8,128)(2,1)S(1)}, u32[]{:S(2)}, u32[]{:S(2)}) collective-permute-start(bf16[13,8,512]{2,1,0:T(8,128)(2,1)S(1)} %collective-permute-done.30.refs_2_), channel_id=1, source_target_pairs={{0,32},{16,48},{32,64},{48,80},{64,96},{80,112},{96,0},{112,16},{1... | collective-permute-start | bytes 319496 | tf_op jit(solution)/shard_map/ppermute | solution.py:56

commit v16 on v13

--- a/solution.py
+++ b/solution.py
@@ -10,7 +10,7 @@
 
 QUAD = 4
 RING = 4
-XTAPS = 13
+XTAPS = 14
 F32 = jnp.float32
 BF16 = jnp.bfloat16
 ANY = pl.BlockSpec(memory_space=pl.ANY)

time: 119 us -> 119 us (level)
  waiting for transfers between devices: 36.6 us -> 35.3 us
    ppermute x13, waiting for transfers between devices: 13.9 us -> 5.57 us  [along_x(): lax.ppermute(block, 'gx', [(g, (g + 2 * step) % count) for g in range(cou...]
    ppermute x11, waiting for transfers between devices: 3.49 us -> 10.4 us  [along_y(): lax.ppermute(block, 'gy', [(s, t) for s, t in pairs if 0 <= t < count])]
  transfers between devices with their start and end apart: 36 -> 36, of which waited for: 14 -> 14; matrix products, arithmetic and copies ran while one was open for 1% -> 1% of each run, Pallas kernels for 17% -> 18%
where the time goes in v16:
time: 119 us; the launch traced here: 118 us
  starting transfers between devices  55.3 us (46%)
  waiting for transfers between devices  35.3 us (30%)
  Pallas kernels  22.2 us (19%)
  other arithmetic  2.97 us (2%)
    ppermute x13, starting transfers between devices, along_x(): lax.ppermute(block, 'gx', [(g, (g + 2 * step) % count) for g in range(cou...  23.9 us
    ppermute x11, starting transfers between devices, along_y(): lax.ppermute(block, 'gy', [(s, t) for s, t in pairs if 0 <= t < count])  21.9 us
    ppermute x11, waiting for transfers between devices, along_y(): lax.ppermute(block, 'gy', [(s, t) for s, t in pairs if 0 <= t < count])  10.4 us
    ppermute x1, waiting for transfers between devices, body(): other = lax.ppermute(mine, 'gx', [(g, g ^ 1) for g in range(count)])  9.24 us
    pallas_call x1, Pallas kernels, input_terms(): pl.pallas_call(input_kernel, out_shape=[jax.ShapeDtypeStruct((2,) + block...  8.7 us
    ppermute x8, waiting for transfers between devices, swap(): return lax.ppermute(block, 'gy', [(g, g ^ k) for g in range(count)])  8.14 us
    pallas_call x1, Pallas kernels, weight_terms(): pl.pallas_call(functools.partial(weight_kernel, norm), out_shape=shapes,...  7.66 us
    ppermute x13, waiting for transfers between devices, along_x(): lax.ppermute(block, 'gx', [(g, (g + 2 * step) % count) for g in range(cou...  5.57 us
  transfers between devices with their start and end apart: 36, of which 14 were waited for; matrix products, arithmetic and copies ran while one was open for 1% of the time, Pallas kernels for 18%

profile of v16, /device:TPU:0, one launch (start us, length us, event | category | flops | bytes accessed | tf_op | source)
XLA Modules:
  0.0 117.8 jit_solution(18338560756692273979)
XLA Ops:
  0.6 1.4 %fusion.3.own_act = bf16[4,8,16,512]{3,2,1,0:T(8,128)(2,1)S(1)} fusion(bf16[4,8,16,512]{3,2,1,0:T(8,128)(2,1)} %pre.1), kind=kLoop, calls=%fused_computation.5 | loop fusion | flops 1572864 | bytes 1048576 | tf_op jit(solution)/shard_map/convert_element_type | solution.py:422
  2.2 2.1 %collective-permute-start.5 = (bf16[4,8,16,512]{3,2,1,0:T(8,128)(2,1)S(1)}, bf16[4,8,16,512]{3,2,1,0:T(8,128)(2,1)S(1)}, u32[]{:S(2)}, u32[]{:S(2)}) collective-permute-start(bf16[4,8,16,512]{3,2,1,0:T(8,128)(2,1)S(1)} %fusion.3.own_act), channel_id=1, source_target_pairs={{0,2},{1,3},{2,0},{3,1},{4,6},{5,7},{6,4},{7,5},{8,10},{9,11},{10,... | collective-permute-start | bytes 1572872 | tf_op jit(solution)/shard_map/ppermute | solution.py:43
  4.3 1.0 select_bitcast_fusion
  5.2 0.7 collective-permute-start
  5.9 1.0 copy-done.1
  7.0 0.7 shard_map.50
  8.0 8.3 %collective-permute-start.8 = (bf16[27,32,512]{2,1,0:T(8,128)(2,1)S(1)}, bf16[27,32,512]{2,1,0:T(8,128)(2,1)S(1)}, u32[]{:S(2)}, u32[]{:S(2)}) collective-permute-start(bf16[27,32,512]{2,1,0:T(8,128)(2,1)S(1)} %copy-done.2), channel_id=1, source_target_pairs={{0,12},{1,13},{2,14},{3,15},{4,0},{5,1},{6,2},{7,3},{8,4},{9,5},{1... | collective-permute-start | bytes 2654216 | tf_op jit(solution)/shard_map/ppermute | solution.py:51
  16.3 1.2 %collective-permute-done.5.far = bf16[4,8,16,512]{3,2,1,0:T(8,128)(2,1)S(1)} collective-permute-done((bf16[4,8,16,512]{3,2,1,0:T(8,128)(2,1)S(1)}, bf16[4,8,16,512]{3,2,1,0:T(8,128)(2,1)S(1)}, u32[]{:S(2)}, u32[]{:S(2)}) %collective-permute-start.5) | collective-permute-done | bytes 524320 | tf_op jit(solution)/shard_map/ppermute | solution.py:43
  17.6 1.6 %collective-permute-start.4 = (bf16[5,8,16,128]{3,2,1,0:T(8,128)(2,1)S(1)}, bf16[5,8,16,128]{3,2,1,0:T(8,128)(2,1)S(1)}, u32[]{:S(2)}, u32[]{:S(2)}) collective-permute-start(bf16[5,8,16,128]{3,2,1,0:T(8,128)(2,1)S(1)} %get-tuple-element.109), channel_id=1, source_target_pairs={{0,3},{1,2},{2,1},{3,0},{4,7},{5,6},{6,5},{7,4},{8,11},{9,10},{10,... | collective-permute-start | bytes 491528 | tf_op jit(solution)/shard_map/ppermute | solution.py:43
  19.2 4.2 %collective-permute-done.3.p2 = bf16[5,8,16,128]{3,2,1,0:T(8,128)(2,1)S(1)} collective-permute-done((bf16[5,8,16,128]{3,2,1,0:T(8,128)(2,1)S(1)}, bf16[5,8,16,128]{3,2,1,0:T(8,128)(2,1)S(1)}, u32[]{:S(2)}, u32[]{:S(2)}) %collective-permute-start.3) | collective-permute-done | bytes 163872 | tf_op jit(solution)/shard_map/ppermute | solution.py:43
  23.3 2.7 %collective-permute-done.4.p3 = bf16[5,8,16,128]{3,2,1,0:T(8,128)(2,1)S(1)} collective-permute-done((bf16[5,8,16,128]{3,2,1,0:T(8,128)(2,1)S(1)}, bf16[5,8,16,128]{3,2,1,0:T(8,128)(2,1)S(1)}, u32[]{:S(2)}, u32[]{:S(2)}) %collective-permute-start.4) | collective-permute-done | bytes 163872 | tf_op jit(solution)/shard_map/ppermute | solution.py:43
  26.1 0.5 collective-permute-start.10
  26.6 3.4 %collective-permute-start.6 = (bf16[4,5,16,128]{3,2,1,0:T(8,128)(2,1)S(1)}, bf16[4,5,16,128]{3,2,1,0:T(8,128)(2,1)S(1)}, u32[]{:S(2)}, u32[]{:S(2)}) collective-permute-start(bf16[4,5,16,128]{3,2,1,0:T(8,128)(2,1)S(1)} %get-tuple-element.114), channel_id=1, source_target_pairs={{0,16},{32,48},{64,80},{96,112},{16,0},{48,32},{80,64},{112,96},{1... | collective-permute-start | bytes 245768 | tf_op jit(solution)/shard_map/ppermute | solution.py:62
  30.0 0.7 collective-permute-start.7
  30.7 2.0 %collective-permute-done.6.even = bf16[4,5,16,128]{3,2,1,0:T(8,128)(2,1)S(1)} collective-permute-done((bf16[4,5,16,128]{3,2,1,0:T(8,128)(2,1)S(1)}, bf16[4,5,16,128]{3,2,1,0:T(8,128)(2,1)S(1)}, u32[]{:S(2)}, u32[]{:S(2)}) %collective-permute-start.6) | collective-permute-done | bytes 81952 | tf_op jit(solution)/shard_map/ppermute | solution.py:62
  32.7 1.1 collective-permute-done.9.below
  33.9 3.3 %collective-permute-start.12 = (bf16[13,32,512]{2,1,0:T(8,128)(2,1)S(1)}, bf16[13,32,512]{2,1,0:T(8,128)(2,1)S(1)}, u32[]{:S(2)}, u32[]{:S(2)}) collective-permute-start(bf16[13,32,512]{2,1,0:T(8,128)(2,1)S(1)} %slice.24), channel_id=1, source_target_pairs={{0,12},{1,13},{2,14},{3,15},{4,0},{5,1},{6,2},{7,3},{8,4},{9,5},{1... | collective-permute-start | bytes 1277960 | tf_op jit(solution)/shard_map/ppermute | solution.py:51
  37.2 1.8 %shard_map.53 = (bf16[18,10,16,128]{3,2,1,0:T(8,128)(2,1)S(1)}, bf16[1152,2304]{1,0:T(8,128)(2,1)S(1)}) custom-call(bf16[5,8,16,128]{3,2,1,0:T(8,128)(2,1)S(1)} %get-tuple-element.110.p0, bf16[5,8,16,128]{3,2,1,0:T(8,128)(2,1)S(1)} %collective-permute-done.2.p1, bf16[5,8,16,128]{3,2,1,0:T(8,128)(2,1)S(1)} %collective-permute-done.3.p2, ...), custom_call_target="tpu_custom_call" | custom-call | flops 1000 | bytes 1000 | tf_op jit(solution)/shard_map/pallas_call | solution.py:174
  39.1 7.7 %shard_map.54 = (bf16[2,14,16,512]{3,2,1,0:T(8,128)(2,1)S(1)}, bf16[2,14,16,512]{3,2,1,0:T(8,128)(2,1)S(1)}, f32[14,16,512]{2,1,0:T(8,128)S(1)}, f32[14,16,512]{...) custom-call(bf16[4,8,16,512]{3,2,1,0:T(8,128)(2,1)S(1)} %fusion.3.ow, ...), custom_call_target="tpu_custom_call" | custom-call | flops 7247757312 | bytes 10000000 | tf_op jit(solution)/shard_map/pallas_call | solution.py:243
  46.7 6.6 %collective-permute-start.13 = (bf16[2,14,16,512]{3,2,1,0:T(8,128)(2,1)S(1)}, bf16[2,14,16,512]{3,2,1,0:T(8,128)(2,1)S(1)}, u32[]{:S(2)}, u32[]{:S(2)}) collective-permute-start(bf16[2,14,16,512]{3,2,1,0:T(8,128)(2,1)S(1)} %get-tuple-element.139), channel_id=1, source_target_pairs={{0,32},{16,48},{32,64},{48,80},{64,96},{80,112},{96,0},{112,16},{1... | collective-permute-start | bytes 1376264 | tf_op jit(solution)/shard_map/ppermute | solution.py:56
  53.3 1.3 %collective-permute-start.14 = (bf16[2,14,16,512]{3,2,1,0:T(8,128)(2,1)S(1)}, bf16[2,14,16,512]{3,2,1,0:T(8,128)(2,1)S(1)}, u32[]{:S(2)}, u32[]{:S(2)}) collective-permute-start(bf16[2,14,16,512]{3,2,1,0:T(8,128)(2,1)S(1)} %get-tuple-element.140), channel_id=1, source_target_pairs={{0,96},{16,112},{32,0},{48,16},{64,32},{80,48},{96,64},{112,80},{1... | collective-permute-start | bytes 1376264 | tf_op jit(solution)/shard_map/ppermute | solution.py:56
  54.6 3.2 %collective-permute-start.16 = (bf16[2,13,16,512]{3,2,1,0:T(8,128)(2,1)S(1)}, bf16[2,13,16,512]{3,2,1,0:T(8,128)(2,1)S(1)}, u32[]{:S(2)}, u32[]{:S(2)}) collective-permute-start(bf16[2,13,16,512]{3,2,1,0:T(8,128)(2,1)S(1)} %get-tuple-element.142), channel_id=1, source_target_pairs={{0,12},{1,13},{2,14},{3,15},{4,0},{5,1},{6,2},{7,3},{8,4},{9,5},{1... | collective-permute-start | bytes 1277960 | tf_op jit(solution)/shard_map/ppermute | solution.py:51
  57.9 8.7 %shard_map.55 = (f32[2,4,8,16,512]{4,3,2,1,0:T(8,128)S(1)}, f32[4,8,16,512]{3,2,1,0:T(8,128)S(1)}, f32[4,8,16,512]{3,2,1,0:T(8,128)S(1)}) custom-call(bf16[18,10,16,128]{3,2,1,0:T(8,128)(2,1)S(1)} %get-tuple-element.133.held, bf16[27,32,512]{2,1,0:T(8,128)(2,1)S(1)} %copy-done.2, bf16[27,32,512]{2,1,0:T(8,128)(2,1)S(1)} %collective-permute-done.8.above, ...), custom_call_target="tpu_custom_call" | custom-call | flops 10192158720 | bytes 10000000 | tf_op jit(solution)/shard_map/pallas_call | solution.py:305
  66.9 0.8 collective-permute-start.17
  67.6 2.6 %collective-permute-start.18 = (bf16[14,16,512]{2,1,0:T(8,128)(2,1)S(1)}, bf16[14,16,512]{2,1,0:T(8,128)(2,1)S(1)}, u32[]{:S(2)}, u32[]{:S(2)}) collective-permute-start(bf16[14,16,512]{2,1,0:T(8,128)(2,1)S(1)} %get-tuple-element.153), channel_id=1, source_target_pairs={{0,96},{16,112},{32,0},{48,16},{64,32},{80,48},{96,64},{112,80},{1... | collective-permute-start | bytes 688136 | tf_op jit(solution)/shard_map/ppermute | solution.py:56
  70.2 3.2 %collective-permute-start.20 = (bf16[13,16,512]{2,1,0:T(8,128)(2,1)S(1)}, bf16[13,16,512]{2,1,0:T(8,128)(2,1)S(1)}, u32[]{:S(2)}, u32[]{:S(2)}) collective-permute-start(bf16[13,16,512]{2,1,0:T(8,128)(2,1)S(1)} %get-tuple-element.155), channel_id=1, source_target_pairs={{0,12},{1,13},{2,14},{3,15},{4,0},{5,1},{6,2},{7,3},{8,4},{9,5},{1... | collective-permute-start | bytes 638984 | tf_op jit(solution)/shard_map/ppermute | solution.py:51
  73.4 5.1 %collective-permute-done.19.refs_8_ = bf16[13,16,512]{2,1,0:T(8,128)(2,1)S(1)} collective-permute-done((bf16[13,16,512]{2,1,0:T(8,128)(2,1)S(1)}, bf16[13,16,512]{2,1,0:T(8,128)(2,1)S(1)}, u32[]{:S(2)}, u32[]{:S(2)}) %collective-permute-start.19) | collective-permute-done | bytes 213024 | tf_op jit(solution)/shard_map/ppermute | solution.py:51
  78.8 0.8 collective-permute-start.27
  79.6 0.8 collective-permute-start.26
  80.4 0.9 collective-permute-start.25
  81.3 2.9 %collective-permute-start.24 = (bf16[14,8,512]{2,1,0:T(8,128)(2,1)S(1)}, bf16[14,8,512]{2,1,0:T(8,128)(2,1)S(1)}, u32[]{:S(2)}, u32[]{:S(2)}) collective-permute-start(bf16[14,8,512]{2,1,0:T(8,128)(2,1)S(1)} %get-tuple-element.167), channel_id=1, source_target_pairs={{0,12},{1,13},{2,14},{3,15},{4,0},{5,1},{6,2},{7,3},{8,4},{9,5},{1... | collective-permute-start | bytes 344072 | tf_op jit(solution)/shard_map/ppermute | solution.py:51
  84.2 0.9 collective-permute-start.22
  85.1 1.3 %collective-permute-done.26 = bf16[13,8,512]{2,1,0:T(8,128)(2,1)S(1)} collective-permute-done((bf16[13,8,512]{2,1,0:T(8,128)(2,1)S(1)}, bf16[13,8,512]{2,1,0:T(8,128)(2,1)S(1)}, u32[]{:S(2)}, u32[]{:S(2)}) %collective-permute-start.26) | collective-permute-done | bytes 106528 | tf_op jit(solution)/shard_map/ppermute | solution.py:56
  86.4 0.8 collective-permute-done.25
  87.3 0.5 collective-permute-done.24
  87.8 2.8 %collective-permute-done.23 = bf16[14,8,512]{2,1,0:T(8,128)(2,1)S(1)} collective-permute-done((bf16[14,8,512]{2,1,0:T(8,128)(2,1)S(1)}, bf16[14,8,512]{2,1,0:T(8,128)(2,1)S(1)}, u32[]{:S(2)}, u32[]{:S(2)}) %collective-permute-start.23) | collective-permute-done | bytes 114720 | tf_op jit(solution)/shard_map/ppermute | solution.py:51
  90.6 0.8 collective-permute-done.22
  91.6 0.4 collective-permute-start.28
  92.2 9.2 %collective-permute-done.28 = bf16[27,8,512]{2,1,0:T(8,128)(2,1)S(1)} collective-permute-done((bf16[27,8,512]{2,1,0:T(8,128)(2,1)S(1)}, bf16[27,8,512]{2,1,0:T(8,128)(2,1)S(1)}, u32[]{:S(2)}, u32[]{:S(2)}) %collective-permute-start.28) | collective-permute-done | bytes 221216 | tf_op jit(solution)/shard_map/ppermute | solution.py:468
  101.6 1.9 %collective-permute-start.30 = (bf16[14,8,512]{2,1,0:T(8,128)(2,1)S(1)}, bf16[14,8,512]{2,1,0:T(8,128)(2,1)S(1)}, u32[]{:S(2)}, u32[]{:S(2)}) collective-permute-start(bf16[14,8,512]{2,1,0:T(8,128)(2,1)S(1)} %get-tuple-element.186), channel_id=1, source_target_pairs={{0,32},{16,48},{32,64},{48,80},{64,96},{80,112},{96,0},{112,16},{1... | collective-permute-start | bytes 344072 | tf_op jit(solution)/shard_map/ppermute | solution.py:56
  103.5 1.4 %collective-permute-start.32 = (f32[14,8,512]{2,1,0:T(8,128)S(1)}, f32[14,8,512]{2,1,0:T(8,128)S(1)}, u32[]{:S(2)}, u32[]{:S(2)}) collective-permute-start(f32[14,8,512]{2,1,0:T(8,128)S(1)} %get-tuple-element.176.refs_0_), channel_id=1, source_target_pairs={{0,96},{16,112},{32,0},{48,16},{64,32},{80,48},{96,64},{112,80},{1... | collective-permute-start | bytes 688136 | tf_op jit(solution)/shard_map/ppermute | solution.py:56
  105.0 0.7 collective-permute-start.31
  105.6 2.6 %collective-permute-start.33 = (bf16[13,8,512]{2,1,0:T(8,128)(2,1)S(1)}, bf16[13,8,512]{2,1,0:T(8,128)(2,1)S(1)}, u32[]{:S(2)}, u32[]{:S(2)}) collective-permute-start(bf16[13,8,512]{2,1,0:T(8,128)(2,1)S(1)} %get-tuple-element.184), channel_id=1, source_target_pairs={{0,96},{16,112},{32,0},{48,16},{64,32},{80,48},{96,64},{112,80},{1... | collective-permute-start | bytes 319496 | tf_op jit(solution)/shard_map/ppermute | solution.py:56
  108.3 2.3 %collective-permute-done.33.refs_5_ = bf16[13,8,512]{2,1,0:T(8,128)(2,1)S(1)} collective-permute-done((bf16[13,8,512]{2,1,0:T(8,128)(2,1)S(1)}, bf16[13,8,512]{2,1,0:T(8,128)(2,1)S(1)}, u32[]{:S(2)}, u32[]{:S(2)}) %collective-permute-start.33) | collective-permute-done | bytes 106528 | tf_op jit(solution)/shard_map/ppermute | solution.py:56
  110.6 3.6 %collective-permute-start.35 = (bf16[13,8,512]{2,1,0:T(8,128)(2,1)S(1)}, bf16[13,8,512]{2,1,0:T(8,128)(2,1)S(1)}, u32[]{:S(2)}, u32[]{:S(2)}) collective-permute-start(bf16[13,8,512]{2,1,0:T(8,128)(2,1)S(1)} %collective-permute-done.33.refs_5_), channel_id=1, source_target_pairs={{0,96},{16,112},{32,0},{48,16},{64,32},{80,48},{96,64},{112,80},{1... | collective-permute-start | bytes 319496 | tf_op jit(solution)/shard_map/ppermute | solution.py:56
  114.2 1.2 %shard_map.58 = bf16[4,8,16,512]{3,2,1,0:T(8,128)(2,1)} custom-call(bf16[4,8,16,512]{3,2,1,0:T(8,128)(2,1)S(1)} %copy-done, f32[4,8,16,512]{3,2,1,0:T(8,128)S(1)} %get-tuple-element.143.keep, f32[2,4,8,16,512]{4,3,2,1,0:T(8,128)S(1)} %collective-permute-done.21.near, bf16[4,8,16,512]{3,2,1,0:T(8,128)(2,1)S(1)} %collective-permute-done.29.far), custom_call_target="tpu_custom_call" | custom-call | tf_op jit(solution)/shard_map/pallas_call | solution.py:330
  115.4 1.1 collective-permute-done.35.refs_7_
  116.5 1.3 %shard_map.59 = f32[27,32,512]{2,1,0:T(8,128)} custom-call(f32[14,8,512]{2,1,0:T(8,128)S(1)} %get-tuple-element.176.refs_0_, f32[13,8,512]{2,1,0:T(8,128)S(1)} %get-tuple-element.177.refs_1_, bf16[14,8,512]{2,1,0:T(8,128)(2,1)S(1)} %collective-permute-done.30.refs_2_, f32[13,8,512]{2,1,0:T(8,128)S(1)} %collective-permute-done.31.refs_3_, ...), custom_call_target="tpu_custom_call" | custom-call | tf_op jit(solution)/shard_map/pallas_call | solution.py:403
  (50 shorter events, 1.8 us)
Async XLA Ops:
  0.6 7.4 %copy-start.2 = (bf16[27,32,512]{2,1,0:T(8,128)(2,1)S(1)}, bf16[27,32,512]{2,1,0:T(8,128)(2,1)}, u32[]{:S(2)}) copy-start(bf16[27,32,512]{2,1,0:T(8,128)(2,1)} %own) | copy-start | bytes 2654212
  2.1 5.6 %collective-permute-start.1 = (bf16[4,8,16,512]{3,2,1,0:T(8,128)(2,1)S(1)}, bf16[4,8,16,512]{3,2,1,0:T(8,128)(2,1)S(1)}, u32[]{:S(2)}, u32[]{:S(2)}) collective-permute-start(bf16[4,8,16,512]{3,2,1,0:T(8,128)(2,1)S(1)} %fusion.3.own_act), channel_id=1, source_target_pairs={{0,1},{1,0},{2,3},{3,2},{4,5},{5,4},{6,7},{7,6},{8,9},{9,8},{10,11... | collective-permute-start | bytes 1572872 | tf_op jit(solution)/shard_map/ppermute | solution.py:43
  2.2 15.4 %collective-permute-start.5 = (bf16[4,8,16,512]{3,2,1,0:T(8,128)(2,1)S(1)}, bf16[4,8,16,512]{3,2,1,0:T(8,128)(2,1)S(1)}, u32[]{:S(2)}, u32[]{:S(2)}) collective-permute-start(bf16[4,8,16,512]{3,2,1,0:T(8,128)(2,1)S(1)} %fusion.3.own_act), channel_id=1, source_target_pairs={{0,2},{1,3},{2,0},{3,1},{4,6},{5,7},{6,4},{7,5},{8,10},{9,11},{10,... | collective-permute-start | bytes 1572872 | tf_op jit(solution)/shard_map/ppermute | solution.py:43
  5.2 2.4 %collective-permute-start = (bf16[8,16,512]{2,1,0:T(8,128)(2,1)S(1)}, bf16[8,16,512]{2,1,0:T(8,128)(2,1)S(1)}, u32[]{:S(2)}, u32[]{:S(2)}) collective-permute-start(bf16[8,16,512]{2,1,0:T(8,128)(2,1)S(1)} %select_bitcast_fusion), channel_id=1, source_target_pairs={{3,4},{7,8},{11,12},{4,3},{8,7},{12,11},{19,20},{23,24},{27,28},{2... | collective-permute-start | bytes 393224 | tf_op jit(solution)/shard_map/ppermute | solution.py:421
  5.9 1.0 copy-start.1
  8.0 24.6 %collective-permute-start.8 = (bf16[27,32,512]{2,1,0:T(8,128)(2,1)S(1)}, bf16[27,32,512]{2,1,0:T(8,128)(2,1)S(1)}, u32[]{:S(2)}, u32[]{:S(2)}) collective-permute-start(bf16[27,32,512]{2,1,0:T(8,128)(2,1)S(1)} %copy-done.2), channel_id=1, source_target_pairs={{0,12},{1,13},{2,14},{3,15},{4,0},{5,1},{6,2},{7,3},{8,4},{9,5},{1... | collective-permute-start | bytes 2654216 | tf_op jit(solution)/shard_map/ppermute | solution.py:51
  16.3 17.4 %collective-permute-start.9 = (bf16[27,32,512]{2,1,0:T(8,128)(2,1)S(1)}, bf16[27,32,512]{2,1,0:T(8,128)(2,1)S(1)}, u32[]{:S(2)}, u32[]{:S(2)}) collective-permute-start(bf16[27,32,512]{2,1,0:T(8,128)(2,1)S(1)} %copy-done.2), channel_id=1, source_target_pairs={{0,4},{1,5},{2,6},{3,7},{4,8},{5,9},{6,10},{7,11},{8,12},{9,13},{1... | collective-permute-start | bytes 2654216 | tf_op jit(solution)/shard_map/ppermute | solution.py:51
  16.3 2.8 %collective-permute-start.2 = (bf16[5,8,16,128]{3,2,1,0:T(8,128)(2,1)S(1)}, bf16[5,8,16,128]{3,2,1,0:T(8,128)(2,1)S(1)}, u32[]{:S(2)}, u32[]{:S(2)}) collective-permute-start(bf16[5,8,16,128]{3,2,1,0:T(8,128)(2,1)S(1)} %get-tuple-element.107), channel_id=1, source_target_pairs={{0,1},{1,0},{2,3},{3,2},{4,5},{5,4},{6,7},{7,6},{8,9},{9,8},{10,11... | collective-permute-start | bytes 491528 | tf_op jit(solution)/shard_map/ppermute | solution.py:43
  16.3 7.0 %collective-permute-start.3 = (bf16[5,8,16,128]{3,2,1,0:T(8,128)(2,1)S(1)}, bf16[5,8,16,128]{3,2,1,0:T(8,128)(2,1)S(1)}, u32[]{:S(2)}, u32[]{:S(2)}) collective-permute-start(bf16[5,8,16,128]{3,2,1,0:T(8,128)(2,1)S(1)} %get-tuple-element.108), channel_id=1, source_target_pairs={{0,2},{1,3},{2,0},{3,1},{4,6},{5,7},{6,4},{7,5},{8,10},{9,11},{10,... | collective-permute-start | bytes 491528 | tf_op jit(solution)/shard_map/ppermute | solution.py:43
  17.6 8.5 %collective-permute-start.4 = (bf16[5,8,16,128]{3,2,1,0:T(8,128)(2,1)S(1)}, bf16[5,8,16,128]{3,2,1,0:T(8,128)(2,1)S(1)}, u32[]{:S(2)}, u32[]{:S(2)}) collective-permute-start(bf16[5,8,16,128]{3,2,1,0:T(8,128)(2,1)S(1)} %get-tuple-element.109), channel_id=1, source_target_pairs={{0,3},{1,2},{2,1},{3,0},{4,7},{5,6},{6,5},{7,4},{8,11},{9,10},{10,... | collective-permute-start | bytes 491528 | tf_op jit(solution)/shard_map/ppermute | solution.py:43
  26.1 13.0 %collective-permute-start.10 = (bf16[4,8,16,512]{3,2,1,0:T(8,128)(2,1)S(1)}, bf16[4,8,16,512]{3,2,1,0:T(8,128)(2,1)S(1)}, u32[]{:S(2)}, u32[]{:S(2)}) collective-permute-start(bf16[4,8,16,512]{3,2,1,0:T(8,128)(2,1)S(1)} %collective-permute-done.5.far), channel_id=1, source_target_pairs={{0,1},{1,0},{2,3},{3,2},{4,5},{5,4},{6,7},{7,6},{8,9},{9,8},{10,11... | collective-permute-start | bytes 1572872 | tf_op jit(solution)/shard_map/ppermute | solution.py:43
  26.6 6.0 %collective-permute-start.6 = (bf16[4,5,16,128]{3,2,1,0:T(8,128)(2,1)S(1)}, bf16[4,5,16,128]{3,2,1,0:T(8,128)(2,1)S(1)}, u32[]{:S(2)}, u32[]{:S(2)}) collective-permute-start(bf16[4,5,16,128]{3,2,1,0:T(8,128)(2,1)S(1)} %get-tuple-element.114), channel_id=1, source_target_pairs={{0,16},{32,48},{64,80},{96,112},{16,0},{48,32},{80,64},{112,96},{1... | collective-permute-start | bytes 245768 | tf_op jit(solution)/shard_map/ppermute | solution.py:62
  30.0 2.6 %collective-permute-start.7 = (bf16[4,5,16,128]{3,2,1,0:T(8,128)(2,1)S(1)}, bf16[4,5,16,128]{3,2,1,0:T(8,128)(2,1)S(1)}, u32[]{:S(2)}, u32[]{:S(2)}) collective-permute-start(bf16[4,5,16,128]{3,2,1,0:T(8,128)(2,1)S(1)} %get-tuple-element.115), channel_id=1, source_target_pairs={{16,32},{48,64},{80,96},{32,16},{64,48},{96,80},{17,33},{49,65},{8... | collective-permute-start | bytes 245768 | tf_op jit(solution)/shard_map/ppermute | solution.py:62
  33.8 24.1 %collective-permute-start.11 = (bf16[14,32,512]{2,1,0:T(8,128)(2,1)S(1)}, bf16[14,32,512]{2,1,0:T(8,128)(2,1)S(1)}, u32[]{:S(2)}, u32[]{:S(2)}) collective-permute-start(bf16[14,32,512]{2,1,0:T(8,128)(2,1)S(1)} %slice.23), channel_id=1, source_target_pairs={{0,4},{1,5},{2,6},{3,7},{4,8},{5,9},{6,10},{7,11},{8,12},{9,13},{1... | collective-permute-start | bytes 1376264 | tf_op jit(solution)/shard_map/ppermute | solution.py:51
  33.9 20.7 %collective-permute-start.12 = (bf16[13,32,512]{2,1,0:T(8,128)(2,1)S(1)}, bf16[13,32,512]{2,1,0:T(8,128)(2,1)S(1)}, u32[]{:S(2)}, u32[]{:S(2)}) collective-permute-start(bf16[13,32,512]{2,1,0:T(8,128)(2,1)S(1)} %slice.24), channel_id=1, source_target_pairs={{0,12},{1,13},{2,14},{3,15},{4,0},{5,1},{6,2},{7,3},{8,4},{9,5},{1... | collective-permute-start | bytes 1277960 | tf_op jit(solution)/shard_map/ppermute | solution.py:51
  46.7 19.9 %collective-permute-start.13 = (bf16[2,14,16,512]{3,2,1,0:T(8,128)(2,1)S(1)}, bf16[2,14,16,512]{3,2,1,0:T(8,128)(2,1)S(1)}, u32[]{:S(2)}, u32[]{:S(2)}) collective-permute-start(bf16[2,14,16,512]{3,2,1,0:T(8,128)(2,1)S(1)} %get-tuple-element.139), channel_id=1, source_target_pairs={{0,32},{16,48},{32,64},{48,80},{64,96},{80,112},{96,0},{112,16},{1... | collective-permute-start | bytes 1376264 | tf_op jit(solution)/shard_map/ppermute | solution.py:56
  53.3 13.3 %collective-permute-start.14 = (bf16[2,14,16,512]{3,2,1,0:T(8,128)(2,1)S(1)}, bf16[2,14,16,512]{3,2,1,0:T(8,128)(2,1)S(1)}, u32[]{:S(2)}, u32[]{:S(2)}) collective-permute-start(bf16[2,14,16,512]{3,2,1,0:T(8,128)(2,1)S(1)} %get-tuple-element.140), channel_id=1, source_target_pairs={{0,96},{16,112},{32,0},{48,16},{64,32},{80,48},{96,64},{112,80},{1... | collective-permute-start | bytes 1376264 | tf_op jit(solution)/shard_map/ppermute | solution.py:56
  54.6 12.0 %collective-permute-start.15 = (bf16[2,13,16,512]{3,2,1,0:T(8,128)(2,1)S(1)}, bf16[2,13,16,512]{3,2,1,0:T(8,128)(2,1)S(1)}, u32[]{:S(2)}, u32[]{:S(2)}) collective-permute-start(bf16[2,13,16,512]{3,2,1,0:T(8,128)(2,1)S(1)} %get-tuple-element.141), channel_id=1, source_target_pairs={{0,4},{1,5},{2,6},{3,7},{4,8},{5,9},{6,10},{7,11},{8,12},{9,13},{1... | collective-permute-start | bytes 1277960 | tf_op jit(solution)/shard_map/ppermute | solution.py:51
  54.6 12.0 %collective-permute-start.16 = (bf16[2,13,16,512]{3,2,1,0:T(8,128)(2,1)S(1)}, bf16[2,13,16,512]{3,2,1,0:T(8,128)(2,1)S(1)}, u32[]{:S(2)}, u32[]{:S(2)}) collective-permute-start(bf16[2,13,16,512]{3,2,1,0:T(8,128)(2,1)S(1)} %get-tuple-element.142), channel_id=1, source_target_pairs={{0,12},{1,13},{2,14},{3,15},{4,0},{5,1},{6,2},{7,3},{8,4},{9,5},{1... | collective-permute-start | bytes 1277960 | tf_op jit(solution)/shard_map/ppermute | solution.py:51
  66.6 11.9 %collective-permute-start.21 = (f32[2,4,8,16,512]{4,3,2,1,0:T(8,128)S(1)}, f32[2,4,8,16,512]{4,3,2,1,0:T(8,128)S(1)}, u32[]{:S(2)}, u32[]{:S(2)}) collective-permute-start(f32[2,4,8,16,512]{4,3,2,1,0:T(8,128)S(1)} %get-tuple-element.156), channel_id=1, source_target_pairs={{0,1},{1,0},{2,3},{3,2},{4,5},{5,4},{6,7},{7,6},{8,9},{9,8},{10,11... | collective-permute-start | bytes 6291464 | tf_op jit(solution)/shard_map/ppermute | solution.py:43
  66.9 11.6 %collective-permute-start.17 = (bf16[14,16,512]{2,1,0:T(8,128)(2,1)S(1)}, bf16[14,16,512]{2,1,0:T(8,128)(2,1)S(1)}, u32[]{:S(2)}, u32[]{:S(2)}) collective-permute-start(bf16[14,16,512]{2,1,0:T(8,128)(2,1)S(1)} %get-tuple-element.152), channel_id=1, source_target_pairs={{0,32},{16,48},{32,64},{48,80},{64,96},{80,112},{96,0},{112,16},{1... | collective-permute-start | bytes 688136 | tf_op jit(solution)/shard_map/ppermute | solution.py:56
  67.6 10.9 %collective-permute-start.18 = (bf16[14,16,512]{2,1,0:T(8,128)(2,1)S(1)}, bf16[14,16,512]{2,1,0:T(8,128)(2,1)S(1)}, u32[]{:S(2)}, u32[]{:S(2)}) collective-permute-start(bf16[14,16,512]{2,1,0:T(8,128)(2,1)S(1)} %get-tuple-element.153), channel_id=1, source_target_pairs={{0,96},{16,112},{32,0},{48,16},{64,32},{80,48},{96,64},{112,80},{1... | collective-permute-start | bytes 688136 | tf_op jit(solution)/shard_map/ppermute | solution.py:56
  70.2 8.3 %collective-permute-start.19 = (bf16[13,16,512]{2,1,0:T(8,128)(2,1)S(1)}, bf16[13,16,512]{2,1,0:T(8,128)(2,1)S(1)}, u32[]{:S(2)}, u32[]{:S(2)}) collective-permute-start(bf16[13,16,512]{2,1,0:T(8,128)(2,1)S(1)} %get-tuple-element.154), channel_id=1, source_target_pairs={{0,4},{1,5},{2,6},{3,7},{4,8},{5,9},{6,10},{7,11},{8,12},{9,13},{1... | collective-permute-start | bytes 638984 | tf_op jit(solution)/shard_map/ppermute | solution.py:51
  70.2 8.3 %collective-permute-start.20 = (bf16[13,16,512]{2,1,0:T(8,128)(2,1)S(1)}, bf16[13,16,512]{2,1,0:T(8,128)(2,1)S(1)}, u32[]{:S(2)}, u32[]{:S(2)}) collective-permute-start(bf16[13,16,512]{2,1,0:T(8,128)(2,1)S(1)} %get-tuple-element.155), channel_id=1, source_target_pairs={{0,12},{1,13},{2,14},{3,15},{4,0},{5,1},{6,2},{7,3},{8,4},{9,5},{1... | collective-permute-start | bytes 638984 | tf_op jit(solution)/shard_map/ppermute | solution.py:51
  78.8 5.4 %collective-permute-start.27 = (bf16[13,8,512]{2,1,0:T(8,128)(2,1)S(1)}, bf16[13,8,512]{2,1,0:T(8,128)(2,1)S(1)}, u32[]{:S(2)}, u32[]{:S(2)}) collective-permute-start(bf16[13,8,512]{2,1,0:T(8,128)(2,1)S(1)} %get-tuple-element.171), channel_id=1, source_target_pairs={{0,96},{16,112},{32,0},{48,16},{64,32},{80,48},{96,64},{112,80},{1... | collective-permute-start | bytes 319496 | tf_op jit(solution)/shard_map/ppermute | solution.py:56
  79.6 6.8 %collective-permute-start.26 = (bf16[13,8,512]{2,1,0:T(8,128)(2,1)S(1)}, bf16[13,8,512]{2,1,0:T(8,128)(2,1)S(1)}, u32[]{:S(2)}, u32[]{:S(2)}) collective-permute-start(bf16[13,8,512]{2,1,0:T(8,128)(2,1)S(1)} %get-tuple-element.170), channel_id=1, source_target_pairs={{0,64},{16,80},{32,96},{48,112},{64,0},{80,16},{96,32},{112,48},{1... | collective-permute-start | bytes 319496 | tf_op jit(solution)/shard_map/ppermute | solution.py:56
  80.4 6.8 %collective-permute-start.25 = (bf16[13,8,512]{2,1,0:T(8,128)(2,1)S(1)}, bf16[13,8,512]{2,1,0:T(8,128)(2,1)S(1)}, u32[]{:S(2)}, u32[]{:S(2)}) collective-permute-start(bf16[13,8,512]{2,1,0:T(8,128)(2,1)S(1)} %get-tuple-element.169), channel_id=1, source_target_pairs={{0,32},{16,48},{32,64},{48,80},{64,96},{80,112},{96,0},{112,16},{1... | collective-permute-start | bytes 319496 | tf_op jit(solution)/shard_map/ppermute | solution.py:56
  81.3 6.5 %collective-permute-start.24 = (bf16[14,8,512]{2,1,0:T(8,128)(2,1)S(1)}, bf16[14,8,512]{2,1,0:T(8,128)(2,1)S(1)}, u32[]{:S(2)}, u32[]{:S(2)}) collective-permute-start(bf16[14,8,512]{2,1,0:T(8,128)(2,1)S(1)} %get-tuple-element.167), channel_id=1, source_target_pairs={{0,12},{1,13},{2,14},{3,15},{4,0},{5,1},{6,2},{7,3},{8,4},{9,5},{1... | collective-permute-start | bytes 344072 | tf_op jit(solution)/shard_map/ppermute | solution.py:51
  84.2 6.4 %collective-permute-start.23 = (bf16[14,8,512]{2,1,0:T(8,128)(2,1)S(1)}, bf16[14,8,512]{2,1,0:T(8,128)(2,1)S(1)}, u32[]{:S(2)}, u32[]{:S(2)}) collective-permute-start(bf16[14,8,512]{2,1,0:T(8,128)(2,1)S(1)} %get-tuple-element.166), channel_id=1, source_target_pairs={{0,8},{1,9},{2,10},{3,11},{4,12},{5,13},{6,14},{7,15},{8,0},{9,1},... | collective-permute-start | bytes 344072 | tf_op jit(solution)/shard_map/ppermute | solution.py:51
  84.2 7.2 %collective-permute-start.22 = (bf16[14,8,512]{2,1,0:T(8,128)(2,1)S(1)}, bf16[14,8,512]{2,1,0:T(8,128)(2,1)S(1)}, u32[]{:S(2)}, u32[]{:S(2)}) collective-permute-start(bf16[14,8,512]{2,1,0:T(8,128)(2,1)S(1)} %get-tuple-element.165), channel_id=1, source_target_pairs={{0,4},{1,5},{2,6},{3,7},{4,8},{5,9},{6,10},{7,11},{8,12},{9,13},{1... | collective-permute-start | bytes 344072 | tf_op jit(solution)/shard_map/ppermute | solution.py:51
  91.6 22.6 %copy-start = (bf16[4,8,16,512]{3,2,1,0:T(8,128)(2,1)S(1)}, bf16[4,8,16,512]{3,2,1,0:T(8,128)(2,1)}, u32[]{:S(2)}) copy-start(bf16[4,8,16,512]{3,2,1,0:T(8,128)(2,1)} %pre.1) | copy-start | bytes 1572868
  91.6 9.9 %collective-permute-start.28 = (bf16[27,8,512]{2,1,0:T(8,128)(2,1)S(1)}, bf16[27,8,512]{2,1,0:T(8,128)(2,1)S(1)}, u32[]{:S(2)}, u32[]{:S(2)}) collective-permute-start(bf16[27,8,512]{2,1,0:T(8,128)(2,1)S(1)} %pad_maximum_fusion), channel_id=1, source_target_pairs={{0,16},{16,0},{32,48},{48,32},{64,80},{80,64},{96,112},{112,96},{1... | collective-permute-start | bytes 663560 | tf_op jit(solution)/shard_map/ppermute | solution.py:468
  101.5 12.7 %collective-permute-start.29 = (bf16[4,8,16,512]{3,2,1,0:T(8,128)(2,1)S(1)}, bf16[4,8,16,512]{3,2,1,0:T(8,128)(2,1)S(1)}, u32[]{:S(2)}, u32[]{:S(2)}) collective-permute-start(bf16[4,8,16,512]{3,2,1,0:T(8,128)(2,1)S(1)} %fusion.4), channel_id=1, source_target_pairs={{0,2},{1,3},{2,0},{3,1},{4,6},{5,7},{6,4},{7,5},{8,10},{9,11},{10,... | collective-permute-start | bytes 1572872 | tf_op jit(solution)/shard_map/ppermute | solution.py:43
  101.6 6.7 %collective-permute-start.30 = (bf16[14,8,512]{2,1,0:T(8,128)(2,1)S(1)}, bf16[14,8,512]{2,1,0:T(8,128)(2,1)S(1)}, u32[]{:S(2)}, u32[]{:S(2)}) collective-permute-start(bf16[14,8,512]{2,1,0:T(8,128)(2,1)S(1)} %get-tuple-element.186), channel_id=1, source_target_pairs={{0,32},{16,48},{32,64},{48,80},{64,96},{80,112},{96,0},{112,16},{1... | collective-permute-start | bytes 344072 | tf_op jit(solution)/shard_map/ppermute | solution.py:56
  103.5 13.0 %collective-permute-start.32 = (f32[14,8,512]{2,1,0:T(8,128)S(1)}, f32[14,8,512]{2,1,0:T(8,128)S(1)}, u32[]{:S(2)}, u32[]{:S(2)}) collective-permute-start(f32[14,8,512]{2,1,0:T(8,128)S(1)} %get-tuple-element.176.refs_0_), channel_id=1, source_target_pairs={{0,96},{16,112},{32,0},{48,16},{64,32},{80,48},{96,64},{112,80},{1... | collective-permute-start | bytes 688136 | tf_op jit(solution)/shard_map/ppermute | solution.py:56
  105.0 10.5 %collective-permute-start.31 = (f32[13,8,512]{2,1,0:T(8,128)S(1)}, f32[13,8,512]{2,1,0:T(8,128)S(1)}, u32[]{:S(2)}, u32[]{:S(2)}) collective-permute-start(f32[13,8,512]{2,1,0:T(8,128)S(1)} %get-tuple-element.177.refs_1_), channel_id=1, source_target_pairs={{0,32},{16,48},{32,64},{48,80},{64,96},{80,112},{96,0},{112,16},{1... | collective-permute-start | bytes 638984 | tf_op jit(solution)/shard_map/ppermute | solution.py:56
  105.6 5.0 %collective-permute-start.33 = (bf16[13,8,512]{2,1,0:T(8,128)(2,1)S(1)}, bf16[13,8,512]{2,1,0:T(8,128)(2,1)S(1)}, u32[]{:S(2)}, u32[]{:S(2)}) collective-permute-start(bf16[13,8,512]{2,1,0:T(8,128)(2,1)S(1)} %get-tuple-element.184), channel_id=1, source_target_pairs={{0,96},{16,112},{32,0},{48,16},{64,32},{80,48},{96,64},{112,80},{1... | collective-permute-start | bytes 319496 | tf_op jit(solution)/shard_map/ppermute | solution.py:56
  108.3 8.2 %collective-permute-start.34 = (bf16[14,8,512]{2,1,0:T(8,128)(2,1)S(1)}, bf16[14,8,512]{2,1,0:T(8,128)(2,1)S(1)}, u32[]{:S(2)}, u32[]{:S(2)}) collective-permute-start(bf16[14,8,512]{2,1,0:T(8,128)(2,1)S(1)} %collective-permute-done.30.refs_2_), channel_id=1, source_target_pairs={{0,32},{16,48},{32,64},{48,80},{64,96},{80,112},{96,0},{112,16},{1... | collective-permute-start | bytes 344072 | tf_op jit(solution)/shard_map/ppermute | solution.py:56
  110.6 5.9 %collective-permute-start.35 = (bf16[13,8,512]{2,1,0:T(8,128)(2,1)S(1)}, bf16[13,8,512]{2,1,0:T(8,128)(2,1)S(1)}, u32[]{:S(2)}, u32[]{:S(2)}) collective-permute-start(bf16[13,8,512]{2,1,0:T(8,128)(2,1)S(1)} %collective-permute-done.33.refs_5_), channel_id=1, source_target_pairs={{0,96},{16,112},{32,0},{48,16},{64,32},{80,48},{96,64},{112,80},{1... | collective-permute-start | bytes 319496 | tf_op jit(solution)/shard_map/ppermute | solution.py:56
